TPU v7x, 32 devices: a whole 2x2x4 slice. The times are simulated.
32 devices in a mesh: pole: 4 (over y, x), row: 4 (over z), col: 2 (over core).
Axes of the slice: x: 2, y: 2, z: 4, core: 2. Of those that a mesh axis runs over, the one named last changes fastest.
Arguments:
- found_inverse: bfloat16 [4, 2, 1024, 4, 2, 128], P('pole', None, 'row', None, 'col'), may hold values from -0.375 to 0.375
- l_panel: bfloat16 [4, 2, 1024, 512], P('pole', None, ('row', 'col')), may hold values from -1.5 to 1.5
- block_pattern: int32 [8, 4], P(('row', 'col')), may hold values 0 or 1
- sup_widths: int32 [4], replicated, may hold values from 1 to 128, 320 in all
- diag_inverse: bfloat16 [4, 2, 512, 128], P('pole'), may hold values from -6 to 6
- pole_weights: float32 [4, 2], P('pole'), may hold values from -4 to 4
Outputs:
- density: float32 [512, 1024], P('col', 'row')
- diagonal: float32 [512, 128], replicated
Inputs may be any that keep to these rules, and one draw needn't show every extreme that they name: `sup_widths`: one supernode has exactly 128 columns.
All inputs are finite; a program needn't handle non-finite values. No bound on the sum of `block_pattern` on one device may be relied on, other than what follows from the above.
Results may differ from a plain program's by a relative error of at most 0.0003.
Values may be sent and summed in bfloat16 or wider, within the bound.
No kernel may reach another device: no remote copies, remote signals or barrier semaphores. Data moves between devices by JAX's collectives and lax.ppermute only.
A program may use at most 128 MiB of HBM per device.

v0:
```python
import jax
import jax.numpy as jnp
from jax import lax
from jax.sharding import PartitionSpec as P


def contract(left, right):
    return jnp.einsum("jk,ij->ki", left, right, preferred_element_type=jnp.float32)


def pair_product(left, right):
    return jnp.einsum("ika,kbi->kab", left, right, precision=lax.Precision.HIGHEST)


def per_device(found_inverse, l_panel, block_pattern, sup_widths, diag_inverse, pole_weights):
    slot_width = diag_inverse.shape[-1]
    total_cols = l_panel.shape[-1]
    supernodes = total_cols // slot_width
    row_count = lax.axis_size("row")
    row_index = lax.axis_index("row")
    col_index = lax.axis_index("col")
    columns = jnp.arange(total_cols, dtype=jnp.int32)
    column_ok = columns % slot_width < jnp.repeat(sup_widths, slot_width)
    block_ok = jnp.repeat(block_pattern[0], slot_width) == 1
    masked = jnp.where(
        (column_ok & block_ok)[None, None, :], l_panel[0], jnp.zeros((), jnp.bfloat16)
    )
    own_rows = lax.all_gather(masked, "col", axis=1, tiled=True)
    column_rows = lax.all_gather(masked, "row", axis=1, tiled=True)
    local_rows = found_inverse.shape[2]
    inverse = found_inverse[0].reshape(2, local_rows, row_count * slot_width)
    part_real = contract(column_rows[1], inverse[1]) - contract(column_rows[0], inverse[0])
    part_imag = -(contract(column_rows[1], inverse[0]) + contract(column_rows[0], inverse[1]))
    w_real = pole_weights[0, 0]
    w_imag = pole_weights[0, 1]
    weighted = w_real * part_real - w_imag * part_imag
    whole = lax.psum(weighted, "pole")
    density = lax.psum_scatter(whole, "col", scatter_dimension=0, tiled=True)
    lifted = own_rows.astype(jnp.float32).reshape(2, local_rows, supernodes, slot_width)
    upper_real = part_real.reshape(supernodes, slot_width, local_rows)
    upper_imag = part_imag.reshape(supernodes, slot_width, local_rows)
    t_real = pair_product(lifted[0], upper_real) - pair_product(lifted[1], upper_imag)
    t_imag = pair_product(lifted[0], upper_imag) + pair_product(lifted[1], upper_real)
    lead_flag = ((row_index == 0) & (col_index == 0)).astype(jnp.float32)
    d_real = diag_inverse[0, 0].astype(jnp.float32).reshape(supernodes, slot_width, slot_width)
    d_imag = diag_inverse[0, 1].astype(jnp.float32).reshape(supernodes, slot_width, slot_width)
    local_term = lead_flag * (w_real * d_real - w_imag * d_imag) - (
        w_real * t_real - w_imag * t_imag
    )
    diagonal = lax.psum(local_term.reshape(total_cols, slot_width), ("pole", "row", "col"))
    return (density, diagonal)


def solution(mesh):
    in_specs = (
        P("pole", None, "row", None, "col", None),
        P("pole", None, ("row", "col"), None),
        P(("row", "col"), None),
        P(),
        P("pole", None, None, None),
        P("pole", None),
    )
    out_specs = (P("col", "row"), P())
    return jax.shard_map(
        per_device, mesh=mesh, in_specs=in_specs, out_specs=out_specs, check_vma=False
    )
```

profile of v0, /device:TPU:0, one launch (start us, length us, event | category | flops | bytes accessed | tf_op | source)
XLA Modules:
  0.0 240.2 jit_solution(9634384942498772122)
XLA Ops:
  7.2 0.0 copy-start.6
  7.2 0.0 all-gather.2.cloned.1.call-start
  7.2 0.7 compare_bitcast_fusion
  7.9 0.0 copy-done.6
  7.9 0.1 fusion.19
  8.0 0.0 copy-start.5
  8.0 1.7 bitcast_select_fusion
  9.6 0.0 copy-start.1
  9.7 0.0 copy-start.2
  9.7 0.0 all-gather.2.cloned.1.call-update
  9.7 0.0 reduce-scatter.2.cloned.1.call-start
  9.7 0.0 copy-done.5
  9.7 0.7 fusion.22
  10.4 0.2 copy-done.1
  10.6 2.2 all_gather.7
  12.8 0.0 copy-done.2
  12.9 0.2 fusion.21
  13.1 27.7 %all-gather.2.cloned.1.call-done = bf16[2,512,512]{2,1,0:T(8,128)(2,1)} async-done(((bf16[2,128,512]{2,1,0:T(8,128)(2,1)}), bf16[2,512,512]{2,1,0:T(8,128)(2,1)}) %all-gather.2.cloned.1.call-update) | async-done | bytes 1048592 | tf_op jit(solution)/shard_map/all_gather | solution.py:29
  40.8 0.0 copy-start
  40.8 1.5 fusion.6
  42.3 0.0 copy-done
  42.3 0.3 fusion.5
  42.7 0.3 convolution_subtract_fusion
  43.0 2.5 %multiply_subtract_fusion = (f32[512,256]{1,0:T(8,128)}, f32[512,256]{1,0:T(8,128)S(1)}) fusion(f32[512,256]{1,0:T(8,128)S(1)} %convolution_subtract_fusion, f32[]{:T(128)} %bitcast.7, f32[]{:T(128)} %bitcast, f32[512,256]{1,0:T(8,128)S(1)} %fusion.5, bf16[32,8,4,128]{3,2,1,0:T(4,128)(2,1)S(1)} %bitcast.65, bf16[2,512,512]{2,1,0:T(8,128)(2,1)S(1)} %copy-done), kind=kOutput, calls=%fused_computation.11 | convolution fusion | flops 134873088 | bytes 2883592 | tf_op jit(solution)/shard_map/jk,ij->ki/dot_general | solution.py:8
  45.5 0.0 copy-start.3
  45.5 0.0 reduce-scatter.2.cloned.1.call-update
  45.5 0.0 all-reduce.3.cloned.1.call-start
  45.6 0.9 copy-done.3
  46.4 1.4 subtract_multiply_fusion
  47.8 0.1 copy.8
  48.0 0.1 copy.9
  48.1 0.4 fusion.24
  48.5 0.4 fusion.23
  49.0 1.1 fusion.4
  50.1 1.8 fusion.3
  51.8 0.0 all-reduce.3.cloned.1.call-update
  51.8 0.0 all-reduce.5.cloned.1.call-start
  51.9 1.2 reduce-scatter.2.cloned.1.call-done
  53.1 0.0 all-reduce.5.cloned.1.call-update
  53.1 133.1 %all-reduce.3.cloned.1.call-done = f32[512,128]{1,0:T(8,128)} async-done(((f32[512,128]{1,0:T(8,128)}), f32[512,128]{1,0:T(8,128)}) %all-reduce.3.cloned.1.call-update) | async-done | bytes 262160 | tf_op jit(solution)/shard_map/psum | solution.py:50
  186.2 0.0 copy-start.4
  186.2 45.0 %all-reduce.5.cloned.1.call-done = f32[256,256]{1,0:T(8,128)} async-done(((f32[256,256]{1,0:T(8,128)}), f32[256,256]{1,0:T(8,128)}) %all-reduce.5.cloned.1.call-update) | async-done | bytes 262160 | tf_op jit(solution)/shard_map/psum | solution.py:37
  231.2 1.7 copy.32
  232.9 0.0 copy-done.4
  232.9 0.7 copy.33
  (1 shorter events, 0.0 us)
Async XLA Ops:
  7.2 0.7 copy-start.6
  7.2 33.6 %all-gather.2.cloned.1.call-start = ((), (), s32[]{:S(2)}) async-start(), calls=%async_computation.1 | async-start | bytes 1310720 | tf_op jit(solution)/shard_map/all_gather | solution.py:29
  8.0 1.8 copy-start.5
  9.6 0.9 copy-start.1
  9.7 3.2 %copy-start.2 = (bf16[1,2,256,4,1,128]{5,3,4,2,1,0:T(4,128)(2,1)S(1)}, bf16[1,2,256,4,1,128]{5,3,4,2,1,0:T(4,128)(2,1)}, u32[]{:S(2)}) copy-start(bf16[1,2,256,4,1,128]{5,3,4,2,1,0:T(4,128)(2,1)} %param.6) | copy-start | bytes 1572868
  9.7 43.4 %reduce-scatter.2.cloned.1.call-start = ((), (), s32[]{:S(2)}) async-start(), calls=%async_computation.3 | async-start | bytes 786432 | tf_op jit(solution)/shard_map/reduce_scatter | solution.py:38
  40.8 1.5 copy-start
  45.5 0.9 copy-start.3
  45.5 140.7 %all-reduce.3.cloned.1.call-start = ((), (), s32[]{:S(2)}) async-start(), calls=%async_computation.2 | async-start | bytes 524288 | tf_op jit(solution)/shard_map/psum | solution.py:50
  51.8 179.4 %all-reduce.5.cloned.1.call-start = ((), (), s32[]{:S(2)}) async-start(), calls=%async_computation.4 | async-start | bytes 524288 | tf_op jit(solution)/shard_map/psum | solution.py:37
  186.2 46.7 %copy-start.4 = (f32[512,128]{1,0:T(8,128)S(1)}, f32[512,128]{1,0:T(8,128)}, u32[]{:S(2)}) copy-start(f32[512,128]{1,0:T(8,128)} %all-reduce.3.cloned.1.call-done) | copy-start | bytes 786436
Sparse Core Ops, SparseCore 0:
  10.2 30.6 all-gather.1
  45.6 7.4 reduce-scatter.1
  60.1 126.1 all-reduce.2
  189.3 41.9 all-reduce.4
where the time goes:
time: 240 us
  waiting for transfers between devices  207 us (86%)
  between operations  13.9 us (6%)
  matrix products  8.32 us (3%)
  local copies, waits for them, and re-layouts  4.6 us (2%)
  other arithmetic  3.81 us (2%)
    psum x1, waiting for transfers between devices, per_device(): lax.psum(local_term.reshape(total_cols, slot_width), ('pole', 'row', 'col'))  133 us
    psum x1, waiting for transfers between devices, per_device(): whole = lax.psum(weighted, 'pole')  45 us
    all_gather x1, waiting for transfers between devices, per_device(): column_rows = lax.all_gather(masked, 'row', axis=1, tiled=True)  27.7 us
  transfers between devices with their start and end apart: 4, of which 4 were waited for; matrix products, arithmetic and copies ran while one was open for 3% of the time, Pallas kernels for 0%

commit v1 on v0

v1 whole, which is shorter than its diff:
```python
import jax
import jax.numpy as jnp
from jax import lax
from jax.sharding import PartitionSpec as P


def is_power_of_two(count):
    return count & (count - 1) == 0


def swap_sum(value, axis, bits):
    count = lax.axis_size(axis)
    for bit in bits:
        value = value + lax.ppermute(value, axis, [(i, i ^ bit) for i in range(count)])
    return value


def bits_of(count):
    return [1 << k for k in range(count.bit_length() - 1)]


def sum_over(value, axis):
    count = lax.axis_size(axis)
    if not is_power_of_two(count):
        return lax.psum(value, axis)
    bits = bits_of(count)
    half = value.shape[0] // 2
    first = swap_sum(value[:half], axis, bits)
    second = swap_sum(value[half:], axis, bits[::-1])
    return jnp.concatenate([first, second], axis=0)


def scatter_sum(value, axis):
    count = lax.axis_size(axis)
    if not is_power_of_two(count):
        return lax.psum_scatter(value, axis, scatter_dimension=0, tiled=True)
    index = lax.axis_index(axis)
    for bit in bits_of(count)[::-1]:
        half = value.shape[0] // 2
        upper = (index & bit) != 0
        keep = jnp.where(upper, value[half:], value[:half])
        send = jnp.where(upper, value[:half], value[half:])
        value = keep + lax.ppermute(send, axis, [(i, i ^ bit) for i in range(count)])
    return value


def gather_pieces(value, axis):
    count = lax.axis_size(axis)
    if not is_power_of_two(count):
        return lax.all_gather(value, axis, axis=0, tiled=True)
    index = lax.axis_index(axis)
    for bit in bits_of(count):
        other = lax.ppermute(value, axis, [(i, i ^ bit) for i in range(count)])
        upper = (index & bit) != 0
        value = jnp.concatenate(
            [jnp.where(upper, other, value), jnp.where(upper, value, other)], axis=0
        )
    return value


def gather_blocks(value, axis):
    count = lax.axis_size(axis)
    index = lax.axis_index(axis)
    pieces = [(index, value)]
    near = max(1, count // 2)
    up, down = {}, {}
    for distance in range(1, count):
        ahead = [(i, i + distance) for i in range(count - distance)]
        back = [(i + distance, i) for i in range(count - distance)]
        if distance <= near:
            up[distance] = lax.ppermute(value, axis, ahead)
            down[distance] = lax.ppermute(value, axis, back)
        else:
            hop = distance - near
            ahead = [(i + near, i + distance) for i in range(count - distance)]
            back = [(i + hop, i) for i in range(count - distance)]
            up[distance] = lax.ppermute(up[near], axis, ahead)
            down[distance] = lax.ppermute(down[near], axis, back)
        pieces.append((index - distance, up[distance]))
        pieces.append((index + distance, down[distance]))
    return pieces


def contract(left, right):
    return jnp.einsum("jk,ij->ki", left, right, preferred_element_type=jnp.float32)


def pair_product(left, right):
    return jnp.einsum("ika,kbi->kab", left, right, preferred_element_type=jnp.float32)


def per_device(found_inverse, l_panel, block_pattern, sup_widths, diag_inverse, pole_weights):
    slot_width = diag_inverse.shape[-1]
    total_cols = l_panel.shape[-1]
    supernodes = total_cols // slot_width
    row_count = lax.axis_size("row")
    lead_flag = ((lax.axis_index("row") == 0) & (lax.axis_index("col") == 0)).astype(jnp.float32)
    columns = jnp.arange(total_cols, dtype=jnp.int32)
    column_ok = columns % slot_width < jnp.repeat(sup_widths, slot_width)
    block_ok = jnp.repeat(block_pattern[0], slot_width) == 1
    masked = jnp.where(
        (column_ok & block_ok)[None, None, :], l_panel[0], jnp.zeros((), jnp.bfloat16)
    )
    own_rows = lax.all_gather(masked, "col", axis=1, tiled=True)
    local_rows = found_inverse.shape[2]
    inverse = found_inverse[0].reshape(2, local_rows, row_count, slot_width)
    part_real = jnp.zeros((total_cols, local_rows), jnp.float32)
    part_imag = jnp.zeros((total_cols, local_rows), jnp.float32)
    for owner, block in gather_blocks(masked, "row"):
        facing = lax.dynamic_index_in_dim(
            inverse, jnp.clip(owner, 0, row_count - 1), axis=2, keepdims=False
        )
        part_real += contract(block[1], facing[1]) - contract(block[0], facing[0])
        part_imag -= contract(block[1], facing[0]) + contract(block[0], facing[1])
    w_real = pole_weights[0, 0]
    w_imag = pole_weights[0, 1]
    weighted = w_real * part_real - w_imag * part_imag
    turned = w_real * part_imag + w_imag * part_real
    density = sum_over(scatter_sum(weighted, "col"), "pole")

    lifted = own_rows.reshape(2, local_rows, supernodes, slot_width)

    def fine_product(left, right):
        right = right.reshape(supernodes, slot_width, local_rows)
        high = lax.reduce_precision(right, 8, 7)
        low = (right - high).astype(jnp.bfloat16)
        return pair_product(left, high.astype(jnp.bfloat16)) + pair_product(left, low)

    update = fine_product(lifted[0], weighted) - fine_product(lifted[1], turned)
    d_real = diag_inverse[0, 0].astype(jnp.float32)
    d_imag = diag_inverse[0, 1].astype(jnp.float32)
    local_term = lead_flag * (w_real * d_real - w_imag * d_imag) - update.reshape(
        total_cols, slot_width
    )
    diagonal = scatter_sum(local_term, "col")
    diagonal = sum_over(diagonal, "pole")
    diagonal = sum_over(diagonal, "row")
    diagonal = gather_pieces(diagonal, "col")
    return (density, diagonal)


def solution(mesh):
    in_specs = (
        P("pole", None, "row", None, "col", None),
        P("pole", None, ("row", "col"), None),
        P(("row", "col"), None),
        P(),
        P("pole", None, None, None),
        P("pole", None),
    )
    out_specs = (P("col", "row"), P())
    return jax.shard_map(
        per_device, mesh=mesh, in_specs=in_specs, out_specs=out_specs, check_vma=False
    )
```

time: 240 us -> 73 us (0.30)
  waiting for transfers between devices: 207 us -> 12.3 us
  starting transfers between devices: 0.16 us -> 31.2 us
  between operations: 13.9 us -> 1.21 us
  local copies, waits for them, and re-layouts: 4.6 us -> 11.5 us
    psum x2 -> x0, waiting for transfers between devices: 178 us -> none  [the longest x1 133 us: per_device(): lax.psum(local_term.reshape(total_cols, slot_width), ('pole', 'row', 'col'))]
    ppermute x0 -> x21, starting transfers between devices: none -> 31.2 us  [the longest x12 15.1 us: swap_sum(): lax.ppermute(value, axis, [(i, i ^ bit) for i in range(count)])]
    all_gather x1 -> x0, waiting for transfers between devices: 27.7 us -> none  [per_device(): column_rows = lax.all_gather(masked, 'row', axis=1, tiled=True)]
    ppermute x0 -> x21, waiting for transfers between devices: none -> 12.3 us  [the longest x12 11 us: swap_sum(): lax.ppermute(value, axis, [(i, i ^ bit) for i in range(count)])]
    unnamed x16 -> x32, local copies, waits for them, and re-layouts: 3.45 us -> 7.15 us
    dot_general x4 -> x28, matrix products: 4.64 us -> 8.31 us  [contract(): jnp.einsum('jk,ij->ki', left, right, preferred_element_type=jnp.float32)]
    slice x4 -> x6, local copies, waits for them, and re-layouts: 0.48 us -> 3.79 us  [the longest x1 2.76 us: per_device(): part_real += contract(block[1], facing[1]) - contract(block[0], facing[0])]
    dot_general x4, matrix products: 3.68 us -> 0.92 us  [pair_product(): jnp.einsum('ika,kbi->kab', left, right, preferred_element_type=jnp.float32)]
  transfers between devices with their start and end apart: 4 -> 21, of which waited for: 4 -> 10; matrix products, arithmetic and copies ran while one was open for 3% -> 16% of each run, Pallas kernels for 0% -> 0%
where the time goes in v1:
time: 73 us; the launch traced here: 72.5 us
  starting transfers between devices  31.2 us (43%)
  waiting for transfers between devices  12.3 us (17%)
  local copies, waits for them, and re-layouts  11.5 us (16%)
  matrix products  9.23 us (13%)
  other arithmetic  4.76 us (7%)
  blocking collectives  2.18 us (3%)
  between operations  1.21 us (2%)
    ppermute x12, starting transfers between devices, swap_sum(): lax.ppermute(value, axis, [(i, i ^ bit) for i in range(count)])  15.1 us
    ppermute x2, starting transfers between devices, gather_blocks(): up[distance] = lax.ppermute(value, axis, ahead)  11 us
    ppermute x12, waiting for transfers between devices, swap_sum(): lax.ppermute(value, axis, [(i, i ^ bit) for i in range(count)])  11 us
    dot_general x28, matrix products, contract(): jnp.einsum('jk,ij->ki', left, right, preferred_element_type=jnp.float32)  8.31 us
    unnamed x32, local copies, waits for them, and re-layouts  7.15 us
    slice x1, local copies, waits for them, and re-layouts, per_device(): part_real += contract(block[1], facing[1]) - contract(block[0], facing[0])  2.76 us
    ppermute x2, starting transfers between devices, gather_blocks(): down[distance] = lax.ppermute(value, axis, back)  2.72 us
    all_gather x1, blocking collectives, per_device(): own_rows = lax.all_gather(masked, 'col', axis=1, tiled=True)  2.18 us
  transfers between devices with their start and end apart: 21, of which 10 were waited for; matrix products, arithmetic and copies ran while one was open for 16% of the time, Pallas kernels for 0%

profile of v1, /device:TPU:0, one launch (start us, length us, event | category | flops | bytes accessed | tf_op | source)
XLA Modules:
  0.0 72.5 jit_solution(12299386816213199065)
XLA Ops:
  0.6 0.7 compare_bitcast_fusion
  1.4 1.0 %bitcast_select_fusion = bf16[2,128,512]{2,1,0:T(8,128)(2,1)S(1)} fusion(bf16[1,2,128,512]{3,2,1,0:T(8,128)(2,1)} %param.7, pred[512]{0:T(512)(128)(4,1)S(1)} %fusion.38), kind=kLoop, calls=%fused_computation.43 | loop fusion | flops 131072 | bytes 524800 | tf_op jit(solution)/shard_map/jit(_where)/select_n | solution.py:101
  2.4 1.4 %collective-permute-start.3 = (bf16[2,128,512]{2,1,0:T(8,128)(2,1)S(1)}, bf16[2,128,512]{2,1,0:T(8,128)(2,1)S(1)}, u32[]{:S(2)}, u32[]{:S(2)}) collective-permute-start(bf16[2,128,512]{2,1,0:T(8,128)(2,1)S(1)} %bitcast_select_fusion), channel_id=1, source_target_pairs={{4,0},{6,2},{5,1},{7,3},{12,8},{14,10},{13,9},{15,11},{20,16},{22,... | collective-permute-start | bytes 786440 | tf_op jit(solution)/shard_map/ppermute | solution.py:72
  3.8 6.0 %collective-permute-start.2 = (bf16[2,128,512]{2,1,0:T(8,128)(2,1)S(1)}, bf16[2,128,512]{2,1,0:T(8,128)(2,1)S(1)}, u32[]{:S(2)}, u32[]{:S(2)}) collective-permute-start(bf16[2,128,512]{2,1,0:T(8,128)(2,1)S(1)} %bitcast_select_fusion), channel_id=1, source_target_pairs={{0,4},{2,6},{1,5},{3,7},{8,12},{10,14},{9,13},{11,15},{16,20},{18,... | collective-permute-start | bytes 786440 | tf_op jit(solution)/shard_map/ppermute | solution.py:71
  9.8 1.3 %collective-permute-start.1 = (bf16[2,128,512]{2,1,0:T(8,128)(2,1)S(1)}, bf16[2,128,512]{2,1,0:T(8,128)(2,1)S(1)}, u32[]{:S(2)}, u32[]{:S(2)}) collective-permute-start(bf16[2,128,512]{2,1,0:T(8,128)(2,1)S(1)} %bitcast_select_fusion), channel_id=1, source_target_pairs={{2,0},{4,2},{6,4},{3,1},{5,3},{7,5},{10,8},{12,10},{14,12},{11,9},... | collective-permute-start | bytes 786440 | tf_op jit(solution)/shard_map/ppermute | solution.py:72
  11.1 5.1 %collective-permute-start = (bf16[2,128,512]{2,1,0:T(8,128)(2,1)S(1)}, bf16[2,128,512]{2,1,0:T(8,128)(2,1)S(1)}, u32[]{:S(2)}, u32[]{:S(2)}) collective-permute-start(bf16[2,128,512]{2,1,0:T(8,128)(2,1)S(1)} %bitcast_select_fusion), channel_id=1, source_target_pairs={{0,2},{2,4},{4,6},{1,3},{3,5},{5,7},{8,10},{10,12},{12,14},{9,11},... | collective-permute-start | bytes 786440 | tf_op jit(solution)/shard_map/ppermute | solution.py:71
  16.2 2.2 %all_gather.3 = bf16[2,256,512]{2,1,0:T(8,128)(2,1)S(1)} all-gather(bf16[2,128,512]{2,1,0:T(8,128)(2,1)S(1)} %bitcast_select_fusion), channel_id=1, replica_groups=mesh['pole'=4,'row'=4,'col'=2] {'col'}, dimensions={1}, use_global_device_ids=true | all-gather | bytes 786432 | tf_op jit(solution)/shard_map/all_gather | solution.py:104
  18.4 2.8 %constant_dynamic-slice_fusion.8 = (bf16[1,1,256,1,1,128]{5,3,4,2,1,0:T(2,128)(2,1)}, bf16[1,1,256,1,1,128]{5,3,4,2,1,0:T(2,128)(2,1)}, bf16[1,1,256,1,1,128]{5,...) fusion(bf16[1,2,256,4,1,128]{5,3,4,2,1,0:T(4,128)(2,1)S(1)} %co, ...), kind=kLoop, calls=%fused_computation.101 | loop fusion | bytes 1835040 | tf_op jit(solution)/shard_map/slice | solution.py:113
  21.6 0.3 convolution_subtract_fusion.6
  21.9 0.2 fusion.6
  22.1 0.7 %fusion.39 = (bf16[1,256,512]{2,1,0:T(8,128)(2,1)}, bf16[1,256,512]{2,1,0:T(8,128)(2,1)S(1)}) fusion(bf16[2,256,512]{2,1,0:T(8,128)(2,1)S(1)} %all_gather.3), kind=kLoop, calls=%fused_computation.119 | loop fusion | bytes 1048576 | tf_op jit(solution)/shard_map/slice | solution.py:129
  22.9 0.6 fusion.42
  23.6 0.8 %copy-done.1 = bf16[1,256,512]{2,1,0:T(8,128)(2,1)S(1)} copy-done((bf16[1,256,512]{2,1,0:T(8,128)(2,1)S(1)}, bf16[1,256,512]{2,1,0:T(8,128)(2,1)}, u32[]{:S(2)}) %copy-start.1) | copy-done | bytes 262168
  24.6 1.3 %collective-permute-start.5 = (bf16[2,128,512]{2,1,0:T(8,128)(2,1)S(1)}, bf16[2,128,512]{2,1,0:T(8,128)(2,1)S(1)}, u32[]{:S(2)}, u32[]{:S(2)}) collective-permute-start(bf16[2,128,512]{2,1,0:T(8,128)(2,1)S(1)} %collective-permute-done.3), channel_id=1, source_target_pairs={{2,0},{3,1},{10,8},{11,9},{18,16},{19,17},{26,24},{27,25}} | collective-permute-start | bytes 786440 | tf_op jit(solution)/shard_map/ppermute | solution.py:78
  26.2 0.7 collective-permute-start.4
  26.9 0.2 fusion.27
  27.1 0.6 copy-done.12
  28.0 0.2 convolution_subtract_fusion.3
  28.3 0.3 convolution_add_fusion.3
  28.5 0.6 copy-done.10
  29.2 0.2 convolution_subtract_fusion.2
  29.4 0.3 fusion.28
  29.7 0.3 convolution_add_fusion.2
  30.0 0.6 copy-done.7
  30.8 0.7 copy-done.8
  31.5 0.2 convolution_subtract_fusion.4
  31.7 0.3 fusion.24
  32.0 0.2 convolution_add_fusion.4
  32.3 0.6 copy-done.5
  32.9 0.2 fusion.23
  33.2 0.7 copy-done.6
  34.1 0.3 fusion.3
  34.4 0.3 fusion.10
  34.8 0.4 copy-done.3
  35.3 0.2 fusion.32
  35.5 0.7 copy-done.4
  36.2 0.2 convolution_add_fusion
  36.7 0.3 convolution_subtract_fusion
  37.2 0.6 copy-done.2
  38.1 0.3 fusion.12
  38.4 1.6 %multiply_add_fusion = (f32[512,256]{1,0:T(8,128)S(1)}, f32[512,256]{1,0:T(8,128)S(1)}) fusion(f32[512,256]{1,0:T(8,128)S(1)} %fusion.12, f32[]{:T(128)} %bitcast.33, f32[]{:T(128)} %bitcast, f32[512,256]{1,0:T(8,128)S(1)} %convolution_subtract_fusion, f32[512,256]{1,0:T(8,128)S(1)} %fusion.3, f32[512,256]{1,0:T(8,128)S(1)} %fusion.31, ...), kind=kOutput, calls=%fused_computation.36 | convolution fusion | flops 34734080 | bytes 3407880 | tf_op jit(solution)/shard_map/jk,ij->ki/dot_general | solution.py:85
  40.9 0.7 copy-done.13
  41.6 1.3 %bitcast_subtract_fusion = f32[512,128]{1,0:T(8,128)S(1)} fusion(f32[4,128,128]{2,1,0:T(8,128)S(1)} %fusion.13, bf16[1,2,512,128]{3,2,1,0:T(8,128)(2,1)S(1)} %copy-done.13, f32[]{:T(128)} %bitcast.33, f32[]{:T(128)} %bitcast, f32[]{:T(128)S(6)} %convert_element_type.23), kind=kLoop, calls=%fused_computation.42 | loop fusion | flops 458752 | bytes 786444 | tf_op jit(solution)/shard_map/sub | solution.py:132
  43.2 1.2 %collective-permute-done.11 = f32[256,128]{1,0:T(8,128)S(1)} collective-permute-done((f32[256,128]{1,0:T(8,128)S(1)}, f32[256,128]{1,0:T(8,128)S(1)}, u32[]{:S(2)}, u32[]{:S(2)}) %collective-permute-start.11) | collective-permute-done | bytes 131104 | tf_op jit(solution)/shard_map/ppermute | solution.py:43
  44.4 2.0 %collective-permute-start.12 = (f32[128,128]{1,0:T(8,128)S(1)}, f32[128,128]{1,0:T(8,128)S(1)}, u32[]{:S(2)}, u32[]{:S(2)}) collective-permute-start(f32[128,128]{1,0:T(8,128)S(1)} %get-tuple-element.28), channel_id=1, source_target_pairs={{0,8},{8,0},{16,24},{24,16},{1,9},{9,1},{17,25},{25,17},{2,10},{10... | collective-permute-start | bytes 196616 | tf_op jit(solution)/shard_map/ppermute | solution.py:14
  46.4 1.5 %collective-permute-start.16 = (f32[128,128]{1,0:T(8,128)S(1)}, f32[128,128]{1,0:T(8,128)S(1)}, u32[]{:S(2)}, u32[]{:S(2)}) collective-permute-start(f32[128,128]{1,0:T(8,128)S(1)} %get-tuple-element.29), channel_id=1, source_target_pairs={{0,16},{8,24},{16,0},{24,8},{1,17},{9,25},{17,1},{25,9},{2,18},{10... | collective-permute-start | bytes 196616 | tf_op jit(solution)/shard_map/ppermute | solution.py:14
  48.0 0.8 %collective-permute-done.12 = f32[128,128]{1,0:T(8,128)S(1)} collective-permute-done((f32[128,128]{1,0:T(8,128)S(1)}, f32[128,128]{1,0:T(8,128)S(1)}, u32[]{:S(2)}, u32[]{:S(2)}) %collective-permute-start.12) | collective-permute-done | bytes 65568 | tf_op jit(solution)/shard_map/ppermute | solution.py:14
  48.8 1.9 %collective-permute-done.16 = f32[128,128]{1,0:T(8,128)S(1)} collective-permute-done((f32[128,128]{1,0:T(8,128)S(1)}, f32[128,128]{1,0:T(8,128)S(1)}, u32[]{:S(2)}, u32[]{:S(2)}) %collective-permute-start.16) | collective-permute-done | bytes 65568 | tf_op jit(solution)/shard_map/ppermute | solution.py:14
  50.7 1.6 %collective-permute-start.13 = (f32[128,128]{1,0:T(8,128)S(1)}, f32[128,128]{1,0:T(8,128)S(1)}, u32[]{:S(2)}, u32[]{:S(2)}) collective-permute-start(f32[128,128]{1,0:T(8,128)S(1)} %get-tuple-element.26), channel_id=1, source_target_pairs={{0,16},{8,24},{16,0},{24,8},{1,17},{9,25},{17,1},{25,9},{2,18},{10... | collective-permute-start | bytes 196616 | tf_op jit(solution)/shard_map/ppermute | solution.py:14
  52.3 0.5 collective-permute-start.17
  52.9 1.6 %collective-permute-start.7 = (f32[128,256]{1,0:T(8,128)S(1)}, f32[128,256]{1,0:T(8,128)S(1)}, u32[]{:S(2)}, u32[]{:S(2)}) collective-permute-start(f32[128,256]{1,0:T(8,128)S(1)} %get-tuple-element.24), channel_id=1, source_target_pairs={{0,8},{8,0},{16,24},{24,16},{1,9},{9,1},{17,25},{25,17},{2,10},{10... | collective-permute-start | bytes 393224 | tf_op jit(solution)/shard_map/ppermute | solution.py:14
  54.5 0.5 collective-permute-start.9
  55.2 2.7 %collective-permute-start.14 = (f32[128,128]{1,0:T(8,128)S(1)}, f32[128,128]{1,0:T(8,128)S(1)}, u32[]{:S(2)}, u32[]{:S(2)}) collective-permute-start(f32[128,128]{1,0:T(8,128)S(1)} %add.147), channel_id=1, source_target_pairs={{0,2},{2,0},{4,6},{6,4},{1,3},{3,1},{5,7},{7,5},{8,10},{10,8},{12,... | collective-permute-start | bytes 196616 | tf_op jit(solution)/shard_map/ppermute | solution.py:14
  58.0 2.1 %collective-permute-done.14 = f32[128,128]{1,0:T(8,128)S(1)} collective-permute-done((f32[128,128]{1,0:T(8,128)S(1)}, f32[128,128]{1,0:T(8,128)S(1)}, u32[]{:S(2)}, u32[]{:S(2)}) %collective-permute-start.14) | collective-permute-done | bytes 65568 | tf_op jit(solution)/shard_map/ppermute | solution.py:14
  60.2 1.3 %collective-permute-start.15 = (f32[128,128]{1,0:T(8,128)S(1)}, f32[128,128]{1,0:T(8,128)S(1)}, u32[]{:S(2)}, u32[]{:S(2)}) collective-permute-start(f32[128,128]{1,0:T(8,128)S(1)} %add.148), channel_id=1, source_target_pairs={{0,4},{2,6},{4,0},{6,2},{1,5},{3,7},{5,1},{7,3},{8,12},{10,14},{12... | collective-permute-start | bytes 196616 | tf_op jit(solution)/shard_map/ppermute | solution.py:14
  61.5 1.8 %collective-permute-done.18 = f32[128,128]{1,0:T(8,128)S(1)} collective-permute-done((f32[128,128]{1,0:T(8,128)S(1)}, f32[128,128]{1,0:T(8,128)S(1)}, u32[]{:S(2)}, u32[]{:S(2)}) %collective-permute-start.18) | collective-permute-done | bytes 65568 | tf_op jit(solution)/shard_map/ppermute | solution.py:14
  63.3 1.2 %collective-permute-start.19 = (f32[128,128]{1,0:T(8,128)S(1)}, f32[128,128]{1,0:T(8,128)S(1)}, u32[]{:S(2)}, u32[]{:S(2)}) collective-permute-start(f32[128,128]{1,0:T(8,128)S(1)} %add.152), channel_id=1, source_target_pairs={{0,2},{2,0},{4,6},{6,4},{1,3},{3,1},{5,7},{7,5},{8,10},{10,8},{12,... | collective-permute-start | bytes 196616 | tf_op jit(solution)/shard_map/ppermute | solution.py:14
  64.6 1.4 %collective-permute-start.8 = (f32[128,256]{1,0:T(8,128)S(1)}, f32[128,256]{1,0:T(8,128)S(1)}, u32[]{:S(2)}, u32[]{:S(2)}) collective-permute-start(f32[128,256]{1,0:T(8,128)S(1)} %get-tuple-element.22), channel_id=1, source_target_pairs={{0,16},{8,24},{16,0},{24,8},{1,17},{9,25},{17,1},{25,9},{2,18},{10... | collective-permute-start | bytes 393224 | tf_op jit(solution)/shard_map/ppermute | solution.py:14
  66.0 0.6 collective-permute-start.10
  66.6 1.0 %collective-permute-done.19 = f32[128,128]{1,0:T(8,128)S(1)} collective-permute-done((f32[128,128]{1,0:T(8,128)S(1)}, f32[128,128]{1,0:T(8,128)S(1)}, u32[]{:S(2)}, u32[]{:S(2)}) %collective-permute-start.19) | collective-permute-done | bytes 65568 | tf_op jit(solution)/shard_map/ppermute | solution.py:14
  67.7 1.9 %collective-permute-done.8 = f32[128,256]{1,0:T(8,128)S(1)} collective-permute-done((f32[128,256]{1,0:T(8,128)S(1)}, f32[128,256]{1,0:T(8,128)S(1)}, u32[]{:S(2)}, u32[]{:S(2)}) %collective-permute-start.8) | collective-permute-done | bytes 131104 | tf_op jit(solution)/shard_map/ppermute | solution.py:14
  69.6 1.3 %collective-permute-done.10 = f32[128,256]{1,0:T(8,128)S(1)} collective-permute-done((f32[128,256]{1,0:T(8,128)S(1)}, f32[128,256]{1,0:T(8,128)S(1)}, u32[]{:S(2)}, u32[]{:S(2)}) %collective-permute-start.10) | collective-permute-done | bytes 131104 | tf_op jit(solution)/shard_map/ppermute | solution.py:14
  71.0 0.7 pad_maximum_fusion
  71.7 0.7 pad_maximum_fusion.1
  (72 shorter events, 4.6 us)
Async XLA Ops:
  0.6 0.7 copy-start.15
  2.4 16.0 %copy-start = (bf16[1,2,256,4,1,128]{5,3,4,2,1,0:T(4,128)(2,1)S(1)}, bf16[1,2,256,4,1,128]{5,3,4,2,1,0:T(4,128)(2,1)}, u32[]{:S(2)}) copy-start(bf16[1,2,256,4,1,128]{5,3,4,2,1,0:T(4,128)(2,1)} %param.6) | copy-start | bytes 1572868
  2.4 22.2 %collective-permute-start.3 = (bf16[2,128,512]{2,1,0:T(8,128)(2,1)S(1)}, bf16[2,128,512]{2,1,0:T(8,128)(2,1)S(1)}, u32[]{:S(2)}, u32[]{:S(2)}) collective-permute-start(bf16[2,128,512]{2,1,0:T(8,128)(2,1)S(1)} %bitcast_select_fusion), channel_id=1, source_target_pairs={{4,0},{6,2},{5,1},{7,3},{12,8},{14,10},{13,9},{15,11},{20,16},{22,... | collective-permute-start | bytes 786440 | tf_op jit(solution)/shard_map/ppermute | solution.py:72
  3.8 22.3 %collective-permute-start.2 = (bf16[2,128,512]{2,1,0:T(8,128)(2,1)S(1)}, bf16[2,128,512]{2,1,0:T(8,128)(2,1)S(1)}, u32[]{:S(2)}, u32[]{:S(2)}) collective-permute-start(bf16[2,128,512]{2,1,0:T(8,128)(2,1)S(1)} %bitcast_select_fusion), channel_id=1, source_target_pairs={{0,4},{2,6},{1,5},{3,7},{8,12},{10,14},{9,13},{11,15},{16,20},{18,... | collective-permute-start | bytes 786440 | tf_op jit(solution)/shard_map/ppermute | solution.py:71
  9.8 20.2 %collective-permute-start.1 = (bf16[2,128,512]{2,1,0:T(8,128)(2,1)S(1)}, bf16[2,128,512]{2,1,0:T(8,128)(2,1)S(1)}, u32[]{:S(2)}, u32[]{:S(2)}) collective-permute-start(bf16[2,128,512]{2,1,0:T(8,128)(2,1)S(1)} %bitcast_select_fusion), channel_id=1, source_target_pairs={{2,0},{4,2},{6,4},{3,1},{5,3},{7,5},{10,8},{12,10},{14,12},{11,9},... | collective-permute-start | bytes 786440 | tf_op jit(solution)/shard_map/ppermute | solution.py:72
  11.1 21.2 %collective-permute-start = (bf16[2,128,512]{2,1,0:T(8,128)(2,1)S(1)}, bf16[2,128,512]{2,1,0:T(8,128)(2,1)S(1)}, u32[]{:S(2)}, u32[]{:S(2)}) collective-permute-start(bf16[2,128,512]{2,1,0:T(8,128)(2,1)S(1)} %bitcast_select_fusion), channel_id=1, source_target_pairs={{0,2},{2,4},{4,6},{1,3},{3,5},{5,7},{8,10},{10,12},{12,14},{9,11},... | collective-permute-start | bytes 786440 | tf_op jit(solution)/shard_map/ppermute | solution.py:71
  22.1 0.8 %copy-start.14 = (f32[1,2]{1,0:T(1,128)S(1)}, f32[1,2]{1,0:T(1,128)}, u32[]{:S(2)}) copy-start(f32[1,2]{1,0:T(1,128)} %param.11) | copy-start | bytes 28
  23.5 1.0 %copy-start.1 = (bf16[1,256,512]{2,1,0:T(8,128)(2,1)S(1)}, bf16[1,256,512]{2,1,0:T(8,128)(2,1)}, u32[]{:S(2)}) copy-start(bf16[1,256,512]{2,1,0:T(8,128)(2,1)} %get-tuple-element.4) | copy-start | bytes 786436
  24.4 1.5 %copy-start.9 = (bf16[1,1,256,1,1,128]{5,3,4,2,1,0:T(2,128)(2,1)S(1)}, bf16[1,1,256,1,1,128]{5,3,4,2,1,0:T(2,128)(2,1)}, u32[]{:S(2)}) copy-start(bf16[1,1,256,1,1,128]{5,3,4,2,1,0:T(2,128)(2,1)} %get-tuple-element.14) | copy-start | bytes 196612
  24.6 10.2 %collective-permute-start.5 = (bf16[2,128,512]{2,1,0:T(8,128)(2,1)S(1)}, bf16[2,128,512]{2,1,0:T(8,128)(2,1)S(1)}, u32[]{:S(2)}, u32[]{:S(2)}) collective-permute-start(bf16[2,128,512]{2,1,0:T(8,128)(2,1)S(1)} %collective-permute-done.3), channel_id=1, source_target_pairs={{2,0},{3,1},{10,8},{11,9},{18,16},{19,17},{26,24},{27,25}} | collective-permute-start | bytes 786440 | tf_op jit(solution)/shard_map/ppermute | solution.py:78
  25.9 1.0 %copy-start.11 = (bf16[1,1,256,1,1,128]{5,3,4,2,1,0:T(2,128)(2,1)S(1)}, bf16[1,1,256,1,1,128]{5,3,4,2,1,0:T(2,128)(2,1)}, u32[]{:S(2)}) copy-start(bf16[1,1,256,1,1,128]{5,3,4,2,1,0:T(2,128)(2,1)} %get-tuple-element.15) | copy-start | bytes 196612
  26.2 10.8 %collective-permute-start.4 = (bf16[2,128,512]{2,1,0:T(8,128)(2,1)S(1)}, bf16[2,128,512]{2,1,0:T(8,128)(2,1)S(1)}, u32[]{:S(2)}, u32[]{:S(2)}) collective-permute-start(bf16[2,128,512]{2,1,0:T(8,128)(2,1)S(1)} %collective-permute-done.2), channel_id=1, source_target_pairs={{4,6},{5,7},{12,14},{13,15},{20,22},{21,23},{28,30},{29,31}} | collective-permute-start | bytes 786440 | tf_op jit(solution)/shard_map/ppermute | solution.py:77
  26.8 0.9 %copy-start.12 = (bf16[1,1,256,1,1,128]{5,3,4,2,1,0:T(2,128)(2,1)S(1)}, bf16[1,1,256,1,1,128]{5,3,4,2,1,0:T(2,128)(2,1)}, u32[]{:S(2)}) copy-start(bf16[1,1,256,1,1,128]{5,3,4,2,1,0:T(2,128)(2,1)} %get-tuple-element.10) | copy-start | bytes 196612
  28.3 0.9 %copy-start.10 = (bf16[1,1,256,1,1,128]{5,3,4,2,1,0:T(2,128)(2,1)S(1)}, bf16[1,1,256,1,1,128]{5,3,4,2,1,0:T(2,128)(2,1)}, u32[]{:S(2)}) copy-start(bf16[1,1,256,1,1,128]{5,3,4,2,1,0:T(2,128)(2,1)} %get-tuple-element.9) | copy-start | bytes 196612
  29.7 0.9 %copy-start.7 = (bf16[1,1,256,1,1,128]{5,3,4,2,1,0:T(2,128)(2,1)S(1)}, bf16[1,1,256,1,1,128]{5,3,4,2,1,0:T(2,128)(2,1)}, u32[]{:S(2)}) copy-start(bf16[1,1,256,1,1,128]{5,3,4,2,1,0:T(2,128)(2,1)} %get-tuple-element.16) | copy-start | bytes 196612
  30.6 0.9 %copy-start.8 = (bf16[1,1,256,1,1,128]{5,3,4,2,1,0:T(2,128)(2,1)S(1)}, bf16[1,1,256,1,1,128]{5,3,4,2,1,0:T(2,128)(2,1)}, u32[]{:S(2)}) copy-start(bf16[1,1,256,1,1,128]{5,3,4,2,1,0:T(2,128)(2,1)} %get-tuple-element.11) | copy-start | bytes 196612
  32.0 0.9 %copy-start.5 = (bf16[1,1,256,1,1,128]{5,3,4,2,1,0:T(2,128)(2,1)S(1)}, bf16[1,1,256,1,1,128]{5,3,4,2,1,0:T(2,128)(2,1)}, u32[]{:S(2)}) copy-start(bf16[1,1,256,1,1,128]{5,3,4,2,1,0:T(2,128)(2,1)} %get-tuple-element.17) | copy-start | bytes 196612
  32.9 0.9 %copy-start.6 = (bf16[1,1,256,1,1,128]{5,3,4,2,1,0:T(2,128)(2,1)S(1)}, bf16[1,1,256,1,1,128]{5,3,4,2,1,0:T(2,128)(2,1)}, u32[]{:S(2)}) copy-start(bf16[1,1,256,1,1,128]{5,3,4,2,1,0:T(2,128)(2,1)} %get-tuple-element.12) | copy-start | bytes 196612
  34.4 0.9 %copy-start.3 = (bf16[1,1,256,1,1,128]{5,3,4,2,1,0:T(2,128)(2,1)S(1)}, bf16[1,1,256,1,1,128]{5,3,4,2,1,0:T(2,128)(2,1)}, u32[]{:S(2)}) copy-start(bf16[1,1,256,1,1,128]{5,3,4,2,1,0:T(2,128)(2,1)} %get-tuple-element.7) | copy-start | bytes 196612
  35.3 0.9 %copy-start.4 = (bf16[1,1,256,1,1,128]{5,3,4,2,1,0:T(2,128)(2,1)S(1)}, bf16[1,1,256,1,1,128]{5,3,4,2,1,0:T(2,128)(2,1)}, u32[]{:S(2)}) copy-start(bf16[1,1,256,1,1,128]{5,3,4,2,1,0:T(2,128)(2,1)} %get-tuple-element.19) | copy-start | bytes 196612
  36.9 0.9 %copy-start.2 = (bf16[1,1,256,1,1,128]{5,3,4,2,1,0:T(2,128)(2,1)S(1)}, bf16[1,1,256,1,1,128]{5,3,4,2,1,0:T(2,128)(2,1)}, u32[]{:S(2)}) copy-start(bf16[1,1,256,1,1,128]{5,3,4,2,1,0:T(2,128)(2,1)} %get-tuple-element.6) | copy-start | bytes 196612
  40.7 1.0 %copy-start.13 = (bf16[1,2,512,128]{3,2,1,0:T(8,128)(2,1)S(1)}, bf16[1,2,512,128]{3,2,1,0:T(8,128)(2,1)}, u32[]{:S(2)}) copy-start(bf16[1,2,512,128]{3,2,1,0:T(8,128)(2,1)} %param.10) | copy-start | bytes 786436
  42.9 1.4 %collective-permute-start.11 = (f32[256,128]{1,0:T(8,128)S(1)}, f32[256,128]{1,0:T(8,128)S(1)}, u32[]{:S(2)}, u32[]{:S(2)}) collective-permute-start(f32[256,128]{1,0:T(8,128)S(1)} %slice_select_fusion.1), channel_id=1, source_target_pairs={{0,1},{1,0},{2,3},{3,2},{4,5},{5,4},{6,7},{7,6},{8,9},{9,8},{10,11... | collective-permute-start | bytes 393224 | tf_op jit(solution)/shard_map/ppermute | solution.py:43
  44.4 4.4 %collective-permute-start.12 = (f32[128,128]{1,0:T(8,128)S(1)}, f32[128,128]{1,0:T(8,128)S(1)}, u32[]{:S(2)}, u32[]{:S(2)}) collective-permute-start(f32[128,128]{1,0:T(8,128)S(1)} %get-tuple-element.28), channel_id=1, source_target_pairs={{0,8},{8,0},{16,24},{24,16},{1,9},{9,1},{17,25},{25,17},{2,10},{10... | collective-permute-start | bytes 196616 | tf_op jit(solution)/shard_map/ppermute | solution.py:14
  46.4 4.3 %collective-permute-start.16 = (f32[128,128]{1,0:T(8,128)S(1)}, f32[128,128]{1,0:T(8,128)S(1)}, u32[]{:S(2)}, u32[]{:S(2)}) collective-permute-start(f32[128,128]{1,0:T(8,128)S(1)} %get-tuple-element.29), channel_id=1, source_target_pairs={{0,16},{8,24},{16,0},{24,8},{1,17},{9,25},{17,1},{25,9},{2,18},{10... | collective-permute-start | bytes 196616 | tf_op jit(solution)/shard_map/ppermute | solution.py:14
  48.0 4.9 %collective-permute-start.6 = (f32[256,256]{1,0:T(8,128)S(1)}, f32[256,256]{1,0:T(8,128)S(1)}, u32[]{:S(2)}, u32[]{:S(2)}) collective-permute-start(f32[256,256]{1,0:T(8,128)S(1)} %slice_select_fusion), channel_id=1, source_target_pairs={{0,1},{1,0},{2,3},{3,2},{4,5},{5,4},{6,7},{7,6},{8,9},{9,8},{10,11... | collective-permute-start | bytes 786440 | tf_op jit(solution)/shard_map/ppermute | solution.py:43
  50.7 4.5 %collective-permute-start.13 = (f32[128,128]{1,0:T(8,128)S(1)}, f32[128,128]{1,0:T(8,128)S(1)}, u32[]{:S(2)}, u32[]{:S(2)}) collective-permute-start(f32[128,128]{1,0:T(8,128)S(1)} %get-tuple-element.26), channel_id=1, source_target_pairs={{0,16},{8,24},{16,0},{24,8},{1,17},{9,25},{17,1},{25,9},{2,18},{10... | collective-permute-start | bytes 196616 | tf_op jit(solution)/shard_map/ppermute | solution.py:14
  52.3 5.6 %collective-permute-start.17 = (f32[128,128]{1,0:T(8,128)S(1)}, f32[128,128]{1,0:T(8,128)S(1)}, u32[]{:S(2)}, u32[]{:S(2)}) collective-permute-start(f32[128,128]{1,0:T(8,128)S(1)} %get-tuple-element.27), channel_id=1, source_target_pairs={{0,8},{8,0},{16,24},{24,16},{1,9},{9,1},{17,25},{25,17},{2,10},{10... | collective-permute-start | bytes 196616 | tf_op jit(solution)/shard_map/ppermute | solution.py:14
  52.9 11.6 %collective-permute-start.7 = (f32[128,256]{1,0:T(8,128)S(1)}, f32[128,256]{1,0:T(8,128)S(1)}, u32[]{:S(2)}, u32[]{:S(2)}) collective-permute-start(f32[128,256]{1,0:T(8,128)S(1)} %get-tuple-element.24), channel_id=1, source_target_pairs={{0,8},{8,0},{16,24},{24,16},{1,9},{9,1},{17,25},{25,17},{2,10},{10... | collective-permute-start | bytes 393224 | tf_op jit(solution)/shard_map/ppermute | solution.py:14
  54.5 10.1 %collective-permute-start.9 = (f32[128,256]{1,0:T(8,128)S(1)}, f32[128,256]{1,0:T(8,128)S(1)}, u32[]{:S(2)}, u32[]{:S(2)}) collective-permute-start(f32[128,256]{1,0:T(8,128)S(1)} %get-tuple-element.25), channel_id=1, source_target_pairs={{0,16},{8,24},{16,0},{24,8},{1,17},{9,25},{17,1},{25,9},{2,18},{10... | collective-permute-start | bytes 393224 | tf_op jit(solution)/shard_map/ppermute | solution.py:14
  55.2 5.0 %collective-permute-start.14 = (f32[128,128]{1,0:T(8,128)S(1)}, f32[128,128]{1,0:T(8,128)S(1)}, u32[]{:S(2)}, u32[]{:S(2)}) collective-permute-start(f32[128,128]{1,0:T(8,128)S(1)} %add.147), channel_id=1, source_target_pairs={{0,2},{2,0},{4,6},{6,4},{1,3},{3,1},{5,7},{7,5},{8,10},{10,8},{12,... | collective-permute-start | bytes 196616 | tf_op jit(solution)/shard_map/ppermute | solution.py:14
  57.9 5.3 %collective-permute-start.18 = (f32[128,128]{1,0:T(8,128)S(1)}, f32[128,128]{1,0:T(8,128)S(1)}, u32[]{:S(2)}, u32[]{:S(2)}) collective-permute-start(f32[128,128]{1,0:T(8,128)S(1)} %add.151), channel_id=1, source_target_pairs={{0,4},{2,6},{4,0},{6,2},{1,5},{3,7},{5,1},{7,3},{8,12},{10,14},{12... | collective-permute-start | bytes 196616 | tf_op jit(solution)/shard_map/ppermute | solution.py:14
  60.2 6.5 %collective-permute-start.15 = (f32[128,128]{1,0:T(8,128)S(1)}, f32[128,128]{1,0:T(8,128)S(1)}, u32[]{:S(2)}, u32[]{:S(2)}) collective-permute-start(f32[128,128]{1,0:T(8,128)S(1)} %add.148), channel_id=1, source_target_pairs={{0,4},{2,6},{4,0},{6,2},{1,5},{3,7},{5,1},{7,3},{8,12},{10,14},{12... | collective-permute-start | bytes 196616 | tf_op jit(solution)/shard_map/ppermute | solution.py:14
  63.3 4.3 %collective-permute-start.19 = (f32[128,128]{1,0:T(8,128)S(1)}, f32[128,128]{1,0:T(8,128)S(1)}, u32[]{:S(2)}, u32[]{:S(2)}) collective-permute-start(f32[128,128]{1,0:T(8,128)S(1)} %add.152), channel_id=1, source_target_pairs={{0,2},{2,0},{4,6},{6,4},{1,3},{3,1},{5,7},{7,5},{8,10},{10,8},{12,... | collective-permute-start | bytes 196616 | tf_op jit(solution)/shard_map/ppermute | solution.py:14
  64.6 5.0 %collective-permute-start.8 = (f32[128,256]{1,0:T(8,128)S(1)}, f32[128,256]{1,0:T(8,128)S(1)}, u32[]{:S(2)}, u32[]{:S(2)}) collective-permute-start(f32[128,256]{1,0:T(8,128)S(1)} %get-tuple-element.22), channel_id=1, source_target_pairs={{0,16},{8,24},{16,0},{24,8},{1,17},{9,25},{17,1},{25,9},{2,18},{10... | collective-permute-start | bytes 393224 | tf_op jit(solution)/shard_map/ppermute | solution.py:14
  66.0 5.0 %collective-permute-start.10 = (f32[128,256]{1,0:T(8,128)S(1)}, f32[128,256]{1,0:T(8,128)S(1)}, u32[]{:S(2)}, u32[]{:S(2)}) collective-permute-start(f32[128,256]{1,0:T(8,128)S(1)} %get-tuple-element.23), channel_id=1, source_target_pairs={{0,8},{8,0},{16,24},{24,16},{1,9},{9,1},{17,25},{25,17},{2,10},{10... | collective-permute-start | bytes 393224 | tf_op jit(solution)/shard_map/ppermute | solution.py:14
  67.6 4.1 %collective-permute-start.20 = (f32[256,128]{1,0:T(8,128)S(1)}, f32[256,128]{1,0:T(8,128)S(1)}, u32[]{:S(2)}, u32[]{:S(2)}) collective-permute-start(f32[256,128]{1,0:T(8,128)S(1)} %pad_maximum_fusion.2), channel_id=1, source_target_pairs={{0,1},{1,0},{2,3},{3,2},{4,5},{5,4},{6,7},{7,6},{8,9},{9,8},{10,11... | collective-permute-start | bytes 393224 | tf_op jit(solution)/shard_map/ppermute | solution.py:53

commit v2 on v0

v2 whole, which is shorter than its diff:
```python
import functools

import jax
import jax.numpy as jnp
from jax import lax
from jax.experimental import pallas as pl
from jax.experimental.pallas import tpu as pltpu
from jax.sharding import PartitionSpec as P

F32 = jnp.float32
BF16 = jnp.bfloat16
VMEM_SPEC = pl.BlockSpec(memory_space=pltpu.VMEM)
SMEM_SPEC = pl.BlockSpec(memory_space=pltpu.SMEM)


def rows_by_rows(left, right):
    return lax.dot_general(left, right, (((1,), (1,)), ((), ())), preferred_element_type=F32)


def offsets_of(widths_ref, supernodes):
    offsets = [0]
    for k in range(supernodes):
        offsets.append(offsets[-1] + widths_ref[k])
    return offsets


def pack_kernel(supernodes, slot, pattern_ref, widths_ref, panel_ref, packed_ref, wide_ref):
    copies, double_width, _ = packed_ref.shape
    packed_width = double_width // 2
    offsets = offsets_of(widths_ref, supernodes)
    place, keep = [], []
    lane = lax.broadcasted_iota(jnp.int32, (1, slot), 1)
    for k in range(supernodes):
        valid = (lane < widths_ref[k]) & (pattern_ref[0, k] == 1)
        place.append(jnp.where(valid, offsets[k] + lane, -1))
    place = jnp.concatenate(place, axis=1)
    target = lax.broadcasted_iota(jnp.int32, (packed_width, supernodes * slot), 0)
    select = jnp.where(target == place, 1.0, 0.0).astype(BF16)
    for part in range(2):
        packed = rows_by_rows(select, panel_ref[part]).astype(BF16)
        for copy in range(copies):
            packed_ref[copy, part * packed_width:(part + 1) * packed_width, :] = packed
        for k in range(supernodes):
            valid = (lane < widths_ref[k]) & (pattern_ref[0, k] == 1)
            row_id = lax.broadcasted_iota(jnp.int32, (slot, slot), 0)
            col_id = lax.broadcasted_iota(jnp.int32, (slot, slot), 1)
            chosen = jnp.where((row_id == col_id) & valid, 1.0, 0.0).astype(BF16)
            piece = panel_ref[part, :, k * slot:(k + 1) * slot]
            wide_ref[part, k * slot:(k + 1) * slot, :] = rows_by_rows(chosen, piece).astype(BF16)


def compute_kernel(
    pieces, widths_ref, weights_ref, lead_ref, inverse_ref, packed_ref, own_ref, diag_ref,
    payload_ref, straight_ref, x_ref, y_ref, diagonal_ref,
):
    pole_count, col_count = pieces
    row_count, double_width, block = packed_ref.shape
    packed_width = double_width // 2
    local_rows = inverse_ref.shape[0] // (2 * row_count)
    slot = diag_ref.shape[2]
    total_cols = diag_ref.shape[1]
    supernodes = total_cols // slot
    w_real = weights_ref[0, 0]
    w_imag = weights_ref[0, 1]
    lead = lead_ref[0].astype(F32)

    group = 256 // row_count
    span = group * row_count
    row_id = lax.broadcasted_iota(jnp.int32, (span, span), 0)
    col_id = lax.broadcasted_iota(jnp.int32, (span, span), 1)
    source = (row_id % group) * row_count + row_id // group
    order = jnp.where(col_id == source, 1.0, 0.0).astype(BF16)
    for part in range(2):
        for chunk in range(local_rows // group):
            base = (part * local_rows + chunk * group) * row_count
            mixed = inverse_ref[base:base + span, :]
            sorted_rows = jnp.dot(order, mixed, preferred_element_type=F32).astype(BF16)
            for owner in range(row_count):
                straight_ref[
                    part, chunk * group:(chunk + 1) * group, owner * block:(owner + 1) * block
                ] = sorted_rows[owner * group:(owner + 1) * group]

    panel = jnp.concatenate([packed_ref[owner] for owner in range(row_count)], axis=1)
    with_real = rows_by_rows(panel, straight_ref[0])
    with_imag = rows_by_rows(panel, straight_ref[1])
    u_real = with_imag[packed_width:] - with_real[:packed_width]
    u_imag = -(with_real[packed_width:] + with_imag[:packed_width])
    weighted = w_real * u_real - w_imag * u_imag
    turned = w_real * u_imag + w_imag * u_real
    strips = local_rows // slot
    for ref, value in ((x_ref, weighted), (y_ref, turned)):
        for s in range(strips):
            ref[s, :packed_width] = value[:, s * slot:(s + 1) * slot]
            ref[s, packed_width:] = jnp.zeros((slot, slot), F32)

    per_col = total_cols // col_count
    per_piece = per_col // pole_count
    offsets = offsets_of(widths_ref, supernodes)
    row_in_slot = lax.broadcasted_iota(jnp.int32, (slot, 1), 0)
    own = [
        jnp.concatenate([own_ref[c, part] for c in range(col_count)], axis=1) for part in range(2)
    ]
    for k in range(supernodes):
        valid = row_in_slot < widths_ref[k]
        x, y = (
            jnp.concatenate(
                [jnp.where(valid, ref[s, pl.ds(offsets[k], slot), :], 0.0) for s in range(strips)],
                axis=1,
            )
            for ref in (x_ref, y_ref)
        )
        x_high, y_high = x.astype(BF16), y.astype(BF16)
        x_low = (x - x_high.astype(F32)).astype(BF16)
        y_low = (y - y_high.astype(F32)).astype(BF16)
        l_real = own[0][k * slot:(k + 1) * slot]
        l_imag = own[1][k * slot:(k + 1) * slot]
        product = (rows_by_rows(l_real, x_high) - rows_by_rows(l_imag, y_high)) + (
            rows_by_rows(l_real, x_low) - rows_by_rows(l_imag, y_low)
        )
        d_real = diag_ref[0, k * slot:(k + 1) * slot].astype(F32)
        d_imag = diag_ref[1, k * slot:(k + 1) * slot].astype(F32)
        diagonal_ref[k * slot:(k + 1) * slot] = lead * (w_real * d_real - w_imag * d_imag) - product
        size = min(per_piece, slot)
        for begin in range(k * slot, (k + 1) * slot, size):
            c, within = divmod(begin, per_col)
            p, inside = divmod(within, per_piece)
            piece = p * col_count + c
            payload_ref[piece, inside:inside + size, :local_rows] = x[begin - k * slot:begin - k * slot + size]
    for piece in range(pole_count * col_count):
        p, c = divmod(piece, col_count)
        begin = c * per_col + p * per_piece
        payload_ref[piece, :, local_rows:] = diagonal_ref[begin:begin + per_piece]


def exchange(value, axis):
    return lax.all_to_all(value, axis, 0, 0, tiled=True)


def spread(value, axis, count):
    return exchange(jnp.broadcast_to(value[None], (count,) + value.shape), axis)


def per_device(found_inverse, l_panel, block_pattern, sup_widths, diag_inverse, pole_weights):
    slot = diag_inverse.shape[-1]
    total_cols = l_panel.shape[-1]
    supernodes = total_cols // slot
    packed_width = slot + (supernodes - 1) * (slot // 2)
    local_rows = found_inverse.shape[2]
    block = l_panel.shape[2]
    pole_count = lax.axis_size("pole")
    row_count = lax.axis_size("row")
    col_count = lax.axis_size("col")
    pieces = pole_count * col_count
    per_piece = total_cols // pieces

    packed, wide = pl.pallas_call(
        functools.partial(pack_kernel, supernodes, slot),
        in_specs=[SMEM_SPEC, SMEM_SPEC, VMEM_SPEC],
        out_specs=[VMEM_SPEC, VMEM_SPEC],
        out_shape=[
            jax.ShapeDtypeStruct((row_count, 2 * packed_width, block), BF16),
            jax.ShapeDtypeStruct((2, total_cols, block), BF16),
        ],
        name="pack",
    )(block_pattern, sup_widths, l_panel[0])

    own = lax.all_gather(wide, "col", axis=0)
    gathered = exchange(packed, "row")

    lead = ((lax.axis_index("row") == 0) & (lax.axis_index("col") == 0)).astype(jnp.int32)
    payload = pl.pallas_call(
        functools.partial(compute_kernel, (pole_count, col_count)),
        in_specs=[SMEM_SPEC] * 3 + [VMEM_SPEC] * 4,
        out_specs=VMEM_SPEC,
        out_shape=jax.ShapeDtypeStruct((pieces, per_piece, local_rows + slot), F32),
        scratch_shapes=[
            pltpu.VMEM((2, local_rows, row_count * block), BF16),
            pltpu.VMEM((local_rows // slot, packed_width + slot, slot), F32),
            pltpu.VMEM((local_rows // slot, packed_width + slot, slot), F32),
            pltpu.VMEM((total_cols, slot), F32),
        ],
        compiler_params=pltpu.CompilerParams(vmem_limit_bytes=48 * 1024 * 1024),
        name="compute",
    )(
        sup_widths, pole_weights, lead.reshape(1),
        found_inverse.reshape(2 * local_rows * row_count, block), gathered, own, diag_inverse[0],
    )

    summed = jnp.sum(exchange(payload, ("pole", "col")), axis=0)
    density = spread(summed[:, :local_rows], "pole", pole_count)
    density = density.reshape(pole_count * per_piece, local_rows)
    diagonal = jnp.sum(spread(summed[:, local_rows:], "row", row_count), axis=0)
    diagonal = spread(diagonal, ("pole", "col"), pieces)
    diagonal = diagonal.reshape(pole_count, col_count, per_piece, slot).transpose(1, 0, 2, 3)
    return (density, diagonal.reshape(total_cols, slot))


def solution(mesh):
    in_specs = (
        P("pole", None, "row", None, "col", None),
        P("pole", None, ("row", "col"), None),
        P(("row", "col"), None),
        P(),
        P("pole", None, None, None),
        P("pole", None),
    )
    out_specs = (P("col", "row"), P())
    return jax.shard_map(
        per_device, mesh=mesh, in_specs=in_specs, out_specs=out_specs, check_vma=False
    )
```

time: 240 us -> 78.3 us (0.33)
  waiting for transfers between devices: 207 us -> 33 us
  starting transfers between devices: 0.16 us -> 16.6 us
  blocking collectives: 2.25 us -> 18.4 us
  between operations: 13.9 us -> 0.7 us
  matrix products: 8.32 us -> 0 us
  Pallas kernels: 0 us -> 4.76 us
  other arithmetic: 3.81 us -> 0.05 us
    psum x2 -> x0, waiting for transfers between devices: 178 us -> none  [the longest x1 133 us: per_device(): lax.psum(local_term.reshape(total_cols, slot_width), ('pole', 'row', 'col'))]
    all_to_all x0 -> x4, waiting for transfers between devices: none -> 33 us  [exchange(): return lax.all_to_all(value, axis, 0, 0, tiled=True)]
    all_gather x1 -> x0, waiting for transfers between devices: 27.7 us -> none  [per_device(): column_rows = lax.all_gather(masked, 'row', axis=1, tiled=True)]
    all_to_all x0 -> x4, starting transfers between devices: none -> 16.6 us  [exchange(): return lax.all_to_all(value, axis, 0, 0, tiled=True)]
    all_to_all x0 -> x1, blocking collectives: none -> 16.1 us  [exchange(): return lax.all_to_all(value, axis, 0, 0, tiled=True)]
    dot_general x8 -> x0, matrix products: 8.32 us -> none  [the longest x4 4.64 us: contract(): jnp.einsum('jk,ij->ki', left, right, preferred_element_type=jnp.float32)]
    pallas_call x0 -> x2, Pallas kernels: none -> 4.76 us  [the longest x1 2.38 us: per_device(): pl.pallas_call(functools.partial(pack_kernel, supernodes, slot), in_specs...]
  transfers between devices with their start and end apart: 4 -> 4, of which waited for: 4 -> 4; matrix products, arithmetic and copies ran while one was open for 3% -> 0% of each run, Pallas kernels for 0% -> 0%
where the time goes in v2:
time: 78.3 us; the launch traced here: 77.7 us
  waiting for transfers between devices  33 us (42%)
  blocking collectives  18.4 us (23%)
  starting transfers between devices  16.6 us (21%)
  Pallas kernels  4.76 us (6%)
  local copies, waits for them, and re-layouts  4.21 us (5%)
    all_to_all x4, waiting for transfers between devices, exchange(): return lax.all_to_all(value, axis, 0, 0, tiled=True)  33 us
    all_to_all x4, starting transfers between devices, exchange(): return lax.all_to_all(value, axis, 0, 0, tiled=True)  16.6 us
    all_to_all x1, blocking collectives, exchange(): return lax.all_to_all(value, axis, 0, 0, tiled=True)  16.1 us
    pallas_call x1, Pallas kernels, per_device(): pl.pallas_call(functools.partial(pack_kernel, supernodes, slot), in_specs...  2.38 us
    pallas_call x1, Pallas kernels, per_device(): pl.pallas_call(functools.partial(compute_kernel, (pole_count, col_count))...  2.37 us
    all_gather x1, blocking collectives, per_device(): own = lax.all_gather(wide, 'col', axis=0)  2.31 us
    broadcast_in_dim x3, local copies, waits for them, and re-layouts, spread(): return exchange(jnp.broadcast_to(value[None], (count,) + value.shape), axis)  2.11 us
  transfers between devices with their start and end apart: 4, of which 4 were waited for; matrix products, arithmetic and copies ran while one was open for 0% of the time, Pallas kernels for 0%

profile of v2, /device:TPU:0, one launch (start us, length us, event | category | flops | bytes accessed | tf_op | source)
XLA Modules:
  0.0 77.7 jit_solution(730262025609630069)
XLA Ops:
  0.6 2.4 %pack.1 = (bf16[4,640,128]{2,1,0:T(8,128)(2,1)}, bf16[2,512,128]{2,1,0:T(8,128)(2,1)}) custom-call(s32[1,4]{1,0:T(1,128)} %pattern_ref.1, s32[4]{0:T(128)} %widths_ref.3, bf16[2,128,512]{2,1,0:T(8,128)(2,1)} %bitcast.15), custom_call_target="tpu_custom_call" | custom-call | tf_op jit(solution)/shard_map/pack/pallas_call | solution.py:156
  3.0 0.0 copy-start.4
  3.0 6.5 %all-to-all-start = ((bf16[4,640,128]{2,1,0:T(8,128)(2,1)}), bf16[4,640,128]{2,1,0:T(8,128)(2,1)S(1)}, u32[]{:S(2)}, u32[]{:S(2)}) async-start(bf16[4,640,128]{2,1,0:T(8,128)(2,1)} %get-tuple-element.4), calls=%async_computation | async-start | bytes 1310720 | tf_op jit(solution)/shard_map/all_to_all | solution.py:136
  9.5 0.0 copy-start
  9.5 0.0 copy-done.4
  9.5 0.0 copy-start.1
  9.5 2.3 %all-gather = bf16[4,512,128]{2,1,0:T(8,128)(2,1)S(1)} all-gather(bf16[2,512,128]{2,1,0:T(8,128)(2,1)S(1)} %copy-done.4), channel_id=2, replica_groups=mesh['pole'=4,'row'=4,'col'=2] {'col'}, dimensions={0}, use_global_device_ids=true | all-gather | bytes 786432 | tf_op jit(solution)/shard_map/all_gather | solution.py:167
  11.8 15.0 %all-to-all-done.packed_ref = bf16[4,640,128]{2,1,0:T(8,128)(2,1)S(1)} async-done(((bf16[4,640,128]{2,1,0:T(8,128)(2,1)}), bf16[4,640,128]{2,1,0:T(8,128)(2,1)S(1)}, u32[]{:S(2)}, u32[]{:S(2)}) %all-to-all-start) | async-done | bytes 655392 | tf_op jit(solution)/shard_map/all_to_all | solution.py:136
  26.8 0.0 copy-start.2
  26.8 0.0 copy-start.3
  26.8 0.0 copy-done
  26.8 0.0 copy-done.1
  26.8 0.6 copy-done.2
  27.4 0.0 copy-done.3
  27.4 2.4 %compute.1 = f32[8,64,384]{2,1,0:T(8,128)S(1)} custom-call(s32[4]{0:T(128)S(1)} %copy-done.2, f32[1,2]{1,0:T(1,128)S(1)} %copy-done.3, s32[1]{0:T(128)} %bitcast.lead_ref, bf16[2048,128]{1,0:T(8,128)(2,1)S(1)} %bitcast.11, bf16[4,640,128]{2,1,0:T(8,128)(2,1)S(1)} %all-to-all-done.packed_ref, bf16[2,2,512,128]{3,2,1,0:T(8,128)(2,1)S(1)} %bitcast.10, ...), custom_call_target="tpu_custom_call" | custom-call | tf_op jit(solution)/shard_map/compute/pallas_call | solution.py:171
  29.8 16.1 %all_to_all.25 = f32[8,64,384]{2,1,0:T(8,128)S(1)} all-to-all(f32[8,64,384]{2,1,0:T(8,128)S(1)} %compute.1), channel_id=1, replica_groups=mesh['pole'=4,'row'=4,'col'=2] {'pole','col'}, dimensions={0} | all-to-all | bytes 1572864 | tf_op jit(solution)/shard_map/all_to_all | solution.py:136
  45.9 0.7 broadcast_in_dim.7
  46.6 3.3 %all-to-all-start.3 = ((f32[4,64,128]{2,1,0:T(8,128)}), f32[4,64,128]{2,1,0:T(8,128)S(1)}, u32[]{:S(2)}, u32[]{:S(2)}) async-start(f32[4,64,128]{2,1,0:T(8,128)} %broadcast_in_dim.7), calls=%async_computation.3 | async-start | bytes 262144 | tf_op jit(solution)/shard_map/all_to_all | solution.py:136
  50.0 5.9 %all-to-all-done.3 = f32[4,64,128]{2,1,0:T(8,128)S(1)} async-done(((f32[4,64,128]{2,1,0:T(8,128)}), f32[4,64,128]{2,1,0:T(8,128)S(1)}, u32[]{:S(2)}, u32[]{:S(2)}) %all-to-all-start.3) | async-done | bytes 131104 | tf_op jit(solution)/shard_map/all_to_all | solution.py:136
  55.8 0.7 broadcast_in_dim.6
  56.5 3.4 %all-to-all-start.2 = ((f32[4,64,256]{2,1,0:T(8,128)}), f32[4,64,256]{2,1,0:T(8,128)S(1)}, u32[]{:S(2)}, u32[]{:S(2)}) async-start(f32[4,64,256]{2,1,0:T(8,128)} %broadcast_in_dim.6), calls=%async_computation.2 | async-start | bytes 524288 | tf_op jit(solution)/shard_map/all_to_all | solution.py:136
  60.0 5.3 %all-to-all-done.2 = f32[4,64,256]{2,1,0:T(8,128)S(1)} async-done(((f32[4,64,256]{2,1,0:T(8,128)}), f32[4,64,256]{2,1,0:T(8,128)S(1)}, u32[]{:S(2)}, u32[]{:S(2)}) %all-to-all-start.2) | async-done | bytes 262176 | tf_op jit(solution)/shard_map/all_to_all | solution.py:136
  65.3 0.7 broadcast_in_dim.8
  66.0 3.4 %all-to-all-start.4 = ((f32[8,64,128]{2,1,0:T(8,128)}), f32[8,64,128]{2,1,0:T(8,128)S(1)}, u32[]{:S(2)}, u32[]{:S(2)}) async-start(f32[8,64,128]{2,1,0:T(8,128)} %broadcast_in_dim.8), calls=%async_computation.4 | async-start | bytes 524288 | tf_op jit(solution)/shard_map/all_to_all | solution.py:136
  69.4 6.9 %all-to-all-done.4 = f32[8,64,128]{2,1,0:T(8,128)S(1)} async-done(((f32[8,64,128]{2,1,0:T(8,128)}), f32[8,64,128]{2,1,0:T(8,128)S(1)}, u32[]{:S(2)}, u32[]{:S(2)}) %all-to-all-start.4) | async-done | bytes 262176 | tf_op jit(solution)/shard_map/all_to_all | solution.py:136
  76.3 0.7 copy.10
  77.0 0.7 copy.12
  (4 shorter events, 0.1 us)
Async XLA Ops:
  3.0 6.5 %copy-start.4 = (bf16[2,512,128]{2,1,0:T(8,128)(2,1)S(1)}, bf16[2,512,128]{2,1,0:T(8,128)(2,1)}, u32[]{:S(2)}) copy-start(bf16[2,512,128]{2,1,0:T(8,128)(2,1)} %get-tuple-element.5) | copy-start | bytes 786436
  3.0 23.7 %all-to-all-start = ((bf16[4,640,128]{2,1,0:T(8,128)(2,1)}), bf16[4,640,128]{2,1,0:T(8,128)(2,1)S(1)}, u32[]{:S(2)}, u32[]{:S(2)}) async-start(bf16[4,640,128]{2,1,0:T(8,128)(2,1)} %get-tuple-element.4), calls=%async_computation | async-start | bytes 1310720 | tf_op jit(solution)/shard_map/all_to_all | solution.py:136
  9.5 17.3 %copy-start = (bf16[1,2,256,4,1,128]{5,3,4,2,1,0:T(4,128)(2,1)S(1)}, bf16[1,2,256,4,1,128]{5,3,4,2,1,0:T(4,128)(2,1)}, u32[]{:S(2)}) copy-start(bf16[1,2,256,4,1,128]{5,3,4,2,1,0:T(4,128)(2,1)} %param.6) | copy-start | bytes 1572868
  9.5 17.3 %copy-start.1 = (bf16[1,2,512,128]{3,2,1,0:T(8,128)(2,1)S(1)}, bf16[1,2,512,128]{3,2,1,0:T(8,128)(2,1)}, u32[]{:S(2)}) copy-start(bf16[1,2,512,128]{3,2,1,0:T(8,128)(2,1)} %param.10) | copy-start | bytes 786436
  26.8 0.7 copy-start.2
  26.8 0.7 copy-start.3
  46.6 9.2 %all-to-all-start.3 = ((f32[4,64,128]{2,1,0:T(8,128)}), f32[4,64,128]{2,1,0:T(8,128)S(1)}, u32[]{:S(2)}, u32[]{:S(2)}) async-start(f32[4,64,128]{2,1,0:T(8,128)} %broadcast_in_dim.7), calls=%async_computation.3 | async-start | bytes 262144 | tf_op jit(solution)/shard_map/all_to_all | solution.py:136
  56.5 8.8 %all-to-all-start.2 = ((f32[4,64,256]{2,1,0:T(8,128)}), f32[4,64,256]{2,1,0:T(8,128)S(1)}, u32[]{:S(2)}, u32[]{:S(2)}) async-start(f32[4,64,256]{2,1,0:T(8,128)} %broadcast_in_dim.6), calls=%async_computation.2 | async-start | bytes 524288 | tf_op jit(solution)/shard_map/all_to_all | solution.py:136
  66.0 10.3 %all-to-all-start.4 = ((f32[8,64,128]{2,1,0:T(8,128)}), f32[8,64,128]{2,1,0:T(8,128)S(1)}, u32[]{:S(2)}, u32[]{:S(2)}) async-start(f32[8,64,128]{2,1,0:T(8,128)} %broadcast_in_dim.8), calls=%async_computation.4 | async-start | bytes 524288 | tf_op jit(solution)/shard_map/all_to_all | solution.py:136

commit v3 on v2

v3 whole, which is shorter than its diff:
```python
import functools

import jax
import jax.numpy as jnp
from jax import lax
from jax.experimental import pallas as pl
from jax.experimental.pallas import tpu as pltpu
from jax.sharding import PartitionSpec as P

F32 = jnp.float32
BF16 = jnp.bfloat16
VMEM_SPEC = pl.BlockSpec(memory_space=pltpu.VMEM)
SMEM_SPEC = pl.BlockSpec(memory_space=pltpu.SMEM)
PARAMS = pltpu.CompilerParams(vmem_limit_bytes=48 * 1024 * 1024)


def rows_by_rows(left, right):
    return lax.dot_general(left, right, (((1,), (1,)), ((), ())), preferred_element_type=F32)


def offsets_of(widths_ref, supernodes):
    offsets = [0]
    for k in range(supernodes):
        offsets.append(offsets[-1] + widths_ref[k])
    return offsets


def pack_kernel(supernodes, slot, pattern_ref, widths_ref, panel_ref, packed_ref):
    packed_width = packed_ref.shape[0] // 2
    offsets = offsets_of(widths_ref, supernodes)
    lane = lax.broadcasted_iota(jnp.int32, (1, slot), 1)
    place = []
    for k in range(supernodes):
        valid = (lane < widths_ref[k]) & (pattern_ref[0, k] == 1)
        place.append(jnp.where(valid, offsets[k] + lane, -1))
    place = jnp.concatenate(place, axis=1)
    target = lax.broadcasted_iota(jnp.int32, (packed_width, supernodes * slot), 0)
    select = jnp.where(target == place, 1.0, 0.0).astype(BF16)
    for part in range(2):
        packed_ref[part * packed_width:(part + 1) * packed_width, :] = rows_by_rows(
            select, panel_ref[part]
        ).astype(BF16)


def prepare_kernel(row_count, place_ref, inverse_ref, straight_ref):
    block = inverse_ref.shape[1]
    local_rows = straight_ref.shape[1]
    row_index = place_ref[0]
    group = max(8, 256 // row_count)
    span = group * row_count
    row_id = lax.broadcasted_iota(jnp.int32, (span, span), 0)
    col_id = lax.broadcasted_iota(jnp.int32, (span, span), 1)
    source = (row_id % group) * row_count + (row_id // group + row_index) % row_count
    order = jnp.where(col_id == source, 1.0, 0.0).astype(BF16)
    for part in range(2):
        for chunk in range(local_rows // group):
            base = (part * local_rows + chunk * group) * row_count
            mixed = inverse_ref[base:base + span, :]
            sorted_rows = jnp.dot(order, mixed, preferred_element_type=F32).astype(BF16)
            for owner in range(row_count):
                straight_ref[
                    part, chunk * group:(chunk + 1) * group, owner * block:(owner + 1) * block
                ] = sorted_rows[owner * group:(owner + 1) * group]


def compute_kernel(
    counts, supernodes, slot, widths_ref, weights_ref, place_ref, straight_ref, diag_ref, *refs
):
    row_count, col_count = counts
    block_refs, refs = refs[:row_count], refs[row_count:]
    own_refs, refs = refs[:col_count], refs[col_count:]
    keep_d_ref, send_d_ref, keep_t_ref, send_t_ref, term_ref, x_ref, y_ref = refs
    packed_width = block_refs[0].shape[0] // 2
    local_rows = straight_ref.shape[1]
    strips = local_rows // slot
    w_real = weights_ref[0, 0]
    w_imag = weights_ref[0, 1]
    col_index = place_ref[1]

    panel = jnp.concatenate([ref[...] for ref in block_refs], axis=1)
    with_real = rows_by_rows(panel, straight_ref[0])
    with_imag = rows_by_rows(panel, straight_ref[1])
    u_real = with_imag[packed_width:] - with_real[:packed_width]
    u_imag = -(with_real[packed_width:] + with_imag[:packed_width])
    weighted = w_real * u_real - w_imag * u_imag
    turned = w_real * u_imag + w_imag * u_real

    half = packed_width // 2
    upper = (col_index & (col_count // 2)) != 0
    keep_d_ref[...] = jnp.where(upper, weighted[half:], weighted[:half])
    send_d_ref[...] = jnp.where(upper, weighted[:half], weighted[half:])

    for ref, value in ((x_ref, weighted), (y_ref, turned)):
        for s in range(strips):
            ref[s, :packed_width] = value[:, s * slot:(s + 1) * slot]
            ref[s, packed_width:] = jnp.zeros((slot, slot), F32)

    own = [jnp.zeros((), BF16)] * col_count
    for c in range(col_count):
        block_of = own_refs[0][...]
        for other in range(1, col_count):
            block_of = jnp.where((col_index ^ c) == other, own_refs[other][...], block_of)
        own[c] = block_of
    own = jnp.concatenate(own, axis=1)
    offsets = offsets_of(widths_ref, supernodes)
    row_in_slot = lax.broadcasted_iota(jnp.int32, (slot, 1), 0)
    row_packed = lax.broadcasted_iota(jnp.int32, (packed_width, 1), 0)
    total = jnp.zeros((packed_width, slot), F32)
    for k in range(supernodes):
        valid = row_in_slot < widths_ref[k]
        x, y = (
            jnp.concatenate(
                [jnp.where(valid, ref[s, pl.ds(offsets[k], slot), :], 0.0) for s in range(strips)],
                axis=1,
            )
            for ref in (x_ref, y_ref)
        )
        x_high, y_high = x.astype(BF16), y.astype(BF16)
        x_low = (x - x_high.astype(F32)).astype(BF16)
        y_low = (y - y_high.astype(F32)).astype(BF16)
        product = (
            rows_by_rows(own[:packed_width], x_high) - rows_by_rows(own[packed_width:], y_high)
        ) + (rows_by_rows(own[:packed_width], x_low) - rows_by_rows(own[packed_width:], y_low))
        inside = (row_packed >= offsets[k]) & (row_packed < offsets[k + 1])
        total = jnp.where(inside, product, total)
    keep_t_ref[...] = jnp.where(upper, total[half:], total[:half])
    send_t_ref[...] = jnp.where(upper, total[:half], total[half:])

    folded = term_ref.shape[0]
    for s in range(strips):
        first = pl.multiple_of((col_index * strips + s) * folded, folded)
        term_ref[:, s * slot:(s + 1) * slot] = w_real * diag_ref[
            0, pl.ds(first, folded), :
        ].astype(F32) - w_imag * diag_ref[1, pl.ds(first, folded), :].astype(F32)


def expand_kernel(
    col_count, slot, widths_ref, place_ref, mine_d_ref, other_d_ref, mine_t_ref, other_t_ref,
    density_ref, diagonal_ref, strip_ref,
):
    supernodes = diagonal_ref.shape[0] // slot
    per_col, local_rows = density_ref.shape
    strips = local_rows // slot
    folded = per_col // strips
    share = col_count // 2
    tall = mine_d_ref.shape[0] // share
    part = tall - folded
    col_index = place_ref[1]
    upper = (col_index & share) != 0
    for side in range(2):
        own_side = upper if side else jnp.logical_not(upper)
        d_value = jnp.where(own_side, mine_d_ref[...], other_d_ref[...])
        t_value = jnp.where(own_side, mine_t_ref[...], other_t_ref[...])
        for q in range(share):
            owner = side * share + q
            base = owner * part
            for s in range(strips):
                lanes = slice(s * slot, (s + 1) * slot)
                strip_ref[s, base:base + part] = d_value[q * tall:q * tall + part, lanes]
                first = (owner * strips + s) * folded
                diagonal_ref[first:first + folded] = d_value[q * tall + part:(q + 1) * tall, lanes]
            rows = slice(q * part // 2, (q + 1) * part // 2)
            strip_ref[strips, base:base + part // 2] = t_value[rows, :slot]
            strip_ref[strips, base + part // 2:base + part] = t_value[rows, slot:]
    for s in range(strips + 1):
        strip_ref[s, col_count * part:] = jnp.zeros((slot, slot), F32)
    offsets = offsets_of(widths_ref, supernodes)
    row_in_slot = lax.broadcasted_iota(jnp.int32, (slot, 1), 0)
    for k in range(supernodes):
        product = strip_ref[strips, pl.ds(offsets[k], slot), :]
        product = jnp.where(row_in_slot < widths_ref[k], product, 0.0)
        diagonal_ref[k * slot:(k + 1) * slot] = diagonal_ref[k * slot:(k + 1) * slot] - product
    size = min(per_col, slot)
    row_in_part = lax.broadcasted_iota(jnp.int32, (size, 1), 0)
    for part in range(per_col // size):
        first = col_index * per_col + part * size
        owner = first // slot
        within = first % slot
        start, count = 0, 0
        for k in range(supernodes):
            start = start + jnp.where(k < owner, widths_ref[k], 0)
            count = count + jnp.where(k == owner, widths_ref[k], 0)
        for s in range(strips):
            piece = strip_ref[s, pl.ds(start + within, size), :]
            density_ref[part * size:(part + 1) * size, s * slot:(s + 1) * slot] = jnp.where(
                row_in_part < count - within, piece, 0.0
            )


def bits_of(count):
    return [1 << k for k in range(count.bit_length() - 1)]


def swap(value, axis, bit):
    return lax.ppermute(value, axis, [(i, i ^ bit) for i in range(lax.axis_size(axis))])


def pole_sum(value):
    bits = bits_of(lax.axis_size("pole"))
    half = value.shape[0] // 2
    first, second = value[:half], value[half:]
    for bit, mirrored in zip(bits, bits[::-1]):
        first, second = first + swap(first, "pole", bit), second + swap(second, "pole", mirrored)
    return first, second


def scatter_rest(value, axis):
    index = lax.axis_index(axis)
    for bit in bits_of(lax.axis_size(axis))[:-1][::-1]:
        half = value.shape[0] // 2
        upper = (index & bit) != 0
        keep = jnp.where(upper, value[half:], value[:half])
        value = keep + swap(jnp.where(upper, value[:half], value[half:]), axis, bit)
    return value


def gather_but_last(value, axis):
    index = lax.axis_index(axis)
    for bit in bits_of(lax.axis_size(axis))[:-1]:
        other = swap(value, axis, bit)
        upper = (index & bit) != 0
        value = jnp.concatenate(
            [jnp.where(upper, other, value), jnp.where(upper, value, other)], axis=0
        )
    return value


def per_device(found_inverse, l_panel, block_pattern, sup_widths, diag_inverse, pole_weights):
    slot = diag_inverse.shape[-1]
    total_cols = l_panel.shape[-1]
    supernodes = total_cols // slot
    packed_width = slot + (supernodes - 1) * (slot // 2)
    half = packed_width // 2
    local_rows = found_inverse.shape[2]
    block = l_panel.shape[2]
    row_count = lax.axis_size("row")
    col_count = lax.axis_size("col")
    top = col_count // 2
    place = jnp.stack([lax.axis_index("row"), lax.axis_index("col")]).astype(jnp.int32)

    packed = pl.pallas_call(
        functools.partial(pack_kernel, supernodes, slot),
        in_specs=[SMEM_SPEC, SMEM_SPEC, VMEM_SPEC],
        out_specs=VMEM_SPEC,
        out_shape=jax.ShapeDtypeStruct((2 * packed_width, block), BF16),
        compiler_params=PARAMS,
        name="pack",
    )(block_pattern, sup_widths, l_panel[0])

    blocks = {0: packed}
    for shift in sorted(range(1, row_count), key=lambda s: -min(s, row_count - s)):
        pairs = [((i + shift) % row_count, i) for i in range(row_count)]
        blocks[shift] = lax.ppermute(packed, "row", pairs)
    own = [packed] + [swap(packed, "col", other) for other in range(1, col_count)]

    straight = pl.pallas_call(
        functools.partial(prepare_kernel, row_count),
        in_specs=[SMEM_SPEC, VMEM_SPEC],
        out_specs=VMEM_SPEC,
        out_shape=jax.ShapeDtypeStruct((2, local_rows, row_count * block), BF16),
        compiler_params=PARAMS,
        cost_estimate=pl.CostEstimate(
            flops=4 * 256 * local_rows * row_count * block,
            bytes_accessed=8 * local_rows * row_count * block,
            transcendentals=0,
        ),
        name="prepare",
    )(place, found_inverse.reshape(2 * local_rows * row_count, block))

    keep_d, send_d, keep_t, send_t, term = pl.pallas_call(
        functools.partial(compute_kernel, (row_count, col_count), supernodes, slot),
        in_specs=[SMEM_SPEC] * 3 + [VMEM_SPEC] * (2 + row_count + col_count),
        out_specs=[VMEM_SPEC] * 5,
        out_shape=[jax.ShapeDtypeStruct((half, local_rows), F32)] * 2
        + [jax.ShapeDtypeStruct((half, slot), F32)] * 2
        + [jax.ShapeDtypeStruct((total_cols * slot // (col_count * local_rows), local_rows), F32)],
        scratch_shapes=[
            pltpu.VMEM((local_rows // slot, packed_width + slot, slot), F32),
            pltpu.VMEM((local_rows // slot, packed_width + slot, slot), F32),
        ],
        compiler_params=PARAMS,
        name="compute",
    )(
        sup_widths, pole_weights, place, straight, diag_inverse[0],
        *[blocks[shift] for shift in range(row_count)], *own,
    )

    products = scatter_rest(keep_t + swap(send_t, "col", top), "col")
    density = scatter_rest(keep_d + swap(send_d, "col", top), "col")
    products = jnp.concatenate(pole_sum(products), axis=1)
    for bit in bits_of(row_count):
        products = products + swap(products, "row", bit)
    density = jnp.concatenate(pole_sum(jnp.concatenate([density, term], axis=0)), axis=0)
    density = gather_but_last(density, "col")
    products = gather_but_last(products, "col")

    return pl.pallas_call(
        functools.partial(expand_kernel, col_count, slot),
        in_specs=[SMEM_SPEC] * 2 + [VMEM_SPEC] * 4,
        out_specs=[VMEM_SPEC] * 2,
        out_shape=[
            jax.ShapeDtypeStruct((total_cols // col_count, local_rows), F32),
            jax.ShapeDtypeStruct((total_cols, slot), F32),
        ],
        scratch_shapes=[pltpu.VMEM((local_rows // slot + 1, packed_width + slot, slot), F32)],
        compiler_params=PARAMS,
        name="expand",
    )(
        sup_widths, place, density, swap(density, "col", top),
        products, swap(products, "col", top),
    )


def solution(mesh):
    in_specs = (
        P("pole", None, "row", None, "col", None),
        P("pole", None, ("row", "col"), None),
        P(("row", "col"), None),
        P(),
        P("pole", None, None, None),
        P("pole", None),
    )
    out_specs = (P("col", "row"), P())
    return jax.shard_map(
        per_device, mesh=mesh, in_specs=in_specs, out_specs=out_specs, check_vma=False
    )
```

time: 78.3 us -> 54.7 us (0.70)
  blocking collectives: 18.4 us -> 0 us
  waiting for transfers between devices: 33 us -> 19.9 us
  starting transfers between devices: 16.6 us -> 24.9 us
  local copies, waits for them, and re-layouts: 4.21 us -> 2.67 us
  Pallas kernels: 4.76 us -> 5.97 us
    all_to_all x4 -> x0, waiting for transfers between devices: 33 us -> none  [exchange(): return lax.all_to_all(value, axis, 0, 0, tiled=True)]
    ppermute x0 -> x18, starting transfers between devices: none -> 24.9 us  [the longest x15 18.3 us: swap(): lax.ppermute(value, axis, [(i, i ^ bit) for i in range(lax.axis_size(axis...]
    ppermute x0 -> x18, waiting for transfers between devices: none -> 19.9 us  [the longest x15 12.1 us: swap(): lax.ppermute(value, axis, [(i, i ^ bit) for i in range(lax.axis_size(axis...]
    all_to_all x4 -> x0, starting transfers between devices: 16.6 us -> none  [exchange(): return lax.all_to_all(value, axis, 0, 0, tiled=True)]
    all_to_all x1 -> x0, blocking collectives: 16.1 us -> none  [exchange(): return lax.all_to_all(value, axis, 0, 0, tiled=True)]
    pallas_call x1 -> x3, Pallas kernels: 2.37 us -> 5.1 us  [the longest x1 2.64 us: per_device(): pl.pallas_call(functools.partial(compute_kernel, (row_count, col_count),...]
    all_gather x1 -> x0, blocking collectives: 2.31 us -> none  [per_device(): own = lax.all_gather(wide, 'col', axis=0)]
    broadcast_in_dim x3 -> x0, local copies, waits for them, and re-layouts: 2.11 us -> none  [spread(): return exchange(jnp.broadcast_to(value[None], (count,) + value.shape), axis)]
  transfers between devices with their start and end apart: 4 -> 18, of which waited for: 4 -> 8; matrix products, arithmetic and copies ran while one was open for 0% -> 0% of each run, Pallas kernels for 0% -> 2%
where the time goes in v3:
time: 54.7 us; the launch traced here: 54.5 us
  starting transfers between devices  24.9 us (46%)
  waiting for transfers between devices  19.9 us (36%)
  Pallas kernels  5.97 us (11%)
  local copies, waits for them, and re-layouts  2.67 us (5%)
  between operations  0.82 us (1%)
    ppermute x15, starting transfers between devices, swap(): lax.ppermute(value, axis, [(i, i ^ bit) for i in range(lax.axis_size(axis...  18.3 us
    ppermute x15, waiting for transfers between devices, swap(): lax.ppermute(value, axis, [(i, i ^ bit) for i in range(lax.axis_size(axis...  12.1 us
    ppermute x3, waiting for transfers between devices, per_device(): blocks[shift] = lax.ppermute(packed, 'row', pairs)  7.87 us
    ppermute x3, starting transfers between devices, per_device(): blocks[shift] = lax.ppermute(packed, 'row', pairs)  6.57 us
    unnamed x12, local copies, waits for them, and re-layouts  2.66 us
    pallas_call x1, Pallas kernels, per_device(): pl.pallas_call(functools.partial(compute_kernel, (row_count, col_count),...  2.64 us
    pallas_call x1, Pallas kernels, per_device(): pl.pallas_call(functools.partial(expand_kernel, col_count, slot), in_spec...  1.47 us
  transfers between devices with their start and end apart: 18, of which 8 were waited for; matrix products, arithmetic and copies ran while one was open for 0% of the time, Pallas kernels for 2%

profile of v3, /device:TPU:0, one launch (start us, length us, event | category | flops | bytes accessed | tf_op | source)
XLA Modules:
  0.0 54.5 jit_solution(17466642856926199288)
XLA Ops:
  0.6 0.0 copy-start.3
  0.6 0.0 copy-start.4
  0.7 0.6 %copy-done.3 = s32[4]{0:T(128)S(1)} copy-done((s32[4]{0:T(128)S(1)}, s32[4]{0:T(128)}, u32[]{:S(2)}) %copy-start.3) | copy-done | bytes 40
  1.3 0.0 copy-done.4
  1.3 0.0 copy-start.2
  1.3 0.9 %copy-done.2 = bf16[1,2,128,512]{3,2,1,0:T(8,128)(2,1)S(1)} copy-done((bf16[1,2,128,512]{3,2,1,0:T(8,128)(2,1)S(1)}, bf16[1,2,128,512]{3,2,1,0:T(8,128)(2,1)}, u32[]{:S(2)}) %copy-start.2) | copy-done | bytes 262168
  2.3 0.9 %pack.1.refs_0_.refs_4_ = bf16[640,128]{1,0:T(8,128)(2,1)S(1)} custom-call(s32[1,4]{1,0:T(1,128)S(1)} %copy-done.4, s32[4]{0:T(128)S(1)} %copy-done.3, bf16[2,128,512]{2,1,0:T(8,128)(2,1)S(1)} %bitcast.7), custom_call_target="tpu_custom_call" | custom-call | tf_op jit(solution)/shard_map/pack/pallas_call | solution.py:241
  3.1 0.5 collective-permute-start.3
  3.6 2.6 %collective-permute-start.2 = (bf16[640,128]{1,0:T(8,128)(2,1)S(1)}, bf16[640,128]{1,0:T(8,128)(2,1)S(1)}, u32[]{:S(2)}, u32[]{:S(2)}) collective-permute-start(bf16[640,128]{1,0:T(8,128)(2,1)S(1)} %pack.1.refs_0_.refs_4_), channel_id=1, source_target_pairs={{6,0},{0,2},{2,4},{4,6},{7,1},{1,3},{3,5},{5,7},{14,8},{8,10},{10,... | collective-permute-start | bytes 491528 | tf_op jit(solution)/shard_map/ppermute | solution.py:253
  6.3 2.6 %collective-permute-start.1 = (bf16[640,128]{1,0:T(8,128)(2,1)S(1)}, bf16[640,128]{1,0:T(8,128)(2,1)S(1)}, u32[]{:S(2)}, u32[]{:S(2)}) collective-permute-start(bf16[640,128]{1,0:T(8,128)(2,1)S(1)} %pack.1.refs_0_.refs_4_), channel_id=1, source_target_pairs={{4,0},{6,2},{0,4},{2,6},{5,1},{7,3},{1,5},{3,7},{12,8},{14,10},{8,... | collective-permute-start | bytes 491528 | tf_op jit(solution)/shard_map/ppermute | solution.py:253
  8.9 1.4 %collective-permute-start = (bf16[640,128]{1,0:T(8,128)(2,1)S(1)}, bf16[640,128]{1,0:T(8,128)(2,1)S(1)}, u32[]{:S(2)}, u32[]{:S(2)}) collective-permute-start(bf16[640,128]{1,0:T(8,128)(2,1)S(1)} %pack.1.refs_0_.refs_4_), channel_id=1, source_target_pairs={{2,0},{4,2},{6,4},{0,6},{3,1},{5,3},{7,5},{1,7},{10,8},{12,10},{14... | collective-permute-start | bytes 491528 | tf_op jit(solution)/shard_map/ppermute | solution.py:253
  10.2 0.1 pad_add_fusion.place_ref
  10.3 0.0 copy-start
  10.3 1.0 %copy-done = bf16[1,2,256,4,1,128]{5,3,4,2,1,0:T(4,128)(2,1)S(1)} copy-done((bf16[1,2,256,4,1,128]{5,3,4,2,1,0:T(4,128)(2,1)S(1)}, bf16[1,2,256,4,1,128]{5,3,4,2,1,0:T(4,128)(2,1)}, u32[]{:S(2)}) %copy-start) | copy-done | bytes 524312
  11.3 0.0 copy-start.1
  11.3 1.0 %prepare.1.straight_ref = bf16[2,256,512]{2,1,0:T(8,128)(2,1)S(1)} custom-call(s32[2]{0:T(128)S(1)} %pad_add_fusion.place_ref, bf16[2048,128]{1,0:T(8,128)(2,1)S(1)} %bitcast.5), custom_call_target="tpu_custom_call" | custom-call | flops 134217728 | bytes 1048576 | tf_op jit(solution)/shard_map/prepare/pallas_call | solution.py:256
  12.3 0.0 copy-start.5
  12.3 0.0 collective-permute-done.3.refs_5_
  12.4 1.1 %collective-permute-done.2.refs_3_ = bf16[640,128]{1,0:T(8,128)(2,1)S(1)} collective-permute-done((bf16[640,128]{1,0:T(8,128)(2,1)S(1)}, bf16[640,128]{1,0:T(8,128)(2,1)S(1)}, u32[]{:S(2)}, u32[]{:S(2)}) %collective-permute-start.2) | collective-permute-done | bytes 163872 | tf_op jit(solution)/shard_map/ppermute | solution.py:253
  13.5 6.7 %collective-permute-done.1.refs_2_ = bf16[640,128]{1,0:T(8,128)(2,1)S(1)} collective-permute-done((bf16[640,128]{1,0:T(8,128)(2,1)S(1)}, bf16[640,128]{1,0:T(8,128)(2,1)S(1)}, u32[]{:S(2)}, u32[]{:S(2)}) %collective-permute-start.1) | collective-permute-done | bytes 163872 | tf_op jit(solution)/shard_map/ppermute | solution.py:253
  20.2 0.0 collective-permute-done.refs_1_
  20.2 0.0 copy-done.1
  20.2 0.0 copy-done.5
  20.2 2.6 %compute.1 = (f32[160,256]{1,0:T(8,128)S(1)}, f32[160,256]{1,0:T(8,128)S(1)}, f32[160,128]{1,0:T(8,128)S(1)}, f32[160,128]{1,0:T(8,128)S(1)}, f32[128,256]{1,0:T(8,128)S(1)}) custom-call(s32[4]{0:T(128)S(1)} %copy-done.3, f32[1,2]{1,0:T(1,128)S(1)} %copy-done.5, s32[2]{0:T(128)S(1)} %pad_add_fusion.place_ref, bf16[2,256,512]{2,1,0:T(8,128)(2,1)S(1)} %prepare.1.straight_ref, ...), custom_call_target="tpu_custom_call" | custom-call | tf_op jit(solution)/shard_map/compute/pallas_call | solution.py:270
  22.9 0.1 collective-permute-start.4
  23.0 0.5 collective-permute-start.10
  23.5 1.0 %collective-permute-done.10 = f32[160,128]{1,0:T(8,128)S(1)} collective-permute-done((f32[160,128]{1,0:T(8,128)S(1)}, f32[160,128]{1,0:T(8,128)S(1)}, u32[]{:S(2)}, u32[]{:S(2)}) %collective-permute-start.10) | collective-permute-done | bytes 81952 | tf_op jit(solution)/shard_map/ppermute | solution.py:195
  24.5 0.0 collective-permute-done.4
  24.5 1.5 %collective-permute-start.5 = (f32[144,256]{1,0:T(8,128)S(1)}, f32[144,256]{1,0:T(8,128)S(1)}, u32[]{:S(2)}, u32[]{:S(2)}) collective-permute-start(f32[144,256]{1,0:T(8,128)S(1)} %slice.16), channel_id=1, source_target_pairs={{0,8},{8,0},{16,24},{24,16},{1,9},{9,1},{17,25},{25,17},{2,10},{10... | collective-permute-start | bytes 442376 | tf_op jit(solution)/shard_map/ppermute | solution.py:195
  26.1 0.6 %collective-permute-start.11 = (f32[80,128]{1,0:T(8,128)S(1)}, f32[80,128]{1,0:T(8,128)S(1)}, u32[]{:S(2)}, u32[]{:S(2)}) collective-permute-start(f32[80,128]{1,0:T(8,128)S(1)} %get-tuple-element.16), channel_id=1, source_target_pairs={{0,8},{8,0},{16,24},{24,16},{1,9},{9,1},{17,25},{25,17},{2,10},{10... | collective-permute-start | bytes 122888 | tf_op jit(solution)/shard_map/ppermute | solution.py:195
  26.6 1.5 %collective-permute-start.13 = (f32[80,128]{1,0:T(8,128)S(1)}, f32[80,128]{1,0:T(8,128)S(1)}, u32[]{:S(2)}, u32[]{:S(2)}) collective-permute-start(f32[80,128]{1,0:T(8,128)S(1)} %get-tuple-element.17), channel_id=1, source_target_pairs={{0,16},{8,24},{16,0},{24,8},{1,17},{9,25},{17,1},{25,9},{2,18},{10... | collective-permute-start | bytes 122888 | tf_op jit(solution)/shard_map/ppermute | solution.py:195
  28.1 2.9 %collective-permute-done.5 = f32[144,256]{1,0:T(8,128)S(1)} collective-permute-done((f32[144,256]{1,0:T(8,128)S(1)}, f32[144,256]{1,0:T(8,128)S(1)}, u32[]{:S(2)}, u32[]{:S(2)}) %collective-permute-start.5) | collective-permute-done | bytes 147488 | tf_op jit(solution)/shard_map/ppermute | solution.py:195
  31.1 1.6 %collective-permute-start.7 = (f32[144,256]{1,0:T(8,128)S(1)}, f32[144,256]{1,0:T(8,128)S(1)}, u32[]{:S(2)}, u32[]{:S(2)}) collective-permute-start(f32[144,256]{1,0:T(8,128)S(1)} %get-tuple-element.13), channel_id=1, source_target_pairs={{0,16},{8,24},{16,0},{24,8},{1,17},{9,25},{17,1},{25,9},{2,18},{10... | collective-permute-start | bytes 442376 | tf_op jit(solution)/shard_map/ppermute | solution.py:195
  32.7 0.0 collective-permute-done.11
  32.7 0.0 collective-permute-done.13
  32.7 0.6 %collective-permute-start.12 = (f32[80,128]{1,0:T(8,128)S(1)}, f32[80,128]{1,0:T(8,128)S(1)}, u32[]{:S(2)}, u32[]{:S(2)}) collective-permute-start(f32[80,128]{1,0:T(8,128)S(1)} %get-tuple-element.14), channel_id=1, source_target_pairs={{0,16},{8,24},{16,0},{24,8},{1,17},{9,25},{17,1},{25,9},{2,18},{10... | collective-permute-start | bytes 122888 | tf_op jit(solution)/shard_map/ppermute | solution.py:195
  33.3 1.5 %collective-permute-start.14 = (f32[80,128]{1,0:T(8,128)S(1)}, f32[80,128]{1,0:T(8,128)S(1)}, u32[]{:S(2)}, u32[]{:S(2)}) collective-permute-start(f32[80,128]{1,0:T(8,128)S(1)} %get-tuple-element.15), channel_id=1, source_target_pairs={{0,8},{8,0},{16,24},{24,16},{1,9},{9,1},{17,25},{25,17},{2,10},{10... | collective-permute-start | bytes 122888 | tf_op jit(solution)/shard_map/ppermute | solution.py:195
  34.8 1.5 %collective-permute-start.6 = (f32[144,256]{1,0:T(8,128)S(1)}, f32[144,256]{1,0:T(8,128)S(1)}, u32[]{:S(2)}, u32[]{:S(2)}) collective-permute-start(f32[144,256]{1,0:T(8,128)S(1)} %get-tuple-element.12), channel_id=1, source_target_pairs={{0,16},{8,24},{16,0},{24,8},{1,17},{9,25},{17,1},{25,9},{2,18},{10... | collective-permute-start | bytes 442376 | tf_op jit(solution)/shard_map/ppermute | solution.py:195
  36.3 0.4 collective-permute-done.7
  36.7 2.5 %collective-permute-start.8 = (f32[144,256]{1,0:T(8,128)S(1)}, f32[144,256]{1,0:T(8,128)S(1)}, u32[]{:S(2)}, u32[]{:S(2)}) collective-permute-start(f32[144,256]{1,0:T(8,128)S(1)} %add.39), channel_id=1, source_target_pairs={{0,8},{8,0},{16,24},{24,16},{1,9},{9,1},{17,25},{25,17},{2,10},{10... | collective-permute-start | bytes 442376 | tf_op jit(solution)/shard_map/ppermute | solution.py:195
  39.2 0.0 collective-permute-done.12
  39.2 0.0 collective-permute-done.14
  39.2 4.1 %collective-permute-start.15 = (f32[80,256]{1,0:T(8,128)S(1)}, f32[80,256]{1,0:T(8,128)S(1)}, u32[]{:S(2)}, u32[]{:S(2)}) collective-permute-start(f32[80,256]{1,0:T(8,128)S(1)} %pad_maximum_fusion.2), channel_id=1, source_target_pairs={{0,2},{2,0},{4,6},{6,4},{1,3},{3,1},{5,7},{7,5},{8,10},{10,8},{12,... | collective-permute-start | bytes 245768 | tf_op jit(solution)/shard_map/ppermute | solution.py:195
  43.3 0.0 collective-permute-done.6
  43.3 0.0 collective-permute-done.8
  43.4 0.1 collective-permute-start.9
  43.5 2.2 %collective-permute-done.15 = f32[80,256]{1,0:T(8,128)S(1)} collective-permute-done((f32[80,256]{1,0:T(8,128)S(1)}, f32[80,256]{1,0:T(8,128)S(1)}, u32[]{:S(2)}, u32[]{:S(2)}) %collective-permute-start.15) | collective-permute-done | bytes 81952 | tf_op jit(solution)/shard_map/ppermute | solution.py:195
  45.7 1.7 %collective-permute-start.16 = (f32[80,256]{1,0:T(8,128)S(1)}, f32[80,256]{1,0:T(8,128)S(1)}, u32[]{:S(2)}, u32[]{:S(2)}) collective-permute-start(f32[80,256]{1,0:T(8,128)S(1)} %fusion), channel_id=1, source_target_pairs={{0,4},{2,6},{4,0},{6,2},{1,5},{3,7},{5,1},{7,3},{8,12},{10,14},{12... | collective-permute-start | bytes 245768 | tf_op jit(solution)/shard_map/ppermute | solution.py:195
  47.5 4.2 %collective-permute-done.16 = f32[80,256]{1,0:T(8,128)S(1)} collective-permute-done((f32[80,256]{1,0:T(8,128)S(1)}, f32[80,256]{1,0:T(8,128)S(1)}, u32[]{:S(2)}, u32[]{:S(2)}) %collective-permute-start.16) | collective-permute-done | bytes 81952 | tf_op jit(solution)/shard_map/ppermute | solution.py:195
  51.7 0.1 collective-permute-start.17
  51.8 1.3 %collective-permute-done.17.other_t_ref = f32[80,256]{1,0:T(8,128)S(1)} collective-permute-done((f32[80,256]{1,0:T(8,128)S(1)}, f32[80,256]{1,0:T(8,128)S(1)}, u32[]{:S(2)}, u32[]{:S(2)}) %collective-permute-start.17) | collective-permute-done | bytes 81952 | tf_op jit(solution)/shard_map/ppermute | solution.py:195
  53.1 0.0 collective-permute-done.9.other_d_ref
  53.1 1.5 %expand.1 = (f32[256,256]{1,0:T(8,128)}, f32[512,128]{1,0:T(8,128)}) custom-call(s32[4]{0:T(128)S(1)} %copy-done.3, s32[2]{0:T(128)S(1)} %pad_add_fusion.place_ref, f32[288,256]{1,0:T(8,128)S(1)} %pad_maximum_fusion.mine_d_ref, f32[288,256]{1,0:T(8,128)S(1)} %collective-permute-done.9.other_d_ref, f32[80,256]{1,0:T(8,128)S(1)} %add.47.mine_t_ref, ...), custom_call_target="tpu_custom_call" | custom-call | tf_op jit(solution)/shard_map/expand/pallas_call | solution.py:297
  (15 shorter events, 0.2 us)
Async XLA Ops:
  0.6 0.7 %copy-start.3 = (s32[4]{0:T(128)S(1)}, s32[4]{0:T(128)}, u32[]{:S(2)}) copy-start(s32[4]{0:T(128)} %widths_ref.5) | copy-start | bytes 52
  0.6 0.7 %copy-start.4 = (s32[1,4]{1,0:T(1,128)S(1)}, s32[1,4]{1,0:T(1,128)}, u32[]{:S(2)}) copy-start(s32[1,4]{1,0:T(1,128)} %pattern_ref.1) | copy-start | bytes 52
  1.3 0.9 %copy-start.2 = (bf16[1,2,128,512]{3,2,1,0:T(8,128)(2,1)S(1)}, bf16[1,2,128,512]{3,2,1,0:T(8,128)(2,1)}, u32[]{:S(2)}) copy-start(bf16[1,2,128,512]{3,2,1,0:T(8,128)(2,1)} %param.7) | copy-start | bytes 786436
  3.1 9.2 %collective-permute-start.3 = (bf16[640,128]{1,0:T(8,128)(2,1)S(1)}, bf16[640,128]{1,0:T(8,128)(2,1)S(1)}, u32[]{:S(2)}, u32[]{:S(2)}) collective-permute-start(bf16[640,128]{1,0:T(8,128)(2,1)S(1)} %pack.1.refs_0_.refs_4_), channel_id=1, source_target_pairs={{0,1},{1,0},{2,3},{3,2},{4,5},{5,4},{6,7},{7,6},{8,9},{9,8},{10,11... | collective-permute-start | bytes 491528 | tf_op jit(solution)/shard_map/ppermute | solution.py:195
  3.6 9.8 %collective-permute-start.2 = (bf16[640,128]{1,0:T(8,128)(2,1)S(1)}, bf16[640,128]{1,0:T(8,128)(2,1)S(1)}, u32[]{:S(2)}, u32[]{:S(2)}) collective-permute-start(bf16[640,128]{1,0:T(8,128)(2,1)S(1)} %pack.1.refs_0_.refs_4_), channel_id=1, source_target_pairs={{6,0},{0,2},{2,4},{4,6},{7,1},{1,3},{3,5},{5,7},{14,8},{8,10},{10,... | collective-permute-start | bytes 491528 | tf_op jit(solution)/shard_map/ppermute | solution.py:253
  6.3 13.9 %collective-permute-start.1 = (bf16[640,128]{1,0:T(8,128)(2,1)S(1)}, bf16[640,128]{1,0:T(8,128)(2,1)S(1)}, u32[]{:S(2)}, u32[]{:S(2)}) collective-permute-start(bf16[640,128]{1,0:T(8,128)(2,1)S(1)} %pack.1.refs_0_.refs_4_), channel_id=1, source_target_pairs={{4,0},{6,2},{0,4},{2,6},{5,1},{7,3},{1,5},{3,7},{12,8},{14,10},{8,... | collective-permute-start | bytes 491528 | tf_op jit(solution)/shard_map/ppermute | solution.py:253
  8.9 11.4 %collective-permute-start = (bf16[640,128]{1,0:T(8,128)(2,1)S(1)}, bf16[640,128]{1,0:T(8,128)(2,1)S(1)}, u32[]{:S(2)}, u32[]{:S(2)}) collective-permute-start(bf16[640,128]{1,0:T(8,128)(2,1)S(1)} %pack.1.refs_0_.refs_4_), channel_id=1, source_target_pairs={{2,0},{4,2},{6,4},{0,6},{3,1},{5,3},{7,5},{1,7},{10,8},{12,10},{14... | collective-permute-start | bytes 491528 | tf_op jit(solution)/shard_map/ppermute | solution.py:253
  10.3 1.0 %copy-start = (bf16[1,2,256,4,1,128]{5,3,4,2,1,0:T(4,128)(2,1)S(1)}, bf16[1,2,256,4,1,128]{5,3,4,2,1,0:T(4,128)(2,1)}, u32[]{:S(2)}) copy-start(bf16[1,2,256,4,1,128]{5,3,4,2,1,0:T(4,128)(2,1)} %param.6) | copy-start | bytes 1572868
  11.3 8.9 %copy-start.1 = (bf16[1,2,512,128]{3,2,1,0:T(8,128)(2,1)S(1)}, bf16[1,2,512,128]{3,2,1,0:T(8,128)(2,1)}, u32[]{:S(2)}) copy-start(bf16[1,2,512,128]{3,2,1,0:T(8,128)(2,1)} %param.10) | copy-start | bytes 786436
  12.3 7.9 %copy-start.5 = (f32[1,2]{1,0:T(1,128)S(1)}, f32[1,2]{1,0:T(1,128)}, u32[]{:S(2)}) copy-start(f32[1,2]{1,0:T(1,128)} %weights_ref.1) | copy-start | bytes 28
  22.9 1.6 %collective-permute-start.4 = (f32[160,256]{1,0:T(8,128)S(1)}, f32[160,256]{1,0:T(8,128)S(1)}, u32[]{:S(2)}, u32[]{:S(2)}) collective-permute-start(f32[160,256]{1,0:T(8,128)S(1)} %get-tuple-element.8), channel_id=1, source_target_pairs={{0,1},{1,0},{2,3},{3,2},{4,5},{5,4},{6,7},{7,6},{8,9},{9,8},{10,11... | collective-permute-start | bytes 491528 | tf_op jit(solution)/shard_map/ppermute | solution.py:195
  23.0 1.5 %collective-permute-start.10 = (f32[160,128]{1,0:T(8,128)S(1)}, f32[160,128]{1,0:T(8,128)S(1)}, u32[]{:S(2)}, u32[]{:S(2)}) collective-permute-start(f32[160,128]{1,0:T(8,128)S(1)} %get-tuple-element.11), channel_id=1, source_target_pairs={{0,1},{1,0},{2,3},{3,2},{4,5},{5,4},{6,7},{7,6},{8,9},{9,8},{10,11... | collective-permute-start | bytes 245768 | tf_op jit(solution)/shard_map/ppermute | solution.py:195
  24.5 6.5 %collective-permute-start.5 = (f32[144,256]{1,0:T(8,128)S(1)}, f32[144,256]{1,0:T(8,128)S(1)}, u32[]{:S(2)}, u32[]{:S(2)}) collective-permute-start(f32[144,256]{1,0:T(8,128)S(1)} %slice.16), channel_id=1, source_target_pairs={{0,8},{8,0},{16,24},{24,16},{1,9},{9,1},{17,25},{25,17},{2,10},{10... | collective-permute-start | bytes 442376 | tf_op jit(solution)/shard_map/ppermute | solution.py:195
  26.1 6.6 %collective-permute-start.11 = (f32[80,128]{1,0:T(8,128)S(1)}, f32[80,128]{1,0:T(8,128)S(1)}, u32[]{:S(2)}, u32[]{:S(2)}) collective-permute-start(f32[80,128]{1,0:T(8,128)S(1)} %get-tuple-element.16), channel_id=1, source_target_pairs={{0,8},{8,0},{16,24},{24,16},{1,9},{9,1},{17,25},{25,17},{2,10},{10... | collective-permute-start | bytes 122888 | tf_op jit(solution)/shard_map/ppermute | solution.py:195
  26.6 6.0 %collective-permute-start.13 = (f32[80,128]{1,0:T(8,128)S(1)}, f32[80,128]{1,0:T(8,128)S(1)}, u32[]{:S(2)}, u32[]{:S(2)}) collective-permute-start(f32[80,128]{1,0:T(8,128)S(1)} %get-tuple-element.17), channel_id=1, source_target_pairs={{0,16},{8,24},{16,0},{24,8},{1,17},{9,25},{17,1},{25,9},{2,18},{10... | collective-permute-start | bytes 122888 | tf_op jit(solution)/shard_map/ppermute | solution.py:195
  31.1 5.5 %collective-permute-start.7 = (f32[144,256]{1,0:T(8,128)S(1)}, f32[144,256]{1,0:T(8,128)S(1)}, u32[]{:S(2)}, u32[]{:S(2)}) collective-permute-start(f32[144,256]{1,0:T(8,128)S(1)} %get-tuple-element.13), channel_id=1, source_target_pairs={{0,16},{8,24},{16,0},{24,8},{1,17},{9,25},{17,1},{25,9},{2,18},{10... | collective-permute-start | bytes 442376 | tf_op jit(solution)/shard_map/ppermute | solution.py:195
  32.7 6.5 %collective-permute-start.12 = (f32[80,128]{1,0:T(8,128)S(1)}, f32[80,128]{1,0:T(8,128)S(1)}, u32[]{:S(2)}, u32[]{:S(2)}) collective-permute-start(f32[80,128]{1,0:T(8,128)S(1)} %get-tuple-element.14), channel_id=1, source_target_pairs={{0,16},{8,24},{16,0},{24,8},{1,17},{9,25},{17,1},{25,9},{2,18},{10... | collective-permute-start | bytes 122888 | tf_op jit(solution)/shard_map/ppermute | solution.py:195
  33.3 5.9 %collective-permute-start.14 = (f32[80,128]{1,0:T(8,128)S(1)}, f32[80,128]{1,0:T(8,128)S(1)}, u32[]{:S(2)}, u32[]{:S(2)}) collective-permute-start(f32[80,128]{1,0:T(8,128)S(1)} %get-tuple-element.15), channel_id=1, source_target_pairs={{0,8},{8,0},{16,24},{24,16},{1,9},{9,1},{17,25},{25,17},{2,10},{10... | collective-permute-start | bytes 122888 | tf_op jit(solution)/shard_map/ppermute | solution.py:195
  34.8 8.5 %collective-permute-start.6 = (f32[144,256]{1,0:T(8,128)S(1)}, f32[144,256]{1,0:T(8,128)S(1)}, u32[]{:S(2)}, u32[]{:S(2)}) collective-permute-start(f32[144,256]{1,0:T(8,128)S(1)} %get-tuple-element.12), channel_id=1, source_target_pairs={{0,16},{8,24},{16,0},{24,8},{1,17},{9,25},{17,1},{25,9},{2,18},{10... | collective-permute-start | bytes 442376 | tf_op jit(solution)/shard_map/ppermute | solution.py:195
  36.7 6.7 %collective-permute-start.8 = (f32[144,256]{1,0:T(8,128)S(1)}, f32[144,256]{1,0:T(8,128)S(1)}, u32[]{:S(2)}, u32[]{:S(2)}) collective-permute-start(f32[144,256]{1,0:T(8,128)S(1)} %add.39), channel_id=1, source_target_pairs={{0,8},{8,0},{16,24},{24,16},{1,9},{9,1},{17,25},{25,17},{2,10},{10... | collective-permute-start | bytes 442376 | tf_op jit(solution)/shard_map/ppermute | solution.py:195
  39.2 6.5 %collective-permute-start.15 = (f32[80,256]{1,0:T(8,128)S(1)}, f32[80,256]{1,0:T(8,128)S(1)}, u32[]{:S(2)}, u32[]{:S(2)}) collective-permute-start(f32[80,256]{1,0:T(8,128)S(1)} %pad_maximum_fusion.2), channel_id=1, source_target_pairs={{0,2},{2,0},{4,6},{6,4},{1,3},{3,1},{5,7},{7,5},{8,10},{10,8},{12,... | collective-permute-start | bytes 245768 | tf_op jit(solution)/shard_map/ppermute | solution.py:195
  43.4 9.7 %collective-permute-start.9 = (f32[288,256]{1,0:T(8,128)S(1)}, f32[288,256]{1,0:T(8,128)S(1)}, u32[]{:S(2)}, u32[]{:S(2)}) collective-permute-start(f32[288,256]{1,0:T(8,128)S(1)} %pad_maximum_fusion.mine_d_ref), channel_id=1, source_target_pairs={{0,1},{1,0},{2,3},{3,2},{4,5},{5,4},{6,7},{7,6},{8,9},{9,8},{10,11... | collective-permute-start | bytes 884744 | tf_op jit(solution)/shard_map/ppermute | solution.py:195
  45.7 6.0 %collective-permute-start.16 = (f32[80,256]{1,0:T(8,128)S(1)}, f32[80,256]{1,0:T(8,128)S(1)}, u32[]{:S(2)}, u32[]{:S(2)}) collective-permute-start(f32[80,256]{1,0:T(8,128)S(1)} %fusion), channel_id=1, source_target_pairs={{0,4},{2,6},{4,0},{6,2},{1,5},{3,7},{5,1},{7,3},{8,12},{10,14},{12... | collective-permute-start | bytes 245768 | tf_op jit(solution)/shard_map/ppermute | solution.py:195
  51.7 1.3 %collective-permute-start.17 = (f32[80,256]{1,0:T(8,128)S(1)}, f32[80,256]{1,0:T(8,128)S(1)}, u32[]{:S(2)}, u32[]{:S(2)}) collective-permute-start(f32[80,256]{1,0:T(8,128)S(1)} %add.47.mine_t_ref), channel_id=1, source_target_pairs={{0,1},{1,0},{2,3},{3,2},{4,5},{5,4},{6,7},{7,6},{8,9},{9,8},{10,11... | collective-permute-start | bytes 245768 | tf_op jit(solution)/shard_map/ppermute | solution.py:195

commit v4 on v3

--- a/solution.py
+++ b/solution.py
@@ -195,13 +195,9 @@
     return lax.ppermute(value, axis, [(i, i ^ bit) for i in range(lax.axis_size(axis))])
 
 
-def pole_sum(value):
-    bits = bits_of(lax.axis_size("pole"))
+def halves_of(value):
     half = value.shape[0] // 2
-    first, second = value[:half], value[half:]
-    for bit, mirrored in zip(bits, bits[::-1]):
-        first, second = first + swap(first, "pole", bit), second + swap(second, "pole", mirrored)
-    return first, second
+    return value[:half], value[half:]
 
 
 def scatter_rest(value, axis):
@@ -285,12 +281,29 @@
         *[blocks[shift] for shift in range(row_count)], *own,
     )
 
-    products = scatter_rest(keep_t + swap(send_t, "col", top), "col")
+    tie = lax.optimization_barrier
+    products = keep_t + swap(send_t, "col", top)
+    products, send_d = tie((scatter_rest(products, "col"), send_d))
+    first, second = halves_of(products)
+    bits = bits_of(lax.axis_size("pole"))
+    for bit, mirrored in zip(bits, bits[::-1]):
+        first, second = tie((
+            first + swap(first, "pole", bit), second + swap(second, "pole", mirrored)
+        ))
+    products = jnp.concatenate([first, second], axis=1)
     density = scatter_rest(keep_d + swap(send_d, "col", top), "col")
-    products = jnp.concatenate(pole_sum(products), axis=1)
-    for bit in bits_of(row_count):
-        products = products + swap(products, "row", bit)
-    density = jnp.concatenate(pole_sum(jnp.concatenate([density, term], axis=0)), axis=0)
+    low, high = halves_of(jnp.concatenate([density, term], axis=0))
+    products, low, high = tie((products, low, high))
+    row_bits = bits_of(row_count)
+    for step in range(max(len(bits), len(row_bits))):
+        if step < len(row_bits):
+            products = products + swap(products, "row", row_bits[step])
+        if step < len(bits):
+            low, high = (
+                low + swap(low, "pole", bits[step]), high + swap(high, "pole", bits[-1 - step])
+            )
+        products, low, high = tie((products, low, high))
+    density = jnp.concatenate([low, high], axis=0)
     density = gather_but_last(density, "col")
     products = gather_but_last(products, "col")
 

time: 54.7 us -> 55 us (level); the launches traced: 54.5 us -> 53.9 us
  starting transfers between devices: 24.9 us -> 23.2 us
  waiting for transfers between devices: 19.9 us -> 21 us
    ppermute x15, starting transfers between devices: 18.3 us -> 16.6 us  [swap(): lax.ppermute(value, axis, [(i, i ^ bit) for i in range(lax.axis_size(axis...]
    ppermute x15, waiting for transfers between devices: 12.1 us -> 13.1 us  [swap(): lax.ppermute(value, axis, [(i, i ^ bit) for i in range(lax.axis_size(axis...]
    unnamed x12 -> x13, local copies, waits for them, and re-layouts: 2.66 us -> 2.67 us
  transfers between devices with their start and end apart: 18 -> 18, of which waited for: 8 -> 10; matrix products, arithmetic and copies ran while one was open for 0% -> 0% of each run, Pallas kernels for 2% -> 2%
where the time goes in v4:
time: 55 us; the launch traced here: 53.9 us
  starting transfers between devices  23.2 us (42%)
  waiting for transfers between devices  21 us (38%)
  Pallas kernels  5.98 us (11%)
  local copies, waits for them, and re-layouts  2.69 us (5%)
  between operations  0.84 us (2%)
    ppermute x15, starting transfers between devices, swap(): lax.ppermute(value, axis, [(i, i ^ bit) for i in range(lax.axis_size(axis...  16.6 us
    ppermute x15, waiting for transfers between devices, swap(): lax.ppermute(value, axis, [(i, i ^ bit) for i in range(lax.axis_size(axis...  13.1 us
    ppermute x3, waiting for transfers between devices, per_device(): blocks[shift] = lax.ppermute(packed, 'row', pairs)  7.87 us
    ppermute x3, starting transfers between devices, per_device(): blocks[shift] = lax.ppermute(packed, 'row', pairs)  6.57 us
    unnamed x13, local copies, waits for them, and re-layouts  2.67 us
    pallas_call x1, Pallas kernels, per_device(): pl.pallas_call(functools.partial(compute_kernel, (row_count, col_count),...  2.66 us
    pallas_call x1, Pallas kernels, per_device(): pl.pallas_call(functools.partial(expand_kernel, col_count, slot), in_spec...  1.47 us
  transfers between devices with their start and end apart: 18, of which 10 were waited for; matrix products, arithmetic and copies ran while one was open for 0% of the time, Pallas kernels for 2%

profile of v4, /device:TPU:0, one launch (start us, length us, event | category | flops | bytes accessed | tf_op | source)
XLA Modules:
  0.0 53.9 jit_solution(13061023253218960581)
XLA Ops:
  0.6 0.0 copy-start.3
  0.6 0.0 copy-start.4
  0.7 0.6 %copy-done.3 = s32[4]{0:T(128)S(1)} copy-done((s32[4]{0:T(128)S(1)}, s32[4]{0:T(128)}, u32[]{:S(2)}) %copy-start.3) | copy-done | bytes 40
  1.3 0.0 copy-done.4
  1.3 0.0 copy-start.2
  1.3 0.9 %copy-done.2 = bf16[1,2,128,512]{3,2,1,0:T(8,128)(2,1)S(1)} copy-done((bf16[1,2,128,512]{3,2,1,0:T(8,128)(2,1)S(1)}, bf16[1,2,128,512]{3,2,1,0:T(8,128)(2,1)}, u32[]{:S(2)}) %copy-start.2) | copy-done | bytes 262168
  2.3 0.9 %pack.1.refs_0_.refs_4_ = bf16[640,128]{1,0:T(8,128)(2,1)S(1)} custom-call(s32[1,4]{1,0:T(1,128)S(1)} %copy-done.4, s32[4]{0:T(128)S(1)} %copy-done.3, bf16[2,128,512]{2,1,0:T(8,128)(2,1)S(1)} %bitcast.7), custom_call_target="tpu_custom_call" | custom-call | tf_op jit(solution)/shard_map/pack/pallas_call | solution.py:237
  3.1 0.5 collective-permute-start.3
  3.6 2.6 %collective-permute-start.2 = (bf16[640,128]{1,0:T(8,128)(2,1)S(1)}, bf16[640,128]{1,0:T(8,128)(2,1)S(1)}, u32[]{:S(2)}, u32[]{:S(2)}) collective-permute-start(bf16[640,128]{1,0:T(8,128)(2,1)S(1)} %pack.1.refs_0_.refs_4_), channel_id=1, source_target_pairs={{6,0},{0,2},{2,4},{4,6},{7,1},{1,3},{3,5},{5,7},{14,8},{8,10},{10,... | collective-permute-start | bytes 491528 | tf_op jit(solution)/shard_map/ppermute | solution.py:249
  6.3 2.6 %collective-permute-start.1 = (bf16[640,128]{1,0:T(8,128)(2,1)S(1)}, bf16[640,128]{1,0:T(8,128)(2,1)S(1)}, u32[]{:S(2)}, u32[]{:S(2)}) collective-permute-start(bf16[640,128]{1,0:T(8,128)(2,1)S(1)} %pack.1.refs_0_.refs_4_), channel_id=1, source_target_pairs={{4,0},{6,2},{0,4},{2,6},{5,1},{7,3},{1,5},{3,7},{12,8},{14,10},{8,... | collective-permute-start | bytes 491528 | tf_op jit(solution)/shard_map/ppermute | solution.py:249
  8.9 1.4 %collective-permute-start = (bf16[640,128]{1,0:T(8,128)(2,1)S(1)}, bf16[640,128]{1,0:T(8,128)(2,1)S(1)}, u32[]{:S(2)}, u32[]{:S(2)}) collective-permute-start(bf16[640,128]{1,0:T(8,128)(2,1)S(1)} %pack.1.refs_0_.refs_4_), channel_id=1, source_target_pairs={{2,0},{4,2},{6,4},{0,6},{3,1},{5,3},{7,5},{1,7},{10,8},{12,10},{14... | collective-permute-start | bytes 491528 | tf_op jit(solution)/shard_map/ppermute | solution.py:249
  10.2 0.1 pad_add_fusion.place_ref
  10.3 0.0 copy-start
  10.3 1.0 %copy-done = bf16[1,2,256,4,1,128]{5,3,4,2,1,0:T(4,128)(2,1)S(1)} copy-done((bf16[1,2,256,4,1,128]{5,3,4,2,1,0:T(4,128)(2,1)S(1)}, bf16[1,2,256,4,1,128]{5,3,4,2,1,0:T(4,128)(2,1)}, u32[]{:S(2)}) %copy-start) | copy-done | bytes 524312
  11.3 0.0 copy-start.1
  11.3 1.0 %prepare.1.straight_ref = bf16[2,256,512]{2,1,0:T(8,128)(2,1)S(1)} custom-call(s32[2]{0:T(128)S(1)} %pad_add_fusion.place_ref, bf16[2048,128]{1,0:T(8,128)(2,1)S(1)} %bitcast.5), custom_call_target="tpu_custom_call" | custom-call | flops 134217728 | bytes 1048576 | tf_op jit(solution)/shard_map/prepare/pallas_call | solution.py:252
  12.3 0.0 copy-start.5
  12.3 0.0 collective-permute-done.3.refs_5_
  12.4 1.1 %collective-permute-done.2.refs_3_ = bf16[640,128]{1,0:T(8,128)(2,1)S(1)} collective-permute-done((bf16[640,128]{1,0:T(8,128)(2,1)S(1)}, bf16[640,128]{1,0:T(8,128)(2,1)S(1)}, u32[]{:S(2)}, u32[]{:S(2)}) %collective-permute-start.2) | collective-permute-done | bytes 163872 | tf_op jit(solution)/shard_map/ppermute | solution.py:249
  13.5 6.7 %collective-permute-done.1.refs_2_ = bf16[640,128]{1,0:T(8,128)(2,1)S(1)} collective-permute-done((bf16[640,128]{1,0:T(8,128)(2,1)S(1)}, bf16[640,128]{1,0:T(8,128)(2,1)S(1)}, u32[]{:S(2)}, u32[]{:S(2)}) %collective-permute-start.1) | collective-permute-done | bytes 163872 | tf_op jit(solution)/shard_map/ppermute | solution.py:249
  20.2 0.0 collective-permute-done.refs_1_
  20.2 0.0 copy-done.1
  20.2 0.0 copy-done.5
  20.2 2.7 %compute.1 = (f32[160,256]{1,0:T(8,128)S(1)}, f32[160,256]{1,0:T(8,128)S(1)}, f32[160,128]{1,0:T(8,128)S(1)}, f32[160,128]{1,0:T(8,128)S(1)}, f32[128,256]{1,0:T(8,128)S(1)}) custom-call(s32[4]{0:T(128)S(1)} %copy-done.3, f32[1,2]{1,0:T(1,128)S(1)} %copy-done.5, s32[2]{0:T(128)S(1)} %pad_add_fusion.place_ref, bf16[2,256,512]{2,1,0:T(8,128)(2,1)S(1)} %prepare.1.straight_ref, ...), custom_call_target="tpu_custom_call" | custom-call | tf_op jit(solution)/shard_map/compute/pallas_call | solution.py:266
  22.9 0.1 collective-permute-start.4
  23.0 1.3 %collective-permute-done.4 = f32[160,128]{1,0:T(8,128)S(1)} collective-permute-done((f32[160,128]{1,0:T(8,128)S(1)}, f32[160,128]{1,0:T(8,128)S(1)}, u32[]{:S(2)}, u32[]{:S(2)}) %collective-permute-start.4) | collective-permute-done | bytes 81952 | tf_op jit(solution)/shard_map/ppermute | solution.py:195
  24.3 1.6 %collective-permute-start.6 = (f32[80,128]{1,0:T(8,128)S(1)}, f32[80,128]{1,0:T(8,128)S(1)}, u32[]{:S(2)}, u32[]{:S(2)}) collective-permute-start(f32[80,128]{1,0:T(8,128)S(1)} %get-tuple-element.46), channel_id=1, source_target_pairs={{0,16},{8,24},{16,0},{24,8},{1,17},{9,25},{17,1},{25,9},{2,18},{10... | collective-permute-start | bytes 122888 | tf_op jit(solution)/shard_map/ppermute | solution.py:195
  25.8 1.5 %collective-permute-start.5 = (f32[80,128]{1,0:T(8,128)S(1)}, f32[80,128]{1,0:T(8,128)S(1)}, u32[]{:S(2)}, u32[]{:S(2)}) collective-permute-start(f32[80,128]{1,0:T(8,128)S(1)} %get-tuple-element.47), channel_id=1, source_target_pairs={{0,8},{8,0},{16,24},{24,16},{1,9},{9,1},{17,25},{25,17},{2,10},{10... | collective-permute-start | bytes 122888 | tf_op jit(solution)/shard_map/ppermute | solution.py:195
  27.3 0.0 collective-permute-start.9
  27.3 1.0 %collective-permute-done.6 = f32[80,128]{1,0:T(8,128)S(1)} collective-permute-done((f32[80,128]{1,0:T(8,128)S(1)}, f32[80,128]{1,0:T(8,128)S(1)}, u32[]{:S(2)}, u32[]{:S(2)}) %collective-permute-start.6) | collective-permute-done | bytes 40992 | tf_op jit(solution)/shard_map/ppermute | solution.py:195
  28.3 1.5 %collective-permute-done.5 = f32[80,128]{1,0:T(8,128)S(1)} collective-permute-done((f32[80,128]{1,0:T(8,128)S(1)}, f32[80,128]{1,0:T(8,128)S(1)}, u32[]{:S(2)}, u32[]{:S(2)}) %collective-permute-start.5) | collective-permute-done | bytes 40992 | tf_op jit(solution)/shard_map/ppermute | solution.py:195
  29.9 0.6 %collective-permute-start.7 = (f32[80,128]{1,0:T(8,128)S(1)}, f32[80,128]{1,0:T(8,128)S(1)}, u32[]{:S(2)}, u32[]{:S(2)}) collective-permute-start(f32[80,128]{1,0:T(8,128)S(1)} %get-tuple-element.26), channel_id=1, source_target_pairs={{0,16},{8,24},{16,0},{24,8},{1,17},{9,25},{17,1},{25,9},{2,18},{10... | collective-permute-start | bytes 122888 | tf_op jit(solution)/shard_map/ppermute | solution.py:195
  30.4 1.5 %collective-permute-start.8 = (f32[80,128]{1,0:T(8,128)S(1)}, f32[80,128]{1,0:T(8,128)S(1)}, u32[]{:S(2)}, u32[]{:S(2)}) collective-permute-start(f32[80,128]{1,0:T(8,128)S(1)} %get-tuple-element.27), channel_id=1, source_target_pairs={{0,8},{8,0},{16,24},{24,16},{1,9},{9,1},{17,25},{25,17},{2,10},{10... | collective-permute-start | bytes 122888 | tf_op jit(solution)/shard_map/ppermute | solution.py:195
  31.9 2.0 %collective-permute-done.7 = f32[80,128]{1,0:T(8,128)S(1)} collective-permute-done((f32[80,128]{1,0:T(8,128)S(1)}, f32[80,128]{1,0:T(8,128)S(1)}, u32[]{:S(2)}, u32[]{:S(2)}) %collective-permute-start.7) | collective-permute-done | bytes 40992 | tf_op jit(solution)/shard_map/ppermute | solution.py:195
  33.9 0.5 collective-permute-done.8
  34.5 0.0 collective-permute-done.9
  34.5 1.5 %collective-permute-start.11 = (f32[144,256]{1,0:T(8,128)S(1)}, f32[144,256]{1,0:T(8,128)S(1)}, u32[]{:S(2)}, u32[]{:S(2)}) collective-permute-start(f32[144,256]{1,0:T(8,128)S(1)} %get-tuple-element.34), channel_id=1, source_target_pairs={{0,8},{8,0},{16,24},{24,16},{1,9},{9,1},{17,25},{25,17},{2,10},{10... | collective-permute-start | bytes 442376 | tf_op jit(solution)/shard_map/ppermute | solution.py:195
  36.1 1.5 %collective-permute-start.12 = (f32[144,256]{1,0:T(8,128)S(1)}, f32[144,256]{1,0:T(8,128)S(1)}, u32[]{:S(2)}, u32[]{:S(2)}) collective-permute-start(f32[144,256]{1,0:T(8,128)S(1)} %get-tuple-element.35), channel_id=1, source_target_pairs={{0,16},{8,24},{16,0},{24,8},{1,17},{9,25},{17,1},{25,9},{2,18},{10... | collective-permute-start | bytes 442376 | tf_op jit(solution)/shard_map/ppermute | solution.py:195
  37.6 4.0 %collective-permute-start.10 = (f32[80,256]{1,0:T(8,128)S(1)}, f32[80,256]{1,0:T(8,128)S(1)}, u32[]{:S(2)}, u32[]{:S(2)}) collective-permute-start(f32[80,256]{1,0:T(8,128)S(1)} %pad_maximum_fusion.1), channel_id=1, source_target_pairs={{0,2},{2,0},{4,6},{6,4},{1,3},{3,1},{5,7},{7,5},{8,10},{10,8},{12,... | collective-permute-start | bytes 245768 | tf_op jit(solution)/shard_map/ppermute | solution.py:195
  41.6 2.4 %collective-permute-done.10 = f32[80,256]{1,0:T(8,128)S(1)} collective-permute-done((f32[80,256]{1,0:T(8,128)S(1)}, f32[80,256]{1,0:T(8,128)S(1)}, u32[]{:S(2)}, u32[]{:S(2)}) %collective-permute-start.10) | collective-permute-done | bytes 81952 | tf_op jit(solution)/shard_map/ppermute | solution.py:195
  44.0 0.0 collective-permute-done.11
  44.1 0.0 collective-permute-done.12
  44.1 0.6 %collective-permute-start.14 = (f32[144,256]{1,0:T(8,128)S(1)}, f32[144,256]{1,0:T(8,128)S(1)}, u32[]{:S(2)}, u32[]{:S(2)}) collective-permute-start(f32[144,256]{1,0:T(8,128)S(1)} %add.43), channel_id=1, source_target_pairs={{0,16},{8,24},{16,0},{24,8},{1,17},{9,25},{17,1},{25,9},{2,18},{10... | collective-permute-start | bytes 442376 | tf_op jit(solution)/shard_map/ppermute | solution.py:195
  44.7 0.6 %collective-permute-start.15 = (f32[144,256]{1,0:T(8,128)S(1)}, f32[144,256]{1,0:T(8,128)S(1)}, u32[]{:S(2)}, u32[]{:S(2)}) collective-permute-start(f32[144,256]{1,0:T(8,128)S(1)} %add.44), channel_id=1, source_target_pairs={{0,8},{8,0},{16,24},{24,16},{1,9},{9,1},{17,25},{25,17},{2,10},{10... | collective-permute-start | bytes 442376 | tf_op jit(solution)/shard_map/ppermute | solution.py:195
  45.2 2.1 %collective-permute-start.13 = (f32[80,256]{1,0:T(8,128)S(1)}, f32[80,256]{1,0:T(8,128)S(1)}, u32[]{:S(2)}, u32[]{:S(2)}) collective-permute-start(f32[80,256]{1,0:T(8,128)S(1)} %add.42), channel_id=1, source_target_pairs={{0,4},{2,6},{4,0},{6,2},{1,5},{3,7},{5,1},{7,3},{8,12},{10,14},{12... | collective-permute-start | bytes 245768 | tf_op jit(solution)/shard_map/ppermute | solution.py:195
  47.4 3.2 %collective-permute-done.13 = f32[80,256]{1,0:T(8,128)S(1)} collective-permute-done((f32[80,256]{1,0:T(8,128)S(1)}, f32[80,256]{1,0:T(8,128)S(1)}, u32[]{:S(2)}, u32[]{:S(2)}) %collective-permute-start.13) | collective-permute-done | bytes 81952 | tf_op jit(solution)/shard_map/ppermute | solution.py:195
  50.6 0.0 collective-permute-done.14
  50.6 0.0 collective-permute-done.15
  50.7 0.1 collective-permute-start.16
  50.8 0.5 collective-permute-start.17
  51.3 1.2 %collective-permute-done.17.other_t_ref = f32[80,256]{1,0:T(8,128)S(1)} collective-permute-done((f32[80,256]{1,0:T(8,128)S(1)}, f32[80,256]{1,0:T(8,128)S(1)}, u32[]{:S(2)}, u32[]{:S(2)}) %collective-permute-start.17) | collective-permute-done | bytes 81952 | tf_op jit(solution)/shard_map/ppermute | solution.py:195
  52.5 0.0 collective-permute-done.16.other_d_ref
  52.5 1.5 %expand.1 = (f32[256,256]{1,0:T(8,128)}, f32[512,128]{1,0:T(8,128)}) custom-call(s32[4]{0:T(128)S(1)} %copy-done.3, s32[2]{0:T(128)S(1)} %pad_add_fusion.place_ref, f32[288,256]{1,0:T(8,128)S(1)} %constant_dynamic-update-slice_fusion.mine_d_ref, f32[288,256]{1,0:T(8,128)S(1)} %collective-permute-done.16.other_d_ref, f32[80,256]{1,0:T(8,128)S(1)} %add.45.mine_t_ref, ...), custom_call_target="tpu_custom_call" | custom-call | tf_op jit(solution)/shard_map/expand/pallas_call | solution.py:310
  (16 shorter events, 0.2 us)
Async XLA Ops:
  0.6 0.7 %copy-start.3 = (s32[4]{0:T(128)S(1)}, s32[4]{0:T(128)}, u32[]{:S(2)}) copy-start(s32[4]{0:T(128)} %widths_ref.5) | copy-start | bytes 52
  0.6 0.7 %copy-start.4 = (s32[1,4]{1,0:T(1,128)S(1)}, s32[1,4]{1,0:T(1,128)}, u32[]{:S(2)}) copy-start(s32[1,4]{1,0:T(1,128)} %pattern_ref.1) | copy-start | bytes 52
  1.3 0.9 %copy-start.2 = (bf16[1,2,128,512]{3,2,1,0:T(8,128)(2,1)S(1)}, bf16[1,2,128,512]{3,2,1,0:T(8,128)(2,1)}, u32[]{:S(2)}) copy-start(bf16[1,2,128,512]{3,2,1,0:T(8,128)(2,1)} %param.7) | copy-start | bytes 786436
  3.1 9.2 %collective-permute-start.3 = (bf16[640,128]{1,0:T(8,128)(2,1)S(1)}, bf16[640,128]{1,0:T(8,128)(2,1)S(1)}, u32[]{:S(2)}, u32[]{:S(2)}) collective-permute-start(bf16[640,128]{1,0:T(8,128)(2,1)S(1)} %pack.1.refs_0_.refs_4_), channel_id=1, source_target_pairs={{0,1},{1,0},{2,3},{3,2},{4,5},{5,4},{6,7},{7,6},{8,9},{9,8},{10,11... | collective-permute-start | bytes 491528 | tf_op jit(solution)/shard_map/ppermute | solution.py:195
  3.6 9.8 %collective-permute-start.2 = (bf16[640,128]{1,0:T(8,128)(2,1)S(1)}, bf16[640,128]{1,0:T(8,128)(2,1)S(1)}, u32[]{:S(2)}, u32[]{:S(2)}) collective-permute-start(bf16[640,128]{1,0:T(8,128)(2,1)S(1)} %pack.1.refs_0_.refs_4_), channel_id=1, source_target_pairs={{6,0},{0,2},{2,4},{4,6},{7,1},{1,3},{3,5},{5,7},{14,8},{8,10},{10,... | collective-permute-start | bytes 491528 | tf_op jit(solution)/shard_map/ppermute | solution.py:249
  6.3 13.9 %collective-permute-start.1 = (bf16[640,128]{1,0:T(8,128)(2,1)S(1)}, bf16[640,128]{1,0:T(8,128)(2,1)S(1)}, u32[]{:S(2)}, u32[]{:S(2)}) collective-permute-start(bf16[640,128]{1,0:T(8,128)(2,1)S(1)} %pack.1.refs_0_.refs_4_), channel_id=1, source_target_pairs={{4,0},{6,2},{0,4},{2,6},{5,1},{7,3},{1,5},{3,7},{12,8},{14,10},{8,... | collective-permute-start | bytes 491528 | tf_op jit(solution)/shard_map/ppermute | solution.py:249
  8.9 11.4 %collective-permute-start = (bf16[640,128]{1,0:T(8,128)(2,1)S(1)}, bf16[640,128]{1,0:T(8,128)(2,1)S(1)}, u32[]{:S(2)}, u32[]{:S(2)}) collective-permute-start(bf16[640,128]{1,0:T(8,128)(2,1)S(1)} %pack.1.refs_0_.refs_4_), channel_id=1, source_target_pairs={{2,0},{4,2},{6,4},{0,6},{3,1},{5,3},{7,5},{1,7},{10,8},{12,10},{14... | collective-permute-start | bytes 491528 | tf_op jit(solution)/shard_map/ppermute | solution.py:249
  10.3 1.0 %copy-start = (bf16[1,2,256,4,1,128]{5,3,4,2,1,0:T(4,128)(2,1)S(1)}, bf16[1,2,256,4,1,128]{5,3,4,2,1,0:T(4,128)(2,1)}, u32[]{:S(2)}) copy-start(bf16[1,2,256,4,1,128]{5,3,4,2,1,0:T(4,128)(2,1)} %param.6) | copy-start | bytes 1572868
  11.3 8.9 %copy-start.1 = (bf16[1,2,512,128]{3,2,1,0:T(8,128)(2,1)S(1)}, bf16[1,2,512,128]{3,2,1,0:T(8,128)(2,1)}, u32[]{:S(2)}) copy-start(bf16[1,2,512,128]{3,2,1,0:T(8,128)(2,1)} %param.10) | copy-start | bytes 786436
  12.3 7.9 %copy-start.5 = (f32[1,2]{1,0:T(1,128)S(1)}, f32[1,2]{1,0:T(1,128)}, u32[]{:S(2)}) copy-start(f32[1,2]{1,0:T(1,128)} %weights_ref.1) | copy-start | bytes 28
  22.9 1.3 %collective-permute-start.4 = (f32[160,128]{1,0:T(8,128)S(1)}, f32[160,128]{1,0:T(8,128)S(1)}, u32[]{:S(2)}, u32[]{:S(2)}) collective-permute-start(f32[160,128]{1,0:T(8,128)S(1)} %get-tuple-element.23), channel_id=1, source_target_pairs={{0,1},{1,0},{2,3},{3,2},{4,5},{5,4},{6,7},{7,6},{8,9},{9,8},{10,11... | collective-permute-start | bytes 245768 | tf_op jit(solution)/shard_map/ppermute | solution.py:195
  24.3 4.1 %collective-permute-start.6 = (f32[80,128]{1,0:T(8,128)S(1)}, f32[80,128]{1,0:T(8,128)S(1)}, u32[]{:S(2)}, u32[]{:S(2)}) collective-permute-start(f32[80,128]{1,0:T(8,128)S(1)} %get-tuple-element.46), channel_id=1, source_target_pairs={{0,16},{8,24},{16,0},{24,8},{1,17},{9,25},{17,1},{25,9},{2,18},{10... | collective-permute-start | bytes 122888 | tf_op jit(solution)/shard_map/ppermute | solution.py:195
  25.8 4.0 %collective-permute-start.5 = (f32[80,128]{1,0:T(8,128)S(1)}, f32[80,128]{1,0:T(8,128)S(1)}, u32[]{:S(2)}, u32[]{:S(2)}) collective-permute-start(f32[80,128]{1,0:T(8,128)S(1)} %get-tuple-element.47), channel_id=1, source_target_pairs={{0,8},{8,0},{16,24},{24,16},{1,9},{9,1},{17,25},{25,17},{2,10},{10... | collective-permute-start | bytes 122888 | tf_op jit(solution)/shard_map/ppermute | solution.py:195
  27.3 7.1 %collective-permute-start.9 = (f32[160,256]{1,0:T(8,128)S(1)}, f32[160,256]{1,0:T(8,128)S(1)}, u32[]{:S(2)}, u32[]{:S(2)}) collective-permute-start(f32[160,256]{1,0:T(8,128)S(1)} %get-tuple-element.31), channel_id=1, source_target_pairs={{0,1},{1,0},{2,3},{3,2},{4,5},{5,4},{6,7},{7,6},{8,9},{9,8},{10,11... | collective-permute-start | bytes 491528 | tf_op jit(solution)/shard_map/ppermute | solution.py:195
  29.9 4.1 %collective-permute-start.7 = (f32[80,128]{1,0:T(8,128)S(1)}, f32[80,128]{1,0:T(8,128)S(1)}, u32[]{:S(2)}, u32[]{:S(2)}) collective-permute-start(f32[80,128]{1,0:T(8,128)S(1)} %get-tuple-element.26), channel_id=1, source_target_pairs={{0,16},{8,24},{16,0},{24,8},{1,17},{9,25},{17,1},{25,9},{2,18},{10... | collective-permute-start | bytes 122888 | tf_op jit(solution)/shard_map/ppermute | solution.py:195
  30.4 4.0 %collective-permute-start.8 = (f32[80,128]{1,0:T(8,128)S(1)}, f32[80,128]{1,0:T(8,128)S(1)}, u32[]{:S(2)}, u32[]{:S(2)}) collective-permute-start(f32[80,128]{1,0:T(8,128)S(1)} %get-tuple-element.27), channel_id=1, source_target_pairs={{0,8},{8,0},{16,24},{24,16},{1,9},{9,1},{17,25},{25,17},{2,10},{10... | collective-permute-start | bytes 122888 | tf_op jit(solution)/shard_map/ppermute | solution.py:195
  34.5 9.5 %collective-permute-start.11 = (f32[144,256]{1,0:T(8,128)S(1)}, f32[144,256]{1,0:T(8,128)S(1)}, u32[]{:S(2)}, u32[]{:S(2)}) collective-permute-start(f32[144,256]{1,0:T(8,128)S(1)} %get-tuple-element.34), channel_id=1, source_target_pairs={{0,8},{8,0},{16,24},{24,16},{1,9},{9,1},{17,25},{25,17},{2,10},{10... | collective-permute-start | bytes 442376 | tf_op jit(solution)/shard_map/ppermute | solution.py:195
  36.1 8.0 %collective-permute-start.12 = (f32[144,256]{1,0:T(8,128)S(1)}, f32[144,256]{1,0:T(8,128)S(1)}, u32[]{:S(2)}, u32[]{:S(2)}) collective-permute-start(f32[144,256]{1,0:T(8,128)S(1)} %get-tuple-element.35), channel_id=1, source_target_pairs={{0,16},{8,24},{16,0},{24,8},{1,17},{9,25},{17,1},{25,9},{2,18},{10... | collective-permute-start | bytes 442376 | tf_op jit(solution)/shard_map/ppermute | solution.py:195
  37.6 6.4 %collective-permute-start.10 = (f32[80,256]{1,0:T(8,128)S(1)}, f32[80,256]{1,0:T(8,128)S(1)}, u32[]{:S(2)}, u32[]{:S(2)}) collective-permute-start(f32[80,256]{1,0:T(8,128)S(1)} %pad_maximum_fusion.1), channel_id=1, source_target_pairs={{0,2},{2,0},{4,6},{6,4},{1,3},{3,1},{5,7},{7,5},{8,10},{10,8},{12,... | collective-permute-start | bytes 245768 | tf_op jit(solution)/shard_map/ppermute | solution.py:195
  44.1 6.5 %collective-permute-start.14 = (f32[144,256]{1,0:T(8,128)S(1)}, f32[144,256]{1,0:T(8,128)S(1)}, u32[]{:S(2)}, u32[]{:S(2)}) collective-permute-start(f32[144,256]{1,0:T(8,128)S(1)} %add.43), channel_id=1, source_target_pairs={{0,16},{8,24},{16,0},{24,8},{1,17},{9,25},{17,1},{25,9},{2,18},{10... | collective-permute-start | bytes 442376 | tf_op jit(solution)/shard_map/ppermute | solution.py:195
  44.7 5.9 %collective-permute-start.15 = (f32[144,256]{1,0:T(8,128)S(1)}, f32[144,256]{1,0:T(8,128)S(1)}, u32[]{:S(2)}, u32[]{:S(2)}) collective-permute-start(f32[144,256]{1,0:T(8,128)S(1)} %add.44), channel_id=1, source_target_pairs={{0,8},{8,0},{16,24},{24,16},{1,9},{9,1},{17,25},{25,17},{2,10},{10... | collective-permute-start | bytes 442376 | tf_op jit(solution)/shard_map/ppermute | solution.py:195
  45.2 5.3 %collective-permute-start.13 = (f32[80,256]{1,0:T(8,128)S(1)}, f32[80,256]{1,0:T(8,128)S(1)}, u32[]{:S(2)}, u32[]{:S(2)}) collective-permute-start(f32[80,256]{1,0:T(8,128)S(1)} %add.42), channel_id=1, source_target_pairs={{0,4},{2,6},{4,0},{6,2},{1,5},{3,7},{5,1},{7,3},{8,12},{10,14},{12... | collective-permute-start | bytes 245768 | tf_op jit(solution)/shard_map/ppermute | solution.py:195
  50.7 1.8 %collective-permute-start.16 = (f32[288,256]{1,0:T(8,128)S(1)}, f32[288,256]{1,0:T(8,128)S(1)}, u32[]{:S(2)}, u32[]{:S(2)}) collective-permute-start(f32[288,256]{1,0:T(8,128)S(1)} %constant_dynamic-update-slice_fusion.mine_d_ref), channel_id=1, source_target_pairs={{0,1},{1,0},{2,3},{3,2},{4,5},{5,4},{6,7},{7,6},{8,9},{9,8},{10,11... | collective-permute-start | bytes 884744 | tf_op jit(solution)/shard_map/ppermute | solution.py:195
  50.8 1.7 %collective-permute-start.17 = (f32[80,256]{1,0:T(8,128)S(1)}, f32[80,256]{1,0:T(8,128)S(1)}, u32[]{:S(2)}, u32[]{:S(2)}) collective-permute-start(f32[80,256]{1,0:T(8,128)S(1)} %add.45.mine_t_ref), channel_id=1, source_target_pairs={{0,1},{1,0},{2,3},{3,2},{4,5},{5,4},{6,7},{7,6},{8,9},{9,8},{10,11... | collective-permute-start | bytes 245768 | tf_op jit(solution)/shard_map/ppermute | solution.py:195

commit v5 on v3

--- a/solution.py
+++ b/solution.py
@@ -69,7 +69,7 @@
     row_count, col_count = counts
     block_refs, refs = refs[:row_count], refs[row_count:]
     own_refs, refs = refs[:col_count], refs[col_count:]
-    keep_d_ref, send_d_ref, keep_t_ref, send_t_ref, term_ref, x_ref, y_ref = refs
+    density_ref, product_ref, term_ref, x_ref, y_ref = refs
     packed_width = block_refs[0].shape[0] // 2
     local_rows = straight_ref.shape[1]
     strips = local_rows // slot
@@ -85,11 +85,7 @@
     weighted = w_real * u_real - w_imag * u_imag
     turned = w_real * u_imag + w_imag * u_real
 
-    half = packed_width // 2
-    upper = (col_index & (col_count // 2)) != 0
-    keep_d_ref[...] = jnp.where(upper, weighted[half:], weighted[:half])
-    send_d_ref[...] = jnp.where(upper, weighted[:half], weighted[half:])
-
+    density_ref[...] = weighted
     for ref, value in ((x_ref, weighted), (y_ref, turned)):
         for s in range(strips):
             ref[s, :packed_width] = value[:, s * slot:(s + 1) * slot]
@@ -123,47 +119,38 @@
         ) + (rows_by_rows(own[:packed_width], x_low) - rows_by_rows(own[packed_width:], y_low))
         inside = (row_packed >= offsets[k]) & (row_packed < offsets[k + 1])
         total = jnp.where(inside, product, total)
-    keep_t_ref[...] = jnp.where(upper, total[half:], total[:half])
-    send_t_ref[...] = jnp.where(upper, total[:half], total[half:])
+    product_ref[...] = total
 
     folded = term_ref.shape[0]
+    flag = (col_index == density_root(col_count)).astype(F32)
     for s in range(strips):
-        first = pl.multiple_of((col_index * strips + s) * folded, folded)
-        term_ref[:, s * slot:(s + 1) * slot] = w_real * diag_ref[
-            0, pl.ds(first, folded), :
-        ].astype(F32) - w_imag * diag_ref[1, pl.ds(first, folded), :].astype(F32)
+        rows = slice(s * folded, (s + 1) * folded)
+        term_ref[:, s * slot:(s + 1) * slot] = flag * (
+            w_real * diag_ref[0, rows].astype(F32) - w_imag * diag_ref[1, rows].astype(F32)
+        )
 
 
 def expand_kernel(
-    col_count, slot, widths_ref, place_ref, mine_d_ref, other_d_ref, mine_t_ref, other_t_ref,
+    slot, widths_ref, place_ref, mine_d_ref, other_d_ref, mine_t_ref, other_t_ref,
     density_ref, diagonal_ref, strip_ref,
 ):
-    supernodes = diagonal_ref.shape[0] // slot
+    total_cols = diagonal_ref.shape[0]
+    supernodes = total_cols // slot
     per_col, local_rows = density_ref.shape
     strips = local_rows // slot
-    folded = per_col // strips
-    share = col_count // 2
-    tall = mine_d_ref.shape[0] // share
-    part = tall - folded
+    folded = total_cols // strips
+    packed_width = mine_t_ref.shape[0]
     col_index = place_ref[1]
-    upper = (col_index & share) != 0
-    for side in range(2):
-        own_side = upper if side else jnp.logical_not(upper)
-        d_value = jnp.where(own_side, mine_d_ref[...], other_d_ref[...])
-        t_value = jnp.where(own_side, mine_t_ref[...], other_t_ref[...])
-        for q in range(share):
-            owner = side * share + q
-            base = owner * part
-            for s in range(strips):
-                lanes = slice(s * slot, (s + 1) * slot)
-                strip_ref[s, base:base + part] = d_value[q * tall:q * tall + part, lanes]
-                first = (owner * strips + s) * folded
-                diagonal_ref[first:first + folded] = d_value[q * tall + part:(q + 1) * tall, lanes]
-            rows = slice(q * part // 2, (q + 1) * part // 2)
-            strip_ref[strips, base:base + part // 2] = t_value[rows, :slot]
-            strip_ref[strips, base + part // 2:base + part] = t_value[rows, slot:]
+    has_d = place_ref[2] != 0
+    has_t = place_ref[3] != 0
+    d_value = jnp.where(has_d, mine_d_ref[...], other_d_ref[...])
+    for s in range(strips):
+        lanes = slice(s * slot, (s + 1) * slot)
+        strip_ref[s, :packed_width] = d_value[:packed_width, lanes]
+        diagonal_ref[s * folded:(s + 1) * folded] = d_value[packed_width:, lanes]
+    strip_ref[strips, :packed_width] = jnp.where(has_t, mine_t_ref[...], other_t_ref[...])
     for s in range(strips + 1):
-        strip_ref[s, col_count * part:] = jnp.zeros((slot, slot), F32)
+        strip_ref[s, packed_width:] = jnp.zeros((slot, slot), F32)
     offsets = offsets_of(widths_ref, supernodes)
     row_in_slot = lax.broadcasted_iota(jnp.int32, (slot, 1), 0)
     for k in range(supernodes):
@@ -191,38 +178,44 @@
     return [1 << k for k in range(count.bit_length() - 1)]
 
 
+def product_root(col_count):
+    return 0
+
+
+def density_root(col_count):
+    return min(1, col_count - 1)
+
+
 def swap(value, axis, bit):
     return lax.ppermute(value, axis, [(i, i ^ bit) for i in range(lax.axis_size(axis))])
 
 
-def pole_sum(value):
-    bits = bits_of(lax.axis_size("pole"))
-    half = value.shape[0] // 2
-    first, second = value[:half], value[half:]
-    for bit, mirrored in zip(bits, bits[::-1]):
-        first, second = first + swap(first, "pole", bit), second + swap(second, "pole", mirrored)
-    return first, second
-
-
-def scatter_rest(value, axis):
-    index = lax.axis_index(axis)
-    for bit in bits_of(lax.axis_size(axis))[:-1][::-1]:
-        half = value.shape[0] // 2
-        upper = (index & bit) != 0
-        keep = jnp.where(upper, value[half:], value[:half])
-        value = keep + swap(jnp.where(upper, value[:half], value[half:]), axis, bit)
+def swap_at(value, axis, bit, col):
+    col_count = lax.axis_size("col")
+    return lax.ppermute(
+        value, (axis, "col"),
+        [(i * col_count + col, (i ^ bit) * col_count + col) for i in range(lax.axis_size(axis))],
+    )
+
+
+def sum_onto(value, root):
+    count = lax.axis_size("col")
+    for bit in bits_of(count):
+        pairs = [(i ^ root, i ^ bit ^ root) for i in range(bit, count, 2 * bit)]
+        value = value + lax.ppermute(value, "col", pairs)
     return value
 
 
-def gather_but_last(value, axis):
-    index = lax.axis_index(axis)
-    for bit in bits_of(lax.axis_size(axis))[:-1]:
-        other = swap(value, axis, bit)
-        upper = (index & bit) != 0
-        value = jnp.concatenate(
-            [jnp.where(upper, other, value), jnp.where(upper, value, other)], axis=0
-        )
-    return value
+def spread_from(value, root):
+    count = lax.axis_size("col")
+    relative = lax.axis_index("col") ^ root
+    received = value
+    for bit in bits_of(count)[::-1]:
+        pairs = [(i ^ root, i ^ bit ^ root) for i in range(0, count, 2 * bit)]
+        received = lax.ppermute(value, "col", pairs)
+        if bit > 1:
+            value = jnp.where(relative % (2 * bit) == bit, received, value)
+    return value, received
 
 
 def per_device(found_inverse, l_panel, block_pattern, sup_widths, diag_inverse, pole_weights):
@@ -230,20 +223,20 @@
     total_cols = l_panel.shape[-1]
     supernodes = total_cols // slot
     packed_width = slot + (supernodes - 1) * (slot // 2)
-    half = packed_width // 2
     local_rows = found_inverse.shape[2]
     block = l_panel.shape[2]
     row_count = lax.axis_size("row")
     col_count = lax.axis_size("col")
-    top = col_count // 2
-    place = jnp.stack([lax.axis_index("row"), lax.axis_index("col")]).astype(jnp.int32)
+    t_root, d_root = product_root(col_count), density_root(col_count)
+    col_index = lax.axis_index("col")
+    has_d, has_t = (col_index ^ d_root) % 2 == 0, (col_index ^ t_root) % 2 == 0
+    place = jnp.stack([lax.axis_index("row"), col_index, has_d, has_t]).astype(jnp.int32)
 
     packed = pl.pallas_call(
         functools.partial(pack_kernel, supernodes, slot),
         in_specs=[SMEM_SPEC, SMEM_SPEC, VMEM_SPEC],
         out_specs=VMEM_SPEC,
         out_shape=jax.ShapeDtypeStruct((2 * packed_width, block), BF16),
-        compiler_params=PARAMS,
         name="pack",
     )(block_pattern, sup_widths, l_panel[0])
 
@@ -267,13 +260,15 @@
         name="prepare",
     )(place, found_inverse.reshape(2 * local_rows * row_count, block))
 
-    keep_d, send_d, keep_t, send_t, term = pl.pallas_call(
+    density, products, term = pl.pallas_call(
         functools.partial(compute_kernel, (row_count, col_count), supernodes, slot),
         in_specs=[SMEM_SPEC] * 3 + [VMEM_SPEC] * (2 + row_count + col_count),
-        out_specs=[VMEM_SPEC] * 5,
-        out_shape=[jax.ShapeDtypeStruct((half, local_rows), F32)] * 2
-        + [jax.ShapeDtypeStruct((half, slot), F32)] * 2
-        + [jax.ShapeDtypeStruct((total_cols * slot // (col_count * local_rows), local_rows), F32)],
+        out_specs=[VMEM_SPEC] * 3,
+        out_shape=[
+            jax.ShapeDtypeStruct((packed_width, local_rows), F32),
+            jax.ShapeDtypeStruct((packed_width, slot), F32),
+            jax.ShapeDtypeStruct((total_cols * slot // local_rows, local_rows), F32),
+        ],
         scratch_shapes=[
             pltpu.VMEM((local_rows // slot, packed_width + slot, slot), F32),
             pltpu.VMEM((local_rows // slot, packed_width + slot, slot), F32),
@@ -285,17 +280,16 @@
         *[blocks[shift] for shift in range(row_count)], *own,
     )
 
-    products = scatter_rest(keep_t + swap(send_t, "col", top), "col")
-    density = scatter_rest(keep_d + swap(send_d, "col", top), "col")
-    products = jnp.concatenate(pole_sum(products), axis=1)
+    products, density = lax.optimization_barrier((sum_onto(products, t_root), density))
+    density = jnp.concatenate([sum_onto(density, d_root), term], axis=0)
+    for bit in bits_of(lax.axis_size("pole")):
+        products = products + swap_at(products, "pole", bit, t_root)
+        density = density + swap_at(density, "pole", bit, d_root)
     for bit in bits_of(row_count):
-        products = products + swap(products, "row", bit)
-    density = jnp.concatenate(pole_sum(jnp.concatenate([density, term], axis=0)), axis=0)
-    density = gather_but_last(density, "col")
-    products = gather_but_last(products, "col")
+        products = products + swap_at(products, "row", bit, t_root)
 
     return pl.pallas_call(
-        functools.partial(expand_kernel, col_count, slot),
+        functools.partial(expand_kernel, slot),
         in_specs=[SMEM_SPEC] * 2 + [VMEM_SPEC] * 4,
         out_specs=[VMEM_SPEC] * 2,
         out_shape=[
@@ -305,10 +299,7 @@
         scratch_shapes=[pltpu.VMEM((local_rows // slot + 1, packed_width + slot, slot), F32)],
         compiler_params=PARAMS,
         name="expand",
-    )(
-        sup_widths, place, density, swap(density, "col", top),
-        products, swap(products, "col", top),
-    )
+    )(sup_widths, place, *spread_from(density, d_root), *spread_from(products, t_root))
 
 
 def solution(mesh):

time: 54.7 us -> 70.7 us (1.29)
  waiting for transfers between devices: 19.9 us -> 33.1 us
  starting transfers between devices: 24.9 us -> 27.8 us
  local copies, waits for them, and re-layouts: 2.67 us -> 1.06 us
  Pallas kernels: 5.97 us -> 7.08 us
    ppermute x0 -> x10, waiting for transfers between devices: none -> 22.1 us  [the longest x6 17.9 us: swap_at(): lax.ppermute(value, (axis, 'col'), [(i * col_count + col, (i ^ bit) * col...]
    ppermute x0 -> x10, starting transfers between devices: none -> 21.8 us  [the longest x6 15.8 us: swap_at(): lax.ppermute(value, (axis, 'col'), [(i * col_count + col, (i ^ bit) * col...]
    ppermute x15 -> x1, starting transfers between devices: 18.3 us -> 0.01 us  [swap(): lax.ppermute(value, axis, [(i, i ^ bit) for i in range(lax.axis_size(axis...]
    ppermute x15 -> x1, waiting for transfers between devices: 12.1 us -> 0.01 us  [swap(): lax.ppermute(value, axis, [(i, i ^ bit) for i in range(lax.axis_size(axis...]
    ppermute x3, waiting for transfers between devices: 7.87 us -> 10.9 us  [per_device(): blocks[shift] = lax.ppermute(packed, 'row', pairs)]
    unnamed x12 -> x10, local copies, waits for them, and re-layouts: 2.66 us -> 1.06 us
    pallas_call x1, Pallas kernels: 0.87 us -> 1.96 us  [per_device(): pl.pallas_call(functools.partial(pack_kernel, supernodes, slot), in_specs...]
  transfers between devices with their start and end apart: 18 -> 14, of which waited for: 8 -> 9; matrix products, arithmetic and copies ran while one was open for 0% -> 0% of each run, Pallas kernels for 2% -> 1%
where the time goes in v5:
time: 70.7 us; the launch traced here: 70.3 us
  waiting for transfers between devices  33.1 us (47%)
  starting transfers between devices  27.8 us (39%)
  Pallas kernels  7.08 us (10%)
  local copies, waits for them, and re-layouts  1.06 us (1%)
  between operations  0.83 us (1%)
    ppermute x6, waiting for transfers between devices, swap_at(): lax.ppermute(value, (axis, 'col'), [(i * col_count + col, (i ^ bit) * col...  17.9 us
    ppermute x6, starting transfers between devices, swap_at(): lax.ppermute(value, (axis, 'col'), [(i * col_count + col, (i ^ bit) * col...  15.8 us
    ppermute x3, waiting for transfers between devices, per_device(): blocks[shift] = lax.ppermute(packed, 'row', pairs)  10.9 us
    ppermute x3, starting transfers between devices, per_device(): blocks[shift] = lax.ppermute(packed, 'row', pairs)  6.06 us
    ppermute x2, starting transfers between devices, sum_onto(): value = value + lax.ppermute(value, 'col', pairs)  3.36 us
    ppermute x2, waiting for transfers between devices, sum_onto(): value = value + lax.ppermute(value, 'col', pairs)  3.21 us
    pallas_call x1, Pallas kernels, per_device(): pl.pallas_call(functools.partial(compute_kernel, (row_count, col_count),...  2.65 us
    ppermute x2, starting transfers between devices, spread_from(): received = lax.ppermute(value, 'col', pairs)  2.59 us
  transfers between devices with their start and end apart: 14, of which 9 were waited for; matrix products, arithmetic and copies ran while one was open for 0% of the time, Pallas kernels for 1%

profile of v5, /device:TPU:0, one launch (start us, length us, event | category | flops | bytes accessed | tf_op | source)
XLA Modules:
  0.0 70.3 jit_solution(9576148906385805871)
XLA Ops:
  0.6 2.0 %pack.1.refs_0_.refs_4_ = bf16[640,128]{1,0:T(8,128)(2,1)} custom-call(s32[1,4]{1,0:T(1,128)} %pattern_ref.1, s32[4]{0:T(128)} %widths_ref.5, bf16[2,128,512]{2,1,0:T(8,128)(2,1)} %bitcast.9), custom_call_target="tpu_custom_call" | custom-call | tf_op jit(solution)/shard_map/pack/pallas_call | solution.py:235
  2.6 5.0 %collective-permute-start = (bf16[640,128]{1,0:T(8,128)(2,1)}, bf16[640,128]{1,0:T(8,128)(2,1)S(1)}, u32[]{:S(2)}, u32[]{:S(2)}) collective-permute-start(bf16[640,128]{1,0:T(8,128)(2,1)} %pack.1.refs_0_.refs_4_), channel_id=1, source_target_pairs={{2,0},{4,2},{6,4},{0,6},{3,1},{5,3},{7,5},{1,7},{10,8},{12,10},{14... | collective-permute-start | bytes 491528 | tf_op jit(solution)/shard_map/ppermute | solution.py:246
  7.6 0.0 collective-permute-start.1
  7.6 1.0 %collective-permute-start.2 = (bf16[640,128]{1,0:T(8,128)(2,1)}, bf16[640,128]{1,0:T(8,128)(2,1)S(1)}, u32[]{:S(2)}, u32[]{:S(2)}) collective-permute-start(bf16[640,128]{1,0:T(8,128)(2,1)} %pack.1.refs_0_.refs_4_), channel_id=1, source_target_pairs={{6,0},{0,2},{2,4},{4,6},{7,1},{1,3},{3,5},{5,7},{14,8},{8,10},{10,... | collective-permute-start | bytes 491528 | tf_op jit(solution)/shard_map/ppermute | solution.py:246
  8.7 0.0 collective-permute-start.3
  8.7 0.1 pad_add_fusion.place_ref
  8.7 0.0 copy-start.1
  8.7 1.0 %copy-done.1 = bf16[1,2,256,4,1,128]{5,3,4,2,1,0:T(4,128)(2,1)S(1)} copy-done((bf16[1,2,256,4,1,128]{5,3,4,2,1,0:T(4,128)(2,1)S(1)}, bf16[1,2,256,4,1,128]{5,3,4,2,1,0:T(4,128)(2,1)}, u32[]{:S(2)}) %copy-start.1) | copy-done | bytes 524312
  9.8 0.0 copy-start
  9.8 0.0 copy-start.2
  9.8 1.0 %prepare.1.straight_ref = bf16[2,256,512]{2,1,0:T(8,128)(2,1)S(1)} custom-call(s32[4]{0:T(128)S(1)} %pad_add_fusion.place_ref, bf16[2048,128]{1,0:T(8,128)(2,1)S(1)} %bitcast.7), custom_call_target="tpu_custom_call" | custom-call | flops 134217728 | bytes 1048576 | tf_op jit(solution)/shard_map/prepare/pallas_call | solution.py:249
  10.8 0.0 copy-start.3
  10.8 0.0 copy-start.4
  10.8 1.8 %collective-permute-done.refs_1_ = bf16[640,128]{1,0:T(8,128)(2,1)S(1)} collective-permute-done((bf16[640,128]{1,0:T(8,128)(2,1)}, bf16[640,128]{1,0:T(8,128)(2,1)S(1)}, u32[]{:S(2)}, u32[]{:S(2)}) %collective-permute-start) | collective-permute-done | bytes 163872 | tf_op jit(solution)/shard_map/ppermute | solution.py:246
  12.6 9.1 %collective-permute-done.1.refs_2_ = bf16[640,128]{1,0:T(8,128)(2,1)S(1)} collective-permute-done((bf16[640,128]{1,0:T(8,128)(2,1)}, bf16[640,128]{1,0:T(8,128)(2,1)S(1)}, u32[]{:S(2)}, u32[]{:S(2)}) %collective-permute-start.1) | collective-permute-done | bytes 163872 | tf_op jit(solution)/shard_map/ppermute | solution.py:246
  21.7 0.0 collective-permute-done.2.refs_3_
  21.7 0.0 collective-permute-done.3.refs_5_
  21.7 0.0 copy-done
  21.7 0.0 copy-done.2
  21.8 0.0 copy-done.3
  21.8 0.0 copy-done.4
  21.8 2.6 %compute.1 = (f32[320,256]{1,0:T(8,128)S(1)}, f32[320,128]{1,0:T(8,128)S(1)}, f32[256,256]{1,0:T(8,128)S(1)}) custom-call(s32[4]{0:T(128)S(1)} %copy-done.3, f32[1,2]{1,0:T(1,128)S(1)} %copy-done.4, s32[4]{0:T(128)S(1)} %pad_add_fusion.place_ref, bf16[2,256,512]{2,1,0:T(8,128)(2,1)S(1)} %prepare.1.straight_ref, bf16[2,512,128]{2,1,0:T(8,128)(2,1)S(1)} %bitcast.8, ...), custom_call_target="tpu_custom_call" | custom-call | tf_op jit(solution)/shard_map/compute/pallas_call | solution.py:263
  24.4 1.3 %collective-permute-start.4 = (f32[320,128]{1,0:T(8,128)S(1)}, f32[320,128]{1,0:T(8,128)S(1)}, u32[]{:S(2)}, u32[]{:S(2)}) collective-permute-start(f32[320,128]{1,0:T(8,128)S(1)} %get-tuple-element.7), channel_id=1, source_target_pairs={{1,0},{3,2},{5,4},{7,6},{9,8},{11,10},{13,12},{15,14},{17,16},{19,... | collective-permute-start | bytes 491528 | tf_op jit(solution)/shard_map/ppermute | solution.py:205
  25.7 2.0 %collective-permute-done.4 = f32[320,128]{1,0:T(8,128)S(1)} collective-permute-done((f32[320,128]{1,0:T(8,128)S(1)}, f32[320,128]{1,0:T(8,128)S(1)}, u32[]{:S(2)}, u32[]{:S(2)}) %collective-permute-start.4) | collective-permute-done | bytes 163872 | tf_op jit(solution)/shard_map/ppermute | solution.py:205
  27.7 2.1 %collective-permute-start.5 = (f32[320,256]{1,0:T(8,128)S(1)}, f32[320,256]{1,0:T(8,128)S(1)}, u32[]{:S(2)}, u32[]{:S(2)}) collective-permute-start(f32[320,256]{1,0:T(8,128)S(1)} %get-tuple-element.9), channel_id=1, source_target_pairs={{0,1},{2,3},{4,5},{6,7},{8,9},{10,11},{12,13},{14,15},{16,17},{18,... | collective-permute-start | bytes 983048 | tf_op jit(solution)/shard_map/ppermute | solution.py:205
  29.8 1.2 %collective-permute-done.5 = f32[320,256]{1,0:T(8,128)S(1)} collective-permute-done((f32[320,256]{1,0:T(8,128)S(1)}, f32[320,256]{1,0:T(8,128)S(1)}, u32[]{:S(2)}, u32[]{:S(2)}) %collective-permute-start.5) | collective-permute-done | bytes 327712 | tf_op jit(solution)/shard_map/ppermute | solution.py:205
  31.1 0.7 collective-permute-start.6
  31.8 0.0 collective-permute-done.6
  31.8 0.1 fusion
  31.9 0.7 collective-permute-start.7
  32.6 3.4 %collective-permute-start.9 = (f32[320,128]{1,0:T(8,128)S(1)}, f32[320,128]{1,0:T(8,128)S(1)}, u32[]{:S(2)}, u32[]{:S(2)}) collective-permute-start(f32[320,128]{1,0:T(8,128)S(1)} %add.33), channel_id=1, source_target_pairs={{0,8},{8,0},{16,24},{24,16},{2,10},{10,2},{18,26},{26,18},{4,12},{... | collective-permute-start | bytes 491528 | tf_op jit(solution)/shard_map/ppermute | solution.py:195
  36.0 5.6 %collective-permute-done.9 = f32[320,128]{1,0:T(8,128)S(1)} collective-permute-done((f32[320,128]{1,0:T(8,128)S(1)}, f32[320,128]{1,0:T(8,128)S(1)}, u32[]{:S(2)}, u32[]{:S(2)}) %collective-permute-start.9) | collective-permute-done | bytes 163872 | tf_op jit(solution)/shard_map/ppermute | solution.py:195
  41.7 3.4 %collective-permute-start.10 = (f32[320,128]{1,0:T(8,128)S(1)}, f32[320,128]{1,0:T(8,128)S(1)}, u32[]{:S(2)}, u32[]{:S(2)}) collective-permute-start(f32[320,128]{1,0:T(8,128)S(1)} %add.37), channel_id=1, source_target_pairs={{0,16},{8,24},{16,0},{24,8},{2,18},{10,26},{18,2},{26,10},{4,20},{... | collective-permute-start | bytes 491528 | tf_op jit(solution)/shard_map/ppermute | solution.py:195
  45.1 0.0 collective-permute-done.7
  45.1 0.1 add.36.mine_d_ref
  45.2 1.3 %collective-permute-start.8 = (f32[576,256]{1,0:T(8,128)S(1)}, f32[576,256]{1,0:T(8,128)S(1)}, u32[]{:S(2)}, u32[]{:S(2)}) collective-permute-start(f32[576,256]{1,0:T(8,128)S(1)} %add.36.mine_d_ref), channel_id=1, source_target_pairs={{1,0},{3,2},{5,4},{7,6},{9,8},{11,10},{13,12},{15,14},{17,16},{19,... | collective-permute-start | bytes 1769480 | tf_op jit(solution)/shard_map/ppermute | solution.py:215
  46.5 2.8 %collective-permute-done.10 = f32[320,128]{1,0:T(8,128)S(1)} collective-permute-done((f32[320,128]{1,0:T(8,128)S(1)}, f32[320,128]{1,0:T(8,128)S(1)}, u32[]{:S(2)}, u32[]{:S(2)}) %collective-permute-start.10) | collective-permute-done | bytes 163872 | tf_op jit(solution)/shard_map/ppermute | solution.py:195
  49.3 2.9 %collective-permute-start.11 = (f32[320,128]{1,0:T(8,128)S(1)}, f32[320,128]{1,0:T(8,128)S(1)}, u32[]{:S(2)}, u32[]{:S(2)}) collective-permute-start(f32[320,128]{1,0:T(8,128)S(1)} %add.38), channel_id=1, source_target_pairs={{0,2},{2,0},{4,6},{6,4},{8,10},{10,8},{12,14},{14,12},{16,18},{18,... | collective-permute-start | bytes 491528 | tf_op jit(solution)/shard_map/ppermute | solution.py:195
  52.2 4.3 %collective-permute-done.11 = f32[320,128]{1,0:T(8,128)S(1)} collective-permute-done((f32[320,128]{1,0:T(8,128)S(1)}, f32[320,128]{1,0:T(8,128)S(1)}, u32[]{:S(2)}, u32[]{:S(2)}) %collective-permute-start.11) | collective-permute-done | bytes 163872 | tf_op jit(solution)/shard_map/ppermute | solution.py:195
  56.6 4.7 %collective-permute-start.12 = (f32[320,128]{1,0:T(8,128)S(1)}, f32[320,128]{1,0:T(8,128)S(1)}, u32[]{:S(2)}, u32[]{:S(2)}) collective-permute-start(f32[320,128]{1,0:T(8,128)S(1)} %add.39), channel_id=1, source_target_pairs={{0,4},{2,6},{4,0},{6,2},{8,12},{10,14},{12,8},{14,10},{16,20},{18,... | collective-permute-start | bytes 491528 | tf_op jit(solution)/shard_map/ppermute | solution.py:195
  61.3 5.2 %collective-permute-done.12 = f32[320,128]{1,0:T(8,128)S(1)} collective-permute-done((f32[320,128]{1,0:T(8,128)S(1)}, f32[320,128]{1,0:T(8,128)S(1)}, u32[]{:S(2)}, u32[]{:S(2)}) %collective-permute-start.12) | collective-permute-done | bytes 163872 | tf_op jit(solution)/shard_map/ppermute | solution.py:195
  66.5 1.3 %collective-permute-start.13 = (f32[320,128]{1,0:T(8,128)S(1)}, f32[320,128]{1,0:T(8,128)S(1)}, u32[]{:S(2)}, u32[]{:S(2)}) collective-permute-start(f32[320,128]{1,0:T(8,128)S(1)} %add.40.mine_t_ref), channel_id=1, source_target_pairs={{0,1},{2,3},{4,5},{6,7},{8,9},{10,11},{12,13},{14,15},{16,17},{18,... | collective-permute-start | bytes 491528 | tf_op jit(solution)/shard_map/ppermute | solution.py:215
  67.8 1.0 %collective-permute-done.13.other_t_ref = f32[320,128]{1,0:T(8,128)S(1)} collective-permute-done((f32[320,128]{1,0:T(8,128)S(1)}, f32[320,128]{1,0:T(8,128)S(1)}, u32[]{:S(2)}, u32[]{:S(2)}) %collective-permute-start.13) | collective-permute-done | bytes 163872 | tf_op jit(solution)/shard_map/ppermute | solution.py:215
  68.8 0.0 collective-permute-done.8.other_d_ref
  68.8 1.5 %expand.1 = (f32[256,256]{1,0:T(8,128)}, f32[512,128]{1,0:T(8,128)}) custom-call(s32[4]{0:T(128)S(1)} %copy-done.3, s32[4]{0:T(128)S(1)} %pad_add_fusion.place_ref, f32[576,256]{1,0:T(8,128)S(1)} %add.36.mine_d_ref, f32[576,256]{1,0:T(8,128)S(1)} %collective-permute-done.8.other_d_ref, f32[320,128]{1,0:T(8,128)S(1)} %add.40.mine_t_ref, ...), custom_call_target="tpu_custom_call" | custom-call | tf_op jit(solution)/shard_map/expand/pallas_call | solution.py:291
  (7 shorter events, 0.2 us)
Async XLA Ops:
  2.6 10.0 %collective-permute-start = (bf16[640,128]{1,0:T(8,128)(2,1)}, bf16[640,128]{1,0:T(8,128)(2,1)S(1)}, u32[]{:S(2)}, u32[]{:S(2)}) collective-permute-start(bf16[640,128]{1,0:T(8,128)(2,1)} %pack.1.refs_0_.refs_4_), channel_id=1, source_target_pairs={{2,0},{4,2},{6,4},{0,6},{3,1},{5,3},{7,5},{1,7},{10,8},{12,10},{14... | collective-permute-start | bytes 491528 | tf_op jit(solution)/shard_map/ppermute | solution.py:246
  7.6 14.1 %collective-permute-start.1 = (bf16[640,128]{1,0:T(8,128)(2,1)}, bf16[640,128]{1,0:T(8,128)(2,1)S(1)}, u32[]{:S(2)}, u32[]{:S(2)}) collective-permute-start(bf16[640,128]{1,0:T(8,128)(2,1)} %pack.1.refs_0_.refs_4_), channel_id=1, source_target_pairs={{4,0},{6,2},{0,4},{2,6},{5,1},{7,3},{1,5},{3,7},{12,8},{14,10},{8,... | collective-permute-start | bytes 491528 | tf_op jit(solution)/shard_map/ppermute | solution.py:246
  7.6 14.1 %collective-permute-start.2 = (bf16[640,128]{1,0:T(8,128)(2,1)}, bf16[640,128]{1,0:T(8,128)(2,1)S(1)}, u32[]{:S(2)}, u32[]{:S(2)}) collective-permute-start(bf16[640,128]{1,0:T(8,128)(2,1)} %pack.1.refs_0_.refs_4_), channel_id=1, source_target_pairs={{6,0},{0,2},{2,4},{4,6},{7,1},{1,3},{3,5},{5,7},{14,8},{8,10},{10,... | collective-permute-start | bytes 491528 | tf_op jit(solution)/shard_map/ppermute | solution.py:246
  8.7 13.1 %collective-permute-start.3 = (bf16[640,128]{1,0:T(8,128)(2,1)}, bf16[640,128]{1,0:T(8,128)(2,1)S(1)}, u32[]{:S(2)}, u32[]{:S(2)}) collective-permute-start(bf16[640,128]{1,0:T(8,128)(2,1)} %pack.1.refs_0_.refs_4_), channel_id=1, source_target_pairs={{0,1},{1,0},{2,3},{3,2},{4,5},{5,4},{6,7},{7,6},{8,9},{9,8},{10,11... | collective-permute-start | bytes 491528 | tf_op jit(solution)/shard_map/ppermute | solution.py:190
  8.7 1.0 %copy-start.1 = (bf16[1,2,256,4,1,128]{5,3,4,2,1,0:T(4,128)(2,1)S(1)}, bf16[1,2,256,4,1,128]{5,3,4,2,1,0:T(4,128)(2,1)}, u32[]{:S(2)}) copy-start(bf16[1,2,256,4,1,128]{5,3,4,2,1,0:T(4,128)(2,1)} %param.6) | copy-start | bytes 1572868
  9.8 12.0 %copy-start = (bf16[640,128]{1,0:T(8,128)(2,1)S(1)}, bf16[640,128]{1,0:T(8,128)(2,1)}, u32[]{:S(2)}) copy-start(bf16[640,128]{1,0:T(8,128)(2,1)} %pack.1.refs_0_.refs_4_) | copy-start | bytes 491524
  9.8 12.0 %copy-start.2 = (bf16[1,2,512,128]{3,2,1,0:T(8,128)(2,1)S(1)}, bf16[1,2,512,128]{3,2,1,0:T(8,128)(2,1)}, u32[]{:S(2)}) copy-start(bf16[1,2,512,128]{3,2,1,0:T(8,128)(2,1)} %param.10) | copy-start | bytes 786436
  10.8 11.0 %copy-start.3 = (s32[4]{0:T(128)S(1)}, s32[4]{0:T(128)}, u32[]{:S(2)}) copy-start(s32[4]{0:T(128)} %widths_ref.5) | copy-start | bytes 52
  10.8 11.0 %copy-start.4 = (f32[1,2]{1,0:T(1,128)S(1)}, f32[1,2]{1,0:T(1,128)}, u32[]{:S(2)}) copy-start(f32[1,2]{1,0:T(1,128)} %weights_ref.1) | copy-start | bytes 28
  24.4 3.3 %collective-permute-start.4 = (f32[320,128]{1,0:T(8,128)S(1)}, f32[320,128]{1,0:T(8,128)S(1)}, u32[]{:S(2)}, u32[]{:S(2)}) collective-permute-start(f32[320,128]{1,0:T(8,128)S(1)} %get-tuple-element.7), channel_id=1, source_target_pairs={{1,0},{3,2},{5,4},{7,6},{9,8},{11,10},{13,12},{15,14},{17,16},{19,... | collective-permute-start | bytes 491528 | tf_op jit(solution)/shard_map/ppermute | solution.py:205
  27.7 3.3 %collective-permute-start.5 = (f32[320,256]{1,0:T(8,128)S(1)}, f32[320,256]{1,0:T(8,128)S(1)}, u32[]{:S(2)}, u32[]{:S(2)}) collective-permute-start(f32[320,256]{1,0:T(8,128)S(1)} %get-tuple-element.9), channel_id=1, source_target_pairs={{0,1},{2,3},{4,5},{6,7},{8,9},{10,11},{12,13},{14,15},{16,17},{18,... | collective-permute-start | bytes 983048 | tf_op jit(solution)/shard_map/ppermute | solution.py:205
  31.1 0.7 %collective-permute-start.6 = (f32[576,256]{1,0:T(8,128)S(1)}, f32[576,256]{1,0:T(8,128)S(1)}, u32[]{:S(2)}, u32[]{:S(2)}) collective-permute-start(f32[576,256]{1,0:T(8,128)S(1)} %pad_maximum_fusion), channel_id=1, source_target_pairs={{1,9},{9,1},{17,25},{25,17},{3,11},{11,3},{19,27},{27,19},{5,13},{... | collective-permute-start | bytes 1769480 | tf_op jit(solution)/shard_map/ppermute | solution.py:195
  31.9 13.2 %collective-permute-start.7 = (f32[576,256]{1,0:T(8,128)S(1)}, f32[576,256]{1,0:T(8,128)S(1)}, u32[]{:S(2)}, u32[]{:S(2)}) collective-permute-start(f32[576,256]{1,0:T(8,128)S(1)} %fusion), channel_id=1, source_target_pairs={{1,17},{9,25},{17,1},{25,9},{3,19},{11,27},{19,3},{27,11},{5,21},{... | collective-permute-start | bytes 1769480 | tf_op jit(solution)/shard_map/ppermute | solution.py:195
  32.6 9.0 %collective-permute-start.9 = (f32[320,128]{1,0:T(8,128)S(1)}, f32[320,128]{1,0:T(8,128)S(1)}, u32[]{:S(2)}, u32[]{:S(2)}) collective-permute-start(f32[320,128]{1,0:T(8,128)S(1)} %add.33), channel_id=1, source_target_pairs={{0,8},{8,0},{16,24},{24,16},{2,10},{10,2},{18,26},{26,18},{4,12},{... | collective-permute-start | bytes 491528 | tf_op jit(solution)/shard_map/ppermute | solution.py:195
  41.7 7.6 %collective-permute-start.10 = (f32[320,128]{1,0:T(8,128)S(1)}, f32[320,128]{1,0:T(8,128)S(1)}, u32[]{:S(2)}, u32[]{:S(2)}) collective-permute-start(f32[320,128]{1,0:T(8,128)S(1)} %add.37), channel_id=1, source_target_pairs={{0,16},{8,24},{16,0},{24,8},{2,18},{10,26},{18,2},{26,10},{4,20},{... | collective-permute-start | bytes 491528 | tf_op jit(solution)/shard_map/ppermute | solution.py:195
  45.2 23.6 %collective-permute-start.8 = (f32[576,256]{1,0:T(8,128)S(1)}, f32[576,256]{1,0:T(8,128)S(1)}, u32[]{:S(2)}, u32[]{:S(2)}) collective-permute-start(f32[576,256]{1,0:T(8,128)S(1)} %add.36.mine_d_ref), channel_id=1, source_target_pairs={{1,0},{3,2},{5,4},{7,6},{9,8},{11,10},{13,12},{15,14},{17,16},{19,... | collective-permute-start | bytes 1769480 | tf_op jit(solution)/shard_map/ppermute | solution.py:215
  49.3 7.2 %collective-permute-start.11 = (f32[320,128]{1,0:T(8,128)S(1)}, f32[320,128]{1,0:T(8,128)S(1)}, u32[]{:S(2)}, u32[]{:S(2)}) collective-permute-start(f32[320,128]{1,0:T(8,128)S(1)} %add.38), channel_id=1, source_target_pairs={{0,2},{2,0},{4,6},{6,4},{8,10},{10,8},{12,14},{14,12},{16,18},{18,... | collective-permute-start | bytes 491528 | tf_op jit(solution)/shard_map/ppermute | solution.py:195
  56.6 9.9 %collective-permute-start.12 = (f32[320,128]{1,0:T(8,128)S(1)}, f32[320,128]{1,0:T(8,128)S(1)}, u32[]{:S(2)}, u32[]{:S(2)}) collective-permute-start(f32[320,128]{1,0:T(8,128)S(1)} %add.39), channel_id=1, source_target_pairs={{0,4},{2,6},{4,0},{6,2},{8,12},{10,14},{12,8},{14,10},{16,20},{18,... | collective-permute-start | bytes 491528 | tf_op jit(solution)/shard_map/ppermute | solution.py:195
  66.5 2.3 %collective-permute-start.13 = (f32[320,128]{1,0:T(8,128)S(1)}, f32[320,128]{1,0:T(8,128)S(1)}, u32[]{:S(2)}, u32[]{:S(2)}) collective-permute-start(f32[320,128]{1,0:T(8,128)S(1)} %add.40.mine_t_ref), channel_id=1, source_target_pairs={{0,1},{2,3},{4,5},{6,7},{8,9},{10,11},{12,13},{14,15},{16,17},{18,... | collective-permute-start | bytes 491528 | tf_op jit(solution)/shard_map/ppermute | solution.py:215

commit v6 on v3

--- a/solution.py
+++ b/solution.py
@@ -63,13 +63,20 @@
                 ] = sorted_rows[owner * group:(owner + 1) * group]
 
 
+def weigh_kernel(weights_ref, diag_ref, packed_ref, term_ref):
+    del packed_ref
+    term_ref[...] = weights_ref[0, 0] * diag_ref[0].astype(F32) - weights_ref[
+        0, 1
+    ] * diag_ref[1].astype(F32)
+
+
 def compute_kernel(
-    counts, supernodes, slot, widths_ref, weights_ref, place_ref, straight_ref, diag_ref, *refs
+    counts, supernodes, slot, widths_ref, weights_ref, place_ref, straight_ref, *refs
 ):
     row_count, col_count = counts
     block_refs, refs = refs[:row_count], refs[row_count:]
     own_refs, refs = refs[:col_count], refs[col_count:]
-    keep_d_ref, send_d_ref, keep_t_ref, send_t_ref, term_ref, x_ref, y_ref = refs
+    keep_d_ref, send_d_ref, keep_t_ref, send_t_ref, x_ref, y_ref = refs
     packed_width = block_refs[0].shape[0] // 2
     local_rows = straight_ref.shape[1]
     strips = local_rows // slot
@@ -126,25 +133,16 @@
     keep_t_ref[...] = jnp.where(upper, total[half:], total[:half])
     send_t_ref[...] = jnp.where(upper, total[:half], total[half:])
 
-    folded = term_ref.shape[0]
-    for s in range(strips):
-        first = pl.multiple_of((col_index * strips + s) * folded, folded)
-        term_ref[:, s * slot:(s + 1) * slot] = w_real * diag_ref[
-            0, pl.ds(first, folded), :
-        ].astype(F32) - w_imag * diag_ref[1, pl.ds(first, folded), :].astype(F32)
-
 
 def expand_kernel(
     col_count, slot, widths_ref, place_ref, mine_d_ref, other_d_ref, mine_t_ref, other_t_ref,
-    density_ref, diagonal_ref, strip_ref,
+    term_ref, density_ref, diagonal_ref, strip_ref,
 ):
     supernodes = diagonal_ref.shape[0] // slot
     per_col, local_rows = density_ref.shape
     strips = local_rows // slot
-    folded = per_col // strips
     share = col_count // 2
-    tall = mine_d_ref.shape[0] // share
-    part = tall - folded
+    part = mine_d_ref.shape[0] // share
     col_index = place_ref[1]
     upper = (col_index & share) != 0
     for side in range(2):
@@ -156,12 +154,8 @@
             base = owner * part
             for s in range(strips):
                 lanes = slice(s * slot, (s + 1) * slot)
-                strip_ref[s, base:base + part] = d_value[q * tall:q * tall + part, lanes]
-                first = (owner * strips + s) * folded
-                diagonal_ref[first:first + folded] = d_value[q * tall + part:(q + 1) * tall, lanes]
-            rows = slice(q * part // 2, (q + 1) * part // 2)
-            strip_ref[strips, base:base + part // 2] = t_value[rows, :slot]
-            strip_ref[strips, base + part // 2:base + part] = t_value[rows, slot:]
+                strip_ref[s, base:base + part] = d_value[q * part:(q + 1) * part, lanes]
+            strip_ref[strips, base:base + part] = t_value[q * part:(q + 1) * part]
     for s in range(strips + 1):
         strip_ref[s, col_count * part:] = jnp.zeros((slot, slot), F32)
     offsets = offsets_of(widths_ref, supernodes)
@@ -169,7 +163,10 @@
     for k in range(supernodes):
         product = strip_ref[strips, pl.ds(offsets[k], slot), :]
         product = jnp.where(row_in_slot < widths_ref[k], product, 0.0)
-        diagonal_ref[k * slot:(k + 1) * slot] = diagonal_ref[k * slot:(k + 1) * slot] - product
+        diagonal_ref[k * slot:(k + 1) * slot] = (
+            tree_sum([term_ref[p, k * slot:(k + 1) * slot] for p in range(term_ref.shape[0])])
+            - product
+        )
     size = min(per_col, slot)
     row_in_part = lax.broadcasted_iota(jnp.int32, (size, 1), 0)
     for part in range(per_col // size):
@@ -195,13 +192,14 @@
     return lax.ppermute(value, axis, [(i, i ^ bit) for i in range(lax.axis_size(axis))])
 
 
-def pole_sum(value):
-    bits = bits_of(lax.axis_size("pole"))
-    half = value.shape[0] // 2
-    first, second = value[:half], value[half:]
-    for bit, mirrored in zip(bits, bits[::-1]):
-        first, second = first + swap(first, "pole", bit), second + swap(second, "pole", mirrored)
-    return first, second
+def tree_sum(terms):
+    while len(terms) > 1:
+        terms = [terms[j] + terms[j + 1] for j in range(0, len(terms), 2)]
+    return terms[0]
+
+
+def sum_direct(value, axis):
+    return tree_sum([value] + [swap(value, axis, j) for j in range(1, lax.axis_size(axis))])
 
 
 def scatter_rest(value, axis):
@@ -243,7 +241,6 @@
         in_specs=[SMEM_SPEC, SMEM_SPEC, VMEM_SPEC],
         out_specs=VMEM_SPEC,
         out_shape=jax.ShapeDtypeStruct((2 * packed_width, block), BF16),
-        compiler_params=PARAMS,
         name="pack",
     )(block_pattern, sup_widths, l_panel[0])
 
@@ -266,14 +263,22 @@
         ),
         name="prepare",
     )(place, found_inverse.reshape(2 * local_rows * row_count, block))
-
-    keep_d, send_d, keep_t, send_t, term = pl.pallas_call(
+    term = pl.pallas_call(
+        weigh_kernel,
+        in_specs=[SMEM_SPEC, VMEM_SPEC, pl.BlockSpec(memory_space=pl.ANY)],
+        out_specs=VMEM_SPEC,
+        out_shape=jax.ShapeDtypeStruct((total_cols, slot), F32),
+        compiler_params=PARAMS,
+        name="weigh",
+    )(pole_weights, diag_inverse[0], own[-1])
+    terms = lax.all_gather(term, "pole", axis=0)
+
+    keep_d, send_d, keep_t, send_t = pl.pallas_call(
         functools.partial(compute_kernel, (row_count, col_count), supernodes, slot),
-        in_specs=[SMEM_SPEC] * 3 + [VMEM_SPEC] * (2 + row_count + col_count),
-        out_specs=[VMEM_SPEC] * 5,
+        in_specs=[SMEM_SPEC] * 3 + [VMEM_SPEC] * (1 + row_count + col_count),
+        out_specs=[VMEM_SPEC] * 4,
         out_shape=[jax.ShapeDtypeStruct((half, local_rows), F32)] * 2
-        + [jax.ShapeDtypeStruct((half, slot), F32)] * 2
-        + [jax.ShapeDtypeStruct((total_cols * slot // (col_count * local_rows), local_rows), F32)],
+        + [jax.ShapeDtypeStruct((half, slot), F32)] * 2,
         scratch_shapes=[
             pltpu.VMEM((local_rows // slot, packed_width + slot, slot), F32),
             pltpu.VMEM((local_rows // slot, packed_width + slot, slot), F32),
@@ -281,22 +286,25 @@
         compiler_params=PARAMS,
         name="compute",
     )(
-        sup_widths, pole_weights, place, straight, diag_inverse[0],
+        sup_widths, pole_weights, place, straight,
         *[blocks[shift] for shift in range(row_count)], *own,
     )
 
-    products = scatter_rest(keep_t + swap(send_t, "col", top), "col")
-    density = scatter_rest(keep_d + swap(send_d, "col", top), "col")
-    products = jnp.concatenate(pole_sum(products), axis=1)
+    tie = lax.optimization_barrier
+    products, send_d = tie((keep_t + swap(send_t, "col", top), send_d))
+    products = scatter_rest(products, "col")
     for bit in bits_of(row_count):
         products = products + swap(products, "row", bit)
-    density = jnp.concatenate(pole_sum(jnp.concatenate([density, term], axis=0)), axis=0)
+    density = scatter_rest(keep_d + swap(send_d, "col", top), "col")
+    density = sum_direct(density, "pole")
+    products, density, terms = tie((products, density, terms))
+    products = sum_direct(products, "pole")
     density = gather_but_last(density, "col")
     products = gather_but_last(products, "col")
 
     return pl.pallas_call(
         functools.partial(expand_kernel, col_count, slot),
-        in_specs=[SMEM_SPEC] * 2 + [VMEM_SPEC] * 4,
+        in_specs=[SMEM_SPEC] * 2 + [VMEM_SPEC] * 5,
         out_specs=[VMEM_SPEC] * 2,
         out_shape=[
             jax.ShapeDtypeStruct((total_cols // col_count, local_rows), F32),
@@ -307,7 +315,7 @@
         name="expand",
     )(
         sup_widths, place, density, swap(density, "col", top),
-        products, swap(products, "col", top),
+        products, swap(products, "col", top), terms,
     )
 
 

time: 54.7 us -> 68.1 us (1.24)
  between operations: 0.82 us -> 14.1 us
  starting transfers between devices: 24.9 us -> 17.7 us
  waiting for transfers between devices: 19.9 us -> 25.4 us
  Pallas kernels: 5.97 us -> 8.33 us
    ppermute x15 -> x13, starting transfers between devices: 18.3 us -> 11.7 us  [swap(): lax.ppermute(value, axis, [(i, i ^ bit) for i in range(lax.axis_size(axis...]
    ppermute x3, waiting for transfers between devices: 7.87 us -> 12.1 us  [per_device(): blocks[shift] = lax.ppermute(packed, 'row', pairs)]
    pallas_call x0 -> x1, Pallas kernels: none -> 1.29 us  [per_device(): pl.pallas_call(weigh_kernel, in_specs=[SMEM_SPEC, VMEM_SPEC, pl.BlockSpec...]
    ppermute x15 -> x13, waiting for transfers between devices: 12.1 us -> 13.3 us  [swap(): lax.ppermute(value, axis, [(i, i ^ bit) for i in range(lax.axis_size(axis...]
    pallas_call x1, Pallas kernels: 0.87 us -> 1.99 us  [per_device(): pl.pallas_call(functools.partial(pack_kernel, supernodes, slot), in_specs...]
  transfers between devices with their start and end apart: 18 -> 17, of which waited for: 8 -> 12; matrix products, arithmetic and copies ran while one was open for 0% -> 0% of each run, Pallas kernels for 2% -> 5%
where the time goes in v6:
time: 68.1 us; the launch traced here: 67.9 us
  waiting for transfers between devices  25.4 us (37%)
  starting transfers between devices  17.7 us (26%)
  between operations  14.1 us (21%)
  Pallas kernels  8.33 us (12%)
  local copies, waits for them, and re-layouts  2.13 us (3%)
    ppermute x13, waiting for transfers between devices, swap(): lax.ppermute(value, axis, [(i, i ^ bit) for i in range(lax.axis_size(axis...  13.3 us
    ppermute x3, waiting for transfers between devices, per_device(): blocks[shift] = lax.ppermute(packed, 'row', pairs)  12.1 us
    ppermute x13, starting transfers between devices, swap(): lax.ppermute(value, axis, [(i, i ^ bit) for i in range(lax.axis_size(axis...  11.7 us
    ppermute x3, starting transfers between devices, per_device(): blocks[shift] = lax.ppermute(packed, 'row', pairs)  5.98 us
    pallas_call x1, Pallas kernels, per_device(): pl.pallas_call(functools.partial(compute_kernel, (row_count, col_count),...  2.61 us
    unnamed x12, local copies, waits for them, and re-layouts  2.13 us
    pallas_call x1, Pallas kernels, per_device(): pl.pallas_call(functools.partial(pack_kernel, supernodes, slot), in_specs...  1.99 us
    pallas_call x1, Pallas kernels, per_device(): pl.pallas_call(functools.partial(expand_kernel, col_count, slot), in_spec...  1.45 us
  transfers between devices with their start and end apart: 17, of which 12 were waited for; matrix products, arithmetic and copies ran while one was open for 0% of the time, Pallas kernels for 5%

profile of v6, /device:TPU:0, one launch (start us, length us, event | category | flops | bytes accessed | tf_op | source)
XLA Modules:
  0.0 67.9 jit_solution(13091579953285032870)
XLA Ops:
  7.2 0.0 copy-start.3
  7.2 0.0 all-gather.3.cloned.1.call-start
  7.2 0.0 copy-start.5
  7.2 2.0 %pack.1.refs_0_.refs_4_ = bf16[640,128]{1,0:T(8,128)(2,1)} custom-call(s32[1,4]{1,0:T(1,128)} %pattern_ref.1, s32[4]{0:T(128)} %widths_ref.5, bf16[2,128,512]{2,1,0:T(8,128)(2,1)} %bitcast.9), custom_call_target="tpu_custom_call" | custom-call | tf_op jit(solution)/shard_map/pack/pallas_call | solution.py:239
  9.2 0.0 copy-start.2
  9.2 0.5 collective-permute-start.3
  9.7 1.2 %collective-permute-done.3.refs_5_.packed_ref = bf16[640,128]{1,0:T(8,128)(2,1)S(1)} collective-permute-done((bf16[640,128]{1,0:T(8,128)(2,1)}, bf16[640,128]{1,0:T(8,128)(2,1)S(1)}, u32[]{:S(2)}, u32[]{:S(2)}) %collective-permute-start.3) | collective-permute-done | bytes 163872 | tf_op jit(solution)/shard_map/ppermute | solution.py:192
  10.9 0.0 copy-done.3
  10.9 0.0 copy-done.5
  10.9 1.3 %weigh.1 = f32[512,128]{1,0:T(8,128)} custom-call(f32[1,2]{1,0:T(1,128)S(1)} %copy-done.5, bf16[2,512,128]{2,1,0:T(8,128)(2,1)S(1)} %bitcast.8, bf16[640,128]{1,0:T(8,128)(2,1)S(1)} %collective-permute-done.3.refs_5_.packed_ref), custom_call_target="tpu_custom_call" | custom-call | tf_op jit(solution)/shard_map/weigh/pallas_call | solution.py:266
  12.2 0.0 copy-start
  12.2 0.0 all-gather.3.cloned.1.call-update
  12.2 0.9 %copy-done = bf16[640,128]{1,0:T(8,128)(2,1)S(1)} copy-done((bf16[640,128]{1,0:T(8,128)(2,1)S(1)}, bf16[640,128]{1,0:T(8,128)(2,1)}, u32[]{:S(2)}) %copy-start) | copy-done | bytes 163864
  13.1 5.0 %collective-permute-start = (bf16[640,128]{1,0:T(8,128)(2,1)S(1)}, bf16[640,128]{1,0:T(8,128)(2,1)S(1)}, u32[]{:S(2)}, u32[]{:S(2)}) collective-permute-start(bf16[640,128]{1,0:T(8,128)(2,1)S(1)} %copy-done), channel_id=1, source_target_pairs={{2,0},{4,2},{6,4},{0,6},{3,1},{5,3},{7,5},{1,7},{10,8},{12,10},{14... | collective-permute-start | bytes 491528 | tf_op jit(solution)/shard_map/ppermute | solution.py:250
  18.1 0.0 collective-permute-start.1
  18.1 1.0 %collective-permute-start.2 = (bf16[640,128]{1,0:T(8,128)(2,1)S(1)}, bf16[640,128]{1,0:T(8,128)(2,1)S(1)}, u32[]{:S(2)}, u32[]{:S(2)}) collective-permute-start(bf16[640,128]{1,0:T(8,128)(2,1)S(1)} %copy-done), channel_id=1, source_target_pairs={{6,0},{0,2},{2,4},{4,6},{7,1},{1,3},{3,5},{5,7},{14,8},{8,10},{10,... | collective-permute-start | bytes 491528 | tf_op jit(solution)/shard_map/ppermute | solution.py:250
  19.1 0.1 pad_add_fusion.place_ref
  19.2 0.0 copy-done.2
  19.2 0.0 copy-start.4
  19.2 1.0 %prepare.1.straight_ref = bf16[2,256,512]{2,1,0:T(8,128)(2,1)S(1)} custom-call(s32[2]{0:T(128)S(1)} %pad_add_fusion.place_ref, bf16[2048,128]{1,0:T(8,128)(2,1)S(1)} %bitcast.7), custom_call_target="tpu_custom_call" | custom-call | flops 134217728 | bytes 1048576 | tf_op jit(solution)/shard_map/prepare/pallas_call | solution.py:253
  20.2 2.6 %collective-permute-done.refs_1_ = bf16[640,128]{1,0:T(8,128)(2,1)S(1)} collective-permute-done((bf16[640,128]{1,0:T(8,128)(2,1)S(1)}, bf16[640,128]{1,0:T(8,128)(2,1)S(1)}, u32[]{:S(2)}, u32[]{:S(2)}) %collective-permute-start) | collective-permute-done | bytes 163872 | tf_op jit(solution)/shard_map/ppermute | solution.py:250
  22.7 9.5 %collective-permute-done.1.refs_2_ = bf16[640,128]{1,0:T(8,128)(2,1)S(1)} collective-permute-done((bf16[640,128]{1,0:T(8,128)(2,1)S(1)}, bf16[640,128]{1,0:T(8,128)(2,1)S(1)}, u32[]{:S(2)}, u32[]{:S(2)}) %collective-permute-start.1) | collective-permute-done | bytes 163872 | tf_op jit(solution)/shard_map/ppermute | solution.py:250
  32.3 0.0 collective-permute-done.2.refs_3_
  32.3 0.0 copy-done.4
  32.3 2.6 %compute.1 = (f32[160,256]{1,0:T(8,128)S(1)}, f32[160,256]{1,0:T(8,128)S(1)}, f32[160,128]{1,0:T(8,128)S(1)}, f32[160,128]{1,0:T(8,128)S(1)}) custom-call(s32[4]{0:T(128)S(1)} %copy-done.4, f32[1,2]{1,0:T(1,128)S(1)} %copy-done.5, s32[2]{0:T(128)S(1)} %pad_add_fusion.place_ref, bf16[2,256,512]{2,1,0:T(8,128)(2,1)S(1)} %prepare.1.straight_ref, ...), custom_call_target="tpu_custom_call" | custom-call | tf_op jit(solution)/shard_map/compute/pallas_call | solution.py:276
  34.9 0.1 collective-permute-start.4
  35.0 1.3 %collective-permute-done.4 = f32[160,128]{1,0:T(8,128)S(1)} collective-permute-done((f32[160,128]{1,0:T(8,128)S(1)}, f32[160,128]{1,0:T(8,128)S(1)}, u32[]{:S(2)}, u32[]{:S(2)}) %collective-permute-start.4) | collective-permute-done | bytes 81952 | tf_op jit(solution)/shard_map/ppermute | solution.py:192
  36.3 0.2 collective-permute-start.7
  36.5 0.9 %collective-permute-start.5 = (f32[160,128]{1,0:T(8,128)S(1)}, f32[160,128]{1,0:T(8,128)S(1)}, u32[]{:S(2)}, u32[]{:S(2)}) collective-permute-start(f32[160,128]{1,0:T(8,128)S(1)} %add.30), channel_id=1, source_target_pairs={{0,2},{2,0},{4,6},{6,4},{1,3},{3,1},{5,7},{7,5},{8,10},{10,8},{12,... | collective-permute-start | bytes 245768 | tf_op jit(solution)/shard_map/ppermute | solution.py:192
  37.4 0.4 collective-permute-done.7
  37.8 2.5 %collective-permute-start.10 = (f32[160,256]{1,0:T(8,128)S(1)}, f32[160,256]{1,0:T(8,128)S(1)}, u32[]{:S(2)}, u32[]{:S(2)}) collective-permute-start(f32[160,256]{1,0:T(8,128)S(1)} %add.33), channel_id=1, source_target_pairs={{0,24},{8,16},{16,8},{24,0},{1,25},{9,17},{17,9},{25,1},{2,26},{10... | collective-permute-start | bytes 491528 | tf_op jit(solution)/shard_map/ppermute | solution.py:192
  40.3 0.5 collective-permute-start.8
  40.8 0.5 collective-permute-start.9
  41.3 0.0 collective-permute-done.5
  41.3 2.9 %collective-permute-start.6 = (f32[160,128]{1,0:T(8,128)S(1)}, f32[160,128]{1,0:T(8,128)S(1)}, u32[]{:S(2)}, u32[]{:S(2)}) collective-permute-start(f32[160,128]{1,0:T(8,128)S(1)} %add.31), channel_id=1, source_target_pairs={{0,4},{2,6},{4,0},{6,2},{1,5},{3,7},{5,1},{7,3},{8,12},{10,14},{12... | collective-permute-start | bytes 245768 | tf_op jit(solution)/shard_map/ppermute | solution.py:192
  44.2 3.9 %collective-permute-done.6 = f32[160,128]{1,0:T(8,128)S(1)} collective-permute-done((f32[160,128]{1,0:T(8,128)S(1)}, f32[160,128]{1,0:T(8,128)S(1)}, u32[]{:S(2)}, u32[]{:S(2)}) %collective-permute-start.6) | collective-permute-done | bytes 81952 | tf_op jit(solution)/shard_map/ppermute | solution.py:192
  48.1 0.0 collective-permute-done.10
  48.1 0.5 collective-permute-done.8
  48.6 0.6 collective-permute-done.9
  49.3 0.0 all-gather.3.cloned.1.call-done
  49.3 0.9 %collective-permute-start.12 = (f32[160,128]{1,0:T(8,128)S(1)}, f32[160,128]{1,0:T(8,128)S(1)}, u32[]{:S(2)}, u32[]{:S(2)}) collective-permute-start(f32[160,128]{1,0:T(8,128)S(1)} %add.32), channel_id=1, source_target_pairs={{0,8},{8,0},{16,24},{24,16},{1,9},{9,1},{17,25},{25,17},{2,10},{10... | collective-permute-start | bytes 245768 | tf_op jit(solution)/shard_map/ppermute | solution.py:192
  50.2 1.4 %collective-permute-start.13 = (f32[160,128]{1,0:T(8,128)S(1)}, f32[160,128]{1,0:T(8,128)S(1)}, u32[]{:S(2)}, u32[]{:S(2)}) collective-permute-start(f32[160,128]{1,0:T(8,128)S(1)} %add.32), channel_id=1, source_target_pairs={{0,16},{8,24},{16,0},{24,8},{1,17},{9,25},{17,1},{25,9},{2,18},{10... | collective-permute-start | bytes 245768 | tf_op jit(solution)/shard_map/ppermute | solution.py:192
  51.6 1.2 %collective-permute-start.14 = (f32[160,128]{1,0:T(8,128)S(1)}, f32[160,128]{1,0:T(8,128)S(1)}, u32[]{:S(2)}, u32[]{:S(2)}) collective-permute-start(f32[160,128]{1,0:T(8,128)S(1)} %add.32), channel_id=1, source_target_pairs={{0,24},{8,16},{16,8},{24,0},{1,25},{9,17},{17,9},{25,1},{2,26},{10... | collective-permute-start | bytes 245768 | tf_op jit(solution)/shard_map/ppermute | solution.py:192
  52.8 0.0 collective-permute-start.11
  52.9 1.2 %collective-permute-done.12 = f32[160,128]{1,0:T(8,128)S(1)} collective-permute-done((f32[160,128]{1,0:T(8,128)S(1)}, f32[160,128]{1,0:T(8,128)S(1)}, u32[]{:S(2)}, u32[]{:S(2)}) %collective-permute-start.12) | collective-permute-done | bytes 81952 | tf_op jit(solution)/shard_map/ppermute | solution.py:192
  54.0 0.7 collective-permute-done.13
  54.7 2.3 %collective-permute-done.14 = f32[160,128]{1,0:T(8,128)S(1)} collective-permute-done((f32[160,128]{1,0:T(8,128)S(1)}, f32[160,128]{1,0:T(8,128)S(1)}, u32[]{:S(2)}, u32[]{:S(2)}) %collective-permute-start.14) | collective-permute-done | bytes 81952 | tf_op jit(solution)/shard_map/ppermute | solution.py:192
  57.0 0.1 collective-permute-start.15
  57.1 1.3 %collective-permute-done.15.other_t_ref = f32[160,128]{1,0:T(8,128)S(1)} collective-permute-done((f32[160,128]{1,0:T(8,128)S(1)}, f32[160,128]{1,0:T(8,128)S(1)}, u32[]{:S(2)}, u32[]{:S(2)}) %collective-permute-start.15) | collective-permute-done | bytes 81952 | tf_op jit(solution)/shard_map/ppermute | solution.py:192
  58.3 0.0 collective-permute-done.11.other_d_ref
  58.3 0.0 copy-start.1
  58.4 1.2 %copy-done.1 = f32[2048,128]{1,0:T(8,128)S(1)} copy-done((f32[2048,128]{1,0:T(8,128)S(1)}, f32[2048,128]{1,0:T(8,128)}, u32[]{:S(2)}) %copy-start.1) | copy-done | bytes 1048600
  59.6 1.5 %expand.1 = (f32[256,256]{1,0:T(8,128)}, f32[512,128]{1,0:T(8,128)}) custom-call(s32[4]{0:T(128)S(1)} %copy-done.4, s32[2]{0:T(128)S(1)} %pad_add_fusion.place_ref, f32[160,256]{1,0:T(8,128)S(1)} %add_add_fusion.mine_d_ref, f32[160,256]{1,0:T(8,128)S(1)} %collective-permute-done.11.other_d_ref, f32[160,128]{1,0:T(8,128)S(1)} %add_add_fusion.1.mine_t_ref, ...), custom_call_target="tpu_custom_call" | custom-call | tf_op jit(solution)/shard_map/expand/pallas_call | solution.py:305
  (6 shorter events, 0.1 us)
Async XLA Ops:
  7.2 3.8 %copy-start.3 = (bf16[1,2,512,128]{3,2,1,0:T(8,128)(2,1)S(1)}, bf16[1,2,512,128]{3,2,1,0:T(8,128)(2,1)}, u32[]{:S(2)}) copy-start(bf16[1,2,512,128]{3,2,1,0:T(8,128)(2,1)} %param.10) | copy-start | bytes 786436
  7.2 42.1 %all-gather.3.cloned.1.call-start = ((), (), s32[]{:S(2)}) async-start(), calls=%async_computation | async-start | bytes 1310720 | tf_op jit(solution)/shard_map/all_gather | solution.py:274
  7.2 3.7 %copy-start.5 = (f32[1,2]{1,0:T(1,128)S(1)}, f32[1,2]{1,0:T(1,128)}, u32[]{:S(2)}) copy-start(f32[1,2]{1,0:T(1,128)} %weights_ref.3) | copy-start | bytes 28
  9.2 10.0 %copy-start.2 = (bf16[1,2,256,4,1,128]{5,3,4,2,1,0:T(4,128)(2,1)S(1)}, bf16[1,2,256,4,1,128]{5,3,4,2,1,0:T(4,128)(2,1)}, u32[]{:S(2)}) copy-start(bf16[1,2,256,4,1,128]{5,3,4,2,1,0:T(4,128)(2,1)} %param.6) | copy-start | bytes 1572868
  9.2 1.7 %collective-permute-start.3 = (bf16[640,128]{1,0:T(8,128)(2,1)}, bf16[640,128]{1,0:T(8,128)(2,1)S(1)}, u32[]{:S(2)}, u32[]{:S(2)}) collective-permute-start(bf16[640,128]{1,0:T(8,128)(2,1)} %pack.1.refs_0_.refs_4_), channel_id=1, source_target_pairs={{0,1},{1,0},{2,3},{3,2},{4,5},{5,4},{6,7},{7,6},{8,9},{9,8},{10,11... | collective-permute-start | bytes 491528 | tf_op jit(solution)/shard_map/ppermute | solution.py:192
  12.2 0.9 %copy-start = (bf16[640,128]{1,0:T(8,128)(2,1)S(1)}, bf16[640,128]{1,0:T(8,128)(2,1)}, u32[]{:S(2)}) copy-start(bf16[640,128]{1,0:T(8,128)(2,1)} %pack.1.refs_0_.refs_4_) | copy-start | bytes 491524
  13.1 9.6 %collective-permute-start = (bf16[640,128]{1,0:T(8,128)(2,1)S(1)}, bf16[640,128]{1,0:T(8,128)(2,1)S(1)}, u32[]{:S(2)}, u32[]{:S(2)}) collective-permute-start(bf16[640,128]{1,0:T(8,128)(2,1)S(1)} %copy-done), channel_id=1, source_target_pairs={{2,0},{4,2},{6,4},{0,6},{3,1},{5,3},{7,5},{1,7},{10,8},{12,10},{14... | collective-permute-start | bytes 491528 | tf_op jit(solution)/shard_map/ppermute | solution.py:250
  18.1 14.2 %collective-permute-start.1 = (bf16[640,128]{1,0:T(8,128)(2,1)S(1)}, bf16[640,128]{1,0:T(8,128)(2,1)S(1)}, u32[]{:S(2)}, u32[]{:S(2)}) collective-permute-start(bf16[640,128]{1,0:T(8,128)(2,1)S(1)} %copy-done), channel_id=1, source_target_pairs={{4,0},{6,2},{0,4},{2,6},{5,1},{7,3},{1,5},{3,7},{12,8},{14,10},{8,... | collective-permute-start | bytes 491528 | tf_op jit(solution)/shard_map/ppermute | solution.py:250
  18.1 14.2 %collective-permute-start.2 = (bf16[640,128]{1,0:T(8,128)(2,1)S(1)}, bf16[640,128]{1,0:T(8,128)(2,1)S(1)}, u32[]{:S(2)}, u32[]{:S(2)}) collective-permute-start(bf16[640,128]{1,0:T(8,128)(2,1)S(1)} %copy-done), channel_id=1, source_target_pairs={{6,0},{0,2},{2,4},{4,6},{7,1},{1,3},{3,5},{5,7},{14,8},{8,10},{10,... | collective-permute-start | bytes 491528 | tf_op jit(solution)/shard_map/ppermute | solution.py:250
  19.2 13.1 %copy-start.4 = (s32[4]{0:T(128)S(1)}, s32[4]{0:T(128)}, u32[]{:S(2)}) copy-start(s32[4]{0:T(128)} %widths_ref.5) | copy-start | bytes 52
  34.9 1.3 %collective-permute-start.4 = (f32[160,128]{1,0:T(8,128)S(1)}, f32[160,128]{1,0:T(8,128)S(1)}, u32[]{:S(2)}, u32[]{:S(2)}) collective-permute-start(f32[160,128]{1,0:T(8,128)S(1)} %get-tuple-element.12), channel_id=1, source_target_pairs={{0,1},{1,0},{2,3},{3,2},{4,5},{5,4},{6,7},{7,6},{8,9},{9,8},{10,11... | collective-permute-start | bytes 245768 | tf_op jit(solution)/shard_map/ppermute | solution.py:192
  36.3 1.5 %collective-permute-start.7 = (f32[160,256]{1,0:T(8,128)S(1)}, f32[160,256]{1,0:T(8,128)S(1)}, u32[]{:S(2)}, u32[]{:S(2)}) collective-permute-start(f32[160,256]{1,0:T(8,128)S(1)} %get-tuple-element.16), channel_id=1, source_target_pairs={{0,1},{1,0},{2,3},{3,2},{4,5},{5,4},{6,7},{7,6},{8,9},{9,8},{10,11... | collective-permute-start | bytes 491528 | tf_op jit(solution)/shard_map/ppermute | solution.py:192
  36.5 4.8 %collective-permute-start.5 = (f32[160,128]{1,0:T(8,128)S(1)}, f32[160,128]{1,0:T(8,128)S(1)}, u32[]{:S(2)}, u32[]{:S(2)}) collective-permute-start(f32[160,128]{1,0:T(8,128)S(1)} %add.30), channel_id=1, source_target_pairs={{0,2},{2,0},{4,6},{6,4},{1,3},{3,1},{5,7},{7,5},{8,10},{10,8},{12,... | collective-permute-start | bytes 245768 | tf_op jit(solution)/shard_map/ppermute | solution.py:192
  37.8 10.4 %collective-permute-start.10 = (f32[160,256]{1,0:T(8,128)S(1)}, f32[160,256]{1,0:T(8,128)S(1)}, u32[]{:S(2)}, u32[]{:S(2)}) collective-permute-start(f32[160,256]{1,0:T(8,128)S(1)} %add.33), channel_id=1, source_target_pairs={{0,24},{8,16},{16,8},{24,0},{1,25},{9,17},{17,9},{25,1},{2,26},{10... | collective-permute-start | bytes 491528 | tf_op jit(solution)/shard_map/ppermute | solution.py:192
  40.3 8.3 %collective-permute-start.8 = (f32[160,256]{1,0:T(8,128)S(1)}, f32[160,256]{1,0:T(8,128)S(1)}, u32[]{:S(2)}, u32[]{:S(2)}) collective-permute-start(f32[160,256]{1,0:T(8,128)S(1)} %add.33), channel_id=1, source_target_pairs={{0,8},{8,0},{16,24},{24,16},{1,9},{9,1},{17,25},{25,17},{2,10},{10... | collective-permute-start | bytes 491528 | tf_op jit(solution)/shard_map/ppermute | solution.py:192
  40.8 8.4 %collective-permute-start.9 = (f32[160,256]{1,0:T(8,128)S(1)}, f32[160,256]{1,0:T(8,128)S(1)}, u32[]{:S(2)}, u32[]{:S(2)}) collective-permute-start(f32[160,256]{1,0:T(8,128)S(1)} %add.33), channel_id=1, source_target_pairs={{0,16},{8,24},{16,0},{24,8},{1,17},{9,25},{17,1},{25,9},{2,18},{10... | collective-permute-start | bytes 491528 | tf_op jit(solution)/shard_map/ppermute | solution.py:192
  41.3 6.8 %collective-permute-start.6 = (f32[160,128]{1,0:T(8,128)S(1)}, f32[160,128]{1,0:T(8,128)S(1)}, u32[]{:S(2)}, u32[]{:S(2)}) collective-permute-start(f32[160,128]{1,0:T(8,128)S(1)} %add.31), channel_id=1, source_target_pairs={{0,4},{2,6},{4,0},{6,2},{1,5},{3,7},{5,1},{7,3},{8,12},{10,14},{12... | collective-permute-start | bytes 245768 | tf_op jit(solution)/shard_map/ppermute | solution.py:192
  49.3 4.7 %collective-permute-start.12 = (f32[160,128]{1,0:T(8,128)S(1)}, f32[160,128]{1,0:T(8,128)S(1)}, u32[]{:S(2)}, u32[]{:S(2)}) collective-permute-start(f32[160,128]{1,0:T(8,128)S(1)} %add.32), channel_id=1, source_target_pairs={{0,8},{8,0},{16,24},{24,16},{1,9},{9,1},{17,25},{25,17},{2,10},{10... | collective-permute-start | bytes 245768 | tf_op jit(solution)/shard_map/ppermute | solution.py:192
  50.2 4.5 %collective-permute-start.13 = (f32[160,128]{1,0:T(8,128)S(1)}, f32[160,128]{1,0:T(8,128)S(1)}, u32[]{:S(2)}, u32[]{:S(2)}) collective-permute-start(f32[160,128]{1,0:T(8,128)S(1)} %add.32), channel_id=1, source_target_pairs={{0,16},{8,24},{16,0},{24,8},{1,17},{9,25},{17,1},{25,9},{2,18},{10... | collective-permute-start | bytes 245768 | tf_op jit(solution)/shard_map/ppermute | solution.py:192
  51.6 5.3 %collective-permute-start.14 = (f32[160,128]{1,0:T(8,128)S(1)}, f32[160,128]{1,0:T(8,128)S(1)}, u32[]{:S(2)}, u32[]{:S(2)}) collective-permute-start(f32[160,128]{1,0:T(8,128)S(1)} %add.32), channel_id=1, source_target_pairs={{0,24},{8,16},{16,8},{24,0},{1,25},{9,17},{17,9},{25,1},{2,26},{10... | collective-permute-start | bytes 245768 | tf_op jit(solution)/shard_map/ppermute | solution.py:192
  52.8 5.5 %collective-permute-start.11 = (f32[160,256]{1,0:T(8,128)S(1)}, f32[160,256]{1,0:T(8,128)S(1)}, u32[]{:S(2)}, u32[]{:S(2)}) collective-permute-start(f32[160,256]{1,0:T(8,128)S(1)} %add_add_fusion.mine_d_ref), channel_id=1, source_target_pairs={{0,1},{1,0},{2,3},{3,2},{4,5},{5,4},{6,7},{7,6},{8,9},{9,8},{10,11... | collective-permute-start | bytes 491528 | tf_op jit(solution)/shard_map/ppermute | solution.py:192
  57.0 1.3 %collective-permute-start.15 = (f32[160,128]{1,0:T(8,128)S(1)}, f32[160,128]{1,0:T(8,128)S(1)}, u32[]{:S(2)}, u32[]{:S(2)}) collective-permute-start(f32[160,128]{1,0:T(8,128)S(1)} %add_add_fusion.1.mine_t_ref), channel_id=1, source_target_pairs={{0,1},{1,0},{2,3},{3,2},{4,5},{5,4},{6,7},{7,6},{8,9},{9,8},{10,11... | collective-permute-start | bytes 245768 | tf_op jit(solution)/shard_map/ppermute | solution.py:192
  58.3 1.2 %copy-start.1 = (f32[2048,128]{1,0:T(8,128)S(1)}, f32[2048,128]{1,0:T(8,128)}, u32[]{:S(2)}) copy-start(f32[2048,128]{1,0:T(8,128)} %all-gather.3.cloned.1.call-done) | copy-start | bytes 3145732
Sparse Core Ops, SparseCore 0:
  12.4 29.2 all-gather.2

commit v7 on v3

--- a/solution.py
+++ b/solution.py
@@ -135,7 +135,7 @@
 
 
 def expand_kernel(
-    col_count, slot, widths_ref, place_ref, mine_d_ref, other_d_ref, mine_t_ref, other_t_ref,
+    pole_count, col_count, slot, widths_ref, place_ref, mine_d_ref, other_d_ref, mine_t_ref, other_t_ref,
     density_ref, diagonal_ref, strip_ref,
 ):
     supernodes = diagonal_ref.shape[0] // slot
@@ -159,9 +159,14 @@
                 strip_ref[s, base:base + part] = d_value[q * tall:q * tall + part, lanes]
                 first = (owner * strips + s) * folded
                 diagonal_ref[first:first + folded] = d_value[q * tall + part:(q + 1) * tall, lanes]
-            rows = slice(q * part // 2, (q + 1) * part // 2)
-            strip_ref[strips, base:base + part // 2] = t_value[rows, :slot]
-            strip_ref[strips, base + part // 2:base + part] = t_value[rows, slot:]
+            step = part // pole_count
+            for j in range(pole_count):
+                first = base + (place_ref[2] ^ j) * step
+                if step % 8 == 0:
+                    first = pl.multiple_of(first, 8)
+                strip_ref[strips, pl.ds(first, step), :] = t_value[
+                    q * part + j * step:q * part + (j + 1) * step
+                ]
     for s in range(strips + 1):
         strip_ref[s, col_count * part:] = jnp.zeros((slot, slot), F32)
     offsets = offsets_of(widths_ref, supernodes)
@@ -195,13 +200,28 @@
     return lax.ppermute(value, axis, [(i, i ^ bit) for i in range(lax.axis_size(axis))])
 
 
-def pole_sum(value):
-    bits = bits_of(lax.axis_size("pole"))
+def halves_of(value):
     half = value.shape[0] // 2
-    first, second = value[:half], value[half:]
-    for bit, mirrored in zip(bits, bits[::-1]):
-        first, second = first + swap(first, "pole", bit), second + swap(second, "pole", mirrored)
-    return first, second
+    return value[:half], value[half:]
+
+
+def tree_sum(terms):
+    while len(terms) > 1:
+        terms = [terms[j] + terms[j + 1] for j in range(0, len(terms), 2)]
+    return terms[0]
+
+
+def scatter_sum(value, axis):
+    count = lax.axis_size(axis)
+    index = lax.axis_index(axis)
+    shares = value.reshape(count, value.shape[0] // count, value.shape[1])
+    shares = [lax.dynamic_index_in_dim(shares, index ^ j, 0, False) for j in range(count)]
+    return tree_sum([shares[0]] + [swap(shares[j], axis, j) for j in range(1, count)])
+
+
+def gather_direct(share, axis):
+    others = [swap(share, axis, j) for j in range(1, lax.axis_size(axis))]
+    return jnp.concatenate([share] + others, axis=0)
 
 
 def scatter_rest(value, axis):
@@ -236,14 +256,13 @@
     row_count = lax.axis_size("row")
     col_count = lax.axis_size("col")
     top = col_count // 2
-    place = jnp.stack([lax.axis_index("row"), lax.axis_index("col")]).astype(jnp.int32)
+    place = jnp.stack([lax.axis_index(axis) for axis in ("row", "col", "pole")]).astype(jnp.int32)
 
     packed = pl.pallas_call(
         functools.partial(pack_kernel, supernodes, slot),
         in_specs=[SMEM_SPEC, SMEM_SPEC, VMEM_SPEC],
         out_specs=VMEM_SPEC,
         out_shape=jax.ShapeDtypeStruct((2 * packed_width, block), BF16),
-        compiler_params=PARAMS,
         name="pack",
     )(block_pattern, sup_widths, l_panel[0])
 
@@ -285,17 +304,27 @@
         *[blocks[shift] for shift in range(row_count)], *own,
     )
 
+    tie = lax.optimization_barrier
     products = scatter_rest(keep_t + swap(send_t, "col", top), "col")
     density = scatter_rest(keep_d + swap(send_d, "col", top), "col")
-    products = jnp.concatenate(pole_sum(products), axis=1)
+    low, high = halves_of(jnp.concatenate([density, term], axis=0))
+    products, low, high = tie((products, low, high))
+    bits = bits_of(lax.axis_size("pole"))
+    for step, bit in enumerate(bits):
+        low, high = low + swap(low, "pole", bit), high + swap(high, "pole", bits[-1 - step])
+        if step == 0:
+            products = scatter_sum(products, "pole")
+            products, low, high = tie((products, low, high))
     for bit in bits_of(row_count):
         products = products + swap(products, "row", bit)
-    density = jnp.concatenate(pole_sum(jnp.concatenate([density, term], axis=0)), axis=0)
+    products, low, high = tie((products, low, high))
+    density = jnp.concatenate([low, high], axis=0)
+    products = gather_direct(products, "pole")
     density = gather_but_last(density, "col")
     products = gather_but_last(products, "col")
 
     return pl.pallas_call(
-        functools.partial(expand_kernel, col_count, slot),
+        functools.partial(expand_kernel, lax.axis_size("pole"), col_count, slot),
         in_specs=[SMEM_SPEC] * 2 + [VMEM_SPEC] * 4,
         out_specs=[VMEM_SPEC] * 2,
         out_shape=[

time: 54.7 us -> 56.7 us (1.037)
  waiting for transfers between devices: 19.9 us -> 24.7 us
  starting transfers between devices: 24.9 us -> 22.6 us
  local copies, waits for them, and re-layouts: 2.67 us -> 1.11 us
  Pallas kernels: 5.97 us -> 7.07 us
    ppermute x3, waiting for transfers between devices: 7.87 us -> 10.9 us  [per_device(): blocks[shift] = lax.ppermute(packed, 'row', pairs)]
    ppermute x15 -> x17, starting transfers between devices: 18.3 us -> 16.6 us  [swap(): lax.ppermute(value, axis, [(i, i ^ bit) for i in range(lax.axis_size(axis...]
    ppermute x15 -> x17, waiting for transfers between devices: 12.1 us -> 13.7 us  [swap(): lax.ppermute(value, axis, [(i, i ^ bit) for i in range(lax.axis_size(axis...]
    unnamed x12 -> x14, local copies, waits for them, and re-layouts: 2.66 us -> 1.08 us
    pallas_call x1, Pallas kernels: 0.87 us -> 1.96 us  [per_device(): pl.pallas_call(functools.partial(pack_kernel, supernodes, slot), in_specs...]
  transfers between devices with their start and end apart: 18 -> 20, of which waited for: 8 -> 12; matrix products, arithmetic and copies ran while one was open for 0% -> 0% of each run, Pallas kernels for 2% -> 2%
where the time goes in v7:
time: 56.7 us; the launch traced here: 56.5 us
  waiting for transfers between devices  24.7 us (44%)
  starting transfers between devices  22.6 us (40%)
  Pallas kernels  7.07 us (12%)
  local copies, waits for them, and re-layouts  1.11 us (2%)
  between operations  0.81 us (1%)
    ppermute x17, starting transfers between devices, swap(): lax.ppermute(value, axis, [(i, i ^ bit) for i in range(lax.axis_size(axis...  16.6 us
    ppermute x17, waiting for transfers between devices, swap(): lax.ppermute(value, axis, [(i, i ^ bit) for i in range(lax.axis_size(axis...  13.7 us
    ppermute x3, waiting for transfers between devices, per_device(): blocks[shift] = lax.ppermute(packed, 'row', pairs)  10.9 us
    ppermute x3, starting transfers between devices, per_device(): blocks[shift] = lax.ppermute(packed, 'row', pairs)  6.06 us
    pallas_call x1, Pallas kernels, per_device(): pl.pallas_call(functools.partial(compute_kernel, (row_count, col_count),...  2.63 us
    pallas_call x1, Pallas kernels, per_device(): pl.pallas_call(functools.partial(pack_kernel, supernodes, slot), in_specs...  1.96 us
    pallas_call x1, Pallas kernels, per_device(): pl.pallas_call(functools.partial(expand_kernel, lax.axis_size('pole'), co...  1.49 us
  transfers between devices with their start and end apart: 20, of which 12 were waited for; matrix products, arithmetic and copies ran while one was open for 0% of the time, Pallas kernels for 2%

profile of v7, /device:TPU:0, one launch (start us, length us, event | category | flops | bytes accessed | tf_op | source)
XLA Modules:
  0.0 56.5 jit_solution(8506739501483833019)
XLA Ops:
  0.6 2.0 %pack.1.refs_0_.refs_4_ = bf16[640,128]{1,0:T(8,128)(2,1)} custom-call(s32[1,4]{1,0:T(1,128)} %pattern_ref.1, s32[4]{0:T(128)} %widths_ref.5, bf16[2,128,512]{2,1,0:T(8,128)(2,1)} %bitcast.21), custom_call_target="tpu_custom_call" | custom-call | tf_op jit(solution)/shard_map/pack/pallas_call | solution.py:261
  2.6 5.0 %collective-permute-start = (bf16[640,128]{1,0:T(8,128)(2,1)}, bf16[640,128]{1,0:T(8,128)(2,1)S(1)}, u32[]{:S(2)}, u32[]{:S(2)}) collective-permute-start(bf16[640,128]{1,0:T(8,128)(2,1)} %pack.1.refs_0_.refs_4_), channel_id=1, source_target_pairs={{2,0},{4,2},{6,4},{0,6},{3,1},{5,3},{7,5},{1,7},{10,8},{12,10},{14... | collective-permute-start | bytes 491528 | tf_op jit(solution)/shard_map/ppermute | solution.py:272
  7.6 0.0 collective-permute-start.1
  7.6 1.0 %collective-permute-start.2 = (bf16[640,128]{1,0:T(8,128)(2,1)}, bf16[640,128]{1,0:T(8,128)(2,1)S(1)}, u32[]{:S(2)}, u32[]{:S(2)}) collective-permute-start(bf16[640,128]{1,0:T(8,128)(2,1)} %pack.1.refs_0_.refs_4_), channel_id=1, source_target_pairs={{6,0},{0,2},{2,4},{4,6},{7,1},{1,3},{3,5},{5,7},{14,8},{8,10},{10,... | collective-permute-start | bytes 491528 | tf_op jit(solution)/shard_map/ppermute | solution.py:272
  8.7 0.0 collective-permute-start.3
  8.7 0.1 pad_add_fusion.place_ref
  8.7 0.0 copy-start.1
  8.7 1.0 %copy-done.1 = bf16[1,2,256,4,1,128]{5,3,4,2,1,0:T(4,128)(2,1)S(1)} copy-done((bf16[1,2,256,4,1,128]{5,3,4,2,1,0:T(4,128)(2,1)S(1)}, bf16[1,2,256,4,1,128]{5,3,4,2,1,0:T(4,128)(2,1)}, u32[]{:S(2)}) %copy-start.1) | copy-done | bytes 524312
  9.8 0.0 copy-start
  9.8 0.0 copy-start.2
  9.8 1.0 %prepare.1.straight_ref = bf16[2,256,512]{2,1,0:T(8,128)(2,1)S(1)} custom-call(s32[3]{0:T(128)S(1)} %pad_add_fusion.place_ref, bf16[2048,128]{1,0:T(8,128)(2,1)S(1)} %bitcast.17), custom_call_target="tpu_custom_call" | custom-call | flops 134217728 | bytes 1048576 | tf_op jit(solution)/shard_map/prepare/pallas_call | solution.py:275
  10.8 0.0 copy-start.3
  10.8 0.0 copy-start.4
  10.8 1.8 %collective-permute-done.refs_1_ = bf16[640,128]{1,0:T(8,128)(2,1)S(1)} collective-permute-done((bf16[640,128]{1,0:T(8,128)(2,1)}, bf16[640,128]{1,0:T(8,128)(2,1)S(1)}, u32[]{:S(2)}, u32[]{:S(2)}) %collective-permute-start) | collective-permute-done | bytes 163872 | tf_op jit(solution)/shard_map/ppermute | solution.py:272
  12.6 9.1 %collective-permute-done.1.refs_2_ = bf16[640,128]{1,0:T(8,128)(2,1)S(1)} collective-permute-done((bf16[640,128]{1,0:T(8,128)(2,1)}, bf16[640,128]{1,0:T(8,128)(2,1)S(1)}, u32[]{:S(2)}, u32[]{:S(2)}) %collective-permute-start.1) | collective-permute-done | bytes 163872 | tf_op jit(solution)/shard_map/ppermute | solution.py:272
  21.7 0.0 collective-permute-done.2.refs_3_
  21.7 0.0 collective-permute-done.3.refs_5_
  21.7 0.0 copy-done
  21.7 0.0 copy-done.2
  21.8 0.0 copy-done.3
  21.8 0.0 copy-done.4
  21.8 2.6 %compute.1 = (f32[160,256]{1,0:T(8,128)S(1)}, f32[160,256]{1,0:T(8,128)S(1)}, f32[160,128]{1,0:T(8,128)S(1)}, f32[160,128]{1,0:T(8,128)S(1)}, f32[128,256]{1,0:T(8,128)S(1)}) custom-call(s32[4]{0:T(128)S(1)} %copy-done.3, f32[1,2]{1,0:T(1,128)S(1)} %copy-done.4, s32[3]{0:T(128)S(1)} %pad_add_fusion.place_ref, bf16[2,256,512]{2,1,0:T(8,128)(2,1)S(1)} %prepare.1.straight_ref, ...), custom_call_target="tpu_custom_call" | custom-call | tf_op jit(solution)/shard_map/compute/pallas_call | solution.py:289
  24.4 0.1 collective-permute-start.5
  24.5 0.5 collective-permute-start.4
  25.0 1.0 %collective-permute-done.4 = f32[160,128]{1,0:T(8,128)S(1)} collective-permute-done((f32[160,128]{1,0:T(8,128)S(1)}, f32[160,128]{1,0:T(8,128)S(1)}, u32[]{:S(2)}, u32[]{:S(2)}) %collective-permute-start.4) | collective-permute-done | bytes 81952 | tf_op jit(solution)/shard_map/ppermute | solution.py:200
  26.0 0.0 collective-permute-done.5
  26.1 1.6 %collective-permute-start.6 = (f32[40,128]{1,0:T(8,128)S(1)}, f32[40,128]{1,0:T(8,128)S(1)}, u32[]{:S(2)}, u32[]{:S(2)}) collective-permute-start(f32[40,128]{1,0:T(8,128)S(1)} %get-tuple-element.34), channel_id=1, source_target_pairs={{0,8},{8,0},{16,24},{24,16},{1,9},{9,1},{17,25},{25,17},{2,10},{10... | collective-permute-start | bytes 61448 | tf_op jit(solution)/shard_map/ppermute | solution.py:200
  27.7 1.5 %collective-permute-start.7 = (f32[40,128]{1,0:T(8,128)S(1)}, f32[40,128]{1,0:T(8,128)S(1)}, u32[]{:S(2)}, u32[]{:S(2)}) collective-permute-start(f32[40,128]{1,0:T(8,128)S(1)} %get-tuple-element.33), channel_id=1, source_target_pairs={{0,16},{8,24},{16,0},{24,8},{1,17},{9,25},{17,1},{25,9},{2,18},{10... | collective-permute-start | bytes 61448 | tf_op jit(solution)/shard_map/ppermute | solution.py:200
  29.2 0.5 collective-permute-start.8
  29.7 1.5 %collective-permute-start.10 = (f32[144,256]{1,0:T(8,128)S(1)}, f32[144,256]{1,0:T(8,128)S(1)}, u32[]{:S(2)}, u32[]{:S(2)}) collective-permute-start(f32[144,256]{1,0:T(8,128)S(1)} %get-tuple-element.23), channel_id=1, source_target_pairs={{0,16},{8,24},{16,0},{24,8},{1,17},{9,25},{17,1},{25,9},{2,18},{10... | collective-permute-start | bytes 442376 | tf_op jit(solution)/shard_map/ppermute | solution.py:200
  31.2 1.5 %collective-permute-start.9 = (f32[144,256]{1,0:T(8,128)S(1)}, f32[144,256]{1,0:T(8,128)S(1)}, u32[]{:S(2)}, u32[]{:S(2)}) collective-permute-start(f32[144,256]{1,0:T(8,128)S(1)} %get-tuple-element.22), channel_id=1, source_target_pairs={{0,8},{8,0},{16,24},{24,16},{1,9},{9,1},{17,25},{25,17},{2,10},{10... | collective-permute-start | bytes 442376 | tf_op jit(solution)/shard_map/ppermute | solution.py:200
  32.7 0.0 collective-permute-done.6
  32.7 0.0 collective-permute-done.7
  32.7 1.4 %collective-permute-done.8 = f32[40,128]{1,0:T(8,128)S(1)} collective-permute-done((f32[40,128]{1,0:T(8,128)S(1)}, f32[40,128]{1,0:T(8,128)S(1)}, u32[]{:S(2)}, u32[]{:S(2)}) %collective-permute-start.8) | collective-permute-done | bytes 20512 | tf_op jit(solution)/shard_map/ppermute | solution.py:200
  34.1 1.2 %collective-permute-done.10 = f32[144,256]{1,0:T(8,128)S(1)} collective-permute-done((f32[144,256]{1,0:T(8,128)S(1)}, f32[144,256]{1,0:T(8,128)S(1)}, u32[]{:S(2)}, u32[]{:S(2)}) %collective-permute-start.10) | collective-permute-done | bytes 147488 | tf_op jit(solution)/shard_map/ppermute | solution.py:200
  35.3 1.0 %collective-permute-done.9 = f32[144,256]{1,0:T(8,128)S(1)} collective-permute-done((f32[144,256]{1,0:T(8,128)S(1)}, f32[144,256]{1,0:T(8,128)S(1)}, u32[]{:S(2)}, u32[]{:S(2)}) %collective-permute-start.9) | collective-permute-done | bytes 147488 | tf_op jit(solution)/shard_map/ppermute | solution.py:200
  36.3 1.6 %collective-permute-start.14 = (f32[144,256]{1,0:T(8,128)S(1)}, f32[144,256]{1,0:T(8,128)S(1)}, u32[]{:S(2)}, u32[]{:S(2)}) collective-permute-start(f32[144,256]{1,0:T(8,128)S(1)} %add.56), channel_id=1, source_target_pairs={{0,8},{8,0},{16,24},{24,16},{1,9},{9,1},{17,25},{25,17},{2,10},{10... | collective-permute-start | bytes 442376 | tf_op jit(solution)/shard_map/ppermute | solution.py:200
  37.9 0.5 collective-permute-start.13
  38.4 1.0 %collective-permute-start.11 = (f32[40,128]{1,0:T(8,128)S(1)}, f32[40,128]{1,0:T(8,128)S(1)}, u32[]{:S(2)}, u32[]{:S(2)}) collective-permute-start(f32[40,128]{1,0:T(8,128)S(1)} %fusion), channel_id=1, source_target_pairs={{0,2},{2,0},{4,6},{6,4},{1,3},{3,1},{5,7},{7,5},{8,10},{10,8},{12,... | collective-permute-start | bytes 61448 | tf_op jit(solution)/shard_map/ppermute | solution.py:200
  39.4 2.8 %collective-permute-done.11 = f32[40,128]{1,0:T(8,128)S(1)} collective-permute-done((f32[40,128]{1,0:T(8,128)S(1)}, f32[40,128]{1,0:T(8,128)S(1)}, u32[]{:S(2)}, u32[]{:S(2)}) %collective-permute-start.11) | collective-permute-done | bytes 20512 | tf_op jit(solution)/shard_map/ppermute | solution.py:200
  42.2 2.8 %collective-permute-start.12 = (f32[40,128]{1,0:T(8,128)S(1)}, f32[40,128]{1,0:T(8,128)S(1)}, u32[]{:S(2)}, u32[]{:S(2)}) collective-permute-start(f32[40,128]{1,0:T(8,128)S(1)} %add.57), channel_id=1, source_target_pairs={{0,4},{2,6},{4,0},{6,2},{1,5},{3,7},{5,1},{7,3},{8,12},{10,14},{12... | collective-permute-start | bytes 61448 | tf_op jit(solution)/shard_map/ppermute | solution.py:200
  45.0 1.9 %collective-permute-done.12 = f32[40,128]{1,0:T(8,128)S(1)} collective-permute-done((f32[40,128]{1,0:T(8,128)S(1)}, f32[40,128]{1,0:T(8,128)S(1)}, u32[]{:S(2)}, u32[]{:S(2)}) %collective-permute-start.12) | collective-permute-done | bytes 20512 | tf_op jit(solution)/shard_map/ppermute | solution.py:200
  46.9 0.0 collective-permute-done.14
  46.9 0.0 collective-permute-done.13
  47.0 0.6 %collective-permute-start.16 = (f32[40,128]{1,0:T(8,128)S(1)}, f32[40,128]{1,0:T(8,128)S(1)}, u32[]{:S(2)}, u32[]{:S(2)}) collective-permute-start(f32[40,128]{1,0:T(8,128)S(1)} %add.58), channel_id=1, source_target_pairs={{0,8},{8,0},{16,24},{24,16},{1,9},{9,1},{17,25},{25,17},{2,10},{10... | collective-permute-start | bytes 61448 | tf_op jit(solution)/shard_map/ppermute | solution.py:200
  47.6 1.5 %collective-permute-start.17 = (f32[40,128]{1,0:T(8,128)S(1)}, f32[40,128]{1,0:T(8,128)S(1)}, u32[]{:S(2)}, u32[]{:S(2)}) collective-permute-start(f32[40,128]{1,0:T(8,128)S(1)} %add.58), channel_id=1, source_target_pairs={{0,16},{8,24},{16,0},{24,8},{1,17},{9,25},{17,1},{25,9},{2,18},{10... | collective-permute-start | bytes 61448 | tf_op jit(solution)/shard_map/ppermute | solution.py:200
  49.1 1.4 %collective-permute-start.18 = (f32[40,128]{1,0:T(8,128)S(1)}, f32[40,128]{1,0:T(8,128)S(1)}, u32[]{:S(2)}, u32[]{:S(2)}) collective-permute-start(f32[40,128]{1,0:T(8,128)S(1)} %add.58), channel_id=1, source_target_pairs={{0,24},{8,16},{16,8},{24,0},{1,25},{9,17},{17,9},{25,1},{2,26},{10... | collective-permute-start | bytes 61448 | tf_op jit(solution)/shard_map/ppermute | solution.py:200
  50.5 0.1 collective-permute-start.15
  50.6 0.2 collective-permute-done.16
  50.8 0.5 collective-permute-done.17
  51.3 2.4 %collective-permute-done.18 = f32[40,128]{1,0:T(8,128)S(1)} collective-permute-done((f32[40,128]{1,0:T(8,128)S(1)}, f32[40,128]{1,0:T(8,128)S(1)}, u32[]{:S(2)}, u32[]{:S(2)}) %collective-permute-start.18) | collective-permute-done | bytes 20512 | tf_op jit(solution)/shard_map/ppermute | solution.py:200
  53.8 0.0 collective-permute-start.19
  53.8 1.3 %collective-permute-done.19.other_t_ref = f32[160,128]{1,0:T(8,128)S(1)} collective-permute-done((f32[160,128]{1,0:T(8,128)S(1)}, f32[160,128]{1,0:T(8,128)S(1)}, u32[]{:S(2)}, u32[]{:S(2)}) %collective-permute-start.19) | collective-permute-done | bytes 81952 | tf_op jit(solution)/shard_map/ppermute | solution.py:200
  55.0 0.0 collective-permute-done.15.other_d_ref
  55.0 1.5 %expand.1 = (f32[256,256]{1,0:T(8,128)}, f32[512,128]{1,0:T(8,128)}) custom-call(s32[4]{0:T(128)S(1)} %copy-done.3, s32[3]{0:T(128)S(1)} %pad_add_fusion.place_ref, f32[288,256]{1,0:T(8,128)S(1)} %constant_dynamic-update-slice_fusion.mine_d_ref, f32[288,256]{1,0:T(8,128)S(1)} %collective-permute-done.15.other_d_ref, ...), custom_call_target="tpu_custom_call" | custom-call | tf_op jit(solution)/shard_map/expand/pallas_call | solution.py:326
  (17 shorter events, 0.2 us)
Async XLA Ops:
  2.6 10.0 %collective-permute-start = (bf16[640,128]{1,0:T(8,128)(2,1)}, bf16[640,128]{1,0:T(8,128)(2,1)S(1)}, u32[]{:S(2)}, u32[]{:S(2)}) collective-permute-start(bf16[640,128]{1,0:T(8,128)(2,1)} %pack.1.refs_0_.refs_4_), channel_id=1, source_target_pairs={{2,0},{4,2},{6,4},{0,6},{3,1},{5,3},{7,5},{1,7},{10,8},{12,10},{14... | collective-permute-start | bytes 491528 | tf_op jit(solution)/shard_map/ppermute | solution.py:272
  7.6 14.1 %collective-permute-start.1 = (bf16[640,128]{1,0:T(8,128)(2,1)}, bf16[640,128]{1,0:T(8,128)(2,1)S(1)}, u32[]{:S(2)}, u32[]{:S(2)}) collective-permute-start(bf16[640,128]{1,0:T(8,128)(2,1)} %pack.1.refs_0_.refs_4_), channel_id=1, source_target_pairs={{4,0},{6,2},{0,4},{2,6},{5,1},{7,3},{1,5},{3,7},{12,8},{14,10},{8,... | collective-permute-start | bytes 491528 | tf_op jit(solution)/shard_map/ppermute | solution.py:272
  7.6 14.1 %collective-permute-start.2 = (bf16[640,128]{1,0:T(8,128)(2,1)}, bf16[640,128]{1,0:T(8,128)(2,1)S(1)}, u32[]{:S(2)}, u32[]{:S(2)}) collective-permute-start(bf16[640,128]{1,0:T(8,128)(2,1)} %pack.1.refs_0_.refs_4_), channel_id=1, source_target_pairs={{6,0},{0,2},{2,4},{4,6},{7,1},{1,3},{3,5},{5,7},{14,8},{8,10},{10,... | collective-permute-start | bytes 491528 | tf_op jit(solution)/shard_map/ppermute | solution.py:272
  8.7 13.1 %collective-permute-start.3 = (bf16[640,128]{1,0:T(8,128)(2,1)}, bf16[640,128]{1,0:T(8,128)(2,1)S(1)}, u32[]{:S(2)}, u32[]{:S(2)}) collective-permute-start(bf16[640,128]{1,0:T(8,128)(2,1)} %pack.1.refs_0_.refs_4_), channel_id=1, source_target_pairs={{0,1},{1,0},{2,3},{3,2},{4,5},{5,4},{6,7},{7,6},{8,9},{9,8},{10,11... | collective-permute-start | bytes 491528 | tf_op jit(solution)/shard_map/ppermute | solution.py:200
  8.7 1.0 %copy-start.1 = (bf16[1,2,256,4,1,128]{5,3,4,2,1,0:T(4,128)(2,1)S(1)}, bf16[1,2,256,4,1,128]{5,3,4,2,1,0:T(4,128)(2,1)}, u32[]{:S(2)}) copy-start(bf16[1,2,256,4,1,128]{5,3,4,2,1,0:T(4,128)(2,1)} %param.6) | copy-start | bytes 1572868
  9.8 12.0 %copy-start = (bf16[640,128]{1,0:T(8,128)(2,1)S(1)}, bf16[640,128]{1,0:T(8,128)(2,1)}, u32[]{:S(2)}) copy-start(bf16[640,128]{1,0:T(8,128)(2,1)} %pack.1.refs_0_.refs_4_) | copy-start | bytes 491524
  9.8 12.0 %copy-start.2 = (bf16[1,2,512,128]{3,2,1,0:T(8,128)(2,1)S(1)}, bf16[1,2,512,128]{3,2,1,0:T(8,128)(2,1)}, u32[]{:S(2)}) copy-start(bf16[1,2,512,128]{3,2,1,0:T(8,128)(2,1)} %param.10) | copy-start | bytes 786436
  10.8 11.0 %copy-start.3 = (s32[4]{0:T(128)S(1)}, s32[4]{0:T(128)}, u32[]{:S(2)}) copy-start(s32[4]{0:T(128)} %widths_ref.5) | copy-start | bytes 52
  10.8 11.0 %copy-start.4 = (f32[1,2]{1,0:T(1,128)S(1)}, f32[1,2]{1,0:T(1,128)}, u32[]{:S(2)}) copy-start(f32[1,2]{1,0:T(1,128)} %weights_ref.1) | copy-start | bytes 28
  24.4 1.6 %collective-permute-start.5 = (f32[160,256]{1,0:T(8,128)S(1)}, f32[160,256]{1,0:T(8,128)S(1)}, u32[]{:S(2)}, u32[]{:S(2)}) collective-permute-start(f32[160,256]{1,0:T(8,128)S(1)} %get-tuple-element.19), channel_id=1, source_target_pairs={{0,1},{1,0},{2,3},{3,2},{4,5},{5,4},{6,7},{7,6},{8,9},{9,8},{10,11... | collective-permute-start | bytes 491528 | tf_op jit(solution)/shard_map/ppermute | solution.py:200
  24.5 1.5 %collective-permute-start.4 = (f32[160,128]{1,0:T(8,128)S(1)}, f32[160,128]{1,0:T(8,128)S(1)}, u32[]{:S(2)}, u32[]{:S(2)}) collective-permute-start(f32[160,128]{1,0:T(8,128)S(1)} %get-tuple-element.17), channel_id=1, source_target_pairs={{0,1},{1,0},{2,3},{3,2},{4,5},{5,4},{6,7},{7,6},{8,9},{9,8},{10,11... | collective-permute-start | bytes 245768 | tf_op jit(solution)/shard_map/ppermute | solution.py:200
  26.1 6.6 %collective-permute-start.6 = (f32[40,128]{1,0:T(8,128)S(1)}, f32[40,128]{1,0:T(8,128)S(1)}, u32[]{:S(2)}, u32[]{:S(2)}) collective-permute-start(f32[40,128]{1,0:T(8,128)S(1)} %get-tuple-element.34), channel_id=1, source_target_pairs={{0,8},{8,0},{16,24},{24,16},{1,9},{9,1},{17,25},{25,17},{2,10},{10... | collective-permute-start | bytes 61448 | tf_op jit(solution)/shard_map/ppermute | solution.py:200
  27.7 5.0 %collective-permute-start.7 = (f32[40,128]{1,0:T(8,128)S(1)}, f32[40,128]{1,0:T(8,128)S(1)}, u32[]{:S(2)}, u32[]{:S(2)}) collective-permute-start(f32[40,128]{1,0:T(8,128)S(1)} %get-tuple-element.33), channel_id=1, source_target_pairs={{0,16},{8,24},{16,0},{24,8},{1,17},{9,25},{17,1},{25,9},{2,18},{10... | collective-permute-start | bytes 61448 | tf_op jit(solution)/shard_map/ppermute | solution.py:200
  29.2 4.9 %collective-permute-start.8 = (f32[40,128]{1,0:T(8,128)S(1)}, f32[40,128]{1,0:T(8,128)S(1)}, u32[]{:S(2)}, u32[]{:S(2)}) collective-permute-start(f32[40,128]{1,0:T(8,128)S(1)} %get-tuple-element.32), channel_id=1, source_target_pairs={{0,24},{8,16},{16,8},{24,0},{1,25},{9,17},{17,9},{25,1},{2,26},{10... | collective-permute-start | bytes 61448 | tf_op jit(solution)/shard_map/ppermute | solution.py:200
  29.7 5.6 %collective-permute-start.10 = (f32[144,256]{1,0:T(8,128)S(1)}, f32[144,256]{1,0:T(8,128)S(1)}, u32[]{:S(2)}, u32[]{:S(2)}) collective-permute-start(f32[144,256]{1,0:T(8,128)S(1)} %get-tuple-element.23), channel_id=1, source_target_pairs={{0,16},{8,24},{16,0},{24,8},{1,17},{9,25},{17,1},{25,9},{2,18},{10... | collective-permute-start | bytes 442376 | tf_op jit(solution)/shard_map/ppermute | solution.py:200
  31.2 5.1 %collective-permute-start.9 = (f32[144,256]{1,0:T(8,128)S(1)}, f32[144,256]{1,0:T(8,128)S(1)}, u32[]{:S(2)}, u32[]{:S(2)}) collective-permute-start(f32[144,256]{1,0:T(8,128)S(1)} %get-tuple-element.22), channel_id=1, source_target_pairs={{0,8},{8,0},{16,24},{24,16},{1,9},{9,1},{17,25},{25,17},{2,10},{10... | collective-permute-start | bytes 442376 | tf_op jit(solution)/shard_map/ppermute | solution.py:200
  36.3 10.5 %collective-permute-start.14 = (f32[144,256]{1,0:T(8,128)S(1)}, f32[144,256]{1,0:T(8,128)S(1)}, u32[]{:S(2)}, u32[]{:S(2)}) collective-permute-start(f32[144,256]{1,0:T(8,128)S(1)} %add.56), channel_id=1, source_target_pairs={{0,8},{8,0},{16,24},{24,16},{1,9},{9,1},{17,25},{25,17},{2,10},{10... | collective-permute-start | bytes 442376 | tf_op jit(solution)/shard_map/ppermute | solution.py:200
  37.9 9.0 %collective-permute-start.13 = (f32[144,256]{1,0:T(8,128)S(1)}, f32[144,256]{1,0:T(8,128)S(1)}, u32[]{:S(2)}, u32[]{:S(2)}) collective-permute-start(f32[144,256]{1,0:T(8,128)S(1)} %add.55), channel_id=1, source_target_pairs={{0,16},{8,24},{16,0},{24,8},{1,17},{9,25},{17,1},{25,9},{2,18},{10... | collective-permute-start | bytes 442376 | tf_op jit(solution)/shard_map/ppermute | solution.py:200
  38.4 3.8 %collective-permute-start.11 = (f32[40,128]{1,0:T(8,128)S(1)}, f32[40,128]{1,0:T(8,128)S(1)}, u32[]{:S(2)}, u32[]{:S(2)}) collective-permute-start(f32[40,128]{1,0:T(8,128)S(1)} %fusion), channel_id=1, source_target_pairs={{0,2},{2,0},{4,6},{6,4},{1,3},{3,1},{5,7},{7,5},{8,10},{10,8},{12,... | collective-permute-start | bytes 61448 | tf_op jit(solution)/shard_map/ppermute | solution.py:200
  42.2 4.7 %collective-permute-start.12 = (f32[40,128]{1,0:T(8,128)S(1)}, f32[40,128]{1,0:T(8,128)S(1)}, u32[]{:S(2)}, u32[]{:S(2)}) collective-permute-start(f32[40,128]{1,0:T(8,128)S(1)} %add.57), channel_id=1, source_target_pairs={{0,4},{2,6},{4,0},{6,2},{1,5},{3,7},{5,1},{7,3},{8,12},{10,14},{12... | collective-permute-start | bytes 61448 | tf_op jit(solution)/shard_map/ppermute | solution.py:200
  47.0 3.8 %collective-permute-start.16 = (f32[40,128]{1,0:T(8,128)S(1)}, f32[40,128]{1,0:T(8,128)S(1)}, u32[]{:S(2)}, u32[]{:S(2)}) collective-permute-start(f32[40,128]{1,0:T(8,128)S(1)} %add.58), channel_id=1, source_target_pairs={{0,8},{8,0},{16,24},{24,16},{1,9},{9,1},{17,25},{25,17},{2,10},{10... | collective-permute-start | bytes 61448 | tf_op jit(solution)/shard_map/ppermute | solution.py:200
  47.6 3.8 %collective-permute-start.17 = (f32[40,128]{1,0:T(8,128)S(1)}, f32[40,128]{1,0:T(8,128)S(1)}, u32[]{:S(2)}, u32[]{:S(2)}) collective-permute-start(f32[40,128]{1,0:T(8,128)S(1)} %add.58), channel_id=1, source_target_pairs={{0,16},{8,24},{16,0},{24,8},{1,17},{9,25},{17,1},{25,9},{2,18},{10... | collective-permute-start | bytes 61448 | tf_op jit(solution)/shard_map/ppermute | solution.py:200
  49.1 4.7 %collective-permute-start.18 = (f32[40,128]{1,0:T(8,128)S(1)}, f32[40,128]{1,0:T(8,128)S(1)}, u32[]{:S(2)}, u32[]{:S(2)}) collective-permute-start(f32[40,128]{1,0:T(8,128)S(1)} %add.58), channel_id=1, source_target_pairs={{0,24},{8,16},{16,8},{24,0},{1,25},{9,17},{17,9},{25,1},{2,26},{10... | collective-permute-start | bytes 61448 | tf_op jit(solution)/shard_map/ppermute | solution.py:200
  50.5 4.5 %collective-permute-start.15 = (f32[288,256]{1,0:T(8,128)S(1)}, f32[288,256]{1,0:T(8,128)S(1)}, u32[]{:S(2)}, u32[]{:S(2)}) collective-permute-start(f32[288,256]{1,0:T(8,128)S(1)} %constant_dynamic-update-slice_fusion.mine_d_ref), channel_id=1, source_target_pairs={{0,1},{1,0},{2,3},{3,2},{4,5},{5,4},{6,7},{7,6},{8,9},{9,8},{10,11... | collective-permute-start | bytes 884744 | tf_op jit(solution)/shard_map/ppermute | solution.py:200
  53.8 1.3 %collective-permute-start.19 = (f32[160,128]{1,0:T(8,128)S(1)}, f32[160,128]{1,0:T(8,128)S(1)}, u32[]{:S(2)}, u32[]{:S(2)}) collective-permute-start(f32[160,128]{1,0:T(8,128)S(1)} %constant_dynamic-update-slice_fusion.2.mine_t_ref), channel_id=1, source_target_pairs={{0,1},{1,0},{2,3},{3,2},{4,5},{5,4},{6,7},{7,6},{8,9},{9,8},{10,11... | collective-permute-start | bytes 245768 | tf_op jit(solution)/shard_map/ppermute | solution.py:200

commit v8 on v6

--- a/solution.py
+++ b/solution.py
@@ -42,7 +42,9 @@
         ).astype(BF16)
 
 
-def prepare_kernel(row_count, place_ref, inverse_ref, straight_ref):
+def prepare_kernel(
+    row_count, weights_ref, place_ref, inverse_ref, diag_ref, straight_ref, term_ref
+):
     block = inverse_ref.shape[1]
     local_rows = straight_ref.shape[1]
     row_index = place_ref[0]
@@ -61,13 +63,11 @@
                 straight_ref[
                     part, chunk * group:(chunk + 1) * group, owner * block:(owner + 1) * block
                 ] = sorted_rows[owner * group:(owner + 1) * group]
-
-
-def weigh_kernel(weights_ref, diag_ref, packed_ref, term_ref):
-    del packed_ref
-    term_ref[...] = weights_ref[0, 0] * diag_ref[0].astype(F32) - weights_ref[
-        0, 1
-    ] * diag_ref[1].astype(F32)
+    per_col = term_ref.shape[0]
+    first = pl.multiple_of(place_ref[1] * per_col, per_col)
+    term_ref[...] = weights_ref[0, 0] * diag_ref[0, pl.ds(first, per_col), :].astype(
+        F32
+    ) - weights_ref[0, 1] * diag_ref[1, pl.ds(first, per_col), :].astype(F32)
 
 
 def compute_kernel(
@@ -136,7 +136,7 @@
 
 def expand_kernel(
     col_count, slot, widths_ref, place_ref, mine_d_ref, other_d_ref, mine_t_ref, other_t_ref,
-    term_ref, density_ref, diagonal_ref, strip_ref,
+    mine_term_ref, other_term_ref, density_ref, diagonal_ref, strip_ref,
 ):
     supernodes = diagonal_ref.shape[0] // slot
     per_col, local_rows = density_ref.shape
@@ -149,6 +149,10 @@
         own_side = upper if side else jnp.logical_not(upper)
         d_value = jnp.where(own_side, mine_d_ref[...], other_d_ref[...])
         t_value = jnp.where(own_side, mine_t_ref[...], other_t_ref[...])
+        rows = mine_term_ref.shape[0]
+        diagonal_ref[side * rows:(side + 1) * rows] = jnp.where(
+            own_side, mine_term_ref[...], other_term_ref[...]
+        )
         for q in range(share):
             owner = side * share + q
             base = owner * part
@@ -163,10 +167,7 @@
     for k in range(supernodes):
         product = strip_ref[strips, pl.ds(offsets[k], slot), :]
         product = jnp.where(row_in_slot < widths_ref[k], product, 0.0)
-        diagonal_ref[k * slot:(k + 1) * slot] = (
-            tree_sum([term_ref[p, k * slot:(k + 1) * slot] for p in range(term_ref.shape[0])])
-            - product
-        )
+        diagonal_ref[k * slot:(k + 1) * slot] -= product
     size = min(per_col, slot)
     row_in_part = lax.broadcasted_iota(jnp.int32, (size, 1), 0)
     for part in range(per_col // size):
@@ -250,11 +251,14 @@
         blocks[shift] = lax.ppermute(packed, "row", pairs)
     own = [packed] + [swap(packed, "col", other) for other in range(1, col_count)]
 
-    straight = pl.pallas_call(
+    straight, term = pl.pallas_call(
         functools.partial(prepare_kernel, row_count),
-        in_specs=[SMEM_SPEC, VMEM_SPEC],
-        out_specs=VMEM_SPEC,
-        out_shape=jax.ShapeDtypeStruct((2, local_rows, row_count * block), BF16),
+        in_specs=[SMEM_SPEC] * 2 + [VMEM_SPEC] * 2,
+        out_specs=[VMEM_SPEC] * 2,
+        out_shape=[
+            jax.ShapeDtypeStruct((2, local_rows, row_count * block), BF16),
+            jax.ShapeDtypeStruct((total_cols // col_count, slot), F32),
+        ],
         compiler_params=PARAMS,
         cost_estimate=pl.CostEstimate(
             flops=4 * 256 * local_rows * row_count * block,
@@ -262,16 +266,13 @@
             transcendentals=0,
         ),
         name="prepare",
-    )(place, found_inverse.reshape(2 * local_rows * row_count, block))
-    term = pl.pallas_call(
-        weigh_kernel,
-        in_specs=[SMEM_SPEC, VMEM_SPEC, pl.BlockSpec(memory_space=pl.ANY)],
-        out_specs=VMEM_SPEC,
-        out_shape=jax.ShapeDtypeStruct((total_cols, slot), F32),
-        compiler_params=PARAMS,
-        name="weigh",
-    )(pole_weights, diag_inverse[0], own[-1])
-    terms = lax.all_gather(term, "pole", axis=0)
+    )(
+        pole_weights, place, found_inverse.reshape(2 * local_rows * row_count, block),
+        diag_inverse[0],
+    )
+    first_arrival = min(blocks, key=lambda shift: (shift == 0, -min(shift, row_count - shift)))
+    term, blocks[first_arrival] = lax.optimization_barrier((term, blocks[first_arrival]))
+    term = sum_direct(term, "pole")
 
     keep_d, send_d, keep_t, send_t = pl.pallas_call(
         functools.partial(compute_kernel, (row_count, col_count), supernodes, slot),
@@ -291,20 +292,21 @@
     )
 
     tie = lax.optimization_barrier
-    products, send_d = tie((keep_t + swap(send_t, "col", top), send_d))
+    products, send_d, term = tie((keep_t + swap(send_t, "col", top), send_d, term))
+    term = gather_but_last(term, "col")
     products = scatter_rest(products, "col")
     for bit in bits_of(row_count):
         products = products + swap(products, "row", bit)
     density = scatter_rest(keep_d + swap(send_d, "col", top), "col")
     density = sum_direct(density, "pole")
-    products, density, terms = tie((products, density, terms))
+    products, density = tie((products, density))
     products = sum_direct(products, "pole")
     density = gather_but_last(density, "col")
     products = gather_but_last(products, "col")
 
     return pl.pallas_call(
         functools.partial(expand_kernel, col_count, slot),
-        in_specs=[SMEM_SPEC] * 2 + [VMEM_SPEC] * 5,
+        in_specs=[SMEM_SPEC] * 2 + [VMEM_SPEC] * 6,
         out_specs=[VMEM_SPEC] * 2,
         out_shape=[
             jax.ShapeDtypeStruct((total_cols // col_count, local_rows), F32),
@@ -315,7 +317,7 @@
         name="expand",
     )(
         sup_widths, place, density, swap(density, "col", top),
-        products, swap(products, "col", top), terms,
+        products, swap(products, "col", top), term, swap(term, "col", top),
     )
 
 

time: 68.1 us -> 49.8 us (0.73)
  between operations: 14.1 us -> 0.76 us
  waiting for transfers between devices: 25.4 us -> 19.4 us
  starting transfers between devices: 17.7 us -> 20.4 us
  Pallas kernels: 8.33 us -> 7.11 us
    ppermute x3, waiting for transfers between devices: 12.1 us -> 5.71 us  [per_device(): blocks[shift] = lax.ppermute(packed, 'row', pairs)]
    ppermute x3, starting transfers between devices: 5.98 us -> 7.86 us  [per_device(): blocks[shift] = lax.ppermute(packed, 'row', pairs)]
    pallas_call x1 -> x0, Pallas kernels: 1.29 us -> none  [per_device(): pl.pallas_call(weigh_kernel, in_specs=[SMEM_SPEC, VMEM_SPEC, pl.BlockSpec...]
    ppermute x13 -> x17, starting transfers between devices: 11.7 us -> 12.6 us  [swap(): lax.ppermute(value, axis, [(i, i ^ bit) for i in range(lax.axis_size(axis...]
    unnamed x12 -> x10, local copies, waits for them, and re-layouts: 2.13 us -> 1.7 us
    ppermute x13 -> x17, waiting for transfers between devices: 13.3 us -> 13.7 us  [swap(): lax.ppermute(value, axis, [(i, i ^ bit) for i in range(lax.axis_size(axis...]
  transfers between devices with their start and end apart: 17 -> 20, of which waited for: 12 -> 12; matrix products, arithmetic and copies ran while one was open for 0% -> 0% of each run, Pallas kernels for 5% -> 7%
where the time goes in v8:
time: 49.8 us; the launch traced here: 49.6 us
  starting transfers between devices  20.4 us (41%)
  waiting for transfers between devices  19.4 us (39%)
  Pallas kernels  7.11 us (14%)
  local copies, waits for them, and re-layouts  1.7 us (3%)
  between operations  0.76 us (2%)
    ppermute x17, waiting for transfers between devices, swap(): lax.ppermute(value, axis, [(i, i ^ bit) for i in range(lax.axis_size(axis...  13.7 us
    ppermute x17, starting transfers between devices, swap(): lax.ppermute(value, axis, [(i, i ^ bit) for i in range(lax.axis_size(axis...  12.6 us
    ppermute x3, starting transfers between devices, per_device(): blocks[shift] = lax.ppermute(packed, 'row', pairs)  7.86 us
    ppermute x3, waiting for transfers between devices, per_device(): blocks[shift] = lax.ppermute(packed, 'row', pairs)  5.71 us
    pallas_call x1, Pallas kernels, per_device(): pl.pallas_call(functools.partial(compute_kernel, (row_count, col_count),...  2.66 us
    pallas_call x1, Pallas kernels, per_device(): pl.pallas_call(functools.partial(pack_kernel, supernodes, slot), in_specs...  2 us
    unnamed x10, local copies, waits for them, and re-layouts  1.7 us
    pallas_call x1, Pallas kernels, per_device(): pl.pallas_call(functools.partial(expand_kernel, col_count, slot), in_spec...  1.45 us
  transfers between devices with their start and end apart: 20, of which 12 were waited for; matrix products, arithmetic and copies ran while one was open for 0% of the time, Pallas kernels for 7%

profile of v8, /device:TPU:0, one launch (start us, length us, event | category | flops | bytes accessed | tf_op | source)
XLA Modules:
  0.0 49.6 jit_solution(9224072022030394618)
XLA Ops:
  0.6 0.0 copy-start.2
  0.6 2.0 %pack.1.refs_0_.refs_4_ = bf16[640,128]{1,0:T(8,128)(2,1)} custom-call(s32[1,4]{1,0:T(1,128)} %pattern_ref.1, s32[4]{0:T(128)} %widths_ref.5, bf16[2,128,512]{2,1,0:T(8,128)(2,1)} %bitcast.7), custom_call_target="tpu_custom_call" | custom-call | tf_op jit(solution)/shard_map/pack/pallas_call | solution.py:240
  2.6 4.0 %collective-permute-start.1 = (bf16[640,128]{1,0:T(8,128)(2,1)}, bf16[640,128]{1,0:T(8,128)(2,1)S(1)}, u32[]{:S(2)}, u32[]{:S(2)}) collective-permute-start(bf16[640,128]{1,0:T(8,128)(2,1)} %pack.1.refs_0_.refs_4_), channel_id=1, source_target_pairs={{4,0},{6,2},{0,4},{2,6},{5,1},{7,3},{1,5},{3,7},{12,8},{14,10},{8,... | collective-permute-start | bytes 491528 | tf_op jit(solution)/shard_map/ppermute | solution.py:251
  6.7 0.0 collective-permute-start.3
  6.7 1.6 %collective-permute-start.2 = (bf16[640,128]{1,0:T(8,128)(2,1)}, bf16[640,128]{1,0:T(8,128)(2,1)S(1)}, u32[]{:S(2)}, u32[]{:S(2)}) collective-permute-start(bf16[640,128]{1,0:T(8,128)(2,1)} %pack.1.refs_0_.refs_4_), channel_id=1, source_target_pairs={{6,0},{0,2},{2,4},{4,6},{7,1},{1,3},{3,5},{5,7},{14,8},{8,10},{10,... | collective-permute-start | bytes 491528 | tf_op jit(solution)/shard_map/ppermute | solution.py:251
  8.3 2.2 %collective-permute-start = (bf16[640,128]{1,0:T(8,128)(2,1)}, bf16[640,128]{1,0:T(8,128)(2,1)S(1)}, u32[]{:S(2)}, u32[]{:S(2)}) collective-permute-start(bf16[640,128]{1,0:T(8,128)(2,1)} %pack.1.refs_0_.refs_4_), channel_id=1, source_target_pairs={{2,0},{4,2},{6,4},{0,6},{3,1},{5,3},{7,5},{1,7},{10,8},{12,10},{14... | collective-permute-start | bytes 491528 | tf_op jit(solution)/shard_map/ppermute | solution.py:251
  10.5 0.1 pad_add_fusion.place_ref
  10.6 0.0 copy-start.4
  10.6 0.0 copy-done.2
  10.6 0.7 %copy-done.4 = f32[1,2]{1,0:T(1,128)S(1)} copy-done((f32[1,2]{1,0:T(1,128)S(1)}, f32[1,2]{1,0:T(1,128)}, u32[]{:S(2)}) %copy-start.4) | copy-done | bytes 32
  11.2 0.0 copy-start.1
  11.2 1.0 %copy-done.1 = bf16[1,2,256,4,1,128]{5,3,4,2,1,0:T(4,128)(2,1)S(1)} copy-done((bf16[1,2,256,4,1,128]{5,3,4,2,1,0:T(4,128)(2,1)S(1)}, bf16[1,2,256,4,1,128]{5,3,4,2,1,0:T(4,128)(2,1)}, u32[]{:S(2)}) %copy-start.1) | copy-done | bytes 524312
  12.3 0.0 copy-start
  12.3 1.0 %prepare.1 = (bf16[2,256,512]{2,1,0:T(8,128)(2,1)S(1)}, f32[256,128]{1,0:T(8,128)S(1)}) custom-call(f32[1,2]{1,0:T(1,128)S(1)} %copy-done.4, s32[2]{0:T(128)S(1)} %pad_add_fusion.place_ref, bf16[2048,128]{1,0:T(8,128)(2,1)S(1)} %bitcast.5, bf16[2,512,128]{2,1,0:T(8,128)(2,1)S(1)} %bitcast.6), custom_call_target="tpu_custom_call" | custom-call | flops 134217728 | bytes 1048576 | tf_op jit(solution)/shard_map/prepare/pallas_call | solution.py:254
  13.3 5.7 %collective-permute-done.1.refs_2_ = bf16[640,128]{1,0:T(8,128)(2,1)S(1)} collective-permute-done((bf16[640,128]{1,0:T(8,128)(2,1)}, bf16[640,128]{1,0:T(8,128)(2,1)S(1)}, u32[]{:S(2)}, u32[]{:S(2)}) %collective-permute-start.1) | collective-permute-done | bytes 163872 | tf_op jit(solution)/shard_map/ppermute | solution.py:251
  19.0 0.0 copy-start.3
  19.0 2.8 %collective-permute-start.7 = (f32[256,128]{1,0:T(8,128)S(1)}, f32[256,128]{1,0:T(8,128)S(1)}, u32[]{:S(2)}, u32[]{:S(2)}) collective-permute-start(f32[256,128]{1,0:T(8,128)S(1)} %get-tuple-element.21), channel_id=1, source_target_pairs={{0,24},{8,16},{16,8},{24,0},{1,25},{9,17},{17,9},{25,1},{2,26},{10... | collective-permute-start | bytes 393224 | tf_op jit(solution)/shard_map/ppermute | solution.py:193
  21.8 0.5 %collective-permute-start.6 = (f32[256,128]{1,0:T(8,128)S(1)}, f32[256,128]{1,0:T(8,128)S(1)}, u32[]{:S(2)}, u32[]{:S(2)}) collective-permute-start(f32[256,128]{1,0:T(8,128)S(1)} %get-tuple-element.21), channel_id=1, source_target_pairs={{0,16},{8,24},{16,0},{24,8},{1,17},{9,25},{17,1},{25,9},{2,18},{10... | collective-permute-start | bytes 393224 | tf_op jit(solution)/shard_map/ppermute | solution.py:193
  22.3 0.0 collective-permute-done.3.refs_5_
  22.3 0.2 collective-permute-start.5
  22.5 0.0 collective-permute-done.2.refs_3_
  22.5 0.0 collective-permute-done.refs_1_
  22.5 0.0 copy-done
  22.5 0.0 copy-done.3
  22.5 2.7 %compute.1 = (f32[160,256]{1,0:T(8,128)S(1)}, f32[160,256]{1,0:T(8,128)S(1)}, f32[160,128]{1,0:T(8,128)S(1)}, f32[160,128]{1,0:T(8,128)S(1)}) custom-call(s32[4]{0:T(128)S(1)} %copy-done.3, f32[1,2]{1,0:T(1,128)S(1)} %copy-done.4, s32[2]{0:T(128)S(1)} %pad_add_fusion.place_ref, bf16[2,256,512]{2,1,0:T(8,128)(2,1)S(1)} %get-tuple-element.15.straight_ref, ...), custom_call_target="tpu_custom_call" | custom-call | tf_op jit(solution)/shard_map/compute/pallas_call | solution.py:277
  25.2 0.1 collective-permute-start.4
  25.2 1.3 %collective-permute-done.4 = f32[160,128]{1,0:T(8,128)S(1)} collective-permute-done((f32[160,128]{1,0:T(8,128)S(1)}, f32[160,128]{1,0:T(8,128)S(1)}, u32[]{:S(2)}, u32[]{:S(2)}) %collective-permute-start.4) | collective-permute-done | bytes 81952 | tf_op jit(solution)/shard_map/ppermute | solution.py:193
  26.5 0.0 collective-permute-done.7
  26.5 0.7 %collective-permute-done.6 = f32[256,128]{1,0:T(8,128)S(1)} collective-permute-done((f32[256,128]{1,0:T(8,128)S(1)}, f32[256,128]{1,0:T(8,128)S(1)}, u32[]{:S(2)}, u32[]{:S(2)}) %collective-permute-start.6) | collective-permute-done | bytes 131104 | tf_op jit(solution)/shard_map/ppermute | solution.py:193
  27.2 0.1 collective-permute-done.5
  27.3 0.1 collective-permute-start.10
  27.4 0.1 collective-permute-start.8
  27.5 1.3 %collective-permute-done.10 = f32[160,256]{1,0:T(8,128)S(1)} collective-permute-done((f32[160,256]{1,0:T(8,128)S(1)}, f32[160,256]{1,0:T(8,128)S(1)}, u32[]{:S(2)}, u32[]{:S(2)}) %collective-permute-start.10) | collective-permute-done | bytes 163872 | tf_op jit(solution)/shard_map/ppermute | solution.py:193
  28.8 2.2 %collective-permute-start.13 = (f32[160,256]{1,0:T(8,128)S(1)}, f32[160,256]{1,0:T(8,128)S(1)}, u32[]{:S(2)}, u32[]{:S(2)}) collective-permute-start(f32[160,256]{1,0:T(8,128)S(1)} %add.45), channel_id=1, source_target_pairs={{0,24},{8,16},{16,8},{24,0},{1,25},{9,17},{17,9},{25,1},{2,26},{10... | collective-permute-start | bytes 491528 | tf_op jit(solution)/shard_map/ppermute | solution.py:193
  30.9 0.5 %collective-permute-start.12 = (f32[160,256]{1,0:T(8,128)S(1)}, f32[160,256]{1,0:T(8,128)S(1)}, u32[]{:S(2)}, u32[]{:S(2)}) collective-permute-start(f32[160,256]{1,0:T(8,128)S(1)} %add.45), channel_id=1, source_target_pairs={{0,16},{8,24},{16,0},{24,8},{1,17},{9,25},{17,1},{25,9},{2,18},{10... | collective-permute-start | bytes 491528 | tf_op jit(solution)/shard_map/ppermute | solution.py:193
  31.5 0.9 %collective-permute-start.11 = (f32[160,256]{1,0:T(8,128)S(1)}, f32[160,256]{1,0:T(8,128)S(1)}, u32[]{:S(2)}, u32[]{:S(2)}) collective-permute-start(f32[160,256]{1,0:T(8,128)S(1)} %add.45), channel_id=1, source_target_pairs={{0,8},{8,0},{16,24},{24,16},{1,9},{9,1},{17,25},{25,17},{2,10},{10... | collective-permute-start | bytes 491528 | tf_op jit(solution)/shard_map/ppermute | solution.py:193
  32.3 0.0 collective-permute-done.8
  32.4 1.2 %collective-permute-start.9 = (f32[160,128]{1,0:T(8,128)S(1)}, f32[160,128]{1,0:T(8,128)S(1)}, u32[]{:S(2)}, u32[]{:S(2)}) collective-permute-start(f32[160,128]{1,0:T(8,128)S(1)} %add.43), channel_id=1, source_target_pairs={{0,4},{2,6},{4,0},{6,2},{1,5},{3,7},{5,1},{7,3},{8,12},{10,14},{12... | collective-permute-start | bytes 245768 | tf_op jit(solution)/shard_map/ppermute | solution.py:193
  33.5 5.4 %collective-permute-done.9 = f32[160,128]{1,0:T(8,128)S(1)} collective-permute-done((f32[160,128]{1,0:T(8,128)S(1)}, f32[160,128]{1,0:T(8,128)S(1)}, u32[]{:S(2)}, u32[]{:S(2)}) %collective-permute-start.9) | collective-permute-done | bytes 81952 | tf_op jit(solution)/shard_map/ppermute | solution.py:193
  38.9 0.0 collective-permute-done.13
  38.9 0.6 %collective-permute-done.12 = f32[160,256]{1,0:T(8,128)S(1)} collective-permute-done((f32[160,256]{1,0:T(8,128)S(1)}, f32[160,256]{1,0:T(8,128)S(1)}, u32[]{:S(2)}, u32[]{:S(2)}) %collective-permute-start.12) | collective-permute-done | bytes 163872 | tf_op jit(solution)/shard_map/ppermute | solution.py:193
  39.5 0.1 collective-permute-done.11
  39.6 0.1 add_add_fusion.mine_d_ref
  39.7 1.7 %collective-permute-start.17 = (f32[160,128]{1,0:T(8,128)S(1)}, f32[160,128]{1,0:T(8,128)S(1)}, u32[]{:S(2)}, u32[]{:S(2)}) collective-permute-start(f32[160,128]{1,0:T(8,128)S(1)} %add.44), channel_id=1, source_target_pairs={{0,24},{8,16},{16,8},{24,0},{1,25},{9,17},{17,9},{25,1},{2,26},{10... | collective-permute-start | bytes 245768 | tf_op jit(solution)/shard_map/ppermute | solution.py:193
  41.4 1.0 %collective-permute-start.16 = (f32[160,128]{1,0:T(8,128)S(1)}, f32[160,128]{1,0:T(8,128)S(1)}, u32[]{:S(2)}, u32[]{:S(2)}) collective-permute-start(f32[160,128]{1,0:T(8,128)S(1)} %add.44), channel_id=1, source_target_pairs={{0,16},{8,24},{16,0},{24,8},{1,17},{9,25},{17,1},{25,9},{2,18},{10... | collective-permute-start | bytes 245768 | tf_op jit(solution)/shard_map/ppermute | solution.py:193
  42.3 0.9 %collective-permute-start.15 = (f32[160,128]{1,0:T(8,128)S(1)}, f32[160,128]{1,0:T(8,128)S(1)}, u32[]{:S(2)}, u32[]{:S(2)}) collective-permute-start(f32[160,128]{1,0:T(8,128)S(1)} %add.44), channel_id=1, source_target_pairs={{0,8},{8,0},{16,24},{24,16},{1,9},{9,1},{17,25},{25,17},{2,10},{10... | collective-permute-start | bytes 245768 | tf_op jit(solution)/shard_map/ppermute | solution.py:193
  43.2 0.0 collective-permute-start.19
  43.2 0.5 %collective-permute-start.14 = (f32[160,256]{1,0:T(8,128)S(1)}, f32[160,256]{1,0:T(8,128)S(1)}, u32[]{:S(2)}, u32[]{:S(2)}) collective-permute-start(f32[160,256]{1,0:T(8,128)S(1)} %add_add_fusion.mine_d_ref), channel_id=1, source_target_pairs={{0,1},{1,0},{2,3},{3,2},{4,5},{5,4},{6,7},{7,6},{8,9},{9,8},{10,11... | collective-permute-start | bytes 491528 | tf_op jit(solution)/shard_map/ppermute | solution.py:193
  43.7 1.9 %collective-permute-done.17 = f32[160,128]{1,0:T(8,128)S(1)} collective-permute-done((f32[160,128]{1,0:T(8,128)S(1)}, f32[160,128]{1,0:T(8,128)S(1)}, u32[]{:S(2)}, u32[]{:S(2)}) %collective-permute-start.17) | collective-permute-done | bytes 81952 | tf_op jit(solution)/shard_map/ppermute | solution.py:193
  45.6 1.0 %collective-permute-done.16 = f32[160,128]{1,0:T(8,128)S(1)} collective-permute-done((f32[160,128]{1,0:T(8,128)S(1)}, f32[160,128]{1,0:T(8,128)S(1)}, u32[]{:S(2)}, u32[]{:S(2)}) %collective-permute-start.16) | collective-permute-done | bytes 81952 | tf_op jit(solution)/shard_map/ppermute | solution.py:193
  46.6 0.1 collective-permute-done.15
  46.8 0.1 collective-permute-start.18
  46.9 0.0 collective-permute-done.19.other_term_ref
  46.9 1.3 %collective-permute-done.18.other_t_ref = f32[160,128]{1,0:T(8,128)S(1)} collective-permute-done((f32[160,128]{1,0:T(8,128)S(1)}, f32[160,128]{1,0:T(8,128)S(1)}, u32[]{:S(2)}, u32[]{:S(2)}) %collective-permute-start.18) | collective-permute-done | bytes 81952 | tf_op jit(solution)/shard_map/ppermute | solution.py:193
  48.1 0.0 collective-permute-done.14.other_d_ref
  48.1 1.5 %expand.1 = (f32[256,256]{1,0:T(8,128)}, f32[512,128]{1,0:T(8,128)}) custom-call(s32[4]{0:T(128)S(1)} %copy-done.3, s32[2]{0:T(128)S(1)} %pad_add_fusion.place_ref, f32[160,256]{1,0:T(8,128)S(1)} %add_add_fusion.mine_d_ref, f32[160,256]{1,0:T(8,128)S(1)} %collective-permute-done.14.other_d_ref, f32[160,128]{1,0:T(8,128)S(1)} %add_add_fusion.2.mine_t_ref, ...), custom_call_target="tpu_custom_call" | custom-call | tf_op jit(solution)/shard_map/expand/pallas_call | solution.py:307
  (6 shorter events, 0.1 us)
Async XLA Ops:
  0.6 10.0 %copy-start.2 = (bf16[1,2,512,128]{3,2,1,0:T(8,128)(2,1)S(1)}, bf16[1,2,512,128]{3,2,1,0:T(8,128)(2,1)}, u32[]{:S(2)}) copy-start(bf16[1,2,512,128]{3,2,1,0:T(8,128)(2,1)} %param.10) | copy-start | bytes 786436
  2.6 16.3 %collective-permute-start.1 = (bf16[640,128]{1,0:T(8,128)(2,1)}, bf16[640,128]{1,0:T(8,128)(2,1)S(1)}, u32[]{:S(2)}, u32[]{:S(2)}) collective-permute-start(bf16[640,128]{1,0:T(8,128)(2,1)} %pack.1.refs_0_.refs_4_), channel_id=1, source_target_pairs={{4,0},{6,2},{0,4},{2,6},{5,1},{7,3},{1,5},{3,7},{12,8},{14,10},{8,... | collective-permute-start | bytes 491528 | tf_op jit(solution)/shard_map/ppermute | solution.py:251
  6.7 15.6 %collective-permute-start.3 = (bf16[640,128]{1,0:T(8,128)(2,1)}, bf16[640,128]{1,0:T(8,128)(2,1)S(1)}, u32[]{:S(2)}, u32[]{:S(2)}) collective-permute-start(bf16[640,128]{1,0:T(8,128)(2,1)} %pack.1.refs_0_.refs_4_), channel_id=1, source_target_pairs={{0,1},{1,0},{2,3},{3,2},{4,5},{5,4},{6,7},{7,6},{8,9},{9,8},{10,11... | collective-permute-start | bytes 491528 | tf_op jit(solution)/shard_map/ppermute | solution.py:193
  6.7 15.8 %collective-permute-start.2 = (bf16[640,128]{1,0:T(8,128)(2,1)}, bf16[640,128]{1,0:T(8,128)(2,1)S(1)}, u32[]{:S(2)}, u32[]{:S(2)}) collective-permute-start(bf16[640,128]{1,0:T(8,128)(2,1)} %pack.1.refs_0_.refs_4_), channel_id=1, source_target_pairs={{6,0},{0,2},{2,4},{4,6},{7,1},{1,3},{3,5},{5,7},{14,8},{8,10},{10,... | collective-permute-start | bytes 491528 | tf_op jit(solution)/shard_map/ppermute | solution.py:251
  8.3 14.2 %collective-permute-start = (bf16[640,128]{1,0:T(8,128)(2,1)}, bf16[640,128]{1,0:T(8,128)(2,1)S(1)}, u32[]{:S(2)}, u32[]{:S(2)}) collective-permute-start(bf16[640,128]{1,0:T(8,128)(2,1)} %pack.1.refs_0_.refs_4_), channel_id=1, source_target_pairs={{2,0},{4,2},{6,4},{0,6},{3,1},{5,3},{7,5},{1,7},{10,8},{12,10},{14... | collective-permute-start | bytes 491528 | tf_op jit(solution)/shard_map/ppermute | solution.py:251
  10.6 0.7 %copy-start.4 = (f32[1,2]{1,0:T(1,128)S(1)}, f32[1,2]{1,0:T(1,128)}, u32[]{:S(2)}) copy-start(f32[1,2]{1,0:T(1,128)} %weights_ref.3) | copy-start | bytes 28
  11.2 1.0 %copy-start.1 = (bf16[1,2,256,4,1,128]{5,3,4,2,1,0:T(4,128)(2,1)S(1)}, bf16[1,2,256,4,1,128]{5,3,4,2,1,0:T(4,128)(2,1)}, u32[]{:S(2)}) copy-start(bf16[1,2,256,4,1,128]{5,3,4,2,1,0:T(4,128)(2,1)} %param.6) | copy-start | bytes 1572868
  12.3 10.2 %copy-start = (bf16[640,128]{1,0:T(8,128)(2,1)S(1)}, bf16[640,128]{1,0:T(8,128)(2,1)}, u32[]{:S(2)}) copy-start(bf16[640,128]{1,0:T(8,128)(2,1)} %pack.1.refs_0_.refs_4_) | copy-start | bytes 491524
  19.0 3.5 %copy-start.3 = (s32[4]{0:T(128)S(1)}, s32[4]{0:T(128)}, u32[]{:S(2)}) copy-start(s32[4]{0:T(128)} %widths_ref.5) | copy-start | bytes 52
  19.0 7.5 %collective-permute-start.7 = (f32[256,128]{1,0:T(8,128)S(1)}, f32[256,128]{1,0:T(8,128)S(1)}, u32[]{:S(2)}, u32[]{:S(2)}) collective-permute-start(f32[256,128]{1,0:T(8,128)S(1)} %get-tuple-element.21), channel_id=1, source_target_pairs={{0,24},{8,16},{16,8},{24,0},{1,25},{9,17},{17,9},{25,1},{2,26},{10... | collective-permute-start | bytes 393224 | tf_op jit(solution)/shard_map/ppermute | solution.py:193
  21.8 5.4 %collective-permute-start.6 = (f32[256,128]{1,0:T(8,128)S(1)}, f32[256,128]{1,0:T(8,128)S(1)}, u32[]{:S(2)}, u32[]{:S(2)}) collective-permute-start(f32[256,128]{1,0:T(8,128)S(1)} %get-tuple-element.21), channel_id=1, source_target_pairs={{0,16},{8,24},{16,0},{24,8},{1,17},{9,25},{17,1},{25,9},{2,18},{10... | collective-permute-start | bytes 393224 | tf_op jit(solution)/shard_map/ppermute | solution.py:193
  22.3 5.0 %collective-permute-start.5 = (f32[256,128]{1,0:T(8,128)S(1)}, f32[256,128]{1,0:T(8,128)S(1)}, u32[]{:S(2)}, u32[]{:S(2)}) collective-permute-start(f32[256,128]{1,0:T(8,128)S(1)} %get-tuple-element.21), channel_id=1, source_target_pairs={{0,8},{8,0},{16,24},{24,16},{1,9},{9,1},{17,25},{25,17},{2,10},{10... | collective-permute-start | bytes 393224 | tf_op jit(solution)/shard_map/ppermute | solution.py:193
  25.2 1.3 %collective-permute-start.4 = (f32[160,128]{1,0:T(8,128)S(1)}, f32[160,128]{1,0:T(8,128)S(1)}, u32[]{:S(2)}, u32[]{:S(2)}) collective-permute-start(f32[160,128]{1,0:T(8,128)S(1)} %get-tuple-element.19), channel_id=1, source_target_pairs={{0,1},{1,0},{2,3},{3,2},{4,5},{5,4},{6,7},{7,6},{8,9},{9,8},{10,11... | collective-permute-start | bytes 245768 | tf_op jit(solution)/shard_map/ppermute | solution.py:193
  27.3 1.5 %collective-permute-start.10 = (f32[160,256]{1,0:T(8,128)S(1)}, f32[160,256]{1,0:T(8,128)S(1)}, u32[]{:S(2)}, u32[]{:S(2)}) collective-permute-start(f32[160,256]{1,0:T(8,128)S(1)} %get-tuple-element.24), channel_id=1, source_target_pairs={{0,1},{1,0},{2,3},{3,2},{4,5},{5,4},{6,7},{7,6},{8,9},{9,8},{10,11... | collective-permute-start | bytes 491528 | tf_op jit(solution)/shard_map/ppermute | solution.py:193
  27.4 5.0 %collective-permute-start.8 = (f32[160,128]{1,0:T(8,128)S(1)}, f32[160,128]{1,0:T(8,128)S(1)}, u32[]{:S(2)}, u32[]{:S(2)}) collective-permute-start(f32[160,128]{1,0:T(8,128)S(1)} %add.39), channel_id=1, source_target_pairs={{0,2},{2,0},{4,6},{6,4},{1,3},{3,1},{5,7},{7,5},{8,10},{10,8},{12,... | collective-permute-start | bytes 245768 | tf_op jit(solution)/shard_map/ppermute | solution.py:193
  28.8 10.1 %collective-permute-start.13 = (f32[160,256]{1,0:T(8,128)S(1)}, f32[160,256]{1,0:T(8,128)S(1)}, u32[]{:S(2)}, u32[]{:S(2)}) collective-permute-start(f32[160,256]{1,0:T(8,128)S(1)} %add.45), channel_id=1, source_target_pairs={{0,24},{8,16},{16,8},{24,0},{1,25},{9,17},{17,9},{25,1},{2,26},{10... | collective-permute-start | bytes 491528 | tf_op jit(solution)/shard_map/ppermute | solution.py:193
  30.9 8.6 %collective-permute-start.12 = (f32[160,256]{1,0:T(8,128)S(1)}, f32[160,256]{1,0:T(8,128)S(1)}, u32[]{:S(2)}, u32[]{:S(2)}) collective-permute-start(f32[160,256]{1,0:T(8,128)S(1)} %add.45), channel_id=1, source_target_pairs={{0,16},{8,24},{16,0},{24,8},{1,17},{9,25},{17,1},{25,9},{2,18},{10... | collective-permute-start | bytes 491528 | tf_op jit(solution)/shard_map/ppermute | solution.py:193
  31.5 8.2 %collective-permute-start.11 = (f32[160,256]{1,0:T(8,128)S(1)}, f32[160,256]{1,0:T(8,128)S(1)}, u32[]{:S(2)}, u32[]{:S(2)}) collective-permute-start(f32[160,256]{1,0:T(8,128)S(1)} %add.45), channel_id=1, source_target_pairs={{0,8},{8,0},{16,24},{24,16},{1,9},{9,1},{17,25},{25,17},{2,10},{10... | collective-permute-start | bytes 491528 | tf_op jit(solution)/shard_map/ppermute | solution.py:193
  32.4 6.5 %collective-permute-start.9 = (f32[160,128]{1,0:T(8,128)S(1)}, f32[160,128]{1,0:T(8,128)S(1)}, u32[]{:S(2)}, u32[]{:S(2)}) collective-permute-start(f32[160,128]{1,0:T(8,128)S(1)} %add.43), channel_id=1, source_target_pairs={{0,4},{2,6},{4,0},{6,2},{1,5},{3,7},{5,1},{7,3},{8,12},{10,14},{12... | collective-permute-start | bytes 245768 | tf_op jit(solution)/shard_map/ppermute | solution.py:193
  39.7 6.0 %collective-permute-start.17 = (f32[160,128]{1,0:T(8,128)S(1)}, f32[160,128]{1,0:T(8,128)S(1)}, u32[]{:S(2)}, u32[]{:S(2)}) collective-permute-start(f32[160,128]{1,0:T(8,128)S(1)} %add.44), channel_id=1, source_target_pairs={{0,24},{8,16},{16,8},{24,0},{1,25},{9,17},{17,9},{25,1},{2,26},{10... | collective-permute-start | bytes 245768 | tf_op jit(solution)/shard_map/ppermute | solution.py:193
  41.4 5.3 %collective-permute-start.16 = (f32[160,128]{1,0:T(8,128)S(1)}, f32[160,128]{1,0:T(8,128)S(1)}, u32[]{:S(2)}, u32[]{:S(2)}) collective-permute-start(f32[160,128]{1,0:T(8,128)S(1)} %add.44), channel_id=1, source_target_pairs={{0,16},{8,24},{16,0},{24,8},{1,17},{9,25},{17,1},{25,9},{2,18},{10... | collective-permute-start | bytes 245768 | tf_op jit(solution)/shard_map/ppermute | solution.py:193
  42.3 4.4 %collective-permute-start.15 = (f32[160,128]{1,0:T(8,128)S(1)}, f32[160,128]{1,0:T(8,128)S(1)}, u32[]{:S(2)}, u32[]{:S(2)}) collective-permute-start(f32[160,128]{1,0:T(8,128)S(1)} %add.44), channel_id=1, source_target_pairs={{0,8},{8,0},{16,24},{24,16},{1,9},{9,1},{17,25},{25,17},{2,10},{10... | collective-permute-start | bytes 245768 | tf_op jit(solution)/shard_map/ppermute | solution.py:193
  43.2 3.7 %collective-permute-start.19 = (f32[256,128]{1,0:T(8,128)S(1)}, f32[256,128]{1,0:T(8,128)S(1)}, u32[]{:S(2)}, u32[]{:S(2)}) collective-permute-start(f32[256,128]{1,0:T(8,128)S(1)} %add_add_fusion.1.mine_term_ref), channel_id=1, source_target_pairs={{0,1},{1,0},{2,3},{3,2},{4,5},{5,4},{6,7},{7,6},{8,9},{9,8},{10,11... | collective-permute-start | bytes 393224 | tf_op jit(solution)/shard_map/ppermute | solution.py:193
  43.2 4.9 %collective-permute-start.14 = (f32[160,256]{1,0:T(8,128)S(1)}, f32[160,256]{1,0:T(8,128)S(1)}, u32[]{:S(2)}, u32[]{:S(2)}) collective-permute-start(f32[160,256]{1,0:T(8,128)S(1)} %add_add_fusion.mine_d_ref), channel_id=1, source_target_pairs={{0,1},{1,0},{2,3},{3,2},{4,5},{5,4},{6,7},{7,6},{8,9},{9,8},{10,11... | collective-permute-start | bytes 491528 | tf_op jit(solution)/shard_map/ppermute | solution.py:193
  46.8 1.3 %collective-permute-start.18 = (f32[160,128]{1,0:T(8,128)S(1)}, f32[160,128]{1,0:T(8,128)S(1)}, u32[]{:S(2)}, u32[]{:S(2)}) collective-permute-start(f32[160,128]{1,0:T(8,128)S(1)} %add_add_fusion.2.mine_t_ref), channel_id=1, source_target_pairs={{0,1},{1,0},{2,3},{3,2},{4,5},{5,4},{6,7},{7,6},{8,9},{9,8},{10,11... | collective-permute-start | bytes 245768 | tf_op jit(solution)/shard_map/ppermute | solution.py:193

commit v9 on v8

--- a/solution.py
+++ b/solution.py
@@ -295,11 +295,9 @@
     products, send_d, term = tie((keep_t + swap(send_t, "col", top), send_d, term))
     term = gather_but_last(term, "col")
     products = scatter_rest(products, "col")
-    for bit in bits_of(row_count):
-        products = products + swap(products, "row", bit)
+    products = sum_direct(products, "row")
     density = scatter_rest(keep_d + swap(send_d, "col", top), "col")
     density = sum_direct(density, "pole")
-    products, density = tie((products, density))
     products = sum_direct(products, "pole")
     density = gather_but_last(density, "col")
     products = gather_but_last(products, "col")

time: 49.8 us -> 50.5 us (1.014)
  starting transfers between devices: 20.4 us -> 24.9 us
  waiting for transfers between devices: 19.4 us -> 15.6 us
    ppermute x17 -> x18, starting transfers between devices: 12.6 us -> 17.1 us  [swap(): lax.ppermute(value, axis, [(i, i ^ bit) for i in range(lax.axis_size(axis...]
    ppermute x17 -> x18, waiting for transfers between devices: 13.7 us -> 9.89 us  [swap(): lax.ppermute(value, axis, [(i, i ^ bit) for i in range(lax.axis_size(axis...]
  transfers between devices with their start and end apart: 20 -> 21, of which waited for: 12 -> 11; matrix products, arithmetic and copies ran while one was open for 0% -> 0% of each run, Pallas kernels for 7% -> 7%
where the time goes in v9:
time: 50.5 us; the launch traced here: 50.3 us
  starting transfers between devices  24.9 us (49%)
  waiting for transfers between devices  15.6 us (31%)
  Pallas kernels  7.08 us (14%)
  local copies, waits for them, and re-layouts  1.7 us (3%)
  between operations  0.75 us (1%)
    ppermute x18, starting transfers between devices, swap(): lax.ppermute(value, axis, [(i, i ^ bit) for i in range(lax.axis_size(axis...  17.1 us
    ppermute x18, waiting for transfers between devices, swap(): lax.ppermute(value, axis, [(i, i ^ bit) for i in range(lax.axis_size(axis...  9.89 us
    ppermute x3, starting transfers between devices, per_device(): blocks[shift] = lax.ppermute(packed, 'row', pairs)  7.86 us
    ppermute x3, waiting for transfers between devices, per_device(): blocks[shift] = lax.ppermute(packed, 'row', pairs)  5.71 us
    pallas_call x1, Pallas kernels, per_device(): pl.pallas_call(functools.partial(compute_kernel, (row_count, col_count),...  2.63 us
    pallas_call x1, Pallas kernels, per_device(): pl.pallas_call(functools.partial(pack_kernel, supernodes, slot), in_specs...  2 us
    unnamed x10, local copies, waits for them, and re-layouts  1.7 us
    pallas_call x1, Pallas kernels, per_device(): pl.pallas_call(functools.partial(expand_kernel, col_count, slot), in_spec...  1.45 us
  transfers between devices with their start and end apart: 21, of which 11 were waited for; matrix products, arithmetic and copies ran while one was open for 0% of the time, Pallas kernels for 7%

profile of v9, /device:TPU:0, one launch (start us, length us, event | category | flops | bytes accessed | tf_op | source)
XLA Modules:
  0.0 50.3 jit_solution(8870894180799749220)
XLA Ops:
  0.6 0.0 copy-start.2
  0.6 2.0 %pack.1.refs_0_.refs_4_ = bf16[640,128]{1,0:T(8,128)(2,1)} custom-call(s32[1,4]{1,0:T(1,128)} %pattern_ref.1, s32[4]{0:T(128)} %widths_ref.5, bf16[2,128,512]{2,1,0:T(8,128)(2,1)} %bitcast.7), custom_call_target="tpu_custom_call" | custom-call | tf_op jit(solution)/shard_map/pack/pallas_call | solution.py:240
  2.6 4.0 %collective-permute-start.1 = (bf16[640,128]{1,0:T(8,128)(2,1)}, bf16[640,128]{1,0:T(8,128)(2,1)S(1)}, u32[]{:S(2)}, u32[]{:S(2)}) collective-permute-start(bf16[640,128]{1,0:T(8,128)(2,1)} %pack.1.refs_0_.refs_4_), channel_id=1, source_target_pairs={{4,0},{6,2},{0,4},{2,6},{5,1},{7,3},{1,5},{3,7},{12,8},{14,10},{8,... | collective-permute-start | bytes 491528 | tf_op jit(solution)/shard_map/ppermute | solution.py:251
  6.7 0.0 collective-permute-start.3
  6.7 1.6 %collective-permute-start.2 = (bf16[640,128]{1,0:T(8,128)(2,1)}, bf16[640,128]{1,0:T(8,128)(2,1)S(1)}, u32[]{:S(2)}, u32[]{:S(2)}) collective-permute-start(bf16[640,128]{1,0:T(8,128)(2,1)} %pack.1.refs_0_.refs_4_), channel_id=1, source_target_pairs={{6,0},{0,2},{2,4},{4,6},{7,1},{1,3},{3,5},{5,7},{14,8},{8,10},{10,... | collective-permute-start | bytes 491528 | tf_op jit(solution)/shard_map/ppermute | solution.py:251
  8.3 2.2 %collective-permute-start = (bf16[640,128]{1,0:T(8,128)(2,1)}, bf16[640,128]{1,0:T(8,128)(2,1)S(1)}, u32[]{:S(2)}, u32[]{:S(2)}) collective-permute-start(bf16[640,128]{1,0:T(8,128)(2,1)} %pack.1.refs_0_.refs_4_), channel_id=1, source_target_pairs={{2,0},{4,2},{6,4},{0,6},{3,1},{5,3},{7,5},{1,7},{10,8},{12,10},{14... | collective-permute-start | bytes 491528 | tf_op jit(solution)/shard_map/ppermute | solution.py:251
  10.5 0.1 pad_add_fusion.place_ref
  10.6 0.0 copy-start.4
  10.6 0.0 copy-done.2
  10.6 0.7 %copy-done.4 = f32[1,2]{1,0:T(1,128)S(1)} copy-done((f32[1,2]{1,0:T(1,128)S(1)}, f32[1,2]{1,0:T(1,128)}, u32[]{:S(2)}) %copy-start.4) | copy-done | bytes 32
  11.2 0.0 copy-start.1
  11.2 1.0 %copy-done.1 = bf16[1,2,256,4,1,128]{5,3,4,2,1,0:T(4,128)(2,1)S(1)} copy-done((bf16[1,2,256,4,1,128]{5,3,4,2,1,0:T(4,128)(2,1)S(1)}, bf16[1,2,256,4,1,128]{5,3,4,2,1,0:T(4,128)(2,1)}, u32[]{:S(2)}) %copy-start.1) | copy-done | bytes 524312
  12.3 0.0 copy-start
  12.3 1.0 %prepare.1 = (bf16[2,256,512]{2,1,0:T(8,128)(2,1)S(1)}, f32[256,128]{1,0:T(8,128)S(1)}) custom-call(f32[1,2]{1,0:T(1,128)S(1)} %copy-done.4, s32[2]{0:T(128)S(1)} %pad_add_fusion.place_ref, bf16[2048,128]{1,0:T(8,128)(2,1)S(1)} %bitcast.5, bf16[2,512,128]{2,1,0:T(8,128)(2,1)S(1)} %bitcast.6), custom_call_target="tpu_custom_call" | custom-call | flops 134217728 | bytes 1048576 | tf_op jit(solution)/shard_map/prepare/pallas_call | solution.py:254
  13.3 5.7 %collective-permute-done.1.refs_2_ = bf16[640,128]{1,0:T(8,128)(2,1)S(1)} collective-permute-done((bf16[640,128]{1,0:T(8,128)(2,1)}, bf16[640,128]{1,0:T(8,128)(2,1)S(1)}, u32[]{:S(2)}, u32[]{:S(2)}) %collective-permute-start.1) | collective-permute-done | bytes 163872 | tf_op jit(solution)/shard_map/ppermute | solution.py:251
  19.0 0.0 copy-start.3
  19.0 2.8 %collective-permute-start.7 = (f32[256,128]{1,0:T(8,128)S(1)}, f32[256,128]{1,0:T(8,128)S(1)}, u32[]{:S(2)}, u32[]{:S(2)}) collective-permute-start(f32[256,128]{1,0:T(8,128)S(1)} %get-tuple-element.20), channel_id=1, source_target_pairs={{0,24},{8,16},{16,8},{24,0},{1,25},{9,17},{17,9},{25,1},{2,26},{10... | collective-permute-start | bytes 393224 | tf_op jit(solution)/shard_map/ppermute | solution.py:193
  21.8 0.5 %collective-permute-start.6 = (f32[256,128]{1,0:T(8,128)S(1)}, f32[256,128]{1,0:T(8,128)S(1)}, u32[]{:S(2)}, u32[]{:S(2)}) collective-permute-start(f32[256,128]{1,0:T(8,128)S(1)} %get-tuple-element.20), channel_id=1, source_target_pairs={{0,16},{8,24},{16,0},{24,8},{1,17},{9,25},{17,1},{25,9},{2,18},{10... | collective-permute-start | bytes 393224 | tf_op jit(solution)/shard_map/ppermute | solution.py:193
  22.3 0.0 collective-permute-done.3.refs_5_
  22.3 0.2 collective-permute-start.5
  22.5 0.0 collective-permute-done.2.refs_3_
  22.5 0.0 collective-permute-done.refs_1_
  22.5 0.0 copy-done
  22.5 0.0 copy-done.3
  22.5 2.6 %compute.1 = (f32[160,256]{1,0:T(8,128)S(1)}, f32[160,256]{1,0:T(8,128)S(1)}, f32[160,128]{1,0:T(8,128)S(1)}, f32[160,128]{1,0:T(8,128)S(1)}) custom-call(s32[4]{0:T(128)S(1)} %copy-done.3, f32[1,2]{1,0:T(1,128)S(1)} %copy-done.4, s32[2]{0:T(128)S(1)} %pad_add_fusion.place_ref, bf16[2,256,512]{2,1,0:T(8,128)(2,1)S(1)} %get-tuple-element.13.straight_ref, ...), custom_call_target="tpu_custom_call" | custom-call | tf_op jit(solution)/shard_map/compute/pallas_call | solution.py:277
  25.1 0.1 collective-permute-start.4
  25.2 1.3 %collective-permute-done.4 = f32[160,128]{1,0:T(8,128)S(1)} collective-permute-done((f32[160,128]{1,0:T(8,128)S(1)}, f32[160,128]{1,0:T(8,128)S(1)}, u32[]{:S(2)}, u32[]{:S(2)}) %collective-permute-start.4) | collective-permute-done | bytes 81952 | tf_op jit(solution)/shard_map/ppermute | solution.py:193
  26.5 0.0 collective-permute-done.7
  26.5 0.7 %collective-permute-done.6 = f32[256,128]{1,0:T(8,128)S(1)} collective-permute-done((f32[256,128]{1,0:T(8,128)S(1)}, f32[256,128]{1,0:T(8,128)S(1)}, u32[]{:S(2)}, u32[]{:S(2)}) %collective-permute-start.6) | collective-permute-done | bytes 131104 | tf_op jit(solution)/shard_map/ppermute | solution.py:193
  27.2 0.1 collective-permute-done.5
  27.3 0.1 collective-permute-start.8
  27.4 1.2 %collective-permute-start.15 = (f32[160,128]{1,0:T(8,128)S(1)}, f32[160,128]{1,0:T(8,128)S(1)}, u32[]{:S(2)}, u32[]{:S(2)}) collective-permute-start(f32[160,128]{1,0:T(8,128)S(1)} %add.42), channel_id=1, source_target_pairs={{0,6},{2,4},{4,2},{6,0},{1,7},{3,5},{5,3},{7,1},{8,14},{10,12},{12... | collective-permute-start | bytes 245768 | tf_op jit(solution)/shard_map/ppermute | solution.py:193
  28.6 0.0 collective-permute-start.14
  28.6 3.2 %collective-permute-start.13 = (f32[160,128]{1,0:T(8,128)S(1)}, f32[160,128]{1,0:T(8,128)S(1)}, u32[]{:S(2)}, u32[]{:S(2)}) collective-permute-start(f32[160,128]{1,0:T(8,128)S(1)} %add.42), channel_id=1, source_target_pairs={{0,2},{2,0},{4,6},{6,4},{1,3},{3,1},{5,7},{7,5},{8,10},{10,8},{12,... | collective-permute-start | bytes 245768 | tf_op jit(solution)/shard_map/ppermute | solution.py:193
  31.8 0.0 collective-permute-start.20
  31.8 0.0 collective-permute-done.8
  31.9 2.2 %collective-permute-start.11 = (f32[160,256]{1,0:T(8,128)S(1)}, f32[160,256]{1,0:T(8,128)S(1)}, u32[]{:S(2)}, u32[]{:S(2)}) collective-permute-start(f32[160,256]{1,0:T(8,128)S(1)} %add.46), channel_id=1, source_target_pairs={{0,24},{8,16},{16,8},{24,0},{1,25},{9,17},{17,9},{25,1},{2,26},{10... | collective-permute-start | bytes 491528 | tf_op jit(solution)/shard_map/ppermute | solution.py:193
  34.1 0.5 %collective-permute-done.15 = f32[160,128]{1,0:T(8,128)S(1)} collective-permute-done((f32[160,128]{1,0:T(8,128)S(1)}, f32[160,128]{1,0:T(8,128)S(1)}, u32[]{:S(2)}, u32[]{:S(2)}) %collective-permute-start.15) | collective-permute-done | bytes 81952 | tf_op jit(solution)/shard_map/ppermute | solution.py:193
  34.6 1.5 %collective-permute-start.10 = (f32[160,256]{1,0:T(8,128)S(1)}, f32[160,256]{1,0:T(8,128)S(1)}, u32[]{:S(2)}, u32[]{:S(2)}) collective-permute-start(f32[160,256]{1,0:T(8,128)S(1)} %add.46), channel_id=1, source_target_pairs={{0,16},{8,24},{16,0},{24,8},{1,17},{9,25},{17,1},{25,9},{2,18},{10... | collective-permute-start | bytes 491528 | tf_op jit(solution)/shard_map/ppermute | solution.py:193
  36.1 1.4 %collective-permute-done.14 = f32[160,128]{1,0:T(8,128)S(1)} collective-permute-done((f32[160,128]{1,0:T(8,128)S(1)}, f32[160,128]{1,0:T(8,128)S(1)}, u32[]{:S(2)}, u32[]{:S(2)}) %collective-permute-start.14) | collective-permute-done | bytes 81952 | tf_op jit(solution)/shard_map/ppermute | solution.py:193
  37.5 1.1 %collective-permute-start.9 = (f32[160,256]{1,0:T(8,128)S(1)}, f32[160,256]{1,0:T(8,128)S(1)}, u32[]{:S(2)}, u32[]{:S(2)}) collective-permute-start(f32[160,256]{1,0:T(8,128)S(1)} %add.46), channel_id=1, source_target_pairs={{0,8},{8,0},{16,24},{24,16},{1,9},{9,1},{17,25},{25,17},{2,10},{10... | collective-permute-start | bytes 491528 | tf_op jit(solution)/shard_map/ppermute | solution.py:193
  38.6 0.0 collective-permute-done.13
  38.7 1.9 %collective-permute-start.18 = (f32[160,128]{1,0:T(8,128)S(1)}, f32[160,128]{1,0:T(8,128)S(1)}, u32[]{:S(2)}, u32[]{:S(2)}) collective-permute-start(f32[160,128]{1,0:T(8,128)S(1)} %add_add_fusion.3), channel_id=1, source_target_pairs={{0,24},{8,16},{16,8},{24,0},{1,25},{9,17},{17,9},{25,1},{2,26},{10... | collective-permute-start | bytes 245768 | tf_op jit(solution)/shard_map/ppermute | solution.py:193
  40.5 0.0 collective-permute-done.11
  40.5 0.6 %collective-permute-start.17 = (f32[160,128]{1,0:T(8,128)S(1)}, f32[160,128]{1,0:T(8,128)S(1)}, u32[]{:S(2)}, u32[]{:S(2)}) collective-permute-start(f32[160,128]{1,0:T(8,128)S(1)} %add_add_fusion.3), channel_id=1, source_target_pairs={{0,16},{8,24},{16,0},{24,8},{1,17},{9,25},{17,1},{25,9},{2,18},{10... | collective-permute-start | bytes 245768 | tf_op jit(solution)/shard_map/ppermute | solution.py:193
  41.1 1.9 %collective-permute-done.10 = f32[160,256]{1,0:T(8,128)S(1)} collective-permute-done((f32[160,256]{1,0:T(8,128)S(1)}, f32[160,256]{1,0:T(8,128)S(1)}, u32[]{:S(2)}, u32[]{:S(2)}) %collective-permute-start.10) | collective-permute-done | bytes 163872 | tf_op jit(solution)/shard_map/ppermute | solution.py:193
  43.0 1.6 %collective-permute-start.16 = (f32[160,128]{1,0:T(8,128)S(1)}, f32[160,128]{1,0:T(8,128)S(1)}, u32[]{:S(2)}, u32[]{:S(2)}) collective-permute-start(f32[160,128]{1,0:T(8,128)S(1)} %add_add_fusion.3), channel_id=1, source_target_pairs={{0,8},{8,0},{16,24},{24,16},{1,9},{9,1},{17,25},{25,17},{2,10},{10... | collective-permute-start | bytes 245768 | tf_op jit(solution)/shard_map/ppermute | solution.py:193
  44.6 0.0 collective-permute-done.9
  44.7 0.1 collective-permute-start.12
  44.7 1.6 %collective-permute-done.18 = f32[160,128]{1,0:T(8,128)S(1)} collective-permute-done((f32[160,128]{1,0:T(8,128)S(1)}, f32[160,128]{1,0:T(8,128)S(1)}, u32[]{:S(2)}, u32[]{:S(2)}) %collective-permute-start.18) | collective-permute-done | bytes 81952 | tf_op jit(solution)/shard_map/ppermute | solution.py:193
  46.3 0.1 collective-permute-done.17
  46.5 1.0 %collective-permute-done.16 = f32[160,128]{1,0:T(8,128)S(1)} collective-permute-done((f32[160,128]{1,0:T(8,128)S(1)}, f32[160,128]{1,0:T(8,128)S(1)}, u32[]{:S(2)}, u32[]{:S(2)}) %collective-permute-start.16) | collective-permute-done | bytes 81952 | tf_op jit(solution)/shard_map/ppermute | solution.py:193
  47.5 0.1 collective-permute-start.19
  47.6 0.0 collective-permute-done.20.other_term_ref
  47.6 1.3 %collective-permute-done.19.other_t_ref = f32[160,128]{1,0:T(8,128)S(1)} collective-permute-done((f32[160,128]{1,0:T(8,128)S(1)}, f32[160,128]{1,0:T(8,128)S(1)}, u32[]{:S(2)}, u32[]{:S(2)}) %collective-permute-start.19) | collective-permute-done | bytes 81952 | tf_op jit(solution)/shard_map/ppermute | solution.py:193
  48.8 0.0 collective-permute-done.12.other_d_ref
  48.9 1.5 %expand.1 = (f32[256,256]{1,0:T(8,128)}, f32[512,128]{1,0:T(8,128)}) custom-call(s32[4]{0:T(128)S(1)} %copy-done.3, s32[2]{0:T(128)S(1)} %pad_add_fusion.place_ref, f32[160,256]{1,0:T(8,128)S(1)} %add_add_fusion.mine_d_ref, f32[160,256]{1,0:T(8,128)S(1)} %collective-permute-done.12.other_d_ref, f32[160,128]{1,0:T(8,128)S(1)} %add_add_fusion.2.mine_t_ref, ...), custom_call_target="tpu_custom_call" | custom-call | tf_op jit(solution)/shard_map/expand/pallas_call | solution.py:305
  (6 shorter events, 0.1 us)
Async XLA Ops:
  0.6 10.0 %copy-start.2 = (bf16[1,2,512,128]{3,2,1,0:T(8,128)(2,1)S(1)}, bf16[1,2,512,128]{3,2,1,0:T(8,128)(2,1)}, u32[]{:S(2)}) copy-start(bf16[1,2,512,128]{3,2,1,0:T(8,128)(2,1)} %param.10) | copy-start | bytes 786436
  2.6 16.3 %collective-permute-start.1 = (bf16[640,128]{1,0:T(8,128)(2,1)}, bf16[640,128]{1,0:T(8,128)(2,1)S(1)}, u32[]{:S(2)}, u32[]{:S(2)}) collective-permute-start(bf16[640,128]{1,0:T(8,128)(2,1)} %pack.1.refs_0_.refs_4_), channel_id=1, source_target_pairs={{4,0},{6,2},{0,4},{2,6},{5,1},{7,3},{1,5},{3,7},{12,8},{14,10},{8,... | collective-permute-start | bytes 491528 | tf_op jit(solution)/shard_map/ppermute | solution.py:251
  6.7 15.6 %collective-permute-start.3 = (bf16[640,128]{1,0:T(8,128)(2,1)}, bf16[640,128]{1,0:T(8,128)(2,1)S(1)}, u32[]{:S(2)}, u32[]{:S(2)}) collective-permute-start(bf16[640,128]{1,0:T(8,128)(2,1)} %pack.1.refs_0_.refs_4_), channel_id=1, source_target_pairs={{0,1},{1,0},{2,3},{3,2},{4,5},{5,4},{6,7},{7,6},{8,9},{9,8},{10,11... | collective-permute-start | bytes 491528 | tf_op jit(solution)/shard_map/ppermute | solution.py:193
  6.7 15.8 %collective-permute-start.2 = (bf16[640,128]{1,0:T(8,128)(2,1)}, bf16[640,128]{1,0:T(8,128)(2,1)S(1)}, u32[]{:S(2)}, u32[]{:S(2)}) collective-permute-start(bf16[640,128]{1,0:T(8,128)(2,1)} %pack.1.refs_0_.refs_4_), channel_id=1, source_target_pairs={{6,0},{0,2},{2,4},{4,6},{7,1},{1,3},{3,5},{5,7},{14,8},{8,10},{10,... | collective-permute-start | bytes 491528 | tf_op jit(solution)/shard_map/ppermute | solution.py:251
  8.3 14.2 %collective-permute-start = (bf16[640,128]{1,0:T(8,128)(2,1)}, bf16[640,128]{1,0:T(8,128)(2,1)S(1)}, u32[]{:S(2)}, u32[]{:S(2)}) collective-permute-start(bf16[640,128]{1,0:T(8,128)(2,1)} %pack.1.refs_0_.refs_4_), channel_id=1, source_target_pairs={{2,0},{4,2},{6,4},{0,6},{3,1},{5,3},{7,5},{1,7},{10,8},{12,10},{14... | collective-permute-start | bytes 491528 | tf_op jit(solution)/shard_map/ppermute | solution.py:251
  10.6 0.7 %copy-start.4 = (f32[1,2]{1,0:T(1,128)S(1)}, f32[1,2]{1,0:T(1,128)}, u32[]{:S(2)}) copy-start(f32[1,2]{1,0:T(1,128)} %weights_ref.3) | copy-start | bytes 28
  11.2 1.0 %copy-start.1 = (bf16[1,2,256,4,1,128]{5,3,4,2,1,0:T(4,128)(2,1)S(1)}, bf16[1,2,256,4,1,128]{5,3,4,2,1,0:T(4,128)(2,1)}, u32[]{:S(2)}) copy-start(bf16[1,2,256,4,1,128]{5,3,4,2,1,0:T(4,128)(2,1)} %param.6) | copy-start | bytes 1572868
  12.3 10.2 %copy-start = (bf16[640,128]{1,0:T(8,128)(2,1)S(1)}, bf16[640,128]{1,0:T(8,128)(2,1)}, u32[]{:S(2)}) copy-start(bf16[640,128]{1,0:T(8,128)(2,1)} %pack.1.refs_0_.refs_4_) | copy-start | bytes 491524
  19.0 3.5 %copy-start.3 = (s32[4]{0:T(128)S(1)}, s32[4]{0:T(128)}, u32[]{:S(2)}) copy-start(s32[4]{0:T(128)} %widths_ref.5) | copy-start | bytes 52
  19.0 7.5 %collective-permute-start.7 = (f32[256,128]{1,0:T(8,128)S(1)}, f32[256,128]{1,0:T(8,128)S(1)}, u32[]{:S(2)}, u32[]{:S(2)}) collective-permute-start(f32[256,128]{1,0:T(8,128)S(1)} %get-tuple-element.20), channel_id=1, source_target_pairs={{0,24},{8,16},{16,8},{24,0},{1,25},{9,17},{17,9},{25,1},{2,26},{10... | collective-permute-start | bytes 393224 | tf_op jit(solution)/shard_map/ppermute | solution.py:193
  21.8 5.4 %collective-permute-start.6 = (f32[256,128]{1,0:T(8,128)S(1)}, f32[256,128]{1,0:T(8,128)S(1)}, u32[]{:S(2)}, u32[]{:S(2)}) collective-permute-start(f32[256,128]{1,0:T(8,128)S(1)} %get-tuple-element.20), channel_id=1, source_target_pairs={{0,16},{8,24},{16,0},{24,8},{1,17},{9,25},{17,1},{25,9},{2,18},{10... | collective-permute-start | bytes 393224 | tf_op jit(solution)/shard_map/ppermute | solution.py:193
  22.3 5.0 %collective-permute-start.5 = (f32[256,128]{1,0:T(8,128)S(1)}, f32[256,128]{1,0:T(8,128)S(1)}, u32[]{:S(2)}, u32[]{:S(2)}) collective-permute-start(f32[256,128]{1,0:T(8,128)S(1)} %get-tuple-element.20), channel_id=1, source_target_pairs={{0,8},{8,0},{16,24},{24,16},{1,9},{9,1},{17,25},{25,17},{2,10},{10... | collective-permute-start | bytes 393224 | tf_op jit(solution)/shard_map/ppermute | solution.py:193
  25.1 1.3 %collective-permute-start.4 = (f32[160,128]{1,0:T(8,128)S(1)}, f32[160,128]{1,0:T(8,128)S(1)}, u32[]{:S(2)}, u32[]{:S(2)}) collective-permute-start(f32[160,128]{1,0:T(8,128)S(1)} %get-tuple-element.18), channel_id=1, source_target_pairs={{0,1},{1,0},{2,3},{3,2},{4,5},{5,4},{6,7},{7,6},{8,9},{9,8},{10,11... | collective-permute-start | bytes 245768 | tf_op jit(solution)/shard_map/ppermute | solution.py:193
  27.3 4.5 %collective-permute-start.8 = (f32[160,256]{1,0:T(8,128)S(1)}, f32[160,256]{1,0:T(8,128)S(1)}, u32[]{:S(2)}, u32[]{:S(2)}) collective-permute-start(f32[160,256]{1,0:T(8,128)S(1)} %get-tuple-element.21), channel_id=1, source_target_pairs={{0,1},{1,0},{2,3},{3,2},{4,5},{5,4},{6,7},{7,6},{8,9},{9,8},{10,11... | collective-permute-start | bytes 491528 | tf_op jit(solution)/shard_map/ppermute | solution.py:193
  27.4 7.2 %collective-permute-start.15 = (f32[160,128]{1,0:T(8,128)S(1)}, f32[160,128]{1,0:T(8,128)S(1)}, u32[]{:S(2)}, u32[]{:S(2)}) collective-permute-start(f32[160,128]{1,0:T(8,128)S(1)} %add.42), channel_id=1, source_target_pairs={{0,6},{2,4},{4,2},{6,0},{1,7},{3,5},{5,3},{7,1},{8,14},{10,12},{12... | collective-permute-start | bytes 245768 | tf_op jit(solution)/shard_map/ppermute | solution.py:193
  28.6 8.9 %collective-permute-start.14 = (f32[160,128]{1,0:T(8,128)S(1)}, f32[160,128]{1,0:T(8,128)S(1)}, u32[]{:S(2)}, u32[]{:S(2)}) collective-permute-start(f32[160,128]{1,0:T(8,128)S(1)} %add.42), channel_id=1, source_target_pairs={{0,4},{2,6},{4,0},{6,2},{1,5},{3,7},{5,1},{7,3},{8,12},{10,14},{12... | collective-permute-start | bytes 245768 | tf_op jit(solution)/shard_map/ppermute | solution.py:193
  28.6 10.0 %collective-permute-start.13 = (f32[160,128]{1,0:T(8,128)S(1)}, f32[160,128]{1,0:T(8,128)S(1)}, u32[]{:S(2)}, u32[]{:S(2)}) collective-permute-start(f32[160,128]{1,0:T(8,128)S(1)} %add.42), channel_id=1, source_target_pairs={{0,2},{2,0},{4,6},{6,4},{1,3},{3,1},{5,7},{7,5},{8,10},{10,8},{12,... | collective-permute-start | bytes 245768 | tf_op jit(solution)/shard_map/ppermute | solution.py:193
  31.8 15.8 %collective-permute-start.20 = (f32[256,128]{1,0:T(8,128)S(1)}, f32[256,128]{1,0:T(8,128)S(1)}, u32[]{:S(2)}, u32[]{:S(2)}) collective-permute-start(f32[256,128]{1,0:T(8,128)S(1)} %add_add_fusion.1.mine_term_ref), channel_id=1, source_target_pairs={{0,1},{1,0},{2,3},{3,2},{4,5},{5,4},{6,7},{7,6},{8,9},{9,8},{10,11... | collective-permute-start | bytes 393224 | tf_op jit(solution)/shard_map/ppermute | solution.py:193
  31.9 8.7 %collective-permute-start.11 = (f32[160,256]{1,0:T(8,128)S(1)}, f32[160,256]{1,0:T(8,128)S(1)}, u32[]{:S(2)}, u32[]{:S(2)}) collective-permute-start(f32[160,256]{1,0:T(8,128)S(1)} %add.46), channel_id=1, source_target_pairs={{0,24},{8,16},{16,8},{24,0},{1,25},{9,17},{17,9},{25,1},{2,26},{10... | collective-permute-start | bytes 491528 | tf_op jit(solution)/shard_map/ppermute | solution.py:193
  34.6 8.5 %collective-permute-start.10 = (f32[160,256]{1,0:T(8,128)S(1)}, f32[160,256]{1,0:T(8,128)S(1)}, u32[]{:S(2)}, u32[]{:S(2)}) collective-permute-start(f32[160,256]{1,0:T(8,128)S(1)} %add.46), channel_id=1, source_target_pairs={{0,16},{8,24},{16,0},{24,8},{1,17},{9,25},{17,1},{25,9},{2,18},{10... | collective-permute-start | bytes 491528 | tf_op jit(solution)/shard_map/ppermute | solution.py:193
  37.5 7.1 %collective-permute-start.9 = (f32[160,256]{1,0:T(8,128)S(1)}, f32[160,256]{1,0:T(8,128)S(1)}, u32[]{:S(2)}, u32[]{:S(2)}) collective-permute-start(f32[160,256]{1,0:T(8,128)S(1)} %add.46), channel_id=1, source_target_pairs={{0,8},{8,0},{16,24},{24,16},{1,9},{9,1},{17,25},{25,17},{2,10},{10... | collective-permute-start | bytes 491528 | tf_op jit(solution)/shard_map/ppermute | solution.py:193
  38.7 7.7 %collective-permute-start.18 = (f32[160,128]{1,0:T(8,128)S(1)}, f32[160,128]{1,0:T(8,128)S(1)}, u32[]{:S(2)}, u32[]{:S(2)}) collective-permute-start(f32[160,128]{1,0:T(8,128)S(1)} %add_add_fusion.3), channel_id=1, source_target_pairs={{0,24},{8,16},{16,8},{24,0},{1,25},{9,17},{17,9},{25,1},{2,26},{10... | collective-permute-start | bytes 245768 | tf_op jit(solution)/shard_map/ppermute | solution.py:193
  40.5 5.9 %collective-permute-start.17 = (f32[160,128]{1,0:T(8,128)S(1)}, f32[160,128]{1,0:T(8,128)S(1)}, u32[]{:S(2)}, u32[]{:S(2)}) collective-permute-start(f32[160,128]{1,0:T(8,128)S(1)} %add_add_fusion.3), channel_id=1, source_target_pairs={{0,16},{8,24},{16,0},{24,8},{1,17},{9,25},{17,1},{25,9},{2,18},{10... | collective-permute-start | bytes 245768 | tf_op jit(solution)/shard_map/ppermute | solution.py:193
  43.0 4.4 %collective-permute-start.16 = (f32[160,128]{1,0:T(8,128)S(1)}, f32[160,128]{1,0:T(8,128)S(1)}, u32[]{:S(2)}, u32[]{:S(2)}) collective-permute-start(f32[160,128]{1,0:T(8,128)S(1)} %add_add_fusion.3), channel_id=1, source_target_pairs={{0,8},{8,0},{16,24},{24,16},{1,9},{9,1},{17,25},{25,17},{2,10},{10... | collective-permute-start | bytes 245768 | tf_op jit(solution)/shard_map/ppermute | solution.py:193
  44.7 4.2 %collective-permute-start.12 = (f32[160,256]{1,0:T(8,128)S(1)}, f32[160,256]{1,0:T(8,128)S(1)}, u32[]{:S(2)}, u32[]{:S(2)}) collective-permute-start(f32[160,256]{1,0:T(8,128)S(1)} %add_add_fusion.mine_d_ref), channel_id=1, source_target_pairs={{0,1},{1,0},{2,3},{3,2},{4,5},{5,4},{6,7},{7,6},{8,9},{9,8},{10,11... | collective-permute-start | bytes 491528 | tf_op jit(solution)/shard_map/ppermute | solution.py:193
  47.5 1.3 %collective-permute-start.19 = (f32[160,128]{1,0:T(8,128)S(1)}, f32[160,128]{1,0:T(8,128)S(1)}, u32[]{:S(2)}, u32[]{:S(2)}) collective-permute-start(f32[160,128]{1,0:T(8,128)S(1)} %add_add_fusion.2.mine_t_ref), channel_id=1, source_target_pairs={{0,1},{1,0},{2,3},{3,2},{4,5},{5,4},{6,7},{7,6},{8,9},{9,8},{10,11... | collective-permute-start | bytes 245768 | tf_op jit(solution)/shard_map/ppermute | solution.py:193

commit v10 on v8

--- a/solution.py
+++ b/solution.py
@@ -134,40 +134,24 @@
     send_t_ref[...] = jnp.where(upper, total[:half], total[half:])
 
 
-def expand_kernel(
-    col_count, slot, widths_ref, place_ref, mine_d_ref, other_d_ref, mine_t_ref, other_t_ref,
-    mine_term_ref, other_term_ref, density_ref, diagonal_ref, strip_ref,
+def fill_strips(strip_ref, mine_ref, other_ref, col_count, slot, upper):
+    half, width = mine_ref.shape
+    for side in range(2):
+        value = jnp.where(upper if side else jnp.logical_not(upper), mine_ref[...], other_ref[...])
+        for s in range(width // slot):
+            strip_ref[s, side * half:(side + 1) * half] = value[:, s * slot:(s + 1) * slot]
+    for s in range(width // slot):
+        strip_ref[s, 2 * half:] = jnp.zeros((slot, slot), F32)
+
+
+def density_kernel(
+    col_count, slot, widths_ref, place_ref, mine_ref, other_ref, density_ref, strip_ref
 ):
-    supernodes = diagonal_ref.shape[0] // slot
     per_col, local_rows = density_ref.shape
-    strips = local_rows // slot
-    share = col_count // 2
-    part = mine_d_ref.shape[0] // share
+    supernodes = per_col * col_count // slot
     col_index = place_ref[1]
-    upper = (col_index & share) != 0
-    for side in range(2):
-        own_side = upper if side else jnp.logical_not(upper)
-        d_value = jnp.where(own_side, mine_d_ref[...], other_d_ref[...])
-        t_value = jnp.where(own_side, mine_t_ref[...], other_t_ref[...])
-        rows = mine_term_ref.shape[0]
-        diagonal_ref[side * rows:(side + 1) * rows] = jnp.where(
-            own_side, mine_term_ref[...], other_term_ref[...]
-        )
-        for q in range(share):
-            owner = side * share + q
-            base = owner * part
-            for s in range(strips):
-                lanes = slice(s * slot, (s + 1) * slot)
-                strip_ref[s, base:base + part] = d_value[q * part:(q + 1) * part, lanes]
-            strip_ref[strips, base:base + part] = t_value[q * part:(q + 1) * part]
-    for s in range(strips + 1):
-        strip_ref[s, col_count * part:] = jnp.zeros((slot, slot), F32)
-    offsets = offsets_of(widths_ref, supernodes)
-    row_in_slot = lax.broadcasted_iota(jnp.int32, (slot, 1), 0)
-    for k in range(supernodes):
-        product = strip_ref[strips, pl.ds(offsets[k], slot), :]
-        product = jnp.where(row_in_slot < widths_ref[k], product, 0.0)
-        diagonal_ref[k * slot:(k + 1) * slot] -= product
+    upper = (col_index & (col_count // 2)) != 0
+    fill_strips(strip_ref, mine_ref, other_ref, col_count, slot, upper)
     size = min(per_col, slot)
     row_in_part = lax.broadcasted_iota(jnp.int32, (size, 1), 0)
     for part in range(per_col // size):
@@ -178,11 +162,31 @@
         for k in range(supernodes):
             start = start + jnp.where(k < owner, widths_ref[k], 0)
             count = count + jnp.where(k == owner, widths_ref[k], 0)
-        for s in range(strips):
+        for s in range(local_rows // slot):
             piece = strip_ref[s, pl.ds(start + within, size), :]
             density_ref[part * size:(part + 1) * size, s * slot:(s + 1) * slot] = jnp.where(
                 row_in_part < count - within, piece, 0.0
             )
+
+
+def diagonal_kernel(
+    col_count, slot, widths_ref, place_ref, mine_ref, other_ref, mine_term_ref, other_term_ref,
+    diagonal_ref, strip_ref,
+):
+    supernodes = diagonal_ref.shape[0] // slot
+    upper = (place_ref[1] & (col_count // 2)) != 0
+    fill_strips(strip_ref, mine_ref, other_ref, col_count, slot, upper)
+    rows = mine_term_ref.shape[0]
+    for side in range(2):
+        diagonal_ref[side * rows:(side + 1) * rows] = jnp.where(
+            upper if side else jnp.logical_not(upper), mine_term_ref[...], other_term_ref[...]
+        )
+    offsets = offsets_of(widths_ref, supernodes)
+    row_in_slot = lax.broadcasted_iota(jnp.int32, (slot, 1), 0)
+    for k in range(supernodes):
+        product = strip_ref[0, pl.ds(offsets[k], slot), :]
+        product = jnp.where(row_in_slot < widths_ref[k], product, 0.0)
+        diagonal_ref[k * slot:(k + 1) * slot] -= product
 
 
 def bits_of(count):
@@ -293,32 +297,46 @@
 
     tie = lax.optimization_barrier
     products, send_d, term = tie((keep_t + swap(send_t, "col", top), send_d, term))
-    term = gather_but_last(term, "col")
     products = scatter_rest(products, "col")
+    density = scatter_rest(keep_d + swap(send_d, "col", top), "col")
     for bit in bits_of(row_count):
         products = products + swap(products, "row", bit)
-    density = scatter_rest(keep_d + swap(send_d, "col", top), "col")
-    density = sum_direct(density, "pole")
+    bits = bits_of(lax.axis_size("pole"))
+    for step, bit in enumerate(bits):
+        density = density + swap(density, "pole", bit)
+        if step < len(bits) - 1:
+            density, _ = tie((density, products))
+            products = products + swap(products, "pole", bit)
     products, density = tie((products, density))
-    products = sum_direct(products, "pole")
     density = gather_but_last(density, "col")
-    products = gather_but_last(products, "col")
-
-    return pl.pallas_call(
-        functools.partial(expand_kernel, col_count, slot),
-        in_specs=[SMEM_SPEC] * 2 + [VMEM_SPEC] * 6,
-        out_specs=[VMEM_SPEC] * 2,
-        out_shape=[
-            jax.ShapeDtypeStruct((total_cols // col_count, local_rows), F32),
-            jax.ShapeDtypeStruct((total_cols, slot), F32),
-        ],
-        scratch_shapes=[pltpu.VMEM((local_rows // slot + 1, packed_width + slot, slot), F32)],
+    grown = [pltpu.VMEM((count, packed_width + slot, slot), F32) for count in (local_rows // slot, 1)]
+    density = pl.pallas_call(
+        functools.partial(density_kernel, col_count, slot),
+        in_specs=[SMEM_SPEC] * 2 + [VMEM_SPEC] * 2,
+        out_specs=VMEM_SPEC,
+        out_shape=jax.ShapeDtypeStruct((total_cols // col_count, local_rows), F32),
+        scratch_shapes=[grown[0]],
         compiler_params=PARAMS,
-        name="expand",
+        cost_estimate=pl.CostEstimate(
+            flops=0, bytes_accessed=16 * total_cols * local_rows, transcendentals=0
+        ),
+        name="expand_density",
+    )(sup_widths, place, density, swap(density, "col", top))
+    density, arrived = tie((density, swap(products, "pole", bits[-1])))
+    products = gather_but_last(products + arrived, "col")
+    term = gather_but_last(term, "col")
+    diagonal = pl.pallas_call(
+        functools.partial(diagonal_kernel, col_count, slot),
+        in_specs=[SMEM_SPEC] * 2 + [VMEM_SPEC] * 4,
+        out_specs=VMEM_SPEC,
+        out_shape=jax.ShapeDtypeStruct((total_cols, slot), F32),
+        scratch_shapes=[grown[1]],
+        compiler_params=PARAMS,
+        name="expand_diagonal",
     )(
-        sup_widths, place, density, swap(density, "col", top),
-        products, swap(products, "col", top), term, swap(term, "col", top),
-    )
+        sup_widths, place, products, swap(products, "col", top), term, swap(term, "col", top)
+    )
+    return (density, diagonal)
 
 
 def solution(mesh):

time: 49.8 us -> 52.8 us (1.060)
  waiting for transfers between devices: 19.4 us -> 23.3 us
  starting transfers between devices: 20.4 us -> 18.4 us
  Pallas kernels: 7.11 us -> 8.24 us
    ppermute x17 -> x15, waiting for transfers between devices: 13.7 us -> 17.6 us  [swap(): lax.ppermute(value, axis, [(i, i ^ bit) for i in range(lax.axis_size(axis...]
    ppermute x17 -> x15, starting transfers between devices: 12.6 us -> 10.5 us  [swap(): lax.ppermute(value, axis, [(i, i ^ bit) for i in range(lax.axis_size(axis...]
    pallas_call x1 -> x2, Pallas kernels: 1.45 us -> 2.61 us  [the longest x1 1.31 us: per_device(): pl.pallas_call(functools.partial(diagonal_kernel, col_count, slot), in_sp...]
  transfers between devices with their start and end apart: 20 -> 18, of which waited for: 12 -> 10; matrix products, arithmetic and copies ran while one was open for 0% -> 0% of each run, Pallas kernels for 7% -> 9%
where the time goes in v10:
time: 52.8 us; the launch traced here: 52.6 us
  waiting for transfers between devices  23.3 us (44%)
  starting transfers between devices  18.4 us (35%)
  Pallas kernels  8.24 us (16%)
  local copies, waits for them, and re-layouts  1.7 us (3%)
  between operations  0.78 us (1%)
    ppermute x15, waiting for transfers between devices, swap(): lax.ppermute(value, axis, [(i, i ^ bit) for i in range(lax.axis_size(axis...  17.6 us
    ppermute x15, starting transfers between devices, swap(): lax.ppermute(value, axis, [(i, i ^ bit) for i in range(lax.axis_size(axis...  10.5 us
    ppermute x3, starting transfers between devices, per_device(): blocks[shift] = lax.ppermute(packed, 'row', pairs)  7.86 us
    ppermute x3, waiting for transfers between devices, per_device(): blocks[shift] = lax.ppermute(packed, 'row', pairs)  5.71 us
    pallas_call x1, Pallas kernels, per_device(): pl.pallas_call(functools.partial(compute_kernel, (row_count, col_count),...  2.63 us
    pallas_call x1, Pallas kernels, per_device(): pl.pallas_call(functools.partial(pack_kernel, supernodes, slot), in_specs...  2 us
    unnamed x10, local copies, waits for them, and re-layouts  1.7 us
    pallas_call x1, Pallas kernels, per_device(): pl.pallas_call(functools.partial(diagonal_kernel, col_count, slot), in_sp...  1.31 us
  transfers between devices with their start and end apart: 18, of which 10 were waited for; matrix products, arithmetic and copies ran while one was open for 0% of the time, Pallas kernels for 9%

profile of v10, /device:TPU:0, one launch (start us, length us, event | category | flops | bytes accessed | tf_op | source)
XLA Modules:
  0.0 52.6 jit_solution(5653296831943832960)
XLA Ops:
  0.6 0.0 copy-start.2
  0.6 2.0 %pack.1.refs_0_.refs_4_ = bf16[640,128]{1,0:T(8,128)(2,1)} custom-call(s32[1,4]{1,0:T(1,128)} %pattern_ref.1, s32[4]{0:T(128)} %widths_ref.7, bf16[2,128,512]{2,1,0:T(8,128)(2,1)} %bitcast.7), custom_call_target="tpu_custom_call" | custom-call | tf_op jit(solution)/shard_map/pack/pallas_call | solution.py:244
  2.6 4.0 %collective-permute-start.1 = (bf16[640,128]{1,0:T(8,128)(2,1)}, bf16[640,128]{1,0:T(8,128)(2,1)S(1)}, u32[]{:S(2)}, u32[]{:S(2)}) collective-permute-start(bf16[640,128]{1,0:T(8,128)(2,1)} %pack.1.refs_0_.refs_4_), channel_id=1, source_target_pairs={{4,0},{6,2},{0,4},{2,6},{5,1},{7,3},{1,5},{3,7},{12,8},{14,10},{8,... | collective-permute-start | bytes 491528 | tf_op jit(solution)/shard_map/ppermute | solution.py:255
  6.7 0.0 collective-permute-start.3
  6.7 1.6 %collective-permute-start.2 = (bf16[640,128]{1,0:T(8,128)(2,1)}, bf16[640,128]{1,0:T(8,128)(2,1)S(1)}, u32[]{:S(2)}, u32[]{:S(2)}) collective-permute-start(bf16[640,128]{1,0:T(8,128)(2,1)} %pack.1.refs_0_.refs_4_), channel_id=1, source_target_pairs={{6,0},{0,2},{2,4},{4,6},{7,1},{1,3},{3,5},{5,7},{14,8},{8,10},{10,... | collective-permute-start | bytes 491528 | tf_op jit(solution)/shard_map/ppermute | solution.py:255
  8.3 2.2 %collective-permute-start = (bf16[640,128]{1,0:T(8,128)(2,1)}, bf16[640,128]{1,0:T(8,128)(2,1)S(1)}, u32[]{:S(2)}, u32[]{:S(2)}) collective-permute-start(bf16[640,128]{1,0:T(8,128)(2,1)} %pack.1.refs_0_.refs_4_), channel_id=1, source_target_pairs={{2,0},{4,2},{6,4},{0,6},{3,1},{5,3},{7,5},{1,7},{10,8},{12,10},{14... | collective-permute-start | bytes 491528 | tf_op jit(solution)/shard_map/ppermute | solution.py:255
  10.5 0.1 pad_add_fusion.place_ref
  10.6 0.0 copy-start.4
  10.6 0.0 copy-done.2
  10.6 0.7 %copy-done.4 = f32[1,2]{1,0:T(1,128)S(1)} copy-done((f32[1,2]{1,0:T(1,128)S(1)}, f32[1,2]{1,0:T(1,128)}, u32[]{:S(2)}) %copy-start.4) | copy-done | bytes 32
  11.2 0.0 copy-start.1
  11.2 1.0 %copy-done.1 = bf16[1,2,256,4,1,128]{5,3,4,2,1,0:T(4,128)(2,1)S(1)} copy-done((bf16[1,2,256,4,1,128]{5,3,4,2,1,0:T(4,128)(2,1)S(1)}, bf16[1,2,256,4,1,128]{5,3,4,2,1,0:T(4,128)(2,1)}, u32[]{:S(2)}) %copy-start.1) | copy-done | bytes 524312
  12.3 0.0 copy-start
  12.3 1.0 %prepare.1 = (bf16[2,256,512]{2,1,0:T(8,128)(2,1)S(1)}, f32[256,128]{1,0:T(8,128)S(1)}) custom-call(f32[1,2]{1,0:T(1,128)S(1)} %copy-done.4, s32[2]{0:T(128)S(1)} %pad_add_fusion.place_ref, bf16[2048,128]{1,0:T(8,128)(2,1)S(1)} %bitcast.5, bf16[2,512,128]{2,1,0:T(8,128)(2,1)S(1)} %bitcast.6), custom_call_target="tpu_custom_call" | custom-call | flops 134217728 | bytes 1048576 | tf_op jit(solution)/shard_map/prepare/pallas_call | solution.py:258
  13.3 5.7 %collective-permute-done.1.refs_2_ = bf16[640,128]{1,0:T(8,128)(2,1)S(1)} collective-permute-done((bf16[640,128]{1,0:T(8,128)(2,1)}, bf16[640,128]{1,0:T(8,128)(2,1)S(1)}, u32[]{:S(2)}, u32[]{:S(2)}) %collective-permute-start.1) | collective-permute-done | bytes 163872 | tf_op jit(solution)/shard_map/ppermute | solution.py:255
  19.0 0.0 copy-start.3
  19.0 2.8 %collective-permute-start.7 = (f32[256,128]{1,0:T(8,128)S(1)}, f32[256,128]{1,0:T(8,128)S(1)}, u32[]{:S(2)}, u32[]{:S(2)}) collective-permute-start(f32[256,128]{1,0:T(8,128)S(1)} %get-tuple-element.24), channel_id=1, source_target_pairs={{0,24},{8,16},{16,8},{24,0},{1,25},{9,17},{17,9},{25,1},{2,26},{10... | collective-permute-start | bytes 393224 | tf_op jit(solution)/shard_map/ppermute | solution.py:197
  21.8 0.5 collective-permute-start.6
  22.3 0.0 collective-permute-done.3.refs_5_
  22.3 0.2 collective-permute-start.5
  22.5 0.0 collective-permute-done.2.refs_3_
  22.5 0.0 collective-permute-done.refs_1_
  22.5 0.0 copy-done
  22.5 0.0 copy-done.3
  22.5 2.6 %compute.1 = (f32[160,256]{1,0:T(8,128)S(1)}, f32[160,256]{1,0:T(8,128)S(1)}, f32[160,128]{1,0:T(8,128)S(1)}, f32[160,128]{1,0:T(8,128)S(1)}) custom-call(s32[4]{0:T(128)S(1)} %copy-done.3, f32[1,2]{1,0:T(1,128)S(1)} %copy-done.4, s32[2]{0:T(128)S(1)} %pad_add_fusion.place_ref, bf16[2,256,512]{2,1,0:T(8,128)(2,1)S(1)} %get-tuple-element.18.straight_ref, ...), custom_call_target="tpu_custom_call" | custom-call | tf_op jit(solution)/shard_map/compute/pallas_call | solution.py:281
  25.1 0.1 collective-permute-start.4
  25.2 1.3 %collective-permute-done.4 = f32[160,128]{1,0:T(8,128)S(1)} collective-permute-done((f32[160,128]{1,0:T(8,128)S(1)}, f32[160,128]{1,0:T(8,128)S(1)}, u32[]{:S(2)}, u32[]{:S(2)}) %collective-permute-start.4) | collective-permute-done | bytes 81952 | tf_op jit(solution)/shard_map/ppermute | solution.py:197
  26.5 0.0 collective-permute-done.7
  26.5 0.7 %collective-permute-done.6 = f32[256,128]{1,0:T(8,128)S(1)} collective-permute-done((f32[256,128]{1,0:T(8,128)S(1)}, f32[256,128]{1,0:T(8,128)S(1)}, u32[]{:S(2)}, u32[]{:S(2)}) %collective-permute-start.6) | collective-permute-done | bytes 131104 | tf_op jit(solution)/shard_map/ppermute | solution.py:197
  27.2 0.1 collective-permute-done.5
  27.3 0.1 collective-permute-start.11
  27.4 0.1 collective-permute-start.8
  27.5 1.3 %collective-permute-done.11 = f32[160,256]{1,0:T(8,128)S(1)} collective-permute-done((f32[160,256]{1,0:T(8,128)S(1)}, f32[160,256]{1,0:T(8,128)S(1)}, u32[]{:S(2)}, u32[]{:S(2)}) %collective-permute-start.11) | collective-permute-done | bytes 163872 | tf_op jit(solution)/shard_map/ppermute | solution.py:197
  28.8 1.2 %collective-permute-start.12 = (f32[160,256]{1,0:T(8,128)S(1)}, f32[160,256]{1,0:T(8,128)S(1)}, u32[]{:S(2)}, u32[]{:S(2)}) collective-permute-start(f32[160,256]{1,0:T(8,128)S(1)} %add.40), channel_id=1, source_target_pairs={{0,8},{8,0},{16,24},{24,16},{1,9},{9,1},{17,25},{25,17},{2,10},{10... | collective-permute-start | bytes 491528 | tf_op jit(solution)/shard_map/ppermute | solution.py:197
  30.0 2.3 %collective-permute-done.8 = f32[160,128]{1,0:T(8,128)S(1)} collective-permute-done((f32[160,128]{1,0:T(8,128)S(1)}, f32[160,128]{1,0:T(8,128)S(1)}, u32[]{:S(2)}, u32[]{:S(2)}) %collective-permute-start.8) | collective-permute-done | bytes 81952 | tf_op jit(solution)/shard_map/ppermute | solution.py:197
  32.3 1.1 %collective-permute-start.9 = (f32[160,128]{1,0:T(8,128)S(1)}, f32[160,128]{1,0:T(8,128)S(1)}, u32[]{:S(2)}, u32[]{:S(2)}) collective-permute-start(f32[160,128]{1,0:T(8,128)S(1)} %add.37), channel_id=1, source_target_pairs={{0,4},{2,6},{4,0},{6,2},{1,5},{3,7},{5,1},{7,3},{8,12},{10,14},{12... | collective-permute-start | bytes 245768 | tf_op jit(solution)/shard_map/ppermute | solution.py:197
  33.4 5.5 %collective-permute-done.9 = f32[160,128]{1,0:T(8,128)S(1)} collective-permute-done((f32[160,128]{1,0:T(8,128)S(1)}, f32[160,128]{1,0:T(8,128)S(1)}, u32[]{:S(2)}, u32[]{:S(2)}) %collective-permute-start.9) | collective-permute-done | bytes 81952 | tf_op jit(solution)/shard_map/ppermute | solution.py:197
  38.9 0.0 collective-permute-done.12
  38.9 1.6 %collective-permute-start.13 = (f32[160,256]{1,0:T(8,128)S(1)}, f32[160,256]{1,0:T(8,128)S(1)}, u32[]{:S(2)}, u32[]{:S(2)}) collective-permute-start(f32[160,256]{1,0:T(8,128)S(1)} %add.41), channel_id=1, source_target_pairs={{0,16},{8,24},{16,0},{24,8},{1,17},{9,25},{17,1},{25,9},{2,18},{10... | collective-permute-start | bytes 491528 | tf_op jit(solution)/shard_map/ppermute | solution.py:197
  40.5 1.0 %collective-permute-start.10 = (f32[160,128]{1,0:T(8,128)S(1)}, f32[160,128]{1,0:T(8,128)S(1)}, u32[]{:S(2)}, u32[]{:S(2)}) collective-permute-start(f32[160,128]{1,0:T(8,128)S(1)} %add.38), channel_id=1, source_target_pairs={{0,8},{8,0},{16,24},{24,16},{1,9},{9,1},{17,25},{25,17},{2,10},{10... | collective-permute-start | bytes 245768 | tf_op jit(solution)/shard_map/ppermute | solution.py:197
  41.6 3.4 %collective-permute-done.10 = f32[160,128]{1,0:T(8,128)S(1)} collective-permute-done((f32[160,128]{1,0:T(8,128)S(1)}, f32[160,128]{1,0:T(8,128)S(1)}, u32[]{:S(2)}, u32[]{:S(2)}) %collective-permute-start.10) | collective-permute-done | bytes 81952 | tf_op jit(solution)/shard_map/ppermute | solution.py:197
  45.0 0.0 collective-permute-done.13
  45.0 0.1 collective-permute-start.14
  45.1 1.6 %collective-permute-start.15 = (f32[160,128]{1,0:T(8,128)S(1)}, f32[160,128]{1,0:T(8,128)S(1)}, u32[]{:S(2)}, u32[]{:S(2)}) collective-permute-start(f32[160,128]{1,0:T(8,128)S(1)} %add.39), channel_id=1, source_target_pairs={{0,16},{8,24},{16,0},{24,8},{1,17},{9,25},{17,1},{25,9},{2,18},{10... | collective-permute-start | bytes 245768 | tf_op jit(solution)/shard_map/ppermute | solution.py:197
  46.7 0.2 collective-permute-start.17
  46.8 0.0 collective-permute-done.14.other_ref
  46.8 1.3 %expand_density.1 = f32[256,256]{1,0:T(8,128)} custom-call(s32[4]{0:T(128)S(1)} %copy-done.3, s32[2]{0:T(128)S(1)} %pad_add_fusion.place_ref, f32[160,256]{1,0:T(8,128)S(1)} %add.42.mine_ref, f32[160,256]{1,0:T(8,128)S(1)} %collective-permute-done.14.other_ref), custom_call_target="tpu_custom_call" | custom-call | bytes 2097152 | tf_op jit(solution)/shard_map/expand_density/pallas_call | solution.py:313
  48.1 1.8 %collective-permute-done.15 = f32[160,128]{1,0:T(8,128)S(1)} collective-permute-done((f32[160,128]{1,0:T(8,128)S(1)}, f32[160,128]{1,0:T(8,128)S(1)}, u32[]{:S(2)}, u32[]{:S(2)}) %collective-permute-start.15) | collective-permute-done | bytes 81952 | tf_op jit(solution)/shard_map/ppermute | solution.py:197
  50.0 0.1 collective-permute-start.16
  50.0 0.0 collective-permute-done.17.other_term_ref
  50.1 1.3 %collective-permute-done.16.other_ref = f32[160,128]{1,0:T(8,128)S(1)} collective-permute-done((f32[160,128]{1,0:T(8,128)S(1)}, f32[160,128]{1,0:T(8,128)S(1)}, u32[]{:S(2)}, u32[]{:S(2)}) %collective-permute-start.16) | collective-permute-done | bytes 81952 | tf_op jit(solution)/shard_map/ppermute | solution.py:197
  51.3 1.3 %expand_diagonal.1 = f32[512,128]{1,0:T(8,128)} custom-call(s32[4]{0:T(128)S(1)} %copy-done.3, s32[2]{0:T(128)S(1)} %pad_add_fusion.place_ref, f32[160,128]{1,0:T(8,128)S(1)} %add.43.mine_ref, f32[160,128]{1,0:T(8,128)S(1)} %collective-permute-done.16.other_ref, f32[256,128]{1,0:T(8,128)S(1)} %add_add_fusion.mine_term_ref, ...), custom_call_target="tpu_custom_call" | custom-call | tf_op jit(solution)/shard_map/expand_diagonal/pallas_call | solution.py:328
  (9 shorter events, 0.2 us)
Async XLA Ops:
  0.6 10.0 %copy-start.2 = (bf16[1,2,512,128]{3,2,1,0:T(8,128)(2,1)S(1)}, bf16[1,2,512,128]{3,2,1,0:T(8,128)(2,1)}, u32[]{:S(2)}) copy-start(bf16[1,2,512,128]{3,2,1,0:T(8,128)(2,1)} %param.10) | copy-start | bytes 786436
  2.6 16.3 %collective-permute-start.1 = (bf16[640,128]{1,0:T(8,128)(2,1)}, bf16[640,128]{1,0:T(8,128)(2,1)S(1)}, u32[]{:S(2)}, u32[]{:S(2)}) collective-permute-start(bf16[640,128]{1,0:T(8,128)(2,1)} %pack.1.refs_0_.refs_4_), channel_id=1, source_target_pairs={{4,0},{6,2},{0,4},{2,6},{5,1},{7,3},{1,5},{3,7},{12,8},{14,10},{8,... | collective-permute-start | bytes 491528 | tf_op jit(solution)/shard_map/ppermute | solution.py:255
  6.7 15.6 %collective-permute-start.3 = (bf16[640,128]{1,0:T(8,128)(2,1)}, bf16[640,128]{1,0:T(8,128)(2,1)S(1)}, u32[]{:S(2)}, u32[]{:S(2)}) collective-permute-start(bf16[640,128]{1,0:T(8,128)(2,1)} %pack.1.refs_0_.refs_4_), channel_id=1, source_target_pairs={{0,1},{1,0},{2,3},{3,2},{4,5},{5,4},{6,7},{7,6},{8,9},{9,8},{10,11... | collective-permute-start | bytes 491528 | tf_op jit(solution)/shard_map/ppermute | solution.py:197
  6.7 15.8 %collective-permute-start.2 = (bf16[640,128]{1,0:T(8,128)(2,1)}, bf16[640,128]{1,0:T(8,128)(2,1)S(1)}, u32[]{:S(2)}, u32[]{:S(2)}) collective-permute-start(bf16[640,128]{1,0:T(8,128)(2,1)} %pack.1.refs_0_.refs_4_), channel_id=1, source_target_pairs={{6,0},{0,2},{2,4},{4,6},{7,1},{1,3},{3,5},{5,7},{14,8},{8,10},{10,... | collective-permute-start | bytes 491528 | tf_op jit(solution)/shard_map/ppermute | solution.py:255
  8.3 14.2 %collective-permute-start = (bf16[640,128]{1,0:T(8,128)(2,1)}, bf16[640,128]{1,0:T(8,128)(2,1)S(1)}, u32[]{:S(2)}, u32[]{:S(2)}) collective-permute-start(bf16[640,128]{1,0:T(8,128)(2,1)} %pack.1.refs_0_.refs_4_), channel_id=1, source_target_pairs={{2,0},{4,2},{6,4},{0,6},{3,1},{5,3},{7,5},{1,7},{10,8},{12,10},{14... | collective-permute-start | bytes 491528 | tf_op jit(solution)/shard_map/ppermute | solution.py:255
  10.6 0.7 %copy-start.4 = (f32[1,2]{1,0:T(1,128)S(1)}, f32[1,2]{1,0:T(1,128)}, u32[]{:S(2)}) copy-start(f32[1,2]{1,0:T(1,128)} %weights_ref.3) | copy-start | bytes 28
  11.2 1.0 %copy-start.1 = (bf16[1,2,256,4,1,128]{5,3,4,2,1,0:T(4,128)(2,1)S(1)}, bf16[1,2,256,4,1,128]{5,3,4,2,1,0:T(4,128)(2,1)}, u32[]{:S(2)}) copy-start(bf16[1,2,256,4,1,128]{5,3,4,2,1,0:T(4,128)(2,1)} %param.6) | copy-start | bytes 1572868
  12.3 10.2 %copy-start = (bf16[640,128]{1,0:T(8,128)(2,1)S(1)}, bf16[640,128]{1,0:T(8,128)(2,1)}, u32[]{:S(2)}) copy-start(bf16[640,128]{1,0:T(8,128)(2,1)} %pack.1.refs_0_.refs_4_) | copy-start | bytes 491524
  19.0 3.5 %copy-start.3 = (s32[4]{0:T(128)S(1)}, s32[4]{0:T(128)}, u32[]{:S(2)}) copy-start(s32[4]{0:T(128)} %widths_ref.7) | copy-start | bytes 52
  19.0 7.5 %collective-permute-start.7 = (f32[256,128]{1,0:T(8,128)S(1)}, f32[256,128]{1,0:T(8,128)S(1)}, u32[]{:S(2)}, u32[]{:S(2)}) collective-permute-start(f32[256,128]{1,0:T(8,128)S(1)} %get-tuple-element.24), channel_id=1, source_target_pairs={{0,24},{8,16},{16,8},{24,0},{1,25},{9,17},{17,9},{25,1},{2,26},{10... | collective-permute-start | bytes 393224 | tf_op jit(solution)/shard_map/ppermute | solution.py:197
  21.8 5.4 %collective-permute-start.6 = (f32[256,128]{1,0:T(8,128)S(1)}, f32[256,128]{1,0:T(8,128)S(1)}, u32[]{:S(2)}, u32[]{:S(2)}) collective-permute-start(f32[256,128]{1,0:T(8,128)S(1)} %get-tuple-element.24), channel_id=1, source_target_pairs={{0,16},{8,24},{16,0},{24,8},{1,17},{9,25},{17,1},{25,9},{2,18},{10... | collective-permute-start | bytes 393224 | tf_op jit(solution)/shard_map/ppermute | solution.py:197
  22.3 5.0 %collective-permute-start.5 = (f32[256,128]{1,0:T(8,128)S(1)}, f32[256,128]{1,0:T(8,128)S(1)}, u32[]{:S(2)}, u32[]{:S(2)}) collective-permute-start(f32[256,128]{1,0:T(8,128)S(1)} %get-tuple-element.24), channel_id=1, source_target_pairs={{0,8},{8,0},{16,24},{24,16},{1,9},{9,1},{17,25},{25,17},{2,10},{10... | collective-permute-start | bytes 393224 | tf_op jit(solution)/shard_map/ppermute | solution.py:197
  25.1 1.3 %collective-permute-start.4 = (f32[160,128]{1,0:T(8,128)S(1)}, f32[160,128]{1,0:T(8,128)S(1)}, u32[]{:S(2)}, u32[]{:S(2)}) collective-permute-start(f32[160,128]{1,0:T(8,128)S(1)} %get-tuple-element.22), channel_id=1, source_target_pairs={{0,1},{1,0},{2,3},{3,2},{4,5},{5,4},{6,7},{7,6},{8,9},{9,8},{10,11... | collective-permute-start | bytes 245768 | tf_op jit(solution)/shard_map/ppermute | solution.py:197
  27.3 1.5 %collective-permute-start.11 = (f32[160,256]{1,0:T(8,128)S(1)}, f32[160,256]{1,0:T(8,128)S(1)}, u32[]{:S(2)}, u32[]{:S(2)}) collective-permute-start(f32[160,256]{1,0:T(8,128)S(1)} %get-tuple-element.27), channel_id=1, source_target_pairs={{0,1},{1,0},{2,3},{3,2},{4,5},{5,4},{6,7},{7,6},{8,9},{9,8},{10,11... | collective-permute-start | bytes 491528 | tf_op jit(solution)/shard_map/ppermute | solution.py:197
  27.4 4.9 %collective-permute-start.8 = (f32[160,128]{1,0:T(8,128)S(1)}, f32[160,128]{1,0:T(8,128)S(1)}, u32[]{:S(2)}, u32[]{:S(2)}) collective-permute-start(f32[160,128]{1,0:T(8,128)S(1)} %add.33), channel_id=1, source_target_pairs={{0,2},{2,0},{4,6},{6,4},{1,3},{3,1},{5,7},{7,5},{8,10},{10,8},{12,... | collective-permute-start | bytes 245768 | tf_op jit(solution)/shard_map/ppermute | solution.py:197
  28.8 10.1 %collective-permute-start.12 = (f32[160,256]{1,0:T(8,128)S(1)}, f32[160,256]{1,0:T(8,128)S(1)}, u32[]{:S(2)}, u32[]{:S(2)}) collective-permute-start(f32[160,256]{1,0:T(8,128)S(1)} %add.40), channel_id=1, source_target_pairs={{0,8},{8,0},{16,24},{24,16},{1,9},{9,1},{17,25},{25,17},{2,10},{10... | collective-permute-start | bytes 491528 | tf_op jit(solution)/shard_map/ppermute | solution.py:197
  32.3 6.6 %collective-permute-start.9 = (f32[160,128]{1,0:T(8,128)S(1)}, f32[160,128]{1,0:T(8,128)S(1)}, u32[]{:S(2)}, u32[]{:S(2)}) collective-permute-start(f32[160,128]{1,0:T(8,128)S(1)} %add.37), channel_id=1, source_target_pairs={{0,4},{2,6},{4,0},{6,2},{1,5},{3,7},{5,1},{7,3},{8,12},{10,14},{12... | collective-permute-start | bytes 245768 | tf_op jit(solution)/shard_map/ppermute | solution.py:197
  38.9 6.0 %collective-permute-start.13 = (f32[160,256]{1,0:T(8,128)S(1)}, f32[160,256]{1,0:T(8,128)S(1)}, u32[]{:S(2)}, u32[]{:S(2)}) collective-permute-start(f32[160,256]{1,0:T(8,128)S(1)} %add.41), channel_id=1, source_target_pairs={{0,16},{8,24},{16,0},{24,8},{1,17},{9,25},{17,1},{25,9},{2,18},{10... | collective-permute-start | bytes 491528 | tf_op jit(solution)/shard_map/ppermute | solution.py:197
  40.5 4.4 %collective-permute-start.10 = (f32[160,128]{1,0:T(8,128)S(1)}, f32[160,128]{1,0:T(8,128)S(1)}, u32[]{:S(2)}, u32[]{:S(2)}) collective-permute-start(f32[160,128]{1,0:T(8,128)S(1)} %add.38), channel_id=1, source_target_pairs={{0,8},{8,0},{16,24},{24,16},{1,9},{9,1},{17,25},{25,17},{2,10},{10... | collective-permute-start | bytes 245768 | tf_op jit(solution)/shard_map/ppermute | solution.py:197
  45.0 1.8 %collective-permute-start.14 = (f32[160,256]{1,0:T(8,128)S(1)}, f32[160,256]{1,0:T(8,128)S(1)}, u32[]{:S(2)}, u32[]{:S(2)}) collective-permute-start(f32[160,256]{1,0:T(8,128)S(1)} %add.42.mine_ref), channel_id=1, source_target_pairs={{0,1},{1,0},{2,3},{3,2},{4,5},{5,4},{6,7},{7,6},{8,9},{9,8},{10,11... | collective-permute-start | bytes 491528 | tf_op jit(solution)/shard_map/ppermute | solution.py:197
  45.1 4.9 %collective-permute-start.15 = (f32[160,128]{1,0:T(8,128)S(1)}, f32[160,128]{1,0:T(8,128)S(1)}, u32[]{:S(2)}, u32[]{:S(2)}) collective-permute-start(f32[160,128]{1,0:T(8,128)S(1)} %add.39), channel_id=1, source_target_pairs={{0,16},{8,24},{16,0},{24,8},{1,17},{9,25},{17,1},{25,9},{2,18},{10... | collective-permute-start | bytes 245768 | tf_op jit(solution)/shard_map/ppermute | solution.py:197
  46.7 3.4 %collective-permute-start.17 = (f32[256,128]{1,0:T(8,128)S(1)}, f32[256,128]{1,0:T(8,128)S(1)}, u32[]{:S(2)}, u32[]{:S(2)}) collective-permute-start(f32[256,128]{1,0:T(8,128)S(1)} %add_add_fusion.mine_term_ref), channel_id=1, source_target_pairs={{0,1},{1,0},{2,3},{3,2},{4,5},{5,4},{6,7},{7,6},{8,9},{9,8},{10,11... | collective-permute-start | bytes 393224 | tf_op jit(solution)/shard_map/ppermute | solution.py:197
  50.0 1.3 %collective-permute-start.16 = (f32[160,128]{1,0:T(8,128)S(1)}, f32[160,128]{1,0:T(8,128)S(1)}, u32[]{:S(2)}, u32[]{:S(2)}) collective-permute-start(f32[160,128]{1,0:T(8,128)S(1)} %add.43.mine_ref), channel_id=1, source_target_pairs={{0,1},{1,0},{2,3},{3,2},{4,5},{5,4},{6,7},{7,6},{8,9},{9,8},{10,11... | collective-permute-start | bytes 245768 | tf_op jit(solution)/shard_map/ppermute | solution.py:197

commit v11 on v8

--- a/solution.py
+++ b/solution.py
@@ -25,8 +25,16 @@
     return offsets
 
 
-def pack_kernel(supernodes, slot, pattern_ref, widths_ref, panel_ref, packed_ref):
+def pack_kernel(
+    supernodes, slot, pattern_ref, widths_ref, panel_ref, packed_ref, held_ref, arrived
+):
     packed_width = packed_ref.shape[0] // 2
+    copies = [
+        pltpu.make_async_copy(panel_ref.at[part], held_ref.at[part], arrived.at[part])
+        for part in range(2)
+    ]
+    for copy in copies:
+        copy.start()
     offsets = offsets_of(widths_ref, supernodes)
     lane = lax.broadcasted_iota(jnp.int32, (1, slot), 1)
     place = []
@@ -37,14 +45,19 @@
     target = lax.broadcasted_iota(jnp.int32, (packed_width, supernodes * slot), 0)
     select = jnp.where(target == place, 1.0, 0.0).astype(BF16)
     for part in range(2):
+        copies[part].wait()
         packed_ref[part * packed_width:(part + 1) * packed_width, :] = rows_by_rows(
-            select, panel_ref[part]
+            select, held_ref[part]
         ).astype(BF16)
 
 
 def prepare_kernel(
-    row_count, weights_ref, place_ref, inverse_ref, diag_ref, straight_ref, term_ref
+    counts, widths_ref, weights_ref, place_ref, inverse_ref, diag_ref, *refs
 ):
+    row_count, col_count = counts
+    own_refs, (straight_ref, own_wide_ref, term_ref) = refs[:col_count], refs[col_count:]
+    packed_width = own_refs[0].shape[0] // 2
+    col_index = place_ref[1]
     block = inverse_ref.shape[1]
     local_rows = straight_ref.shape[1]
     row_index = place_ref[0]
@@ -63,20 +76,39 @@
                 straight_ref[
                     part, chunk * group:(chunk + 1) * group, owner * block:(owner + 1) * block
                 ] = sorted_rows[owner * group:(owner + 1) * group]
+    own = []
+    for c in range(col_count):
+        block_of = own_refs[0][...]
+        for other in range(1, col_count):
+            block_of = jnp.where((col_index ^ c) == other, own_refs[other][...], block_of)
+        own.append(block_of)
+    own = jnp.concatenate(own, axis=1)
+    total_cols = own_wide_ref.shape[0]
+    slot = diag_ref.shape[2]
+    offsets = offsets_of(widths_ref, total_cols // slot)
+    row_in_slot = lax.broadcasted_iota(jnp.int32, (slot, packed_width), 0)
+    column = lax.broadcasted_iota(jnp.int32, (slot, packed_width), 1)
+    for k in range(total_cols // slot):
+        chosen = (column == row_in_slot + offsets[k]) & (row_in_slot < widths_ref[k])
+        chosen = jnp.where(chosen, 1.0, 0.0).astype(BF16)
+        for part, sign in enumerate((1.0, -1.0)):
+            rows = own[part * packed_width:(part + 1) * packed_width]
+            own_wide_ref[k * slot:(k + 1) * slot, part * local_rows:(part + 1) * local_rows] = (
+                sign * jnp.dot(chosen, rows, preferred_element_type=F32)
+            ).astype(BF16)
     per_col = term_ref.shape[0]
-    first = pl.multiple_of(place_ref[1] * per_col, per_col)
+    first = pl.multiple_of(col_index * per_col, per_col)
     term_ref[...] = weights_ref[0, 0] * diag_ref[0, pl.ds(first, per_col), :].astype(
         F32
     ) - weights_ref[0, 1] * diag_ref[1, pl.ds(first, per_col), :].astype(F32)
 
 
 def compute_kernel(
-    counts, supernodes, slot, widths_ref, weights_ref, place_ref, straight_ref, *refs
+    col_count, supernodes, slot, widths_ref, weights_ref, place_ref, straight_ref, own_wide_ref,
+    *refs
 ):
-    row_count, col_count = counts
-    block_refs, refs = refs[:row_count], refs[row_count:]
-    own_refs, refs = refs[:col_count], refs[col_count:]
-    keep_d_ref, send_d_ref, keep_t_ref, send_t_ref, x_ref, y_ref = refs
+    block_refs, refs = refs[:-7], refs[-7:]
+    keep_d_ref, send_d_ref, keep_t_ref, send_t_ref, x_ref, y_ref, t_ref = refs
     packed_width = block_refs[0].shape[0] // 2
     local_rows = straight_ref.shape[1]
     strips = local_rows // slot
@@ -102,36 +134,20 @@
             ref[s, :packed_width] = value[:, s * slot:(s + 1) * slot]
             ref[s, packed_width:] = jnp.zeros((slot, slot), F32)
 
-    own = [jnp.zeros((), BF16)] * col_count
-    for c in range(col_count):
-        block_of = own_refs[0][...]
-        for other in range(1, col_count):
-            block_of = jnp.where((col_index ^ c) == other, own_refs[other][...], block_of)
-        own[c] = block_of
-    own = jnp.concatenate(own, axis=1)
     offsets = offsets_of(widths_ref, supernodes)
-    row_in_slot = lax.broadcasted_iota(jnp.int32, (slot, 1), 0)
-    row_packed = lax.broadcasted_iota(jnp.int32, (packed_width, 1), 0)
-    total = jnp.zeros((packed_width, slot), F32)
     for k in range(supernodes):
-        valid = row_in_slot < widths_ref[k]
-        x, y = (
-            jnp.concatenate(
-                [jnp.where(valid, ref[s, pl.ds(offsets[k], slot), :], 0.0) for s in range(strips)],
-                axis=1,
-            )
-            for ref in (x_ref, y_ref)
+        right = jnp.concatenate(
+            [ref[s, pl.ds(offsets[k], slot), :] for ref in (x_ref, y_ref) for s in range(strips)],
+            axis=1,
         )
-        x_high, y_high = x.astype(BF16), y.astype(BF16)
-        x_low = (x - x_high.astype(F32)).astype(BF16)
-        y_low = (y - y_high.astype(F32)).astype(BF16)
-        product = (
-            rows_by_rows(own[:packed_width], x_high) - rows_by_rows(own[packed_width:], y_high)
-        ) + (rows_by_rows(own[:packed_width], x_low) - rows_by_rows(own[packed_width:], y_low))
-        inside = (row_packed >= offsets[k]) & (row_packed < offsets[k + 1])
-        total = jnp.where(inside, product, total)
-    keep_t_ref[...] = jnp.where(upper, total[half:], total[:half])
-    send_t_ref[...] = jnp.where(upper, total[:half], total[half:])
+        high = right.astype(BF16)
+        low = (right - high.astype(F32)).astype(BF16)
+        product = rows_by_rows(
+            own_wide_ref[k * slot:(k + 1) * slot, :], jnp.concatenate([high, low], axis=0)
+        )
+        t_ref[pl.ds(offsets[k], slot), :] = product[:, :slot] + product[:, slot:]
+    keep_t_ref[...] = jnp.where(upper, t_ref[half:2 * half], t_ref[:half])
+    send_t_ref[...] = jnp.where(upper, t_ref[:half], t_ref[half:2 * half])
 
 
 def expand_kernel(
@@ -163,10 +179,12 @@
     for s in range(strips + 1):
         strip_ref[s, col_count * part:] = jnp.zeros((slot, slot), F32)
     offsets = offsets_of(widths_ref, supernodes)
+    lane = lax.broadcasted_iota(jnp.int32, (1, slot), 1)
     row_in_slot = lax.broadcasted_iota(jnp.int32, (slot, 1), 0)
     for k in range(supernodes):
         product = strip_ref[strips, pl.ds(offsets[k], slot), :]
-        product = jnp.where(row_in_slot < widths_ref[k], product, 0.0)
+        valid = (row_in_slot < widths_ref[k]) & (lane < widths_ref[k])
+        product = jnp.where(valid, product, 0.0)
         diagonal_ref[k * slot:(k + 1) * slot] -= product
     size = min(per_col, slot)
     row_in_part = lax.broadcasted_iota(jnp.int32, (size, 1), 0)
@@ -239,9 +257,12 @@
 
     packed = pl.pallas_call(
         functools.partial(pack_kernel, supernodes, slot),
-        in_specs=[SMEM_SPEC, SMEM_SPEC, VMEM_SPEC],
+        in_specs=[SMEM_SPEC, SMEM_SPEC, pl.BlockSpec(memory_space=pl.ANY)],
         out_specs=VMEM_SPEC,
         out_shape=jax.ShapeDtypeStruct((2 * packed_width, block), BF16),
+        scratch_shapes=[
+            pltpu.VMEM((2, block, total_cols), BF16), pltpu.SemaphoreType.DMA((2,))
+        ],
         name="pack",
     )(block_pattern, sup_widths, l_panel[0])
 
@@ -251,12 +272,13 @@
         blocks[shift] = lax.ppermute(packed, "row", pairs)
     own = [packed] + [swap(packed, "col", other) for other in range(1, col_count)]
 
-    straight, term = pl.pallas_call(
-        functools.partial(prepare_kernel, row_count),
-        in_specs=[SMEM_SPEC] * 2 + [VMEM_SPEC] * 2,
-        out_specs=[VMEM_SPEC] * 2,
+    straight, own_wide, term = pl.pallas_call(
+        functools.partial(prepare_kernel, (row_count, col_count)),
+        in_specs=[SMEM_SPEC] * 3 + [VMEM_SPEC] * (2 + col_count),
+        out_specs=[VMEM_SPEC] * 3,
         out_shape=[
             jax.ShapeDtypeStruct((2, local_rows, row_count * block), BF16),
+            jax.ShapeDtypeStruct((total_cols, 2 * local_rows), BF16),
             jax.ShapeDtypeStruct((total_cols // col_count, slot), F32),
         ],
         compiler_params=PARAMS,
@@ -267,28 +289,29 @@
         ),
         name="prepare",
     )(
-        pole_weights, place, found_inverse.reshape(2 * local_rows * row_count, block),
-        diag_inverse[0],
+        sup_widths, pole_weights, place,
+        found_inverse.reshape(2 * local_rows * row_count, block), diag_inverse[0], *own,
     )
     first_arrival = min(blocks, key=lambda shift: (shift == 0, -min(shift, row_count - shift)))
     term, blocks[first_arrival] = lax.optimization_barrier((term, blocks[first_arrival]))
     term = sum_direct(term, "pole")
 
     keep_d, send_d, keep_t, send_t = pl.pallas_call(
-        functools.partial(compute_kernel, (row_count, col_count), supernodes, slot),
-        in_specs=[SMEM_SPEC] * 3 + [VMEM_SPEC] * (1 + row_count + col_count),
+        functools.partial(compute_kernel, col_count, supernodes, slot),
+        in_specs=[SMEM_SPEC] * 3 + [VMEM_SPEC] * (2 + row_count),
         out_specs=[VMEM_SPEC] * 4,
         out_shape=[jax.ShapeDtypeStruct((half, local_rows), F32)] * 2
         + [jax.ShapeDtypeStruct((half, slot), F32)] * 2,
         scratch_shapes=[
             pltpu.VMEM((local_rows // slot, packed_width + slot, slot), F32),
             pltpu.VMEM((local_rows // slot, packed_width + slot, slot), F32),
+            pltpu.VMEM((packed_width + slot, slot), F32),
         ],
         compiler_params=PARAMS,
         name="compute",
     )(
-        sup_widths, pole_weights, place, straight,
-        *[blocks[shift] for shift in range(row_count)], *own,
+        sup_widths, pole_weights, place, straight, own_wide,
+        *[blocks[shift] for shift in range(row_count)],
     )
 
     tie = lax.optimization_barrier

time: 49.8 us -> 51.7 us (1.038)
  local copies, waits for them, and re-layouts: 1.7 us -> 2.63 us
  waiting for transfers between devices: 19.4 us -> 20.1 us
  Pallas kernels: 7.11 us -> 7.73 us
    ppermute x17, waiting for transfers between devices: 13.7 us -> 15.5 us  [swap(): lax.ppermute(value, axis, [(i, i ^ bit) for i in range(lax.axis_size(axis...]
    ppermute x3, waiting for transfers between devices: 5.71 us -> 4.51 us  [per_device(): blocks[shift] = lax.ppermute(packed, 'row', pairs)]
    pallas_call x1, Pallas kernels: 2 us -> 3.02 us  [per_device(): pl.pallas_call(functools.partial(pack_kernel, supernodes, slot), in_specs...]
    unnamed x10 -> x12, local copies, waits for them, and re-layouts: 1.7 us -> 2.63 us
  transfers between devices with their start and end apart: 20 -> 20, of which waited for: 12 -> 10; matrix products, arithmetic and copies ran while one was open for 0% -> 0% of each run, Pallas kernels for 7% -> 6%
where the time goes in v11:
time: 51.7 us; the launch traced here: 51.4 us
  waiting for transfers between devices  20.1 us (39%)
  starting transfers between devices  20 us (39%)
  Pallas kernels  7.73 us (15%)
  local copies, waits for them, and re-layouts  2.63 us (5%)
  between operations  0.77 us (1%)
    ppermute x17, waiting for transfers between devices, swap(): lax.ppermute(value, axis, [(i, i ^ bit) for i in range(lax.axis_size(axis...  15.5 us
    ppermute x17, starting transfers between devices, swap(): lax.ppermute(value, axis, [(i, i ^ bit) for i in range(lax.axis_size(axis...  12.5 us
    ppermute x3, starting transfers between devices, per_device(): blocks[shift] = lax.ppermute(packed, 'row', pairs)  7.48 us
    ppermute x3, waiting for transfers between devices, per_device(): blocks[shift] = lax.ppermute(packed, 'row', pairs)  4.51 us
    pallas_call x1, Pallas kernels, per_device(): pl.pallas_call(functools.partial(pack_kernel, supernodes, slot), in_specs...  3.02 us
    unnamed x12, local copies, waits for them, and re-layouts  2.63 us
    pallas_call x1, Pallas kernels, per_device(): pl.pallas_call(functools.partial(compute_kernel, col_count, supernodes, s...  1.99 us
    pallas_call x1, Pallas kernels, per_device(): pl.pallas_call(functools.partial(expand_kernel, col_count, slot), in_spec...  1.44 us
  transfers between devices with their start and end apart: 20, of which 10 were waited for; matrix products, arithmetic and copies ran while one was open for 0% of the time, Pallas kernels for 6%

profile of v11, /device:TPU:0, one launch (start us, length us, event | category | flops | bytes accessed | tf_op | source)
XLA Modules:
  0.0 51.4 jit_solution(1440868063854076810)
XLA Ops:
  0.6 0.0 copy-start.3
  0.6 3.0 %pack.1.refs_0_ = bf16[640,128]{1,0:T(8,128)(2,1)} custom-call(s32[1,4]{1,0:T(1,128)} %pattern_ref.1, s32[4]{0:T(128)} %widths_ref.7, bf16[2,128,512]{2,1,0:T(8,128)(2,1)} %bitcast.7), custom_call_target="tpu_custom_call" | custom-call | tf_op jit(solution)/shard_map/pack/pallas_call | solution.py:258
  3.7 0.5 %collective-permute-start = (bf16[640,128]{1,0:T(8,128)(2,1)}, bf16[640,128]{1,0:T(8,128)(2,1)S(1)}, u32[]{:S(2)}, u32[]{:S(2)}) collective-permute-start(bf16[640,128]{1,0:T(8,128)(2,1)} %pack.1.refs_0_), channel_id=1, source_target_pairs={{0,1},{1,0},{2,3},{3,2},{4,5},{5,4},{6,7},{7,6},{8,9},{9,8},{10,11... | collective-permute-start | bytes 491528 | tf_op jit(solution)/shard_map/ppermute | solution.py:211
  4.2 3.7 %collective-permute-start.2 = (bf16[640,128]{1,0:T(8,128)(2,1)}, bf16[640,128]{1,0:T(8,128)(2,1)S(1)}, u32[]{:S(2)}, u32[]{:S(2)}) collective-permute-start(bf16[640,128]{1,0:T(8,128)(2,1)} %pack.1.refs_0_), channel_id=1, source_target_pairs={{4,0},{6,2},{0,4},{2,6},{5,1},{7,3},{1,5},{3,7},{12,8},{14,10},{8,... | collective-permute-start | bytes 491528 | tf_op jit(solution)/shard_map/ppermute | solution.py:272
  7.9 1.6 %collective-permute-start.3 = (bf16[640,128]{1,0:T(8,128)(2,1)}, bf16[640,128]{1,0:T(8,128)(2,1)S(1)}, u32[]{:S(2)}, u32[]{:S(2)}) collective-permute-start(bf16[640,128]{1,0:T(8,128)(2,1)} %pack.1.refs_0_), channel_id=1, source_target_pairs={{6,0},{0,2},{2,4},{4,6},{7,1},{1,3},{3,5},{5,7},{14,8},{8,10},{10,... | collective-permute-start | bytes 491528 | tf_op jit(solution)/shard_map/ppermute | solution.py:272
  9.4 2.2 %collective-permute-start.1 = (bf16[640,128]{1,0:T(8,128)(2,1)}, bf16[640,128]{1,0:T(8,128)(2,1)S(1)}, u32[]{:S(2)}, u32[]{:S(2)}) collective-permute-start(bf16[640,128]{1,0:T(8,128)(2,1)} %pack.1.refs_0_), channel_id=1, source_target_pairs={{2,0},{4,2},{6,4},{0,6},{3,1},{5,3},{7,5},{1,7},{10,8},{12,10},{14... | collective-permute-start | bytes 491528 | tf_op jit(solution)/shard_map/ppermute | solution.py:272
  11.7 0.1 pad_add_fusion.place_ref
  11.8 0.0 collective-permute-done.refs_1_
  11.8 0.0 copy-start.4
  11.8 0.0 copy-start.5
  11.8 0.0 copy-done.3
  11.8 0.6 %copy-done.4 = s32[4]{0:T(128)S(1)} copy-done((s32[4]{0:T(128)S(1)}, s32[4]{0:T(128)}, u32[]{:S(2)}) %copy-start.4) | copy-done | bytes 40
  12.4 0.0 copy-done.5
  12.4 0.0 copy-start
  12.4 0.9 %copy-done = bf16[640,128]{1,0:T(8,128)(2,1)S(1)} copy-done((bf16[640,128]{1,0:T(8,128)(2,1)S(1)}, bf16[640,128]{1,0:T(8,128)(2,1)}, u32[]{:S(2)}) %copy-start) | copy-done | bytes 163864
  13.3 0.0 copy-start.2
  13.3 1.0 %copy-done.2 = bf16[1,2,256,4,1,128]{5,3,4,2,1,0:T(4,128)(2,1)S(1)} copy-done((bf16[1,2,256,4,1,128]{5,3,4,2,1,0:T(4,128)(2,1)S(1)}, bf16[1,2,256,4,1,128]{5,3,4,2,1,0:T(4,128)(2,1)}, u32[]{:S(2)}) %copy-start.2) | copy-done | bytes 524312
  14.4 0.0 copy-start.1
  14.4 1.3 %prepare.1 = (bf16[2,256,512]{2,1,0:T(8,128)(2,1)S(1)}, bf16[512,512]{1,0:T(8,128)(2,1)S(1)}, f32[256,128]{1,0:T(8,128)S(1)}) custom-call(s32[4]{0:T(128)S(1)} %copy-done.4, f32[1,2]{1,0:T(1,128)S(1)} %copy-done.5, s32[2]{0:T(128)S(1)} %pad_add_fusion.place_ref, bf16[2048,128]{1,0:T(8,128)(2,1)S(1)} %bitcast.5, bf16[2,512,128]{2,1,0:T(8,128)(2,1)S(1)} %bitcast.6, ...), custom_call_target="tpu_custom_call" | custom-call | flops 134217728 | bytes 1048576 | tf_op jit(solution)/shard_map/prepare/pallas_call | solution.py:275
  15.7 4.5 %collective-permute-done.2.refs_2_ = bf16[640,128]{1,0:T(8,128)(2,1)S(1)} collective-permute-done((bf16[640,128]{1,0:T(8,128)(2,1)}, bf16[640,128]{1,0:T(8,128)(2,1)S(1)}, u32[]{:S(2)}, u32[]{:S(2)}) %collective-permute-start.2) | collective-permute-done | bytes 163872 | tf_op jit(solution)/shard_map/ppermute | solution.py:272
  20.2 2.7 %collective-permute-start.7 = (f32[256,128]{1,0:T(8,128)S(1)}, f32[256,128]{1,0:T(8,128)S(1)}, u32[]{:S(2)}, u32[]{:S(2)}) collective-permute-start(f32[256,128]{1,0:T(8,128)S(1)} %get-tuple-element.23), channel_id=1, source_target_pairs={{0,24},{8,16},{16,8},{24,0},{1,25},{9,17},{17,9},{25,1},{2,26},{10... | collective-permute-start | bytes 393224 | tf_op jit(solution)/shard_map/ppermute | solution.py:211
  22.9 0.5 collective-permute-start.6
  23.4 0.3 collective-permute-start.5
  23.7 0.0 collective-permute-done.3.refs_3_
  23.7 0.0 collective-permute-done.1.refs_1_
  23.7 0.0 copy-done.1
  23.7 2.0 %compute.1 = (f32[160,256]{1,0:T(8,128)S(1)}, f32[160,256]{1,0:T(8,128)S(1)}, f32[160,128]{1,0:T(8,128)S(1)}, f32[160,128]{1,0:T(8,128)S(1)}) custom-call(s32[4]{0:T(128)S(1)} %copy-done.4, f32[1,2]{1,0:T(1,128)S(1)} %copy-done.5, s32[2]{0:T(128)S(1)} %pad_add_fusion.place_ref, bf16[2,256,512]{2,1,0:T(8,128)(2,1)S(1)} %get-tuple-element.16.straight_ref, ...), custom_call_target="tpu_custom_call" | custom-call | tf_op jit(solution)/shard_map/compute/pallas_call | solution.py:299
  25.7 0.1 collective-permute-start.4
  25.8 1.3 %collective-permute-done.4 = f32[160,128]{1,0:T(8,128)S(1)} collective-permute-done((f32[160,128]{1,0:T(8,128)S(1)}, f32[160,128]{1,0:T(8,128)S(1)}, u32[]{:S(2)}, u32[]{:S(2)}) %collective-permute-start.4) | collective-permute-done | bytes 81952 | tf_op jit(solution)/shard_map/ppermute | solution.py:211
  27.0 0.0 collective-permute-done.7
  27.1 1.8 %collective-permute-done.6 = f32[256,128]{1,0:T(8,128)S(1)} collective-permute-done((f32[256,128]{1,0:T(8,128)S(1)}, f32[256,128]{1,0:T(8,128)S(1)}, u32[]{:S(2)}, u32[]{:S(2)}) %collective-permute-start.6) | collective-permute-done | bytes 131104 | tf_op jit(solution)/shard_map/ppermute | solution.py:211
  28.9 0.0 collective-permute-done.5
  28.9 0.1 collective-permute-start.10
  29.0 0.1 collective-permute-start.8
  29.1 1.3 %collective-permute-done.10 = f32[160,256]{1,0:T(8,128)S(1)} collective-permute-done((f32[160,256]{1,0:T(8,128)S(1)}, f32[160,256]{1,0:T(8,128)S(1)}, u32[]{:S(2)}, u32[]{:S(2)}) %collective-permute-start.10) | collective-permute-done | bytes 163872 | tf_op jit(solution)/shard_map/ppermute | solution.py:211
  30.4 1.8 %collective-permute-start.13 = (f32[160,256]{1,0:T(8,128)S(1)}, f32[160,256]{1,0:T(8,128)S(1)}, u32[]{:S(2)}, u32[]{:S(2)}) collective-permute-start(f32[160,256]{1,0:T(8,128)S(1)} %add.45), channel_id=1, source_target_pairs={{0,24},{8,16},{16,8},{24,0},{1,25},{9,17},{17,9},{25,1},{2,26},{10... | collective-permute-start | bytes 491528 | tf_op jit(solution)/shard_map/ppermute | solution.py:211
  32.2 1.2 %collective-permute-start.12 = (f32[160,256]{1,0:T(8,128)S(1)}, f32[160,256]{1,0:T(8,128)S(1)}, u32[]{:S(2)}, u32[]{:S(2)}) collective-permute-start(f32[160,256]{1,0:T(8,128)S(1)} %add.45), channel_id=1, source_target_pairs={{0,16},{8,24},{16,0},{24,8},{1,17},{9,25},{17,1},{25,9},{2,18},{10... | collective-permute-start | bytes 491528 | tf_op jit(solution)/shard_map/ppermute | solution.py:211
  33.4 0.6 %collective-permute-start.11 = (f32[160,256]{1,0:T(8,128)S(1)}, f32[160,256]{1,0:T(8,128)S(1)}, u32[]{:S(2)}, u32[]{:S(2)}) collective-permute-start(f32[160,256]{1,0:T(8,128)S(1)} %add.45), channel_id=1, source_target_pairs={{0,8},{8,0},{16,24},{24,16},{1,9},{9,1},{17,25},{25,17},{2,10},{10... | collective-permute-start | bytes 491528 | tf_op jit(solution)/shard_map/ppermute | solution.py:211
  34.0 0.0 collective-permute-done.8
  34.0 0.6 %collective-permute-start.9 = (f32[160,128]{1,0:T(8,128)S(1)}, f32[160,128]{1,0:T(8,128)S(1)}, u32[]{:S(2)}, u32[]{:S(2)}) collective-permute-start(f32[160,128]{1,0:T(8,128)S(1)} %add.43), channel_id=1, source_target_pairs={{0,4},{2,6},{4,0},{6,2},{1,5},{3,7},{5,1},{7,3},{8,12},{10,14},{12... | collective-permute-start | bytes 245768 | tf_op jit(solution)/shard_map/ppermute | solution.py:211
  34.6 5.9 %collective-permute-done.9 = f32[160,128]{1,0:T(8,128)S(1)} collective-permute-done((f32[160,128]{1,0:T(8,128)S(1)}, f32[160,128]{1,0:T(8,128)S(1)}, u32[]{:S(2)}, u32[]{:S(2)}) %collective-permute-start.9) | collective-permute-done | bytes 81952 | tf_op jit(solution)/shard_map/ppermute | solution.py:211
  40.5 0.0 collective-permute-done.13
  40.6 0.6 %collective-permute-done.12 = f32[160,256]{1,0:T(8,128)S(1)} collective-permute-done((f32[160,256]{1,0:T(8,128)S(1)}, f32[160,256]{1,0:T(8,128)S(1)}, u32[]{:S(2)}, u32[]{:S(2)}) %collective-permute-start.12) | collective-permute-done | bytes 163872 | tf_op jit(solution)/shard_map/ppermute | solution.py:211
  41.1 0.0 collective-permute-done.11
  41.2 1.8 %collective-permute-start.17 = (f32[160,128]{1,0:T(8,128)S(1)}, f32[160,128]{1,0:T(8,128)S(1)}, u32[]{:S(2)}, u32[]{:S(2)}) collective-permute-start(f32[160,128]{1,0:T(8,128)S(1)} %add.44), channel_id=1, source_target_pairs={{0,24},{8,16},{16,8},{24,0},{1,25},{9,17},{17,9},{25,1},{2,26},{10... | collective-permute-start | bytes 245768 | tf_op jit(solution)/shard_map/ppermute | solution.py:211
  43.0 1.2 %collective-permute-start.16 = (f32[160,128]{1,0:T(8,128)S(1)}, f32[160,128]{1,0:T(8,128)S(1)}, u32[]{:S(2)}, u32[]{:S(2)}) collective-permute-start(f32[160,128]{1,0:T(8,128)S(1)} %add.44), channel_id=1, source_target_pairs={{0,16},{8,24},{16,0},{24,8},{1,17},{9,25},{17,1},{25,9},{2,18},{10... | collective-permute-start | bytes 245768 | tf_op jit(solution)/shard_map/ppermute | solution.py:211
  44.2 0.6 %collective-permute-start.15 = (f32[160,128]{1,0:T(8,128)S(1)}, f32[160,128]{1,0:T(8,128)S(1)}, u32[]{:S(2)}, u32[]{:S(2)}) collective-permute-start(f32[160,128]{1,0:T(8,128)S(1)} %add.44), channel_id=1, source_target_pairs={{0,8},{8,0},{16,24},{24,16},{1,9},{9,1},{17,25},{25,17},{2,10},{10... | collective-permute-start | bytes 245768 | tf_op jit(solution)/shard_map/ppermute | solution.py:211
  44.7 0.0 collective-permute-start.19
  44.7 0.5 collective-permute-start.14
  45.2 1.4 %collective-permute-done.17 = f32[160,128]{1,0:T(8,128)S(1)} collective-permute-done((f32[160,128]{1,0:T(8,128)S(1)}, f32[160,128]{1,0:T(8,128)S(1)}, u32[]{:S(2)}, u32[]{:S(2)}) %collective-permute-start.17) | collective-permute-done | bytes 81952 | tf_op jit(solution)/shard_map/ppermute | solution.py:211
  46.7 1.6 %collective-permute-done.16 = f32[160,128]{1,0:T(8,128)S(1)} collective-permute-done((f32[160,128]{1,0:T(8,128)S(1)}, f32[160,128]{1,0:T(8,128)S(1)}, u32[]{:S(2)}, u32[]{:S(2)}) %collective-permute-start.16) | collective-permute-done | bytes 81952 | tf_op jit(solution)/shard_map/ppermute | solution.py:211
  48.3 0.3 collective-permute-done.15
  48.6 0.1 collective-permute-start.18
  48.7 0.0 collective-permute-done.19.other_term_ref
  48.7 1.3 %collective-permute-done.18.other_t_ref = f32[160,128]{1,0:T(8,128)S(1)} collective-permute-done((f32[160,128]{1,0:T(8,128)S(1)}, f32[160,128]{1,0:T(8,128)S(1)}, u32[]{:S(2)}, u32[]{:S(2)}) %collective-permute-start.18) | collective-permute-done | bytes 81952 | tf_op jit(solution)/shard_map/ppermute | solution.py:211
  50.0 0.0 collective-permute-done.14.other_d_ref
  50.0 1.4 %expand.1 = (f32[256,256]{1,0:T(8,128)}, f32[512,128]{1,0:T(8,128)}) custom-call(s32[4]{0:T(128)S(1)} %copy-done.4, s32[2]{0:T(128)S(1)} %pad_add_fusion.place_ref, f32[160,256]{1,0:T(8,128)S(1)} %add_add_fusion.mine_d_ref, f32[160,256]{1,0:T(8,128)S(1)} %collective-permute-done.14.other_d_ref, f32[160,128]{1,0:T(8,128)S(1)} %add_add_fusion.2.mine_t_ref, ...), custom_call_target="tpu_custom_call" | custom-call | tf_op jit(solution)/shard_map/expand/pallas_call | solution.py:330
  (7 shorter events, 0.1 us)
Async XLA Ops:
  0.6 11.1 %copy-start.3 = (bf16[1,2,512,128]{3,2,1,0:T(8,128)(2,1)S(1)}, bf16[1,2,512,128]{3,2,1,0:T(8,128)(2,1)}, u32[]{:S(2)}) copy-start(bf16[1,2,512,128]{3,2,1,0:T(8,128)(2,1)} %param.10) | copy-start | bytes 786436
  3.7 8.1 %collective-permute-start = (bf16[640,128]{1,0:T(8,128)(2,1)}, bf16[640,128]{1,0:T(8,128)(2,1)S(1)}, u32[]{:S(2)}, u32[]{:S(2)}) collective-permute-start(bf16[640,128]{1,0:T(8,128)(2,1)} %pack.1.refs_0_), channel_id=1, source_target_pairs={{0,1},{1,0},{2,3},{3,2},{4,5},{5,4},{6,7},{7,6},{8,9},{9,8},{10,11... | collective-permute-start | bytes 491528 | tf_op jit(solution)/shard_map/ppermute | solution.py:211
  4.2 16.0 %collective-permute-start.2 = (bf16[640,128]{1,0:T(8,128)(2,1)}, bf16[640,128]{1,0:T(8,128)(2,1)S(1)}, u32[]{:S(2)}, u32[]{:S(2)}) collective-permute-start(bf16[640,128]{1,0:T(8,128)(2,1)} %pack.1.refs_0_), channel_id=1, source_target_pairs={{4,0},{6,2},{0,4},{2,6},{5,1},{7,3},{1,5},{3,7},{12,8},{14,10},{8,... | collective-permute-start | bytes 491528 | tf_op jit(solution)/shard_map/ppermute | solution.py:272
  7.9 15.8 %collective-permute-start.3 = (bf16[640,128]{1,0:T(8,128)(2,1)}, bf16[640,128]{1,0:T(8,128)(2,1)S(1)}, u32[]{:S(2)}, u32[]{:S(2)}) collective-permute-start(bf16[640,128]{1,0:T(8,128)(2,1)} %pack.1.refs_0_), channel_id=1, source_target_pairs={{6,0},{0,2},{2,4},{4,6},{7,1},{1,3},{3,5},{5,7},{14,8},{8,10},{10,... | collective-permute-start | bytes 491528 | tf_op jit(solution)/shard_map/ppermute | solution.py:272
  9.4 14.3 %collective-permute-start.1 = (bf16[640,128]{1,0:T(8,128)(2,1)}, bf16[640,128]{1,0:T(8,128)(2,1)S(1)}, u32[]{:S(2)}, u32[]{:S(2)}) collective-permute-start(bf16[640,128]{1,0:T(8,128)(2,1)} %pack.1.refs_0_), channel_id=1, source_target_pairs={{2,0},{4,2},{6,4},{0,6},{3,1},{5,3},{7,5},{1,7},{10,8},{12,10},{14... | collective-permute-start | bytes 491528 | tf_op jit(solution)/shard_map/ppermute | solution.py:272
  11.8 0.7 %copy-start.4 = (s32[4]{0:T(128)S(1)}, s32[4]{0:T(128)}, u32[]{:S(2)}) copy-start(s32[4]{0:T(128)} %widths_ref.7) | copy-start | bytes 52
  11.8 0.7 %copy-start.5 = (f32[1,2]{1,0:T(1,128)S(1)}, f32[1,2]{1,0:T(1,128)}, u32[]{:S(2)}) copy-start(f32[1,2]{1,0:T(1,128)} %weights_ref.3) | copy-start | bytes 28
  12.4 0.9 %copy-start = (bf16[640,128]{1,0:T(8,128)(2,1)S(1)}, bf16[640,128]{1,0:T(8,128)(2,1)}, u32[]{:S(2)}) copy-start(bf16[640,128]{1,0:T(8,128)(2,1)} %pack.1.refs_0_) | copy-start | bytes 491524
  13.3 1.0 %copy-start.2 = (bf16[1,2,256,4,1,128]{5,3,4,2,1,0:T(4,128)(2,1)S(1)}, bf16[1,2,256,4,1,128]{5,3,4,2,1,0:T(4,128)(2,1)}, u32[]{:S(2)}) copy-start(bf16[1,2,256,4,1,128]{5,3,4,2,1,0:T(4,128)(2,1)} %param.6) | copy-start | bytes 1572868
  14.4 9.3 %copy-start.1 = (bf16[640,128]{1,0:T(8,128)(2,1)S(1)}, bf16[640,128]{1,0:T(8,128)(2,1)}, u32[]{:S(2)}) copy-start(bf16[640,128]{1,0:T(8,128)(2,1)} %pack.1.refs_0_) | copy-start | bytes 491524
  20.2 6.9 %collective-permute-start.7 = (f32[256,128]{1,0:T(8,128)S(1)}, f32[256,128]{1,0:T(8,128)S(1)}, u32[]{:S(2)}, u32[]{:S(2)}) collective-permute-start(f32[256,128]{1,0:T(8,128)S(1)} %get-tuple-element.23), channel_id=1, source_target_pairs={{0,24},{8,16},{16,8},{24,0},{1,25},{9,17},{17,9},{25,1},{2,26},{10... | collective-permute-start | bytes 393224 | tf_op jit(solution)/shard_map/ppermute | solution.py:211
  22.9 6.0 %collective-permute-start.6 = (f32[256,128]{1,0:T(8,128)S(1)}, f32[256,128]{1,0:T(8,128)S(1)}, u32[]{:S(2)}, u32[]{:S(2)}) collective-permute-start(f32[256,128]{1,0:T(8,128)S(1)} %get-tuple-element.23), channel_id=1, source_target_pairs={{0,16},{8,24},{16,0},{24,8},{1,17},{9,25},{17,1},{25,9},{2,18},{10... | collective-permute-start | bytes 393224 | tf_op jit(solution)/shard_map/ppermute | solution.py:211
  23.4 5.5 %collective-permute-start.5 = (f32[256,128]{1,0:T(8,128)S(1)}, f32[256,128]{1,0:T(8,128)S(1)}, u32[]{:S(2)}, u32[]{:S(2)}) collective-permute-start(f32[256,128]{1,0:T(8,128)S(1)} %get-tuple-element.23), channel_id=1, source_target_pairs={{0,8},{8,0},{16,24},{24,16},{1,9},{9,1},{17,25},{25,17},{2,10},{10... | collective-permute-start | bytes 393224 | tf_op jit(solution)/shard_map/ppermute | solution.py:211
  25.7 1.3 %collective-permute-start.4 = (f32[160,128]{1,0:T(8,128)S(1)}, f32[160,128]{1,0:T(8,128)S(1)}, u32[]{:S(2)}, u32[]{:S(2)}) collective-permute-start(f32[160,128]{1,0:T(8,128)S(1)} %get-tuple-element.21), channel_id=1, source_target_pairs={{0,1},{1,0},{2,3},{3,2},{4,5},{5,4},{6,7},{7,6},{8,9},{9,8},{10,11... | collective-permute-start | bytes 245768 | tf_op jit(solution)/shard_map/ppermute | solution.py:211
  28.9 1.5 %collective-permute-start.10 = (f32[160,256]{1,0:T(8,128)S(1)}, f32[160,256]{1,0:T(8,128)S(1)}, u32[]{:S(2)}, u32[]{:S(2)}) collective-permute-start(f32[160,256]{1,0:T(8,128)S(1)} %get-tuple-element.26), channel_id=1, source_target_pairs={{0,1},{1,0},{2,3},{3,2},{4,5},{5,4},{6,7},{7,6},{8,9},{9,8},{10,11... | collective-permute-start | bytes 491528 | tf_op jit(solution)/shard_map/ppermute | solution.py:211
  29.0 5.0 %collective-permute-start.8 = (f32[160,128]{1,0:T(8,128)S(1)}, f32[160,128]{1,0:T(8,128)S(1)}, u32[]{:S(2)}, u32[]{:S(2)}) collective-permute-start(f32[160,128]{1,0:T(8,128)S(1)} %add.39), channel_id=1, source_target_pairs={{0,2},{2,0},{4,6},{6,4},{1,3},{3,1},{5,7},{7,5},{8,10},{10,8},{12,... | collective-permute-start | bytes 245768 | tf_op jit(solution)/shard_map/ppermute | solution.py:211
  30.4 10.1 %collective-permute-start.13 = (f32[160,256]{1,0:T(8,128)S(1)}, f32[160,256]{1,0:T(8,128)S(1)}, u32[]{:S(2)}, u32[]{:S(2)}) collective-permute-start(f32[160,256]{1,0:T(8,128)S(1)} %add.45), channel_id=1, source_target_pairs={{0,24},{8,16},{16,8},{24,0},{1,25},{9,17},{17,9},{25,1},{2,26},{10... | collective-permute-start | bytes 491528 | tf_op jit(solution)/shard_map/ppermute | solution.py:211
  32.2 8.9 %collective-permute-start.12 = (f32[160,256]{1,0:T(8,128)S(1)}, f32[160,256]{1,0:T(8,128)S(1)}, u32[]{:S(2)}, u32[]{:S(2)}) collective-permute-start(f32[160,256]{1,0:T(8,128)S(1)} %add.45), channel_id=1, source_target_pairs={{0,16},{8,24},{16,0},{24,8},{1,17},{9,25},{17,1},{25,9},{2,18},{10... | collective-permute-start | bytes 491528 | tf_op jit(solution)/shard_map/ppermute | solution.py:211
  33.4 7.7 %collective-permute-start.11 = (f32[160,256]{1,0:T(8,128)S(1)}, f32[160,256]{1,0:T(8,128)S(1)}, u32[]{:S(2)}, u32[]{:S(2)}) collective-permute-start(f32[160,256]{1,0:T(8,128)S(1)} %add.45), channel_id=1, source_target_pairs={{0,8},{8,0},{16,24},{24,16},{1,9},{9,1},{17,25},{25,17},{2,10},{10... | collective-permute-start | bytes 491528 | tf_op jit(solution)/shard_map/ppermute | solution.py:211
  34.0 6.5 %collective-permute-start.9 = (f32[160,128]{1,0:T(8,128)S(1)}, f32[160,128]{1,0:T(8,128)S(1)}, u32[]{:S(2)}, u32[]{:S(2)}) collective-permute-start(f32[160,128]{1,0:T(8,128)S(1)} %add.43), channel_id=1, source_target_pairs={{0,4},{2,6},{4,0},{6,2},{1,5},{3,7},{5,1},{7,3},{8,12},{10,14},{12... | collective-permute-start | bytes 245768 | tf_op jit(solution)/shard_map/ppermute | solution.py:211
  41.2 5.5 %collective-permute-start.17 = (f32[160,128]{1,0:T(8,128)S(1)}, f32[160,128]{1,0:T(8,128)S(1)}, u32[]{:S(2)}, u32[]{:S(2)}) collective-permute-start(f32[160,128]{1,0:T(8,128)S(1)} %add.44), channel_id=1, source_target_pairs={{0,24},{8,16},{16,8},{24,0},{1,25},{9,17},{17,9},{25,1},{2,26},{10... | collective-permute-start | bytes 245768 | tf_op jit(solution)/shard_map/ppermute | solution.py:211
  43.0 5.3 %collective-permute-start.16 = (f32[160,128]{1,0:T(8,128)S(1)}, f32[160,128]{1,0:T(8,128)S(1)}, u32[]{:S(2)}, u32[]{:S(2)}) collective-permute-start(f32[160,128]{1,0:T(8,128)S(1)} %add.44), channel_id=1, source_target_pairs={{0,16},{8,24},{16,0},{24,8},{1,17},{9,25},{17,1},{25,9},{2,18},{10... | collective-permute-start | bytes 245768 | tf_op jit(solution)/shard_map/ppermute | solution.py:211
  44.2 4.4 %collective-permute-start.15 = (f32[160,128]{1,0:T(8,128)S(1)}, f32[160,128]{1,0:T(8,128)S(1)}, u32[]{:S(2)}, u32[]{:S(2)}) collective-permute-start(f32[160,128]{1,0:T(8,128)S(1)} %add.44), channel_id=1, source_target_pairs={{0,8},{8,0},{16,24},{24,16},{1,9},{9,1},{17,25},{25,17},{2,10},{10... | collective-permute-start | bytes 245768 | tf_op jit(solution)/shard_map/ppermute | solution.py:211
  44.7 4.0 %collective-permute-start.19 = (f32[256,128]{1,0:T(8,128)S(1)}, f32[256,128]{1,0:T(8,128)S(1)}, u32[]{:S(2)}, u32[]{:S(2)}) collective-permute-start(f32[256,128]{1,0:T(8,128)S(1)} %add_add_fusion.1.mine_term_ref), channel_id=1, source_target_pairs={{0,1},{1,0},{2,3},{3,2},{4,5},{5,4},{6,7},{7,6},{8,9},{9,8},{10,11... | collective-permute-start | bytes 393224 | tf_op jit(solution)/shard_map/ppermute | solution.py:211
  44.7 5.2 %collective-permute-start.14 = (f32[160,256]{1,0:T(8,128)S(1)}, f32[160,256]{1,0:T(8,128)S(1)}, u32[]{:S(2)}, u32[]{:S(2)}) collective-permute-start(f32[160,256]{1,0:T(8,128)S(1)} %add_add_fusion.mine_d_ref), channel_id=1, source_target_pairs={{0,1},{1,0},{2,3},{3,2},{4,5},{5,4},{6,7},{7,6},{8,9},{9,8},{10,11... | collective-permute-start | bytes 491528 | tf_op jit(solution)/shard_map/ppermute | solution.py:211
  48.6 1.3 %collective-permute-start.18 = (f32[160,128]{1,0:T(8,128)S(1)}, f32[160,128]{1,0:T(8,128)S(1)}, u32[]{:S(2)}, u32[]{:S(2)}) collective-permute-start(f32[160,128]{1,0:T(8,128)S(1)} %add_add_fusion.2.mine_t_ref), channel_id=1, source_target_pairs={{0,1},{1,0},{2,3},{3,2},{4,5},{5,4},{6,7},{7,6},{8,9},{9,8},{10,11... | collective-permute-start | bytes 245768 | tf_op jit(solution)/shard_map/ppermute | solution.py:211

commit v12 on v11

--- a/solution.py
+++ b/solution.py
@@ -25,16 +25,8 @@
     return offsets
 
 
-def pack_kernel(
-    supernodes, slot, pattern_ref, widths_ref, panel_ref, packed_ref, held_ref, arrived
-):
+def pack_kernel(supernodes, slot, pattern_ref, widths_ref, panel_ref, packed_ref):
     packed_width = packed_ref.shape[0] // 2
-    copies = [
-        pltpu.make_async_copy(panel_ref.at[part], held_ref.at[part], arrived.at[part])
-        for part in range(2)
-    ]
-    for copy in copies:
-        copy.start()
     offsets = offsets_of(widths_ref, supernodes)
     lane = lax.broadcasted_iota(jnp.int32, (1, slot), 1)
     place = []
@@ -45,9 +37,8 @@
     target = lax.broadcasted_iota(jnp.int32, (packed_width, supernodes * slot), 0)
     select = jnp.where(target == place, 1.0, 0.0).astype(BF16)
     for part in range(2):
-        copies[part].wait()
         packed_ref[part * packed_width:(part + 1) * packed_width, :] = rows_by_rows(
-            select, held_ref[part]
+            select, panel_ref[part]
         ).astype(BF16)
 
 
@@ -257,12 +248,9 @@
 
     packed = pl.pallas_call(
         functools.partial(pack_kernel, supernodes, slot),
-        in_specs=[SMEM_SPEC, SMEM_SPEC, pl.BlockSpec(memory_space=pl.ANY)],
+        in_specs=[SMEM_SPEC, SMEM_SPEC, VMEM_SPEC],
         out_specs=VMEM_SPEC,
         out_shape=jax.ShapeDtypeStruct((2 * packed_width, block), BF16),
-        scratch_shapes=[
-            pltpu.VMEM((2, block, total_cols), BF16), pltpu.SemaphoreType.DMA((2,))
-        ],
         name="pack",
     )(block_pattern, sup_widths, l_panel[0])
 
@@ -292,8 +280,6 @@
         sup_widths, pole_weights, place,
         found_inverse.reshape(2 * local_rows * row_count, block), diag_inverse[0], *own,
     )
-    first_arrival = min(blocks, key=lambda shift: (shift == 0, -min(shift, row_count - shift)))
-    term, blocks[first_arrival] = lax.optimization_barrier((term, blocks[first_arrival]))
     term = sum_direct(term, "pole")
 
     keep_d, send_d, keep_t, send_t = pl.pallas_call(

time: 51.7 us -> 48.8 us (0.944)
  waiting for transfers between devices: 20.1 us -> 14.1 us
  starting transfers between devices: 20 us -> 24.2 us
  Pallas kernels: 7.73 us -> 6.71 us
    ppermute x17, starting transfers between devices: 12.5 us -> 17.7 us  [swap(): lax.ppermute(value, axis, [(i, i ^ bit) for i in range(lax.axis_size(axis...]
    ppermute x17, waiting for transfers between devices: 15.5 us -> 11.4 us  [swap(): lax.ppermute(value, axis, [(i, i ^ bit) for i in range(lax.axis_size(axis...]
    ppermute x3, waiting for transfers between devices: 4.51 us -> 2.72 us  [per_device(): blocks[shift] = lax.ppermute(packed, 'row', pairs)]
    pallas_call x1, Pallas kernels: 3.02 us -> 2 us  [per_device(): pl.pallas_call(functools.partial(pack_kernel, supernodes, slot), in_specs...]
    ppermute x3, starting transfers between devices: 7.48 us -> 6.51 us  [per_device(): blocks[shift] = lax.ppermute(packed, 'row', pairs)]
  transfers between devices with their start and end apart: 20 -> 20, of which waited for: 10 -> 9; matrix products, arithmetic and copies ran while one was open for 0% -> 0% of each run, Pallas kernels for 6% -> 7%
where the time goes in v12:
time: 48.8 us; the launch traced here: 48.6 us
  starting transfers between devices  24.2 us (50%)
  waiting for transfers between devices  14.1 us (29%)
  Pallas kernels  6.71 us (14%)
  local copies, waits for them, and re-layouts  2.63 us (5%)
  between operations  0.76 us (2%)
    ppermute x17, starting transfers between devices, swap(): lax.ppermute(value, axis, [(i, i ^ bit) for i in range(lax.axis_size(axis...  17.7 us
    ppermute x17, waiting for transfers between devices, swap(): lax.ppermute(value, axis, [(i, i ^ bit) for i in range(lax.axis_size(axis...  11.4 us
    ppermute x3, starting transfers between devices, per_device(): blocks[shift] = lax.ppermute(packed, 'row', pairs)  6.51 us
    ppermute x3, waiting for transfers between devices, per_device(): blocks[shift] = lax.ppermute(packed, 'row', pairs)  2.72 us
    unnamed x12, local copies, waits for them, and re-layouts  2.63 us
    pallas_call x1, Pallas kernels, per_device(): pl.pallas_call(functools.partial(pack_kernel, supernodes, slot), in_specs...  2 us
    pallas_call x1, Pallas kernels, per_device(): pl.pallas_call(functools.partial(compute_kernel, col_count, supernodes, s...  1.99 us
    pallas_call x1, Pallas kernels, per_device(): pl.pallas_call(functools.partial(expand_kernel, col_count, slot), in_spec...  1.44 us
  transfers between devices with their start and end apart: 20, of which 9 were waited for; matrix products, arithmetic and copies ran while one was open for 0% of the time, Pallas kernels for 7%

profile of v12, /device:TPU:0, one launch (start us, length us, event | category | flops | bytes accessed | tf_op | source)
XLA Modules:
  0.0 48.6 jit_solution(16220630947472892043)
XLA Ops:
  0.6 0.0 copy-start.3
  0.6 2.0 %pack.1.refs_0_ = bf16[640,128]{1,0:T(8,128)(2,1)} custom-call(s32[1,4]{1,0:T(1,128)} %pattern_ref.1, s32[4]{0:T(128)} %widths_ref.7, bf16[2,128,512]{2,1,0:T(8,128)(2,1)} %bitcast.7), custom_call_target="tpu_custom_call" | custom-call | tf_op jit(solution)/shard_map/pack/pallas_call | solution.py:249
  2.6 0.5 collective-permute-start
  3.1 2.6 %collective-permute-start.3 = (bf16[640,128]{1,0:T(8,128)(2,1)}, bf16[640,128]{1,0:T(8,128)(2,1)S(1)}, u32[]{:S(2)}, u32[]{:S(2)}) collective-permute-start(bf16[640,128]{1,0:T(8,128)(2,1)} %pack.1.refs_0_), channel_id=1, source_target_pairs={{6,0},{0,2},{2,4},{4,6},{7,1},{1,3},{3,5},{5,7},{14,8},{8,10},{10,... | collective-permute-start | bytes 491528 | tf_op jit(solution)/shard_map/ppermute | solution.py:260
  5.7 2.6 %collective-permute-start.2 = (bf16[640,128]{1,0:T(8,128)(2,1)}, bf16[640,128]{1,0:T(8,128)(2,1)S(1)}, u32[]{:S(2)}, u32[]{:S(2)}) collective-permute-start(bf16[640,128]{1,0:T(8,128)(2,1)} %pack.1.refs_0_), channel_id=1, source_target_pairs={{4,0},{6,2},{0,4},{2,6},{5,1},{7,3},{1,5},{3,7},{12,8},{14,10},{8,... | collective-permute-start | bytes 491528 | tf_op jit(solution)/shard_map/ppermute | solution.py:260
  8.3 1.3 %collective-permute-start.1 = (bf16[640,128]{1,0:T(8,128)(2,1)}, bf16[640,128]{1,0:T(8,128)(2,1)S(1)}, u32[]{:S(2)}, u32[]{:S(2)}) collective-permute-start(bf16[640,128]{1,0:T(8,128)(2,1)} %pack.1.refs_0_), channel_id=1, source_target_pairs={{2,0},{4,2},{6,4},{0,6},{3,1},{5,3},{7,5},{1,7},{10,8},{12,10},{14... | collective-permute-start | bytes 491528 | tf_op jit(solution)/shard_map/ppermute | solution.py:260
  9.6 0.1 pad_add_fusion.place_ref
  9.7 0.0 collective-permute-done.refs_1_
  9.7 0.0 copy-start.4
  9.7 0.0 copy-start.5
  9.7 0.0 copy-done.3
  9.7 0.6 %copy-done.4 = s32[4]{0:T(128)S(1)} copy-done((s32[4]{0:T(128)S(1)}, s32[4]{0:T(128)}, u32[]{:S(2)}) %copy-start.4) | copy-done | bytes 40
  10.3 0.0 copy-done.5
  10.4 0.0 copy-start
  10.4 0.9 %copy-done = bf16[640,128]{1,0:T(8,128)(2,1)S(1)} copy-done((bf16[640,128]{1,0:T(8,128)(2,1)S(1)}, bf16[640,128]{1,0:T(8,128)(2,1)}, u32[]{:S(2)}) %copy-start) | copy-done | bytes 163864
  11.3 0.0 copy-start.2
  11.3 1.0 %copy-done.2 = bf16[1,2,256,4,1,128]{5,3,4,2,1,0:T(4,128)(2,1)S(1)} copy-done((bf16[1,2,256,4,1,128]{5,3,4,2,1,0:T(4,128)(2,1)S(1)}, bf16[1,2,256,4,1,128]{5,3,4,2,1,0:T(4,128)(2,1)}, u32[]{:S(2)}) %copy-start.2) | copy-done | bytes 524312
  12.3 0.0 copy-start.1
  12.3 1.3 %prepare.1 = (bf16[2,256,512]{2,1,0:T(8,128)(2,1)S(1)}, bf16[512,512]{1,0:T(8,128)(2,1)S(1)}, f32[256,128]{1,0:T(8,128)S(1)}) custom-call(s32[4]{0:T(128)S(1)} %copy-done.4, f32[1,2]{1,0:T(1,128)S(1)} %copy-done.5, s32[2]{0:T(128)S(1)} %pad_add_fusion.place_ref, bf16[2048,128]{1,0:T(8,128)(2,1)S(1)} %bitcast.5, bf16[2,512,128]{2,1,0:T(8,128)(2,1)S(1)} %bitcast.6, ...), custom_call_target="tpu_custom_call" | custom-call | flops 134217728 | bytes 1048576 | tf_op jit(solution)/shard_map/prepare/pallas_call | solution.py:263
  13.6 2.5 %collective-permute-start.7 = (f32[256,128]{1,0:T(8,128)S(1)}, f32[256,128]{1,0:T(8,128)S(1)}, u32[]{:S(2)}, u32[]{:S(2)}) collective-permute-start(f32[256,128]{1,0:T(8,128)S(1)} %get-tuple-element.19), channel_id=1, source_target_pairs={{0,24},{8,16},{16,8},{24,0},{1,25},{9,17},{17,9},{25,1},{2,26},{10... | collective-permute-start | bytes 393224 | tf_op jit(solution)/shard_map/ppermute | solution.py:202
  16.1 0.5 %collective-permute-start.6 = (f32[256,128]{1,0:T(8,128)S(1)}, f32[256,128]{1,0:T(8,128)S(1)}, u32[]{:S(2)}, u32[]{:S(2)}) collective-permute-start(f32[256,128]{1,0:T(8,128)S(1)} %get-tuple-element.19), channel_id=1, source_target_pairs={{0,16},{8,24},{16,0},{24,8},{1,17},{9,25},{17,1},{25,9},{2,18},{10... | collective-permute-start | bytes 393224 | tf_op jit(solution)/shard_map/ppermute | solution.py:202
  16.6 0.0 collective-permute-done.3.refs_3_
  16.6 0.5 %collective-permute-start.5 = (f32[256,128]{1,0:T(8,128)S(1)}, f32[256,128]{1,0:T(8,128)S(1)}, u32[]{:S(2)}, u32[]{:S(2)}) collective-permute-start(f32[256,128]{1,0:T(8,128)S(1)} %get-tuple-element.19), channel_id=1, source_target_pairs={{0,8},{8,0},{16,24},{24,16},{1,9},{9,1},{17,25},{25,17},{2,10},{10... | collective-permute-start | bytes 393224 | tf_op jit(solution)/shard_map/ppermute | solution.py:202
  17.2 2.7 %collective-permute-done.2.refs_2_ = bf16[640,128]{1,0:T(8,128)(2,1)S(1)} collective-permute-done((bf16[640,128]{1,0:T(8,128)(2,1)}, bf16[640,128]{1,0:T(8,128)(2,1)S(1)}, u32[]{:S(2)}, u32[]{:S(2)}) %collective-permute-start.2) | collective-permute-done | bytes 163872 | tf_op jit(solution)/shard_map/ppermute | solution.py:260
  19.9 0.0 collective-permute-done.1.refs_1_
  19.9 0.0 copy-done.1
  19.9 2.0 %compute.1 = (f32[160,256]{1,0:T(8,128)S(1)}, f32[160,256]{1,0:T(8,128)S(1)}, f32[160,128]{1,0:T(8,128)S(1)}, f32[160,128]{1,0:T(8,128)S(1)}) custom-call(s32[4]{0:T(128)S(1)} %copy-done.4, f32[1,2]{1,0:T(1,128)S(1)} %copy-done.5, s32[2]{0:T(128)S(1)} %pad_add_fusion.place_ref, bf16[2,256,512]{2,1,0:T(8,128)(2,1)S(1)} %get-tuple-element.14.straight_ref, ...), custom_call_target="tpu_custom_call" | custom-call | tf_op jit(solution)/shard_map/compute/pallas_call | solution.py:285
  21.9 0.1 collective-permute-start.4
  22.0 1.3 %collective-permute-done.4 = f32[160,128]{1,0:T(8,128)S(1)} collective-permute-done((f32[160,128]{1,0:T(8,128)S(1)}, f32[160,128]{1,0:T(8,128)S(1)}, u32[]{:S(2)}, u32[]{:S(2)}) %collective-permute-start.4) | collective-permute-done | bytes 81952 | tf_op jit(solution)/shard_map/ppermute | solution.py:202
  23.2 0.0 collective-permute-done.7
  23.2 0.0 collective-permute-done.6
  23.3 0.0 collective-permute-done.5
  23.3 0.2 collective-permute-start.10
  23.5 4.0 %collective-permute-start.8 = (f32[160,128]{1,0:T(8,128)S(1)}, f32[160,128]{1,0:T(8,128)S(1)}, u32[]{:S(2)}, u32[]{:S(2)}) collective-permute-start(f32[160,128]{1,0:T(8,128)S(1)} %add.39), channel_id=1, source_target_pairs={{0,2},{2,0},{4,6},{6,4},{1,3},{3,1},{5,7},{7,5},{8,10},{10,8},{12,... | collective-permute-start | bytes 245768 | tf_op jit(solution)/shard_map/ppermute | solution.py:202
  27.5 0.0 collective-permute-done.10
  27.6 2.5 %collective-permute-start.13 = (f32[160,256]{1,0:T(8,128)S(1)}, f32[160,256]{1,0:T(8,128)S(1)}, u32[]{:S(2)}, u32[]{:S(2)}) collective-permute-start(f32[160,256]{1,0:T(8,128)S(1)} %add.45), channel_id=1, source_target_pairs={{0,24},{8,16},{16,8},{24,0},{1,25},{9,17},{17,9},{25,1},{2,26},{10... | collective-permute-start | bytes 491528 | tf_op jit(solution)/shard_map/ppermute | solution.py:202
  30.1 0.5 %collective-permute-start.12 = (f32[160,256]{1,0:T(8,128)S(1)}, f32[160,256]{1,0:T(8,128)S(1)}, u32[]{:S(2)}, u32[]{:S(2)}) collective-permute-start(f32[160,256]{1,0:T(8,128)S(1)} %add.45), channel_id=1, source_target_pairs={{0,16},{8,24},{16,0},{24,8},{1,17},{9,25},{17,1},{25,9},{2,18},{10... | collective-permute-start | bytes 491528 | tf_op jit(solution)/shard_map/ppermute | solution.py:202
  30.6 0.6 %collective-permute-start.11 = (f32[160,256]{1,0:T(8,128)S(1)}, f32[160,256]{1,0:T(8,128)S(1)}, u32[]{:S(2)}, u32[]{:S(2)}) collective-permute-start(f32[160,256]{1,0:T(8,128)S(1)} %add.45), channel_id=1, source_target_pairs={{0,8},{8,0},{16,24},{24,16},{1,9},{9,1},{17,25},{25,17},{2,10},{10... | collective-permute-start | bytes 491528 | tf_op jit(solution)/shard_map/ppermute | solution.py:202
  31.1 0.0 collective-permute-done.8
  31.1 1.7 %collective-permute-start.9 = (f32[160,128]{1,0:T(8,128)S(1)}, f32[160,128]{1,0:T(8,128)S(1)}, u32[]{:S(2)}, u32[]{:S(2)}) collective-permute-start(f32[160,128]{1,0:T(8,128)S(1)} %add.43), channel_id=1, source_target_pairs={{0,4},{2,6},{4,0},{6,2},{1,5},{3,7},{5,1},{7,3},{8,12},{10,14},{12... | collective-permute-start | bytes 245768 | tf_op jit(solution)/shard_map/ppermute | solution.py:202
  32.8 4.6 %collective-permute-done.9 = f32[160,128]{1,0:T(8,128)S(1)} collective-permute-done((f32[160,128]{1,0:T(8,128)S(1)}, f32[160,128]{1,0:T(8,128)S(1)}, u32[]{:S(2)}, u32[]{:S(2)}) %collective-permute-start.9) | collective-permute-done | bytes 81952 | tf_op jit(solution)/shard_map/ppermute | solution.py:202
  37.5 0.0 collective-permute-done.13
  37.5 0.8 %collective-permute-done.12 = f32[160,256]{1,0:T(8,128)S(1)} collective-permute-done((f32[160,256]{1,0:T(8,128)S(1)}, f32[160,256]{1,0:T(8,128)S(1)}, u32[]{:S(2)}, u32[]{:S(2)}) %collective-permute-start.12) | collective-permute-done | bytes 163872 | tf_op jit(solution)/shard_map/ppermute | solution.py:202
  38.2 0.1 collective-permute-done.11
  38.3 1.7 %collective-permute-start.17 = (f32[160,128]{1,0:T(8,128)S(1)}, f32[160,128]{1,0:T(8,128)S(1)}, u32[]{:S(2)}, u32[]{:S(2)}) collective-permute-start(f32[160,128]{1,0:T(8,128)S(1)} %add.44), channel_id=1, source_target_pairs={{0,24},{8,16},{16,8},{24,0},{1,25},{9,17},{17,9},{25,1},{2,26},{10... | collective-permute-start | bytes 245768 | tf_op jit(solution)/shard_map/ppermute | solution.py:202
  40.1 1.3 %collective-permute-start.16 = (f32[160,128]{1,0:T(8,128)S(1)}, f32[160,128]{1,0:T(8,128)S(1)}, u32[]{:S(2)}, u32[]{:S(2)}) collective-permute-start(f32[160,128]{1,0:T(8,128)S(1)} %add.44), channel_id=1, source_target_pairs={{0,16},{8,24},{16,0},{24,8},{1,17},{9,25},{17,1},{25,9},{2,18},{10... | collective-permute-start | bytes 245768 | tf_op jit(solution)/shard_map/ppermute | solution.py:202
  41.4 0.5 %collective-permute-start.15 = (f32[160,128]{1,0:T(8,128)S(1)}, f32[160,128]{1,0:T(8,128)S(1)}, u32[]{:S(2)}, u32[]{:S(2)}) collective-permute-start(f32[160,128]{1,0:T(8,128)S(1)} %add.44), channel_id=1, source_target_pairs={{0,8},{8,0},{16,24},{24,16},{1,9},{9,1},{17,25},{25,17},{2,10},{10... | collective-permute-start | bytes 245768 | tf_op jit(solution)/shard_map/ppermute | solution.py:202
  41.9 0.0 collective-permute-start.19
  41.9 0.5 %collective-permute-start.14 = (f32[160,256]{1,0:T(8,128)S(1)}, f32[160,256]{1,0:T(8,128)S(1)}, u32[]{:S(2)}, u32[]{:S(2)}) collective-permute-start(f32[160,256]{1,0:T(8,128)S(1)} %add_add_fusion.mine_d_ref), channel_id=1, source_target_pairs={{0,1},{1,0},{2,3},{3,2},{4,5},{5,4},{6,7},{7,6},{8,9},{9,8},{10,11... | collective-permute-start | bytes 491528 | tf_op jit(solution)/shard_map/ppermute | solution.py:202
  42.4 2.0 %collective-permute-done.17 = f32[160,128]{1,0:T(8,128)S(1)} collective-permute-done((f32[160,128]{1,0:T(8,128)S(1)}, f32[160,128]{1,0:T(8,128)S(1)}, u32[]{:S(2)}, u32[]{:S(2)}) %collective-permute-start.17) | collective-permute-done | bytes 81952 | tf_op jit(solution)/shard_map/ppermute | solution.py:202
  44.4 0.9 %collective-permute-done.16 = f32[160,128]{1,0:T(8,128)S(1)} collective-permute-done((f32[160,128]{1,0:T(8,128)S(1)}, f32[160,128]{1,0:T(8,128)S(1)}, u32[]{:S(2)}, u32[]{:S(2)}) %collective-permute-start.16) | collective-permute-done | bytes 81952 | tf_op jit(solution)/shard_map/ppermute | solution.py:202
  45.4 0.5 collective-permute-done.15
  45.8 0.1 collective-permute-start.18
  45.9 0.0 collective-permute-done.19.other_term_ref
  45.9 1.3 %collective-permute-done.18.other_t_ref = f32[160,128]{1,0:T(8,128)S(1)} collective-permute-done((f32[160,128]{1,0:T(8,128)S(1)}, f32[160,128]{1,0:T(8,128)S(1)}, u32[]{:S(2)}, u32[]{:S(2)}) %collective-permute-start.18) | collective-permute-done | bytes 81952 | tf_op jit(solution)/shard_map/ppermute | solution.py:202
  47.2 0.0 collective-permute-done.14.other_d_ref
  47.2 1.4 %expand.1 = (f32[256,256]{1,0:T(8,128)}, f32[512,128]{1,0:T(8,128)}) custom-call(s32[4]{0:T(128)S(1)} %copy-done.4, s32[2]{0:T(128)S(1)} %pad_add_fusion.place_ref, f32[160,256]{1,0:T(8,128)S(1)} %add_add_fusion.mine_d_ref, f32[160,256]{1,0:T(8,128)S(1)} %collective-permute-done.14.other_d_ref, f32[160,128]{1,0:T(8,128)S(1)} %add_add_fusion.2.mine_t_ref, ...), custom_call_target="tpu_custom_call" | custom-call | tf_op jit(solution)/shard_map/expand/pallas_call | solution.py:316
  (7 shorter events, 0.1 us)
Async XLA Ops:
  0.6 9.1 %copy-start.3 = (bf16[1,2,512,128]{3,2,1,0:T(8,128)(2,1)S(1)}, bf16[1,2,512,128]{3,2,1,0:T(8,128)(2,1)}, u32[]{:S(2)}) copy-start(bf16[1,2,512,128]{3,2,1,0:T(8,128)(2,1)} %param.10) | copy-start | bytes 786436
  2.6 7.0 %collective-permute-start = (bf16[640,128]{1,0:T(8,128)(2,1)}, bf16[640,128]{1,0:T(8,128)(2,1)S(1)}, u32[]{:S(2)}, u32[]{:S(2)}) collective-permute-start(bf16[640,128]{1,0:T(8,128)(2,1)} %pack.1.refs_0_), channel_id=1, source_target_pairs={{0,1},{1,0},{2,3},{3,2},{4,5},{5,4},{6,7},{7,6},{8,9},{9,8},{10,11... | collective-permute-start | bytes 491528 | tf_op jit(solution)/shard_map/ppermute | solution.py:202
  3.1 13.5 %collective-permute-start.3 = (bf16[640,128]{1,0:T(8,128)(2,1)}, bf16[640,128]{1,0:T(8,128)(2,1)S(1)}, u32[]{:S(2)}, u32[]{:S(2)}) collective-permute-start(bf16[640,128]{1,0:T(8,128)(2,1)} %pack.1.refs_0_), channel_id=1, source_target_pairs={{6,0},{0,2},{2,4},{4,6},{7,1},{1,3},{3,5},{5,7},{14,8},{8,10},{10,... | collective-permute-start | bytes 491528 | tf_op jit(solution)/shard_map/ppermute | solution.py:260
  5.7 14.2 %collective-permute-start.2 = (bf16[640,128]{1,0:T(8,128)(2,1)}, bf16[640,128]{1,0:T(8,128)(2,1)S(1)}, u32[]{:S(2)}, u32[]{:S(2)}) collective-permute-start(bf16[640,128]{1,0:T(8,128)(2,1)} %pack.1.refs_0_), channel_id=1, source_target_pairs={{4,0},{6,2},{0,4},{2,6},{5,1},{7,3},{1,5},{3,7},{12,8},{14,10},{8,... | collective-permute-start | bytes 491528 | tf_op jit(solution)/shard_map/ppermute | solution.py:260
  8.3 11.6 %collective-permute-start.1 = (bf16[640,128]{1,0:T(8,128)(2,1)}, bf16[640,128]{1,0:T(8,128)(2,1)S(1)}, u32[]{:S(2)}, u32[]{:S(2)}) collective-permute-start(bf16[640,128]{1,0:T(8,128)(2,1)} %pack.1.refs_0_), channel_id=1, source_target_pairs={{2,0},{4,2},{6,4},{0,6},{3,1},{5,3},{7,5},{1,7},{10,8},{12,10},{14... | collective-permute-start | bytes 491528 | tf_op jit(solution)/shard_map/ppermute | solution.py:260
  9.7 0.7 %copy-start.4 = (s32[4]{0:T(128)S(1)}, s32[4]{0:T(128)}, u32[]{:S(2)}) copy-start(s32[4]{0:T(128)} %widths_ref.7) | copy-start | bytes 52
  9.7 0.7 %copy-start.5 = (f32[1,2]{1,0:T(1,128)S(1)}, f32[1,2]{1,0:T(1,128)}, u32[]{:S(2)}) copy-start(f32[1,2]{1,0:T(1,128)} %weights_ref.3) | copy-start | bytes 28
  10.4 0.9 %copy-start = (bf16[640,128]{1,0:T(8,128)(2,1)S(1)}, bf16[640,128]{1,0:T(8,128)(2,1)}, u32[]{:S(2)}) copy-start(bf16[640,128]{1,0:T(8,128)(2,1)} %pack.1.refs_0_) | copy-start | bytes 491524
  11.3 1.0 %copy-start.2 = (bf16[1,2,256,4,1,128]{5,3,4,2,1,0:T(4,128)(2,1)S(1)}, bf16[1,2,256,4,1,128]{5,3,4,2,1,0:T(4,128)(2,1)}, u32[]{:S(2)}) copy-start(bf16[1,2,256,4,1,128]{5,3,4,2,1,0:T(4,128)(2,1)} %param.6) | copy-start | bytes 1572868
  12.3 7.6 %copy-start.1 = (bf16[640,128]{1,0:T(8,128)(2,1)S(1)}, bf16[640,128]{1,0:T(8,128)(2,1)}, u32[]{:S(2)}) copy-start(bf16[640,128]{1,0:T(8,128)(2,1)} %pack.1.refs_0_) | copy-start | bytes 491524
  13.6 9.6 %collective-permute-start.7 = (f32[256,128]{1,0:T(8,128)S(1)}, f32[256,128]{1,0:T(8,128)S(1)}, u32[]{:S(2)}, u32[]{:S(2)}) collective-permute-start(f32[256,128]{1,0:T(8,128)S(1)} %get-tuple-element.19), channel_id=1, source_target_pairs={{0,24},{8,16},{16,8},{24,0},{1,25},{9,17},{17,9},{25,1},{2,26},{10... | collective-permute-start | bytes 393224 | tf_op jit(solution)/shard_map/ppermute | solution.py:202
  16.1 7.1 %collective-permute-start.6 = (f32[256,128]{1,0:T(8,128)S(1)}, f32[256,128]{1,0:T(8,128)S(1)}, u32[]{:S(2)}, u32[]{:S(2)}) collective-permute-start(f32[256,128]{1,0:T(8,128)S(1)} %get-tuple-element.19), channel_id=1, source_target_pairs={{0,16},{8,24},{16,0},{24,8},{1,17},{9,25},{17,1},{25,9},{2,18},{10... | collective-permute-start | bytes 393224 | tf_op jit(solution)/shard_map/ppermute | solution.py:202
  16.6 6.6 %collective-permute-start.5 = (f32[256,128]{1,0:T(8,128)S(1)}, f32[256,128]{1,0:T(8,128)S(1)}, u32[]{:S(2)}, u32[]{:S(2)}) collective-permute-start(f32[256,128]{1,0:T(8,128)S(1)} %get-tuple-element.19), channel_id=1, source_target_pairs={{0,8},{8,0},{16,24},{24,16},{1,9},{9,1},{17,25},{25,17},{2,10},{10... | collective-permute-start | bytes 393224 | tf_op jit(solution)/shard_map/ppermute | solution.py:202
  21.9 1.3 %collective-permute-start.4 = (f32[160,128]{1,0:T(8,128)S(1)}, f32[160,128]{1,0:T(8,128)S(1)}, u32[]{:S(2)}, u32[]{:S(2)}) collective-permute-start(f32[160,128]{1,0:T(8,128)S(1)} %get-tuple-element.17), channel_id=1, source_target_pairs={{0,1},{1,0},{2,3},{3,2},{4,5},{5,4},{6,7},{7,6},{8,9},{9,8},{10,11... | collective-permute-start | bytes 245768 | tf_op jit(solution)/shard_map/ppermute | solution.py:202
  23.3 4.2 %collective-permute-start.10 = (f32[160,256]{1,0:T(8,128)S(1)}, f32[160,256]{1,0:T(8,128)S(1)}, u32[]{:S(2)}, u32[]{:S(2)}) collective-permute-start(f32[160,256]{1,0:T(8,128)S(1)} %get-tuple-element.22), channel_id=1, source_target_pairs={{0,1},{1,0},{2,3},{3,2},{4,5},{5,4},{6,7},{7,6},{8,9},{9,8},{10,11... | collective-permute-start | bytes 491528 | tf_op jit(solution)/shard_map/ppermute | solution.py:202
  23.5 7.6 %collective-permute-start.8 = (f32[160,128]{1,0:T(8,128)S(1)}, f32[160,128]{1,0:T(8,128)S(1)}, u32[]{:S(2)}, u32[]{:S(2)}) collective-permute-start(f32[160,128]{1,0:T(8,128)S(1)} %add.39), channel_id=1, source_target_pairs={{0,2},{2,0},{4,6},{6,4},{1,3},{3,1},{5,7},{7,5},{8,10},{10,8},{12,... | collective-permute-start | bytes 245768 | tf_op jit(solution)/shard_map/ppermute | solution.py:202
  27.6 9.9 %collective-permute-start.13 = (f32[160,256]{1,0:T(8,128)S(1)}, f32[160,256]{1,0:T(8,128)S(1)}, u32[]{:S(2)}, u32[]{:S(2)}) collective-permute-start(f32[160,256]{1,0:T(8,128)S(1)} %add.45), channel_id=1, source_target_pairs={{0,24},{8,16},{16,8},{24,0},{1,25},{9,17},{17,9},{25,1},{2,26},{10... | collective-permute-start | bytes 491528 | tf_op jit(solution)/shard_map/ppermute | solution.py:202
  30.1 8.2 %collective-permute-start.12 = (f32[160,256]{1,0:T(8,128)S(1)}, f32[160,256]{1,0:T(8,128)S(1)}, u32[]{:S(2)}, u32[]{:S(2)}) collective-permute-start(f32[160,256]{1,0:T(8,128)S(1)} %add.45), channel_id=1, source_target_pairs={{0,16},{8,24},{16,0},{24,8},{1,17},{9,25},{17,1},{25,9},{2,18},{10... | collective-permute-start | bytes 491528 | tf_op jit(solution)/shard_map/ppermute | solution.py:202
  30.6 7.7 %collective-permute-start.11 = (f32[160,256]{1,0:T(8,128)S(1)}, f32[160,256]{1,0:T(8,128)S(1)}, u32[]{:S(2)}, u32[]{:S(2)}) collective-permute-start(f32[160,256]{1,0:T(8,128)S(1)} %add.45), channel_id=1, source_target_pairs={{0,8},{8,0},{16,24},{24,16},{1,9},{9,1},{17,25},{25,17},{2,10},{10... | collective-permute-start | bytes 491528 | tf_op jit(solution)/shard_map/ppermute | solution.py:202
  31.1 6.3 %collective-permute-start.9 = (f32[160,128]{1,0:T(8,128)S(1)}, f32[160,128]{1,0:T(8,128)S(1)}, u32[]{:S(2)}, u32[]{:S(2)}) collective-permute-start(f32[160,128]{1,0:T(8,128)S(1)} %add.43), channel_id=1, source_target_pairs={{0,4},{2,6},{4,0},{6,2},{1,5},{3,7},{5,1},{7,3},{8,12},{10,14},{12... | collective-permute-start | bytes 245768 | tf_op jit(solution)/shard_map/ppermute | solution.py:202
  38.3 6.1 %collective-permute-start.17 = (f32[160,128]{1,0:T(8,128)S(1)}, f32[160,128]{1,0:T(8,128)S(1)}, u32[]{:S(2)}, u32[]{:S(2)}) collective-permute-start(f32[160,128]{1,0:T(8,128)S(1)} %add.44), channel_id=1, source_target_pairs={{0,24},{8,16},{16,8},{24,0},{1,25},{9,17},{17,9},{25,1},{2,26},{10... | collective-permute-start | bytes 245768 | tf_op jit(solution)/shard_map/ppermute | solution.py:202
  40.1 5.3 %collective-permute-start.16 = (f32[160,128]{1,0:T(8,128)S(1)}, f32[160,128]{1,0:T(8,128)S(1)}, u32[]{:S(2)}, u32[]{:S(2)}) collective-permute-start(f32[160,128]{1,0:T(8,128)S(1)} %add.44), channel_id=1, source_target_pairs={{0,16},{8,24},{16,0},{24,8},{1,17},{9,25},{17,1},{25,9},{2,18},{10... | collective-permute-start | bytes 245768 | tf_op jit(solution)/shard_map/ppermute | solution.py:202
  41.4 4.4 %collective-permute-start.15 = (f32[160,128]{1,0:T(8,128)S(1)}, f32[160,128]{1,0:T(8,128)S(1)}, u32[]{:S(2)}, u32[]{:S(2)}) collective-permute-start(f32[160,128]{1,0:T(8,128)S(1)} %add.44), channel_id=1, source_target_pairs={{0,8},{8,0},{16,24},{24,16},{1,9},{9,1},{17,25},{25,17},{2,10},{10... | collective-permute-start | bytes 245768 | tf_op jit(solution)/shard_map/ppermute | solution.py:202
  41.9 4.0 %collective-permute-start.19 = (f32[256,128]{1,0:T(8,128)S(1)}, f32[256,128]{1,0:T(8,128)S(1)}, u32[]{:S(2)}, u32[]{:S(2)}) collective-permute-start(f32[256,128]{1,0:T(8,128)S(1)} %add_add_fusion.1.mine_term_ref), channel_id=1, source_target_pairs={{0,1},{1,0},{2,3},{3,2},{4,5},{5,4},{6,7},{7,6},{8,9},{9,8},{10,11... | collective-permute-start | bytes 393224 | tf_op jit(solution)/shard_map/ppermute | solution.py:202
  41.9 5.3 %collective-permute-start.14 = (f32[160,256]{1,0:T(8,128)S(1)}, f32[160,256]{1,0:T(8,128)S(1)}, u32[]{:S(2)}, u32[]{:S(2)}) collective-permute-start(f32[160,256]{1,0:T(8,128)S(1)} %add_add_fusion.mine_d_ref), channel_id=1, source_target_pairs={{0,1},{1,0},{2,3},{3,2},{4,5},{5,4},{6,7},{7,6},{8,9},{9,8},{10,11... | collective-permute-start | bytes 491528 | tf_op jit(solution)/shard_map/ppermute | solution.py:202
  45.8 1.3 %collective-permute-start.18 = (f32[160,128]{1,0:T(8,128)S(1)}, f32[160,128]{1,0:T(8,128)S(1)}, u32[]{:S(2)}, u32[]{:S(2)}) collective-permute-start(f32[160,128]{1,0:T(8,128)S(1)} %add_add_fusion.2.mine_t_ref), channel_id=1, source_target_pairs={{0,1},{1,0},{2,3},{3,2},{4,5},{5,4},{6,7},{7,6},{8,9},{9,8},{10,11... | collective-permute-start | bytes 245768 | tf_op jit(solution)/shard_map/ppermute | solution.py:202

commit v13 on v12

--- a/solution.py
+++ b/solution.py
@@ -95,10 +95,11 @@
 
 
 def compute_kernel(
-    col_count, supernodes, slot, widths_ref, weights_ref, place_ref, straight_ref, own_wide_ref,
-    *refs
+    shifts, col_count, supernodes, slot, widths_ref, weights_ref, place_ref, straight_ref,
+    own_wide_ref, *refs
 ):
     block_refs, refs = refs[:-7], refs[-7:]
+    block_refs = [block_refs[shifts.index(shift)] for shift in range(len(shifts))]
     keep_d_ref, send_d_ref, keep_t_ref, send_t_ref, x_ref, y_ref, t_ref = refs
     packed_width = block_refs[0].shape[0] // 2
     local_rows = straight_ref.shape[1]
@@ -255,7 +256,8 @@
     )(block_pattern, sup_widths, l_panel[0])
 
     blocks = {0: packed}
-    for shift in sorted(range(1, row_count), key=lambda s: -min(s, row_count - s)):
+    shifts = sorted(range(row_count), key=lambda shift: min(shift, row_count - shift))
+    for shift in shifts[1:]:
         pairs = [((i + shift) % row_count, i) for i in range(row_count)]
         blocks[shift] = lax.ppermute(packed, "row", pairs)
     own = [packed] + [swap(packed, "col", other) for other in range(1, col_count)]
@@ -283,7 +285,7 @@
     term = sum_direct(term, "pole")
 
     keep_d, send_d, keep_t, send_t = pl.pallas_call(
-        functools.partial(compute_kernel, col_count, supernodes, slot),
+        functools.partial(compute_kernel, shifts, col_count, supernodes, slot),
         in_specs=[SMEM_SPEC] * 3 + [VMEM_SPEC] * (2 + row_count),
         out_specs=[VMEM_SPEC] * 4,
         out_shape=[jax.ShapeDtypeStruct((half, local_rows), F32)] * 2
@@ -297,7 +299,7 @@
         name="compute",
     )(
         sup_widths, pole_weights, place, straight, own_wide,
-        *[blocks[shift] for shift in range(row_count)],
+        *[blocks[shift] for shift in shifts],
     )
 
     tie = lax.optimization_barrier
@@ -308,7 +310,6 @@
         products = products + swap(products, "row", bit)
     density = scatter_rest(keep_d + swap(send_d, "col", top), "col")
     density = sum_direct(density, "pole")
-    products, density = tie((products, density))
     products = sum_direct(products, "pole")
     density = gather_but_last(density, "col")
     products = gather_but_last(products, "col")

time: 48.8 us -> 47.8 us (0.980)
  waiting for transfers between devices: 14.1 us -> 11.6 us
  starting transfers between devices: 24.2 us -> 25.6 us
    ppermute x17, waiting for transfers between devices: 11.4 us -> 10.1 us  [swap(): lax.ppermute(value, axis, [(i, i ^ bit) for i in range(lax.axis_size(axis...]
    ppermute x3, waiting for transfers between devices: 2.72 us -> 1.48 us  [per_device(): blocks[shift] = lax.ppermute(packed, 'row', pairs)]
    ppermute x3, starting transfers between devices: 6.51 us -> 7.41 us  [per_device(): blocks[shift] = lax.ppermute(packed, 'row', pairs)]
    ppermute x17, starting transfers between devices: 17.7 us -> 18.2 us  [swap(): lax.ppermute(value, axis, [(i, i ^ bit) for i in range(lax.axis_size(axis...]
  transfers between devices with their start and end apart: 20 -> 20, of which waited for: 9 -> 7; matrix products, arithmetic and copies ran while one was open for 0% -> 0% of each run, Pallas kernels for 7% -> 7%
where the time goes in v13:
time: 47.8 us; the launch traced here: 47.6 us
  starting transfers between devices  25.6 us (54%)
  waiting for transfers between devices  11.6 us (24%)
  Pallas kernels  6.72 us (14%)
  local copies, waits for them, and re-layouts  2.63 us (6%)
  between operations  0.76 us (2%)
    ppermute x17, starting transfers between devices, swap(): lax.ppermute(value, axis, [(i, i ^ bit) for i in range(lax.axis_size(axis...  18.2 us
    ppermute x17, waiting for transfers between devices, swap(): lax.ppermute(value, axis, [(i, i ^ bit) for i in range(lax.axis_size(axis...  10.1 us
    ppermute x3, starting transfers between devices, per_device(): blocks[shift] = lax.ppermute(packed, 'row', pairs)  7.41 us
    unnamed x12, local copies, waits for them, and re-layouts  2.63 us
    pallas_call x1, Pallas kernels, per_device(): pl.pallas_call(functools.partial(pack_kernel, supernodes, slot), in_specs...  2 us
    pallas_call x1, Pallas kernels, per_device(): pl.pallas_call(functools.partial(compute_kernel, shifts, col_count, super...  1.99 us
    ppermute x3, waiting for transfers between devices, per_device(): blocks[shift] = lax.ppermute(packed, 'row', pairs)  1.48 us
    pallas_call x1, Pallas kernels, per_device(): pl.pallas_call(functools.partial(expand_kernel, col_count, slot), in_spec...  1.44 us
  transfers between devices with their start and end apart: 20, of which 7 were waited for; matrix products, arithmetic and copies ran while one was open for 0% of the time, Pallas kernels for 7%

profile of v13, /device:TPU:0, one launch (start us, length us, event | category | flops | bytes accessed | tf_op | source)
XLA Modules:
  0.0 47.6 jit_solution(18362834312347795173)
XLA Ops:
  0.6 0.0 copy-start.3
  0.6 2.0 %pack.1.refs_0_ = bf16[640,128]{1,0:T(8,128)(2,1)} custom-call(s32[1,4]{1,0:T(1,128)} %pattern_ref.1, s32[4]{0:T(128)} %widths_ref.7, bf16[2,128,512]{2,1,0:T(8,128)(2,1)} %bitcast.7), custom_call_target="tpu_custom_call" | custom-call | tf_op jit(solution)/shard_map/pack/pallas_call | solution.py:250
  2.6 0.5 collective-permute-start
  3.1 3.6 %collective-permute-start.3 = (bf16[640,128]{1,0:T(8,128)(2,1)}, bf16[640,128]{1,0:T(8,128)(2,1)S(1)}, u32[]{:S(2)}, u32[]{:S(2)}) collective-permute-start(bf16[640,128]{1,0:T(8,128)(2,1)} %pack.1.refs_0_), channel_id=1, source_target_pairs={{4,0},{6,2},{0,4},{2,6},{5,1},{7,3},{1,5},{3,7},{12,8},{14,10},{8,... | collective-permute-start | bytes 491528 | tf_op jit(solution)/shard_map/ppermute | solution.py:262
  6.7 1.6 %collective-permute-start.2 = (bf16[640,128]{1,0:T(8,128)(2,1)}, bf16[640,128]{1,0:T(8,128)(2,1)S(1)}, u32[]{:S(2)}, u32[]{:S(2)}) collective-permute-start(bf16[640,128]{1,0:T(8,128)(2,1)} %pack.1.refs_0_), channel_id=1, source_target_pairs={{6,0},{0,2},{2,4},{4,6},{7,1},{1,3},{3,5},{5,7},{14,8},{8,10},{10,... | collective-permute-start | bytes 491528 | tf_op jit(solution)/shard_map/ppermute | solution.py:262
  8.3 2.2 %collective-permute-start.1 = (bf16[640,128]{1,0:T(8,128)(2,1)}, bf16[640,128]{1,0:T(8,128)(2,1)S(1)}, u32[]{:S(2)}, u32[]{:S(2)}) collective-permute-start(bf16[640,128]{1,0:T(8,128)(2,1)} %pack.1.refs_0_), channel_id=1, source_target_pairs={{2,0},{4,2},{6,4},{0,6},{3,1},{5,3},{7,5},{1,7},{10,8},{12,10},{14... | collective-permute-start | bytes 491528 | tf_op jit(solution)/shard_map/ppermute | solution.py:262
  10.5 0.1 pad_add_fusion.place_ref
  10.6 0.0 collective-permute-done.refs_1_
  10.6 0.0 copy-start.4
  10.6 0.0 copy-start.5
  10.6 0.0 copy-done.3
  10.6 0.6 %copy-done.4 = s32[4]{0:T(128)S(1)} copy-done((s32[4]{0:T(128)S(1)}, s32[4]{0:T(128)}, u32[]{:S(2)}) %copy-start.4) | copy-done | bytes 40
  11.2 0.0 copy-done.5
  11.3 0.0 copy-start
  11.3 0.9 %copy-done = bf16[640,128]{1,0:T(8,128)(2,1)S(1)} copy-done((bf16[640,128]{1,0:T(8,128)(2,1)S(1)}, bf16[640,128]{1,0:T(8,128)(2,1)}, u32[]{:S(2)}) %copy-start) | copy-done | bytes 163864
  12.2 0.0 copy-start.2
  12.2 1.0 %copy-done.2 = bf16[1,2,256,4,1,128]{5,3,4,2,1,0:T(4,128)(2,1)S(1)} copy-done((bf16[1,2,256,4,1,128]{5,3,4,2,1,0:T(4,128)(2,1)S(1)}, bf16[1,2,256,4,1,128]{5,3,4,2,1,0:T(4,128)(2,1)}, u32[]{:S(2)}) %copy-start.2) | copy-done | bytes 524312
  13.2 0.0 copy-start.1
  13.2 1.3 %prepare.1 = (bf16[2,256,512]{2,1,0:T(8,128)(2,1)S(1)}, bf16[512,512]{1,0:T(8,128)(2,1)S(1)}, f32[256,128]{1,0:T(8,128)S(1)}) custom-call(s32[4]{0:T(128)S(1)} %copy-done.4, f32[1,2]{1,0:T(1,128)S(1)} %copy-done.5, s32[2]{0:T(128)S(1)} %pad_add_fusion.place_ref, bf16[2048,128]{1,0:T(8,128)(2,1)S(1)} %bitcast.5, bf16[2,512,128]{2,1,0:T(8,128)(2,1)S(1)} %bitcast.6, ...), custom_call_target="tpu_custom_call" | custom-call | flops 134217728 | bytes 1048576 | tf_op jit(solution)/shard_map/prepare/pallas_call | solution.py:265
  14.5 2.5 %collective-permute-start.7 = (f32[256,128]{1,0:T(8,128)S(1)}, f32[256,128]{1,0:T(8,128)S(1)}, u32[]{:S(2)}, u32[]{:S(2)}) collective-permute-start(f32[256,128]{1,0:T(8,128)S(1)} %get-tuple-element.18), channel_id=1, source_target_pairs={{0,24},{8,16},{16,8},{24,0},{1,25},{9,17},{17,9},{25,1},{2,26},{10... | collective-permute-start | bytes 393224 | tf_op jit(solution)/shard_map/ppermute | solution.py:203
  17.0 0.5 %collective-permute-start.6 = (f32[256,128]{1,0:T(8,128)S(1)}, f32[256,128]{1,0:T(8,128)S(1)}, u32[]{:S(2)}, u32[]{:S(2)}) collective-permute-start(f32[256,128]{1,0:T(8,128)S(1)} %get-tuple-element.18), channel_id=1, source_target_pairs={{0,16},{8,24},{16,0},{24,8},{1,17},{9,25},{17,1},{25,9},{2,18},{10... | collective-permute-start | bytes 393224 | tf_op jit(solution)/shard_map/ppermute | solution.py:203
  17.5 1.5 %collective-permute-done.3.refs_3_ = bf16[640,128]{1,0:T(8,128)(2,1)S(1)} collective-permute-done((bf16[640,128]{1,0:T(8,128)(2,1)}, bf16[640,128]{1,0:T(8,128)(2,1)S(1)}, u32[]{:S(2)}, u32[]{:S(2)}) %collective-permute-start.3) | collective-permute-done | bytes 163872 | tf_op jit(solution)/shard_map/ppermute | solution.py:262
  19.0 1.8 %collective-permute-start.5 = (f32[256,128]{1,0:T(8,128)S(1)}, f32[256,128]{1,0:T(8,128)S(1)}, u32[]{:S(2)}, u32[]{:S(2)}) collective-permute-start(f32[256,128]{1,0:T(8,128)S(1)} %get-tuple-element.18), channel_id=1, source_target_pairs={{0,8},{8,0},{16,24},{24,16},{1,9},{9,1},{17,25},{25,17},{2,10},{10... | collective-permute-start | bytes 393224 | tf_op jit(solution)/shard_map/ppermute | solution.py:203
  20.8 0.0 collective-permute-done.2.refs_2_
  20.8 0.0 collective-permute-done.1.refs_1_
  20.8 0.0 copy-done.1
  20.8 2.0 %compute.1 = (f32[160,256]{1,0:T(8,128)S(1)}, f32[160,256]{1,0:T(8,128)S(1)}, f32[160,128]{1,0:T(8,128)S(1)}, f32[160,128]{1,0:T(8,128)S(1)}) custom-call(s32[4]{0:T(128)S(1)} %copy-done.4, f32[1,2]{1,0:T(1,128)S(1)} %copy-done.5, s32[2]{0:T(128)S(1)} %pad_add_fusion.place_ref, bf16[2,256,512]{2,1,0:T(8,128)(2,1)S(1)} %get-tuple-element.12.straight_ref, ...), custom_call_target="tpu_custom_call" | custom-call | tf_op jit(solution)/shard_map/compute/pallas_call | solution.py:287
  22.8 0.1 collective-permute-start.4
  22.8 1.3 %collective-permute-done.4 = f32[160,128]{1,0:T(8,128)S(1)} collective-permute-done((f32[160,128]{1,0:T(8,128)S(1)}, f32[160,128]{1,0:T(8,128)S(1)}, u32[]{:S(2)}, u32[]{:S(2)}) %collective-permute-start.4) | collective-permute-done | bytes 81952 | tf_op jit(solution)/shard_map/ppermute | solution.py:203
  24.1 0.0 collective-permute-done.7
  24.1 0.0 collective-permute-done.6
  24.1 0.0 collective-permute-done.5
  24.2 0.2 collective-permute-start.8
  24.4 2.4 %collective-permute-start.13 = (f32[160,128]{1,0:T(8,128)S(1)}, f32[160,128]{1,0:T(8,128)S(1)}, u32[]{:S(2)}, u32[]{:S(2)}) collective-permute-start(f32[160,128]{1,0:T(8,128)S(1)} %add.39), channel_id=1, source_target_pairs={{0,2},{2,0},{4,6},{6,4},{1,3},{3,1},{5,7},{7,5},{8,10},{10,8},{12,... | collective-permute-start | bytes 245768 | tf_op jit(solution)/shard_map/ppermute | solution.py:203
  26.8 0.0 collective-permute-done.8
  26.8 2.5 %collective-permute-start.11 = (f32[160,256]{1,0:T(8,128)S(1)}, f32[160,256]{1,0:T(8,128)S(1)}, u32[]{:S(2)}, u32[]{:S(2)}) collective-permute-start(f32[160,256]{1,0:T(8,128)S(1)} %add.43), channel_id=1, source_target_pairs={{0,24},{8,16},{16,8},{24,0},{1,25},{9,17},{17,9},{25,1},{2,26},{10... | collective-permute-start | bytes 491528 | tf_op jit(solution)/shard_map/ppermute | solution.py:203
  29.3 0.5 %collective-permute-start.10 = (f32[160,256]{1,0:T(8,128)S(1)}, f32[160,256]{1,0:T(8,128)S(1)}, u32[]{:S(2)}, u32[]{:S(2)}) collective-permute-start(f32[160,256]{1,0:T(8,128)S(1)} %add.43), channel_id=1, source_target_pairs={{0,16},{8,24},{16,0},{24,8},{1,17},{9,25},{17,1},{25,9},{2,18},{10... | collective-permute-start | bytes 491528 | tf_op jit(solution)/shard_map/ppermute | solution.py:203
  29.8 0.5 %collective-permute-start.9 = (f32[160,256]{1,0:T(8,128)S(1)}, f32[160,256]{1,0:T(8,128)S(1)}, u32[]{:S(2)}, u32[]{:S(2)}) collective-permute-start(f32[160,256]{1,0:T(8,128)S(1)} %add.43), channel_id=1, source_target_pairs={{0,8},{8,0},{16,24},{24,16},{1,9},{9,1},{17,25},{25,17},{2,10},{10... | collective-permute-start | bytes 491528 | tf_op jit(solution)/shard_map/ppermute | solution.py:203
  30.4 0.0 collective-permute-done.13
  30.4 3.1 %collective-permute-start.14 = (f32[160,128]{1,0:T(8,128)S(1)}, f32[160,128]{1,0:T(8,128)S(1)}, u32[]{:S(2)}, u32[]{:S(2)}) collective-permute-start(f32[160,128]{1,0:T(8,128)S(1)} %add.47), channel_id=1, source_target_pairs={{0,4},{2,6},{4,0},{6,2},{1,5},{3,7},{5,1},{7,3},{8,12},{10,14},{12... | collective-permute-start | bytes 245768 | tf_op jit(solution)/shard_map/ppermute | solution.py:203
  33.5 0.0 collective-permute-start.19
  33.5 3.8 %collective-permute-done.14 = f32[160,128]{1,0:T(8,128)S(1)} collective-permute-done((f32[160,128]{1,0:T(8,128)S(1)}, f32[160,128]{1,0:T(8,128)S(1)}, u32[]{:S(2)}, u32[]{:S(2)}) %collective-permute-start.14) | collective-permute-done | bytes 81952 | tf_op jit(solution)/shard_map/ppermute | solution.py:203
  37.3 2.5 %collective-permute-start.17 = (f32[160,128]{1,0:T(8,128)S(1)}, f32[160,128]{1,0:T(8,128)S(1)}, u32[]{:S(2)}, u32[]{:S(2)}) collective-permute-start(f32[160,128]{1,0:T(8,128)S(1)} %add.48), channel_id=1, source_target_pairs={{0,24},{8,16},{16,8},{24,0},{1,25},{9,17},{17,9},{25,1},{2,26},{10... | collective-permute-start | bytes 245768 | tf_op jit(solution)/shard_map/ppermute | solution.py:203
  39.8 0.0 collective-permute-done.11
  39.8 0.5 %collective-permute-start.16 = (f32[160,128]{1,0:T(8,128)S(1)}, f32[160,128]{1,0:T(8,128)S(1)}, u32[]{:S(2)}, u32[]{:S(2)}) collective-permute-start(f32[160,128]{1,0:T(8,128)S(1)} %add.48), channel_id=1, source_target_pairs={{0,16},{8,24},{16,0},{24,8},{1,17},{9,25},{17,1},{25,9},{2,18},{10... | collective-permute-start | bytes 245768 | tf_op jit(solution)/shard_map/ppermute | solution.py:203
  40.3 0.0 collective-permute-done.10
  40.3 0.5 %collective-permute-start.15 = (f32[160,128]{1,0:T(8,128)S(1)}, f32[160,128]{1,0:T(8,128)S(1)}, u32[]{:S(2)}, u32[]{:S(2)}) collective-permute-start(f32[160,128]{1,0:T(8,128)S(1)} %add.48), channel_id=1, source_target_pairs={{0,8},{8,0},{16,24},{24,16},{1,9},{9,1},{17,25},{25,17},{2,10},{10... | collective-permute-start | bytes 245768 | tf_op jit(solution)/shard_map/ppermute | solution.py:203
  40.9 0.0 collective-permute-done.9
  40.9 0.1 collective-permute-start.12
  41.0 1.8 %collective-permute-done.17 = f32[160,128]{1,0:T(8,128)S(1)} collective-permute-done((f32[160,128]{1,0:T(8,128)S(1)}, f32[160,128]{1,0:T(8,128)S(1)}, u32[]{:S(2)}, u32[]{:S(2)}) %collective-permute-start.17) | collective-permute-done | bytes 81952 | tf_op jit(solution)/shard_map/ppermute | solution.py:203
  42.8 1.6 %collective-permute-done.16 = f32[160,128]{1,0:T(8,128)S(1)} collective-permute-done((f32[160,128]{1,0:T(8,128)S(1)}, f32[160,128]{1,0:T(8,128)S(1)}, u32[]{:S(2)}, u32[]{:S(2)}) %collective-permute-start.16) | collective-permute-done | bytes 81952 | tf_op jit(solution)/shard_map/ppermute | solution.py:203
  44.5 0.3 collective-permute-done.15
  44.8 0.1 collective-permute-start.18
  44.9 0.0 collective-permute-done.19.other_term_ref
  44.9 1.3 %collective-permute-done.18.other_t_ref = f32[160,128]{1,0:T(8,128)S(1)} collective-permute-done((f32[160,128]{1,0:T(8,128)S(1)}, f32[160,128]{1,0:T(8,128)S(1)}, u32[]{:S(2)}, u32[]{:S(2)}) %collective-permute-start.18) | collective-permute-done | bytes 81952 | tf_op jit(solution)/shard_map/ppermute | solution.py:203
  46.1 0.0 collective-permute-done.12.other_d_ref
  46.1 1.4 %expand.1 = (f32[256,256]{1,0:T(8,128)}, f32[512,128]{1,0:T(8,128)}) custom-call(s32[4]{0:T(128)S(1)} %copy-done.4, s32[2]{0:T(128)S(1)} %pad_add_fusion.place_ref, f32[160,256]{1,0:T(8,128)S(1)} %add_add_fusion.mine_d_ref, f32[160,256]{1,0:T(8,128)S(1)} %collective-permute-done.12.other_d_ref, f32[160,128]{1,0:T(8,128)S(1)} %add_add_fusion.2.mine_t_ref, ...), custom_call_target="tpu_custom_call" | custom-call | tf_op jit(solution)/shard_map/expand/pallas_call | solution.py:317
  (7 shorter events, 0.1 us)
Async XLA Ops:
  0.6 10.0 %copy-start.3 = (bf16[1,2,512,128]{3,2,1,0:T(8,128)(2,1)S(1)}, bf16[1,2,512,128]{3,2,1,0:T(8,128)(2,1)}, u32[]{:S(2)}) copy-start(bf16[1,2,512,128]{3,2,1,0:T(8,128)(2,1)} %param.10) | copy-start | bytes 786436
  2.6 7.9 %collective-permute-start = (bf16[640,128]{1,0:T(8,128)(2,1)}, bf16[640,128]{1,0:T(8,128)(2,1)S(1)}, u32[]{:S(2)}, u32[]{:S(2)}) collective-permute-start(bf16[640,128]{1,0:T(8,128)(2,1)} %pack.1.refs_0_), channel_id=1, source_target_pairs={{0,1},{1,0},{2,3},{3,2},{4,5},{5,4},{6,7},{7,6},{8,9},{9,8},{10,11... | collective-permute-start | bytes 491528 | tf_op jit(solution)/shard_map/ppermute | solution.py:203
  3.1 15.9 %collective-permute-start.3 = (bf16[640,128]{1,0:T(8,128)(2,1)}, bf16[640,128]{1,0:T(8,128)(2,1)S(1)}, u32[]{:S(2)}, u32[]{:S(2)}) collective-permute-start(bf16[640,128]{1,0:T(8,128)(2,1)} %pack.1.refs_0_), channel_id=1, source_target_pairs={{4,0},{6,2},{0,4},{2,6},{5,1},{7,3},{1,5},{3,7},{12,8},{14,10},{8,... | collective-permute-start | bytes 491528 | tf_op jit(solution)/shard_map/ppermute | solution.py:262
  6.7 14.1 %collective-permute-start.2 = (bf16[640,128]{1,0:T(8,128)(2,1)}, bf16[640,128]{1,0:T(8,128)(2,1)S(1)}, u32[]{:S(2)}, u32[]{:S(2)}) collective-permute-start(bf16[640,128]{1,0:T(8,128)(2,1)} %pack.1.refs_0_), channel_id=1, source_target_pairs={{6,0},{0,2},{2,4},{4,6},{7,1},{1,3},{3,5},{5,7},{14,8},{8,10},{10,... | collective-permute-start | bytes 491528 | tf_op jit(solution)/shard_map/ppermute | solution.py:262
  8.3 12.5 %collective-permute-start.1 = (bf16[640,128]{1,0:T(8,128)(2,1)}, bf16[640,128]{1,0:T(8,128)(2,1)S(1)}, u32[]{:S(2)}, u32[]{:S(2)}) collective-permute-start(bf16[640,128]{1,0:T(8,128)(2,1)} %pack.1.refs_0_), channel_id=1, source_target_pairs={{2,0},{4,2},{6,4},{0,6},{3,1},{5,3},{7,5},{1,7},{10,8},{12,10},{14... | collective-permute-start | bytes 491528 | tf_op jit(solution)/shard_map/ppermute | solution.py:262
  10.6 0.7 %copy-start.4 = (s32[4]{0:T(128)S(1)}, s32[4]{0:T(128)}, u32[]{:S(2)}) copy-start(s32[4]{0:T(128)} %widths_ref.7) | copy-start | bytes 52
  10.6 0.7 %copy-start.5 = (f32[1,2]{1,0:T(1,128)S(1)}, f32[1,2]{1,0:T(1,128)}, u32[]{:S(2)}) copy-start(f32[1,2]{1,0:T(1,128)} %weights_ref.3) | copy-start | bytes 28
  11.3 0.9 %copy-start = (bf16[640,128]{1,0:T(8,128)(2,1)S(1)}, bf16[640,128]{1,0:T(8,128)(2,1)}, u32[]{:S(2)}) copy-start(bf16[640,128]{1,0:T(8,128)(2,1)} %pack.1.refs_0_) | copy-start | bytes 491524
  12.2 1.0 %copy-start.2 = (bf16[1,2,256,4,1,128]{5,3,4,2,1,0:T(4,128)(2,1)S(1)}, bf16[1,2,256,4,1,128]{5,3,4,2,1,0:T(4,128)(2,1)}, u32[]{:S(2)}) copy-start(bf16[1,2,256,4,1,128]{5,3,4,2,1,0:T(4,128)(2,1)} %param.6) | copy-start | bytes 1572868
  13.2 7.6 %copy-start.1 = (bf16[640,128]{1,0:T(8,128)(2,1)S(1)}, bf16[640,128]{1,0:T(8,128)(2,1)}, u32[]{:S(2)}) copy-start(bf16[640,128]{1,0:T(8,128)(2,1)} %pack.1.refs_0_) | copy-start | bytes 491524
  14.5 9.6 %collective-permute-start.7 = (f32[256,128]{1,0:T(8,128)S(1)}, f32[256,128]{1,0:T(8,128)S(1)}, u32[]{:S(2)}, u32[]{:S(2)}) collective-permute-start(f32[256,128]{1,0:T(8,128)S(1)} %get-tuple-element.18), channel_id=1, source_target_pairs={{0,24},{8,16},{16,8},{24,0},{1,25},{9,17},{17,9},{25,1},{2,26},{10... | collective-permute-start | bytes 393224 | tf_op jit(solution)/shard_map/ppermute | solution.py:203
  17.0 7.1 %collective-permute-start.6 = (f32[256,128]{1,0:T(8,128)S(1)}, f32[256,128]{1,0:T(8,128)S(1)}, u32[]{:S(2)}, u32[]{:S(2)}) collective-permute-start(f32[256,128]{1,0:T(8,128)S(1)} %get-tuple-element.18), channel_id=1, source_target_pairs={{0,16},{8,24},{16,0},{24,8},{1,17},{9,25},{17,1},{25,9},{2,18},{10... | collective-permute-start | bytes 393224 | tf_op jit(solution)/shard_map/ppermute | solution.py:203
  19.0 5.1 %collective-permute-start.5 = (f32[256,128]{1,0:T(8,128)S(1)}, f32[256,128]{1,0:T(8,128)S(1)}, u32[]{:S(2)}, u32[]{:S(2)}) collective-permute-start(f32[256,128]{1,0:T(8,128)S(1)} %get-tuple-element.18), channel_id=1, source_target_pairs={{0,8},{8,0},{16,24},{24,16},{1,9},{9,1},{17,25},{25,17},{2,10},{10... | collective-permute-start | bytes 393224 | tf_op jit(solution)/shard_map/ppermute | solution.py:203
  22.8 1.3 %collective-permute-start.4 = (f32[160,128]{1,0:T(8,128)S(1)}, f32[160,128]{1,0:T(8,128)S(1)}, u32[]{:S(2)}, u32[]{:S(2)}) collective-permute-start(f32[160,128]{1,0:T(8,128)S(1)} %get-tuple-element.16), channel_id=1, source_target_pairs={{0,1},{1,0},{2,3},{3,2},{4,5},{5,4},{6,7},{7,6},{8,9},{9,8},{10,11... | collective-permute-start | bytes 245768 | tf_op jit(solution)/shard_map/ppermute | solution.py:203
  24.2 2.6 %collective-permute-start.8 = (f32[160,256]{1,0:T(8,128)S(1)}, f32[160,256]{1,0:T(8,128)S(1)}, u32[]{:S(2)}, u32[]{:S(2)}) collective-permute-start(f32[160,256]{1,0:T(8,128)S(1)} %get-tuple-element.19), channel_id=1, source_target_pairs={{0,1},{1,0},{2,3},{3,2},{4,5},{5,4},{6,7},{7,6},{8,9},{9,8},{10,11... | collective-permute-start | bytes 491528 | tf_op jit(solution)/shard_map/ppermute | solution.py:203
  24.4 5.9 %collective-permute-start.13 = (f32[160,128]{1,0:T(8,128)S(1)}, f32[160,128]{1,0:T(8,128)S(1)}, u32[]{:S(2)}, u32[]{:S(2)}) collective-permute-start(f32[160,128]{1,0:T(8,128)S(1)} %add.39), channel_id=1, source_target_pairs={{0,2},{2,0},{4,6},{6,4},{1,3},{3,1},{5,7},{7,5},{8,10},{10,8},{12,... | collective-permute-start | bytes 245768 | tf_op jit(solution)/shard_map/ppermute | solution.py:203
  26.8 13.0 %collective-permute-start.11 = (f32[160,256]{1,0:T(8,128)S(1)}, f32[160,256]{1,0:T(8,128)S(1)}, u32[]{:S(2)}, u32[]{:S(2)}) collective-permute-start(f32[160,256]{1,0:T(8,128)S(1)} %add.43), channel_id=1, source_target_pairs={{0,24},{8,16},{16,8},{24,0},{1,25},{9,17},{17,9},{25,1},{2,26},{10... | collective-permute-start | bytes 491528 | tf_op jit(solution)/shard_map/ppermute | solution.py:203
  29.3 11.0 %collective-permute-start.10 = (f32[160,256]{1,0:T(8,128)S(1)}, f32[160,256]{1,0:T(8,128)S(1)}, u32[]{:S(2)}, u32[]{:S(2)}) collective-permute-start(f32[160,256]{1,0:T(8,128)S(1)} %add.43), channel_id=1, source_target_pairs={{0,16},{8,24},{16,0},{24,8},{1,17},{9,25},{17,1},{25,9},{2,18},{10... | collective-permute-start | bytes 491528 | tf_op jit(solution)/shard_map/ppermute | solution.py:203
  29.8 11.0 %collective-permute-start.9 = (f32[160,256]{1,0:T(8,128)S(1)}, f32[160,256]{1,0:T(8,128)S(1)}, u32[]{:S(2)}, u32[]{:S(2)}) collective-permute-start(f32[160,256]{1,0:T(8,128)S(1)} %add.43), channel_id=1, source_target_pairs={{0,8},{8,0},{16,24},{24,16},{1,9},{9,1},{17,25},{25,17},{2,10},{10... | collective-permute-start | bytes 491528 | tf_op jit(solution)/shard_map/ppermute | solution.py:203
  30.4 6.9 %collective-permute-start.14 = (f32[160,128]{1,0:T(8,128)S(1)}, f32[160,128]{1,0:T(8,128)S(1)}, u32[]{:S(2)}, u32[]{:S(2)}) collective-permute-start(f32[160,128]{1,0:T(8,128)S(1)} %add.47), channel_id=1, source_target_pairs={{0,4},{2,6},{4,0},{6,2},{1,5},{3,7},{5,1},{7,3},{8,12},{10,14},{12... | collective-permute-start | bytes 245768 | tf_op jit(solution)/shard_map/ppermute | solution.py:203
  33.5 11.4 %collective-permute-start.19 = (f32[256,128]{1,0:T(8,128)S(1)}, f32[256,128]{1,0:T(8,128)S(1)}, u32[]{:S(2)}, u32[]{:S(2)}) collective-permute-start(f32[256,128]{1,0:T(8,128)S(1)} %add_add_fusion.1.mine_term_ref), channel_id=1, source_target_pairs={{0,1},{1,0},{2,3},{3,2},{4,5},{5,4},{6,7},{7,6},{8,9},{9,8},{10,11... | collective-permute-start | bytes 393224 | tf_op jit(solution)/shard_map/ppermute | solution.py:203
  37.3 5.5 %collective-permute-start.17 = (f32[160,128]{1,0:T(8,128)S(1)}, f32[160,128]{1,0:T(8,128)S(1)}, u32[]{:S(2)}, u32[]{:S(2)}) collective-permute-start(f32[160,128]{1,0:T(8,128)S(1)} %add.48), channel_id=1, source_target_pairs={{0,24},{8,16},{16,8},{24,0},{1,25},{9,17},{17,9},{25,1},{2,26},{10... | collective-permute-start | bytes 245768 | tf_op jit(solution)/shard_map/ppermute | solution.py:203
  39.8 4.6 %collective-permute-start.16 = (f32[160,128]{1,0:T(8,128)S(1)}, f32[160,128]{1,0:T(8,128)S(1)}, u32[]{:S(2)}, u32[]{:S(2)}) collective-permute-start(f32[160,128]{1,0:T(8,128)S(1)} %add.48), channel_id=1, source_target_pairs={{0,16},{8,24},{16,0},{24,8},{1,17},{9,25},{17,1},{25,9},{2,18},{10... | collective-permute-start | bytes 245768 | tf_op jit(solution)/shard_map/ppermute | solution.py:203
  40.3 4.4 %collective-permute-start.15 = (f32[160,128]{1,0:T(8,128)S(1)}, f32[160,128]{1,0:T(8,128)S(1)}, u32[]{:S(2)}, u32[]{:S(2)}) collective-permute-start(f32[160,128]{1,0:T(8,128)S(1)} %add.48), channel_id=1, source_target_pairs={{0,8},{8,0},{16,24},{24,16},{1,9},{9,1},{17,25},{25,17},{2,10},{10... | collective-permute-start | bytes 245768 | tf_op jit(solution)/shard_map/ppermute | solution.py:203
  40.9 5.2 %collective-permute-start.12 = (f32[160,256]{1,0:T(8,128)S(1)}, f32[160,256]{1,0:T(8,128)S(1)}, u32[]{:S(2)}, u32[]{:S(2)}) collective-permute-start(f32[160,256]{1,0:T(8,128)S(1)} %add_add_fusion.mine_d_ref), channel_id=1, source_target_pairs={{0,1},{1,0},{2,3},{3,2},{4,5},{5,4},{6,7},{7,6},{8,9},{9,8},{10,11... | collective-permute-start | bytes 491528 | tf_op jit(solution)/shard_map/ppermute | solution.py:203
  44.8 1.3 %collective-permute-start.18 = (f32[160,128]{1,0:T(8,128)S(1)}, f32[160,128]{1,0:T(8,128)S(1)}, u32[]{:S(2)}, u32[]{:S(2)}) collective-permute-start(f32[160,128]{1,0:T(8,128)S(1)} %add_add_fusion.2.mine_t_ref), channel_id=1, source_target_pairs={{0,1},{1,0},{2,3},{3,2},{4,5},{5,4},{6,7},{7,6},{8,9},{9,8},{10,11... | collective-permute-start | bytes 245768 | tf_op jit(solution)/shard_map/ppermute | solution.py:203

commit v14 on v13

--- a/solution.py
+++ b/solution.py
@@ -46,7 +46,8 @@
     counts, widths_ref, weights_ref, place_ref, inverse_ref, diag_ref, *refs
 ):
     row_count, col_count = counts
-    own_refs, (straight_ref, own_wide_ref, term_ref) = refs[:col_count], refs[col_count:]
+    own_refs, refs = refs[:col_count], refs[col_count:]
+    straight_ref, own_wide_ref, term_ref, pick_d_ref, pick_t_ref, keep_ref, upper_ref = refs
     packed_width = own_refs[0].shape[0] // 2
     col_index = place_ref[1]
     block = inverse_ref.shape[1]
@@ -92,6 +93,28 @@
     term_ref[...] = weights_ref[0, 0] * diag_ref[0, pl.ds(first, per_col), :].astype(
         F32
     ) - weights_ref[0, 1] * diag_ref[1, pl.ds(first, per_col), :].astype(F32)
+    side = jnp.where((col_index & (col_count // 2)) != 0, 1, 0)
+    half = packed_width // 2
+    position = jnp.where(column < half, column + side * half, column - side * half)
+    lane = lax.broadcasted_iota(jnp.int32, (slot, slot), 1)
+    for k in range(total_cols // slot):
+        chosen = (position == row_in_slot + offsets[k]) & (row_in_slot < widths_ref[k])
+        rows = slice(k * slot, (k + 1) * slot)
+        pick_t_ref[rows, :] = jnp.where(chosen, 1.0, 0.0).astype(BF16)
+        keep_ref[rows, :] = jnp.where(
+            (lane < widths_ref[k]) & (row_in_slot[:, :slot] < widths_ref[k]), 1.0, 0.0
+        )
+    size = min(per_col, slot)
+    for part in range(per_col // size):
+        begin = col_index * per_col + part * size
+        start, count = 0, 0
+        for k in range(total_cols // slot):
+            start = start + jnp.where(k < begin // slot, widths_ref[k], 0)
+            count = count + jnp.where(k == begin // slot, widths_ref[k], 0)
+        within = row_in_slot[:size] + begin % slot
+        chosen = (position[:size] == within + start) & (within < count)
+        pick_d_ref[part * size:(part + 1) * size, :] = jnp.where(chosen, 1.0, 0.0).astype(BF16)
+    upper_ref[...] = jnp.full(upper_ref.shape, side, jnp.int32).astype(F32)
 
 
 def compute_kernel(
@@ -142,57 +165,29 @@
     send_t_ref[...] = jnp.where(upper, t_ref[:half], t_ref[half:2 * half])
 
 
+def picked(pick_ref, value):
+    high = value.astype(BF16)
+    low = (value - high.astype(F32)).astype(BF16)
+    return jnp.dot(pick_ref[...], high, preferred_element_type=F32) + jnp.dot(
+        pick_ref[...], low, preferred_element_type=F32
+    )
+
+
 def expand_kernel(
-    col_count, slot, widths_ref, place_ref, mine_d_ref, other_d_ref, mine_t_ref, other_t_ref,
-    mine_term_ref, other_term_ref, density_ref, diagonal_ref, strip_ref,
+    pick_d_ref, pick_t_ref, keep_ref, upper_ref, mine_d_ref, other_d_ref, mine_t_ref, other_t_ref,
+    mine_term_ref, other_term_ref, density_ref, diagonal_ref,
 ):
-    supernodes = diagonal_ref.shape[0] // slot
-    per_col, local_rows = density_ref.shape
-    strips = local_rows // slot
-    share = col_count // 2
-    part = mine_d_ref.shape[0] // share
-    col_index = place_ref[1]
-    upper = (col_index & share) != 0
+    density_ref[...] = picked(pick_d_ref, jnp.concatenate([mine_d_ref[...], other_d_ref[...]], axis=0))
+    product = picked(pick_t_ref, jnp.concatenate([mine_t_ref[...], other_t_ref[...]], axis=0))
+    rows = mine_term_ref.shape[0]
+    upper = upper_ref[:1, :] > 0.5
+    terms = (
+        jnp.where(upper, other_term_ref[...], mine_term_ref[...]),
+        jnp.where(upper, mine_term_ref[...], other_term_ref[...]),
+    )
     for side in range(2):
-        own_side = upper if side else jnp.logical_not(upper)
-        d_value = jnp.where(own_side, mine_d_ref[...], other_d_ref[...])
-        t_value = jnp.where(own_side, mine_t_ref[...], other_t_ref[...])
-        rows = mine_term_ref.shape[0]
-        diagonal_ref[side * rows:(side + 1) * rows] = jnp.where(
-            own_side, mine_term_ref[...], other_term_ref[...]
-        )
-        for q in range(share):
-            owner = side * share + q
-            base = owner * part
-            for s in range(strips):
-                lanes = slice(s * slot, (s + 1) * slot)
-                strip_ref[s, base:base + part] = d_value[q * part:(q + 1) * part, lanes]
-            strip_ref[strips, base:base + part] = t_value[q * part:(q + 1) * part]
-    for s in range(strips + 1):
-        strip_ref[s, col_count * part:] = jnp.zeros((slot, slot), F32)
-    offsets = offsets_of(widths_ref, supernodes)
-    lane = lax.broadcasted_iota(jnp.int32, (1, slot), 1)
-    row_in_slot = lax.broadcasted_iota(jnp.int32, (slot, 1), 0)
-    for k in range(supernodes):
-        product = strip_ref[strips, pl.ds(offsets[k], slot), :]
-        valid = (row_in_slot < widths_ref[k]) & (lane < widths_ref[k])
-        product = jnp.where(valid, product, 0.0)
-        diagonal_ref[k * slot:(k + 1) * slot] -= product
-    size = min(per_col, slot)
-    row_in_part = lax.broadcasted_iota(jnp.int32, (size, 1), 0)
-    for part in range(per_col // size):
-        first = col_index * per_col + part * size
-        owner = first // slot
-        within = first % slot
-        start, count = 0, 0
-        for k in range(supernodes):
-            start = start + jnp.where(k < owner, widths_ref[k], 0)
-            count = count + jnp.where(k == owner, widths_ref[k], 0)
-        for s in range(strips):
-            piece = strip_ref[s, pl.ds(start + within, size), :]
-            density_ref[part * size:(part + 1) * size, s * slot:(s + 1) * slot] = jnp.where(
-                row_in_part < count - within, piece, 0.0
-            )
+        part = slice(side * rows, (side + 1) * rows)
+        diagonal_ref[part] = terms[side] - jnp.where(keep_ref[part] > 0.5, product[part], 0.0)
 
 
 def bits_of(count):
@@ -262,14 +257,18 @@
         blocks[shift] = lax.ppermute(packed, "row", pairs)
     own = [packed] + [swap(packed, "col", other) for other in range(1, col_count)]
 
-    straight, own_wide, term = pl.pallas_call(
+    straight, own_wide, term, *picks = pl.pallas_call(
         functools.partial(prepare_kernel, (row_count, col_count)),
         in_specs=[SMEM_SPEC] * 3 + [VMEM_SPEC] * (2 + col_count),
-        out_specs=[VMEM_SPEC] * 3,
+        out_specs=[VMEM_SPEC] * 7,
         out_shape=[
             jax.ShapeDtypeStruct((2, local_rows, row_count * block), BF16),
             jax.ShapeDtypeStruct((total_cols, 2 * local_rows), BF16),
             jax.ShapeDtypeStruct((total_cols // col_count, slot), F32),
+            jax.ShapeDtypeStruct((total_cols // col_count, packed_width), BF16),
+            jax.ShapeDtypeStruct((total_cols, packed_width), BF16),
+            jax.ShapeDtypeStruct((total_cols, slot), F32),
+            jax.ShapeDtypeStruct((8, slot), F32),
         ],
         compiler_params=PARAMS,
         cost_estimate=pl.CostEstimate(
@@ -315,19 +314,18 @@
     products = gather_but_last(products, "col")
 
     return pl.pallas_call(
-        functools.partial(expand_kernel, col_count, slot),
-        in_specs=[SMEM_SPEC] * 2 + [VMEM_SPEC] * 6,
+        expand_kernel,
+        in_specs=[VMEM_SPEC] * 10,
         out_specs=[VMEM_SPEC] * 2,
         out_shape=[
             jax.ShapeDtypeStruct((total_cols // col_count, local_rows), F32),
             jax.ShapeDtypeStruct((total_cols, slot), F32),
         ],
-        scratch_shapes=[pltpu.VMEM((local_rows // slot + 1, packed_width + slot, slot), F32)],
         compiler_params=PARAMS,
         name="expand",
     )(
-        sup_widths, place, density, swap(density, "col", top),
-        products, swap(products, "col", top), term, swap(term, "col", top),
+        *picks, density, swap(density, "col", top), products, swap(products, "col", top),
+        term, swap(term, "col", top),
     )
 
 

time: 47.8 us -> 47.6 us (level)
    unnamed x12 -> x10, local copies, waits for them, and re-layouts: 2.63 us -> 2.63 us
where the time goes in v14:
time: 47.6 us; the launch traced here: 47.4 us
  starting transfers between devices  25.6 us (54%)
  waiting for transfers between devices  11.5 us (24%)
  Pallas kernels  6.64 us (14%)
  local copies, waits for them, and re-layouts  2.63 us (6%)
  between operations  0.75 us (2%)
    ppermute x17, starting transfers between devices, swap(): lax.ppermute(value, axis, [(i, i ^ bit) for i in range(lax.axis_size(axis...  18.2 us
    ppermute x17, waiting for transfers between devices, swap(): lax.ppermute(value, axis, [(i, i ^ bit) for i in range(lax.axis_size(axis...  10.1 us
    ppermute x3, starting transfers between devices, per_device(): blocks[shift] = lax.ppermute(packed, 'row', pairs)  7.41 us
    unnamed x10, local copies, waits for them, and re-layouts  2.63 us
    pallas_call x1, Pallas kernels, per_device(): pl.pallas_call(functools.partial(pack_kernel, supernodes, slot), in_specs...  2 us
    pallas_call x1, Pallas kernels, per_device(): pl.pallas_call(functools.partial(compute_kernel, shifts, col_count, super...  1.99 us
    pallas_call x1, Pallas kernels, per_device(): pl.pallas_call(functools.partial(prepare_kernel, (row_count, col_count)),...  1.41 us
    ppermute x3, waiting for transfers between devices, per_device(): blocks[shift] = lax.ppermute(packed, 'row', pairs)  1.37 us
  transfers between devices with their start and end apart: 20, of which 7 were waited for; matrix products, arithmetic and copies ran while one was open for 0% of the time, Pallas kernels for 7%

profile of v14, /device:TPU:0, one launch (start us, length us, event | category | flops | bytes accessed | tf_op | source)
XLA Modules:
  0.0 47.4 jit_solution(13554070809304398528)
XLA Ops:
  0.6 0.0 copy-start.2
  0.6 2.0 %pack.1.refs_0_ = bf16[640,128]{1,0:T(8,128)(2,1)} custom-call(s32[1,4]{1,0:T(1,128)} %pattern_ref.1, s32[4]{0:T(128)} %widths_ref.5, bf16[2,128,512]{2,1,0:T(8,128)(2,1)} %bitcast.7), custom_call_target="tpu_custom_call" | custom-call | tf_op jit(solution)/shard_map/pack/pallas_call | solution.py:245
  2.6 0.5 collective-permute-start
  3.1 3.6 %collective-permute-start.3 = (bf16[640,128]{1,0:T(8,128)(2,1)}, bf16[640,128]{1,0:T(8,128)(2,1)S(1)}, u32[]{:S(2)}, u32[]{:S(2)}) collective-permute-start(bf16[640,128]{1,0:T(8,128)(2,1)} %pack.1.refs_0_), channel_id=1, source_target_pairs={{4,0},{6,2},{0,4},{2,6},{5,1},{7,3},{1,5},{3,7},{12,8},{14,10},{8,... | collective-permute-start | bytes 491528 | tf_op jit(solution)/shard_map/ppermute | solution.py:257
  6.7 1.6 %collective-permute-start.2 = (bf16[640,128]{1,0:T(8,128)(2,1)}, bf16[640,128]{1,0:T(8,128)(2,1)S(1)}, u32[]{:S(2)}, u32[]{:S(2)}) collective-permute-start(bf16[640,128]{1,0:T(8,128)(2,1)} %pack.1.refs_0_), channel_id=1, source_target_pairs={{6,0},{0,2},{2,4},{4,6},{7,1},{1,3},{3,5},{5,7},{14,8},{8,10},{10,... | collective-permute-start | bytes 491528 | tf_op jit(solution)/shard_map/ppermute | solution.py:257
  8.3 2.2 %collective-permute-start.1 = (bf16[640,128]{1,0:T(8,128)(2,1)}, bf16[640,128]{1,0:T(8,128)(2,1)S(1)}, u32[]{:S(2)}, u32[]{:S(2)}) collective-permute-start(bf16[640,128]{1,0:T(8,128)(2,1)} %pack.1.refs_0_), channel_id=1, source_target_pairs={{2,0},{4,2},{6,4},{0,6},{3,1},{5,3},{7,5},{1,7},{10,8},{12,10},{14... | collective-permute-start | bytes 491528 | tf_op jit(solution)/shard_map/ppermute | solution.py:257
  10.5 0.1 pad_add_fusion.place_ref
  10.6 0.0 collective-permute-done.refs_1_
  10.6 0.0 copy-start.3
  10.6 0.0 copy-start.4
  10.6 0.0 copy-done.2
  10.6 0.6 %copy-done.3 = s32[4]{0:T(128)S(1)} copy-done((s32[4]{0:T(128)S(1)}, s32[4]{0:T(128)}, u32[]{:S(2)}) %copy-start.3) | copy-done | bytes 40
  11.2 0.0 copy-done.4
  11.3 0.0 copy-start
  11.3 0.9 %copy-done = bf16[640,128]{1,0:T(8,128)(2,1)S(1)} copy-done((bf16[640,128]{1,0:T(8,128)(2,1)S(1)}, bf16[640,128]{1,0:T(8,128)(2,1)}, u32[]{:S(2)}) %copy-start) | copy-done | bytes 163864
  12.2 0.0 copy-start.1
  12.2 1.0 %copy-done.1 = bf16[1,2,256,4,1,128]{5,3,4,2,1,0:T(4,128)(2,1)S(1)} copy-done((bf16[1,2,256,4,1,128]{5,3,4,2,1,0:T(4,128)(2,1)S(1)}, bf16[1,2,256,4,1,128]{5,3,4,2,1,0:T(4,128)(2,1)}, u32[]{:S(2)}) %copy-start.1) | copy-done | bytes 524312
  13.2 1.4 %prepare.1 = (bf16[2,256,512]{2,1,0:T(8,128)(2,1)S(1)}, bf16[512,512]{1,0:T(8,128)(2,1)S(1)}, f32[256,128]{1,0:T(8,128)S(1)}, bf16[256,320]{1,0:T(8,128)(2,1)S(1...) custom-call(s32[4]{0:T(128)S(1)} %copy-done.3, f32[1,2]{1,0:T(1,128)S(1)} %copy-done.4, ...), custom_call_target="tpu_custom_call" | custom-call | flops 134217728 | bytes 1048576 | tf_op jit(solution)/shard_map/prepare/pallas_call | solution.py:260
  14.6 2.5 %collective-permute-start.7 = (f32[256,128]{1,0:T(8,128)S(1)}, f32[256,128]{1,0:T(8,128)S(1)}, u32[]{:S(2)}, u32[]{:S(2)}) collective-permute-start(f32[256,128]{1,0:T(8,128)S(1)} %get-tuple-element.26), channel_id=1, source_target_pairs={{0,24},{8,16},{16,8},{24,0},{1,25},{9,17},{17,9},{25,1},{2,26},{10... | collective-permute-start | bytes 393224 | tf_op jit(solution)/shard_map/ppermute | solution.py:198
  17.1 0.5 %collective-permute-start.6 = (f32[256,128]{1,0:T(8,128)S(1)}, f32[256,128]{1,0:T(8,128)S(1)}, u32[]{:S(2)}, u32[]{:S(2)}) collective-permute-start(f32[256,128]{1,0:T(8,128)S(1)} %get-tuple-element.26), channel_id=1, source_target_pairs={{0,16},{8,24},{16,0},{24,8},{1,17},{9,25},{17,1},{25,9},{2,18},{10... | collective-permute-start | bytes 393224 | tf_op jit(solution)/shard_map/ppermute | solution.py:198
  17.6 1.4 %collective-permute-done.3.refs_3_ = bf16[640,128]{1,0:T(8,128)(2,1)S(1)} collective-permute-done((bf16[640,128]{1,0:T(8,128)(2,1)}, bf16[640,128]{1,0:T(8,128)(2,1)S(1)}, u32[]{:S(2)}, u32[]{:S(2)}) %collective-permute-start.3) | collective-permute-done | bytes 163872 | tf_op jit(solution)/shard_map/ppermute | solution.py:257
  19.0 1.8 %collective-permute-start.5 = (f32[256,128]{1,0:T(8,128)S(1)}, f32[256,128]{1,0:T(8,128)S(1)}, u32[]{:S(2)}, u32[]{:S(2)}) collective-permute-start(f32[256,128]{1,0:T(8,128)S(1)} %get-tuple-element.26), channel_id=1, source_target_pairs={{0,8},{8,0},{16,24},{24,16},{1,9},{9,1},{17,25},{25,17},{2,10},{10... | collective-permute-start | bytes 393224 | tf_op jit(solution)/shard_map/ppermute | solution.py:198
  20.8 0.0 collective-permute-done.2.refs_2_
  20.8 0.0 collective-permute-done.1.refs_1_
  20.8 2.0 %compute.1 = (f32[160,256]{1,0:T(8,128)S(1)}, f32[160,256]{1,0:T(8,128)S(1)}, f32[160,128]{1,0:T(8,128)S(1)}, f32[160,128]{1,0:T(8,128)S(1)}) custom-call(s32[4]{0:T(128)S(1)} %copy-done.3, f32[1,2]{1,0:T(1,128)S(1)} %copy-done.4, s32[2]{0:T(128)S(1)} %pad_add_fusion.place_ref, bf16[2,256,512]{2,1,0:T(8,128)(2,1)S(1)} %get-tuple-element.20.straight_ref, ...), custom_call_target="tpu_custom_call" | custom-call | tf_op jit(solution)/shard_map/compute/pallas_call | solution.py:286
  22.8 0.1 collective-permute-start.4
  22.8 1.3 %collective-permute-done.4 = f32[160,128]{1,0:T(8,128)S(1)} collective-permute-done((f32[160,128]{1,0:T(8,128)S(1)}, f32[160,128]{1,0:T(8,128)S(1)}, u32[]{:S(2)}, u32[]{:S(2)}) %collective-permute-start.4) | collective-permute-done | bytes 81952 | tf_op jit(solution)/shard_map/ppermute | solution.py:198
  24.1 0.0 collective-permute-done.7
  24.1 0.0 collective-permute-done.6
  24.1 0.0 collective-permute-done.5
  24.2 0.2 collective-permute-start.8
  24.4 2.4 %collective-permute-start.13 = (f32[160,128]{1,0:T(8,128)S(1)}, f32[160,128]{1,0:T(8,128)S(1)}, u32[]{:S(2)}, u32[]{:S(2)}) collective-permute-start(f32[160,128]{1,0:T(8,128)S(1)} %add.39), channel_id=1, source_target_pairs={{0,2},{2,0},{4,6},{6,4},{1,3},{3,1},{5,7},{7,5},{8,10},{10,8},{12,... | collective-permute-start | bytes 245768 | tf_op jit(solution)/shard_map/ppermute | solution.py:198
  26.8 0.0 collective-permute-done.8
  26.8 2.5 %collective-permute-start.11 = (f32[160,256]{1,0:T(8,128)S(1)}, f32[160,256]{1,0:T(8,128)S(1)}, u32[]{:S(2)}, u32[]{:S(2)}) collective-permute-start(f32[160,256]{1,0:T(8,128)S(1)} %add.43), channel_id=1, source_target_pairs={{0,24},{8,16},{16,8},{24,0},{1,25},{9,17},{17,9},{25,1},{2,26},{10... | collective-permute-start | bytes 491528 | tf_op jit(solution)/shard_map/ppermute | solution.py:198
  29.3 0.5 %collective-permute-start.10 = (f32[160,256]{1,0:T(8,128)S(1)}, f32[160,256]{1,0:T(8,128)S(1)}, u32[]{:S(2)}, u32[]{:S(2)}) collective-permute-start(f32[160,256]{1,0:T(8,128)S(1)} %add.43), channel_id=1, source_target_pairs={{0,16},{8,24},{16,0},{24,8},{1,17},{9,25},{17,1},{25,9},{2,18},{10... | collective-permute-start | bytes 491528 | tf_op jit(solution)/shard_map/ppermute | solution.py:198
  29.8 0.5 %collective-permute-start.9 = (f32[160,256]{1,0:T(8,128)S(1)}, f32[160,256]{1,0:T(8,128)S(1)}, u32[]{:S(2)}, u32[]{:S(2)}) collective-permute-start(f32[160,256]{1,0:T(8,128)S(1)} %add.43), channel_id=1, source_target_pairs={{0,8},{8,0},{16,24},{24,16},{1,9},{9,1},{17,25},{25,17},{2,10},{10... | collective-permute-start | bytes 491528 | tf_op jit(solution)/shard_map/ppermute | solution.py:198
  30.4 0.0 collective-permute-done.13
  30.4 3.1 %collective-permute-start.14 = (f32[160,128]{1,0:T(8,128)S(1)}, f32[160,128]{1,0:T(8,128)S(1)}, u32[]{:S(2)}, u32[]{:S(2)}) collective-permute-start(f32[160,128]{1,0:T(8,128)S(1)} %add.47), channel_id=1, source_target_pairs={{0,4},{2,6},{4,0},{6,2},{1,5},{3,7},{5,1},{7,3},{8,12},{10,14},{12... | collective-permute-start | bytes 245768 | tf_op jit(solution)/shard_map/ppermute | solution.py:198
  33.5 0.0 collective-permute-start.19
  33.5 3.8 %collective-permute-done.14 = f32[160,128]{1,0:T(8,128)S(1)} collective-permute-done((f32[160,128]{1,0:T(8,128)S(1)}, f32[160,128]{1,0:T(8,128)S(1)}, u32[]{:S(2)}, u32[]{:S(2)}) %collective-permute-start.14) | collective-permute-done | bytes 81952 | tf_op jit(solution)/shard_map/ppermute | solution.py:198
  37.3 2.5 %collective-permute-start.17 = (f32[160,128]{1,0:T(8,128)S(1)}, f32[160,128]{1,0:T(8,128)S(1)}, u32[]{:S(2)}, u32[]{:S(2)}) collective-permute-start(f32[160,128]{1,0:T(8,128)S(1)} %add.48), channel_id=1, source_target_pairs={{0,24},{8,16},{16,8},{24,0},{1,25},{9,17},{17,9},{25,1},{2,26},{10... | collective-permute-start | bytes 245768 | tf_op jit(solution)/shard_map/ppermute | solution.py:198
  39.8 0.0 collective-permute-done.11
  39.8 0.5 %collective-permute-start.16 = (f32[160,128]{1,0:T(8,128)S(1)}, f32[160,128]{1,0:T(8,128)S(1)}, u32[]{:S(2)}, u32[]{:S(2)}) collective-permute-start(f32[160,128]{1,0:T(8,128)S(1)} %add.48), channel_id=1, source_target_pairs={{0,16},{8,24},{16,0},{24,8},{1,17},{9,25},{17,1},{25,9},{2,18},{10... | collective-permute-start | bytes 245768 | tf_op jit(solution)/shard_map/ppermute | solution.py:198
  40.3 0.0 collective-permute-done.10
  40.3 0.5 %collective-permute-start.15 = (f32[160,128]{1,0:T(8,128)S(1)}, f32[160,128]{1,0:T(8,128)S(1)}, u32[]{:S(2)}, u32[]{:S(2)}) collective-permute-start(f32[160,128]{1,0:T(8,128)S(1)} %add.48), channel_id=1, source_target_pairs={{0,8},{8,0},{16,24},{24,16},{1,9},{9,1},{17,25},{25,17},{2,10},{10... | collective-permute-start | bytes 245768 | tf_op jit(solution)/shard_map/ppermute | solution.py:198
  40.9 0.0 collective-permute-done.9
  40.9 0.1 collective-permute-start.12
  41.0 1.8 %collective-permute-done.17 = f32[160,128]{1,0:T(8,128)S(1)} collective-permute-done((f32[160,128]{1,0:T(8,128)S(1)}, f32[160,128]{1,0:T(8,128)S(1)}, u32[]{:S(2)}, u32[]{:S(2)}) %collective-permute-start.17) | collective-permute-done | bytes 81952 | tf_op jit(solution)/shard_map/ppermute | solution.py:198
  42.8 1.7 %collective-permute-done.16 = f32[160,128]{1,0:T(8,128)S(1)} collective-permute-done((f32[160,128]{1,0:T(8,128)S(1)}, f32[160,128]{1,0:T(8,128)S(1)}, u32[]{:S(2)}, u32[]{:S(2)}) %collective-permute-start.16) | collective-permute-done | bytes 81952 | tf_op jit(solution)/shard_map/ppermute | solution.py:198
  44.5 0.3 collective-permute-done.15
  44.8 0.1 collective-permute-start.18
  44.9 0.0 collective-permute-done.19.other_term_ref
  44.9 1.3 %collective-permute-done.18.other_t_ref = f32[160,128]{1,0:T(8,128)S(1)} collective-permute-done((f32[160,128]{1,0:T(8,128)S(1)}, f32[160,128]{1,0:T(8,128)S(1)}, u32[]{:S(2)}, u32[]{:S(2)}) %collective-permute-start.18) | collective-permute-done | bytes 81952 | tf_op jit(solution)/shard_map/ppermute | solution.py:198
  46.1 0.0 collective-permute-done.12.other_d_ref
  46.1 1.2 %expand.1 = (f32[256,256]{1,0:T(8,128)}, f32[512,128]{1,0:T(8,128)}) custom-call(bf16[256,320]{1,0:T(8,128)(2,1)S(1)} %get-tuple-element.16.pick_d_ref, bf16[512,320]{1,0:T(8,128)(2,1)S(1)} %get-tuple-element.17.pick_t_ref, f32[512,128]{1,0:T(8,128)S(1)} %get-tuple-element.18.keep_ref, f32[8,128]{1,0:T(8,128)S(1)} %get-tuple-element.19.upper_ref, ...), custom_call_target="tpu_custom_call" | custom-call | tf_op jit(solution)/shard_map/expand/pallas_call | solution.py:316
  (7 shorter events, 0.2 us)
Async XLA Ops:
  0.6 10.0 %copy-start.2 = (bf16[1,2,512,128]{3,2,1,0:T(8,128)(2,1)S(1)}, bf16[1,2,512,128]{3,2,1,0:T(8,128)(2,1)}, u32[]{:S(2)}) copy-start(bf16[1,2,512,128]{3,2,1,0:T(8,128)(2,1)} %param.10) | copy-start | bytes 786436
  2.6 7.9 %collective-permute-start = (bf16[640,128]{1,0:T(8,128)(2,1)}, bf16[640,128]{1,0:T(8,128)(2,1)S(1)}, u32[]{:S(2)}, u32[]{:S(2)}) collective-permute-start(bf16[640,128]{1,0:T(8,128)(2,1)} %pack.1.refs_0_), channel_id=1, source_target_pairs={{0,1},{1,0},{2,3},{3,2},{4,5},{5,4},{6,7},{7,6},{8,9},{9,8},{10,11... | collective-permute-start | bytes 491528 | tf_op jit(solution)/shard_map/ppermute | solution.py:198
  3.1 15.9 %collective-permute-start.3 = (bf16[640,128]{1,0:T(8,128)(2,1)}, bf16[640,128]{1,0:T(8,128)(2,1)S(1)}, u32[]{:S(2)}, u32[]{:S(2)}) collective-permute-start(bf16[640,128]{1,0:T(8,128)(2,1)} %pack.1.refs_0_), channel_id=1, source_target_pairs={{4,0},{6,2},{0,4},{2,6},{5,1},{7,3},{1,5},{3,7},{12,8},{14,10},{8,... | collective-permute-start | bytes 491528 | tf_op jit(solution)/shard_map/ppermute | solution.py:257
  6.7 14.1 %collective-permute-start.2 = (bf16[640,128]{1,0:T(8,128)(2,1)}, bf16[640,128]{1,0:T(8,128)(2,1)S(1)}, u32[]{:S(2)}, u32[]{:S(2)}) collective-permute-start(bf16[640,128]{1,0:T(8,128)(2,1)} %pack.1.refs_0_), channel_id=1, source_target_pairs={{6,0},{0,2},{2,4},{4,6},{7,1},{1,3},{3,5},{5,7},{14,8},{8,10},{10,... | collective-permute-start | bytes 491528 | tf_op jit(solution)/shard_map/ppermute | solution.py:257
  8.3 12.5 %collective-permute-start.1 = (bf16[640,128]{1,0:T(8,128)(2,1)}, bf16[640,128]{1,0:T(8,128)(2,1)S(1)}, u32[]{:S(2)}, u32[]{:S(2)}) collective-permute-start(bf16[640,128]{1,0:T(8,128)(2,1)} %pack.1.refs_0_), channel_id=1, source_target_pairs={{2,0},{4,2},{6,4},{0,6},{3,1},{5,3},{7,5},{1,7},{10,8},{12,10},{14... | collective-permute-start | bytes 491528 | tf_op jit(solution)/shard_map/ppermute | solution.py:257
  10.6 0.7 %copy-start.3 = (s32[4]{0:T(128)S(1)}, s32[4]{0:T(128)}, u32[]{:S(2)}) copy-start(s32[4]{0:T(128)} %widths_ref.5) | copy-start | bytes 52
  10.6 0.7 %copy-start.4 = (f32[1,2]{1,0:T(1,128)S(1)}, f32[1,2]{1,0:T(1,128)}, u32[]{:S(2)}) copy-start(f32[1,2]{1,0:T(1,128)} %weights_ref.3) | copy-start | bytes 28
  11.3 0.9 %copy-start = (bf16[640,128]{1,0:T(8,128)(2,1)S(1)}, bf16[640,128]{1,0:T(8,128)(2,1)}, u32[]{:S(2)}) copy-start(bf16[640,128]{1,0:T(8,128)(2,1)} %pack.1.refs_0_) | copy-start | bytes 491524
  12.2 1.0 %copy-start.1 = (bf16[1,2,256,4,1,128]{5,3,4,2,1,0:T(4,128)(2,1)S(1)}, bf16[1,2,256,4,1,128]{5,3,4,2,1,0:T(4,128)(2,1)}, u32[]{:S(2)}) copy-start(bf16[1,2,256,4,1,128]{5,3,4,2,1,0:T(4,128)(2,1)} %param.6) | copy-start | bytes 1572868
  14.6 9.5 %collective-permute-start.7 = (f32[256,128]{1,0:T(8,128)S(1)}, f32[256,128]{1,0:T(8,128)S(1)}, u32[]{:S(2)}, u32[]{:S(2)}) collective-permute-start(f32[256,128]{1,0:T(8,128)S(1)} %get-tuple-element.26), channel_id=1, source_target_pairs={{0,24},{8,16},{16,8},{24,0},{1,25},{9,17},{17,9},{25,1},{2,26},{10... | collective-permute-start | bytes 393224 | tf_op jit(solution)/shard_map/ppermute | solution.py:198
  17.1 7.0 %collective-permute-start.6 = (f32[256,128]{1,0:T(8,128)S(1)}, f32[256,128]{1,0:T(8,128)S(1)}, u32[]{:S(2)}, u32[]{:S(2)}) collective-permute-start(f32[256,128]{1,0:T(8,128)S(1)} %get-tuple-element.26), channel_id=1, source_target_pairs={{0,16},{8,24},{16,0},{24,8},{1,17},{9,25},{17,1},{25,9},{2,18},{10... | collective-permute-start | bytes 393224 | tf_op jit(solution)/shard_map/ppermute | solution.py:198
  19.0 5.1 %collective-permute-start.5 = (f32[256,128]{1,0:T(8,128)S(1)}, f32[256,128]{1,0:T(8,128)S(1)}, u32[]{:S(2)}, u32[]{:S(2)}) collective-permute-start(f32[256,128]{1,0:T(8,128)S(1)} %get-tuple-element.26), channel_id=1, source_target_pairs={{0,8},{8,0},{16,24},{24,16},{1,9},{9,1},{17,25},{25,17},{2,10},{10... | collective-permute-start | bytes 393224 | tf_op jit(solution)/shard_map/ppermute | solution.py:198
  22.8 1.3 %collective-permute-start.4 = (f32[160,128]{1,0:T(8,128)S(1)}, f32[160,128]{1,0:T(8,128)S(1)}, u32[]{:S(2)}, u32[]{:S(2)}) collective-permute-start(f32[160,128]{1,0:T(8,128)S(1)} %get-tuple-element.24), channel_id=1, source_target_pairs={{0,1},{1,0},{2,3},{3,2},{4,5},{5,4},{6,7},{7,6},{8,9},{9,8},{10,11... | collective-permute-start | bytes 245768 | tf_op jit(solution)/shard_map/ppermute | solution.py:198
  24.2 2.6 %collective-permute-start.8 = (f32[160,256]{1,0:T(8,128)S(1)}, f32[160,256]{1,0:T(8,128)S(1)}, u32[]{:S(2)}, u32[]{:S(2)}) collective-permute-start(f32[160,256]{1,0:T(8,128)S(1)} %get-tuple-element.27), channel_id=1, source_target_pairs={{0,1},{1,0},{2,3},{3,2},{4,5},{5,4},{6,7},{7,6},{8,9},{9,8},{10,11... | collective-permute-start | bytes 491528 | tf_op jit(solution)/shard_map/ppermute | solution.py:198
  24.4 5.9 %collective-permute-start.13 = (f32[160,128]{1,0:T(8,128)S(1)}, f32[160,128]{1,0:T(8,128)S(1)}, u32[]{:S(2)}, u32[]{:S(2)}) collective-permute-start(f32[160,128]{1,0:T(8,128)S(1)} %add.39), channel_id=1, source_target_pairs={{0,2},{2,0},{4,6},{6,4},{1,3},{3,1},{5,7},{7,5},{8,10},{10,8},{12,... | collective-permute-start | bytes 245768 | tf_op jit(solution)/shard_map/ppermute | solution.py:198
  26.8 13.0 %collective-permute-start.11 = (f32[160,256]{1,0:T(8,128)S(1)}, f32[160,256]{1,0:T(8,128)S(1)}, u32[]{:S(2)}, u32[]{:S(2)}) collective-permute-start(f32[160,256]{1,0:T(8,128)S(1)} %add.43), channel_id=1, source_target_pairs={{0,24},{8,16},{16,8},{24,0},{1,25},{9,17},{17,9},{25,1},{2,26},{10... | collective-permute-start | bytes 491528 | tf_op jit(solution)/shard_map/ppermute | solution.py:198
  29.3 11.0 %collective-permute-start.10 = (f32[160,256]{1,0:T(8,128)S(1)}, f32[160,256]{1,0:T(8,128)S(1)}, u32[]{:S(2)}, u32[]{:S(2)}) collective-permute-start(f32[160,256]{1,0:T(8,128)S(1)} %add.43), channel_id=1, source_target_pairs={{0,16},{8,24},{16,0},{24,8},{1,17},{9,25},{17,1},{25,9},{2,18},{10... | collective-permute-start | bytes 491528 | tf_op jit(solution)/shard_map/ppermute | solution.py:198
  29.8 11.0 %collective-permute-start.9 = (f32[160,256]{1,0:T(8,128)S(1)}, f32[160,256]{1,0:T(8,128)S(1)}, u32[]{:S(2)}, u32[]{:S(2)}) collective-permute-start(f32[160,256]{1,0:T(8,128)S(1)} %add.43), channel_id=1, source_target_pairs={{0,8},{8,0},{16,24},{24,16},{1,9},{9,1},{17,25},{25,17},{2,10},{10... | collective-permute-start | bytes 491528 | tf_op jit(solution)/shard_map/ppermute | solution.py:198
  30.4 6.9 %collective-permute-start.14 = (f32[160,128]{1,0:T(8,128)S(1)}, f32[160,128]{1,0:T(8,128)S(1)}, u32[]{:S(2)}, u32[]{:S(2)}) collective-permute-start(f32[160,128]{1,0:T(8,128)S(1)} %add.47), channel_id=1, source_target_pairs={{0,4},{2,6},{4,0},{6,2},{1,5},{3,7},{5,1},{7,3},{8,12},{10,14},{12... | collective-permute-start | bytes 245768 | tf_op jit(solution)/shard_map/ppermute | solution.py:198
  33.5 11.4 %collective-permute-start.19 = (f32[256,128]{1,0:T(8,128)S(1)}, f32[256,128]{1,0:T(8,128)S(1)}, u32[]{:S(2)}, u32[]{:S(2)}) collective-permute-start(f32[256,128]{1,0:T(8,128)S(1)} %add_add_fusion.1.mine_term_ref), channel_id=1, source_target_pairs={{0,1},{1,0},{2,3},{3,2},{4,5},{5,4},{6,7},{7,6},{8,9},{9,8},{10,11... | collective-permute-start | bytes 393224 | tf_op jit(solution)/shard_map/ppermute | solution.py:198
  37.3 5.5 %collective-permute-start.17 = (f32[160,128]{1,0:T(8,128)S(1)}, f32[160,128]{1,0:T(8,128)S(1)}, u32[]{:S(2)}, u32[]{:S(2)}) collective-permute-start(f32[160,128]{1,0:T(8,128)S(1)} %add.48), channel_id=1, source_target_pairs={{0,24},{8,16},{16,8},{24,0},{1,25},{9,17},{17,9},{25,1},{2,26},{10... | collective-permute-start | bytes 245768 | tf_op jit(solution)/shard_map/ppermute | solution.py:198
  39.8 4.6 %collective-permute-start.16 = (f32[160,128]{1,0:T(8,128)S(1)}, f32[160,128]{1,0:T(8,128)S(1)}, u32[]{:S(2)}, u32[]{:S(2)}) collective-permute-start(f32[160,128]{1,0:T(8,128)S(1)} %add.48), channel_id=1, source_target_pairs={{0,16},{8,24},{16,0},{24,8},{1,17},{9,25},{17,1},{25,9},{2,18},{10... | collective-permute-start | bytes 245768 | tf_op jit(solution)/shard_map/ppermute | solution.py:198
  40.3 4.4 %collective-permute-start.15 = (f32[160,128]{1,0:T(8,128)S(1)}, f32[160,128]{1,0:T(8,128)S(1)}, u32[]{:S(2)}, u32[]{:S(2)}) collective-permute-start(f32[160,128]{1,0:T(8,128)S(1)} %add.48), channel_id=1, source_target_pairs={{0,8},{8,0},{16,24},{24,16},{1,9},{9,1},{17,25},{25,17},{2,10},{10... | collective-permute-start | bytes 245768 | tf_op jit(solution)/shard_map/ppermute | solution.py:198
  40.9 5.2 %collective-permute-start.12 = (f32[160,256]{1,0:T(8,128)S(1)}, f32[160,256]{1,0:T(8,128)S(1)}, u32[]{:S(2)}, u32[]{:S(2)}) collective-permute-start(f32[160,256]{1,0:T(8,128)S(1)} %add_add_fusion.mine_d_ref), channel_id=1, source_target_pairs={{0,1},{1,0},{2,3},{3,2},{4,5},{5,4},{6,7},{7,6},{8,9},{9,8},{10,11... | collective-permute-start | bytes 491528 | tf_op jit(solution)/shard_map/ppermute | solution.py:198
  44.8 1.3 %collective-permute-start.18 = (f32[160,128]{1,0:T(8,128)S(1)}, f32[160,128]{1,0:T(8,128)S(1)}, u32[]{:S(2)}, u32[]{:S(2)}) collective-permute-start(f32[160,128]{1,0:T(8,128)S(1)} %add_add_fusion.2.mine_t_ref), channel_id=1, source_target_pairs={{0,1},{1,0},{2,3},{3,2},{4,5},{5,4},{6,7},{7,6},{8,9},{9,8},{10,11... | collective-permute-start | bytes 245768 | tf_op jit(solution)/shard_map/ppermute | solution.py:198

commit v15 on v14

--- a/solution.py
+++ b/solution.py
@@ -57,7 +57,7 @@
     span = group * row_count
     row_id = lax.broadcasted_iota(jnp.int32, (span, span), 0)
     col_id = lax.broadcasted_iota(jnp.int32, (span, span), 1)
-    source = (row_id % group) * row_count + (row_id // group + row_index) % row_count
+    source = (row_id % group) * row_count + ((row_id // group) ^ row_index)
     order = jnp.where(col_id == source, 1.0, 0.0).astype(BF16)
     for part in range(2):
         for chunk in range(local_rows // group):
@@ -118,11 +118,10 @@
 
 
 def compute_kernel(
-    shifts, col_count, supernodes, slot, widths_ref, weights_ref, place_ref, straight_ref,
+    col_count, supernodes, slot, widths_ref, weights_ref, place_ref, straight_ref,
     own_wide_ref, *refs
 ):
     block_refs, refs = refs[:-7], refs[-7:]
-    block_refs = [block_refs[shifts.index(shift)] for shift in range(len(shifts))]
     keep_d_ref, send_d_ref, keep_t_ref, send_t_ref, x_ref, y_ref, t_ref = refs
     packed_width = block_refs[0].shape[0] // 2
     local_rows = straight_ref.shape[1]
@@ -251,10 +250,8 @@
     )(block_pattern, sup_widths, l_panel[0])
 
     blocks = {0: packed}
-    shifts = sorted(range(row_count), key=lambda shift: min(shift, row_count - shift))
-    for shift in shifts[1:]:
-        pairs = [((i + shift) % row_count, i) for i in range(row_count)]
-        blocks[shift] = lax.ppermute(packed, "row", pairs)
+    for other in range(1, row_count):
+        blocks[other] = swap(packed, "row", other)
     own = [packed] + [swap(packed, "col", other) for other in range(1, col_count)]
 
     straight, own_wide, term, *picks = pl.pallas_call(
@@ -284,7 +281,7 @@
     term = sum_direct(term, "pole")
 
     keep_d, send_d, keep_t, send_t = pl.pallas_call(
-        functools.partial(compute_kernel, shifts, col_count, supernodes, slot),
+        functools.partial(compute_kernel, col_count, supernodes, slot),
         in_specs=[SMEM_SPEC] * 3 + [VMEM_SPEC] * (2 + row_count),
         out_specs=[VMEM_SPEC] * 4,
         out_shape=[jax.ShapeDtypeStruct((half, local_rows), F32)] * 2
@@ -298,15 +295,15 @@
         name="compute",
     )(
         sup_widths, pole_weights, place, straight, own_wide,
-        *[blocks[shift] for shift in shifts],
+        *[blocks[other] for other in range(row_count)],
     )
 
     tie = lax.optimization_barrier
     products, send_d, term = tie((keep_t + swap(send_t, "col", top), send_d, term))
     term = gather_but_last(term, "col")
     products = scatter_rest(products, "col")
-    for bit in bits_of(row_count):
-        products = products + swap(products, "row", bit)
+    for bit in bits_of(row_count)[::-1]:
+        products = products + swap(products, "row", 2 * bit - 1)
     density = scatter_rest(keep_d + swap(send_d, "col", top), "col")
     density = sum_direct(density, "pole")
     products = sum_direct(products, "pole")

time: 47.6 us -> 47.4 us (level)
  starting transfers between devices: 25.6 us -> 19.4 us
  waiting for transfers between devices: 11.5 us -> 17.6 us
    ppermute x17 -> x20, waiting for transfers between devices: 10.1 us -> 17.6 us  [swap(): lax.ppermute(value, axis, [(i, i ^ bit) for i in range(lax.axis_size(axis...]
    ppermute x3 -> x0, starting transfers between devices: 7.41 us -> none  [per_device(): blocks[shift] = lax.ppermute(packed, 'row', pairs)]
    ppermute x3 -> x0, waiting for transfers between devices: 1.37 us -> none  [per_device(): blocks[shift] = lax.ppermute(packed, 'row', pairs)]
    ppermute x17 -> x20, starting transfers between devices: 18.2 us -> 19.4 us  [swap(): lax.ppermute(value, axis, [(i, i ^ bit) for i in range(lax.axis_size(axis...]
  transfers between devices with their start and end apart: 20 -> 20, of which waited for: 7 -> 8; matrix products, arithmetic and copies ran while one was open for 0% -> 0% of each run, Pallas kernels for 7% -> 7%
where the time goes in v15:
time: 47.4 us; the launch traced here: 47.2 us
  starting transfers between devices  19.4 us (41%)
  waiting for transfers between devices  17.6 us (37%)
  Pallas kernels  6.61 us (14%)
  local copies, waits for them, and re-layouts  2.63 us (6%)
  between operations  0.77 us (2%)
    ppermute x20, starting transfers between devices, swap(): lax.ppermute(value, axis, [(i, i ^ bit) for i in range(lax.axis_size(axis...  19.4 us
    ppermute x20, waiting for transfers between devices, swap(): lax.ppermute(value, axis, [(i, i ^ bit) for i in range(lax.axis_size(axis...  17.6 us
    unnamed x10, local copies, waits for them, and re-layouts  2.63 us
    pallas_call x1, Pallas kernels, per_device(): pl.pallas_call(functools.partial(pack_kernel, supernodes, slot), in_specs...  2 us
    pallas_call x1, Pallas kernels, per_device(): pl.pallas_call(functools.partial(compute_kernel, col_count, supernodes, s...  1.99 us
    pallas_call x1, Pallas kernels, per_device(): pl.pallas_call(functools.partial(prepare_kernel, (row_count, col_count)),...  1.37 us
    pallas_call x1, Pallas kernels, per_device(): pl.pallas_call(expand_kernel, in_specs=[VMEM_SPEC] * 10, out_specs=[VMEM_...  1.24 us
  transfers between devices with their start and end apart: 20, of which 8 were waited for; matrix products, arithmetic and copies ran while one was open for 0% of the time, Pallas kernels for 7%

profile of v15, /device:TPU:0, one launch (start us, length us, event | category | flops | bytes accessed | tf_op | source)
XLA Modules:
  0.0 47.2 jit_solution(11101958150380059419)
XLA Ops:
  0.6 0.0 copy-start.2
  0.6 2.0 %pack.1.refs_0_ = bf16[640,128]{1,0:T(8,128)(2,1)} custom-call(s32[1,4]{1,0:T(1,128)} %pattern_ref.1, s32[4]{0:T(128)} %widths_ref.5, bf16[2,128,512]{2,1,0:T(8,128)(2,1)} %bitcast.7), custom_call_target="tpu_custom_call" | custom-call | tf_op jit(solution)/shard_map/pack/pallas_call | solution.py:244
  2.6 0.5 collective-permute-start
  3.1 4.6 %collective-permute-start.3 = (bf16[640,128]{1,0:T(8,128)(2,1)}, bf16[640,128]{1,0:T(8,128)(2,1)S(1)}, u32[]{:S(2)}, u32[]{:S(2)}) collective-permute-start(bf16[640,128]{1,0:T(8,128)(2,1)} %pack.1.refs_0_), channel_id=1, source_target_pairs={{0,6},{2,4},{4,2},{6,0},{1,7},{3,5},{5,3},{7,1},{8,14},{10,12},{12... | collective-permute-start | bytes 491528 | tf_op jit(solution)/shard_map/ppermute | solution.py:197
  7.7 0.0 collective-permute-start.2
  7.7 0.6 %collective-permute-start.1 = (bf16[640,128]{1,0:T(8,128)(2,1)}, bf16[640,128]{1,0:T(8,128)(2,1)S(1)}, u32[]{:S(2)}, u32[]{:S(2)}) collective-permute-start(bf16[640,128]{1,0:T(8,128)(2,1)} %pack.1.refs_0_), channel_id=1, source_target_pairs={{0,2},{2,0},{4,6},{6,4},{1,3},{3,1},{5,7},{7,5},{8,10},{10,8},{12,... | collective-permute-start | bytes 491528 | tf_op jit(solution)/shard_map/ppermute | solution.py:197
  8.3 0.1 pad_add_fusion.place_ref
  8.4 0.0 collective-permute-done.refs_1_
  8.4 0.0 copy-start.3
  8.4 0.0 copy-start.4
  8.4 0.0 copy-done.2
  8.4 0.6 %copy-done.3 = s32[4]{0:T(128)S(1)} copy-done((s32[4]{0:T(128)S(1)}, s32[4]{0:T(128)}, u32[]{:S(2)}) %copy-start.3) | copy-done | bytes 40
  9.1 0.0 copy-done.4
  9.1 0.0 copy-start
  9.1 0.9 %copy-done = bf16[640,128]{1,0:T(8,128)(2,1)S(1)} copy-done((bf16[640,128]{1,0:T(8,128)(2,1)S(1)}, bf16[640,128]{1,0:T(8,128)(2,1)}, u32[]{:S(2)}) %copy-start) | copy-done | bytes 163864
  10.0 0.0 copy-start.1
  10.0 1.0 %copy-done.1 = bf16[1,2,256,4,1,128]{5,3,4,2,1,0:T(4,128)(2,1)S(1)} copy-done((bf16[1,2,256,4,1,128]{5,3,4,2,1,0:T(4,128)(2,1)S(1)}, bf16[1,2,256,4,1,128]{5,3,4,2,1,0:T(4,128)(2,1)}, u32[]{:S(2)}) %copy-start.1) | copy-done | bytes 524312
  11.0 1.4 %prepare.1 = (bf16[2,256,512]{2,1,0:T(8,128)(2,1)S(1)}, bf16[512,512]{1,0:T(8,128)(2,1)S(1)}, f32[256,128]{1,0:T(8,128)S(1)}, bf16[256,320]{1,0:T(8,128)(2,1)S(1...) custom-call(s32[4]{0:T(128)S(1)} %copy-done.3, f32[1,2]{1,0:T(1,128)S(1)} %copy-done.4, ...), custom_call_target="tpu_custom_call" | custom-call | flops 134217728 | bytes 1048576 | tf_op jit(solution)/shard_map/prepare/pallas_call | solution.py:257
  12.4 2.7 %collective-permute-start.7 = (f32[256,128]{1,0:T(8,128)S(1)}, f32[256,128]{1,0:T(8,128)S(1)}, u32[]{:S(2)}, u32[]{:S(2)}) collective-permute-start(f32[256,128]{1,0:T(8,128)S(1)} %get-tuple-element.26), channel_id=1, source_target_pairs={{0,24},{8,16},{16,8},{24,0},{1,25},{9,17},{17,9},{25,1},{2,26},{10... | collective-permute-start | bytes 393224 | tf_op jit(solution)/shard_map/ppermute | solution.py:197
  15.1 0.5 %collective-permute-start.6 = (f32[256,128]{1,0:T(8,128)S(1)}, f32[256,128]{1,0:T(8,128)S(1)}, u32[]{:S(2)}, u32[]{:S(2)}) collective-permute-start(f32[256,128]{1,0:T(8,128)S(1)} %get-tuple-element.26), channel_id=1, source_target_pairs={{0,16},{8,24},{16,0},{24,8},{1,17},{9,25},{17,1},{25,9},{2,18},{10... | collective-permute-start | bytes 393224 | tf_op jit(solution)/shard_map/ppermute | solution.py:197
  15.6 0.0 collective-permute-done.3.refs_3_
  15.6 0.4 collective-permute-start.5
  16.0 6.5 %collective-permute-done.2.refs_2_ = bf16[640,128]{1,0:T(8,128)(2,1)S(1)} collective-permute-done((bf16[640,128]{1,0:T(8,128)(2,1)}, bf16[640,128]{1,0:T(8,128)(2,1)S(1)}, u32[]{:S(2)}, u32[]{:S(2)}) %collective-permute-start.2) | collective-permute-done | bytes 163872 | tf_op jit(solution)/shard_map/ppermute | solution.py:197
  22.5 0.0 collective-permute-done.1.refs_1_
  22.5 2.0 %compute.1 = (f32[160,256]{1,0:T(8,128)S(1)}, f32[160,256]{1,0:T(8,128)S(1)}, f32[160,128]{1,0:T(8,128)S(1)}, f32[160,128]{1,0:T(8,128)S(1)}) custom-call(s32[4]{0:T(128)S(1)} %copy-done.3, f32[1,2]{1,0:T(1,128)S(1)} %copy-done.4, s32[2]{0:T(128)S(1)} %pad_add_fusion.place_ref, bf16[2,256,512]{2,1,0:T(8,128)(2,1)S(1)} %get-tuple-element.20.straight_ref, ...), custom_call_target="tpu_custom_call" | custom-call | tf_op jit(solution)/shard_map/compute/pallas_call | solution.py:283
  24.5 0.1 collective-permute-start.4
  24.5 1.3 %collective-permute-done.4 = f32[160,128]{1,0:T(8,128)S(1)} collective-permute-done((f32[160,128]{1,0:T(8,128)S(1)}, f32[160,128]{1,0:T(8,128)S(1)}, u32[]{:S(2)}, u32[]{:S(2)}) %collective-permute-start.4) | collective-permute-done | bytes 81952 | tf_op jit(solution)/shard_map/ppermute | solution.py:197
  25.8 0.0 collective-permute-done.7
  25.8 0.0 collective-permute-done.6
  25.8 0.0 collective-permute-done.5
  25.9 0.2 collective-permute-start.8
  26.1 2.5 %collective-permute-start.13 = (f32[160,128]{1,0:T(8,128)S(1)}, f32[160,128]{1,0:T(8,128)S(1)}, u32[]{:S(2)}, u32[]{:S(2)}) collective-permute-start(f32[160,128]{1,0:T(8,128)S(1)} %add.39), channel_id=1, source_target_pairs={{0,6},{2,4},{4,2},{6,0},{1,7},{3,5},{5,3},{7,1},{8,14},{10,12},{12... | collective-permute-start | bytes 245768 | tf_op jit(solution)/shard_map/ppermute | solution.py:197
  28.6 0.0 collective-permute-done.8
  28.6 2.5 %collective-permute-start.11 = (f32[160,256]{1,0:T(8,128)S(1)}, f32[160,256]{1,0:T(8,128)S(1)}, u32[]{:S(2)}, u32[]{:S(2)}) collective-permute-start(f32[160,256]{1,0:T(8,128)S(1)} %add.43), channel_id=1, source_target_pairs={{0,24},{8,16},{16,8},{24,0},{1,25},{9,17},{17,9},{25,1},{2,26},{10... | collective-permute-start | bytes 491528 | tf_op jit(solution)/shard_map/ppermute | solution.py:197
  31.1 0.5 %collective-permute-start.10 = (f32[160,256]{1,0:T(8,128)S(1)}, f32[160,256]{1,0:T(8,128)S(1)}, u32[]{:S(2)}, u32[]{:S(2)}) collective-permute-start(f32[160,256]{1,0:T(8,128)S(1)} %add.43), channel_id=1, source_target_pairs={{0,16},{8,24},{16,0},{24,8},{1,17},{9,25},{17,1},{25,9},{2,18},{10... | collective-permute-start | bytes 491528 | tf_op jit(solution)/shard_map/ppermute | solution.py:197
  31.6 0.5 %collective-permute-start.9 = (f32[160,256]{1,0:T(8,128)S(1)}, f32[160,256]{1,0:T(8,128)S(1)}, u32[]{:S(2)}, u32[]{:S(2)}) collective-permute-start(f32[160,256]{1,0:T(8,128)S(1)} %add.43), channel_id=1, source_target_pairs={{0,8},{8,0},{16,24},{24,16},{1,9},{9,1},{17,25},{25,17},{2,10},{10... | collective-permute-start | bytes 491528 | tf_op jit(solution)/shard_map/ppermute | solution.py:197
  32.2 0.4 collective-permute-done.13
  32.6 0.1 collective-permute-start.14
  32.7 0.1 collective-permute-start.19
  32.8 4.3 %collective-permute-done.14 = f32[160,128]{1,0:T(8,128)S(1)} collective-permute-done((f32[160,128]{1,0:T(8,128)S(1)}, f32[160,128]{1,0:T(8,128)S(1)}, u32[]{:S(2)}, u32[]{:S(2)}) %collective-permute-start.14) | collective-permute-done | bytes 81952 | tf_op jit(solution)/shard_map/ppermute | solution.py:197
  37.1 2.5 %collective-permute-start.17 = (f32[160,128]{1,0:T(8,128)S(1)}, f32[160,128]{1,0:T(8,128)S(1)}, u32[]{:S(2)}, u32[]{:S(2)}) collective-permute-start(f32[160,128]{1,0:T(8,128)S(1)} %add.48), channel_id=1, source_target_pairs={{0,24},{8,16},{16,8},{24,0},{1,25},{9,17},{17,9},{25,1},{2,26},{10... | collective-permute-start | bytes 245768 | tf_op jit(solution)/shard_map/ppermute | solution.py:197
  39.7 0.0 collective-permute-done.11
  39.7 0.5 %collective-permute-start.16 = (f32[160,128]{1,0:T(8,128)S(1)}, f32[160,128]{1,0:T(8,128)S(1)}, u32[]{:S(2)}, u32[]{:S(2)}) collective-permute-start(f32[160,128]{1,0:T(8,128)S(1)} %add.48), channel_id=1, source_target_pairs={{0,16},{8,24},{16,0},{24,8},{1,17},{9,25},{17,1},{25,9},{2,18},{10... | collective-permute-start | bytes 245768 | tf_op jit(solution)/shard_map/ppermute | solution.py:197
  40.2 0.0 collective-permute-done.10
  40.2 0.6 %collective-permute-start.15 = (f32[160,128]{1,0:T(8,128)S(1)}, f32[160,128]{1,0:T(8,128)S(1)}, u32[]{:S(2)}, u32[]{:S(2)}) collective-permute-start(f32[160,128]{1,0:T(8,128)S(1)} %add.48), channel_id=1, source_target_pairs={{0,8},{8,0},{16,24},{24,16},{1,9},{9,1},{17,25},{25,17},{2,10},{10... | collective-permute-start | bytes 245768 | tf_op jit(solution)/shard_map/ppermute | solution.py:197
  40.8 0.0 collective-permute-done.9
  40.8 0.1 collective-permute-start.12
  40.9 1.7 %collective-permute-done.17 = f32[160,128]{1,0:T(8,128)S(1)} collective-permute-done((f32[160,128]{1,0:T(8,128)S(1)}, f32[160,128]{1,0:T(8,128)S(1)}, u32[]{:S(2)}, u32[]{:S(2)}) %collective-permute-start.17) | collective-permute-done | bytes 81952 | tf_op jit(solution)/shard_map/ppermute | solution.py:197
  42.6 1.6 %collective-permute-done.16 = f32[160,128]{1,0:T(8,128)S(1)} collective-permute-done((f32[160,128]{1,0:T(8,128)S(1)}, f32[160,128]{1,0:T(8,128)S(1)}, u32[]{:S(2)}, u32[]{:S(2)}) %collective-permute-start.16) | collective-permute-done | bytes 81952 | tf_op jit(solution)/shard_map/ppermute | solution.py:197
  44.1 0.5 %collective-permute-done.15 = f32[160,128]{1,0:T(8,128)S(1)} collective-permute-done((f32[160,128]{1,0:T(8,128)S(1)}, f32[160,128]{1,0:T(8,128)S(1)}, u32[]{:S(2)}, u32[]{:S(2)}) %collective-permute-start.15) | collective-permute-done | bytes 81952 | tf_op jit(solution)/shard_map/ppermute | solution.py:197
  44.6 0.1 collective-permute-start.18
  44.7 0.0 collective-permute-done.19.other_term_ref
  44.7 1.3 %collective-permute-done.18.other_t_ref = f32[160,128]{1,0:T(8,128)S(1)} collective-permute-done((f32[160,128]{1,0:T(8,128)S(1)}, f32[160,128]{1,0:T(8,128)S(1)}, u32[]{:S(2)}, u32[]{:S(2)}) %collective-permute-start.18) | collective-permute-done | bytes 81952 | tf_op jit(solution)/shard_map/ppermute | solution.py:197
  46.0 0.0 collective-permute-done.12.other_d_ref
  46.0 1.2 %expand.1 = (f32[256,256]{1,0:T(8,128)}, f32[512,128]{1,0:T(8,128)}) custom-call(bf16[256,320]{1,0:T(8,128)(2,1)S(1)} %get-tuple-element.16.pick_d_ref, bf16[512,320]{1,0:T(8,128)(2,1)S(1)} %get-tuple-element.17.pick_t_ref, f32[512,128]{1,0:T(8,128)S(1)} %get-tuple-element.18.keep_ref, f32[8,128]{1,0:T(8,128)S(1)} %get-tuple-element.19.upper_ref, ...), custom_call_target="tpu_custom_call" | custom-call | tf_op jit(solution)/shard_map/expand/pallas_call | solution.py:313
  (7 shorter events, 0.2 us)
Async XLA Ops:
  0.6 7.8 %copy-start.2 = (bf16[1,2,512,128]{3,2,1,0:T(8,128)(2,1)S(1)}, bf16[1,2,512,128]{3,2,1,0:T(8,128)(2,1)}, u32[]{:S(2)}) copy-start(bf16[1,2,512,128]{3,2,1,0:T(8,128)(2,1)} %param.10) | copy-start | bytes 786436
  2.6 5.8 %collective-permute-start = (bf16[640,128]{1,0:T(8,128)(2,1)}, bf16[640,128]{1,0:T(8,128)(2,1)S(1)}, u32[]{:S(2)}, u32[]{:S(2)}) collective-permute-start(bf16[640,128]{1,0:T(8,128)(2,1)} %pack.1.refs_0_), channel_id=1, source_target_pairs={{0,1},{1,0},{2,3},{3,2},{4,5},{5,4},{6,7},{7,6},{8,9},{9,8},{10,11... | collective-permute-start | bytes 491528 | tf_op jit(solution)/shard_map/ppermute | solution.py:197
  3.1 12.5 %collective-permute-start.3 = (bf16[640,128]{1,0:T(8,128)(2,1)}, bf16[640,128]{1,0:T(8,128)(2,1)S(1)}, u32[]{:S(2)}, u32[]{:S(2)}) collective-permute-start(bf16[640,128]{1,0:T(8,128)(2,1)} %pack.1.refs_0_), channel_id=1, source_target_pairs={{0,6},{2,4},{4,2},{6,0},{1,7},{3,5},{5,3},{7,1},{8,14},{10,12},{12... | collective-permute-start | bytes 491528 | tf_op jit(solution)/shard_map/ppermute | solution.py:197
  7.7 14.8 %collective-permute-start.2 = (bf16[640,128]{1,0:T(8,128)(2,1)}, bf16[640,128]{1,0:T(8,128)(2,1)S(1)}, u32[]{:S(2)}, u32[]{:S(2)}) collective-permute-start(bf16[640,128]{1,0:T(8,128)(2,1)} %pack.1.refs_0_), channel_id=1, source_target_pairs={{0,4},{2,6},{4,0},{6,2},{1,5},{3,7},{5,1},{7,3},{8,12},{10,14},{12... | collective-permute-start | bytes 491528 | tf_op jit(solution)/shard_map/ppermute | solution.py:197
  7.7 14.8 %collective-permute-start.1 = (bf16[640,128]{1,0:T(8,128)(2,1)}, bf16[640,128]{1,0:T(8,128)(2,1)S(1)}, u32[]{:S(2)}, u32[]{:S(2)}) collective-permute-start(bf16[640,128]{1,0:T(8,128)(2,1)} %pack.1.refs_0_), channel_id=1, source_target_pairs={{0,2},{2,0},{4,6},{6,4},{1,3},{3,1},{5,7},{7,5},{8,10},{10,8},{12,... | collective-permute-start | bytes 491528 | tf_op jit(solution)/shard_map/ppermute | solution.py:197
  8.4 0.7 %copy-start.3 = (s32[4]{0:T(128)S(1)}, s32[4]{0:T(128)}, u32[]{:S(2)}) copy-start(s32[4]{0:T(128)} %widths_ref.5) | copy-start | bytes 52
  8.4 0.7 %copy-start.4 = (f32[1,2]{1,0:T(1,128)S(1)}, f32[1,2]{1,0:T(1,128)}, u32[]{:S(2)}) copy-start(f32[1,2]{1,0:T(1,128)} %weights_ref.3) | copy-start | bytes 28
  9.1 0.9 %copy-start = (bf16[640,128]{1,0:T(8,128)(2,1)S(1)}, bf16[640,128]{1,0:T(8,128)(2,1)}, u32[]{:S(2)}) copy-start(bf16[640,128]{1,0:T(8,128)(2,1)} %pack.1.refs_0_) | copy-start | bytes 491524
  10.0 1.0 %copy-start.1 = (bf16[1,2,256,4,1,128]{5,3,4,2,1,0:T(4,128)(2,1)S(1)}, bf16[1,2,256,4,1,128]{5,3,4,2,1,0:T(4,128)(2,1)}, u32[]{:S(2)}) copy-start(bf16[1,2,256,4,1,128]{5,3,4,2,1,0:T(4,128)(2,1)} %param.6) | copy-start | bytes 1572868
  12.4 13.4 %collective-permute-start.7 = (f32[256,128]{1,0:T(8,128)S(1)}, f32[256,128]{1,0:T(8,128)S(1)}, u32[]{:S(2)}, u32[]{:S(2)}) collective-permute-start(f32[256,128]{1,0:T(8,128)S(1)} %get-tuple-element.26), channel_id=1, source_target_pairs={{0,24},{8,16},{16,8},{24,0},{1,25},{9,17},{17,9},{25,1},{2,26},{10... | collective-permute-start | bytes 393224 | tf_op jit(solution)/shard_map/ppermute | solution.py:197
  15.1 10.8 %collective-permute-start.6 = (f32[256,128]{1,0:T(8,128)S(1)}, f32[256,128]{1,0:T(8,128)S(1)}, u32[]{:S(2)}, u32[]{:S(2)}) collective-permute-start(f32[256,128]{1,0:T(8,128)S(1)} %get-tuple-element.26), channel_id=1, source_target_pairs={{0,16},{8,24},{16,0},{24,8},{1,17},{9,25},{17,1},{25,9},{2,18},{10... | collective-permute-start | bytes 393224 | tf_op jit(solution)/shard_map/ppermute | solution.py:197
  15.6 10.3 %collective-permute-start.5 = (f32[256,128]{1,0:T(8,128)S(1)}, f32[256,128]{1,0:T(8,128)S(1)}, u32[]{:S(2)}, u32[]{:S(2)}) collective-permute-start(f32[256,128]{1,0:T(8,128)S(1)} %get-tuple-element.26), channel_id=1, source_target_pairs={{0,8},{8,0},{16,24},{24,16},{1,9},{9,1},{17,25},{25,17},{2,10},{10... | collective-permute-start | bytes 393224 | tf_op jit(solution)/shard_map/ppermute | solution.py:197
  24.5 1.3 %collective-permute-start.4 = (f32[160,128]{1,0:T(8,128)S(1)}, f32[160,128]{1,0:T(8,128)S(1)}, u32[]{:S(2)}, u32[]{:S(2)}) collective-permute-start(f32[160,128]{1,0:T(8,128)S(1)} %get-tuple-element.24), channel_id=1, source_target_pairs={{0,1},{1,0},{2,3},{3,2},{4,5},{5,4},{6,7},{7,6},{8,9},{9,8},{10,11... | collective-permute-start | bytes 245768 | tf_op jit(solution)/shard_map/ppermute | solution.py:197
  25.9 2.7 %collective-permute-start.8 = (f32[160,256]{1,0:T(8,128)S(1)}, f32[160,256]{1,0:T(8,128)S(1)}, u32[]{:S(2)}, u32[]{:S(2)}) collective-permute-start(f32[160,256]{1,0:T(8,128)S(1)} %get-tuple-element.27), channel_id=1, source_target_pairs={{0,1},{1,0},{2,3},{3,2},{4,5},{5,4},{6,7},{7,6},{8,9},{9,8},{10,11... | collective-permute-start | bytes 491528 | tf_op jit(solution)/shard_map/ppermute | solution.py:197
  26.1 6.5 %collective-permute-start.13 = (f32[160,128]{1,0:T(8,128)S(1)}, f32[160,128]{1,0:T(8,128)S(1)}, u32[]{:S(2)}, u32[]{:S(2)}) collective-permute-start(f32[160,128]{1,0:T(8,128)S(1)} %add.39), channel_id=1, source_target_pairs={{0,6},{2,4},{4,2},{6,0},{1,7},{3,5},{5,3},{7,1},{8,14},{10,12},{12... | collective-permute-start | bytes 245768 | tf_op jit(solution)/shard_map/ppermute | solution.py:197
  28.6 11.0 %collective-permute-start.11 = (f32[160,256]{1,0:T(8,128)S(1)}, f32[160,256]{1,0:T(8,128)S(1)}, u32[]{:S(2)}, u32[]{:S(2)}) collective-permute-start(f32[160,256]{1,0:T(8,128)S(1)} %add.43), channel_id=1, source_target_pairs={{0,24},{8,16},{16,8},{24,0},{1,25},{9,17},{17,9},{25,1},{2,26},{10... | collective-permute-start | bytes 491528 | tf_op jit(solution)/shard_map/ppermute | solution.py:197
  31.1 9.0 %collective-permute-start.10 = (f32[160,256]{1,0:T(8,128)S(1)}, f32[160,256]{1,0:T(8,128)S(1)}, u32[]{:S(2)}, u32[]{:S(2)}) collective-permute-start(f32[160,256]{1,0:T(8,128)S(1)} %add.43), channel_id=1, source_target_pairs={{0,16},{8,24},{16,0},{24,8},{1,17},{9,25},{17,1},{25,9},{2,18},{10... | collective-permute-start | bytes 491528 | tf_op jit(solution)/shard_map/ppermute | solution.py:197
  31.6 9.1 %collective-permute-start.9 = (f32[160,256]{1,0:T(8,128)S(1)}, f32[160,256]{1,0:T(8,128)S(1)}, u32[]{:S(2)}, u32[]{:S(2)}) collective-permute-start(f32[160,256]{1,0:T(8,128)S(1)} %add.43), channel_id=1, source_target_pairs={{0,8},{8,0},{16,24},{24,16},{1,9},{9,1},{17,25},{25,17},{2,10},{10... | collective-permute-start | bytes 491528 | tf_op jit(solution)/shard_map/ppermute | solution.py:197
  32.6 4.5 %collective-permute-start.14 = (f32[160,128]{1,0:T(8,128)S(1)}, f32[160,128]{1,0:T(8,128)S(1)}, u32[]{:S(2)}, u32[]{:S(2)}) collective-permute-start(f32[160,128]{1,0:T(8,128)S(1)} %add.47), channel_id=1, source_target_pairs={{0,2},{2,0},{4,6},{6,4},{1,3},{3,1},{5,7},{7,5},{8,10},{10,8},{12,... | collective-permute-start | bytes 245768 | tf_op jit(solution)/shard_map/ppermute | solution.py:197
  32.7 12.0 %collective-permute-start.19 = (f32[256,128]{1,0:T(8,128)S(1)}, f32[256,128]{1,0:T(8,128)S(1)}, u32[]{:S(2)}, u32[]{:S(2)}) collective-permute-start(f32[256,128]{1,0:T(8,128)S(1)} %add_add_fusion.1.mine_term_ref), channel_id=1, source_target_pairs={{0,1},{1,0},{2,3},{3,2},{4,5},{5,4},{6,7},{7,6},{8,9},{9,8},{10,11... | collective-permute-start | bytes 393224 | tf_op jit(solution)/shard_map/ppermute | solution.py:197
  37.1 5.4 %collective-permute-start.17 = (f32[160,128]{1,0:T(8,128)S(1)}, f32[160,128]{1,0:T(8,128)S(1)}, u32[]{:S(2)}, u32[]{:S(2)}) collective-permute-start(f32[160,128]{1,0:T(8,128)S(1)} %add.48), channel_id=1, source_target_pairs={{0,24},{8,16},{16,8},{24,0},{1,25},{9,17},{17,9},{25,1},{2,26},{10... | collective-permute-start | bytes 245768 | tf_op jit(solution)/shard_map/ppermute | solution.py:197
  39.7 4.4 %collective-permute-start.16 = (f32[160,128]{1,0:T(8,128)S(1)}, f32[160,128]{1,0:T(8,128)S(1)}, u32[]{:S(2)}, u32[]{:S(2)}) collective-permute-start(f32[160,128]{1,0:T(8,128)S(1)} %add.48), channel_id=1, source_target_pairs={{0,16},{8,24},{16,0},{24,8},{1,17},{9,25},{17,1},{25,9},{2,18},{10... | collective-permute-start | bytes 245768 | tf_op jit(solution)/shard_map/ppermute | solution.py:197
  40.2 4.4 %collective-permute-start.15 = (f32[160,128]{1,0:T(8,128)S(1)}, f32[160,128]{1,0:T(8,128)S(1)}, u32[]{:S(2)}, u32[]{:S(2)}) collective-permute-start(f32[160,128]{1,0:T(8,128)S(1)} %add.48), channel_id=1, source_target_pairs={{0,8},{8,0},{16,24},{24,16},{1,9},{9,1},{17,25},{25,17},{2,10},{10... | collective-permute-start | bytes 245768 | tf_op jit(solution)/shard_map/ppermute | solution.py:197
  40.8 5.2 %collective-permute-start.12 = (f32[160,256]{1,0:T(8,128)S(1)}, f32[160,256]{1,0:T(8,128)S(1)}, u32[]{:S(2)}, u32[]{:S(2)}) collective-permute-start(f32[160,256]{1,0:T(8,128)S(1)} %add_add_fusion.mine_d_ref), channel_id=1, source_target_pairs={{0,1},{1,0},{2,3},{3,2},{4,5},{5,4},{6,7},{7,6},{8,9},{9,8},{10,11... | collective-permute-start | bytes 491528 | tf_op jit(solution)/shard_map/ppermute | solution.py:197
  44.6 1.3 %collective-permute-start.18 = (f32[160,128]{1,0:T(8,128)S(1)}, f32[160,128]{1,0:T(8,128)S(1)}, u32[]{:S(2)}, u32[]{:S(2)}) collective-permute-start(f32[160,128]{1,0:T(8,128)S(1)} %add_add_fusion.2.mine_t_ref), channel_id=1, source_target_pairs={{0,1},{1,0},{2,3},{3,2},{4,5},{5,4},{6,7},{7,6},{8,9},{9,8},{10,11... | collective-permute-start | bytes 245768 | tf_op jit(solution)/shard_map/ppermute | solution.py:197

commit v16 on v15

--- a/solution.py
+++ b/solution.py
@@ -36,10 +36,12 @@
     place = jnp.concatenate(place, axis=1)
     target = lax.broadcasted_iota(jnp.int32, (packed_width, supernodes * slot), 0)
     select = jnp.where(target == place, 1.0, 0.0).astype(BF16)
+    block = packed_ref.shape[1]
+    both = rows_by_rows(select, panel_ref[...]).astype(BF16)
     for part in range(2):
-        packed_ref[part * packed_width:(part + 1) * packed_width, :] = rows_by_rows(
-            select, panel_ref[part]
-        ).astype(BF16)
+        packed_ref[part * packed_width:(part + 1) * packed_width, :] = both[
+            :, part * block:(part + 1) * block
+        ]
 
 
 def prepare_kernel(
@@ -247,7 +249,7 @@
         out_specs=VMEM_SPEC,
         out_shape=jax.ShapeDtypeStruct((2 * packed_width, block), BF16),
         name="pack",
-    )(block_pattern, sup_widths, l_panel[0])
+    )(block_pattern, sup_widths, l_panel[0].reshape(2 * block, total_cols))
 
     blocks = {0: packed}
     for other in range(1, row_count):
@@ -302,8 +304,8 @@
     products, send_d, term = tie((keep_t + swap(send_t, "col", top), send_d, term))
     term = gather_but_last(term, "col")
     products = scatter_rest(products, "col")
-    for bit in bits_of(row_count)[::-1]:
-        products = products + swap(products, "row", 2 * bit - 1)
+    for bit in bits_of(row_count):
+        products = products + swap(products, "row", bit)
     density = scatter_rest(keep_d + swap(send_d, "col", top), "col")
     density = sum_direct(density, "pole")
     products = sum_direct(products, "pole")

time: 47.4 us -> 47.7 us (level)
  waiting for transfers between devices: 17.6 us -> 18.7 us
  starting transfers between devices: 19.4 us -> 18.7 us
    ppermute x20, waiting for transfers between devices: 17.6 us -> 18.7 us  [swap(): lax.ppermute(value, axis, [(i, i ^ bit) for i in range(lax.axis_size(axis...]
    ppermute x20, starting transfers between devices: 19.4 us -> 18.7 us  [swap(): lax.ppermute(value, axis, [(i, i ^ bit) for i in range(lax.axis_size(axis...]
where the time goes in v16:
time: 47.7 us; the launch traced here: 47.5 us
  starting transfers between devices  18.7 us (39%)
  waiting for transfers between devices  18.7 us (39%)
  Pallas kernels  6.56 us (14%)
  local copies, waits for them, and re-layouts  2.63 us (6%)
  between operations  0.76 us (2%)
    ppermute x20, waiting for transfers between devices, swap(): lax.ppermute(value, axis, [(i, i ^ bit) for i in range(lax.axis_size(axis...  18.7 us
    ppermute x20, starting transfers between devices, swap(): lax.ppermute(value, axis, [(i, i ^ bit) for i in range(lax.axis_size(axis...  18.7 us
    unnamed x10, local copies, waits for them, and re-layouts  2.63 us
    pallas_call x1, Pallas kernels, per_device(): pl.pallas_call(functools.partial(compute_kernel, col_count, supernodes, s...  1.99 us
    pallas_call x1, Pallas kernels, per_device(): pl.pallas_call(functools.partial(pack_kernel, supernodes, slot), in_specs...  1.95 us
    pallas_call x1, Pallas kernels, per_device(): pl.pallas_call(functools.partial(prepare_kernel, (row_count, col_count)),...  1.38 us
    pallas_call x1, Pallas kernels, per_device(): pl.pallas_call(expand_kernel, in_specs=[VMEM_SPEC] * 10, out_specs=[VMEM_...  1.24 us
  transfers between devices with their start and end apart: 20, of which 8 were waited for; matrix products, arithmetic and copies ran while one was open for 0% of the time, Pallas kernels for 7%

profile of v16, /device:TPU:0, one launch (start us, length us, event | category | flops | bytes accessed | tf_op | source)
XLA Modules:
  0.0 47.5 jit_solution(3024950863022899422)
XLA Ops:
  0.6 0.0 copy-start.2
  0.6 1.9 %pack.1.refs_0_ = bf16[640,128]{1,0:T(8,128)(2,1)} custom-call(s32[1,4]{1,0:T(1,128)} %pattern_ref.1, s32[4]{0:T(128)} %widths_ref.5, bf16[256,512]{1,0:T(8,128)(2,1)} %bitcast.7), custom_call_target="tpu_custom_call" | custom-call | tf_op jit(solution)/shard_map/pack/pallas_call | solution.py:246
  2.6 0.5 collective-permute-start
  3.1 4.6 %collective-permute-start.3 = (bf16[640,128]{1,0:T(8,128)(2,1)}, bf16[640,128]{1,0:T(8,128)(2,1)S(1)}, u32[]{:S(2)}, u32[]{:S(2)}) collective-permute-start(bf16[640,128]{1,0:T(8,128)(2,1)} %pack.1.refs_0_), channel_id=1, source_target_pairs={{0,6},{2,4},{4,2},{6,0},{1,7},{3,5},{5,3},{7,1},{8,14},{10,12},{12... | collective-permute-start | bytes 491528 | tf_op jit(solution)/shard_map/ppermute | solution.py:199
  7.6 0.0 collective-permute-start.2
  7.6 0.6 %collective-permute-start.1 = (bf16[640,128]{1,0:T(8,128)(2,1)}, bf16[640,128]{1,0:T(8,128)(2,1)S(1)}, u32[]{:S(2)}, u32[]{:S(2)}) collective-permute-start(bf16[640,128]{1,0:T(8,128)(2,1)} %pack.1.refs_0_), channel_id=1, source_target_pairs={{0,2},{2,0},{4,6},{6,4},{1,3},{3,1},{5,7},{7,5},{8,10},{10,8},{12,... | collective-permute-start | bytes 491528 | tf_op jit(solution)/shard_map/ppermute | solution.py:199
  8.3 0.1 pad_add_fusion.place_ref
  8.3 0.0 collective-permute-done.refs_1_
  8.4 0.0 copy-start.3
  8.4 0.0 copy-start.4
  8.4 0.0 copy-done.2
  8.4 0.6 %copy-done.3 = s32[4]{0:T(128)S(1)} copy-done((s32[4]{0:T(128)S(1)}, s32[4]{0:T(128)}, u32[]{:S(2)}) %copy-start.3) | copy-done | bytes 40
  9.0 0.0 copy-done.4
  9.0 0.0 copy-start
  9.0 0.9 %copy-done = bf16[640,128]{1,0:T(8,128)(2,1)S(1)} copy-done((bf16[640,128]{1,0:T(8,128)(2,1)S(1)}, bf16[640,128]{1,0:T(8,128)(2,1)}, u32[]{:S(2)}) %copy-start) | copy-done | bytes 163864
  9.9 0.0 copy-start.1
  9.9 1.0 %copy-done.1 = bf16[1,2,256,4,1,128]{5,3,4,2,1,0:T(4,128)(2,1)S(1)} copy-done((bf16[1,2,256,4,1,128]{5,3,4,2,1,0:T(4,128)(2,1)S(1)}, bf16[1,2,256,4,1,128]{5,3,4,2,1,0:T(4,128)(2,1)}, u32[]{:S(2)}) %copy-start.1) | copy-done | bytes 524312
  11.0 1.4 %prepare.1 = (bf16[2,256,512]{2,1,0:T(8,128)(2,1)S(1)}, bf16[512,512]{1,0:T(8,128)(2,1)S(1)}, f32[256,128]{1,0:T(8,128)S(1)}, bf16[256,320]{1,0:T(8,128)(2,1)S(1...) custom-call(s32[4]{0:T(128)S(1)} %copy-done.3, f32[1,2]{1,0:T(1,128)S(1)} %copy-done.4, ...), custom_call_target="tpu_custom_call" | custom-call | flops 134217728 | bytes 1048576 | tf_op jit(solution)/shard_map/prepare/pallas_call | solution.py:259
  12.4 2.7 %collective-permute-start.7 = (f32[256,128]{1,0:T(8,128)S(1)}, f32[256,128]{1,0:T(8,128)S(1)}, u32[]{:S(2)}, u32[]{:S(2)}) collective-permute-start(f32[256,128]{1,0:T(8,128)S(1)} %get-tuple-element.26), channel_id=1, source_target_pairs={{0,24},{8,16},{16,8},{24,0},{1,25},{9,17},{17,9},{25,1},{2,26},{10... | collective-permute-start | bytes 393224 | tf_op jit(solution)/shard_map/ppermute | solution.py:199
  15.0 0.5 %collective-permute-start.6 = (f32[256,128]{1,0:T(8,128)S(1)}, f32[256,128]{1,0:T(8,128)S(1)}, u32[]{:S(2)}, u32[]{:S(2)}) collective-permute-start(f32[256,128]{1,0:T(8,128)S(1)} %get-tuple-element.26), channel_id=1, source_target_pairs={{0,16},{8,24},{16,0},{24,8},{1,17},{9,25},{17,1},{25,9},{2,18},{10... | collective-permute-start | bytes 393224 | tf_op jit(solution)/shard_map/ppermute | solution.py:199
  15.5 0.0 collective-permute-done.3.refs_3_
  15.6 0.4 collective-permute-start.5
  15.9 6.5 %collective-permute-done.2.refs_2_ = bf16[640,128]{1,0:T(8,128)(2,1)S(1)} collective-permute-done((bf16[640,128]{1,0:T(8,128)(2,1)}, bf16[640,128]{1,0:T(8,128)(2,1)S(1)}, u32[]{:S(2)}, u32[]{:S(2)}) %collective-permute-start.2) | collective-permute-done | bytes 163872 | tf_op jit(solution)/shard_map/ppermute | solution.py:199
  22.4 0.0 collective-permute-done.1.refs_1_
  22.4 2.0 %compute.1 = (f32[160,256]{1,0:T(8,128)S(1)}, f32[160,256]{1,0:T(8,128)S(1)}, f32[160,128]{1,0:T(8,128)S(1)}, f32[160,128]{1,0:T(8,128)S(1)}) custom-call(s32[4]{0:T(128)S(1)} %copy-done.3, f32[1,2]{1,0:T(1,128)S(1)} %copy-done.4, s32[2]{0:T(128)S(1)} %pad_add_fusion.place_ref, bf16[2,256,512]{2,1,0:T(8,128)(2,1)S(1)} %get-tuple-element.20.straight_ref, ...), custom_call_target="tpu_custom_call" | custom-call | tf_op jit(solution)/shard_map/compute/pallas_call | solution.py:285
  24.4 0.1 collective-permute-start.4
  24.5 1.3 %collective-permute-done.4 = f32[160,128]{1,0:T(8,128)S(1)} collective-permute-done((f32[160,128]{1,0:T(8,128)S(1)}, f32[160,128]{1,0:T(8,128)S(1)}, u32[]{:S(2)}, u32[]{:S(2)}) %collective-permute-start.4) | collective-permute-done | bytes 81952 | tf_op jit(solution)/shard_map/ppermute | solution.py:199
  25.8 0.0 collective-permute-done.7
  25.8 0.0 collective-permute-done.6
  25.8 0.0 collective-permute-done.5
  25.8 0.2 collective-permute-start.8
  26.1 0.0 collective-permute-start.13
  26.1 1.2 %collective-permute-done.8 = f32[160,256]{1,0:T(8,128)S(1)} collective-permute-done((f32[160,256]{1,0:T(8,128)S(1)}, f32[160,256]{1,0:T(8,128)S(1)}, u32[]{:S(2)}, u32[]{:S(2)}) %collective-permute-start.8) | collective-permute-done | bytes 163872 | tf_op jit(solution)/shard_map/ppermute | solution.py:199
  27.3 2.5 %collective-permute-start.11 = (f32[160,256]{1,0:T(8,128)S(1)}, f32[160,256]{1,0:T(8,128)S(1)}, u32[]{:S(2)}, u32[]{:S(2)}) collective-permute-start(f32[160,256]{1,0:T(8,128)S(1)} %add.43), channel_id=1, source_target_pairs={{0,24},{8,16},{16,8},{24,0},{1,25},{9,17},{17,9},{25,1},{2,26},{10... | collective-permute-start | bytes 491528 | tf_op jit(solution)/shard_map/ppermute | solution.py:199
  29.8 0.5 %collective-permute-start.10 = (f32[160,256]{1,0:T(8,128)S(1)}, f32[160,256]{1,0:T(8,128)S(1)}, u32[]{:S(2)}, u32[]{:S(2)}) collective-permute-start(f32[160,256]{1,0:T(8,128)S(1)} %add.43), channel_id=1, source_target_pairs={{0,16},{8,24},{16,0},{24,8},{1,17},{9,25},{17,1},{25,9},{2,18},{10... | collective-permute-start | bytes 491528 | tf_op jit(solution)/shard_map/ppermute | solution.py:199
  30.3 0.5 %collective-permute-start.9 = (f32[160,256]{1,0:T(8,128)S(1)}, f32[160,256]{1,0:T(8,128)S(1)}, u32[]{:S(2)}, u32[]{:S(2)}) collective-permute-start(f32[160,256]{1,0:T(8,128)S(1)} %add.43), channel_id=1, source_target_pairs={{0,8},{8,0},{16,24},{24,16},{1,9},{9,1},{17,25},{25,17},{2,10},{10... | collective-permute-start | bytes 491528 | tf_op jit(solution)/shard_map/ppermute | solution.py:199
  30.9 0.0 collective-permute-done.13
  30.9 1.9 %collective-permute-start.14 = (f32[160,128]{1,0:T(8,128)S(1)}, f32[160,128]{1,0:T(8,128)S(1)}, u32[]{:S(2)}, u32[]{:S(2)}) collective-permute-start(f32[160,128]{1,0:T(8,128)S(1)} %add.47), channel_id=1, source_target_pairs={{0,4},{2,6},{4,0},{6,2},{1,5},{3,7},{5,1},{7,3},{8,12},{10,14},{12... | collective-permute-start | bytes 245768 | tf_op jit(solution)/shard_map/ppermute | solution.py:199
  32.8 0.0 collective-permute-start.19
  32.8 4.6 %collective-permute-done.14 = f32[160,128]{1,0:T(8,128)S(1)} collective-permute-done((f32[160,128]{1,0:T(8,128)S(1)}, f32[160,128]{1,0:T(8,128)S(1)}, u32[]{:S(2)}, u32[]{:S(2)}) %collective-permute-start.14) | collective-permute-done | bytes 81952 | tf_op jit(solution)/shard_map/ppermute | solution.py:199
  37.4 2.5 %collective-permute-start.17 = (f32[160,128]{1,0:T(8,128)S(1)}, f32[160,128]{1,0:T(8,128)S(1)}, u32[]{:S(2)}, u32[]{:S(2)}) collective-permute-start(f32[160,128]{1,0:T(8,128)S(1)} %add.48), channel_id=1, source_target_pairs={{0,24},{8,16},{16,8},{24,0},{1,25},{9,17},{17,9},{25,1},{2,26},{10... | collective-permute-start | bytes 245768 | tf_op jit(solution)/shard_map/ppermute | solution.py:199
  39.9 0.0 collective-permute-done.11
  39.9 0.5 %collective-permute-start.16 = (f32[160,128]{1,0:T(8,128)S(1)}, f32[160,128]{1,0:T(8,128)S(1)}, u32[]{:S(2)}, u32[]{:S(2)}) collective-permute-start(f32[160,128]{1,0:T(8,128)S(1)} %add.48), channel_id=1, source_target_pairs={{0,16},{8,24},{16,0},{24,8},{1,17},{9,25},{17,1},{25,9},{2,18},{10... | collective-permute-start | bytes 245768 | tf_op jit(solution)/shard_map/ppermute | solution.py:199
  40.4 0.0 collective-permute-done.10
  40.4 0.5 %collective-permute-start.15 = (f32[160,128]{1,0:T(8,128)S(1)}, f32[160,128]{1,0:T(8,128)S(1)}, u32[]{:S(2)}, u32[]{:S(2)}) collective-permute-start(f32[160,128]{1,0:T(8,128)S(1)} %add.48), channel_id=1, source_target_pairs={{0,8},{8,0},{16,24},{24,16},{1,9},{9,1},{17,25},{25,17},{2,10},{10... | collective-permute-start | bytes 245768 | tf_op jit(solution)/shard_map/ppermute | solution.py:199
  41.0 0.0 collective-permute-done.9
  41.0 0.1 collective-permute-start.12
  41.1 1.8 %collective-permute-done.17 = f32[160,128]{1,0:T(8,128)S(1)} collective-permute-done((f32[160,128]{1,0:T(8,128)S(1)}, f32[160,128]{1,0:T(8,128)S(1)}, u32[]{:S(2)}, u32[]{:S(2)}) %collective-permute-start.17) | collective-permute-done | bytes 81952 | tf_op jit(solution)/shard_map/ppermute | solution.py:199
  42.9 1.4 %collective-permute-done.16 = f32[160,128]{1,0:T(8,128)S(1)} collective-permute-done((f32[160,128]{1,0:T(8,128)S(1)}, f32[160,128]{1,0:T(8,128)S(1)}, u32[]{:S(2)}, u32[]{:S(2)}) %collective-permute-start.16) | collective-permute-done | bytes 81952 | tf_op jit(solution)/shard_map/ppermute | solution.py:199
  44.4 0.5 %collective-permute-done.15 = f32[160,128]{1,0:T(8,128)S(1)} collective-permute-done((f32[160,128]{1,0:T(8,128)S(1)}, f32[160,128]{1,0:T(8,128)S(1)}, u32[]{:S(2)}, u32[]{:S(2)}) %collective-permute-start.15) | collective-permute-done | bytes 81952 | tf_op jit(solution)/shard_map/ppermute | solution.py:199
  44.9 0.1 collective-permute-start.18
  45.0 0.0 collective-permute-done.19.other_term_ref
  45.0 1.3 %collective-permute-done.18.other_t_ref = f32[160,128]{1,0:T(8,128)S(1)} collective-permute-done((f32[160,128]{1,0:T(8,128)S(1)}, f32[160,128]{1,0:T(8,128)S(1)}, u32[]{:S(2)}, u32[]{:S(2)}) %collective-permute-start.18) | collective-permute-done | bytes 81952 | tf_op jit(solution)/shard_map/ppermute | solution.py:199
  46.2 0.0 collective-permute-done.12.other_d_ref
  46.2 1.2 %expand.1 = (f32[256,256]{1,0:T(8,128)}, f32[512,128]{1,0:T(8,128)}) custom-call(bf16[256,320]{1,0:T(8,128)(2,1)S(1)} %get-tuple-element.16.pick_d_ref, bf16[512,320]{1,0:T(8,128)(2,1)S(1)} %get-tuple-element.17.pick_t_ref, f32[512,128]{1,0:T(8,128)S(1)} %get-tuple-element.18.keep_ref, f32[8,128]{1,0:T(8,128)S(1)} %get-tuple-element.19.upper_ref, ...), custom_call_target="tpu_custom_call" | custom-call | tf_op jit(solution)/shard_map/expand/pallas_call | solution.py:315
  (7 shorter events, 0.2 us)
Async XLA Ops:
  0.6 7.7 %copy-start.2 = (bf16[1,2,512,128]{3,2,1,0:T(8,128)(2,1)S(1)}, bf16[1,2,512,128]{3,2,1,0:T(8,128)(2,1)}, u32[]{:S(2)}) copy-start(bf16[1,2,512,128]{3,2,1,0:T(8,128)(2,1)} %param.10) | copy-start | bytes 786436
  2.6 5.8 %collective-permute-start = (bf16[640,128]{1,0:T(8,128)(2,1)}, bf16[640,128]{1,0:T(8,128)(2,1)S(1)}, u32[]{:S(2)}, u32[]{:S(2)}) collective-permute-start(bf16[640,128]{1,0:T(8,128)(2,1)} %pack.1.refs_0_), channel_id=1, source_target_pairs={{0,1},{1,0},{2,3},{3,2},{4,5},{5,4},{6,7},{7,6},{8,9},{9,8},{10,11... | collective-permute-start | bytes 491528 | tf_op jit(solution)/shard_map/ppermute | solution.py:199
  3.1 12.5 %collective-permute-start.3 = (bf16[640,128]{1,0:T(8,128)(2,1)}, bf16[640,128]{1,0:T(8,128)(2,1)S(1)}, u32[]{:S(2)}, u32[]{:S(2)}) collective-permute-start(bf16[640,128]{1,0:T(8,128)(2,1)} %pack.1.refs_0_), channel_id=1, source_target_pairs={{0,6},{2,4},{4,2},{6,0},{1,7},{3,5},{5,3},{7,1},{8,14},{10,12},{12... | collective-permute-start | bytes 491528 | tf_op jit(solution)/shard_map/ppermute | solution.py:199
  7.6 14.8 %collective-permute-start.2 = (bf16[640,128]{1,0:T(8,128)(2,1)}, bf16[640,128]{1,0:T(8,128)(2,1)S(1)}, u32[]{:S(2)}, u32[]{:S(2)}) collective-permute-start(bf16[640,128]{1,0:T(8,128)(2,1)} %pack.1.refs_0_), channel_id=1, source_target_pairs={{0,4},{2,6},{4,0},{6,2},{1,5},{3,7},{5,1},{7,3},{8,12},{10,14},{12... | collective-permute-start | bytes 491528 | tf_op jit(solution)/shard_map/ppermute | solution.py:199
  7.6 14.8 %collective-permute-start.1 = (bf16[640,128]{1,0:T(8,128)(2,1)}, bf16[640,128]{1,0:T(8,128)(2,1)S(1)}, u32[]{:S(2)}, u32[]{:S(2)}) collective-permute-start(bf16[640,128]{1,0:T(8,128)(2,1)} %pack.1.refs_0_), channel_id=1, source_target_pairs={{0,2},{2,0},{4,6},{6,4},{1,3},{3,1},{5,7},{7,5},{8,10},{10,8},{12,... | collective-permute-start | bytes 491528 | tf_op jit(solution)/shard_map/ppermute | solution.py:199
  8.4 0.7 %copy-start.3 = (s32[4]{0:T(128)S(1)}, s32[4]{0:T(128)}, u32[]{:S(2)}) copy-start(s32[4]{0:T(128)} %widths_ref.5) | copy-start | bytes 52
  8.4 0.7 %copy-start.4 = (f32[1,2]{1,0:T(1,128)S(1)}, f32[1,2]{1,0:T(1,128)}, u32[]{:S(2)}) copy-start(f32[1,2]{1,0:T(1,128)} %weights_ref.3) | copy-start | bytes 28
  9.0 0.9 %copy-start = (bf16[640,128]{1,0:T(8,128)(2,1)S(1)}, bf16[640,128]{1,0:T(8,128)(2,1)}, u32[]{:S(2)}) copy-start(bf16[640,128]{1,0:T(8,128)(2,1)} %pack.1.refs_0_) | copy-start | bytes 491524
  9.9 1.0 %copy-start.1 = (bf16[1,2,256,4,1,128]{5,3,4,2,1,0:T(4,128)(2,1)S(1)}, bf16[1,2,256,4,1,128]{5,3,4,2,1,0:T(4,128)(2,1)}, u32[]{:S(2)}) copy-start(bf16[1,2,256,4,1,128]{5,3,4,2,1,0:T(4,128)(2,1)} %param.6) | copy-start | bytes 1572868
  12.4 13.4 %collective-permute-start.7 = (f32[256,128]{1,0:T(8,128)S(1)}, f32[256,128]{1,0:T(8,128)S(1)}, u32[]{:S(2)}, u32[]{:S(2)}) collective-permute-start(f32[256,128]{1,0:T(8,128)S(1)} %get-tuple-element.26), channel_id=1, source_target_pairs={{0,24},{8,16},{16,8},{24,0},{1,25},{9,17},{17,9},{25,1},{2,26},{10... | collective-permute-start | bytes 393224 | tf_op jit(solution)/shard_map/ppermute | solution.py:199
  15.0 10.7 %collective-permute-start.6 = (f32[256,128]{1,0:T(8,128)S(1)}, f32[256,128]{1,0:T(8,128)S(1)}, u32[]{:S(2)}, u32[]{:S(2)}) collective-permute-start(f32[256,128]{1,0:T(8,128)S(1)} %get-tuple-element.26), channel_id=1, source_target_pairs={{0,16},{8,24},{16,0},{24,8},{1,17},{9,25},{17,1},{25,9},{2,18},{10... | collective-permute-start | bytes 393224 | tf_op jit(solution)/shard_map/ppermute | solution.py:199
  15.6 10.2 %collective-permute-start.5 = (f32[256,128]{1,0:T(8,128)S(1)}, f32[256,128]{1,0:T(8,128)S(1)}, u32[]{:S(2)}, u32[]{:S(2)}) collective-permute-start(f32[256,128]{1,0:T(8,128)S(1)} %get-tuple-element.26), channel_id=1, source_target_pairs={{0,8},{8,0},{16,24},{24,16},{1,9},{9,1},{17,25},{25,17},{2,10},{10... | collective-permute-start | bytes 393224 | tf_op jit(solution)/shard_map/ppermute | solution.py:199
  24.4 1.3 %collective-permute-start.4 = (f32[160,128]{1,0:T(8,128)S(1)}, f32[160,128]{1,0:T(8,128)S(1)}, u32[]{:S(2)}, u32[]{:S(2)}) collective-permute-start(f32[160,128]{1,0:T(8,128)S(1)} %get-tuple-element.24), channel_id=1, source_target_pairs={{0,1},{1,0},{2,3},{3,2},{4,5},{5,4},{6,7},{7,6},{8,9},{9,8},{10,11... | collective-permute-start | bytes 245768 | tf_op jit(solution)/shard_map/ppermute | solution.py:199
  25.8 1.5 %collective-permute-start.8 = (f32[160,256]{1,0:T(8,128)S(1)}, f32[160,256]{1,0:T(8,128)S(1)}, u32[]{:S(2)}, u32[]{:S(2)}) collective-permute-start(f32[160,256]{1,0:T(8,128)S(1)} %get-tuple-element.27), channel_id=1, source_target_pairs={{0,1},{1,0},{2,3},{3,2},{4,5},{5,4},{6,7},{7,6},{8,9},{9,8},{10,11... | collective-permute-start | bytes 491528 | tf_op jit(solution)/shard_map/ppermute | solution.py:199
  26.1 4.8 %collective-permute-start.13 = (f32[160,128]{1,0:T(8,128)S(1)}, f32[160,128]{1,0:T(8,128)S(1)}, u32[]{:S(2)}, u32[]{:S(2)}) collective-permute-start(f32[160,128]{1,0:T(8,128)S(1)} %add.39), channel_id=1, source_target_pairs={{0,2},{2,0},{4,6},{6,4},{1,3},{3,1},{5,7},{7,5},{8,10},{10,8},{12,... | collective-permute-start | bytes 245768 | tf_op jit(solution)/shard_map/ppermute | solution.py:199
  27.3 12.6 %collective-permute-start.11 = (f32[160,256]{1,0:T(8,128)S(1)}, f32[160,256]{1,0:T(8,128)S(1)}, u32[]{:S(2)}, u32[]{:S(2)}) collective-permute-start(f32[160,256]{1,0:T(8,128)S(1)} %add.43), channel_id=1, source_target_pairs={{0,24},{8,16},{16,8},{24,0},{1,25},{9,17},{17,9},{25,1},{2,26},{10... | collective-permute-start | bytes 491528 | tf_op jit(solution)/shard_map/ppermute | solution.py:199
  29.8 10.6 %collective-permute-start.10 = (f32[160,256]{1,0:T(8,128)S(1)}, f32[160,256]{1,0:T(8,128)S(1)}, u32[]{:S(2)}, u32[]{:S(2)}) collective-permute-start(f32[160,256]{1,0:T(8,128)S(1)} %add.43), channel_id=1, source_target_pairs={{0,16},{8,24},{16,0},{24,8},{1,17},{9,25},{17,1},{25,9},{2,18},{10... | collective-permute-start | bytes 491528 | tf_op jit(solution)/shard_map/ppermute | solution.py:199
  30.3 10.6 %collective-permute-start.9 = (f32[160,256]{1,0:T(8,128)S(1)}, f32[160,256]{1,0:T(8,128)S(1)}, u32[]{:S(2)}, u32[]{:S(2)}) collective-permute-start(f32[160,256]{1,0:T(8,128)S(1)} %add.43), channel_id=1, source_target_pairs={{0,8},{8,0},{16,24},{24,16},{1,9},{9,1},{17,25},{25,17},{2,10},{10... | collective-permute-start | bytes 491528 | tf_op jit(solution)/shard_map/ppermute | solution.py:199
  30.9 6.5 %collective-permute-start.14 = (f32[160,128]{1,0:T(8,128)S(1)}, f32[160,128]{1,0:T(8,128)S(1)}, u32[]{:S(2)}, u32[]{:S(2)}) collective-permute-start(f32[160,128]{1,0:T(8,128)S(1)} %add.47), channel_id=1, source_target_pairs={{0,4},{2,6},{4,0},{6,2},{1,5},{3,7},{5,1},{7,3},{8,12},{10,14},{12... | collective-permute-start | bytes 245768 | tf_op jit(solution)/shard_map/ppermute | solution.py:199
  32.8 12.2 %collective-permute-start.19 = (f32[256,128]{1,0:T(8,128)S(1)}, f32[256,128]{1,0:T(8,128)S(1)}, u32[]{:S(2)}, u32[]{:S(2)}) collective-permute-start(f32[256,128]{1,0:T(8,128)S(1)} %add_add_fusion.1.mine_term_ref), channel_id=1, source_target_pairs={{0,1},{1,0},{2,3},{3,2},{4,5},{5,4},{6,7},{7,6},{8,9},{9,8},{10,11... | collective-permute-start | bytes 393224 | tf_op jit(solution)/shard_map/ppermute | solution.py:199
  37.4 5.5 %collective-permute-start.17 = (f32[160,128]{1,0:T(8,128)S(1)}, f32[160,128]{1,0:T(8,128)S(1)}, u32[]{:S(2)}, u32[]{:S(2)}) collective-permute-start(f32[160,128]{1,0:T(8,128)S(1)} %add.48), channel_id=1, source_target_pairs={{0,24},{8,16},{16,8},{24,0},{1,25},{9,17},{17,9},{25,1},{2,26},{10... | collective-permute-start | bytes 245768 | tf_op jit(solution)/shard_map/ppermute | solution.py:199
  39.9 4.4 %collective-permute-start.16 = (f32[160,128]{1,0:T(8,128)S(1)}, f32[160,128]{1,0:T(8,128)S(1)}, u32[]{:S(2)}, u32[]{:S(2)}) collective-permute-start(f32[160,128]{1,0:T(8,128)S(1)} %add.48), channel_id=1, source_target_pairs={{0,16},{8,24},{16,0},{24,8},{1,17},{9,25},{17,1},{25,9},{2,18},{10... | collective-permute-start | bytes 245768 | tf_op jit(solution)/shard_map/ppermute | solution.py:199
  40.4 4.4 %collective-permute-start.15 = (f32[160,128]{1,0:T(8,128)S(1)}, f32[160,128]{1,0:T(8,128)S(1)}, u32[]{:S(2)}, u32[]{:S(2)}) collective-permute-start(f32[160,128]{1,0:T(8,128)S(1)} %add.48), channel_id=1, source_target_pairs={{0,8},{8,0},{16,24},{24,16},{1,9},{9,1},{17,25},{25,17},{2,10},{10... | collective-permute-start | bytes 245768 | tf_op jit(solution)/shard_map/ppermute | solution.py:199
  41.0 5.2 %collective-permute-start.12 = (f32[160,256]{1,0:T(8,128)S(1)}, f32[160,256]{1,0:T(8,128)S(1)}, u32[]{:S(2)}, u32[]{:S(2)}) collective-permute-start(f32[160,256]{1,0:T(8,128)S(1)} %add_add_fusion.mine_d_ref), channel_id=1, source_target_pairs={{0,1},{1,0},{2,3},{3,2},{4,5},{5,4},{6,7},{7,6},{8,9},{9,8},{10,11... | collective-permute-start | bytes 491528 | tf_op jit(solution)/shard_map/ppermute | solution.py:199
  44.9 1.3 %collective-permute-start.18 = (f32[160,128]{1,0:T(8,128)S(1)}, f32[160,128]{1,0:T(8,128)S(1)}, u32[]{:S(2)}, u32[]{:S(2)}) collective-permute-start(f32[160,128]{1,0:T(8,128)S(1)} %add_add_fusion.2.mine_t_ref), channel_id=1, source_target_pairs={{0,1},{1,0},{2,3},{3,2},{4,5},{5,4},{6,7},{7,6},{8,9},{9,8},{10,11... | collective-permute-start | bytes 245768 | tf_op jit(solution)/shard_map/ppermute | solution.py:199

commit v17 on v15

--- a/solution.py
+++ b/solution.py
@@ -47,7 +47,7 @@
 ):
     row_count, col_count = counts
     own_refs, refs = refs[:col_count], refs[col_count:]
-    straight_ref, own_wide_ref, term_ref, pick_d_ref, pick_t_ref, keep_ref, upper_ref = refs
+    straight_ref, own_wide_ref, term_ref, pick_d_ref, mine_ref, other_ref, keep_ref, upper_ref = refs
     packed_width = own_refs[0].shape[0] // 2
     col_index = place_ref[1]
     block = inverse_ref.shape[1]
@@ -98,9 +98,11 @@
     position = jnp.where(column < half, column + side * half, column - side * half)
     lane = lax.broadcasted_iota(jnp.int32, (slot, slot), 1)
     for k in range(total_cols // slot):
-        chosen = (position == row_in_slot + offsets[k]) & (row_in_slot < widths_ref[k])
         rows = slice(k * slot, (k + 1) * slot)
-        pick_t_ref[rows, :] = jnp.where(chosen, 1.0, 0.0).astype(BF16)
+        for ref, at in ((mine_ref, side), (other_ref, 1 - side)):
+            inside = row_in_slot[:, :half]
+            chosen = (column[:, :half] + at * half == inside + offsets[k]) & (inside < widths_ref[k])
+            ref[rows, :] = jnp.where(chosen, 1.0, 0.0).astype(BF16)
         keep_ref[rows, :] = jnp.where(
             (lane < widths_ref[k]) & (row_in_slot[:, :slot] < widths_ref[k]), 1.0, 0.0
         )
@@ -173,11 +175,11 @@
 
 
 def expand_kernel(
-    pick_d_ref, pick_t_ref, keep_ref, upper_ref, mine_d_ref, other_d_ref, mine_t_ref, other_t_ref,
+    pick_d_ref, pick_ref, keep_ref, upper_ref, mine_d_ref, other_d_ref, mine_t_ref,
     mine_term_ref, other_term_ref, density_ref, diagonal_ref,
 ):
     density_ref[...] = picked(pick_d_ref, jnp.concatenate([mine_d_ref[...], other_d_ref[...]], axis=0))
-    product = picked(pick_t_ref, jnp.concatenate([mine_t_ref[...], other_t_ref[...]], axis=0))
+    product = picked(pick_ref, mine_t_ref[...])
     rows = mine_term_ref.shape[0]
     upper = upper_ref[:1, :] > 0.5
     terms = (
@@ -187,6 +189,11 @@
     for side in range(2):
         part = slice(side * rows, (side + 1) * rows)
         diagonal_ref[part] = terms[side] - jnp.where(keep_ref[part] > 0.5, product[part], 0.0)
+
+
+def finish_kernel(pick_ref, keep_ref, other_t_ref, partial_ref, diagonal_ref):
+    product = picked(pick_ref, other_t_ref[...])
+    diagonal_ref[...] = partial_ref[...] - jnp.where(keep_ref[...] > 0.5, product, 0.0)
 
 
 def bits_of(count):
@@ -254,16 +261,17 @@
         blocks[other] = swap(packed, "row", other)
     own = [packed] + [swap(packed, "col", other) for other in range(1, col_count)]
 
-    straight, own_wide, term, *picks = pl.pallas_call(
+    straight, own_wide, term, pick_d, pick_mine, pick_other, keep, upper = pl.pallas_call(
         functools.partial(prepare_kernel, (row_count, col_count)),
         in_specs=[SMEM_SPEC] * 3 + [VMEM_SPEC] * (2 + col_count),
-        out_specs=[VMEM_SPEC] * 7,
+        out_specs=[VMEM_SPEC] * 8,
         out_shape=[
             jax.ShapeDtypeStruct((2, local_rows, row_count * block), BF16),
             jax.ShapeDtypeStruct((total_cols, 2 * local_rows), BF16),
             jax.ShapeDtypeStruct((total_cols // col_count, slot), F32),
             jax.ShapeDtypeStruct((total_cols // col_count, packed_width), BF16),
-            jax.ShapeDtypeStruct((total_cols, packed_width), BF16),
+            jax.ShapeDtypeStruct((total_cols, packed_width // 2), BF16),
+            jax.ShapeDtypeStruct((total_cols, packed_width // 2), BF16),
             jax.ShapeDtypeStruct((total_cols, slot), F32),
             jax.ShapeDtypeStruct((8, slot), F32),
         ],
@@ -310,20 +318,34 @@
     density = gather_but_last(density, "col")
     products = gather_but_last(products, "col")
 
-    return pl.pallas_call(
+    density, partial = pl.pallas_call(
         expand_kernel,
-        in_specs=[VMEM_SPEC] * 10,
+        in_specs=[VMEM_SPEC] * 9,
         out_specs=[VMEM_SPEC] * 2,
         out_shape=[
             jax.ShapeDtypeStruct((total_cols // col_count, local_rows), F32),
             jax.ShapeDtypeStruct((total_cols, slot), F32),
         ],
         compiler_params=PARAMS,
+        cost_estimate=pl.CostEstimate(
+            flops=8 * total_cols * packed_width * (local_rows + slot),
+            bytes_accessed=16 * total_cols * local_rows,
+            transcendentals=0,
+        ),
         name="expand",
     )(
-        *picks, density, swap(density, "col", top), products, swap(products, "col", top),
+        pick_d, pick_mine, keep, upper, density, swap(density, "col", top), products,
         term, swap(term, "col", top),
     )
+    diagonal = pl.pallas_call(
+        finish_kernel,
+        in_specs=[VMEM_SPEC] * 4,
+        out_specs=VMEM_SPEC,
+        out_shape=jax.ShapeDtypeStruct((total_cols, slot), F32),
+        compiler_params=PARAMS,
+        name="finish",
+    )(pick_other, keep, swap(products, "col", top), partial)
+    return (density, diagonal)
 
 
 def solution(mesh):

time: 47.4 us -> 47.2 us (level)
  waiting for transfers between devices: 17.6 us -> 16.4 us
  Pallas kernels: 6.61 us -> 7.5 us
    ppermute x20, waiting for transfers between devices: 17.6 us -> 16.4 us  [swap(): lax.ppermute(value, axis, [(i, i ^ bit) for i in range(lax.axis_size(axis...]
    pallas_call x1 -> x2, Pallas kernels: 1.24 us -> 2.13 us  [the longest x1 1.14 us: per_device(): pl.pallas_call(expand_kernel, in_specs=[VMEM_SPEC] * 9, out_specs=[VMEM_S...]
  transfers between devices with their start and end apart: 20 -> 20, of which waited for: 8 -> 8; matrix products, arithmetic and copies ran while one was open for 0% -> 0% of each run, Pallas kernels for 7% -> 10%
where the time goes in v17:
time: 47.2 us; the launch traced here: 47 us
  starting transfers between devices  19.4 us (41%)
  waiting for transfers between devices  16.4 us (35%)
  Pallas kernels  7.5 us (16%)
  local copies, waits for them, and re-layouts  2.63 us (6%)
  between operations  0.78 us (2%)
    ppermute x20, starting transfers between devices, swap(): lax.ppermute(value, axis, [(i, i ^ bit) for i in range(lax.axis_size(axis...  19.4 us
    ppermute x20, waiting for transfers between devices, swap(): lax.ppermute(value, axis, [(i, i ^ bit) for i in range(lax.axis_size(axis...  16.4 us
    unnamed x10, local copies, waits for them, and re-layouts  2.63 us
    pallas_call x1, Pallas kernels, per_device(): pl.pallas_call(functools.partial(pack_kernel, supernodes, slot), in_specs...  2 us
    pallas_call x1, Pallas kernels, per_device(): pl.pallas_call(functools.partial(compute_kernel, col_count, supernodes, s...  1.99 us
    pallas_call x1, Pallas kernels, per_device(): pl.pallas_call(functools.partial(prepare_kernel, (row_count, col_count)),...  1.38 us
    pallas_call x1, Pallas kernels, per_device(): pl.pallas_call(expand_kernel, in_specs=[VMEM_SPEC] * 9, out_specs=[VMEM_S...  1.14 us
    pallas_call x1, Pallas kernels, per_device(): pl.pallas_call(finish_kernel, in_specs=[VMEM_SPEC] * 4, out_specs=VMEM_SP...  0.99 us
  transfers between devices with their start and end apart: 20, of which 8 were waited for; matrix products, arithmetic and copies ran while one was open for 0% of the time, Pallas kernels for 10%

profile of v17, /device:TPU:0, one launch (start us, length us, event | category | flops | bytes accessed | tf_op | source)
XLA Modules:
  0.0 47.0 jit_solution(2305021152965636244)
XLA Ops:
  0.6 0.0 copy-start.2
  0.6 2.0 %pack.1.refs_0_ = bf16[640,128]{1,0:T(8,128)(2,1)} custom-call(s32[1,4]{1,0:T(1,128)} %pattern_ref.1, s32[4]{0:T(128)} %widths_ref.5, bf16[2,128,512]{2,1,0:T(8,128)(2,1)} %bitcast.7), custom_call_target="tpu_custom_call" | custom-call | tf_op jit(solution)/shard_map/pack/pallas_call | solution.py:251
  2.6 0.5 collective-permute-start
  3.1 4.6 %collective-permute-start.3 = (bf16[640,128]{1,0:T(8,128)(2,1)}, bf16[640,128]{1,0:T(8,128)(2,1)S(1)}, u32[]{:S(2)}, u32[]{:S(2)}) collective-permute-start(bf16[640,128]{1,0:T(8,128)(2,1)} %pack.1.refs_0_), channel_id=1, source_target_pairs={{0,6},{2,4},{4,2},{6,0},{1,7},{3,5},{5,3},{7,1},{8,14},{10,12},{12... | collective-permute-start | bytes 491528 | tf_op jit(solution)/shard_map/ppermute | solution.py:204
  7.7 0.0 collective-permute-start.2
  7.7 0.6 %collective-permute-start.1 = (bf16[640,128]{1,0:T(8,128)(2,1)}, bf16[640,128]{1,0:T(8,128)(2,1)S(1)}, u32[]{:S(2)}, u32[]{:S(2)}) collective-permute-start(bf16[640,128]{1,0:T(8,128)(2,1)} %pack.1.refs_0_), channel_id=1, source_target_pairs={{0,2},{2,0},{4,6},{6,4},{1,3},{3,1},{5,7},{7,5},{8,10},{10,8},{12,... | collective-permute-start | bytes 491528 | tf_op jit(solution)/shard_map/ppermute | solution.py:204
  8.3 0.1 pad_add_fusion.place_ref
  8.4 0.0 collective-permute-done.refs_1_
  8.4 0.0 copy-start.3
  8.4 0.0 copy-start.4
  8.4 0.0 copy-done.2
  8.4 0.6 %copy-done.3 = s32[4]{0:T(128)S(1)} copy-done((s32[4]{0:T(128)S(1)}, s32[4]{0:T(128)}, u32[]{:S(2)}) %copy-start.3) | copy-done | bytes 40
  9.1 0.0 copy-done.4
  9.1 0.0 copy-start
  9.1 0.9 %copy-done = bf16[640,128]{1,0:T(8,128)(2,1)S(1)} copy-done((bf16[640,128]{1,0:T(8,128)(2,1)S(1)}, bf16[640,128]{1,0:T(8,128)(2,1)}, u32[]{:S(2)}) %copy-start) | copy-done | bytes 163864
  10.0 0.0 copy-start.1
  10.0 1.0 %copy-done.1 = bf16[1,2,256,4,1,128]{5,3,4,2,1,0:T(4,128)(2,1)S(1)} copy-done((bf16[1,2,256,4,1,128]{5,3,4,2,1,0:T(4,128)(2,1)S(1)}, bf16[1,2,256,4,1,128]{5,3,4,2,1,0:T(4,128)(2,1)}, u32[]{:S(2)}) %copy-start.1) | copy-done | bytes 524312
  11.0 1.4 %prepare.1 = (bf16[2,256,512]{2,1,0:T(8,128)(2,1)S(1)}, bf16[512,512]{1,0:T(8,128)(2,1)S(1)}, f32[256,128]{1,0:T(8,128)S(1)}, bf16[256,320]{1,0:T(8,128)(2,1)S(1...) custom-call(s32[4]{0:T(128)S(1)} %copy-done.3, ...), custom_call_target="tpu_custom_call" | custom-call | flops 134217728 | bytes 1048576 | tf_op jit(solution)/shard_map/prepare/pallas_call | solution.py:264
  12.4 2.7 %collective-permute-start.7 = (f32[256,128]{1,0:T(8,128)S(1)}, f32[256,128]{1,0:T(8,128)S(1)}, u32[]{:S(2)}, u32[]{:S(2)}) collective-permute-start(f32[256,128]{1,0:T(8,128)S(1)} %get-tuple-element.29), channel_id=1, source_target_pairs={{0,24},{8,16},{16,8},{24,0},{1,25},{9,17},{17,9},{25,1},{2,26},{10... | collective-permute-start | bytes 393224 | tf_op jit(solution)/shard_map/ppermute | solution.py:204
  15.1 0.5 %collective-permute-start.6 = (f32[256,128]{1,0:T(8,128)S(1)}, f32[256,128]{1,0:T(8,128)S(1)}, u32[]{:S(2)}, u32[]{:S(2)}) collective-permute-start(f32[256,128]{1,0:T(8,128)S(1)} %get-tuple-element.29), channel_id=1, source_target_pairs={{0,16},{8,24},{16,0},{24,8},{1,17},{9,25},{17,1},{25,9},{2,18},{10... | collective-permute-start | bytes 393224 | tf_op jit(solution)/shard_map/ppermute | solution.py:204
  15.6 0.0 collective-permute-done.3.refs_3_
  15.6 0.4 collective-permute-start.5
  16.0 6.5 %collective-permute-done.2.refs_2_ = bf16[640,128]{1,0:T(8,128)(2,1)S(1)} collective-permute-done((bf16[640,128]{1,0:T(8,128)(2,1)}, bf16[640,128]{1,0:T(8,128)(2,1)S(1)}, u32[]{:S(2)}, u32[]{:S(2)}) %collective-permute-start.2) | collective-permute-done | bytes 163872 | tf_op jit(solution)/shard_map/ppermute | solution.py:204
  22.5 0.0 collective-permute-done.1.refs_1_
  22.5 2.0 %compute.1 = (f32[160,256]{1,0:T(8,128)S(1)}, f32[160,256]{1,0:T(8,128)S(1)}, f32[160,128]{1,0:T(8,128)S(1)}, f32[160,128]{1,0:T(8,128)S(1)}) custom-call(s32[4]{0:T(128)S(1)} %copy-done.3, f32[1,2]{1,0:T(1,128)S(1)} %copy-done.4, s32[2]{0:T(128)S(1)} %pad_add_fusion.place_ref, bf16[2,256,512]{2,1,0:T(8,128)(2,1)S(1)} %get-tuple-element.23.straight_ref, ...), custom_call_target="tpu_custom_call" | custom-call | tf_op jit(solution)/shard_map/compute/pallas_call | solution.py:291
  24.5 0.1 collective-permute-start.4
  24.5 1.3 %collective-permute-done.4 = f32[160,128]{1,0:T(8,128)S(1)} collective-permute-done((f32[160,128]{1,0:T(8,128)S(1)}, f32[160,128]{1,0:T(8,128)S(1)}, u32[]{:S(2)}, u32[]{:S(2)}) %collective-permute-start.4) | collective-permute-done | bytes 81952 | tf_op jit(solution)/shard_map/ppermute | solution.py:204
  25.8 0.0 collective-permute-done.7
  25.8 0.0 collective-permute-done.6
  25.8 0.0 collective-permute-done.5
  25.9 0.2 collective-permute-start.8
  26.1 2.5 %collective-permute-start.13 = (f32[160,128]{1,0:T(8,128)S(1)}, f32[160,128]{1,0:T(8,128)S(1)}, u32[]{:S(2)}, u32[]{:S(2)}) collective-permute-start(f32[160,128]{1,0:T(8,128)S(1)} %add.39), channel_id=1, source_target_pairs={{0,6},{2,4},{4,2},{6,0},{1,7},{3,5},{5,3},{7,1},{8,14},{10,12},{12... | collective-permute-start | bytes 245768 | tf_op jit(solution)/shard_map/ppermute | solution.py:204
  28.6 0.0 collective-permute-done.8
  28.6 2.5 %collective-permute-start.11 = (f32[160,256]{1,0:T(8,128)S(1)}, f32[160,256]{1,0:T(8,128)S(1)}, u32[]{:S(2)}, u32[]{:S(2)}) collective-permute-start(f32[160,256]{1,0:T(8,128)S(1)} %add.43), channel_id=1, source_target_pairs={{0,24},{8,16},{16,8},{24,0},{1,25},{9,17},{17,9},{25,1},{2,26},{10... | collective-permute-start | bytes 491528 | tf_op jit(solution)/shard_map/ppermute | solution.py:204
  31.1 0.5 %collective-permute-start.10 = (f32[160,256]{1,0:T(8,128)S(1)}, f32[160,256]{1,0:T(8,128)S(1)}, u32[]{:S(2)}, u32[]{:S(2)}) collective-permute-start(f32[160,256]{1,0:T(8,128)S(1)} %add.43), channel_id=1, source_target_pairs={{0,16},{8,24},{16,0},{24,8},{1,17},{9,25},{17,1},{25,9},{2,18},{10... | collective-permute-start | bytes 491528 | tf_op jit(solution)/shard_map/ppermute | solution.py:204
  31.6 0.5 %collective-permute-start.9 = (f32[160,256]{1,0:T(8,128)S(1)}, f32[160,256]{1,0:T(8,128)S(1)}, u32[]{:S(2)}, u32[]{:S(2)}) collective-permute-start(f32[160,256]{1,0:T(8,128)S(1)} %add.43), channel_id=1, source_target_pairs={{0,8},{8,0},{16,24},{24,16},{1,9},{9,1},{17,25},{25,17},{2,10},{10... | collective-permute-start | bytes 491528 | tf_op jit(solution)/shard_map/ppermute | solution.py:204
  32.2 0.4 collective-permute-done.13
  32.6 0.1 collective-permute-start.14
  32.7 0.1 collective-permute-start.18
  32.8 4.3 %collective-permute-done.14 = f32[160,128]{1,0:T(8,128)S(1)} collective-permute-done((f32[160,128]{1,0:T(8,128)S(1)}, f32[160,128]{1,0:T(8,128)S(1)}, u32[]{:S(2)}, u32[]{:S(2)}) %collective-permute-start.14) | collective-permute-done | bytes 81952 | tf_op jit(solution)/shard_map/ppermute | solution.py:204
  37.1 2.5 %collective-permute-start.17 = (f32[160,128]{1,0:T(8,128)S(1)}, f32[160,128]{1,0:T(8,128)S(1)}, u32[]{:S(2)}, u32[]{:S(2)}) collective-permute-start(f32[160,128]{1,0:T(8,128)S(1)} %add.48), channel_id=1, source_target_pairs={{0,24},{8,16},{16,8},{24,0},{1,25},{9,17},{17,9},{25,1},{2,26},{10... | collective-permute-start | bytes 245768 | tf_op jit(solution)/shard_map/ppermute | solution.py:204
  39.7 0.0 collective-permute-done.11
  39.7 0.5 %collective-permute-start.16 = (f32[160,128]{1,0:T(8,128)S(1)}, f32[160,128]{1,0:T(8,128)S(1)}, u32[]{:S(2)}, u32[]{:S(2)}) collective-permute-start(f32[160,128]{1,0:T(8,128)S(1)} %add.48), channel_id=1, source_target_pairs={{0,16},{8,24},{16,0},{24,8},{1,17},{9,25},{17,1},{25,9},{2,18},{10... | collective-permute-start | bytes 245768 | tf_op jit(solution)/shard_map/ppermute | solution.py:204
  40.2 0.0 collective-permute-done.10
  40.2 0.6 %collective-permute-start.15 = (f32[160,128]{1,0:T(8,128)S(1)}, f32[160,128]{1,0:T(8,128)S(1)}, u32[]{:S(2)}, u32[]{:S(2)}) collective-permute-start(f32[160,128]{1,0:T(8,128)S(1)} %add.48), channel_id=1, source_target_pairs={{0,8},{8,0},{16,24},{24,16},{1,9},{9,1},{17,25},{25,17},{2,10},{10... | collective-permute-start | bytes 245768 | tf_op jit(solution)/shard_map/ppermute | solution.py:204
  40.8 0.0 collective-permute-done.9
  40.8 0.1 collective-permute-start.12
  40.9 1.7 %collective-permute-done.17 = f32[160,128]{1,0:T(8,128)S(1)} collective-permute-done((f32[160,128]{1,0:T(8,128)S(1)}, f32[160,128]{1,0:T(8,128)S(1)}, u32[]{:S(2)}, u32[]{:S(2)}) %collective-permute-start.17) | collective-permute-done | bytes 81952 | tf_op jit(solution)/shard_map/ppermute | solution.py:204
  42.5 1.5 %collective-permute-done.16 = f32[160,128]{1,0:T(8,128)S(1)} collective-permute-done((f32[160,128]{1,0:T(8,128)S(1)}, f32[160,128]{1,0:T(8,128)S(1)}, u32[]{:S(2)}, u32[]{:S(2)}) %collective-permute-start.16) | collective-permute-done | bytes 81952 | tf_op jit(solution)/shard_map/ppermute | solution.py:204
  44.1 0.5 %collective-permute-done.15 = f32[160,128]{1,0:T(8,128)S(1)} collective-permute-done((f32[160,128]{1,0:T(8,128)S(1)}, f32[160,128]{1,0:T(8,128)S(1)}, u32[]{:S(2)}, u32[]{:S(2)}) %collective-permute-start.15) | collective-permute-done | bytes 81952 | tf_op jit(solution)/shard_map/ppermute | solution.py:204
  44.6 0.1 collective-permute-start.19
  44.7 0.0 collective-permute-done.18.other_term_ref
  44.7 0.0 collective-permute-done.12.other_d_ref
  44.7 1.1 %expand.1 = (f32[256,256]{1,0:T(8,128)}, f32[512,128]{1,0:T(8,128)S(1)}) custom-call(bf16[256,320]{1,0:T(8,128)(2,1)S(1)} %get-tuple-element.19.pick_d_ref, bf16[512,160]{1,0:T(8,128)(2,1)S(1)} %get-tuple-element.20.pick_ref, f32[512,128]{1,0:T(8,128)S(1)} %get-tuple-element.21.keep_ref, f32[8,128]{1,0:T(8,128)S(1)} %get-tuple-element.22.upper_ref, ...), custom_call_target="tpu_custom_call" | custom-call | flops 503316480 | bytes 2097152 | tf_op jit(solution)/shard_map/expand/pallas_call | solution.py:321
  45.9 0.1 collective-permute-done.19.other_t_ref
  46.0 1.0 %finish.1 = f32[512,128]{1,0:T(8,128)} custom-call(bf16[512,160]{1,0:T(8,128)(2,1)S(1)} %get-tuple-element.34.pick_ref, f32[512,128]{1,0:T(8,128)S(1)} %get-tuple-element.21.keep_ref, f32[160,128]{1,0:T(8,128)S(1)} %collective-permute-done.19.other_t_ref, f32[512,128]{1,0:T(8,128)S(1)} %get-tuple-element.35.partial_ref), custom_call_target="tpu_custom_call" | custom-call | tf_op jit(solution)/shard_map/finish/pallas_call | solution.py:340
  (7 shorter events, 0.1 us)
Async XLA Ops:
  0.6 7.8 %copy-start.2 = (bf16[1,2,512,128]{3,2,1,0:T(8,128)(2,1)S(1)}, bf16[1,2,512,128]{3,2,1,0:T(8,128)(2,1)}, u32[]{:S(2)}) copy-start(bf16[1,2,512,128]{3,2,1,0:T(8,128)(2,1)} %param.10) | copy-start | bytes 786436
  2.6 5.8 %collective-permute-start = (bf16[640,128]{1,0:T(8,128)(2,1)}, bf16[640,128]{1,0:T(8,128)(2,1)S(1)}, u32[]{:S(2)}, u32[]{:S(2)}) collective-permute-start(bf16[640,128]{1,0:T(8,128)(2,1)} %pack.1.refs_0_), channel_id=1, source_target_pairs={{0,1},{1,0},{2,3},{3,2},{4,5},{5,4},{6,7},{7,6},{8,9},{9,8},{10,11... | collective-permute-start | bytes 491528 | tf_op jit(solution)/shard_map/ppermute | solution.py:204
  3.1 12.5 %collective-permute-start.3 = (bf16[640,128]{1,0:T(8,128)(2,1)}, bf16[640,128]{1,0:T(8,128)(2,1)S(1)}, u32[]{:S(2)}, u32[]{:S(2)}) collective-permute-start(bf16[640,128]{1,0:T(8,128)(2,1)} %pack.1.refs_0_), channel_id=1, source_target_pairs={{0,6},{2,4},{4,2},{6,0},{1,7},{3,5},{5,3},{7,1},{8,14},{10,12},{12... | collective-permute-start | bytes 491528 | tf_op jit(solution)/shard_map/ppermute | solution.py:204
  7.7 14.8 %collective-permute-start.2 = (bf16[640,128]{1,0:T(8,128)(2,1)}, bf16[640,128]{1,0:T(8,128)(2,1)S(1)}, u32[]{:S(2)}, u32[]{:S(2)}) collective-permute-start(bf16[640,128]{1,0:T(8,128)(2,1)} %pack.1.refs_0_), channel_id=1, source_target_pairs={{0,4},{2,6},{4,0},{6,2},{1,5},{3,7},{5,1},{7,3},{8,12},{10,14},{12... | collective-permute-start | bytes 491528 | tf_op jit(solution)/shard_map/ppermute | solution.py:204
  7.7 14.8 %collective-permute-start.1 = (bf16[640,128]{1,0:T(8,128)(2,1)}, bf16[640,128]{1,0:T(8,128)(2,1)S(1)}, u32[]{:S(2)}, u32[]{:S(2)}) collective-permute-start(bf16[640,128]{1,0:T(8,128)(2,1)} %pack.1.refs_0_), channel_id=1, source_target_pairs={{0,2},{2,0},{4,6},{6,4},{1,3},{3,1},{5,7},{7,5},{8,10},{10,8},{12,... | collective-permute-start | bytes 491528 | tf_op jit(solution)/shard_map/ppermute | solution.py:204
  8.4 0.7 %copy-start.3 = (s32[4]{0:T(128)S(1)}, s32[4]{0:T(128)}, u32[]{:S(2)}) copy-start(s32[4]{0:T(128)} %widths_ref.5) | copy-start | bytes 52
  8.4 0.7 %copy-start.4 = (f32[1,2]{1,0:T(1,128)S(1)}, f32[1,2]{1,0:T(1,128)}, u32[]{:S(2)}) copy-start(f32[1,2]{1,0:T(1,128)} %weights_ref.3) | copy-start | bytes 28
  9.1 0.9 %copy-start = (bf16[640,128]{1,0:T(8,128)(2,1)S(1)}, bf16[640,128]{1,0:T(8,128)(2,1)}, u32[]{:S(2)}) copy-start(bf16[640,128]{1,0:T(8,128)(2,1)} %pack.1.refs_0_) | copy-start | bytes 491524
  10.0 1.0 %copy-start.1 = (bf16[1,2,256,4,1,128]{5,3,4,2,1,0:T(4,128)(2,1)S(1)}, bf16[1,2,256,4,1,128]{5,3,4,2,1,0:T(4,128)(2,1)}, u32[]{:S(2)}) copy-start(bf16[1,2,256,4,1,128]{5,3,4,2,1,0:T(4,128)(2,1)} %param.6) | copy-start | bytes 1572868
  12.4 13.4 %collective-permute-start.7 = (f32[256,128]{1,0:T(8,128)S(1)}, f32[256,128]{1,0:T(8,128)S(1)}, u32[]{:S(2)}, u32[]{:S(2)}) collective-permute-start(f32[256,128]{1,0:T(8,128)S(1)} %get-tuple-element.29), channel_id=1, source_target_pairs={{0,24},{8,16},{16,8},{24,0},{1,25},{9,17},{17,9},{25,1},{2,26},{10... | collective-permute-start | bytes 393224 | tf_op jit(solution)/shard_map/ppermute | solution.py:204
  15.1 10.7 %collective-permute-start.6 = (f32[256,128]{1,0:T(8,128)S(1)}, f32[256,128]{1,0:T(8,128)S(1)}, u32[]{:S(2)}, u32[]{:S(2)}) collective-permute-start(f32[256,128]{1,0:T(8,128)S(1)} %get-tuple-element.29), channel_id=1, source_target_pairs={{0,16},{8,24},{16,0},{24,8},{1,17},{9,25},{17,1},{25,9},{2,18},{10... | collective-permute-start | bytes 393224 | tf_op jit(solution)/shard_map/ppermute | solution.py:204
  15.6 10.2 %collective-permute-start.5 = (f32[256,128]{1,0:T(8,128)S(1)}, f32[256,128]{1,0:T(8,128)S(1)}, u32[]{:S(2)}, u32[]{:S(2)}) collective-permute-start(f32[256,128]{1,0:T(8,128)S(1)} %get-tuple-element.29), channel_id=1, source_target_pairs={{0,8},{8,0},{16,24},{24,16},{1,9},{9,1},{17,25},{25,17},{2,10},{10... | collective-permute-start | bytes 393224 | tf_op jit(solution)/shard_map/ppermute | solution.py:204
  24.5 1.3 %collective-permute-start.4 = (f32[160,128]{1,0:T(8,128)S(1)}, f32[160,128]{1,0:T(8,128)S(1)}, u32[]{:S(2)}, u32[]{:S(2)}) collective-permute-start(f32[160,128]{1,0:T(8,128)S(1)} %get-tuple-element.27), channel_id=1, source_target_pairs={{0,1},{1,0},{2,3},{3,2},{4,5},{5,4},{6,7},{7,6},{8,9},{9,8},{10,11... | collective-permute-start | bytes 245768 | tf_op jit(solution)/shard_map/ppermute | solution.py:204
  25.9 2.7 %collective-permute-start.8 = (f32[160,256]{1,0:T(8,128)S(1)}, f32[160,256]{1,0:T(8,128)S(1)}, u32[]{:S(2)}, u32[]{:S(2)}) collective-permute-start(f32[160,256]{1,0:T(8,128)S(1)} %get-tuple-element.30), channel_id=1, source_target_pairs={{0,1},{1,0},{2,3},{3,2},{4,5},{5,4},{6,7},{7,6},{8,9},{9,8},{10,11... | collective-permute-start | bytes 491528 | tf_op jit(solution)/shard_map/ppermute | solution.py:204
  26.1 6.5 %collective-permute-start.13 = (f32[160,128]{1,0:T(8,128)S(1)}, f32[160,128]{1,0:T(8,128)S(1)}, u32[]{:S(2)}, u32[]{:S(2)}) collective-permute-start(f32[160,128]{1,0:T(8,128)S(1)} %add.39), channel_id=1, source_target_pairs={{0,6},{2,4},{4,2},{6,0},{1,7},{3,5},{5,3},{7,1},{8,14},{10,12},{12... | collective-permute-start | bytes 245768 | tf_op jit(solution)/shard_map/ppermute | solution.py:204
  28.6 11.0 %collective-permute-start.11 = (f32[160,256]{1,0:T(8,128)S(1)}, f32[160,256]{1,0:T(8,128)S(1)}, u32[]{:S(2)}, u32[]{:S(2)}) collective-permute-start(f32[160,256]{1,0:T(8,128)S(1)} %add.43), channel_id=1, source_target_pairs={{0,24},{8,16},{16,8},{24,0},{1,25},{9,17},{17,9},{25,1},{2,26},{10... | collective-permute-start | bytes 491528 | tf_op jit(solution)/shard_map/ppermute | solution.py:204
  31.1 9.0 %collective-permute-start.10 = (f32[160,256]{1,0:T(8,128)S(1)}, f32[160,256]{1,0:T(8,128)S(1)}, u32[]{:S(2)}, u32[]{:S(2)}) collective-permute-start(f32[160,256]{1,0:T(8,128)S(1)} %add.43), channel_id=1, source_target_pairs={{0,16},{8,24},{16,0},{24,8},{1,17},{9,25},{17,1},{25,9},{2,18},{10... | collective-permute-start | bytes 491528 | tf_op jit(solution)/shard_map/ppermute | solution.py:204
  31.6 9.1 %collective-permute-start.9 = (f32[160,256]{1,0:T(8,128)S(1)}, f32[160,256]{1,0:T(8,128)S(1)}, u32[]{:S(2)}, u32[]{:S(2)}) collective-permute-start(f32[160,256]{1,0:T(8,128)S(1)} %add.43), channel_id=1, source_target_pairs={{0,8},{8,0},{16,24},{24,16},{1,9},{9,1},{17,25},{25,17},{2,10},{10... | collective-permute-start | bytes 491528 | tf_op jit(solution)/shard_map/ppermute | solution.py:204
  32.6 4.5 %collective-permute-start.14 = (f32[160,128]{1,0:T(8,128)S(1)}, f32[160,128]{1,0:T(8,128)S(1)}, u32[]{:S(2)}, u32[]{:S(2)}) collective-permute-start(f32[160,128]{1,0:T(8,128)S(1)} %add.47), channel_id=1, source_target_pairs={{0,2},{2,0},{4,6},{6,4},{1,3},{3,1},{5,7},{7,5},{8,10},{10,8},{12,... | collective-permute-start | bytes 245768 | tf_op jit(solution)/shard_map/ppermute | solution.py:204
  32.7 12.0 %collective-permute-start.18 = (f32[256,128]{1,0:T(8,128)S(1)}, f32[256,128]{1,0:T(8,128)S(1)}, u32[]{:S(2)}, u32[]{:S(2)}) collective-permute-start(f32[256,128]{1,0:T(8,128)S(1)} %add_add_fusion.1.mine_term_ref), channel_id=1, source_target_pairs={{0,1},{1,0},{2,3},{3,2},{4,5},{5,4},{6,7},{7,6},{8,9},{9,8},{10,11... | collective-permute-start | bytes 393224 | tf_op jit(solution)/shard_map/ppermute | solution.py:204
  37.1 5.4 %collective-permute-start.17 = (f32[160,128]{1,0:T(8,128)S(1)}, f32[160,128]{1,0:T(8,128)S(1)}, u32[]{:S(2)}, u32[]{:S(2)}) collective-permute-start(f32[160,128]{1,0:T(8,128)S(1)} %add.48), channel_id=1, source_target_pairs={{0,24},{8,16},{16,8},{24,0},{1,25},{9,17},{17,9},{25,1},{2,26},{10... | collective-permute-start | bytes 245768 | tf_op jit(solution)/shard_map/ppermute | solution.py:204
  39.7 4.4 %collective-permute-start.16 = (f32[160,128]{1,0:T(8,128)S(1)}, f32[160,128]{1,0:T(8,128)S(1)}, u32[]{:S(2)}, u32[]{:S(2)}) collective-permute-start(f32[160,128]{1,0:T(8,128)S(1)} %add.48), channel_id=1, source_target_pairs={{0,16},{8,24},{16,0},{24,8},{1,17},{9,25},{17,1},{25,9},{2,18},{10... | collective-permute-start | bytes 245768 | tf_op jit(solution)/shard_map/ppermute | solution.py:204
  40.2 4.4 %collective-permute-start.15 = (f32[160,128]{1,0:T(8,128)S(1)}, f32[160,128]{1,0:T(8,128)S(1)}, u32[]{:S(2)}, u32[]{:S(2)}) collective-permute-start(f32[160,128]{1,0:T(8,128)S(1)} %add.48), channel_id=1, source_target_pairs={{0,8},{8,0},{16,24},{24,16},{1,9},{9,1},{17,25},{25,17},{2,10},{10... | collective-permute-start | bytes 245768 | tf_op jit(solution)/shard_map/ppermute | solution.py:204
  40.8 3.9 %collective-permute-start.12 = (f32[160,256]{1,0:T(8,128)S(1)}, f32[160,256]{1,0:T(8,128)S(1)}, u32[]{:S(2)}, u32[]{:S(2)}) collective-permute-start(f32[160,256]{1,0:T(8,128)S(1)} %add_add_fusion.mine_d_ref), channel_id=1, source_target_pairs={{0,1},{1,0},{2,3},{3,2},{4,5},{5,4},{6,7},{7,6},{8,9},{9,8},{10,11... | collective-permute-start | bytes 491528 | tf_op jit(solution)/shard_map/ppermute | solution.py:204
  44.6 1.3 %collective-permute-start.19 = (f32[160,128]{1,0:T(8,128)S(1)}, f32[160,128]{1,0:T(8,128)S(1)}, u32[]{:S(2)}, u32[]{:S(2)}) collective-permute-start(f32[160,128]{1,0:T(8,128)S(1)} %add_add_fusion.2.mine_t_ref), channel_id=1, source_target_pairs={{0,1},{1,0},{2,3},{3,2},{4,5},{5,4},{6,7},{7,6},{8,9},{9,8},{10,11... | collective-permute-start | bytes 245768 | tf_op jit(solution)/shard_map/ppermute | solution.py:204

commit v18 on v17

--- a/solution.py
+++ b/solution.py
@@ -211,7 +211,7 @@
 
 
 def sum_direct(value, axis):
-    return tree_sum([value] + [swap(value, axis, j) for j in range(1, lax.axis_size(axis))])
+    return tree_sum([swap(value, axis, j) for j in range(1, lax.axis_size(axis))][::-1] + [value])
 
 
 def scatter_rest(value, axis):

time: 47.2 us -> 48.1 us (1.019)
  waiting for transfers between devices: 16.4 us -> 17 us
    ppermute x20, waiting for transfers between devices: 16.4 us -> 17 us  [swap(): lax.ppermute(value, axis, [(i, i ^ bit) for i in range(lax.axis_size(axis...]
  transfers between devices with their start and end apart: 20 -> 20, of which waited for: 8 -> 8; matrix products, arithmetic and copies ran while one was open for 0% -> 0% of each run, Pallas kernels for 10% -> 9%
where the time goes in v18:
time: 48.1 us; the launch traced here: 47.9 us
  starting transfers between devices  19.8 us (41%)
  waiting for transfers between devices  17 us (35%)
  Pallas kernels  7.5 us (16%)
  local copies, waits for them, and re-layouts  2.63 us (5%)
  between operations  0.78 us (2%)
    ppermute x20, starting transfers between devices, swap(): lax.ppermute(value, axis, [(i, i ^ bit) for i in range(lax.axis_size(axis...  19.8 us
    ppermute x20, waiting for transfers between devices, swap(): lax.ppermute(value, axis, [(i, i ^ bit) for i in range(lax.axis_size(axis...  17 us
    unnamed x10, local copies, waits for them, and re-layouts  2.63 us
    pallas_call x1, Pallas kernels, per_device(): pl.pallas_call(functools.partial(pack_kernel, supernodes, slot), in_specs...  2 us
    pallas_call x1, Pallas kernels, per_device(): pl.pallas_call(functools.partial(compute_kernel, col_count, supernodes, s...  1.99 us
    pallas_call x1, Pallas kernels, per_device(): pl.pallas_call(functools.partial(prepare_kernel, (row_count, col_count)),...  1.38 us
    pallas_call x1, Pallas kernels, per_device(): pl.pallas_call(expand_kernel, in_specs=[VMEM_SPEC] * 9, out_specs=[VMEM_S...  1.14 us
    pallas_call x1, Pallas kernels, per_device(): pl.pallas_call(finish_kernel, in_specs=[VMEM_SPEC] * 4, out_specs=VMEM_SP...  0.99 us
  transfers between devices with their start and end apart: 20, of which 8 were waited for; matrix products, arithmetic and copies ran while one was open for 0% of the time, Pallas kernels for 9%

profile of v18, /device:TPU:0, one launch (start us, length us, event | category | flops | bytes accessed | tf_op | source)
XLA Modules:
  0.0 47.9 jit_solution(3858060271269471965)
XLA Ops:
  0.6 0.0 copy-start.2
  0.6 2.0 %pack.1.refs_0_ = bf16[640,128]{1,0:T(8,128)(2,1)} custom-call(s32[1,4]{1,0:T(1,128)} %pattern_ref.1, s32[4]{0:T(128)} %widths_ref.5, bf16[2,128,512]{2,1,0:T(8,128)(2,1)} %bitcast.7), custom_call_target="tpu_custom_call" | custom-call | tf_op jit(solution)/shard_map/pack/pallas_call | solution.py:251
  2.6 0.5 collective-permute-start
  3.1 4.6 %collective-permute-start.3 = (bf16[640,128]{1,0:T(8,128)(2,1)}, bf16[640,128]{1,0:T(8,128)(2,1)S(1)}, u32[]{:S(2)}, u32[]{:S(2)}) collective-permute-start(bf16[640,128]{1,0:T(8,128)(2,1)} %pack.1.refs_0_), channel_id=1, source_target_pairs={{0,6},{2,4},{4,2},{6,0},{1,7},{3,5},{5,3},{7,1},{8,14},{10,12},{12... | collective-permute-start | bytes 491528 | tf_op jit(solution)/shard_map/ppermute | solution.py:204
  7.7 0.0 collective-permute-start.2
  7.7 0.6 %collective-permute-start.1 = (bf16[640,128]{1,0:T(8,128)(2,1)}, bf16[640,128]{1,0:T(8,128)(2,1)S(1)}, u32[]{:S(2)}, u32[]{:S(2)}) collective-permute-start(bf16[640,128]{1,0:T(8,128)(2,1)} %pack.1.refs_0_), channel_id=1, source_target_pairs={{0,2},{2,0},{4,6},{6,4},{1,3},{3,1},{5,7},{7,5},{8,10},{10,8},{12,... | collective-permute-start | bytes 491528 | tf_op jit(solution)/shard_map/ppermute | solution.py:204
  8.3 0.1 pad_add_fusion.place_ref
  8.4 0.0 collective-permute-done.refs_1_
  8.4 0.0 copy-start.3
  8.4 0.0 copy-start.4
  8.4 0.0 copy-done.2
  8.4 0.6 %copy-done.3 = s32[4]{0:T(128)S(1)} copy-done((s32[4]{0:T(128)S(1)}, s32[4]{0:T(128)}, u32[]{:S(2)}) %copy-start.3) | copy-done | bytes 40
  9.1 0.0 copy-done.4
  9.1 0.0 copy-start
  9.1 0.9 %copy-done = bf16[640,128]{1,0:T(8,128)(2,1)S(1)} copy-done((bf16[640,128]{1,0:T(8,128)(2,1)S(1)}, bf16[640,128]{1,0:T(8,128)(2,1)}, u32[]{:S(2)}) %copy-start) | copy-done | bytes 163864
  10.0 0.0 copy-start.1
  10.0 1.0 %copy-done.1 = bf16[1,2,256,4,1,128]{5,3,4,2,1,0:T(4,128)(2,1)S(1)} copy-done((bf16[1,2,256,4,1,128]{5,3,4,2,1,0:T(4,128)(2,1)S(1)}, bf16[1,2,256,4,1,128]{5,3,4,2,1,0:T(4,128)(2,1)}, u32[]{:S(2)}) %copy-start.1) | copy-done | bytes 524312
  11.0 1.4 %prepare.1 = (bf16[2,256,512]{2,1,0:T(8,128)(2,1)S(1)}, bf16[512,512]{1,0:T(8,128)(2,1)S(1)}, f32[256,128]{1,0:T(8,128)S(1)}, bf16[256,320]{1,0:T(8,128)(2,1)S(1...) custom-call(s32[4]{0:T(128)S(1)} %copy-done.3, ...), custom_call_target="tpu_custom_call" | custom-call | flops 134217728 | bytes 1048576 | tf_op jit(solution)/shard_map/prepare/pallas_call | solution.py:264
  12.4 1.7 %collective-permute-start.7 = (f32[256,128]{1,0:T(8,128)S(1)}, f32[256,128]{1,0:T(8,128)S(1)}, u32[]{:S(2)}, u32[]{:S(2)}) collective-permute-start(f32[256,128]{1,0:T(8,128)S(1)} %get-tuple-element.29), channel_id=1, source_target_pairs={{0,8},{8,0},{16,24},{24,16},{1,9},{9,1},{17,25},{25,17},{2,10},{10... | collective-permute-start | bytes 393224 | tf_op jit(solution)/shard_map/ppermute | solution.py:204
  14.1 1.5 %collective-permute-start.6 = (f32[256,128]{1,0:T(8,128)S(1)}, f32[256,128]{1,0:T(8,128)S(1)}, u32[]{:S(2)}, u32[]{:S(2)}) collective-permute-start(f32[256,128]{1,0:T(8,128)S(1)} %get-tuple-element.29), channel_id=1, source_target_pairs={{0,16},{8,24},{16,0},{24,8},{1,17},{9,25},{17,1},{25,9},{2,18},{10... | collective-permute-start | bytes 393224 | tf_op jit(solution)/shard_map/ppermute | solution.py:204
  15.7 0.0 collective-permute-done.3.refs_3_
  15.7 0.3 collective-permute-start.5
  16.0 6.5 %collective-permute-done.2.refs_2_ = bf16[640,128]{1,0:T(8,128)(2,1)S(1)} collective-permute-done((bf16[640,128]{1,0:T(8,128)(2,1)}, bf16[640,128]{1,0:T(8,128)(2,1)S(1)}, u32[]{:S(2)}, u32[]{:S(2)}) %collective-permute-start.2) | collective-permute-done | bytes 163872 | tf_op jit(solution)/shard_map/ppermute | solution.py:204
  22.5 0.0 collective-permute-done.1.refs_1_
  22.5 2.0 %compute.1 = (f32[160,256]{1,0:T(8,128)S(1)}, f32[160,256]{1,0:T(8,128)S(1)}, f32[160,128]{1,0:T(8,128)S(1)}, f32[160,128]{1,0:T(8,128)S(1)}) custom-call(s32[4]{0:T(128)S(1)} %copy-done.3, f32[1,2]{1,0:T(1,128)S(1)} %copy-done.4, s32[2]{0:T(128)S(1)} %pad_add_fusion.place_ref, bf16[2,256,512]{2,1,0:T(8,128)(2,1)S(1)} %get-tuple-element.23.straight_ref, ...), custom_call_target="tpu_custom_call" | custom-call | tf_op jit(solution)/shard_map/compute/pallas_call | solution.py:291
  24.5 0.1 collective-permute-start.4
  24.5 1.3 %collective-permute-done.4 = f32[160,128]{1,0:T(8,128)S(1)} collective-permute-done((f32[160,128]{1,0:T(8,128)S(1)}, f32[160,128]{1,0:T(8,128)S(1)}, u32[]{:S(2)}, u32[]{:S(2)}) %collective-permute-start.4) | collective-permute-done | bytes 81952 | tf_op jit(solution)/shard_map/ppermute | solution.py:204
  25.8 0.0 collective-permute-done.7
  25.8 0.0 collective-permute-done.6
  25.8 0.0 collective-permute-done.5
  25.9 0.2 collective-permute-start.8
  26.1 2.5 %collective-permute-start.13 = (f32[160,128]{1,0:T(8,128)S(1)}, f32[160,128]{1,0:T(8,128)S(1)}, u32[]{:S(2)}, u32[]{:S(2)}) collective-permute-start(f32[160,128]{1,0:T(8,128)S(1)} %add.39), channel_id=1, source_target_pairs={{0,6},{2,4},{4,2},{6,0},{1,7},{3,5},{5,3},{7,1},{8,14},{10,12},{12... | collective-permute-start | bytes 245768 | tf_op jit(solution)/shard_map/ppermute | solution.py:204
  28.6 0.0 collective-permute-done.8
  28.6 1.6 %collective-permute-start.11 = (f32[160,256]{1,0:T(8,128)S(1)}, f32[160,256]{1,0:T(8,128)S(1)}, u32[]{:S(2)}, u32[]{:S(2)}) collective-permute-start(f32[160,256]{1,0:T(8,128)S(1)} %add.43), channel_id=1, source_target_pairs={{0,8},{8,0},{16,24},{24,16},{1,9},{9,1},{17,25},{25,17},{2,10},{10... | collective-permute-start | bytes 491528 | tf_op jit(solution)/shard_map/ppermute | solution.py:204
  30.2 1.5 %collective-permute-start.10 = (f32[160,256]{1,0:T(8,128)S(1)}, f32[160,256]{1,0:T(8,128)S(1)}, u32[]{:S(2)}, u32[]{:S(2)}) collective-permute-start(f32[160,256]{1,0:T(8,128)S(1)} %add.43), channel_id=1, source_target_pairs={{0,16},{8,24},{16,0},{24,8},{1,17},{9,25},{17,1},{25,9},{2,18},{10... | collective-permute-start | bytes 491528 | tf_op jit(solution)/shard_map/ppermute | solution.py:204
  31.7 0.5 collective-permute-start.9
  32.2 0.4 collective-permute-done.13
  32.6 0.1 collective-permute-start.14
  32.7 0.1 collective-permute-start.18
  32.8 4.3 %collective-permute-done.14 = f32[160,128]{1,0:T(8,128)S(1)} collective-permute-done((f32[160,128]{1,0:T(8,128)S(1)}, f32[160,128]{1,0:T(8,128)S(1)}, u32[]{:S(2)}, u32[]{:S(2)}) %collective-permute-start.14) | collective-permute-done | bytes 81952 | tf_op jit(solution)/shard_map/ppermute | solution.py:204
  37.1 1.6 %collective-permute-start.17 = (f32[160,128]{1,0:T(8,128)S(1)}, f32[160,128]{1,0:T(8,128)S(1)}, u32[]{:S(2)}, u32[]{:S(2)}) collective-permute-start(f32[160,128]{1,0:T(8,128)S(1)} %add.48), channel_id=1, source_target_pairs={{0,8},{8,0},{16,24},{24,16},{1,9},{9,1},{17,25},{25,17},{2,10},{10... | collective-permute-start | bytes 245768 | tf_op jit(solution)/shard_map/ppermute | solution.py:204
  38.7 0.0 collective-permute-done.11
  38.7 1.5 %collective-permute-start.16 = (f32[160,128]{1,0:T(8,128)S(1)}, f32[160,128]{1,0:T(8,128)S(1)}, u32[]{:S(2)}, u32[]{:S(2)}) collective-permute-start(f32[160,128]{1,0:T(8,128)S(1)} %add.48), channel_id=1, source_target_pairs={{0,16},{8,24},{16,0},{24,8},{1,17},{9,25},{17,1},{25,9},{2,18},{10... | collective-permute-start | bytes 245768 | tf_op jit(solution)/shard_map/ppermute | solution.py:204
  40.2 0.0 collective-permute-done.10
  40.2 0.8 %collective-permute-start.15 = (f32[160,128]{1,0:T(8,128)S(1)}, f32[160,128]{1,0:T(8,128)S(1)}, u32[]{:S(2)}, u32[]{:S(2)}) collective-permute-start(f32[160,128]{1,0:T(8,128)S(1)} %add.48), channel_id=1, source_target_pairs={{0,24},{8,16},{16,8},{24,0},{1,25},{9,17},{17,9},{25,1},{2,26},{10... | collective-permute-start | bytes 245768 | tf_op jit(solution)/shard_map/ppermute | solution.py:204
  41.1 0.0 collective-permute-done.9
  41.1 0.1 collective-permute-start.12
  41.2 1.2 %collective-permute-done.17 = f32[160,128]{1,0:T(8,128)S(1)} collective-permute-done((f32[160,128]{1,0:T(8,128)S(1)}, f32[160,128]{1,0:T(8,128)S(1)}, u32[]{:S(2)}, u32[]{:S(2)}) %collective-permute-start.17) | collective-permute-done | bytes 81952 | tf_op jit(solution)/shard_map/ppermute | solution.py:204
  42.4 1.4 %collective-permute-done.16 = f32[160,128]{1,0:T(8,128)S(1)} collective-permute-done((f32[160,128]{1,0:T(8,128)S(1)}, f32[160,128]{1,0:T(8,128)S(1)}, u32[]{:S(2)}, u32[]{:S(2)}) %collective-permute-start.16) | collective-permute-done | bytes 81952 | tf_op jit(solution)/shard_map/ppermute | solution.py:204
  43.8 1.8 %collective-permute-done.15 = f32[160,128]{1,0:T(8,128)S(1)} collective-permute-done((f32[160,128]{1,0:T(8,128)S(1)}, f32[160,128]{1,0:T(8,128)S(1)}, u32[]{:S(2)}, u32[]{:S(2)}) %collective-permute-start.15) | collective-permute-done | bytes 81952 | tf_op jit(solution)/shard_map/ppermute | solution.py:204
  45.6 0.1 collective-permute-start.19
  45.7 0.0 collective-permute-done.18.other_term_ref
  45.7 0.0 collective-permute-done.12.other_d_ref
  45.7 1.1 %expand.1 = (f32[256,256]{1,0:T(8,128)}, f32[512,128]{1,0:T(8,128)S(1)}) custom-call(bf16[256,320]{1,0:T(8,128)(2,1)S(1)} %get-tuple-element.19.pick_d_ref, bf16[512,160]{1,0:T(8,128)(2,1)S(1)} %get-tuple-element.20.pick_ref, f32[512,128]{1,0:T(8,128)S(1)} %get-tuple-element.21.keep_ref, f32[8,128]{1,0:T(8,128)S(1)} %get-tuple-element.22.upper_ref, ...), custom_call_target="tpu_custom_call" | custom-call | flops 503316480 | bytes 2097152 | tf_op jit(solution)/shard_map/expand/pallas_call | solution.py:321
  46.8 0.1 collective-permute-done.19.other_t_ref
  46.9 1.0 %finish.1 = f32[512,128]{1,0:T(8,128)} custom-call(bf16[512,160]{1,0:T(8,128)(2,1)S(1)} %get-tuple-element.34.pick_ref, f32[512,128]{1,0:T(8,128)S(1)} %get-tuple-element.21.keep_ref, f32[160,128]{1,0:T(8,128)S(1)} %collective-permute-done.19.other_t_ref, f32[512,128]{1,0:T(8,128)S(1)} %get-tuple-element.35.partial_ref), custom_call_target="tpu_custom_call" | custom-call | tf_op jit(solution)/shard_map/finish/pallas_call | solution.py:340
  (7 shorter events, 0.2 us)
Async XLA Ops:
  0.6 7.8 %copy-start.2 = (bf16[1,2,512,128]{3,2,1,0:T(8,128)(2,1)S(1)}, bf16[1,2,512,128]{3,2,1,0:T(8,128)(2,1)}, u32[]{:S(2)}) copy-start(bf16[1,2,512,128]{3,2,1,0:T(8,128)(2,1)} %param.10) | copy-start | bytes 786436
  2.6 5.8 %collective-permute-start = (bf16[640,128]{1,0:T(8,128)(2,1)}, bf16[640,128]{1,0:T(8,128)(2,1)S(1)}, u32[]{:S(2)}, u32[]{:S(2)}) collective-permute-start(bf16[640,128]{1,0:T(8,128)(2,1)} %pack.1.refs_0_), channel_id=1, source_target_pairs={{0,1},{1,0},{2,3},{3,2},{4,5},{5,4},{6,7},{7,6},{8,9},{9,8},{10,11... | collective-permute-start | bytes 491528 | tf_op jit(solution)/shard_map/ppermute | solution.py:204
  3.1 12.6 %collective-permute-start.3 = (bf16[640,128]{1,0:T(8,128)(2,1)}, bf16[640,128]{1,0:T(8,128)(2,1)S(1)}, u32[]{:S(2)}, u32[]{:S(2)}) collective-permute-start(bf16[640,128]{1,0:T(8,128)(2,1)} %pack.1.refs_0_), channel_id=1, source_target_pairs={{0,6},{2,4},{4,2},{6,0},{1,7},{3,5},{5,3},{7,1},{8,14},{10,12},{12... | collective-permute-start | bytes 491528 | tf_op jit(solution)/shard_map/ppermute | solution.py:204
  7.7 14.8 %collective-permute-start.2 = (bf16[640,128]{1,0:T(8,128)(2,1)}, bf16[640,128]{1,0:T(8,128)(2,1)S(1)}, u32[]{:S(2)}, u32[]{:S(2)}) collective-permute-start(bf16[640,128]{1,0:T(8,128)(2,1)} %pack.1.refs_0_), channel_id=1, source_target_pairs={{0,4},{2,6},{4,0},{6,2},{1,5},{3,7},{5,1},{7,3},{8,12},{10,14},{12... | collective-permute-start | bytes 491528 | tf_op jit(solution)/shard_map/ppermute | solution.py:204
  7.7 14.8 %collective-permute-start.1 = (bf16[640,128]{1,0:T(8,128)(2,1)}, bf16[640,128]{1,0:T(8,128)(2,1)S(1)}, u32[]{:S(2)}, u32[]{:S(2)}) collective-permute-start(bf16[640,128]{1,0:T(8,128)(2,1)} %pack.1.refs_0_), channel_id=1, source_target_pairs={{0,2},{2,0},{4,6},{6,4},{1,3},{3,1},{5,7},{7,5},{8,10},{10,8},{12,... | collective-permute-start | bytes 491528 | tf_op jit(solution)/shard_map/ppermute | solution.py:204
  8.4 0.7 %copy-start.3 = (s32[4]{0:T(128)S(1)}, s32[4]{0:T(128)}, u32[]{:S(2)}) copy-start(s32[4]{0:T(128)} %widths_ref.5) | copy-start | bytes 52
  8.4 0.7 %copy-start.4 = (f32[1,2]{1,0:T(1,128)S(1)}, f32[1,2]{1,0:T(1,128)}, u32[]{:S(2)}) copy-start(f32[1,2]{1,0:T(1,128)} %weights_ref.3) | copy-start | bytes 28
  9.1 0.9 %copy-start = (bf16[640,128]{1,0:T(8,128)(2,1)S(1)}, bf16[640,128]{1,0:T(8,128)(2,1)}, u32[]{:S(2)}) copy-start(bf16[640,128]{1,0:T(8,128)(2,1)} %pack.1.refs_0_) | copy-start | bytes 491524
  10.0 1.0 %copy-start.1 = (bf16[1,2,256,4,1,128]{5,3,4,2,1,0:T(4,128)(2,1)S(1)}, bf16[1,2,256,4,1,128]{5,3,4,2,1,0:T(4,128)(2,1)}, u32[]{:S(2)}) copy-start(bf16[1,2,256,4,1,128]{5,3,4,2,1,0:T(4,128)(2,1)} %param.6) | copy-start | bytes 1572868
  12.4 13.4 %collective-permute-start.7 = (f32[256,128]{1,0:T(8,128)S(1)}, f32[256,128]{1,0:T(8,128)S(1)}, u32[]{:S(2)}, u32[]{:S(2)}) collective-permute-start(f32[256,128]{1,0:T(8,128)S(1)} %get-tuple-element.29), channel_id=1, source_target_pairs={{0,8},{8,0},{16,24},{24,16},{1,9},{9,1},{17,25},{25,17},{2,10},{10... | collective-permute-start | bytes 393224 | tf_op jit(solution)/shard_map/ppermute | solution.py:204
  14.1 11.7 %collective-permute-start.6 = (f32[256,128]{1,0:T(8,128)S(1)}, f32[256,128]{1,0:T(8,128)S(1)}, u32[]{:S(2)}, u32[]{:S(2)}) collective-permute-start(f32[256,128]{1,0:T(8,128)S(1)} %get-tuple-element.29), channel_id=1, source_target_pairs={{0,16},{8,24},{16,0},{24,8},{1,17},{9,25},{17,1},{25,9},{2,18},{10... | collective-permute-start | bytes 393224 | tf_op jit(solution)/shard_map/ppermute | solution.py:204
  15.7 10.2 %collective-permute-start.5 = (f32[256,128]{1,0:T(8,128)S(1)}, f32[256,128]{1,0:T(8,128)S(1)}, u32[]{:S(2)}, u32[]{:S(2)}) collective-permute-start(f32[256,128]{1,0:T(8,128)S(1)} %get-tuple-element.29), channel_id=1, source_target_pairs={{0,24},{8,16},{16,8},{24,0},{1,25},{9,17},{17,9},{25,1},{2,26},{10... | collective-permute-start | bytes 393224 | tf_op jit(solution)/shard_map/ppermute | solution.py:204
  24.5 1.3 %collective-permute-start.4 = (f32[160,128]{1,0:T(8,128)S(1)}, f32[160,128]{1,0:T(8,128)S(1)}, u32[]{:S(2)}, u32[]{:S(2)}) collective-permute-start(f32[160,128]{1,0:T(8,128)S(1)} %get-tuple-element.27), channel_id=1, source_target_pairs={{0,1},{1,0},{2,3},{3,2},{4,5},{5,4},{6,7},{7,6},{8,9},{9,8},{10,11... | collective-permute-start | bytes 245768 | tf_op jit(solution)/shard_map/ppermute | solution.py:204
  25.9 2.7 %collective-permute-start.8 = (f32[160,256]{1,0:T(8,128)S(1)}, f32[160,256]{1,0:T(8,128)S(1)}, u32[]{:S(2)}, u32[]{:S(2)}) collective-permute-start(f32[160,256]{1,0:T(8,128)S(1)} %get-tuple-element.30), channel_id=1, source_target_pairs={{0,1},{1,0},{2,3},{3,2},{4,5},{5,4},{6,7},{7,6},{8,9},{9,8},{10,11... | collective-permute-start | bytes 491528 | tf_op jit(solution)/shard_map/ppermute | solution.py:204
  26.1 6.5 %collective-permute-start.13 = (f32[160,128]{1,0:T(8,128)S(1)}, f32[160,128]{1,0:T(8,128)S(1)}, u32[]{:S(2)}, u32[]{:S(2)}) collective-permute-start(f32[160,128]{1,0:T(8,128)S(1)} %add.39), channel_id=1, source_target_pairs={{0,6},{2,4},{4,2},{6,0},{1,7},{3,5},{5,3},{7,1},{8,14},{10,12},{12... | collective-permute-start | bytes 245768 | tf_op jit(solution)/shard_map/ppermute | solution.py:204
  28.6 10.1 %collective-permute-start.11 = (f32[160,256]{1,0:T(8,128)S(1)}, f32[160,256]{1,0:T(8,128)S(1)}, u32[]{:S(2)}, u32[]{:S(2)}) collective-permute-start(f32[160,256]{1,0:T(8,128)S(1)} %add.43), channel_id=1, source_target_pairs={{0,8},{8,0},{16,24},{24,16},{1,9},{9,1},{17,25},{25,17},{2,10},{10... | collective-permute-start | bytes 491528 | tf_op jit(solution)/shard_map/ppermute | solution.py:204
  30.2 10.1 %collective-permute-start.10 = (f32[160,256]{1,0:T(8,128)S(1)}, f32[160,256]{1,0:T(8,128)S(1)}, u32[]{:S(2)}, u32[]{:S(2)}) collective-permute-start(f32[160,256]{1,0:T(8,128)S(1)} %add.43), channel_id=1, source_target_pairs={{0,16},{8,24},{16,0},{24,8},{1,17},{9,25},{17,1},{25,9},{2,18},{10... | collective-permute-start | bytes 491528 | tf_op jit(solution)/shard_map/ppermute | solution.py:204
  31.7 9.4 %collective-permute-start.9 = (f32[160,256]{1,0:T(8,128)S(1)}, f32[160,256]{1,0:T(8,128)S(1)}, u32[]{:S(2)}, u32[]{:S(2)}) collective-permute-start(f32[160,256]{1,0:T(8,128)S(1)} %add.43), channel_id=1, source_target_pairs={{0,24},{8,16},{16,8},{24,0},{1,25},{9,17},{17,9},{25,1},{2,26},{10... | collective-permute-start | bytes 491528 | tf_op jit(solution)/shard_map/ppermute | solution.py:204
  32.6 4.5 %collective-permute-start.14 = (f32[160,128]{1,0:T(8,128)S(1)}, f32[160,128]{1,0:T(8,128)S(1)}, u32[]{:S(2)}, u32[]{:S(2)}) collective-permute-start(f32[160,128]{1,0:T(8,128)S(1)} %add.47), channel_id=1, source_target_pairs={{0,2},{2,0},{4,6},{6,4},{1,3},{3,1},{5,7},{7,5},{8,10},{10,8},{12,... | collective-permute-start | bytes 245768 | tf_op jit(solution)/shard_map/ppermute | solution.py:204
  32.7 13.0 %collective-permute-start.18 = (f32[256,128]{1,0:T(8,128)S(1)}, f32[256,128]{1,0:T(8,128)S(1)}, u32[]{:S(2)}, u32[]{:S(2)}) collective-permute-start(f32[256,128]{1,0:T(8,128)S(1)} %add_add_fusion.1.mine_term_ref), channel_id=1, source_target_pairs={{0,1},{1,0},{2,3},{3,2},{4,5},{5,4},{6,7},{7,6},{8,9},{9,8},{10,11... | collective-permute-start | bytes 393224 | tf_op jit(solution)/shard_map/ppermute | solution.py:204
  37.1 5.3 %collective-permute-start.17 = (f32[160,128]{1,0:T(8,128)S(1)}, f32[160,128]{1,0:T(8,128)S(1)}, u32[]{:S(2)}, u32[]{:S(2)}) collective-permute-start(f32[160,128]{1,0:T(8,128)S(1)} %add.48), channel_id=1, source_target_pairs={{0,8},{8,0},{16,24},{24,16},{1,9},{9,1},{17,25},{25,17},{2,10},{10... | collective-permute-start | bytes 245768 | tf_op jit(solution)/shard_map/ppermute | solution.py:204
  38.7 5.1 %collective-permute-start.16 = (f32[160,128]{1,0:T(8,128)S(1)}, f32[160,128]{1,0:T(8,128)S(1)}, u32[]{:S(2)}, u32[]{:S(2)}) collective-permute-start(f32[160,128]{1,0:T(8,128)S(1)} %add.48), channel_id=1, source_target_pairs={{0,16},{8,24},{16,0},{24,8},{1,17},{9,25},{17,1},{25,9},{2,18},{10... | collective-permute-start | bytes 245768 | tf_op jit(solution)/shard_map/ppermute | solution.py:204
  40.2 5.3 %collective-permute-start.15 = (f32[160,128]{1,0:T(8,128)S(1)}, f32[160,128]{1,0:T(8,128)S(1)}, u32[]{:S(2)}, u32[]{:S(2)}) collective-permute-start(f32[160,128]{1,0:T(8,128)S(1)} %add.48), channel_id=1, source_target_pairs={{0,24},{8,16},{16,8},{24,0},{1,25},{9,17},{17,9},{25,1},{2,26},{10... | collective-permute-start | bytes 245768 | tf_op jit(solution)/shard_map/ppermute | solution.py:204
  41.1 4.6 %collective-permute-start.12 = (f32[160,256]{1,0:T(8,128)S(1)}, f32[160,256]{1,0:T(8,128)S(1)}, u32[]{:S(2)}, u32[]{:S(2)}) collective-permute-start(f32[160,256]{1,0:T(8,128)S(1)} %add_add_fusion.mine_d_ref), channel_id=1, source_target_pairs={{0,1},{1,0},{2,3},{3,2},{4,5},{5,4},{6,7},{7,6},{8,9},{9,8},{10,11... | collective-permute-start | bytes 491528 | tf_op jit(solution)/shard_map/ppermute | solution.py:204
  45.6 1.3 %collective-permute-start.19 = (f32[160,128]{1,0:T(8,128)S(1)}, f32[160,128]{1,0:T(8,128)S(1)}, u32[]{:S(2)}, u32[]{:S(2)}) collective-permute-start(f32[160,128]{1,0:T(8,128)S(1)} %add_add_fusion.2.mine_t_ref), channel_id=1, source_target_pairs={{0,1},{1,0},{2,3},{3,2},{4,5},{5,4},{6,7},{7,6},{8,9},{9,8},{10,11... | collective-permute-start | bytes 245768 | tf_op jit(solution)/shard_map/ppermute | solution.py:204

commit v19 on v17

--- a/solution.py
+++ b/solution.py
@@ -120,10 +120,11 @@
 
 
 def compute_kernel(
-    col_count, supernodes, slot, widths_ref, weights_ref, place_ref, straight_ref,
+    others, col_count, supernodes, slot, widths_ref, weights_ref, place_ref, straight_ref,
     own_wide_ref, *refs
 ):
     block_refs, refs = refs[:-7], refs[-7:]
+    block_refs = [block_refs[others.index(other)] for other in range(len(others))]
     keep_d_ref, send_d_ref, keep_t_ref, send_t_ref, x_ref, y_ref, t_ref = refs
     packed_width = block_refs[0].shape[0] // 2
     local_rows = straight_ref.shape[1]
@@ -257,6 +258,7 @@
     )(block_pattern, sup_widths, l_panel[0])
 
     blocks = {0: packed}
+    others = sorted(range(row_count), key=lambda other: other > 0 and other % 2 == 0)
     for other in range(1, row_count):
         blocks[other] = swap(packed, "row", other)
     own = [packed] + [swap(packed, "col", other) for other in range(1, col_count)]
@@ -289,7 +291,7 @@
     term = sum_direct(term, "pole")
 
     keep_d, send_d, keep_t, send_t = pl.pallas_call(
-        functools.partial(compute_kernel, col_count, supernodes, slot),
+        functools.partial(compute_kernel, others, col_count, supernodes, slot),
         in_specs=[SMEM_SPEC] * 3 + [VMEM_SPEC] * (2 + row_count),
         out_specs=[VMEM_SPEC] * 4,
         out_shape=[jax.ShapeDtypeStruct((half, local_rows), F32)] * 2
@@ -303,7 +305,7 @@
         name="compute",
     )(
         sup_widths, pole_weights, place, straight, own_wide,
-        *[blocks[other] for other in range(row_count)],
+        *[blocks[other] for other in others],
     )
 
     tie = lax.optimization_barrier

time: 47.2 us -> 46.2 us (0.979)
  waiting for transfers between devices: 16.4 us -> 10.9 us
  starting transfers between devices: 19.4 us -> 23.9 us
    ppermute x20, waiting for transfers between devices: 16.4 us -> 10.9 us  [swap(): lax.ppermute(value, axis, [(i, i ^ bit) for i in range(lax.axis_size(axis...]
    ppermute x20, starting transfers between devices: 19.4 us -> 23.9 us  [swap(): lax.ppermute(value, axis, [(i, i ^ bit) for i in range(lax.axis_size(axis...]
  transfers between devices with their start and end apart: 20 -> 20, of which waited for: 8 -> 7; matrix products, arithmetic and copies ran while one was open for 0% -> 0% of each run, Pallas kernels for 10% -> 10%
where the time goes in v19:
time: 46.2 us; the launch traced here: 46 us
  starting transfers between devices  23.9 us (52%)
  waiting for transfers between devices  10.9 us (24%)
  Pallas kernels  7.5 us (16%)
  local copies, waits for them, and re-layouts  2.63 us (6%)
  between operations  0.76 us (2%)
    ppermute x20, starting transfers between devices, swap(): lax.ppermute(value, axis, [(i, i ^ bit) for i in range(lax.axis_size(axis...  23.9 us
    ppermute x20, waiting for transfers between devices, swap(): lax.ppermute(value, axis, [(i, i ^ bit) for i in range(lax.axis_size(axis...  10.9 us
    unnamed x10, local copies, waits for them, and re-layouts  2.63 us
    pallas_call x1, Pallas kernels, per_device(): pl.pallas_call(functools.partial(pack_kernel, supernodes, slot), in_specs...  2 us
    pallas_call x1, Pallas kernels, per_device(): pl.pallas_call(functools.partial(compute_kernel, others, col_count, super...  1.99 us
    pallas_call x1, Pallas kernels, per_device(): pl.pallas_call(functools.partial(prepare_kernel, (row_count, col_count)),...  1.38 us
    pallas_call x1, Pallas kernels, per_device(): pl.pallas_call(expand_kernel, in_specs=[VMEM_SPEC] * 9, out_specs=[VMEM_S...  1.14 us
    pallas_call x1, Pallas kernels, per_device(): pl.pallas_call(finish_kernel, in_specs=[VMEM_SPEC] * 4, out_specs=VMEM_SP...  0.99 us
  transfers between devices with their start and end apart: 20, of which 7 were waited for; matrix products, arithmetic and copies ran while one was open for 0% of the time, Pallas kernels for 10%

profile of v19, /device:TPU:0, one launch (start us, length us, event | category | flops | bytes accessed | tf_op | source)
XLA Modules:
  0.0 46.0 jit_solution(12491675319622324991)
XLA Ops:
  0.6 0.0 copy-start.2
  0.6 2.0 %pack.1.refs_0_ = bf16[640,128]{1,0:T(8,128)(2,1)} custom-call(s32[1,4]{1,0:T(1,128)} %pattern_ref.1, s32[4]{0:T(128)} %widths_ref.5, bf16[2,128,512]{2,1,0:T(8,128)(2,1)} %bitcast.7), custom_call_target="tpu_custom_call" | custom-call | tf_op jit(solution)/shard_map/pack/pallas_call | solution.py:252
  2.6 0.5 collective-permute-start
  3.1 3.6 %collective-permute-start.3 = (bf16[640,128]{1,0:T(8,128)(2,1)}, bf16[640,128]{1,0:T(8,128)(2,1)S(1)}, u32[]{:S(2)}, u32[]{:S(2)}) collective-permute-start(bf16[640,128]{1,0:T(8,128)(2,1)} %pack.1.refs_0_), channel_id=1, source_target_pairs={{0,4},{2,6},{4,0},{6,2},{1,5},{3,7},{5,1},{7,3},{8,12},{10,14},{12... | collective-permute-start | bytes 491528 | tf_op jit(solution)/shard_map/ppermute | solution.py:205
  6.7 1.4 %collective-permute-start.2 = (bf16[640,128]{1,0:T(8,128)(2,1)}, bf16[640,128]{1,0:T(8,128)(2,1)S(1)}, u32[]{:S(2)}, u32[]{:S(2)}) collective-permute-start(bf16[640,128]{1,0:T(8,128)(2,1)} %pack.1.refs_0_), channel_id=1, source_target_pairs={{0,6},{2,4},{4,2},{6,0},{1,7},{3,5},{5,3},{7,1},{8,14},{10,12},{12... | collective-permute-start | bytes 491528 | tf_op jit(solution)/shard_map/ppermute | solution.py:205
  8.0 0.2 collective-permute-start.1
  8.3 0.1 pad_add_fusion.place_ref
  8.3 0.0 collective-permute-done.refs_1_
  8.3 0.0 copy-start.3
  8.3 0.0 copy-start.4
  8.3 0.0 copy-done.2
  8.3 0.6 %copy-done.3 = s32[4]{0:T(128)S(1)} copy-done((s32[4]{0:T(128)S(1)}, s32[4]{0:T(128)}, u32[]{:S(2)}) %copy-start.3) | copy-done | bytes 40
  9.0 0.0 copy-done.4
  9.0 0.0 copy-start
  9.0 0.9 %copy-done = bf16[640,128]{1,0:T(8,128)(2,1)S(1)} copy-done((bf16[640,128]{1,0:T(8,128)(2,1)S(1)}, bf16[640,128]{1,0:T(8,128)(2,1)}, u32[]{:S(2)}) %copy-start) | copy-done | bytes 163864
  9.9 0.0 copy-start.1
  9.9 1.0 %copy-done.1 = bf16[1,2,256,4,1,128]{5,3,4,2,1,0:T(4,128)(2,1)S(1)} copy-done((bf16[1,2,256,4,1,128]{5,3,4,2,1,0:T(4,128)(2,1)S(1)}, bf16[1,2,256,4,1,128]{5,3,4,2,1,0:T(4,128)(2,1)}, u32[]{:S(2)}) %copy-start.1) | copy-done | bytes 524312
  11.0 1.4 %prepare.1 = (bf16[2,256,512]{2,1,0:T(8,128)(2,1)S(1)}, bf16[512,512]{1,0:T(8,128)(2,1)S(1)}, f32[256,128]{1,0:T(8,128)S(1)}, bf16[256,320]{1,0:T(8,128)(2,1)S(1...) custom-call(s32[4]{0:T(128)S(1)} %copy-done.3, ...), custom_call_target="tpu_custom_call" | custom-call | flops 134217728 | bytes 1048576 | tf_op jit(solution)/shard_map/prepare/pallas_call | solution.py:266
  12.4 2.5 %collective-permute-start.7 = (f32[256,128]{1,0:T(8,128)S(1)}, f32[256,128]{1,0:T(8,128)S(1)}, u32[]{:S(2)}, u32[]{:S(2)}) collective-permute-start(f32[256,128]{1,0:T(8,128)S(1)} %get-tuple-element.29), channel_id=1, source_target_pairs={{0,24},{8,16},{16,8},{24,0},{1,25},{9,17},{17,9},{25,1},{2,26},{10... | collective-permute-start | bytes 393224 | tf_op jit(solution)/shard_map/ppermute | solution.py:205
  14.9 0.5 %collective-permute-start.6 = (f32[256,128]{1,0:T(8,128)S(1)}, f32[256,128]{1,0:T(8,128)S(1)}, u32[]{:S(2)}, u32[]{:S(2)}) collective-permute-start(f32[256,128]{1,0:T(8,128)S(1)} %get-tuple-element.29), channel_id=1, source_target_pairs={{0,16},{8,24},{16,0},{24,8},{1,17},{9,25},{17,1},{25,9},{2,18},{10... | collective-permute-start | bytes 393224 | tf_op jit(solution)/shard_map/ppermute | solution.py:205
  15.4 3.6 %collective-permute-done.3.refs_3_ = bf16[640,128]{1,0:T(8,128)(2,1)S(1)} collective-permute-done((bf16[640,128]{1,0:T(8,128)(2,1)}, bf16[640,128]{1,0:T(8,128)(2,1)S(1)}, u32[]{:S(2)}, u32[]{:S(2)}) %collective-permute-start.3) | collective-permute-done | bytes 163872 | tf_op jit(solution)/shard_map/ppermute | solution.py:205
  19.0 1.7 %collective-permute-start.5 = (f32[256,128]{1,0:T(8,128)S(1)}, f32[256,128]{1,0:T(8,128)S(1)}, u32[]{:S(2)}, u32[]{:S(2)}) collective-permute-start(f32[256,128]{1,0:T(8,128)S(1)} %get-tuple-element.29), channel_id=1, source_target_pairs={{0,8},{8,0},{16,24},{24,16},{1,9},{9,1},{17,25},{25,17},{2,10},{10... | collective-permute-start | bytes 393224 | tf_op jit(solution)/shard_map/ppermute | solution.py:205
  20.8 0.0 collective-permute-done.2.refs_2_
  20.8 0.0 collective-permute-done.1.refs_1_
  20.8 2.0 %compute.1 = (f32[160,256]{1,0:T(8,128)S(1)}, f32[160,256]{1,0:T(8,128)S(1)}, f32[160,128]{1,0:T(8,128)S(1)}, f32[160,128]{1,0:T(8,128)S(1)}) custom-call(s32[4]{0:T(128)S(1)} %copy-done.3, f32[1,2]{1,0:T(1,128)S(1)} %copy-done.4, s32[2]{0:T(128)S(1)} %pad_add_fusion.place_ref, bf16[2,256,512]{2,1,0:T(8,128)(2,1)S(1)} %get-tuple-element.23.straight_ref, ...), custom_call_target="tpu_custom_call" | custom-call | tf_op jit(solution)/shard_map/compute/pallas_call | solution.py:293
  22.8 0.1 collective-permute-start.4
  22.8 1.3 %collective-permute-done.4 = f32[160,128]{1,0:T(8,128)S(1)} collective-permute-done((f32[160,128]{1,0:T(8,128)S(1)}, f32[160,128]{1,0:T(8,128)S(1)}, u32[]{:S(2)}, u32[]{:S(2)}) %collective-permute-start.4) | collective-permute-done | bytes 81952 | tf_op jit(solution)/shard_map/ppermute | solution.py:205
  24.1 0.0 collective-permute-done.7
  24.1 0.0 collective-permute-done.6
  24.1 0.0 collective-permute-done.5
  24.2 0.2 collective-permute-start.8
  24.4 3.6 %collective-permute-start.13 = (f32[160,128]{1,0:T(8,128)S(1)}, f32[160,128]{1,0:T(8,128)S(1)}, u32[]{:S(2)}, u32[]{:S(2)}) collective-permute-start(f32[160,128]{1,0:T(8,128)S(1)} %add.39), channel_id=1, source_target_pairs={{0,6},{2,4},{4,2},{6,0},{1,7},{3,5},{5,3},{7,1},{8,14},{10,12},{12... | collective-permute-start | bytes 245768 | tf_op jit(solution)/shard_map/ppermute | solution.py:205
  28.0 0.0 collective-permute-done.8
  28.0 2.5 %collective-permute-start.11 = (f32[160,256]{1,0:T(8,128)S(1)}, f32[160,256]{1,0:T(8,128)S(1)}, u32[]{:S(2)}, u32[]{:S(2)}) collective-permute-start(f32[160,256]{1,0:T(8,128)S(1)} %add.43), channel_id=1, source_target_pairs={{0,24},{8,16},{16,8},{24,0},{1,25},{9,17},{17,9},{25,1},{2,26},{10... | collective-permute-start | bytes 491528 | tf_op jit(solution)/shard_map/ppermute | solution.py:205
  30.6 0.5 %collective-permute-start.10 = (f32[160,256]{1,0:T(8,128)S(1)}, f32[160,256]{1,0:T(8,128)S(1)}, u32[]{:S(2)}, u32[]{:S(2)}) collective-permute-start(f32[160,256]{1,0:T(8,128)S(1)} %add.43), channel_id=1, source_target_pairs={{0,16},{8,24},{16,0},{24,8},{1,17},{9,25},{17,1},{25,9},{2,18},{10... | collective-permute-start | bytes 491528 | tf_op jit(solution)/shard_map/ppermute | solution.py:205
  31.1 0.5 %collective-permute-start.9 = (f32[160,256]{1,0:T(8,128)S(1)}, f32[160,256]{1,0:T(8,128)S(1)}, u32[]{:S(2)}, u32[]{:S(2)}) collective-permute-start(f32[160,256]{1,0:T(8,128)S(1)} %add.43), channel_id=1, source_target_pairs={{0,8},{8,0},{16,24},{24,16},{1,9},{9,1},{17,25},{25,17},{2,10},{10... | collective-permute-start | bytes 491528 | tf_op jit(solution)/shard_map/ppermute | solution.py:205
  31.6 0.0 collective-permute-done.13
  31.6 1.8 %collective-permute-start.14 = (f32[160,128]{1,0:T(8,128)S(1)}, f32[160,128]{1,0:T(8,128)S(1)}, u32[]{:S(2)}, u32[]{:S(2)}) collective-permute-start(f32[160,128]{1,0:T(8,128)S(1)} %add.47), channel_id=1, source_target_pairs={{0,2},{2,0},{4,6},{6,4},{1,3},{3,1},{5,7},{7,5},{8,10},{10,8},{12,... | collective-permute-start | bytes 245768 | tf_op jit(solution)/shard_map/ppermute | solution.py:205
  33.5 0.0 collective-permute-start.18
  33.5 2.7 %collective-permute-done.14 = f32[160,128]{1,0:T(8,128)S(1)} collective-permute-done((f32[160,128]{1,0:T(8,128)S(1)}, f32[160,128]{1,0:T(8,128)S(1)}, u32[]{:S(2)}, u32[]{:S(2)}) %collective-permute-start.14) | collective-permute-done | bytes 81952 | tf_op jit(solution)/shard_map/ppermute | solution.py:205
  36.2 2.5 %collective-permute-start.17 = (f32[160,128]{1,0:T(8,128)S(1)}, f32[160,128]{1,0:T(8,128)S(1)}, u32[]{:S(2)}, u32[]{:S(2)}) collective-permute-start(f32[160,128]{1,0:T(8,128)S(1)} %add.48), channel_id=1, source_target_pairs={{0,24},{8,16},{16,8},{24,0},{1,25},{9,17},{17,9},{25,1},{2,26},{10... | collective-permute-start | bytes 245768 | tf_op jit(solution)/shard_map/ppermute | solution.py:205
  38.7 0.0 collective-permute-done.11
  38.7 0.5 %collective-permute-start.16 = (f32[160,128]{1,0:T(8,128)S(1)}, f32[160,128]{1,0:T(8,128)S(1)}, u32[]{:S(2)}, u32[]{:S(2)}) collective-permute-start(f32[160,128]{1,0:T(8,128)S(1)} %add.48), channel_id=1, source_target_pairs={{0,16},{8,24},{16,0},{24,8},{1,17},{9,25},{17,1},{25,9},{2,18},{10... | collective-permute-start | bytes 245768 | tf_op jit(solution)/shard_map/ppermute | solution.py:205
  39.2 0.0 collective-permute-done.10
  39.2 1.1 %collective-permute-start.15 = (f32[160,128]{1,0:T(8,128)S(1)}, f32[160,128]{1,0:T(8,128)S(1)}, u32[]{:S(2)}, u32[]{:S(2)}) collective-permute-start(f32[160,128]{1,0:T(8,128)S(1)} %add.48), channel_id=1, source_target_pairs={{0,8},{8,0},{16,24},{24,16},{1,9},{9,1},{17,25},{25,17},{2,10},{10... | collective-permute-start | bytes 245768 | tf_op jit(solution)/shard_map/ppermute | solution.py:205
  40.3 0.0 collective-permute-done.9
  40.3 0.1 collective-permute-start.12
  40.4 1.3 %collective-permute-done.17 = f32[160,128]{1,0:T(8,128)S(1)} collective-permute-done((f32[160,128]{1,0:T(8,128)S(1)}, f32[160,128]{1,0:T(8,128)S(1)}, u32[]{:S(2)}, u32[]{:S(2)}) %collective-permute-start.17) | collective-permute-done | bytes 81952 | tf_op jit(solution)/shard_map/ppermute | solution.py:205
  41.7 1.4 %collective-permute-done.16 = f32[160,128]{1,0:T(8,128)S(1)} collective-permute-done((f32[160,128]{1,0:T(8,128)S(1)}, f32[160,128]{1,0:T(8,128)S(1)}, u32[]{:S(2)}, u32[]{:S(2)}) %collective-permute-start.16) | collective-permute-done | bytes 81952 | tf_op jit(solution)/shard_map/ppermute | solution.py:205
  43.1 0.5 %collective-permute-done.15 = f32[160,128]{1,0:T(8,128)S(1)} collective-permute-done((f32[160,128]{1,0:T(8,128)S(1)}, f32[160,128]{1,0:T(8,128)S(1)}, u32[]{:S(2)}, u32[]{:S(2)}) %collective-permute-start.15) | collective-permute-done | bytes 81952 | tf_op jit(solution)/shard_map/ppermute | solution.py:205
  43.7 0.1 collective-permute-start.19
  43.7 0.0 collective-permute-done.18.other_term_ref
  43.7 0.0 collective-permute-done.12.other_d_ref
  43.8 1.1 %expand.1 = (f32[256,256]{1,0:T(8,128)}, f32[512,128]{1,0:T(8,128)S(1)}) custom-call(bf16[256,320]{1,0:T(8,128)(2,1)S(1)} %get-tuple-element.19.pick_d_ref, bf16[512,160]{1,0:T(8,128)(2,1)S(1)} %get-tuple-element.20.pick_ref, f32[512,128]{1,0:T(8,128)S(1)} %get-tuple-element.21.keep_ref, f32[8,128]{1,0:T(8,128)S(1)} %get-tuple-element.22.upper_ref, ...), custom_call_target="tpu_custom_call" | custom-call | flops 503316480 | bytes 2097152 | tf_op jit(solution)/shard_map/expand/pallas_call | solution.py:323
  44.9 0.1 collective-permute-done.19.other_t_ref
  45.0 1.0 %finish.1 = f32[512,128]{1,0:T(8,128)} custom-call(bf16[512,160]{1,0:T(8,128)(2,1)S(1)} %get-tuple-element.34.pick_ref, f32[512,128]{1,0:T(8,128)S(1)} %get-tuple-element.21.keep_ref, f32[160,128]{1,0:T(8,128)S(1)} %collective-permute-done.19.other_t_ref, f32[512,128]{1,0:T(8,128)S(1)} %get-tuple-element.35.partial_ref), custom_call_target="tpu_custom_call" | custom-call | tf_op jit(solution)/shard_map/finish/pallas_call | solution.py:342
  (7 shorter events, 0.1 us)
Async XLA Ops:
  0.6 7.7 %copy-start.2 = (bf16[1,2,512,128]{3,2,1,0:T(8,128)(2,1)S(1)}, bf16[1,2,512,128]{3,2,1,0:T(8,128)(2,1)}, u32[]{:S(2)}) copy-start(bf16[1,2,512,128]{3,2,1,0:T(8,128)(2,1)} %param.10) | copy-start | bytes 786436
  2.6 5.7 %collective-permute-start = (bf16[640,128]{1,0:T(8,128)(2,1)}, bf16[640,128]{1,0:T(8,128)(2,1)S(1)}, u32[]{:S(2)}, u32[]{:S(2)}) collective-permute-start(bf16[640,128]{1,0:T(8,128)(2,1)} %pack.1.refs_0_), channel_id=1, source_target_pairs={{0,1},{1,0},{2,3},{3,2},{4,5},{5,4},{6,7},{7,6},{8,9},{9,8},{10,11... | collective-permute-start | bytes 491528 | tf_op jit(solution)/shard_map/ppermute | solution.py:205
  3.1 15.9 %collective-permute-start.3 = (bf16[640,128]{1,0:T(8,128)(2,1)}, bf16[640,128]{1,0:T(8,128)(2,1)S(1)}, u32[]{:S(2)}, u32[]{:S(2)}) collective-permute-start(bf16[640,128]{1,0:T(8,128)(2,1)} %pack.1.refs_0_), channel_id=1, source_target_pairs={{0,4},{2,6},{4,0},{6,2},{1,5},{3,7},{5,1},{7,3},{8,12},{10,14},{12... | collective-permute-start | bytes 491528 | tf_op jit(solution)/shard_map/ppermute | solution.py:205
  6.7 14.1 %collective-permute-start.2 = (bf16[640,128]{1,0:T(8,128)(2,1)}, bf16[640,128]{1,0:T(8,128)(2,1)S(1)}, u32[]{:S(2)}, u32[]{:S(2)}) collective-permute-start(bf16[640,128]{1,0:T(8,128)(2,1)} %pack.1.refs_0_), channel_id=1, source_target_pairs={{0,6},{2,4},{4,2},{6,0},{1,7},{3,5},{5,3},{7,1},{8,14},{10,12},{12... | collective-permute-start | bytes 491528 | tf_op jit(solution)/shard_map/ppermute | solution.py:205
  8.0 12.7 %collective-permute-start.1 = (bf16[640,128]{1,0:T(8,128)(2,1)}, bf16[640,128]{1,0:T(8,128)(2,1)S(1)}, u32[]{:S(2)}, u32[]{:S(2)}) collective-permute-start(bf16[640,128]{1,0:T(8,128)(2,1)} %pack.1.refs_0_), channel_id=1, source_target_pairs={{0,2},{2,0},{4,6},{6,4},{1,3},{3,1},{5,7},{7,5},{8,10},{10,8},{12,... | collective-permute-start | bytes 491528 | tf_op jit(solution)/shard_map/ppermute | solution.py:205
  8.3 0.7 %copy-start.3 = (s32[4]{0:T(128)S(1)}, s32[4]{0:T(128)}, u32[]{:S(2)}) copy-start(s32[4]{0:T(128)} %widths_ref.5) | copy-start | bytes 52
  8.3 0.7 %copy-start.4 = (f32[1,2]{1,0:T(1,128)S(1)}, f32[1,2]{1,0:T(1,128)}, u32[]{:S(2)}) copy-start(f32[1,2]{1,0:T(1,128)} %weights_ref.3) | copy-start | bytes 28
  9.0 0.9 %copy-start = (bf16[640,128]{1,0:T(8,128)(2,1)S(1)}, bf16[640,128]{1,0:T(8,128)(2,1)}, u32[]{:S(2)}) copy-start(bf16[640,128]{1,0:T(8,128)(2,1)} %pack.1.refs_0_) | copy-start | bytes 491524
  9.9 1.0 %copy-start.1 = (bf16[1,2,256,4,1,128]{5,3,4,2,1,0:T(4,128)(2,1)S(1)}, bf16[1,2,256,4,1,128]{5,3,4,2,1,0:T(4,128)(2,1)}, u32[]{:S(2)}) copy-start(bf16[1,2,256,4,1,128]{5,3,4,2,1,0:T(4,128)(2,1)} %param.6) | copy-start | bytes 1572868
  12.4 11.8 %collective-permute-start.7 = (f32[256,128]{1,0:T(8,128)S(1)}, f32[256,128]{1,0:T(8,128)S(1)}, u32[]{:S(2)}, u32[]{:S(2)}) collective-permute-start(f32[256,128]{1,0:T(8,128)S(1)} %get-tuple-element.29), channel_id=1, source_target_pairs={{0,24},{8,16},{16,8},{24,0},{1,25},{9,17},{17,9},{25,1},{2,26},{10... | collective-permute-start | bytes 393224 | tf_op jit(solution)/shard_map/ppermute | solution.py:205
  14.9 9.3 %collective-permute-start.6 = (f32[256,128]{1,0:T(8,128)S(1)}, f32[256,128]{1,0:T(8,128)S(1)}, u32[]{:S(2)}, u32[]{:S(2)}) collective-permute-start(f32[256,128]{1,0:T(8,128)S(1)} %get-tuple-element.29), channel_id=1, source_target_pairs={{0,16},{8,24},{16,0},{24,8},{1,17},{9,25},{17,1},{25,9},{2,18},{10... | collective-permute-start | bytes 393224 | tf_op jit(solution)/shard_map/ppermute | solution.py:205
  19.0 5.1 %collective-permute-start.5 = (f32[256,128]{1,0:T(8,128)S(1)}, f32[256,128]{1,0:T(8,128)S(1)}, u32[]{:S(2)}, u32[]{:S(2)}) collective-permute-start(f32[256,128]{1,0:T(8,128)S(1)} %get-tuple-element.29), channel_id=1, source_target_pairs={{0,8},{8,0},{16,24},{24,16},{1,9},{9,1},{17,25},{25,17},{2,10},{10... | collective-permute-start | bytes 393224 | tf_op jit(solution)/shard_map/ppermute | solution.py:205
  22.8 1.3 %collective-permute-start.4 = (f32[160,128]{1,0:T(8,128)S(1)}, f32[160,128]{1,0:T(8,128)S(1)}, u32[]{:S(2)}, u32[]{:S(2)}) collective-permute-start(f32[160,128]{1,0:T(8,128)S(1)} %get-tuple-element.27), channel_id=1, source_target_pairs={{0,1},{1,0},{2,3},{3,2},{4,5},{5,4},{6,7},{7,6},{8,9},{9,8},{10,11... | collective-permute-start | bytes 245768 | tf_op jit(solution)/shard_map/ppermute | solution.py:205
  24.2 3.8 %collective-permute-start.8 = (f32[160,256]{1,0:T(8,128)S(1)}, f32[160,256]{1,0:T(8,128)S(1)}, u32[]{:S(2)}, u32[]{:S(2)}) collective-permute-start(f32[160,256]{1,0:T(8,128)S(1)} %get-tuple-element.30), channel_id=1, source_target_pairs={{0,1},{1,0},{2,3},{3,2},{4,5},{5,4},{6,7},{7,6},{8,9},{9,8},{10,11... | collective-permute-start | bytes 491528 | tf_op jit(solution)/shard_map/ppermute | solution.py:205
  24.4 7.2 %collective-permute-start.13 = (f32[160,128]{1,0:T(8,128)S(1)}, f32[160,128]{1,0:T(8,128)S(1)}, u32[]{:S(2)}, u32[]{:S(2)}) collective-permute-start(f32[160,128]{1,0:T(8,128)S(1)} %add.39), channel_id=1, source_target_pairs={{0,6},{2,4},{4,2},{6,0},{1,7},{3,5},{5,3},{7,1},{8,14},{10,12},{12... | collective-permute-start | bytes 245768 | tf_op jit(solution)/shard_map/ppermute | solution.py:205
  28.0 10.6 %collective-permute-start.11 = (f32[160,256]{1,0:T(8,128)S(1)}, f32[160,256]{1,0:T(8,128)S(1)}, u32[]{:S(2)}, u32[]{:S(2)}) collective-permute-start(f32[160,256]{1,0:T(8,128)S(1)} %add.43), channel_id=1, source_target_pairs={{0,24},{8,16},{16,8},{24,0},{1,25},{9,17},{17,9},{25,1},{2,26},{10... | collective-permute-start | bytes 491528 | tf_op jit(solution)/shard_map/ppermute | solution.py:205
  30.6 8.6 %collective-permute-start.10 = (f32[160,256]{1,0:T(8,128)S(1)}, f32[160,256]{1,0:T(8,128)S(1)}, u32[]{:S(2)}, u32[]{:S(2)}) collective-permute-start(f32[160,256]{1,0:T(8,128)S(1)} %add.43), channel_id=1, source_target_pairs={{0,16},{8,24},{16,0},{24,8},{1,17},{9,25},{17,1},{25,9},{2,18},{10... | collective-permute-start | bytes 491528 | tf_op jit(solution)/shard_map/ppermute | solution.py:205
  31.1 9.2 %collective-permute-start.9 = (f32[160,256]{1,0:T(8,128)S(1)}, f32[160,256]{1,0:T(8,128)S(1)}, u32[]{:S(2)}, u32[]{:S(2)}) collective-permute-start(f32[160,256]{1,0:T(8,128)S(1)} %add.43), channel_id=1, source_target_pairs={{0,8},{8,0},{16,24},{24,16},{1,9},{9,1},{17,25},{25,17},{2,10},{10... | collective-permute-start | bytes 491528 | tf_op jit(solution)/shard_map/ppermute | solution.py:205
  31.6 4.5 %collective-permute-start.14 = (f32[160,128]{1,0:T(8,128)S(1)}, f32[160,128]{1,0:T(8,128)S(1)}, u32[]{:S(2)}, u32[]{:S(2)}) collective-permute-start(f32[160,128]{1,0:T(8,128)S(1)} %add.47), channel_id=1, source_target_pairs={{0,2},{2,0},{4,6},{6,4},{1,3},{3,1},{5,7},{7,5},{8,10},{10,8},{12,... | collective-permute-start | bytes 245768 | tf_op jit(solution)/shard_map/ppermute | solution.py:205
  33.5 10.3 %collective-permute-start.18 = (f32[256,128]{1,0:T(8,128)S(1)}, f32[256,128]{1,0:T(8,128)S(1)}, u32[]{:S(2)}, u32[]{:S(2)}) collective-permute-start(f32[256,128]{1,0:T(8,128)S(1)} %add_add_fusion.1.mine_term_ref), channel_id=1, source_target_pairs={{0,1},{1,0},{2,3},{3,2},{4,5},{5,4},{6,7},{7,6},{8,9},{9,8},{10,11... | collective-permute-start | bytes 393224 | tf_op jit(solution)/shard_map/ppermute | solution.py:205
  36.2 5.5 %collective-permute-start.17 = (f32[160,128]{1,0:T(8,128)S(1)}, f32[160,128]{1,0:T(8,128)S(1)}, u32[]{:S(2)}, u32[]{:S(2)}) collective-permute-start(f32[160,128]{1,0:T(8,128)S(1)} %add.48), channel_id=1, source_target_pairs={{0,24},{8,16},{16,8},{24,0},{1,25},{9,17},{17,9},{25,1},{2,26},{10... | collective-permute-start | bytes 245768 | tf_op jit(solution)/shard_map/ppermute | solution.py:205
  38.7 4.4 %collective-permute-start.16 = (f32[160,128]{1,0:T(8,128)S(1)}, f32[160,128]{1,0:T(8,128)S(1)}, u32[]{:S(2)}, u32[]{:S(2)}) collective-permute-start(f32[160,128]{1,0:T(8,128)S(1)} %add.48), channel_id=1, source_target_pairs={{0,16},{8,24},{16,0},{24,8},{1,17},{9,25},{17,1},{25,9},{2,18},{10... | collective-permute-start | bytes 245768 | tf_op jit(solution)/shard_map/ppermute | solution.py:205
  39.2 4.4 %collective-permute-start.15 = (f32[160,128]{1,0:T(8,128)S(1)}, f32[160,128]{1,0:T(8,128)S(1)}, u32[]{:S(2)}, u32[]{:S(2)}) collective-permute-start(f32[160,128]{1,0:T(8,128)S(1)} %add.48), channel_id=1, source_target_pairs={{0,8},{8,0},{16,24},{24,16},{1,9},{9,1},{17,25},{25,17},{2,10},{10... | collective-permute-start | bytes 245768 | tf_op jit(solution)/shard_map/ppermute | solution.py:205
  40.3 3.4 %collective-permute-start.12 = (f32[160,256]{1,0:T(8,128)S(1)}, f32[160,256]{1,0:T(8,128)S(1)}, u32[]{:S(2)}, u32[]{:S(2)}) collective-permute-start(f32[160,256]{1,0:T(8,128)S(1)} %add_add_fusion.mine_d_ref), channel_id=1, source_target_pairs={{0,1},{1,0},{2,3},{3,2},{4,5},{5,4},{6,7},{7,6},{8,9},{9,8},{10,11... | collective-permute-start | bytes 491528 | tf_op jit(solution)/shard_map/ppermute | solution.py:205
  43.7 1.3 %collective-permute-start.19 = (f32[160,128]{1,0:T(8,128)S(1)}, f32[160,128]{1,0:T(8,128)S(1)}, u32[]{:S(2)}, u32[]{:S(2)}) collective-permute-start(f32[160,128]{1,0:T(8,128)S(1)} %add_add_fusion.2.mine_t_ref), channel_id=1, source_target_pairs={{0,1},{1,0},{2,3},{3,2},{4,5},{5,4},{6,7},{7,6},{8,9},{9,8},{10,11... | collective-permute-start | bytes 245768 | tf_op jit(solution)/shard_map/ppermute | solution.py:205

commit v20 on v19

--- a/solution.py
+++ b/solution.py
@@ -313,7 +313,7 @@
     term = gather_but_last(term, "col")
     products = scatter_rest(products, "col")
     for bit in bits_of(row_count)[::-1]:
-        products = products + swap(products, "row", 2 * bit - 1)
+        products = products + swap(products, "row", bit)
     density = scatter_rest(keep_d + swap(send_d, "col", top), "col")
     density = sum_direct(density, "pole")
     products = sum_direct(products, "pole")

time: 46.2 us -> 47.9 us (1.037)
  waiting for transfers between devices: 10.9 us -> 14.3 us
  starting transfers between devices: 23.9 us -> 22.3 us
    ppermute x20, waiting for transfers between devices: 10.9 us -> 14.3 us  [swap(): lax.ppermute(value, axis, [(i, i ^ bit) for i in range(lax.axis_size(axis...]
    ppermute x20, starting transfers between devices: 23.9 us -> 22.3 us  [swap(): lax.ppermute(value, axis, [(i, i ^ bit) for i in range(lax.axis_size(axis...]
  transfers between devices with their start and end apart: 20 -> 20, of which waited for: 7 -> 8; matrix products, arithmetic and copies ran while one was open for 0% -> 0% of each run, Pallas kernels for 10% -> 9%
where the time goes in v20:
time: 47.9 us; the launch traced here: 47.7 us
  starting transfers between devices  22.3 us (47%)
  waiting for transfers between devices  14.3 us (30%)
  Pallas kernels  7.5 us (16%)
  local copies, waits for them, and re-layouts  2.63 us (5%)
  between operations  0.77 us (2%)
    ppermute x20, starting transfers between devices, swap(): lax.ppermute(value, axis, [(i, i ^ bit) for i in range(lax.axis_size(axis...  22.3 us
    ppermute x20, waiting for transfers between devices, swap(): lax.ppermute(value, axis, [(i, i ^ bit) for i in range(lax.axis_size(axis...  14.3 us
    unnamed x10, local copies, waits for them, and re-layouts  2.63 us
    pallas_call x1, Pallas kernels, per_device(): pl.pallas_call(functools.partial(pack_kernel, supernodes, slot), in_specs...  2 us
    pallas_call x1, Pallas kernels, per_device(): pl.pallas_call(functools.partial(compute_kernel, others, col_count, super...  1.99 us
    pallas_call x1, Pallas kernels, per_device(): pl.pallas_call(functools.partial(prepare_kernel, (row_count, col_count)),...  1.38 us
    pallas_call x1, Pallas kernels, per_device(): pl.pallas_call(expand_kernel, in_specs=[VMEM_SPEC] * 9, out_specs=[VMEM_S...  1.14 us
    pallas_call x1, Pallas kernels, per_device(): pl.pallas_call(finish_kernel, in_specs=[VMEM_SPEC] * 4, out_specs=VMEM_SP...  0.99 us
  transfers between devices with their start and end apart: 20, of which 8 were waited for; matrix products, arithmetic and copies ran while one was open for 0% of the time, Pallas kernels for 9%

profile of v20, /device:TPU:0, one launch (start us, length us, event | category | flops | bytes accessed | tf_op | source)
XLA Modules:
  0.0 47.7 jit_solution(7213608689652378710)
XLA Ops:
  0.6 0.0 copy-start.2
  0.6 2.0 %pack.1.refs_0_ = bf16[640,128]{1,0:T(8,128)(2,1)} custom-call(s32[1,4]{1,0:T(1,128)} %pattern_ref.1, s32[4]{0:T(128)} %widths_ref.5, bf16[2,128,512]{2,1,0:T(8,128)(2,1)} %bitcast.7), custom_call_target="tpu_custom_call" | custom-call | tf_op jit(solution)/shard_map/pack/pallas_call | solution.py:252
  2.6 0.5 collective-permute-start
  3.1 3.6 %collective-permute-start.3 = (bf16[640,128]{1,0:T(8,128)(2,1)}, bf16[640,128]{1,0:T(8,128)(2,1)S(1)}, u32[]{:S(2)}, u32[]{:S(2)}) collective-permute-start(bf16[640,128]{1,0:T(8,128)(2,1)} %pack.1.refs_0_), channel_id=1, source_target_pairs={{0,4},{2,6},{4,0},{6,2},{1,5},{3,7},{5,1},{7,3},{8,12},{10,14},{12... | collective-permute-start | bytes 491528 | tf_op jit(solution)/shard_map/ppermute | solution.py:205
  6.7 1.4 %collective-permute-start.2 = (bf16[640,128]{1,0:T(8,128)(2,1)}, bf16[640,128]{1,0:T(8,128)(2,1)S(1)}, u32[]{:S(2)}, u32[]{:S(2)}) collective-permute-start(bf16[640,128]{1,0:T(8,128)(2,1)} %pack.1.refs_0_), channel_id=1, source_target_pairs={{0,6},{2,4},{4,2},{6,0},{1,7},{3,5},{5,3},{7,1},{8,14},{10,12},{12... | collective-permute-start | bytes 491528 | tf_op jit(solution)/shard_map/ppermute | solution.py:205
  8.0 0.2 collective-permute-start.1
  8.3 0.1 pad_add_fusion.place_ref
  8.3 0.0 collective-permute-done.refs_1_
  8.3 0.0 copy-start.3
  8.3 0.0 copy-start.4
  8.3 0.0 copy-done.2
  8.3 0.6 %copy-done.3 = s32[4]{0:T(128)S(1)} copy-done((s32[4]{0:T(128)S(1)}, s32[4]{0:T(128)}, u32[]{:S(2)}) %copy-start.3) | copy-done | bytes 40
  9.0 0.0 copy-done.4
  9.0 0.0 copy-start
  9.0 0.9 %copy-done = bf16[640,128]{1,0:T(8,128)(2,1)S(1)} copy-done((bf16[640,128]{1,0:T(8,128)(2,1)S(1)}, bf16[640,128]{1,0:T(8,128)(2,1)}, u32[]{:S(2)}) %copy-start) | copy-done | bytes 163864
  9.9 0.0 copy-start.1
  9.9 1.0 %copy-done.1 = bf16[1,2,256,4,1,128]{5,3,4,2,1,0:T(4,128)(2,1)S(1)} copy-done((bf16[1,2,256,4,1,128]{5,3,4,2,1,0:T(4,128)(2,1)S(1)}, bf16[1,2,256,4,1,128]{5,3,4,2,1,0:T(4,128)(2,1)}, u32[]{:S(2)}) %copy-start.1) | copy-done | bytes 524312
  11.0 1.4 %prepare.1 = (bf16[2,256,512]{2,1,0:T(8,128)(2,1)S(1)}, bf16[512,512]{1,0:T(8,128)(2,1)S(1)}, f32[256,128]{1,0:T(8,128)S(1)}, bf16[256,320]{1,0:T(8,128)(2,1)S(1...) custom-call(s32[4]{0:T(128)S(1)} %copy-done.3, ...), custom_call_target="tpu_custom_call" | custom-call | flops 134217728 | bytes 1048576 | tf_op jit(solution)/shard_map/prepare/pallas_call | solution.py:266
  12.4 2.5 %collective-permute-start.7 = (f32[256,128]{1,0:T(8,128)S(1)}, f32[256,128]{1,0:T(8,128)S(1)}, u32[]{:S(2)}, u32[]{:S(2)}) collective-permute-start(f32[256,128]{1,0:T(8,128)S(1)} %get-tuple-element.29), channel_id=1, source_target_pairs={{0,24},{8,16},{16,8},{24,0},{1,25},{9,17},{17,9},{25,1},{2,26},{10... | collective-permute-start | bytes 393224 | tf_op jit(solution)/shard_map/ppermute | solution.py:205
  14.9 0.5 %collective-permute-start.6 = (f32[256,128]{1,0:T(8,128)S(1)}, f32[256,128]{1,0:T(8,128)S(1)}, u32[]{:S(2)}, u32[]{:S(2)}) collective-permute-start(f32[256,128]{1,0:T(8,128)S(1)} %get-tuple-element.29), channel_id=1, source_target_pairs={{0,16},{8,24},{16,0},{24,8},{1,17},{9,25},{17,1},{25,9},{2,18},{10... | collective-permute-start | bytes 393224 | tf_op jit(solution)/shard_map/ppermute | solution.py:205
  15.4 3.6 %collective-permute-done.3.refs_3_ = bf16[640,128]{1,0:T(8,128)(2,1)S(1)} collective-permute-done((bf16[640,128]{1,0:T(8,128)(2,1)}, bf16[640,128]{1,0:T(8,128)(2,1)S(1)}, u32[]{:S(2)}, u32[]{:S(2)}) %collective-permute-start.3) | collective-permute-done | bytes 163872 | tf_op jit(solution)/shard_map/ppermute | solution.py:205
  19.0 1.7 %collective-permute-start.5 = (f32[256,128]{1,0:T(8,128)S(1)}, f32[256,128]{1,0:T(8,128)S(1)}, u32[]{:S(2)}, u32[]{:S(2)}) collective-permute-start(f32[256,128]{1,0:T(8,128)S(1)} %get-tuple-element.29), channel_id=1, source_target_pairs={{0,8},{8,0},{16,24},{24,16},{1,9},{9,1},{17,25},{25,17},{2,10},{10... | collective-permute-start | bytes 393224 | tf_op jit(solution)/shard_map/ppermute | solution.py:205
  20.8 0.0 collective-permute-done.2.refs_2_
  20.8 0.0 collective-permute-done.1.refs_1_
  20.8 2.0 %compute.1 = (f32[160,256]{1,0:T(8,128)S(1)}, f32[160,256]{1,0:T(8,128)S(1)}, f32[160,128]{1,0:T(8,128)S(1)}, f32[160,128]{1,0:T(8,128)S(1)}) custom-call(s32[4]{0:T(128)S(1)} %copy-done.3, f32[1,2]{1,0:T(1,128)S(1)} %copy-done.4, s32[2]{0:T(128)S(1)} %pad_add_fusion.place_ref, bf16[2,256,512]{2,1,0:T(8,128)(2,1)S(1)} %get-tuple-element.23.straight_ref, ...), custom_call_target="tpu_custom_call" | custom-call | tf_op jit(solution)/shard_map/compute/pallas_call | solution.py:293
  22.8 0.1 collective-permute-start.4
  22.8 1.3 %collective-permute-done.4 = f32[160,128]{1,0:T(8,128)S(1)} collective-permute-done((f32[160,128]{1,0:T(8,128)S(1)}, f32[160,128]{1,0:T(8,128)S(1)}, u32[]{:S(2)}, u32[]{:S(2)}) %collective-permute-start.4) | collective-permute-done | bytes 81952 | tf_op jit(solution)/shard_map/ppermute | solution.py:205
  24.1 0.0 collective-permute-done.7
  24.1 0.0 collective-permute-done.6
  24.1 0.0 collective-permute-done.5
  24.2 0.2 collective-permute-start.8
  24.4 4.2 %collective-permute-start.13 = (f32[160,128]{1,0:T(8,128)S(1)}, f32[160,128]{1,0:T(8,128)S(1)}, u32[]{:S(2)}, u32[]{:S(2)}) collective-permute-start(f32[160,128]{1,0:T(8,128)S(1)} %add.39), channel_id=1, source_target_pairs={{0,4},{2,6},{4,0},{6,2},{1,5},{3,7},{5,1},{7,3},{8,12},{10,14},{12... | collective-permute-start | bytes 245768 | tf_op jit(solution)/shard_map/ppermute | solution.py:205
  28.6 0.0 collective-permute-done.8
  28.6 2.5 %collective-permute-start.11 = (f32[160,256]{1,0:T(8,128)S(1)}, f32[160,256]{1,0:T(8,128)S(1)}, u32[]{:S(2)}, u32[]{:S(2)}) collective-permute-start(f32[160,256]{1,0:T(8,128)S(1)} %add.43), channel_id=1, source_target_pairs={{0,24},{8,16},{16,8},{24,0},{1,25},{9,17},{17,9},{25,1},{2,26},{10... | collective-permute-start | bytes 491528 | tf_op jit(solution)/shard_map/ppermute | solution.py:205
  31.2 0.5 %collective-permute-start.10 = (f32[160,256]{1,0:T(8,128)S(1)}, f32[160,256]{1,0:T(8,128)S(1)}, u32[]{:S(2)}, u32[]{:S(2)}) collective-permute-start(f32[160,256]{1,0:T(8,128)S(1)} %add.43), channel_id=1, source_target_pairs={{0,16},{8,24},{16,0},{24,8},{1,17},{9,25},{17,1},{25,9},{2,18},{10... | collective-permute-start | bytes 491528 | tf_op jit(solution)/shard_map/ppermute | solution.py:205
  31.7 0.5 %collective-permute-start.9 = (f32[160,256]{1,0:T(8,128)S(1)}, f32[160,256]{1,0:T(8,128)S(1)}, u32[]{:S(2)}, u32[]{:S(2)}) collective-permute-start(f32[160,256]{1,0:T(8,128)S(1)} %add.43), channel_id=1, source_target_pairs={{0,8},{8,0},{16,24},{24,16},{1,9},{9,1},{17,25},{25,17},{2,10},{10... | collective-permute-start | bytes 491528 | tf_op jit(solution)/shard_map/ppermute | solution.py:205
  32.2 1.1 %collective-permute-done.13 = f32[160,128]{1,0:T(8,128)S(1)} collective-permute-done((f32[160,128]{1,0:T(8,128)S(1)}, f32[160,128]{1,0:T(8,128)S(1)}, u32[]{:S(2)}, u32[]{:S(2)}) %collective-permute-start.13) | collective-permute-done | bytes 81952 | tf_op jit(solution)/shard_map/ppermute | solution.py:205
  33.4 0.1 collective-permute-start.14
  33.4 0.1 collective-permute-start.18
  33.5 4.3 %collective-permute-done.14 = f32[160,128]{1,0:T(8,128)S(1)} collective-permute-done((f32[160,128]{1,0:T(8,128)S(1)}, f32[160,128]{1,0:T(8,128)S(1)}, u32[]{:S(2)}, u32[]{:S(2)}) %collective-permute-start.14) | collective-permute-done | bytes 81952 | tf_op jit(solution)/shard_map/ppermute | solution.py:205
  37.9 2.5 %collective-permute-start.17 = (f32[160,128]{1,0:T(8,128)S(1)}, f32[160,128]{1,0:T(8,128)S(1)}, u32[]{:S(2)}, u32[]{:S(2)}) collective-permute-start(f32[160,128]{1,0:T(8,128)S(1)} %add.48), channel_id=1, source_target_pairs={{0,24},{8,16},{16,8},{24,0},{1,25},{9,17},{17,9},{25,1},{2,26},{10... | collective-permute-start | bytes 245768 | tf_op jit(solution)/shard_map/ppermute | solution.py:205
  40.4 0.0 collective-permute-done.11
  40.4 0.5 %collective-permute-start.16 = (f32[160,128]{1,0:T(8,128)S(1)}, f32[160,128]{1,0:T(8,128)S(1)}, u32[]{:S(2)}, u32[]{:S(2)}) collective-permute-start(f32[160,128]{1,0:T(8,128)S(1)} %add.48), channel_id=1, source_target_pairs={{0,16},{8,24},{16,0},{24,8},{1,17},{9,25},{17,1},{25,9},{2,18},{10... | collective-permute-start | bytes 245768 | tf_op jit(solution)/shard_map/ppermute | solution.py:205
  40.9 0.0 collective-permute-done.10
  40.9 0.5 %collective-permute-start.15 = (f32[160,128]{1,0:T(8,128)S(1)}, f32[160,128]{1,0:T(8,128)S(1)}, u32[]{:S(2)}, u32[]{:S(2)}) collective-permute-start(f32[160,128]{1,0:T(8,128)S(1)} %add.48), channel_id=1, source_target_pairs={{0,8},{8,0},{16,24},{24,16},{1,9},{9,1},{17,25},{25,17},{2,10},{10... | collective-permute-start | bytes 245768 | tf_op jit(solution)/shard_map/ppermute | solution.py:205
  41.4 0.0 collective-permute-done.9
  41.5 0.1 collective-permute-start.12
  41.6 2.2 %collective-permute-done.17 = f32[160,128]{1,0:T(8,128)S(1)} collective-permute-done((f32[160,128]{1,0:T(8,128)S(1)}, f32[160,128]{1,0:T(8,128)S(1)}, u32[]{:S(2)}, u32[]{:S(2)}) %collective-permute-start.17) | collective-permute-done | bytes 81952 | tf_op jit(solution)/shard_map/ppermute | solution.py:205
  43.8 1.1 %collective-permute-done.16 = f32[160,128]{1,0:T(8,128)S(1)} collective-permute-done((f32[160,128]{1,0:T(8,128)S(1)}, f32[160,128]{1,0:T(8,128)S(1)}, u32[]{:S(2)}, u32[]{:S(2)}) %collective-permute-start.16) | collective-permute-done | bytes 81952 | tf_op jit(solution)/shard_map/ppermute | solution.py:205
  44.8 0.5 %collective-permute-done.15 = f32[160,128]{1,0:T(8,128)S(1)} collective-permute-done((f32[160,128]{1,0:T(8,128)S(1)}, f32[160,128]{1,0:T(8,128)S(1)}, u32[]{:S(2)}, u32[]{:S(2)}) %collective-permute-start.15) | collective-permute-done | bytes 81952 | tf_op jit(solution)/shard_map/ppermute | solution.py:205
  45.4 0.1 collective-permute-start.19
  45.4 0.0 collective-permute-done.18.other_term_ref
  45.5 0.0 collective-permute-done.12.other_d_ref
  45.5 1.1 %expand.1 = (f32[256,256]{1,0:T(8,128)}, f32[512,128]{1,0:T(8,128)S(1)}) custom-call(bf16[256,320]{1,0:T(8,128)(2,1)S(1)} %get-tuple-element.19.pick_d_ref, bf16[512,160]{1,0:T(8,128)(2,1)S(1)} %get-tuple-element.20.pick_ref, f32[512,128]{1,0:T(8,128)S(1)} %get-tuple-element.21.keep_ref, f32[8,128]{1,0:T(8,128)S(1)} %get-tuple-element.22.upper_ref, ...), custom_call_target="tpu_custom_call" | custom-call | flops 503316480 | bytes 2097152 | tf_op jit(solution)/shard_map/expand/pallas_call | solution.py:323
  46.6 0.1 collective-permute-done.19.other_t_ref
  46.7 1.0 %finish.1 = f32[512,128]{1,0:T(8,128)} custom-call(bf16[512,160]{1,0:T(8,128)(2,1)S(1)} %get-tuple-element.34.pick_ref, f32[512,128]{1,0:T(8,128)S(1)} %get-tuple-element.21.keep_ref, f32[160,128]{1,0:T(8,128)S(1)} %collective-permute-done.19.other_t_ref, f32[512,128]{1,0:T(8,128)S(1)} %get-tuple-element.35.partial_ref), custom_call_target="tpu_custom_call" | custom-call | tf_op jit(solution)/shard_map/finish/pallas_call | solution.py:342
  (7 shorter events, 0.1 us)
Async XLA Ops:
  0.6 7.7 %copy-start.2 = (bf16[1,2,512,128]{3,2,1,0:T(8,128)(2,1)S(1)}, bf16[1,2,512,128]{3,2,1,0:T(8,128)(2,1)}, u32[]{:S(2)}) copy-start(bf16[1,2,512,128]{3,2,1,0:T(8,128)(2,1)} %param.10) | copy-start | bytes 786436
  2.6 5.7 %collective-permute-start = (bf16[640,128]{1,0:T(8,128)(2,1)}, bf16[640,128]{1,0:T(8,128)(2,1)S(1)}, u32[]{:S(2)}, u32[]{:S(2)}) collective-permute-start(bf16[640,128]{1,0:T(8,128)(2,1)} %pack.1.refs_0_), channel_id=1, source_target_pairs={{0,1},{1,0},{2,3},{3,2},{4,5},{5,4},{6,7},{7,6},{8,9},{9,8},{10,11... | collective-permute-start | bytes 491528 | tf_op jit(solution)/shard_map/ppermute | solution.py:205
  3.1 15.9 %collective-permute-start.3 = (bf16[640,128]{1,0:T(8,128)(2,1)}, bf16[640,128]{1,0:T(8,128)(2,1)S(1)}, u32[]{:S(2)}, u32[]{:S(2)}) collective-permute-start(bf16[640,128]{1,0:T(8,128)(2,1)} %pack.1.refs_0_), channel_id=1, source_target_pairs={{0,4},{2,6},{4,0},{6,2},{1,5},{3,7},{5,1},{7,3},{8,12},{10,14},{12... | collective-permute-start | bytes 491528 | tf_op jit(solution)/shard_map/ppermute | solution.py:205
  6.7 14.1 %collective-permute-start.2 = (bf16[640,128]{1,0:T(8,128)(2,1)}, bf16[640,128]{1,0:T(8,128)(2,1)S(1)}, u32[]{:S(2)}, u32[]{:S(2)}) collective-permute-start(bf16[640,128]{1,0:T(8,128)(2,1)} %pack.1.refs_0_), channel_id=1, source_target_pairs={{0,6},{2,4},{4,2},{6,0},{1,7},{3,5},{5,3},{7,1},{8,14},{10,12},{12... | collective-permute-start | bytes 491528 | tf_op jit(solution)/shard_map/ppermute | solution.py:205
  8.0 12.7 %collective-permute-start.1 = (bf16[640,128]{1,0:T(8,128)(2,1)}, bf16[640,128]{1,0:T(8,128)(2,1)S(1)}, u32[]{:S(2)}, u32[]{:S(2)}) collective-permute-start(bf16[640,128]{1,0:T(8,128)(2,1)} %pack.1.refs_0_), channel_id=1, source_target_pairs={{0,2},{2,0},{4,6},{6,4},{1,3},{3,1},{5,7},{7,5},{8,10},{10,8},{12,... | collective-permute-start | bytes 491528 | tf_op jit(solution)/shard_map/ppermute | solution.py:205
  8.3 0.7 %copy-start.3 = (s32[4]{0:T(128)S(1)}, s32[4]{0:T(128)}, u32[]{:S(2)}) copy-start(s32[4]{0:T(128)} %widths_ref.5) | copy-start | bytes 52
  8.3 0.7 %copy-start.4 = (f32[1,2]{1,0:T(1,128)S(1)}, f32[1,2]{1,0:T(1,128)}, u32[]{:S(2)}) copy-start(f32[1,2]{1,0:T(1,128)} %weights_ref.3) | copy-start | bytes 28
  9.0 0.9 %copy-start = (bf16[640,128]{1,0:T(8,128)(2,1)S(1)}, bf16[640,128]{1,0:T(8,128)(2,1)}, u32[]{:S(2)}) copy-start(bf16[640,128]{1,0:T(8,128)(2,1)} %pack.1.refs_0_) | copy-start | bytes 491524
  9.9 1.0 %copy-start.1 = (bf16[1,2,256,4,1,128]{5,3,4,2,1,0:T(4,128)(2,1)S(1)}, bf16[1,2,256,4,1,128]{5,3,4,2,1,0:T(4,128)(2,1)}, u32[]{:S(2)}) copy-start(bf16[1,2,256,4,1,128]{5,3,4,2,1,0:T(4,128)(2,1)} %param.6) | copy-start | bytes 1572868
  12.4 11.8 %collective-permute-start.7 = (f32[256,128]{1,0:T(8,128)S(1)}, f32[256,128]{1,0:T(8,128)S(1)}, u32[]{:S(2)}, u32[]{:S(2)}) collective-permute-start(f32[256,128]{1,0:T(8,128)S(1)} %get-tuple-element.29), channel_id=1, source_target_pairs={{0,24},{8,16},{16,8},{24,0},{1,25},{9,17},{17,9},{25,1},{2,26},{10... | collective-permute-start | bytes 393224 | tf_op jit(solution)/shard_map/ppermute | solution.py:205
  14.9 9.3 %collective-permute-start.6 = (f32[256,128]{1,0:T(8,128)S(1)}, f32[256,128]{1,0:T(8,128)S(1)}, u32[]{:S(2)}, u32[]{:S(2)}) collective-permute-start(f32[256,128]{1,0:T(8,128)S(1)} %get-tuple-element.29), channel_id=1, source_target_pairs={{0,16},{8,24},{16,0},{24,8},{1,17},{9,25},{17,1},{25,9},{2,18},{10... | collective-permute-start | bytes 393224 | tf_op jit(solution)/shard_map/ppermute | solution.py:205
  19.0 5.1 %collective-permute-start.5 = (f32[256,128]{1,0:T(8,128)S(1)}, f32[256,128]{1,0:T(8,128)S(1)}, u32[]{:S(2)}, u32[]{:S(2)}) collective-permute-start(f32[256,128]{1,0:T(8,128)S(1)} %get-tuple-element.29), channel_id=1, source_target_pairs={{0,8},{8,0},{16,24},{24,16},{1,9},{9,1},{17,25},{25,17},{2,10},{10... | collective-permute-start | bytes 393224 | tf_op jit(solution)/shard_map/ppermute | solution.py:205
  22.8 1.3 %collective-permute-start.4 = (f32[160,128]{1,0:T(8,128)S(1)}, f32[160,128]{1,0:T(8,128)S(1)}, u32[]{:S(2)}, u32[]{:S(2)}) collective-permute-start(f32[160,128]{1,0:T(8,128)S(1)} %get-tuple-element.27), channel_id=1, source_target_pairs={{0,1},{1,0},{2,3},{3,2},{4,5},{5,4},{6,7},{7,6},{8,9},{9,8},{10,11... | collective-permute-start | bytes 245768 | tf_op jit(solution)/shard_map/ppermute | solution.py:205
  24.2 4.4 %collective-permute-start.8 = (f32[160,256]{1,0:T(8,128)S(1)}, f32[160,256]{1,0:T(8,128)S(1)}, u32[]{:S(2)}, u32[]{:S(2)}) collective-permute-start(f32[160,256]{1,0:T(8,128)S(1)} %get-tuple-element.30), channel_id=1, source_target_pairs={{0,1},{1,0},{2,3},{3,2},{4,5},{5,4},{6,7},{7,6},{8,9},{9,8},{10,11... | collective-permute-start | bytes 491528 | tf_op jit(solution)/shard_map/ppermute | solution.py:205
  24.4 8.9 %collective-permute-start.13 = (f32[160,128]{1,0:T(8,128)S(1)}, f32[160,128]{1,0:T(8,128)S(1)}, u32[]{:S(2)}, u32[]{:S(2)}) collective-permute-start(f32[160,128]{1,0:T(8,128)S(1)} %add.39), channel_id=1, source_target_pairs={{0,4},{2,6},{4,0},{6,2},{1,5},{3,7},{5,1},{7,3},{8,12},{10,14},{12... | collective-permute-start | bytes 245768 | tf_op jit(solution)/shard_map/ppermute | solution.py:205
  28.6 11.7 %collective-permute-start.11 = (f32[160,256]{1,0:T(8,128)S(1)}, f32[160,256]{1,0:T(8,128)S(1)}, u32[]{:S(2)}, u32[]{:S(2)}) collective-permute-start(f32[160,256]{1,0:T(8,128)S(1)} %add.43), channel_id=1, source_target_pairs={{0,24},{8,16},{16,8},{24,0},{1,25},{9,17},{17,9},{25,1},{2,26},{10... | collective-permute-start | bytes 491528 | tf_op jit(solution)/shard_map/ppermute | solution.py:205
  31.2 9.7 %collective-permute-start.10 = (f32[160,256]{1,0:T(8,128)S(1)}, f32[160,256]{1,0:T(8,128)S(1)}, u32[]{:S(2)}, u32[]{:S(2)}) collective-permute-start(f32[160,256]{1,0:T(8,128)S(1)} %add.43), channel_id=1, source_target_pairs={{0,16},{8,24},{16,0},{24,8},{1,17},{9,25},{17,1},{25,9},{2,18},{10... | collective-permute-start | bytes 491528 | tf_op jit(solution)/shard_map/ppermute | solution.py:205
  31.7 9.8 %collective-permute-start.9 = (f32[160,256]{1,0:T(8,128)S(1)}, f32[160,256]{1,0:T(8,128)S(1)}, u32[]{:S(2)}, u32[]{:S(2)}) collective-permute-start(f32[160,256]{1,0:T(8,128)S(1)} %add.43), channel_id=1, source_target_pairs={{0,8},{8,0},{16,24},{24,16},{1,9},{9,1},{17,25},{25,17},{2,10},{10... | collective-permute-start | bytes 491528 | tf_op jit(solution)/shard_map/ppermute | solution.py:205
  33.4 4.5 %collective-permute-start.14 = (f32[160,128]{1,0:T(8,128)S(1)}, f32[160,128]{1,0:T(8,128)S(1)}, u32[]{:S(2)}, u32[]{:S(2)}) collective-permute-start(f32[160,128]{1,0:T(8,128)S(1)} %add.47), channel_id=1, source_target_pairs={{0,2},{2,0},{4,6},{6,4},{1,3},{3,1},{5,7},{7,5},{8,10},{10,8},{12,... | collective-permute-start | bytes 245768 | tf_op jit(solution)/shard_map/ppermute | solution.py:205
  33.4 12.0 %collective-permute-start.18 = (f32[256,128]{1,0:T(8,128)S(1)}, f32[256,128]{1,0:T(8,128)S(1)}, u32[]{:S(2)}, u32[]{:S(2)}) collective-permute-start(f32[256,128]{1,0:T(8,128)S(1)} %add_add_fusion.1.mine_term_ref), channel_id=1, source_target_pairs={{0,1},{1,0},{2,3},{3,2},{4,5},{5,4},{6,7},{7,6},{8,9},{9,8},{10,11... | collective-permute-start | bytes 393224 | tf_op jit(solution)/shard_map/ppermute | solution.py:205
  37.9 5.9 %collective-permute-start.17 = (f32[160,128]{1,0:T(8,128)S(1)}, f32[160,128]{1,0:T(8,128)S(1)}, u32[]{:S(2)}, u32[]{:S(2)}) collective-permute-start(f32[160,128]{1,0:T(8,128)S(1)} %add.48), channel_id=1, source_target_pairs={{0,24},{8,16},{16,8},{24,0},{1,25},{9,17},{17,9},{25,1},{2,26},{10... | collective-permute-start | bytes 245768 | tf_op jit(solution)/shard_map/ppermute | solution.py:205
  40.4 4.4 %collective-permute-start.16 = (f32[160,128]{1,0:T(8,128)S(1)}, f32[160,128]{1,0:T(8,128)S(1)}, u32[]{:S(2)}, u32[]{:S(2)}) collective-permute-start(f32[160,128]{1,0:T(8,128)S(1)} %add.48), channel_id=1, source_target_pairs={{0,16},{8,24},{16,0},{24,8},{1,17},{9,25},{17,1},{25,9},{2,18},{10... | collective-permute-start | bytes 245768 | tf_op jit(solution)/shard_map/ppermute | solution.py:205
  40.9 4.4 %collective-permute-start.15 = (f32[160,128]{1,0:T(8,128)S(1)}, f32[160,128]{1,0:T(8,128)S(1)}, u32[]{:S(2)}, u32[]{:S(2)}) collective-permute-start(f32[160,128]{1,0:T(8,128)S(1)} %add.48), channel_id=1, source_target_pairs={{0,8},{8,0},{16,24},{24,16},{1,9},{9,1},{17,25},{25,17},{2,10},{10... | collective-permute-start | bytes 245768 | tf_op jit(solution)/shard_map/ppermute | solution.py:205
  41.5 4.0 %collective-permute-start.12 = (f32[160,256]{1,0:T(8,128)S(1)}, f32[160,256]{1,0:T(8,128)S(1)}, u32[]{:S(2)}, u32[]{:S(2)}) collective-permute-start(f32[160,256]{1,0:T(8,128)S(1)} %add_add_fusion.mine_d_ref), channel_id=1, source_target_pairs={{0,1},{1,0},{2,3},{3,2},{4,5},{5,4},{6,7},{7,6},{8,9},{9,8},{10,11... | collective-permute-start | bytes 491528 | tf_op jit(solution)/shard_map/ppermute | solution.py:205
  45.4 1.3 %collective-permute-start.19 = (f32[160,128]{1,0:T(8,128)S(1)}, f32[160,128]{1,0:T(8,128)S(1)}, u32[]{:S(2)}, u32[]{:S(2)}) collective-permute-start(f32[160,128]{1,0:T(8,128)S(1)} %add_add_fusion.2.mine_t_ref), channel_id=1, source_target_pairs={{0,1},{1,0},{2,3},{3,2},{4,5},{5,4},{6,7},{7,6},{8,9},{9,8},{10,11... | collective-permute-start | bytes 245768 | tf_op jit(solution)/shard_map/ppermute | solution.py:205

commit v21 on v19

--- a/solution.py
+++ b/solution.py
@@ -288,7 +288,11 @@
         sup_widths, pole_weights, place,
         found_inverse.reshape(2 * local_rows * row_count, block), diag_inverse[0], *own,
     )
-    term = sum_direct(term, "pole")
+    later, blocks[1] = lax.optimization_barrier((term, blocks[1]))
+    term = tree_sum(
+        [term]
+        + [swap(later if j == 1 else term, "pole", j) for j in range(1, lax.axis_size("pole"))]
+    )
 
     keep_d, send_d, keep_t, send_t = pl.pallas_call(
         functools.partial(compute_kernel, others, col_count, supernodes, slot),

time: 46.2 us -> 46.3 us (level)
  waiting for transfers between devices: 10.9 us -> 13.3 us
  starting transfers between devices: 23.9 us -> 21.6 us
    ppermute x20, waiting for transfers between devices: 10.9 us -> 13.3 us  [swap(): lax.ppermute(value, axis, [(i, i ^ bit) for i in range(lax.axis_size(axis...]
    ppermute x20, starting transfers between devices: 23.9 us -> 21.6 us  [swap(): lax.ppermute(value, axis, [(i, i ^ bit) for i in range(lax.axis_size(axis...]
  transfers between devices with their start and end apart: 20 -> 20, of which waited for: 7 -> 10; matrix products, arithmetic and copies ran while one was open for 0% -> 0% of each run, Pallas kernels for 10% -> 10%
where the time goes in v21:
time: 46.3 us; the launch traced here: 46.1 us
  starting transfers between devices  21.6 us (47%)
  waiting for transfers between devices  13.3 us (29%)
  Pallas kernels  7.51 us (16%)
  local copies, waits for them, and re-layouts  2.63 us (6%)
  between operations  0.76 us (2%)
    ppermute x20, starting transfers between devices, swap(): lax.ppermute(value, axis, [(i, i ^ bit) for i in range(lax.axis_size(axis...  21.6 us
    ppermute x20, waiting for transfers between devices, swap(): lax.ppermute(value, axis, [(i, i ^ bit) for i in range(lax.axis_size(axis...  13.3 us
    unnamed x10, local copies, waits for them, and re-layouts  2.63 us
    pallas_call x1, Pallas kernels, per_device(): pl.pallas_call(functools.partial(pack_kernel, supernodes, slot), in_specs...  2 us
    pallas_call x1, Pallas kernels, per_device(): pl.pallas_call(functools.partial(compute_kernel, others, col_count, super...  1.99 us
    pallas_call x1, Pallas kernels, per_device(): pl.pallas_call(functools.partial(prepare_kernel, (row_count, col_count)),...  1.38 us
    pallas_call x1, Pallas kernels, per_device(): pl.pallas_call(expand_kernel, in_specs=[VMEM_SPEC] * 9, out_specs=[VMEM_S...  1.14 us
    pallas_call x1, Pallas kernels, per_device(): pl.pallas_call(finish_kernel, in_specs=[VMEM_SPEC] * 4, out_specs=VMEM_SP...  0.99 us
  transfers between devices with their start and end apart: 20, of which 10 were waited for; matrix products, arithmetic and copies ran while one was open for 0% of the time, Pallas kernels for 10%

profile of v21, /device:TPU:0, one launch (start us, length us, event | category | flops | bytes accessed | tf_op | source)
XLA Modules:
  0.0 46.1 jit_solution(13242262585673266492)
XLA Ops:
  0.6 0.0 copy-start.2
  0.6 2.0 %pack.1.refs_0_ = bf16[640,128]{1,0:T(8,128)(2,1)} custom-call(s32[1,4]{1,0:T(1,128)} %pattern_ref.1, s32[4]{0:T(128)} %widths_ref.5, bf16[2,128,512]{2,1,0:T(8,128)(2,1)} %bitcast.7), custom_call_target="tpu_custom_call" | custom-call | tf_op jit(solution)/shard_map/pack/pallas_call | solution.py:252
  2.6 0.5 collective-permute-start
  3.1 2.6 %collective-permute-start.1 = (bf16[640,128]{1,0:T(8,128)(2,1)}, bf16[640,128]{1,0:T(8,128)(2,1)S(1)}, u32[]{:S(2)}, u32[]{:S(2)}) collective-permute-start(bf16[640,128]{1,0:T(8,128)(2,1)} %pack.1.refs_0_), channel_id=1, source_target_pairs={{0,2},{2,0},{4,6},{6,4},{1,3},{3,1},{5,7},{7,5},{8,10},{10,8},{12,... | collective-permute-start | bytes 491528 | tf_op jit(solution)/shard_map/ppermute | solution.py:205
  5.7 2.6 %collective-permute-start.3 = (bf16[640,128]{1,0:T(8,128)(2,1)}, bf16[640,128]{1,0:T(8,128)(2,1)S(1)}, u32[]{:S(2)}, u32[]{:S(2)}) collective-permute-start(bf16[640,128]{1,0:T(8,128)(2,1)} %pack.1.refs_0_), channel_id=1, source_target_pairs={{0,4},{2,6},{4,0},{6,2},{1,5},{3,7},{5,1},{7,3},{8,12},{10,14},{12... | collective-permute-start | bytes 491528 | tf_op jit(solution)/shard_map/ppermute | solution.py:205
  8.3 0.0 collective-permute-start.2
  8.3 0.1 pad_add_fusion.place_ref
  8.3 0.0 collective-permute-done.refs_1_
  8.3 0.0 copy-start.3
  8.3 0.0 copy-start.4
  8.3 0.0 copy-done.2
  8.3 0.6 %copy-done.3 = s32[4]{0:T(128)S(1)} copy-done((s32[4]{0:T(128)S(1)}, s32[4]{0:T(128)}, u32[]{:S(2)}) %copy-start.3) | copy-done | bytes 40
  9.0 0.0 copy-done.4
  9.0 0.0 copy-start
  9.0 0.9 %copy-done = bf16[640,128]{1,0:T(8,128)(2,1)S(1)} copy-done((bf16[640,128]{1,0:T(8,128)(2,1)S(1)}, bf16[640,128]{1,0:T(8,128)(2,1)}, u32[]{:S(2)}) %copy-start) | copy-done | bytes 163864
  9.9 0.0 copy-start.1
  9.9 1.0 %copy-done.1 = bf16[1,2,256,4,1,128]{5,3,4,2,1,0:T(4,128)(2,1)S(1)} copy-done((bf16[1,2,256,4,1,128]{5,3,4,2,1,0:T(4,128)(2,1)S(1)}, bf16[1,2,256,4,1,128]{5,3,4,2,1,0:T(4,128)(2,1)}, u32[]{:S(2)}) %copy-start.1) | copy-done | bytes 524312
  11.0 1.4 %prepare.1 = (bf16[2,256,512]{2,1,0:T(8,128)(2,1)S(1)}, bf16[512,512]{1,0:T(8,128)(2,1)S(1)}, f32[256,128]{1,0:T(8,128)S(1)}, bf16[256,320]{1,0:T(8,128)(2,1)S(1...) custom-call(s32[4]{0:T(128)S(1)} %copy-done.3, ...), custom_call_target="tpu_custom_call" | custom-call | flops 134217728 | bytes 1048576 | tf_op jit(solution)/shard_map/prepare/pallas_call | solution.py:266
  12.4 1.5 %collective-permute-done.1.refs_1_ = bf16[640,128]{1,0:T(8,128)(2,1)S(1)} collective-permute-done((bf16[640,128]{1,0:T(8,128)(2,1)}, bf16[640,128]{1,0:T(8,128)(2,1)S(1)}, u32[]{:S(2)}, u32[]{:S(2)}) %collective-permute-start.1) | collective-permute-done | bytes 163872 | tf_op jit(solution)/shard_map/ppermute | solution.py:205
  13.8 1.7 %collective-permute-start.5 = (f32[256,128]{1,0:T(8,128)S(1)}, f32[256,128]{1,0:T(8,128)S(1)}, u32[]{:S(2)}, u32[]{:S(2)}) collective-permute-start(f32[256,128]{1,0:T(8,128)S(1)} %get-tuple-element.33), channel_id=1, source_target_pairs={{0,8},{8,0},{16,24},{24,16},{1,9},{9,1},{17,25},{25,17},{2,10},{10... | collective-permute-start | bytes 393224 | tf_op jit(solution)/shard_map/ppermute | solution.py:205
  15.5 1.5 %collective-permute-start.7 = (f32[256,128]{1,0:T(8,128)S(1)}, f32[256,128]{1,0:T(8,128)S(1)}, u32[]{:S(2)}, u32[]{:S(2)}) collective-permute-start(f32[256,128]{1,0:T(8,128)S(1)} %get-tuple-element.33), channel_id=1, source_target_pairs={{0,24},{8,16},{16,8},{24,0},{1,25},{9,17},{17,9},{25,1},{2,26},{10... | collective-permute-start | bytes 393224 | tf_op jit(solution)/shard_map/ppermute | solution.py:205
  17.0 0.3 collective-permute-start.6
  17.3 3.5 %collective-permute-done.3.refs_3_ = bf16[640,128]{1,0:T(8,128)(2,1)S(1)} collective-permute-done((bf16[640,128]{1,0:T(8,128)(2,1)}, bf16[640,128]{1,0:T(8,128)(2,1)S(1)}, u32[]{:S(2)}, u32[]{:S(2)}) %collective-permute-start.3) | collective-permute-done | bytes 163872 | tf_op jit(solution)/shard_map/ppermute | solution.py:205
  20.9 0.0 collective-permute-done.2.refs_2_
  20.9 2.0 %compute.1 = (f32[160,256]{1,0:T(8,128)S(1)}, f32[160,256]{1,0:T(8,128)S(1)}, f32[160,128]{1,0:T(8,128)S(1)}, f32[160,128]{1,0:T(8,128)S(1)}) custom-call(s32[4]{0:T(128)S(1)} %copy-done.3, f32[1,2]{1,0:T(1,128)S(1)} %copy-done.4, s32[2]{0:T(128)S(1)} %pad_add_fusion.place_ref, bf16[2,256,512]{2,1,0:T(8,128)(2,1)S(1)} %get-tuple-element.25.straight_ref, ...), custom_call_target="tpu_custom_call" | custom-call | tf_op jit(solution)/shard_map/compute/pallas_call | solution.py:297
  22.9 0.1 collective-permute-start.4
  23.0 1.3 %collective-permute-done.4 = f32[160,128]{1,0:T(8,128)S(1)} collective-permute-done((f32[160,128]{1,0:T(8,128)S(1)}, f32[160,128]{1,0:T(8,128)S(1)}, u32[]{:S(2)}, u32[]{:S(2)}) %collective-permute-start.4) | collective-permute-done | bytes 81952 | tf_op jit(solution)/shard_map/ppermute | solution.py:205
  24.2 0.0 collective-permute-done.5
  24.2 0.0 collective-permute-done.7
  24.3 0.1 collective-permute-done.6
  24.4 0.1 collective-permute-start.8
  24.5 2.8 %collective-permute-start.13 = (f32[160,128]{1,0:T(8,128)S(1)}, f32[160,128]{1,0:T(8,128)S(1)}, u32[]{:S(2)}, u32[]{:S(2)}) collective-permute-start(f32[160,128]{1,0:T(8,128)S(1)} %add.39), channel_id=1, source_target_pairs={{0,6},{2,4},{4,2},{6,0},{1,7},{3,5},{5,3},{7,1},{8,14},{10,12},{12... | collective-permute-start | bytes 245768 | tf_op jit(solution)/shard_map/ppermute | solution.py:205
  27.3 0.0 collective-permute-done.8
  27.3 2.2 %collective-permute-start.11 = (f32[160,256]{1,0:T(8,128)S(1)}, f32[160,256]{1,0:T(8,128)S(1)}, u32[]{:S(2)}, u32[]{:S(2)}) collective-permute-start(f32[160,256]{1,0:T(8,128)S(1)} %add.43), channel_id=1, source_target_pairs={{0,24},{8,16},{16,8},{24,0},{1,25},{9,17},{17,9},{25,1},{2,26},{10... | collective-permute-start | bytes 491528 | tf_op jit(solution)/shard_map/ppermute | solution.py:205
  29.5 0.8 %collective-permute-start.10 = (f32[160,256]{1,0:T(8,128)S(1)}, f32[160,256]{1,0:T(8,128)S(1)}, u32[]{:S(2)}, u32[]{:S(2)}) collective-permute-start(f32[160,256]{1,0:T(8,128)S(1)} %add.43), channel_id=1, source_target_pairs={{0,16},{8,24},{16,0},{24,8},{1,17},{9,25},{17,1},{25,9},{2,18},{10... | collective-permute-start | bytes 491528 | tf_op jit(solution)/shard_map/ppermute | solution.py:205
  30.4 0.5 %collective-permute-start.9 = (f32[160,256]{1,0:T(8,128)S(1)}, f32[160,256]{1,0:T(8,128)S(1)}, u32[]{:S(2)}, u32[]{:S(2)}) collective-permute-start(f32[160,256]{1,0:T(8,128)S(1)} %add.43), channel_id=1, source_target_pairs={{0,8},{8,0},{16,24},{24,16},{1,9},{9,1},{17,25},{25,17},{2,10},{10... | collective-permute-start | bytes 491528 | tf_op jit(solution)/shard_map/ppermute | solution.py:205
  30.9 0.3 collective-permute-done.13
  31.2 2.3 %collective-permute-start.14 = (f32[160,128]{1,0:T(8,128)S(1)}, f32[160,128]{1,0:T(8,128)S(1)}, u32[]{:S(2)}, u32[]{:S(2)}) collective-permute-start(f32[160,128]{1,0:T(8,128)S(1)} %add.47), channel_id=1, source_target_pairs={{0,2},{2,0},{4,6},{6,4},{1,3},{3,1},{5,7},{7,5},{8,10},{10,8},{12,... | collective-permute-start | bytes 245768 | tf_op jit(solution)/shard_map/ppermute | solution.py:205
  33.5 0.0 collective-permute-start.18
  33.5 2.7 %collective-permute-done.14 = f32[160,128]{1,0:T(8,128)S(1)} collective-permute-done((f32[160,128]{1,0:T(8,128)S(1)}, f32[160,128]{1,0:T(8,128)S(1)}, u32[]{:S(2)}, u32[]{:S(2)}) %collective-permute-start.14) | collective-permute-done | bytes 81952 | tf_op jit(solution)/shard_map/ppermute | solution.py:205
  36.2 2.4 %collective-permute-start.17 = (f32[160,128]{1,0:T(8,128)S(1)}, f32[160,128]{1,0:T(8,128)S(1)}, u32[]{:S(2)}, u32[]{:S(2)}) collective-permute-start(f32[160,128]{1,0:T(8,128)S(1)} %add.48), channel_id=1, source_target_pairs={{0,24},{8,16},{16,8},{24,0},{1,25},{9,17},{17,9},{25,1},{2,26},{10... | collective-permute-start | bytes 245768 | tf_op jit(solution)/shard_map/ppermute | solution.py:205
  38.6 0.0 collective-permute-done.11
  38.6 0.6 %collective-permute-start.16 = (f32[160,128]{1,0:T(8,128)S(1)}, f32[160,128]{1,0:T(8,128)S(1)}, u32[]{:S(2)}, u32[]{:S(2)}) collective-permute-start(f32[160,128]{1,0:T(8,128)S(1)} %add.48), channel_id=1, source_target_pairs={{0,16},{8,24},{16,0},{24,8},{1,17},{9,25},{17,1},{25,9},{2,18},{10... | collective-permute-start | bytes 245768 | tf_op jit(solution)/shard_map/ppermute | solution.py:205
  39.2 0.0 collective-permute-done.10
  39.3 0.5 %collective-permute-start.15 = (f32[160,128]{1,0:T(8,128)S(1)}, f32[160,128]{1,0:T(8,128)S(1)}, u32[]{:S(2)}, u32[]{:S(2)}) collective-permute-start(f32[160,128]{1,0:T(8,128)S(1)} %add.48), channel_id=1, source_target_pairs={{0,8},{8,0},{16,24},{24,16},{1,9},{9,1},{17,25},{25,17},{2,10},{10... | collective-permute-start | bytes 245768 | tf_op jit(solution)/shard_map/ppermute | solution.py:205
  39.8 0.0 collective-permute-done.9
  39.8 0.1 collective-permute-start.12
  39.9 1.8 %collective-permute-done.17 = f32[160,128]{1,0:T(8,128)S(1)} collective-permute-done((f32[160,128]{1,0:T(8,128)S(1)}, f32[160,128]{1,0:T(8,128)S(1)}, u32[]{:S(2)}, u32[]{:S(2)}) %collective-permute-start.17) | collective-permute-done | bytes 81952 | tf_op jit(solution)/shard_map/ppermute | solution.py:205
  41.7 1.4 %collective-permute-done.16 = f32[160,128]{1,0:T(8,128)S(1)} collective-permute-done((f32[160,128]{1,0:T(8,128)S(1)}, f32[160,128]{1,0:T(8,128)S(1)}, u32[]{:S(2)}, u32[]{:S(2)}) %collective-permute-start.16) | collective-permute-done | bytes 81952 | tf_op jit(solution)/shard_map/ppermute | solution.py:205
  43.1 0.6 %collective-permute-done.15 = f32[160,128]{1,0:T(8,128)S(1)} collective-permute-done((f32[160,128]{1,0:T(8,128)S(1)}, f32[160,128]{1,0:T(8,128)S(1)}, u32[]{:S(2)}, u32[]{:S(2)}) %collective-permute-start.15) | collective-permute-done | bytes 81952 | tf_op jit(solution)/shard_map/ppermute | solution.py:205
  43.7 0.1 collective-permute-start.19
  43.8 0.0 collective-permute-done.18.other_term_ref
  43.8 0.0 collective-permute-done.12.other_d_ref
  43.8 1.1 %expand.1 = (f32[256,256]{1,0:T(8,128)}, f32[512,128]{1,0:T(8,128)S(1)}) custom-call(bf16[256,320]{1,0:T(8,128)(2,1)S(1)} %get-tuple-element.21.pick_d_ref, bf16[512,160]{1,0:T(8,128)(2,1)S(1)} %get-tuple-element.22.pick_ref, f32[512,128]{1,0:T(8,128)S(1)} %get-tuple-element.23.keep_ref, f32[8,128]{1,0:T(8,128)S(1)} %get-tuple-element.24.upper_ref, ...), custom_call_target="tpu_custom_call" | custom-call | flops 503316480 | bytes 2097152 | tf_op jit(solution)/shard_map/expand/pallas_call | solution.py:327
  45.0 0.1 collective-permute-done.19.other_t_ref
  45.1 1.0 %finish.1 = f32[512,128]{1,0:T(8,128)} custom-call(bf16[512,160]{1,0:T(8,128)(2,1)S(1)} %get-tuple-element.38.pick_ref, f32[512,128]{1,0:T(8,128)S(1)} %get-tuple-element.23.keep_ref, f32[160,128]{1,0:T(8,128)S(1)} %collective-permute-done.19.other_t_ref, f32[512,128]{1,0:T(8,128)S(1)} %get-tuple-element.39.partial_ref), custom_call_target="tpu_custom_call" | custom-call | tf_op jit(solution)/shard_map/finish/pallas_call | solution.py:346
  (7 shorter events, 0.1 us)
Async XLA Ops:
  0.6 7.7 %copy-start.2 = (bf16[1,2,512,128]{3,2,1,0:T(8,128)(2,1)S(1)}, bf16[1,2,512,128]{3,2,1,0:T(8,128)(2,1)}, u32[]{:S(2)}) copy-start(bf16[1,2,512,128]{3,2,1,0:T(8,128)(2,1)} %param.10) | copy-start | bytes 786436
  2.6 5.7 %collective-permute-start = (bf16[640,128]{1,0:T(8,128)(2,1)}, bf16[640,128]{1,0:T(8,128)(2,1)S(1)}, u32[]{:S(2)}, u32[]{:S(2)}) collective-permute-start(bf16[640,128]{1,0:T(8,128)(2,1)} %pack.1.refs_0_), channel_id=1, source_target_pairs={{0,1},{1,0},{2,3},{3,2},{4,5},{5,4},{6,7},{7,6},{8,9},{9,8},{10,11... | collective-permute-start | bytes 491528 | tf_op jit(solution)/shard_map/ppermute | solution.py:205
  3.1 10.8 %collective-permute-start.1 = (bf16[640,128]{1,0:T(8,128)(2,1)}, bf16[640,128]{1,0:T(8,128)(2,1)S(1)}, u32[]{:S(2)}, u32[]{:S(2)}) collective-permute-start(bf16[640,128]{1,0:T(8,128)(2,1)} %pack.1.refs_0_), channel_id=1, source_target_pairs={{0,2},{2,0},{4,6},{6,4},{1,3},{3,1},{5,7},{7,5},{8,10},{10,8},{12,... | collective-permute-start | bytes 491528 | tf_op jit(solution)/shard_map/ppermute | solution.py:205
  5.7 15.2 %collective-permute-start.3 = (bf16[640,128]{1,0:T(8,128)(2,1)}, bf16[640,128]{1,0:T(8,128)(2,1)S(1)}, u32[]{:S(2)}, u32[]{:S(2)}) collective-permute-start(bf16[640,128]{1,0:T(8,128)(2,1)} %pack.1.refs_0_), channel_id=1, source_target_pairs={{0,4},{2,6},{4,0},{6,2},{1,5},{3,7},{5,1},{7,3},{8,12},{10,14},{12... | collective-permute-start | bytes 491528 | tf_op jit(solution)/shard_map/ppermute | solution.py:205
  8.3 12.6 %collective-permute-start.2 = (bf16[640,128]{1,0:T(8,128)(2,1)}, bf16[640,128]{1,0:T(8,128)(2,1)S(1)}, u32[]{:S(2)}, u32[]{:S(2)}) collective-permute-start(bf16[640,128]{1,0:T(8,128)(2,1)} %pack.1.refs_0_), channel_id=1, source_target_pairs={{0,6},{2,4},{4,2},{6,0},{1,7},{3,5},{5,3},{7,1},{8,14},{10,12},{12... | collective-permute-start | bytes 491528 | tf_op jit(solution)/shard_map/ppermute | solution.py:205
  8.3 0.7 %copy-start.3 = (s32[4]{0:T(128)S(1)}, s32[4]{0:T(128)}, u32[]{:S(2)}) copy-start(s32[4]{0:T(128)} %widths_ref.5) | copy-start | bytes 52
  8.3 0.7 %copy-start.4 = (f32[1,2]{1,0:T(1,128)S(1)}, f32[1,2]{1,0:T(1,128)}, u32[]{:S(2)}) copy-start(f32[1,2]{1,0:T(1,128)} %weights_ref.3) | copy-start | bytes 28
  9.0 0.9 %copy-start = (bf16[640,128]{1,0:T(8,128)(2,1)S(1)}, bf16[640,128]{1,0:T(8,128)(2,1)}, u32[]{:S(2)}) copy-start(bf16[640,128]{1,0:T(8,128)(2,1)} %pack.1.refs_0_) | copy-start | bytes 491524
  9.9 1.0 %copy-start.1 = (bf16[1,2,256,4,1,128]{5,3,4,2,1,0:T(4,128)(2,1)S(1)}, bf16[1,2,256,4,1,128]{5,3,4,2,1,0:T(4,128)(2,1)}, u32[]{:S(2)}) copy-start(bf16[1,2,256,4,1,128]{5,3,4,2,1,0:T(4,128)(2,1)} %param.6) | copy-start | bytes 1572868
  13.8 10.4 %collective-permute-start.5 = (f32[256,128]{1,0:T(8,128)S(1)}, f32[256,128]{1,0:T(8,128)S(1)}, u32[]{:S(2)}, u32[]{:S(2)}) collective-permute-start(f32[256,128]{1,0:T(8,128)S(1)} %get-tuple-element.33), channel_id=1, source_target_pairs={{0,8},{8,0},{16,24},{24,16},{1,9},{9,1},{17,25},{25,17},{2,10},{10... | collective-permute-start | bytes 393224 | tf_op jit(solution)/shard_map/ppermute | solution.py:205
  15.5 8.7 %collective-permute-start.7 = (f32[256,128]{1,0:T(8,128)S(1)}, f32[256,128]{1,0:T(8,128)S(1)}, u32[]{:S(2)}, u32[]{:S(2)}) collective-permute-start(f32[256,128]{1,0:T(8,128)S(1)} %get-tuple-element.33), channel_id=1, source_target_pairs={{0,24},{8,16},{16,8},{24,0},{1,25},{9,17},{17,9},{25,1},{2,26},{10... | collective-permute-start | bytes 393224 | tf_op jit(solution)/shard_map/ppermute | solution.py:205
  17.0 7.4 %collective-permute-start.6 = (f32[256,128]{1,0:T(8,128)S(1)}, f32[256,128]{1,0:T(8,128)S(1)}, u32[]{:S(2)}, u32[]{:S(2)}) collective-permute-start(f32[256,128]{1,0:T(8,128)S(1)} %get-tuple-element.33), channel_id=1, source_target_pairs={{0,16},{8,24},{16,0},{24,8},{1,17},{9,25},{17,1},{25,9},{2,18},{10... | collective-permute-start | bytes 393224 | tf_op jit(solution)/shard_map/ppermute | solution.py:205
  22.9 1.3 %collective-permute-start.4 = (f32[160,128]{1,0:T(8,128)S(1)}, f32[160,128]{1,0:T(8,128)S(1)}, u32[]{:S(2)}, u32[]{:S(2)}) collective-permute-start(f32[160,128]{1,0:T(8,128)S(1)} %get-tuple-element.31), channel_id=1, source_target_pairs={{0,1},{1,0},{2,3},{3,2},{4,5},{5,4},{6,7},{7,6},{8,9},{9,8},{10,11... | collective-permute-start | bytes 245768 | tf_op jit(solution)/shard_map/ppermute | solution.py:205
  24.4 2.9 %collective-permute-start.8 = (f32[160,256]{1,0:T(8,128)S(1)}, f32[160,256]{1,0:T(8,128)S(1)}, u32[]{:S(2)}, u32[]{:S(2)}) collective-permute-start(f32[160,256]{1,0:T(8,128)S(1)} %get-tuple-element.34), channel_id=1, source_target_pairs={{0,1},{1,0},{2,3},{3,2},{4,5},{5,4},{6,7},{7,6},{8,9},{9,8},{10,11... | collective-permute-start | bytes 491528 | tf_op jit(solution)/shard_map/ppermute | solution.py:205
  24.5 6.7 %collective-permute-start.13 = (f32[160,128]{1,0:T(8,128)S(1)}, f32[160,128]{1,0:T(8,128)S(1)}, u32[]{:S(2)}, u32[]{:S(2)}) collective-permute-start(f32[160,128]{1,0:T(8,128)S(1)} %add.39), channel_id=1, source_target_pairs={{0,6},{2,4},{4,2},{6,0},{1,7},{3,5},{5,3},{7,1},{8,14},{10,12},{12... | collective-permute-start | bytes 245768 | tf_op jit(solution)/shard_map/ppermute | solution.py:205
  27.3 11.3 %collective-permute-start.11 = (f32[160,256]{1,0:T(8,128)S(1)}, f32[160,256]{1,0:T(8,128)S(1)}, u32[]{:S(2)}, u32[]{:S(2)}) collective-permute-start(f32[160,256]{1,0:T(8,128)S(1)} %add.43), channel_id=1, source_target_pairs={{0,24},{8,16},{16,8},{24,0},{1,25},{9,17},{17,9},{25,1},{2,26},{10... | collective-permute-start | bytes 491528 | tf_op jit(solution)/shard_map/ppermute | solution.py:205
  29.5 9.7 %collective-permute-start.10 = (f32[160,256]{1,0:T(8,128)S(1)}, f32[160,256]{1,0:T(8,128)S(1)}, u32[]{:S(2)}, u32[]{:S(2)}) collective-permute-start(f32[160,256]{1,0:T(8,128)S(1)} %add.43), channel_id=1, source_target_pairs={{0,16},{8,24},{16,0},{24,8},{1,17},{9,25},{17,1},{25,9},{2,18},{10... | collective-permute-start | bytes 491528 | tf_op jit(solution)/shard_map/ppermute | solution.py:205
  30.4 9.4 %collective-permute-start.9 = (f32[160,256]{1,0:T(8,128)S(1)}, f32[160,256]{1,0:T(8,128)S(1)}, u32[]{:S(2)}, u32[]{:S(2)}) collective-permute-start(f32[160,256]{1,0:T(8,128)S(1)} %add.43), channel_id=1, source_target_pairs={{0,8},{8,0},{16,24},{24,16},{1,9},{9,1},{17,25},{25,17},{2,10},{10... | collective-permute-start | bytes 491528 | tf_op jit(solution)/shard_map/ppermute | solution.py:205
  31.2 5.0 %collective-permute-start.14 = (f32[160,128]{1,0:T(8,128)S(1)}, f32[160,128]{1,0:T(8,128)S(1)}, u32[]{:S(2)}, u32[]{:S(2)}) collective-permute-start(f32[160,128]{1,0:T(8,128)S(1)} %add.47), channel_id=1, source_target_pairs={{0,2},{2,0},{4,6},{6,4},{1,3},{3,1},{5,7},{7,5},{8,10},{10,8},{12,... | collective-permute-start | bytes 245768 | tf_op jit(solution)/shard_map/ppermute | solution.py:205
  33.5 10.3 %collective-permute-start.18 = (f32[256,128]{1,0:T(8,128)S(1)}, f32[256,128]{1,0:T(8,128)S(1)}, u32[]{:S(2)}, u32[]{:S(2)}) collective-permute-start(f32[256,128]{1,0:T(8,128)S(1)} %add_add_fusion.1.mine_term_ref), channel_id=1, source_target_pairs={{0,1},{1,0},{2,3},{3,2},{4,5},{5,4},{6,7},{7,6},{8,9},{9,8},{10,11... | collective-permute-start | bytes 393224 | tf_op jit(solution)/shard_map/ppermute | solution.py:205
  36.2 5.5 %collective-permute-start.17 = (f32[160,128]{1,0:T(8,128)S(1)}, f32[160,128]{1,0:T(8,128)S(1)}, u32[]{:S(2)}, u32[]{:S(2)}) collective-permute-start(f32[160,128]{1,0:T(8,128)S(1)} %add.48), channel_id=1, source_target_pairs={{0,24},{8,16},{16,8},{24,0},{1,25},{9,17},{17,9},{25,1},{2,26},{10... | collective-permute-start | bytes 245768 | tf_op jit(solution)/shard_map/ppermute | solution.py:205
  38.6 4.5 %collective-permute-start.16 = (f32[160,128]{1,0:T(8,128)S(1)}, f32[160,128]{1,0:T(8,128)S(1)}, u32[]{:S(2)}, u32[]{:S(2)}) collective-permute-start(f32[160,128]{1,0:T(8,128)S(1)} %add.48), channel_id=1, source_target_pairs={{0,16},{8,24},{16,0},{24,8},{1,17},{9,25},{17,1},{25,9},{2,18},{10... | collective-permute-start | bytes 245768 | tf_op jit(solution)/shard_map/ppermute | solution.py:205
  39.3 4.4 %collective-permute-start.15 = (f32[160,128]{1,0:T(8,128)S(1)}, f32[160,128]{1,0:T(8,128)S(1)}, u32[]{:S(2)}, u32[]{:S(2)}) collective-permute-start(f32[160,128]{1,0:T(8,128)S(1)} %add.48), channel_id=1, source_target_pairs={{0,8},{8,0},{16,24},{24,16},{1,9},{9,1},{17,25},{25,17},{2,10},{10... | collective-permute-start | bytes 245768 | tf_op jit(solution)/shard_map/ppermute | solution.py:205
  39.8 4.0 %collective-permute-start.12 = (f32[160,256]{1,0:T(8,128)S(1)}, f32[160,256]{1,0:T(8,128)S(1)}, u32[]{:S(2)}, u32[]{:S(2)}) collective-permute-start(f32[160,256]{1,0:T(8,128)S(1)} %add_add_fusion.mine_d_ref), channel_id=1, source_target_pairs={{0,1},{1,0},{2,3},{3,2},{4,5},{5,4},{6,7},{7,6},{8,9},{9,8},{10,11... | collective-permute-start | bytes 491528 | tf_op jit(solution)/shard_map/ppermute | solution.py:205
  43.7 1.3 %collective-permute-start.19 = (f32[160,128]{1,0:T(8,128)S(1)}, f32[160,128]{1,0:T(8,128)S(1)}, u32[]{:S(2)}, u32[]{:S(2)}) collective-permute-start(f32[160,128]{1,0:T(8,128)S(1)} %add_add_fusion.2.mine_t_ref), channel_id=1, source_target_pairs={{0,1},{1,0},{2,3},{3,2},{4,5},{5,4},{6,7},{7,6},{8,9},{9,8},{10,11... | collective-permute-start | bytes 245768 | tf_op jit(solution)/shard_map/ppermute | solution.py:205

commit v22 on v21

--- a/solution.py
+++ b/solution.py
@@ -25,7 +25,9 @@
     return offsets
 
 
-def pack_kernel(supernodes, slot, pattern_ref, widths_ref, panel_ref, packed_ref):
+def pack_kernel(
+    supernodes, slot, pattern_ref, widths_ref, panel_ref, packed_ref, *half_refs
+):
     packed_width = packed_ref.shape[0] // 2
     offsets = offsets_of(widths_ref, supernodes)
     lane = lax.broadcasted_iota(jnp.int32, (1, slot), 1)
@@ -37,9 +39,9 @@
     target = lax.broadcasted_iota(jnp.int32, (packed_width, supernodes * slot), 0)
     select = jnp.where(target == place, 1.0, 0.0).astype(BF16)
     for part in range(2):
-        packed_ref[part * packed_width:(part + 1) * packed_width, :] = rows_by_rows(
-            select, panel_ref[part]
-        ).astype(BF16)
+        packed = rows_by_rows(select, panel_ref[part]).astype(BF16)
+        packed_ref[part * packed_width:(part + 1) * packed_width, :] = packed
+        half_refs[part][...] = packed
 
 
 def prepare_kernel(
@@ -124,7 +126,6 @@
     own_wide_ref, *refs
 ):
     block_refs, refs = refs[:-7], refs[-7:]
-    block_refs = [block_refs[others.index(other)] for other in range(len(others))]
     keep_d_ref, send_d_ref, keep_t_ref, send_t_ref, x_ref, y_ref, t_ref = refs
     packed_width = block_refs[0].shape[0] // 2
     local_rows = straight_ref.shape[1]
@@ -133,7 +134,11 @@
     w_imag = weights_ref[0, 1]
     col_index = place_ref[1]
 
-    panel = jnp.concatenate([ref[...] for ref in block_refs], axis=1)
+    pieces = iter(block_refs)
+    panels = {other: [next(pieces)[...] for _ in range(2 if other == 1 else 1)] for other in others}
+    panel = jnp.concatenate(
+        [jnp.concatenate(panels[other], axis=0) for other in range(len(others))], axis=1
+    )
     with_real = rows_by_rows(panel, straight_ref[0])
     with_imag = rows_by_rows(panel, straight_ref[1])
     u_real = with_imag[packed_width:] - with_real[:packed_width]
@@ -249,17 +254,22 @@
     top = col_count // 2
     place = jnp.stack([lax.axis_index("row"), lax.axis_index("col")]).astype(jnp.int32)
 
-    packed = pl.pallas_call(
+    packed, *halves = pl.pallas_call(
         functools.partial(pack_kernel, supernodes, slot),
         in_specs=[SMEM_SPEC, SMEM_SPEC, VMEM_SPEC],
-        out_specs=VMEM_SPEC,
-        out_shape=jax.ShapeDtypeStruct((2 * packed_width, block), BF16),
+        out_specs=[VMEM_SPEC] * 3,
+        out_shape=[
+            jax.ShapeDtypeStruct((2 * packed_width, block), BF16),
+            jax.ShapeDtypeStruct((packed_width, block), BF16),
+            jax.ShapeDtypeStruct((packed_width, block), BF16),
+        ],
         name="pack",
     )(block_pattern, sup_widths, l_panel[0])
 
     blocks = {0: packed}
     others = sorted(range(row_count), key=lambda other: other > 0 and other % 2 == 0)
-    for other in range(1, row_count):
+    near = [swap(half, "row", 1) for half in halves]
+    for other in range(2, row_count):
         blocks[other] = swap(packed, "row", other)
     own = [packed] + [swap(packed, "col", other) for other in range(1, col_count)]
 
@@ -288,7 +298,7 @@
         sup_widths, pole_weights, place,
         found_inverse.reshape(2 * local_rows * row_count, block), diag_inverse[0], *own,
     )
-    later, blocks[1] = lax.optimization_barrier((term, blocks[1]))
+    later, *near = lax.optimization_barrier((term, *near))
     term = tree_sum(
         [term]
         + [swap(later if j == 1 else term, "pole", j) for j in range(1, lax.axis_size("pole"))]
@@ -296,7 +306,7 @@
 
     keep_d, send_d, keep_t, send_t = pl.pallas_call(
         functools.partial(compute_kernel, others, col_count, supernodes, slot),
-        in_specs=[SMEM_SPEC] * 3 + [VMEM_SPEC] * (2 + row_count),
+        in_specs=[SMEM_SPEC] * 3 + [VMEM_SPEC] * (3 + row_count),
         out_specs=[VMEM_SPEC] * 4,
         out_shape=[jax.ShapeDtypeStruct((half, local_rows), F32)] * 2
         + [jax.ShapeDtypeStruct((half, slot), F32)] * 2,
@@ -309,7 +319,7 @@
         name="compute",
     )(
         sup_widths, pole_weights, place, straight, own_wide,
-        *[blocks[other] for other in others],
+        *[piece for other in others for piece in (near if other == 1 else [blocks[other]])],
     )
 
     tie = lax.optimization_barrier

time: 46.3 us -> 52.1 us (1.13)
  waiting for transfers between devices: 13.3 us -> 17.1 us
  starting transfers between devices: 21.6 us -> 23.6 us
    ppermute x20 -> x21, waiting for transfers between devices: 13.3 us -> 17.1 us  [swap(): lax.ppermute(value, axis, [(i, i ^ bit) for i in range(lax.axis_size(axis...]
    ppermute x20 -> x21, starting transfers between devices: 21.6 us -> 23.6 us  [swap(): lax.ppermute(value, axis, [(i, i ^ bit) for i in range(lax.axis_size(axis...]
  transfers between devices with their start and end apart: 20 -> 21, of which waited for: 10 -> 11; matrix products, arithmetic and copies ran while one was open for 0% -> 0% of each run, Pallas kernels for 10% -> 9%
where the time goes in v22:
time: 52.1 us; the launch traced here: 51.8 us
  starting transfers between devices  23.6 us (45%)
  waiting for transfers between devices  17.1 us (33%)
  Pallas kernels  7.55 us (14%)
  local copies, waits for them, and re-layouts  2.63 us (5%)
  between operations  0.75 us (1%)
    ppermute x21, starting transfers between devices, swap(): lax.ppermute(value, axis, [(i, i ^ bit) for i in range(lax.axis_size(axis...  23.6 us
    ppermute x21, waiting for transfers between devices, swap(): lax.ppermute(value, axis, [(i, i ^ bit) for i in range(lax.axis_size(axis...  17.1 us
    unnamed x10, local copies, waits for them, and re-layouts  2.63 us
    pallas_call x1, Pallas kernels, per_device(): pl.pallas_call(functools.partial(pack_kernel, supernodes, slot), in_specs...  2.04 us
    pallas_call x1, Pallas kernels, per_device(): pl.pallas_call(functools.partial(compute_kernel, others, col_count, super...  1.99 us
    pallas_call x1, Pallas kernels, per_device(): pl.pallas_call(functools.partial(prepare_kernel, (row_count, col_count)),...  1.38 us
    pallas_call x1, Pallas kernels, per_device(): pl.pallas_call(expand_kernel, in_specs=[VMEM_SPEC] * 9, out_specs=[VMEM_S...  1.14 us
  transfers between devices with their start and end apart: 21, of which 11 were waited for; matrix products, arithmetic and copies ran while one was open for 0% of the time, Pallas kernels for 9%

profile of v22, /device:TPU:0, one launch (start us, length us, event | category | flops | bytes accessed | tf_op | source)
XLA Modules:
  0.0 51.8 jit_solution(16733180006127973955)
XLA Ops:
  0.6 0.0 copy-start.2
  0.6 2.0 %pack.1 = (bf16[640,128]{1,0:T(8,128)(2,1)}, bf16[320,128]{1,0:T(8,128)(2,1)}, bf16[320,128]{1,0:T(8,128)(2,1)}) custom-call(s32[1,4]{1,0:T(1,128)} %pattern_ref.1, s32[4]{0:T(128)} %widths_ref.5, bf16[2,128,512]{2,1,0:T(8,128)(2,1)} %bitcast.7), custom_call_target="tpu_custom_call" | custom-call | tf_op jit(solution)/shard_map/pack/pallas_call | solution.py:257
  2.7 0.5 collective-permute-start
  3.1 3.6 %collective-permute-start.4 = (bf16[640,128]{1,0:T(8,128)(2,1)}, bf16[640,128]{1,0:T(8,128)(2,1)S(1)}, u32[]{:S(2)}, u32[]{:S(2)}) collective-permute-start(bf16[640,128]{1,0:T(8,128)(2,1)} %get-tuple-element.25.refs_0_), channel_id=1, source_target_pairs={{0,4},{2,6},{4,0},{6,2},{1,5},{3,7},{5,1},{7,3},{8,12},{10,14},{12... | collective-permute-start | bytes 491528 | tf_op jit(solution)/shard_map/ppermute | solution.py:210
  6.7 1.3 %collective-permute-start.3 = (bf16[640,128]{1,0:T(8,128)(2,1)}, bf16[640,128]{1,0:T(8,128)(2,1)S(1)}, u32[]{:S(2)}, u32[]{:S(2)}) collective-permute-start(bf16[640,128]{1,0:T(8,128)(2,1)} %get-tuple-element.25.refs_0_), channel_id=1, source_target_pairs={{0,6},{2,4},{4,2},{6,0},{1,7},{3,5},{5,3},{7,1},{8,14},{10,12},{12... | collective-permute-start | bytes 491528 | tf_op jit(solution)/shard_map/ppermute | solution.py:210
  8.1 0.2 collective-permute-start.1
  8.3 1.8 %collective-permute-start.2 = (bf16[320,128]{1,0:T(8,128)(2,1)}, bf16[320,128]{1,0:T(8,128)(2,1)S(1)}, u32[]{:S(2)}, u32[]{:S(2)}) collective-permute-start(bf16[320,128]{1,0:T(8,128)(2,1)} %get-tuple-element.34), channel_id=1, source_target_pairs={{0,2},{2,0},{4,6},{6,4},{1,3},{3,1},{5,7},{7,5},{8,10},{10,8},{12,... | collective-permute-start | bytes 245768 | tf_op jit(solution)/shard_map/ppermute | solution.py:210
  10.1 0.1 pad_add_fusion.place_ref
  10.2 0.0 collective-permute-done.refs_1_
  10.2 0.0 copy-start.3
  10.2 0.0 copy-start.4
  10.2 0.0 copy-done.2
  10.2 0.6 %copy-done.3 = s32[4]{0:T(128)S(1)} copy-done((s32[4]{0:T(128)S(1)}, s32[4]{0:T(128)}, u32[]{:S(2)}) %copy-start.3) | copy-done | bytes 40
  10.8 0.0 copy-done.4
  10.9 0.0 copy-start
  10.9 0.9 %copy-done = bf16[640,128]{1,0:T(8,128)(2,1)S(1)} copy-done((bf16[640,128]{1,0:T(8,128)(2,1)S(1)}, bf16[640,128]{1,0:T(8,128)(2,1)}, u32[]{:S(2)}) %copy-start) | copy-done | bytes 163864
  11.8 0.0 copy-start.1
  11.8 1.0 %copy-done.1 = bf16[1,2,256,4,1,128]{5,3,4,2,1,0:T(4,128)(2,1)S(1)} copy-done((bf16[1,2,256,4,1,128]{5,3,4,2,1,0:T(4,128)(2,1)S(1)}, bf16[1,2,256,4,1,128]{5,3,4,2,1,0:T(4,128)(2,1)}, u32[]{:S(2)}) %copy-start.1) | copy-done | bytes 524312
  12.8 1.4 %prepare.1 = (bf16[2,256,512]{2,1,0:T(8,128)(2,1)S(1)}, bf16[512,512]{1,0:T(8,128)(2,1)S(1)}, f32[256,128]{1,0:T(8,128)S(1)}, bf16[256,320]{1,0:T(8,128)(2,1)S(1...) custom-call(s32[4]{0:T(128)S(1)} %copy-done.3, ...), custom_call_target="tpu_custom_call" | custom-call | flops 134217728 | bytes 1048576 | tf_op jit(solution)/shard_map/prepare/pallas_call | solution.py:276
  14.2 5.1 %collective-permute-done.1.refs_1_ = bf16[320,128]{1,0:T(8,128)(2,1)S(1)} collective-permute-done((bf16[320,128]{1,0:T(8,128)(2,1)}, bf16[320,128]{1,0:T(8,128)(2,1)S(1)}, u32[]{:S(2)}, u32[]{:S(2)}) %collective-permute-start.1) | collective-permute-done | bytes 81952 | tf_op jit(solution)/shard_map/ppermute | solution.py:210
  19.3 0.9 %collective-permute-done.2.refs_2_ = bf16[320,128]{1,0:T(8,128)(2,1)S(1)} collective-permute-done((bf16[320,128]{1,0:T(8,128)(2,1)}, bf16[320,128]{1,0:T(8,128)(2,1)S(1)}, u32[]{:S(2)}, u32[]{:S(2)}) %collective-permute-start.2) | collective-permute-done | bytes 81952 | tf_op jit(solution)/shard_map/ppermute | solution.py:210
  20.2 1.5 %collective-permute-start.6 = (f32[256,128]{1,0:T(8,128)S(1)}, f32[256,128]{1,0:T(8,128)S(1)}, u32[]{:S(2)}, u32[]{:S(2)}) collective-permute-start(f32[256,128]{1,0:T(8,128)S(1)} %get-tuple-element.41), channel_id=1, source_target_pairs={{0,8},{8,0},{16,24},{24,16},{1,9},{9,1},{17,25},{25,17},{2,10},{10... | collective-permute-start | bytes 393224 | tf_op jit(solution)/shard_map/ppermute | solution.py:210
  21.7 1.5 %collective-permute-start.8 = (f32[256,128]{1,0:T(8,128)S(1)}, f32[256,128]{1,0:T(8,128)S(1)}, u32[]{:S(2)}, u32[]{:S(2)}) collective-permute-start(f32[256,128]{1,0:T(8,128)S(1)} %get-tuple-element.41), channel_id=1, source_target_pairs={{0,24},{8,16},{16,8},{24,0},{1,25},{9,17},{17,9},{25,1},{2,26},{10... | collective-permute-start | bytes 393224 | tf_op jit(solution)/shard_map/ppermute | solution.py:210
  23.2 0.5 collective-permute-start.7
  23.7 0.0 collective-permute-done.4.refs_4_
  23.7 0.0 collective-permute-done.3.refs_3_
  23.7 2.0 %compute.1 = (f32[160,256]{1,0:T(8,128)S(1)}, f32[160,256]{1,0:T(8,128)S(1)}, f32[160,128]{1,0:T(8,128)S(1)}, f32[160,128]{1,0:T(8,128)S(1)}) custom-call(s32[4]{0:T(128)S(1)} %copy-done.3, f32[1,2]{1,0:T(1,128)S(1)} %copy-done.4, s32[2]{0:T(128)S(1)} %pad_add_fusion.place_ref, bf16[2,256,512]{2,1,0:T(8,128)(2,1)S(1)} %get-tuple-element.30.straight_ref, ...), custom_call_target="tpu_custom_call" | custom-call | tf_op jit(solution)/shard_map/compute/pallas_call | solution.py:307
  25.7 0.1 collective-permute-start.5
  25.8 1.3 %collective-permute-done.5 = f32[160,128]{1,0:T(8,128)S(1)} collective-permute-done((f32[160,128]{1,0:T(8,128)S(1)}, f32[160,128]{1,0:T(8,128)S(1)}, u32[]{:S(2)}, u32[]{:S(2)}) %collective-permute-start.5) | collective-permute-done | bytes 81952 | tf_op jit(solution)/shard_map/ppermute | solution.py:210
  27.0 0.0 collective-permute-done.6
  27.1 1.5 %collective-permute-done.8 = f32[256,128]{1,0:T(8,128)S(1)} collective-permute-done((f32[256,128]{1,0:T(8,128)S(1)}, f32[256,128]{1,0:T(8,128)S(1)}, u32[]{:S(2)}, u32[]{:S(2)}) %collective-permute-start.8) | collective-permute-done | bytes 131104 | tf_op jit(solution)/shard_map/ppermute | solution.py:210
  28.5 1.3 %collective-permute-done.7 = f32[256,128]{1,0:T(8,128)S(1)} collective-permute-done((f32[256,128]{1,0:T(8,128)S(1)}, f32[256,128]{1,0:T(8,128)S(1)}, u32[]{:S(2)}, u32[]{:S(2)}) %collective-permute-start.7) | collective-permute-done | bytes 131104 | tf_op jit(solution)/shard_map/ppermute | solution.py:210
  29.8 0.1 collective-permute-start.9
  29.9 3.6 %collective-permute-start.14 = (f32[160,128]{1,0:T(8,128)S(1)}, f32[160,128]{1,0:T(8,128)S(1)}, u32[]{:S(2)}, u32[]{:S(2)}) collective-permute-start(f32[160,128]{1,0:T(8,128)S(1)} %add.39), channel_id=1, source_target_pairs={{0,6},{2,4},{4,2},{6,0},{1,7},{3,5},{5,3},{7,1},{8,14},{10,12},{12... | collective-permute-start | bytes 245768 | tf_op jit(solution)/shard_map/ppermute | solution.py:210
  33.6 0.0 collective-permute-done.9
  33.6 1.5 %collective-permute-start.12 = (f32[160,256]{1,0:T(8,128)S(1)}, f32[160,256]{1,0:T(8,128)S(1)}, u32[]{:S(2)}, u32[]{:S(2)}) collective-permute-start(f32[160,256]{1,0:T(8,128)S(1)} %add.43), channel_id=1, source_target_pairs={{0,24},{8,16},{16,8},{24,0},{1,25},{9,17},{17,9},{25,1},{2,26},{10... | collective-permute-start | bytes 491528 | tf_op jit(solution)/shard_map/ppermute | solution.py:210
  35.1 1.5 %collective-permute-start.11 = (f32[160,256]{1,0:T(8,128)S(1)}, f32[160,256]{1,0:T(8,128)S(1)}, u32[]{:S(2)}, u32[]{:S(2)}) collective-permute-start(f32[160,256]{1,0:T(8,128)S(1)} %add.43), channel_id=1, source_target_pairs={{0,16},{8,24},{16,0},{24,8},{1,17},{9,25},{17,1},{25,9},{2,18},{10... | collective-permute-start | bytes 491528 | tf_op jit(solution)/shard_map/ppermute | solution.py:210
  36.6 0.5 %collective-permute-start.10 = (f32[160,256]{1,0:T(8,128)S(1)}, f32[160,256]{1,0:T(8,128)S(1)}, u32[]{:S(2)}, u32[]{:S(2)}) collective-permute-start(f32[160,256]{1,0:T(8,128)S(1)} %add.43), channel_id=1, source_target_pairs={{0,8},{8,0},{16,24},{24,16},{1,9},{9,1},{17,25},{25,17},{2,10},{10... | collective-permute-start | bytes 491528 | tf_op jit(solution)/shard_map/ppermute | solution.py:210
  37.2 0.0 collective-permute-done.14
  37.2 0.7 %collective-permute-start.15 = (f32[160,128]{1,0:T(8,128)S(1)}, f32[160,128]{1,0:T(8,128)S(1)}, u32[]{:S(2)}, u32[]{:S(2)}) collective-permute-start(f32[160,128]{1,0:T(8,128)S(1)} %add.47), channel_id=1, source_target_pairs={{0,2},{2,0},{4,6},{6,4},{1,3},{3,1},{5,7},{7,5},{8,10},{10,8},{12,... | collective-permute-start | bytes 245768 | tf_op jit(solution)/shard_map/ppermute | solution.py:210
  37.8 0.0 collective-permute-start.19
  37.8 3.9 %collective-permute-done.15 = f32[160,128]{1,0:T(8,128)S(1)} collective-permute-done((f32[160,128]{1,0:T(8,128)S(1)}, f32[160,128]{1,0:T(8,128)S(1)}, u32[]{:S(2)}, u32[]{:S(2)}) %collective-permute-start.15) | collective-permute-done | bytes 81952 | tf_op jit(solution)/shard_map/ppermute | solution.py:210
  41.7 1.5 %collective-permute-start.18 = (f32[160,128]{1,0:T(8,128)S(1)}, f32[160,128]{1,0:T(8,128)S(1)}, u32[]{:S(2)}, u32[]{:S(2)}) collective-permute-start(f32[160,128]{1,0:T(8,128)S(1)} %add.48), channel_id=1, source_target_pairs={{0,24},{8,16},{16,8},{24,0},{1,25},{9,17},{17,9},{25,1},{2,26},{10... | collective-permute-start | bytes 245768 | tf_op jit(solution)/shard_map/ppermute | solution.py:210
  43.2 0.0 collective-permute-done.12
  43.2 1.5 %collective-permute-start.17 = (f32[160,128]{1,0:T(8,128)S(1)}, f32[160,128]{1,0:T(8,128)S(1)}, u32[]{:S(2)}, u32[]{:S(2)}) collective-permute-start(f32[160,128]{1,0:T(8,128)S(1)} %add.48), channel_id=1, source_target_pairs={{0,16},{8,24},{16,0},{24,8},{1,17},{9,25},{17,1},{25,9},{2,18},{10... | collective-permute-start | bytes 245768 | tf_op jit(solution)/shard_map/ppermute | solution.py:210
  44.7 0.3 collective-permute-done.11
  45.0 1.5 %collective-permute-start.16 = (f32[160,128]{1,0:T(8,128)S(1)}, f32[160,128]{1,0:T(8,128)S(1)}, u32[]{:S(2)}, u32[]{:S(2)}) collective-permute-start(f32[160,128]{1,0:T(8,128)S(1)} %add.48), channel_id=1, source_target_pairs={{0,8},{8,0},{16,24},{24,16},{1,9},{9,1},{17,25},{25,17},{2,10},{10... | collective-permute-start | bytes 245768 | tf_op jit(solution)/shard_map/ppermute | solution.py:210
  46.6 0.0 collective-permute-done.10
  46.6 0.1 add_add_fusion.mine_d_ref
  46.6 0.1 collective-permute-start.13
  46.7 0.4 collective-permute-done.18
  47.1 0.8 %collective-permute-done.17 = f32[160,128]{1,0:T(8,128)S(1)} collective-permute-done((f32[160,128]{1,0:T(8,128)S(1)}, f32[160,128]{1,0:T(8,128)S(1)}, u32[]{:S(2)}, u32[]{:S(2)}) %collective-permute-start.17) | collective-permute-done | bytes 81952 | tf_op jit(solution)/shard_map/ppermute | solution.py:210
  48.0 1.5 %collective-permute-done.16 = f32[160,128]{1,0:T(8,128)S(1)} collective-permute-done((f32[160,128]{1,0:T(8,128)S(1)}, f32[160,128]{1,0:T(8,128)S(1)}, u32[]{:S(2)}, u32[]{:S(2)}) %collective-permute-start.16) | collective-permute-done | bytes 81952 | tf_op jit(solution)/shard_map/ppermute | solution.py:210
  49.5 0.1 collective-permute-start.20
  49.6 0.0 collective-permute-done.19.other_term_ref
  49.6 0.0 collective-permute-done.13.other_d_ref
  49.6 1.1 %expand.1 = (f32[256,256]{1,0:T(8,128)}, f32[512,128]{1,0:T(8,128)S(1)}) custom-call(bf16[256,320]{1,0:T(8,128)(2,1)S(1)} %get-tuple-element.26.pick_d_ref, bf16[512,160]{1,0:T(8,128)(2,1)S(1)} %get-tuple-element.27.pick_ref, f32[512,128]{1,0:T(8,128)S(1)} %get-tuple-element.28.keep_ref, f32[8,128]{1,0:T(8,128)S(1)} %get-tuple-element.29.upper_ref, ...), custom_call_target="tpu_custom_call" | custom-call | flops 503316480 | bytes 2097152 | tf_op jit(solution)/shard_map/expand/pallas_call | solution.py:337
  50.8 0.1 collective-permute-done.20.other_t_ref
  50.9 1.0 %finish.1 = f32[512,128]{1,0:T(8,128)} custom-call(bf16[512,160]{1,0:T(8,128)(2,1)S(1)} %get-tuple-element.46.pick_ref, f32[512,128]{1,0:T(8,128)S(1)} %get-tuple-element.28.keep_ref, f32[160,128]{1,0:T(8,128)S(1)} %collective-permute-done.20.other_t_ref, f32[512,128]{1,0:T(8,128)S(1)} %get-tuple-element.47.partial_ref), custom_call_target="tpu_custom_call" | custom-call | tf_op jit(solution)/shard_map/finish/pallas_call | solution.py:356
  (6 shorter events, 0.1 us)
Async XLA Ops:
  0.6 9.6 %copy-start.2 = (bf16[1,2,512,128]{3,2,1,0:T(8,128)(2,1)S(1)}, bf16[1,2,512,128]{3,2,1,0:T(8,128)(2,1)}, u32[]{:S(2)}) copy-start(bf16[1,2,512,128]{3,2,1,0:T(8,128)(2,1)} %param.10) | copy-start | bytes 786436
  2.7 7.5 %collective-permute-start = (bf16[640,128]{1,0:T(8,128)(2,1)}, bf16[640,128]{1,0:T(8,128)(2,1)S(1)}, u32[]{:S(2)}, u32[]{:S(2)}) collective-permute-start(bf16[640,128]{1,0:T(8,128)(2,1)} %get-tuple-element.25.refs_0_), channel_id=1, source_target_pairs={{0,1},{1,0},{2,3},{3,2},{4,5},{5,4},{6,7},{7,6},{8,9},{9,8},{10,11... | collective-permute-start | bytes 491528 | tf_op jit(solution)/shard_map/ppermute | solution.py:210
  3.1 20.5 %collective-permute-start.4 = (bf16[640,128]{1,0:T(8,128)(2,1)}, bf16[640,128]{1,0:T(8,128)(2,1)S(1)}, u32[]{:S(2)}, u32[]{:S(2)}) collective-permute-start(bf16[640,128]{1,0:T(8,128)(2,1)} %get-tuple-element.25.refs_0_), channel_id=1, source_target_pairs={{0,4},{2,6},{4,0},{6,2},{1,5},{3,7},{5,1},{7,3},{8,12},{10,14},{12... | collective-permute-start | bytes 491528 | tf_op jit(solution)/shard_map/ppermute | solution.py:210
  6.7 17.0 %collective-permute-start.3 = (bf16[640,128]{1,0:T(8,128)(2,1)}, bf16[640,128]{1,0:T(8,128)(2,1)S(1)}, u32[]{:S(2)}, u32[]{:S(2)}) collective-permute-start(bf16[640,128]{1,0:T(8,128)(2,1)} %get-tuple-element.25.refs_0_), channel_id=1, source_target_pairs={{0,6},{2,4},{4,2},{6,0},{1,7},{3,5},{5,3},{7,1},{8,14},{10,12},{12... | collective-permute-start | bytes 491528 | tf_op jit(solution)/shard_map/ppermute | solution.py:210
  8.1 11.2 %collective-permute-start.1 = (bf16[320,128]{1,0:T(8,128)(2,1)}, bf16[320,128]{1,0:T(8,128)(2,1)S(1)}, u32[]{:S(2)}, u32[]{:S(2)}) collective-permute-start(bf16[320,128]{1,0:T(8,128)(2,1)} %get-tuple-element.33), channel_id=1, source_target_pairs={{0,2},{2,0},{4,6},{6,4},{1,3},{3,1},{5,7},{7,5},{8,10},{10,8},{12,... | collective-permute-start | bytes 245768 | tf_op jit(solution)/shard_map/ppermute | solution.py:210
  8.3 11.9 %collective-permute-start.2 = (bf16[320,128]{1,0:T(8,128)(2,1)}, bf16[320,128]{1,0:T(8,128)(2,1)S(1)}, u32[]{:S(2)}, u32[]{:S(2)}) collective-permute-start(bf16[320,128]{1,0:T(8,128)(2,1)} %get-tuple-element.34), channel_id=1, source_target_pairs={{0,2},{2,0},{4,6},{6,4},{1,3},{3,1},{5,7},{7,5},{8,10},{10,8},{12,... | collective-permute-start | bytes 245768 | tf_op jit(solution)/shard_map/ppermute | solution.py:210
  10.2 0.7 %copy-start.3 = (s32[4]{0:T(128)S(1)}, s32[4]{0:T(128)}, u32[]{:S(2)}) copy-start(s32[4]{0:T(128)} %widths_ref.5) | copy-start | bytes 52
  10.2 0.7 %copy-start.4 = (f32[1,2]{1,0:T(1,128)S(1)}, f32[1,2]{1,0:T(1,128)}, u32[]{:S(2)}) copy-start(f32[1,2]{1,0:T(1,128)} %weights_ref.3) | copy-start | bytes 28
  10.9 0.9 %copy-start = (bf16[640,128]{1,0:T(8,128)(2,1)S(1)}, bf16[640,128]{1,0:T(8,128)(2,1)}, u32[]{:S(2)}) copy-start(bf16[640,128]{1,0:T(8,128)(2,1)} %get-tuple-element.25.refs_0_) | copy-start | bytes 491524
  11.8 1.0 %copy-start.1 = (bf16[1,2,256,4,1,128]{5,3,4,2,1,0:T(4,128)(2,1)S(1)}, bf16[1,2,256,4,1,128]{5,3,4,2,1,0:T(4,128)(2,1)}, u32[]{:S(2)}) copy-start(bf16[1,2,256,4,1,128]{5,3,4,2,1,0:T(4,128)(2,1)} %param.6) | copy-start | bytes 1572868
  20.2 6.9 %collective-permute-start.6 = (f32[256,128]{1,0:T(8,128)S(1)}, f32[256,128]{1,0:T(8,128)S(1)}, u32[]{:S(2)}, u32[]{:S(2)}) collective-permute-start(f32[256,128]{1,0:T(8,128)S(1)} %get-tuple-element.41), channel_id=1, source_target_pairs={{0,8},{8,0},{16,24},{24,16},{1,9},{9,1},{17,25},{25,17},{2,10},{10... | collective-permute-start | bytes 393224 | tf_op jit(solution)/shard_map/ppermute | solution.py:210
  21.7 6.8 %collective-permute-start.8 = (f32[256,128]{1,0:T(8,128)S(1)}, f32[256,128]{1,0:T(8,128)S(1)}, u32[]{:S(2)}, u32[]{:S(2)}) collective-permute-start(f32[256,128]{1,0:T(8,128)S(1)} %get-tuple-element.41), channel_id=1, source_target_pairs={{0,24},{8,16},{16,8},{24,0},{1,25},{9,17},{17,9},{25,1},{2,26},{10... | collective-permute-start | bytes 393224 | tf_op jit(solution)/shard_map/ppermute | solution.py:210
  23.2 6.6 %collective-permute-start.7 = (f32[256,128]{1,0:T(8,128)S(1)}, f32[256,128]{1,0:T(8,128)S(1)}, u32[]{:S(2)}, u32[]{:S(2)}) collective-permute-start(f32[256,128]{1,0:T(8,128)S(1)} %get-tuple-element.41), channel_id=1, source_target_pairs={{0,16},{8,24},{16,0},{24,8},{1,17},{9,25},{17,1},{25,9},{2,18},{10... | collective-permute-start | bytes 393224 | tf_op jit(solution)/shard_map/ppermute | solution.py:210
  25.7 1.3 %collective-permute-start.5 = (f32[160,128]{1,0:T(8,128)S(1)}, f32[160,128]{1,0:T(8,128)S(1)}, u32[]{:S(2)}, u32[]{:S(2)}) collective-permute-start(f32[160,128]{1,0:T(8,128)S(1)} %get-tuple-element.39), channel_id=1, source_target_pairs={{0,1},{1,0},{2,3},{3,2},{4,5},{5,4},{6,7},{7,6},{8,9},{9,8},{10,11... | collective-permute-start | bytes 245768 | tf_op jit(solution)/shard_map/ppermute | solution.py:210
  29.8 3.7 %collective-permute-start.9 = (f32[160,256]{1,0:T(8,128)S(1)}, f32[160,256]{1,0:T(8,128)S(1)}, u32[]{:S(2)}, u32[]{:S(2)}) collective-permute-start(f32[160,256]{1,0:T(8,128)S(1)} %get-tuple-element.42), channel_id=1, source_target_pairs={{0,1},{1,0},{2,3},{3,2},{4,5},{5,4},{6,7},{7,6},{8,9},{9,8},{10,11... | collective-permute-start | bytes 491528 | tf_op jit(solution)/shard_map/ppermute | solution.py:210
  29.9 7.2 %collective-permute-start.14 = (f32[160,128]{1,0:T(8,128)S(1)}, f32[160,128]{1,0:T(8,128)S(1)}, u32[]{:S(2)}, u32[]{:S(2)}) collective-permute-start(f32[160,128]{1,0:T(8,128)S(1)} %add.39), channel_id=1, source_target_pairs={{0,6},{2,4},{4,2},{6,0},{1,7},{3,5},{5,3},{7,1},{8,14},{10,12},{12... | collective-permute-start | bytes 245768 | tf_op jit(solution)/shard_map/ppermute | solution.py:210
  33.6 9.6 %collective-permute-start.12 = (f32[160,256]{1,0:T(8,128)S(1)}, f32[160,256]{1,0:T(8,128)S(1)}, u32[]{:S(2)}, u32[]{:S(2)}) collective-permute-start(f32[160,256]{1,0:T(8,128)S(1)} %add.43), channel_id=1, source_target_pairs={{0,24},{8,16},{16,8},{24,0},{1,25},{9,17},{17,9},{25,1},{2,26},{10... | collective-permute-start | bytes 491528 | tf_op jit(solution)/shard_map/ppermute | solution.py:210
  35.1 9.9 %collective-permute-start.11 = (f32[160,256]{1,0:T(8,128)S(1)}, f32[160,256]{1,0:T(8,128)S(1)}, u32[]{:S(2)}, u32[]{:S(2)}) collective-permute-start(f32[160,256]{1,0:T(8,128)S(1)} %add.43), channel_id=1, source_target_pairs={{0,16},{8,24},{16,0},{24,8},{1,17},{9,25},{17,1},{25,9},{2,18},{10... | collective-permute-start | bytes 491528 | tf_op jit(solution)/shard_map/ppermute | solution.py:210
  36.6 9.9 %collective-permute-start.10 = (f32[160,256]{1,0:T(8,128)S(1)}, f32[160,256]{1,0:T(8,128)S(1)}, u32[]{:S(2)}, u32[]{:S(2)}) collective-permute-start(f32[160,256]{1,0:T(8,128)S(1)} %add.43), channel_id=1, source_target_pairs={{0,8},{8,0},{16,24},{24,16},{1,9},{9,1},{17,25},{25,17},{2,10},{10... | collective-permute-start | bytes 491528 | tf_op jit(solution)/shard_map/ppermute | solution.py:210
  37.2 4.5 %collective-permute-start.15 = (f32[160,128]{1,0:T(8,128)S(1)}, f32[160,128]{1,0:T(8,128)S(1)}, u32[]{:S(2)}, u32[]{:S(2)}) collective-permute-start(f32[160,128]{1,0:T(8,128)S(1)} %add.47), channel_id=1, source_target_pairs={{0,2},{2,0},{4,6},{6,4},{1,3},{3,1},{5,7},{7,5},{8,10},{10,8},{12,... | collective-permute-start | bytes 245768 | tf_op jit(solution)/shard_map/ppermute | solution.py:210
  37.8 11.8 %collective-permute-start.19 = (f32[256,128]{1,0:T(8,128)S(1)}, f32[256,128]{1,0:T(8,128)S(1)}, u32[]{:S(2)}, u32[]{:S(2)}) collective-permute-start(f32[256,128]{1,0:T(8,128)S(1)} %add_add_fusion.1.mine_term_ref), channel_id=1, source_target_pairs={{0,1},{1,0},{2,3},{3,2},{4,5},{5,4},{6,7},{7,6},{8,9},{9,8},{10,11... | collective-permute-start | bytes 393224 | tf_op jit(solution)/shard_map/ppermute | solution.py:210
  41.7 5.4 %collective-permute-start.18 = (f32[160,128]{1,0:T(8,128)S(1)}, f32[160,128]{1,0:T(8,128)S(1)}, u32[]{:S(2)}, u32[]{:S(2)}) collective-permute-start(f32[160,128]{1,0:T(8,128)S(1)} %add.48), channel_id=1, source_target_pairs={{0,24},{8,16},{16,8},{24,0},{1,25},{9,17},{17,9},{25,1},{2,26},{10... | collective-permute-start | bytes 245768 | tf_op jit(solution)/shard_map/ppermute | solution.py:210
  43.2 4.8 %collective-permute-start.17 = (f32[160,128]{1,0:T(8,128)S(1)}, f32[160,128]{1,0:T(8,128)S(1)}, u32[]{:S(2)}, u32[]{:S(2)}) collective-permute-start(f32[160,128]{1,0:T(8,128)S(1)} %add.48), channel_id=1, source_target_pairs={{0,16},{8,24},{16,0},{24,8},{1,17},{9,25},{17,1},{25,9},{2,18},{10... | collective-permute-start | bytes 245768 | tf_op jit(solution)/shard_map/ppermute | solution.py:210
  45.0 4.4 %collective-permute-start.16 = (f32[160,128]{1,0:T(8,128)S(1)}, f32[160,128]{1,0:T(8,128)S(1)}, u32[]{:S(2)}, u32[]{:S(2)}) collective-permute-start(f32[160,128]{1,0:T(8,128)S(1)} %add.48), channel_id=1, source_target_pairs={{0,8},{8,0},{16,24},{24,16},{1,9},{9,1},{17,25},{25,17},{2,10},{10... | collective-permute-start | bytes 245768 | tf_op jit(solution)/shard_map/ppermute | solution.py:210
  46.6 3.0 %collective-permute-start.13 = (f32[160,256]{1,0:T(8,128)S(1)}, f32[160,256]{1,0:T(8,128)S(1)}, u32[]{:S(2)}, u32[]{:S(2)}) collective-permute-start(f32[160,256]{1,0:T(8,128)S(1)} %add_add_fusion.mine_d_ref), channel_id=1, source_target_pairs={{0,1},{1,0},{2,3},{3,2},{4,5},{5,4},{6,7},{7,6},{8,9},{9,8},{10,11... | collective-permute-start | bytes 491528 | tf_op jit(solution)/shard_map/ppermute | solution.py:210
  49.5 1.3 %collective-permute-start.20 = (f32[160,128]{1,0:T(8,128)S(1)}, f32[160,128]{1,0:T(8,128)S(1)}, u32[]{:S(2)}, u32[]{:S(2)}) collective-permute-start(f32[160,128]{1,0:T(8,128)S(1)} %add_add_fusion.2.mine_t_ref), channel_id=1, source_target_pairs={{0,1},{1,0},{2,3},{3,2},{4,5},{5,4},{6,7},{7,6},{8,9},{9,8},{10,11... | collective-permute-start | bytes 245768 | tf_op jit(solution)/shard_map/ppermute | solution.py:210

commit v23 on v21

--- a/solution.py
+++ b/solution.py
@@ -258,7 +258,7 @@
     )(block_pattern, sup_widths, l_panel[0])
 
     blocks = {0: packed}
-    others = sorted(range(row_count), key=lambda other: other > 0 and other % 2 == 0)
+    others = list(range(row_count))
     for other in range(1, row_count):
         blocks[other] = swap(packed, "row", other)
     own = [packed] + [swap(packed, "col", other) for other in range(1, col_count)]

time: 46.3 us -> 48.3 us (1.043)
  waiting for transfers between devices: 13.3 us -> 17.3 us
  starting transfers between devices: 21.6 us -> 19.6 us
    ppermute x20, waiting for transfers between devices: 13.3 us -> 17.3 us  [swap(): lax.ppermute(value, axis, [(i, i ^ bit) for i in range(lax.axis_size(axis...]
    ppermute x20, starting transfers between devices: 21.6 us -> 19.6 us  [swap(): lax.ppermute(value, axis, [(i, i ^ bit) for i in range(lax.axis_size(axis...]
  transfers between devices with their start and end apart: 20 -> 20, of which waited for: 10 -> 9; matrix products, arithmetic and copies ran while one was open for 0% -> 0% of each run, Pallas kernels for 10% -> 9%
where the time goes in v23:
time: 48.3 us; the launch traced here: 48.1 us
  starting transfers between devices  19.6 us (41%)
  waiting for transfers between devices  17.3 us (36%)
  Pallas kernels  7.5 us (16%)
  local copies, waits for them, and re-layouts  2.63 us (5%)
  between operations  0.79 us (2%)
    ppermute x20, starting transfers between devices, swap(): lax.ppermute(value, axis, [(i, i ^ bit) for i in range(lax.axis_size(axis...  19.6 us
    ppermute x20, waiting for transfers between devices, swap(): lax.ppermute(value, axis, [(i, i ^ bit) for i in range(lax.axis_size(axis...  17.3 us
    unnamed x10, local copies, waits for them, and re-layouts  2.63 us
    pallas_call x1, Pallas kernels, per_device(): pl.pallas_call(functools.partial(pack_kernel, supernodes, slot), in_specs...  2 us
    pallas_call x1, Pallas kernels, per_device(): pl.pallas_call(functools.partial(compute_kernel, others, col_count, super...  1.99 us
    pallas_call x1, Pallas kernels, per_device(): pl.pallas_call(functools.partial(prepare_kernel, (row_count, col_count)),...  1.38 us
    pallas_call x1, Pallas kernels, per_device(): pl.pallas_call(expand_kernel, in_specs=[VMEM_SPEC] * 9, out_specs=[VMEM_S...  1.14 us
    pallas_call x1, Pallas kernels, per_device(): pl.pallas_call(finish_kernel, in_specs=[VMEM_SPEC] * 4, out_specs=VMEM_SP...  0.99 us
  transfers between devices with their start and end apart: 20, of which 9 were waited for; matrix products, arithmetic and copies ran while one was open for 0% of the time, Pallas kernels for 9%

profile of v23, /device:TPU:0, one launch (start us, length us, event | category | flops | bytes accessed | tf_op | source)
XLA Modules:
  0.0 48.1 jit_solution(11981871666165507821)
XLA Ops:
  0.6 0.0 copy-start.2
  0.6 2.0 %pack.1.refs_0_ = bf16[640,128]{1,0:T(8,128)(2,1)} custom-call(s32[1,4]{1,0:T(1,128)} %pattern_ref.1, s32[4]{0:T(128)} %widths_ref.5, bf16[2,128,512]{2,1,0:T(8,128)(2,1)} %bitcast.7), custom_call_target="tpu_custom_call" | custom-call | tf_op jit(solution)/shard_map/pack/pallas_call | solution.py:252
  2.6 0.5 collective-permute-start
  3.1 2.6 %collective-permute-start.1 = (bf16[640,128]{1,0:T(8,128)(2,1)}, bf16[640,128]{1,0:T(8,128)(2,1)S(1)}, u32[]{:S(2)}, u32[]{:S(2)}) collective-permute-start(bf16[640,128]{1,0:T(8,128)(2,1)} %pack.1.refs_0_), channel_id=1, source_target_pairs={{0,2},{2,0},{4,6},{6,4},{1,3},{3,1},{5,7},{7,5},{8,10},{10,8},{12,... | collective-permute-start | bytes 491528 | tf_op jit(solution)/shard_map/ppermute | solution.py:205
  5.7 2.5 %collective-permute-start.3 = (bf16[640,128]{1,0:T(8,128)(2,1)}, bf16[640,128]{1,0:T(8,128)(2,1)S(1)}, u32[]{:S(2)}, u32[]{:S(2)}) collective-permute-start(bf16[640,128]{1,0:T(8,128)(2,1)} %pack.1.refs_0_), channel_id=1, source_target_pairs={{0,6},{2,4},{4,2},{6,0},{1,7},{3,5},{5,3},{7,1},{8,14},{10,12},{12... | collective-permute-start | bytes 491528 | tf_op jit(solution)/shard_map/ppermute | solution.py:205
  8.1 0.1 collective-permute-start.2
  8.3 0.1 pad_add_fusion.place_ref
  8.3 0.0 collective-permute-done.refs_1_
  8.3 0.0 copy-start.3
  8.3 0.0 copy-start.4
  8.3 0.0 copy-done.2
  8.3 0.6 %copy-done.3 = s32[4]{0:T(128)S(1)} copy-done((s32[4]{0:T(128)S(1)}, s32[4]{0:T(128)}, u32[]{:S(2)}) %copy-start.3) | copy-done | bytes 40
  9.0 0.0 copy-done.4
  9.0 0.0 copy-start
  9.0 0.9 %copy-done = bf16[640,128]{1,0:T(8,128)(2,1)S(1)} copy-done((bf16[640,128]{1,0:T(8,128)(2,1)S(1)}, bf16[640,128]{1,0:T(8,128)(2,1)}, u32[]{:S(2)}) %copy-start) | copy-done | bytes 163864
  9.9 0.0 copy-start.1
  9.9 1.0 %copy-done.1 = bf16[1,2,256,4,1,128]{5,3,4,2,1,0:T(4,128)(2,1)S(1)} copy-done((bf16[1,2,256,4,1,128]{5,3,4,2,1,0:T(4,128)(2,1)S(1)}, bf16[1,2,256,4,1,128]{5,3,4,2,1,0:T(4,128)(2,1)}, u32[]{:S(2)}) %copy-start.1) | copy-done | bytes 524312
  11.0 1.4 %prepare.1 = (bf16[2,256,512]{2,1,0:T(8,128)(2,1)S(1)}, bf16[512,512]{1,0:T(8,128)(2,1)S(1)}, f32[256,128]{1,0:T(8,128)S(1)}, bf16[256,320]{1,0:T(8,128)(2,1)S(1...) custom-call(s32[4]{0:T(128)S(1)} %copy-done.3, ...), custom_call_target="tpu_custom_call" | custom-call | flops 134217728 | bytes 1048576 | tf_op jit(solution)/shard_map/prepare/pallas_call | solution.py:266
  12.4 0.0 collective-permute-done.1.refs_1_
  12.4 1.6 %collective-permute-start.5 = (f32[256,128]{1,0:T(8,128)S(1)}, f32[256,128]{1,0:T(8,128)S(1)}, u32[]{:S(2)}, u32[]{:S(2)}) collective-permute-start(f32[256,128]{1,0:T(8,128)S(1)} %get-tuple-element.33), channel_id=1, source_target_pairs={{0,8},{8,0},{16,24},{24,16},{1,9},{9,1},{17,25},{25,17},{2,10},{10... | collective-permute-start | bytes 393224 | tf_op jit(solution)/shard_map/ppermute | solution.py:205
  13.9 1.5 %collective-permute-start.7 = (f32[256,128]{1,0:T(8,128)S(1)}, f32[256,128]{1,0:T(8,128)S(1)}, u32[]{:S(2)}, u32[]{:S(2)}) collective-permute-start(f32[256,128]{1,0:T(8,128)S(1)} %get-tuple-element.33), channel_id=1, source_target_pairs={{0,24},{8,16},{16,8},{24,0},{1,25},{9,17},{17,9},{25,1},{2,26},{10... | collective-permute-start | bytes 393224 | tf_op jit(solution)/shard_map/ppermute | solution.py:205
  15.4 0.5 %collective-permute-start.6 = (f32[256,128]{1,0:T(8,128)S(1)}, f32[256,128]{1,0:T(8,128)S(1)}, u32[]{:S(2)}, u32[]{:S(2)}) collective-permute-start(f32[256,128]{1,0:T(8,128)S(1)} %get-tuple-element.33), channel_id=1, source_target_pairs={{0,16},{8,24},{16,0},{24,8},{1,17},{9,25},{17,1},{25,9},{2,18},{10... | collective-permute-start | bytes 393224 | tf_op jit(solution)/shard_map/ppermute | solution.py:205
  15.9 1.0 %collective-permute-done.3.refs_3_ = bf16[640,128]{1,0:T(8,128)(2,1)S(1)} collective-permute-done((bf16[640,128]{1,0:T(8,128)(2,1)}, bf16[640,128]{1,0:T(8,128)(2,1)S(1)}, u32[]{:S(2)}, u32[]{:S(2)}) %collective-permute-start.3) | collective-permute-done | bytes 163872 | tf_op jit(solution)/shard_map/ppermute | solution.py:205
  16.9 6.7 %collective-permute-done.2.refs_2_ = bf16[640,128]{1,0:T(8,128)(2,1)S(1)} collective-permute-done((bf16[640,128]{1,0:T(8,128)(2,1)}, bf16[640,128]{1,0:T(8,128)(2,1)S(1)}, u32[]{:S(2)}, u32[]{:S(2)}) %collective-permute-start.2) | collective-permute-done | bytes 163872 | tf_op jit(solution)/shard_map/ppermute | solution.py:205
  23.6 2.0 %compute.1 = (f32[160,256]{1,0:T(8,128)S(1)}, f32[160,256]{1,0:T(8,128)S(1)}, f32[160,128]{1,0:T(8,128)S(1)}, f32[160,128]{1,0:T(8,128)S(1)}) custom-call(s32[4]{0:T(128)S(1)} %copy-done.3, f32[1,2]{1,0:T(1,128)S(1)} %copy-done.4, s32[2]{0:T(128)S(1)} %pad_add_fusion.place_ref, bf16[2,256,512]{2,1,0:T(8,128)(2,1)S(1)} %get-tuple-element.25.straight_ref, ...), custom_call_target="tpu_custom_call" | custom-call | tf_op jit(solution)/shard_map/compute/pallas_call | solution.py:297
  25.6 0.1 collective-permute-start.4
  25.7 1.3 %collective-permute-done.4 = f32[160,128]{1,0:T(8,128)S(1)} collective-permute-done((f32[160,128]{1,0:T(8,128)S(1)}, f32[160,128]{1,0:T(8,128)S(1)}, u32[]{:S(2)}, u32[]{:S(2)}) %collective-permute-start.4) | collective-permute-done | bytes 81952 | tf_op jit(solution)/shard_map/ppermute | solution.py:205
  27.0 0.0 collective-permute-done.5
  27.0 0.0 collective-permute-done.7
  27.0 0.0 collective-permute-done.6
  27.0 0.2 collective-permute-start.8
  27.3 2.6 %collective-permute-start.13 = (f32[160,128]{1,0:T(8,128)S(1)}, f32[160,128]{1,0:T(8,128)S(1)}, u32[]{:S(2)}, u32[]{:S(2)}) collective-permute-start(f32[160,128]{1,0:T(8,128)S(1)} %add.39), channel_id=1, source_target_pairs={{0,6},{2,4},{4,2},{6,0},{1,7},{3,5},{5,3},{7,1},{8,14},{10,12},{12... | collective-permute-start | bytes 245768 | tf_op jit(solution)/shard_map/ppermute | solution.py:205
  29.9 0.0 collective-permute-done.8
  29.9 2.5 %collective-permute-start.11 = (f32[160,256]{1,0:T(8,128)S(1)}, f32[160,256]{1,0:T(8,128)S(1)}, u32[]{:S(2)}, u32[]{:S(2)}) collective-permute-start(f32[160,256]{1,0:T(8,128)S(1)} %add.43), channel_id=1, source_target_pairs={{0,24},{8,16},{16,8},{24,0},{1,25},{9,17},{17,9},{25,1},{2,26},{10... | collective-permute-start | bytes 491528 | tf_op jit(solution)/shard_map/ppermute | solution.py:205
  32.4 0.5 %collective-permute-start.10 = (f32[160,256]{1,0:T(8,128)S(1)}, f32[160,256]{1,0:T(8,128)S(1)}, u32[]{:S(2)}, u32[]{:S(2)}) collective-permute-start(f32[160,256]{1,0:T(8,128)S(1)} %add.43), channel_id=1, source_target_pairs={{0,16},{8,24},{16,0},{24,8},{1,17},{9,25},{17,1},{25,9},{2,18},{10... | collective-permute-start | bytes 491528 | tf_op jit(solution)/shard_map/ppermute | solution.py:205
  32.9 0.5 %collective-permute-start.9 = (f32[160,256]{1,0:T(8,128)S(1)}, f32[160,256]{1,0:T(8,128)S(1)}, u32[]{:S(2)}, u32[]{:S(2)}) collective-permute-start(f32[160,256]{1,0:T(8,128)S(1)} %add.43), channel_id=1, source_target_pairs={{0,8},{8,0},{16,24},{24,16},{1,9},{9,1},{17,25},{25,17},{2,10},{10... | collective-permute-start | bytes 491528 | tf_op jit(solution)/shard_map/ppermute | solution.py:205
  33.5 0.3 collective-permute-done.13
  33.8 0.1 collective-permute-start.14
  33.9 0.1 collective-permute-start.18
  33.9 4.3 %collective-permute-done.14 = f32[160,128]{1,0:T(8,128)S(1)} collective-permute-done((f32[160,128]{1,0:T(8,128)S(1)}, f32[160,128]{1,0:T(8,128)S(1)}, u32[]{:S(2)}, u32[]{:S(2)}) %collective-permute-start.14) | collective-permute-done | bytes 81952 | tf_op jit(solution)/shard_map/ppermute | solution.py:205
  38.3 2.5 %collective-permute-start.17 = (f32[160,128]{1,0:T(8,128)S(1)}, f32[160,128]{1,0:T(8,128)S(1)}, u32[]{:S(2)}, u32[]{:S(2)}) collective-permute-start(f32[160,128]{1,0:T(8,128)S(1)} %add.48), channel_id=1, source_target_pairs={{0,24},{8,16},{16,8},{24,0},{1,25},{9,17},{17,9},{25,1},{2,26},{10... | collective-permute-start | bytes 245768 | tf_op jit(solution)/shard_map/ppermute | solution.py:205
  40.8 0.0 collective-permute-done.11
  40.8 0.5 %collective-permute-start.16 = (f32[160,128]{1,0:T(8,128)S(1)}, f32[160,128]{1,0:T(8,128)S(1)}, u32[]{:S(2)}, u32[]{:S(2)}) collective-permute-start(f32[160,128]{1,0:T(8,128)S(1)} %add.48), channel_id=1, source_target_pairs={{0,16},{8,24},{16,0},{24,8},{1,17},{9,25},{17,1},{25,9},{2,18},{10... | collective-permute-start | bytes 245768 | tf_op jit(solution)/shard_map/ppermute | solution.py:205
  41.3 0.0 collective-permute-done.10
  41.3 0.7 %collective-permute-start.15 = (f32[160,128]{1,0:T(8,128)S(1)}, f32[160,128]{1,0:T(8,128)S(1)}, u32[]{:S(2)}, u32[]{:S(2)}) collective-permute-start(f32[160,128]{1,0:T(8,128)S(1)} %add.48), channel_id=1, source_target_pairs={{0,8},{8,0},{16,24},{24,16},{1,9},{9,1},{17,25},{25,17},{2,10},{10... | collective-permute-start | bytes 245768 | tf_op jit(solution)/shard_map/ppermute | solution.py:205
  42.1 0.0 collective-permute-done.9
  42.1 0.1 collective-permute-start.12
  42.2 1.5 %collective-permute-done.17 = f32[160,128]{1,0:T(8,128)S(1)} collective-permute-done((f32[160,128]{1,0:T(8,128)S(1)}, f32[160,128]{1,0:T(8,128)S(1)}, u32[]{:S(2)}, u32[]{:S(2)}) %collective-permute-start.17) | collective-permute-done | bytes 81952 | tf_op jit(solution)/shard_map/ppermute | solution.py:205
  43.7 1.6 %collective-permute-done.16 = f32[160,128]{1,0:T(8,128)S(1)} collective-permute-done((f32[160,128]{1,0:T(8,128)S(1)}, f32[160,128]{1,0:T(8,128)S(1)}, u32[]{:S(2)}, u32[]{:S(2)}) %collective-permute-start.16) | collective-permute-done | bytes 81952 | tf_op jit(solution)/shard_map/ppermute | solution.py:205
  45.3 0.5 %collective-permute-done.15 = f32[160,128]{1,0:T(8,128)S(1)} collective-permute-done((f32[160,128]{1,0:T(8,128)S(1)}, f32[160,128]{1,0:T(8,128)S(1)}, u32[]{:S(2)}, u32[]{:S(2)}) %collective-permute-start.15) | collective-permute-done | bytes 81952 | tf_op jit(solution)/shard_map/ppermute | solution.py:205
  45.8 0.1 collective-permute-start.19
  45.9 0.0 collective-permute-done.18.other_term_ref
  45.9 0.0 collective-permute-done.12.other_d_ref
  45.9 1.1 %expand.1 = (f32[256,256]{1,0:T(8,128)}, f32[512,128]{1,0:T(8,128)S(1)}) custom-call(bf16[256,320]{1,0:T(8,128)(2,1)S(1)} %get-tuple-element.21.pick_d_ref, bf16[512,160]{1,0:T(8,128)(2,1)S(1)} %get-tuple-element.22.pick_ref, f32[512,128]{1,0:T(8,128)S(1)} %get-tuple-element.23.keep_ref, f32[8,128]{1,0:T(8,128)S(1)} %get-tuple-element.24.upper_ref, ...), custom_call_target="tpu_custom_call" | custom-call | flops 503316480 | bytes 2097152 | tf_op jit(solution)/shard_map/expand/pallas_call | solution.py:327
  47.0 0.1 collective-permute-done.19.other_t_ref
  47.1 1.0 %finish.1 = f32[512,128]{1,0:T(8,128)} custom-call(bf16[512,160]{1,0:T(8,128)(2,1)S(1)} %get-tuple-element.38.pick_ref, f32[512,128]{1,0:T(8,128)S(1)} %get-tuple-element.23.keep_ref, f32[160,128]{1,0:T(8,128)S(1)} %collective-permute-done.19.other_t_ref, f32[512,128]{1,0:T(8,128)S(1)} %get-tuple-element.39.partial_ref), custom_call_target="tpu_custom_call" | custom-call | tf_op jit(solution)/shard_map/finish/pallas_call | solution.py:346
  (7 shorter events, 0.1 us)
Async XLA Ops:
  0.6 7.7 %copy-start.2 = (bf16[1,2,512,128]{3,2,1,0:T(8,128)(2,1)S(1)}, bf16[1,2,512,128]{3,2,1,0:T(8,128)(2,1)}, u32[]{:S(2)}) copy-start(bf16[1,2,512,128]{3,2,1,0:T(8,128)(2,1)} %param.10) | copy-start | bytes 786436
  2.6 5.7 %collective-permute-start = (bf16[640,128]{1,0:T(8,128)(2,1)}, bf16[640,128]{1,0:T(8,128)(2,1)S(1)}, u32[]{:S(2)}, u32[]{:S(2)}) collective-permute-start(bf16[640,128]{1,0:T(8,128)(2,1)} %pack.1.refs_0_), channel_id=1, source_target_pairs={{0,1},{1,0},{2,3},{3,2},{4,5},{5,4},{6,7},{7,6},{8,9},{9,8},{10,11... | collective-permute-start | bytes 491528 | tf_op jit(solution)/shard_map/ppermute | solution.py:205
  3.1 9.3 %collective-permute-start.1 = (bf16[640,128]{1,0:T(8,128)(2,1)}, bf16[640,128]{1,0:T(8,128)(2,1)S(1)}, u32[]{:S(2)}, u32[]{:S(2)}) collective-permute-start(bf16[640,128]{1,0:T(8,128)(2,1)} %pack.1.refs_0_), channel_id=1, source_target_pairs={{0,2},{2,0},{4,6},{6,4},{1,3},{3,1},{5,7},{7,5},{8,10},{10,8},{12,... | collective-permute-start | bytes 491528 | tf_op jit(solution)/shard_map/ppermute | solution.py:205
  5.7 11.3 %collective-permute-start.3 = (bf16[640,128]{1,0:T(8,128)(2,1)}, bf16[640,128]{1,0:T(8,128)(2,1)S(1)}, u32[]{:S(2)}, u32[]{:S(2)}) collective-permute-start(bf16[640,128]{1,0:T(8,128)(2,1)} %pack.1.refs_0_), channel_id=1, source_target_pairs={{0,6},{2,4},{4,2},{6,0},{1,7},{3,5},{5,3},{7,1},{8,14},{10,12},{12... | collective-permute-start | bytes 491528 | tf_op jit(solution)/shard_map/ppermute | solution.py:205
  8.1 15.5 %collective-permute-start.2 = (bf16[640,128]{1,0:T(8,128)(2,1)}, bf16[640,128]{1,0:T(8,128)(2,1)S(1)}, u32[]{:S(2)}, u32[]{:S(2)}) collective-permute-start(bf16[640,128]{1,0:T(8,128)(2,1)} %pack.1.refs_0_), channel_id=1, source_target_pairs={{0,4},{2,6},{4,0},{6,2},{1,5},{3,7},{5,1},{7,3},{8,12},{10,14},{12... | collective-permute-start | bytes 491528 | tf_op jit(solution)/shard_map/ppermute | solution.py:205
  8.3 0.7 %copy-start.3 = (s32[4]{0:T(128)S(1)}, s32[4]{0:T(128)}, u32[]{:S(2)}) copy-start(s32[4]{0:T(128)} %widths_ref.5) | copy-start | bytes 52
  8.3 0.7 %copy-start.4 = (f32[1,2]{1,0:T(1,128)S(1)}, f32[1,2]{1,0:T(1,128)}, u32[]{:S(2)}) copy-start(f32[1,2]{1,0:T(1,128)} %weights_ref.3) | copy-start | bytes 28
  9.0 0.9 %copy-start = (bf16[640,128]{1,0:T(8,128)(2,1)S(1)}, bf16[640,128]{1,0:T(8,128)(2,1)}, u32[]{:S(2)}) copy-start(bf16[640,128]{1,0:T(8,128)(2,1)} %pack.1.refs_0_) | copy-start | bytes 491524
  9.9 1.0 %copy-start.1 = (bf16[1,2,256,4,1,128]{5,3,4,2,1,0:T(4,128)(2,1)S(1)}, bf16[1,2,256,4,1,128]{5,3,4,2,1,0:T(4,128)(2,1)}, u32[]{:S(2)}) copy-start(bf16[1,2,256,4,1,128]{5,3,4,2,1,0:T(4,128)(2,1)} %param.6) | copy-start | bytes 1572868
  12.4 14.6 %collective-permute-start.5 = (f32[256,128]{1,0:T(8,128)S(1)}, f32[256,128]{1,0:T(8,128)S(1)}, u32[]{:S(2)}, u32[]{:S(2)}) collective-permute-start(f32[256,128]{1,0:T(8,128)S(1)} %get-tuple-element.33), channel_id=1, source_target_pairs={{0,8},{8,0},{16,24},{24,16},{1,9},{9,1},{17,25},{25,17},{2,10},{10... | collective-permute-start | bytes 393224 | tf_op jit(solution)/shard_map/ppermute | solution.py:205
  13.9 13.1 %collective-permute-start.7 = (f32[256,128]{1,0:T(8,128)S(1)}, f32[256,128]{1,0:T(8,128)S(1)}, u32[]{:S(2)}, u32[]{:S(2)}) collective-permute-start(f32[256,128]{1,0:T(8,128)S(1)} %get-tuple-element.33), channel_id=1, source_target_pairs={{0,24},{8,16},{16,8},{24,0},{1,25},{9,17},{17,9},{25,1},{2,26},{10... | collective-permute-start | bytes 393224 | tf_op jit(solution)/shard_map/ppermute | solution.py:205
  15.4 11.6 %collective-permute-start.6 = (f32[256,128]{1,0:T(8,128)S(1)}, f32[256,128]{1,0:T(8,128)S(1)}, u32[]{:S(2)}, u32[]{:S(2)}) collective-permute-start(f32[256,128]{1,0:T(8,128)S(1)} %get-tuple-element.33), channel_id=1, source_target_pairs={{0,16},{8,24},{16,0},{24,8},{1,17},{9,25},{17,1},{25,9},{2,18},{10... | collective-permute-start | bytes 393224 | tf_op jit(solution)/shard_map/ppermute | solution.py:205
  25.6 1.3 %collective-permute-start.4 = (f32[160,128]{1,0:T(8,128)S(1)}, f32[160,128]{1,0:T(8,128)S(1)}, u32[]{:S(2)}, u32[]{:S(2)}) collective-permute-start(f32[160,128]{1,0:T(8,128)S(1)} %get-tuple-element.31), channel_id=1, source_target_pairs={{0,1},{1,0},{2,3},{3,2},{4,5},{5,4},{6,7},{7,6},{8,9},{9,8},{10,11... | collective-permute-start | bytes 245768 | tf_op jit(solution)/shard_map/ppermute | solution.py:205
  27.0 2.8 %collective-permute-start.8 = (f32[160,256]{1,0:T(8,128)S(1)}, f32[160,256]{1,0:T(8,128)S(1)}, u32[]{:S(2)}, u32[]{:S(2)}) collective-permute-start(f32[160,256]{1,0:T(8,128)S(1)} %get-tuple-element.34), channel_id=1, source_target_pairs={{0,1},{1,0},{2,3},{3,2},{4,5},{5,4},{6,7},{7,6},{8,9},{9,8},{10,11... | collective-permute-start | bytes 491528 | tf_op jit(solution)/shard_map/ppermute | solution.py:205
  27.3 6.5 %collective-permute-start.13 = (f32[160,128]{1,0:T(8,128)S(1)}, f32[160,128]{1,0:T(8,128)S(1)}, u32[]{:S(2)}, u32[]{:S(2)}) collective-permute-start(f32[160,128]{1,0:T(8,128)S(1)} %add.39), channel_id=1, source_target_pairs={{0,6},{2,4},{4,2},{6,0},{1,7},{3,5},{5,3},{7,1},{8,14},{10,12},{12... | collective-permute-start | bytes 245768 | tf_op jit(solution)/shard_map/ppermute | solution.py:205
  29.9 10.9 %collective-permute-start.11 = (f32[160,256]{1,0:T(8,128)S(1)}, f32[160,256]{1,0:T(8,128)S(1)}, u32[]{:S(2)}, u32[]{:S(2)}) collective-permute-start(f32[160,256]{1,0:T(8,128)S(1)} %add.43), channel_id=1, source_target_pairs={{0,24},{8,16},{16,8},{24,0},{1,25},{9,17},{17,9},{25,1},{2,26},{10... | collective-permute-start | bytes 491528 | tf_op jit(solution)/shard_map/ppermute | solution.py:205
  32.4 8.9 %collective-permute-start.10 = (f32[160,256]{1,0:T(8,128)S(1)}, f32[160,256]{1,0:T(8,128)S(1)}, u32[]{:S(2)}, u32[]{:S(2)}) collective-permute-start(f32[160,256]{1,0:T(8,128)S(1)} %add.43), channel_id=1, source_target_pairs={{0,16},{8,24},{16,0},{24,8},{1,17},{9,25},{17,1},{25,9},{2,18},{10... | collective-permute-start | bytes 491528 | tf_op jit(solution)/shard_map/ppermute | solution.py:205
  32.9 9.1 %collective-permute-start.9 = (f32[160,256]{1,0:T(8,128)S(1)}, f32[160,256]{1,0:T(8,128)S(1)}, u32[]{:S(2)}, u32[]{:S(2)}) collective-permute-start(f32[160,256]{1,0:T(8,128)S(1)} %add.43), channel_id=1, source_target_pairs={{0,8},{8,0},{16,24},{24,16},{1,9},{9,1},{17,25},{25,17},{2,10},{10... | collective-permute-start | bytes 491528 | tf_op jit(solution)/shard_map/ppermute | solution.py:205
  33.8 4.5 %collective-permute-start.14 = (f32[160,128]{1,0:T(8,128)S(1)}, f32[160,128]{1,0:T(8,128)S(1)}, u32[]{:S(2)}, u32[]{:S(2)}) collective-permute-start(f32[160,128]{1,0:T(8,128)S(1)} %add.47), channel_id=1, source_target_pairs={{0,2},{2,0},{4,6},{6,4},{1,3},{3,1},{5,7},{7,5},{8,10},{10,8},{12,... | collective-permute-start | bytes 245768 | tf_op jit(solution)/shard_map/ppermute | solution.py:205
  33.9 12.0 %collective-permute-start.18 = (f32[256,128]{1,0:T(8,128)S(1)}, f32[256,128]{1,0:T(8,128)S(1)}, u32[]{:S(2)}, u32[]{:S(2)}) collective-permute-start(f32[256,128]{1,0:T(8,128)S(1)} %add_add_fusion.1.mine_term_ref), channel_id=1, source_target_pairs={{0,1},{1,0},{2,3},{3,2},{4,5},{5,4},{6,7},{7,6},{8,9},{9,8},{10,11... | collective-permute-start | bytes 393224 | tf_op jit(solution)/shard_map/ppermute | solution.py:205
  38.3 5.4 %collective-permute-start.17 = (f32[160,128]{1,0:T(8,128)S(1)}, f32[160,128]{1,0:T(8,128)S(1)}, u32[]{:S(2)}, u32[]{:S(2)}) collective-permute-start(f32[160,128]{1,0:T(8,128)S(1)} %add.48), channel_id=1, source_target_pairs={{0,24},{8,16},{16,8},{24,0},{1,25},{9,17},{17,9},{25,1},{2,26},{10... | collective-permute-start | bytes 245768 | tf_op jit(solution)/shard_map/ppermute | solution.py:205
  40.8 4.4 %collective-permute-start.16 = (f32[160,128]{1,0:T(8,128)S(1)}, f32[160,128]{1,0:T(8,128)S(1)}, u32[]{:S(2)}, u32[]{:S(2)}) collective-permute-start(f32[160,128]{1,0:T(8,128)S(1)} %add.48), channel_id=1, source_target_pairs={{0,16},{8,24},{16,0},{24,8},{1,17},{9,25},{17,1},{25,9},{2,18},{10... | collective-permute-start | bytes 245768 | tf_op jit(solution)/shard_map/ppermute | solution.py:205
  41.3 4.4 %collective-permute-start.15 = (f32[160,128]{1,0:T(8,128)S(1)}, f32[160,128]{1,0:T(8,128)S(1)}, u32[]{:S(2)}, u32[]{:S(2)}) collective-permute-start(f32[160,128]{1,0:T(8,128)S(1)} %add.48), channel_id=1, source_target_pairs={{0,8},{8,0},{16,24},{24,16},{1,9},{9,1},{17,25},{25,17},{2,10},{10... | collective-permute-start | bytes 245768 | tf_op jit(solution)/shard_map/ppermute | solution.py:205
  42.1 3.8 %collective-permute-start.12 = (f32[160,256]{1,0:T(8,128)S(1)}, f32[160,256]{1,0:T(8,128)S(1)}, u32[]{:S(2)}, u32[]{:S(2)}) collective-permute-start(f32[160,256]{1,0:T(8,128)S(1)} %add_add_fusion.mine_d_ref), channel_id=1, source_target_pairs={{0,1},{1,0},{2,3},{3,2},{4,5},{5,4},{6,7},{7,6},{8,9},{9,8},{10,11... | collective-permute-start | bytes 491528 | tf_op jit(solution)/shard_map/ppermute | solution.py:205
  45.8 1.3 %collective-permute-start.19 = (f32[160,128]{1,0:T(8,128)S(1)}, f32[160,128]{1,0:T(8,128)S(1)}, u32[]{:S(2)}, u32[]{:S(2)}) collective-permute-start(f32[160,128]{1,0:T(8,128)S(1)} %add_add_fusion.2.mine_t_ref), channel_id=1, source_target_pairs={{0,1},{1,0},{2,3},{3,2},{4,5},{5,4},{6,7},{7,6},{8,9},{9,8},{10,11... | collective-permute-start | bytes 245768 | tf_op jit(solution)/shard_map/ppermute | solution.py:205

commit v24 on v21

--- a/solution.py
+++ b/solution.py
@@ -313,7 +313,7 @@
     )
 
     tie = lax.optimization_barrier
-    products, send_d, term = tie((keep_t + swap(send_t, "col", top), send_d, term))
+    products, term = tie((keep_t + swap(send_t, "col", top), term))
     term = gather_but_last(term, "col")
     products = scatter_rest(products, "col")
     for bit in bits_of(row_count)[::-1]:

time: 46.3 us -> 45.8 us (0.989)
  waiting for transfers between devices: 13.3 us -> 12.5 us
    ppermute x20, waiting for transfers between devices: 13.3 us -> 12.5 us  [swap(): lax.ppermute(value, axis, [(i, i ^ bit) for i in range(lax.axis_size(axis...]
  transfers between devices with their start and end apart: 20 -> 20, of which waited for: 10 -> 9; matrix products, arithmetic and copies ran while one was open for 0% -> 0% of each run, Pallas kernels for 10% -> 10%
where the time goes in v24:
time: 45.8 us; the launch traced here: 45.6 us
  starting transfers between devices  22 us (48%)
  waiting for transfers between devices  12.5 us (27%)
  Pallas kernels  7.51 us (16%)
  local copies, waits for them, and re-layouts  2.63 us (6%)
  between operations  0.76 us (2%)
    ppermute x20, starting transfers between devices, swap(): lax.ppermute(value, axis, [(i, i ^ bit) for i in range(lax.axis_size(axis...  22 us
    ppermute x20, waiting for transfers between devices, swap(): lax.ppermute(value, axis, [(i, i ^ bit) for i in range(lax.axis_size(axis...  12.5 us
    unnamed x10, local copies, waits for them, and re-layouts  2.63 us
    pallas_call x1, Pallas kernels, per_device(): pl.pallas_call(functools.partial(pack_kernel, supernodes, slot), in_specs...  2 us
    pallas_call x1, Pallas kernels, per_device(): pl.pallas_call(functools.partial(compute_kernel, others, col_count, super...  1.99 us
    pallas_call x1, Pallas kernels, per_device(): pl.pallas_call(functools.partial(prepare_kernel, (row_count, col_count)),...  1.38 us
    pallas_call x1, Pallas kernels, per_device(): pl.pallas_call(expand_kernel, in_specs=[VMEM_SPEC] * 9, out_specs=[VMEM_S...  1.14 us
    pallas_call x1, Pallas kernels, per_device(): pl.pallas_call(finish_kernel, in_specs=[VMEM_SPEC] * 4, out_specs=VMEM_SP...  0.99 us
  transfers between devices with their start and end apart: 20, of which 9 were waited for; matrix products, arithmetic and copies ran while one was open for 0% of the time, Pallas kernels for 10%

profile of v24, /device:TPU:0, one launch (start us, length us, event | category | flops | bytes accessed | tf_op | source)
XLA Modules:
  0.0 45.6 jit_solution(9232913141012928065)
XLA Ops:
  0.6 0.0 copy-start.2
  0.6 2.0 %pack.1.refs_0_ = bf16[640,128]{1,0:T(8,128)(2,1)} custom-call(s32[1,4]{1,0:T(1,128)} %pattern_ref.1, s32[4]{0:T(128)} %widths_ref.5, bf16[2,128,512]{2,1,0:T(8,128)(2,1)} %bitcast.7), custom_call_target="tpu_custom_call" | custom-call | tf_op jit(solution)/shard_map/pack/pallas_call | solution.py:252
  2.6 0.5 collective-permute-start
  3.1 2.6 %collective-permute-start.1 = (bf16[640,128]{1,0:T(8,128)(2,1)}, bf16[640,128]{1,0:T(8,128)(2,1)S(1)}, u32[]{:S(2)}, u32[]{:S(2)}) collective-permute-start(bf16[640,128]{1,0:T(8,128)(2,1)} %pack.1.refs_0_), channel_id=1, source_target_pairs={{0,2},{2,0},{4,6},{6,4},{1,3},{3,1},{5,7},{7,5},{8,10},{10,8},{12,... | collective-permute-start | bytes 491528 | tf_op jit(solution)/shard_map/ppermute | solution.py:205
  5.7 2.6 %collective-permute-start.3 = (bf16[640,128]{1,0:T(8,128)(2,1)}, bf16[640,128]{1,0:T(8,128)(2,1)S(1)}, u32[]{:S(2)}, u32[]{:S(2)}) collective-permute-start(bf16[640,128]{1,0:T(8,128)(2,1)} %pack.1.refs_0_), channel_id=1, source_target_pairs={{0,4},{2,6},{4,0},{6,2},{1,5},{3,7},{5,1},{7,3},{8,12},{10,14},{12... | collective-permute-start | bytes 491528 | tf_op jit(solution)/shard_map/ppermute | solution.py:205
  8.3 0.0 collective-permute-start.2
  8.3 0.1 pad_add_fusion.place_ref
  8.3 0.0 collective-permute-done.refs_1_
  8.3 0.0 copy-start.3
  8.3 0.0 copy-start.4
  8.3 0.0 copy-done.2
  8.3 0.6 %copy-done.3 = s32[4]{0:T(128)S(1)} copy-done((s32[4]{0:T(128)S(1)}, s32[4]{0:T(128)}, u32[]{:S(2)}) %copy-start.3) | copy-done | bytes 40
  9.0 0.0 copy-done.4
  9.0 0.0 copy-start
  9.0 0.9 %copy-done = bf16[640,128]{1,0:T(8,128)(2,1)S(1)} copy-done((bf16[640,128]{1,0:T(8,128)(2,1)S(1)}, bf16[640,128]{1,0:T(8,128)(2,1)}, u32[]{:S(2)}) %copy-start) | copy-done | bytes 163864
  9.9 0.0 copy-start.1
  9.9 1.0 %copy-done.1 = bf16[1,2,256,4,1,128]{5,3,4,2,1,0:T(4,128)(2,1)S(1)} copy-done((bf16[1,2,256,4,1,128]{5,3,4,2,1,0:T(4,128)(2,1)S(1)}, bf16[1,2,256,4,1,128]{5,3,4,2,1,0:T(4,128)(2,1)}, u32[]{:S(2)}) %copy-start.1) | copy-done | bytes 524312
  11.0 1.4 %prepare.1 = (bf16[2,256,512]{2,1,0:T(8,128)(2,1)S(1)}, bf16[512,512]{1,0:T(8,128)(2,1)S(1)}, f32[256,128]{1,0:T(8,128)S(1)}, bf16[256,320]{1,0:T(8,128)(2,1)S(1...) custom-call(s32[4]{0:T(128)S(1)} %copy-done.3, ...), custom_call_target="tpu_custom_call" | custom-call | flops 134217728 | bytes 1048576 | tf_op jit(solution)/shard_map/prepare/pallas_call | solution.py:266
  12.4 1.5 %collective-permute-done.1.refs_1_ = bf16[640,128]{1,0:T(8,128)(2,1)S(1)} collective-permute-done((bf16[640,128]{1,0:T(8,128)(2,1)}, bf16[640,128]{1,0:T(8,128)(2,1)S(1)}, u32[]{:S(2)}, u32[]{:S(2)}) %collective-permute-start.1) | collective-permute-done | bytes 163872 | tf_op jit(solution)/shard_map/ppermute | solution.py:205
  13.8 1.7 %collective-permute-start.10 = (f32[256,128]{1,0:T(8,128)S(1)}, f32[256,128]{1,0:T(8,128)S(1)}, u32[]{:S(2)}, u32[]{:S(2)}) collective-permute-start(f32[256,128]{1,0:T(8,128)S(1)} %get-tuple-element.32), channel_id=1, source_target_pairs={{0,8},{8,0},{16,24},{24,16},{1,9},{9,1},{17,25},{25,17},{2,10},{10... | collective-permute-start | bytes 393224 | tf_op jit(solution)/shard_map/ppermute | solution.py:205
  15.5 1.5 %collective-permute-start.12 = (f32[256,128]{1,0:T(8,128)S(1)}, f32[256,128]{1,0:T(8,128)S(1)}, u32[]{:S(2)}, u32[]{:S(2)}) collective-permute-start(f32[256,128]{1,0:T(8,128)S(1)} %get-tuple-element.32), channel_id=1, source_target_pairs={{0,24},{8,16},{16,8},{24,0},{1,25},{9,17},{17,9},{25,1},{2,26},{10... | collective-permute-start | bytes 393224 | tf_op jit(solution)/shard_map/ppermute | solution.py:205
  17.0 0.3 collective-permute-start.11
  17.3 3.5 %collective-permute-done.3.refs_3_ = bf16[640,128]{1,0:T(8,128)(2,1)S(1)} collective-permute-done((bf16[640,128]{1,0:T(8,128)(2,1)}, bf16[640,128]{1,0:T(8,128)(2,1)S(1)}, u32[]{:S(2)}, u32[]{:S(2)}) %collective-permute-start.3) | collective-permute-done | bytes 163872 | tf_op jit(solution)/shard_map/ppermute | solution.py:205
  20.9 0.0 collective-permute-done.2.refs_2_
  20.9 2.0 %compute.1 = (f32[160,256]{1,0:T(8,128)S(1)}, f32[160,256]{1,0:T(8,128)S(1)}, f32[160,128]{1,0:T(8,128)S(1)}, f32[160,128]{1,0:T(8,128)S(1)}) custom-call(s32[4]{0:T(128)S(1)} %copy-done.3, f32[1,2]{1,0:T(1,128)S(1)} %copy-done.4, s32[2]{0:T(128)S(1)} %pad_add_fusion.place_ref, bf16[2,256,512]{2,1,0:T(8,128)(2,1)S(1)} %get-tuple-element.24.straight_ref, ...), custom_call_target="tpu_custom_call" | custom-call | tf_op jit(solution)/shard_map/compute/pallas_call | solution.py:297
  22.9 0.1 collective-permute-start.9
  23.0 0.5 %collective-permute-start.4 = (f32[160,256]{1,0:T(8,128)S(1)}, f32[160,256]{1,0:T(8,128)S(1)}, u32[]{:S(2)}, u32[]{:S(2)}) collective-permute-start(f32[160,256]{1,0:T(8,128)S(1)} %get-tuple-element.29), channel_id=1, source_target_pairs={{0,1},{1,0},{2,3},{3,2},{4,5},{5,4},{6,7},{7,6},{8,9},{9,8},{10,11... | collective-permute-start | bytes 491528 | tf_op jit(solution)/shard_map/ppermute | solution.py:205
  23.5 0.8 %collective-permute-done.9 = f32[160,128]{1,0:T(8,128)S(1)} collective-permute-done((f32[160,128]{1,0:T(8,128)S(1)}, f32[160,128]{1,0:T(8,128)S(1)}, u32[]{:S(2)}, u32[]{:S(2)}) %collective-permute-start.9) | collective-permute-done | bytes 81952 | tf_op jit(solution)/shard_map/ppermute | solution.py:205
  24.2 0.0 collective-permute-done.10
  24.3 0.0 collective-permute-done.12
  24.3 0.1 collective-permute-done.11
  24.4 2.8 %collective-permute-start.13 = (f32[160,128]{1,0:T(8,128)S(1)}, f32[160,128]{1,0:T(8,128)S(1)}, u32[]{:S(2)}, u32[]{:S(2)}) collective-permute-start(f32[160,128]{1,0:T(8,128)S(1)} %add.43), channel_id=1, source_target_pairs={{0,6},{2,4},{4,2},{6,0},{1,7},{3,5},{5,3},{7,1},{8,14},{10,12},{12... | collective-permute-start | bytes 245768 | tf_op jit(solution)/shard_map/ppermute | solution.py:205
  27.2 0.0 collective-permute-done.4
  27.3 2.1 %collective-permute-start.7 = (f32[160,256]{1,0:T(8,128)S(1)}, f32[160,256]{1,0:T(8,128)S(1)}, u32[]{:S(2)}, u32[]{:S(2)}) collective-permute-start(f32[160,256]{1,0:T(8,128)S(1)} %add.39), channel_id=1, source_target_pairs={{0,24},{8,16},{16,8},{24,0},{1,25},{9,17},{17,9},{25,1},{2,26},{10... | collective-permute-start | bytes 491528 | tf_op jit(solution)/shard_map/ppermute | solution.py:205
  29.4 0.9 %collective-permute-start.6 = (f32[160,256]{1,0:T(8,128)S(1)}, f32[160,256]{1,0:T(8,128)S(1)}, u32[]{:S(2)}, u32[]{:S(2)}) collective-permute-start(f32[160,256]{1,0:T(8,128)S(1)} %add.39), channel_id=1, source_target_pairs={{0,16},{8,24},{16,0},{24,8},{1,17},{9,25},{17,1},{25,9},{2,18},{10... | collective-permute-start | bytes 491528 | tf_op jit(solution)/shard_map/ppermute | solution.py:205
  30.3 0.5 %collective-permute-start.5 = (f32[160,256]{1,0:T(8,128)S(1)}, f32[160,256]{1,0:T(8,128)S(1)}, u32[]{:S(2)}, u32[]{:S(2)}) collective-permute-start(f32[160,256]{1,0:T(8,128)S(1)} %add.39), channel_id=1, source_target_pairs={{0,8},{8,0},{16,24},{24,16},{1,9},{9,1},{17,25},{25,17},{2,10},{10... | collective-permute-start | bytes 491528 | tf_op jit(solution)/shard_map/ppermute | solution.py:205
  30.8 0.0 collective-permute-done.13
  30.8 2.3 %collective-permute-start.14 = (f32[160,128]{1,0:T(8,128)S(1)}, f32[160,128]{1,0:T(8,128)S(1)}, u32[]{:S(2)}, u32[]{:S(2)}) collective-permute-start(f32[160,128]{1,0:T(8,128)S(1)} %add.47), channel_id=1, source_target_pairs={{0,2},{2,0},{4,6},{6,4},{1,3},{3,1},{5,7},{7,5},{8,10},{10,8},{12,... | collective-permute-start | bytes 245768 | tf_op jit(solution)/shard_map/ppermute | solution.py:205
  33.1 0.0 collective-permute-start.18
  33.1 2.6 %collective-permute-done.14 = f32[160,128]{1,0:T(8,128)S(1)} collective-permute-done((f32[160,128]{1,0:T(8,128)S(1)}, f32[160,128]{1,0:T(8,128)S(1)}, u32[]{:S(2)}, u32[]{:S(2)}) %collective-permute-start.14) | collective-permute-done | bytes 81952 | tf_op jit(solution)/shard_map/ppermute | solution.py:205
  35.8 2.5 %collective-permute-start.17 = (f32[160,128]{1,0:T(8,128)S(1)}, f32[160,128]{1,0:T(8,128)S(1)}, u32[]{:S(2)}, u32[]{:S(2)}) collective-permute-start(f32[160,128]{1,0:T(8,128)S(1)} %add.48), channel_id=1, source_target_pairs={{0,24},{8,16},{16,8},{24,0},{1,25},{9,17},{17,9},{25,1},{2,26},{10... | collective-permute-start | bytes 245768 | tf_op jit(solution)/shard_map/ppermute | solution.py:205
  38.2 0.0 collective-permute-done.7
  38.2 0.6 %collective-permute-start.16 = (f32[160,128]{1,0:T(8,128)S(1)}, f32[160,128]{1,0:T(8,128)S(1)}, u32[]{:S(2)}, u32[]{:S(2)}) collective-permute-start(f32[160,128]{1,0:T(8,128)S(1)} %add.48), channel_id=1, source_target_pairs={{0,16},{8,24},{16,0},{24,8},{1,17},{9,25},{17,1},{25,9},{2,18},{10... | collective-permute-start | bytes 245768 | tf_op jit(solution)/shard_map/ppermute | solution.py:205
  38.8 0.0 collective-permute-done.6
  38.8 0.5 %collective-permute-start.15 = (f32[160,128]{1,0:T(8,128)S(1)}, f32[160,128]{1,0:T(8,128)S(1)}, u32[]{:S(2)}, u32[]{:S(2)}) collective-permute-start(f32[160,128]{1,0:T(8,128)S(1)} %add.48), channel_id=1, source_target_pairs={{0,8},{8,0},{16,24},{24,16},{1,9},{9,1},{17,25},{25,17},{2,10},{10... | collective-permute-start | bytes 245768 | tf_op jit(solution)/shard_map/ppermute | solution.py:205
  39.3 0.0 collective-permute-done.5
  39.4 0.1 collective-permute-start.8
  39.5 1.8 %collective-permute-done.17 = f32[160,128]{1,0:T(8,128)S(1)} collective-permute-done((f32[160,128]{1,0:T(8,128)S(1)}, f32[160,128]{1,0:T(8,128)S(1)}, u32[]{:S(2)}, u32[]{:S(2)}) %collective-permute-start.17) | collective-permute-done | bytes 81952 | tf_op jit(solution)/shard_map/ppermute | solution.py:205
  41.3 1.4 %collective-permute-done.16 = f32[160,128]{1,0:T(8,128)S(1)} collective-permute-done((f32[160,128]{1,0:T(8,128)S(1)}, f32[160,128]{1,0:T(8,128)S(1)}, u32[]{:S(2)}, u32[]{:S(2)}) %collective-permute-start.16) | collective-permute-done | bytes 81952 | tf_op jit(solution)/shard_map/ppermute | solution.py:205
  42.7 0.6 %collective-permute-done.15 = f32[160,128]{1,0:T(8,128)S(1)} collective-permute-done((f32[160,128]{1,0:T(8,128)S(1)}, f32[160,128]{1,0:T(8,128)S(1)}, u32[]{:S(2)}, u32[]{:S(2)}) %collective-permute-start.15) | collective-permute-done | bytes 81952 | tf_op jit(solution)/shard_map/ppermute | solution.py:205
  43.3 0.1 collective-permute-start.19
  43.3 0.0 collective-permute-done.18.other_term_ref
  43.4 0.0 collective-permute-done.8.other_d_ref
  43.4 1.1 %expand.1 = (f32[256,256]{1,0:T(8,128)}, f32[512,128]{1,0:T(8,128)S(1)}) custom-call(bf16[256,320]{1,0:T(8,128)(2,1)S(1)} %get-tuple-element.20.pick_d_ref, bf16[512,160]{1,0:T(8,128)(2,1)S(1)} %get-tuple-element.21.pick_ref, f32[512,128]{1,0:T(8,128)S(1)} %get-tuple-element.22.keep_ref, f32[8,128]{1,0:T(8,128)S(1)} %get-tuple-element.23.upper_ref, ...), custom_call_target="tpu_custom_call" | custom-call | flops 503316480 | bytes 2097152 | tf_op jit(solution)/shard_map/expand/pallas_call | solution.py:327
  44.5 0.1 collective-permute-done.19.other_t_ref
  44.6 1.0 %finish.1 = f32[512,128]{1,0:T(8,128)} custom-call(bf16[512,160]{1,0:T(8,128)(2,1)S(1)} %get-tuple-element.36.pick_ref, f32[512,128]{1,0:T(8,128)S(1)} %get-tuple-element.22.keep_ref, f32[160,128]{1,0:T(8,128)S(1)} %collective-permute-done.19.other_t_ref, f32[512,128]{1,0:T(8,128)S(1)} %get-tuple-element.37.partial_ref), custom_call_target="tpu_custom_call" | custom-call | tf_op jit(solution)/shard_map/finish/pallas_call | solution.py:346
  (7 shorter events, 0.1 us)
Async XLA Ops:
  0.6 7.7 %copy-start.2 = (bf16[1,2,512,128]{3,2,1,0:T(8,128)(2,1)S(1)}, bf16[1,2,512,128]{3,2,1,0:T(8,128)(2,1)}, u32[]{:S(2)}) copy-start(bf16[1,2,512,128]{3,2,1,0:T(8,128)(2,1)} %param.10) | copy-start | bytes 786436
  2.6 5.7 %collective-permute-start = (bf16[640,128]{1,0:T(8,128)(2,1)}, bf16[640,128]{1,0:T(8,128)(2,1)S(1)}, u32[]{:S(2)}, u32[]{:S(2)}) collective-permute-start(bf16[640,128]{1,0:T(8,128)(2,1)} %pack.1.refs_0_), channel_id=1, source_target_pairs={{0,1},{1,0},{2,3},{3,2},{4,5},{5,4},{6,7},{7,6},{8,9},{9,8},{10,11... | collective-permute-start | bytes 491528 | tf_op jit(solution)/shard_map/ppermute | solution.py:205
  3.1 10.8 %collective-permute-start.1 = (bf16[640,128]{1,0:T(8,128)(2,1)}, bf16[640,128]{1,0:T(8,128)(2,1)S(1)}, u32[]{:S(2)}, u32[]{:S(2)}) collective-permute-start(bf16[640,128]{1,0:T(8,128)(2,1)} %pack.1.refs_0_), channel_id=1, source_target_pairs={{0,2},{2,0},{4,6},{6,4},{1,3},{3,1},{5,7},{7,5},{8,10},{10,8},{12,... | collective-permute-start | bytes 491528 | tf_op jit(solution)/shard_map/ppermute | solution.py:205
  5.7 15.2 %collective-permute-start.3 = (bf16[640,128]{1,0:T(8,128)(2,1)}, bf16[640,128]{1,0:T(8,128)(2,1)S(1)}, u32[]{:S(2)}, u32[]{:S(2)}) collective-permute-start(bf16[640,128]{1,0:T(8,128)(2,1)} %pack.1.refs_0_), channel_id=1, source_target_pairs={{0,4},{2,6},{4,0},{6,2},{1,5},{3,7},{5,1},{7,3},{8,12},{10,14},{12... | collective-permute-start | bytes 491528 | tf_op jit(solution)/shard_map/ppermute | solution.py:205
  8.3 12.6 %collective-permute-start.2 = (bf16[640,128]{1,0:T(8,128)(2,1)}, bf16[640,128]{1,0:T(8,128)(2,1)S(1)}, u32[]{:S(2)}, u32[]{:S(2)}) collective-permute-start(bf16[640,128]{1,0:T(8,128)(2,1)} %pack.1.refs_0_), channel_id=1, source_target_pairs={{0,6},{2,4},{4,2},{6,0},{1,7},{3,5},{5,3},{7,1},{8,14},{10,12},{12... | collective-permute-start | bytes 491528 | tf_op jit(solution)/shard_map/ppermute | solution.py:205
  8.3 0.7 %copy-start.3 = (s32[4]{0:T(128)S(1)}, s32[4]{0:T(128)}, u32[]{:S(2)}) copy-start(s32[4]{0:T(128)} %widths_ref.5) | copy-start | bytes 52
  8.3 0.7 %copy-start.4 = (f32[1,2]{1,0:T(1,128)S(1)}, f32[1,2]{1,0:T(1,128)}, u32[]{:S(2)}) copy-start(f32[1,2]{1,0:T(1,128)} %weights_ref.3) | copy-start | bytes 28
  9.0 0.9 %copy-start = (bf16[640,128]{1,0:T(8,128)(2,1)S(1)}, bf16[640,128]{1,0:T(8,128)(2,1)}, u32[]{:S(2)}) copy-start(bf16[640,128]{1,0:T(8,128)(2,1)} %pack.1.refs_0_) | copy-start | bytes 491524
  9.9 1.0 %copy-start.1 = (bf16[1,2,256,4,1,128]{5,3,4,2,1,0:T(4,128)(2,1)S(1)}, bf16[1,2,256,4,1,128]{5,3,4,2,1,0:T(4,128)(2,1)}, u32[]{:S(2)}) copy-start(bf16[1,2,256,4,1,128]{5,3,4,2,1,0:T(4,128)(2,1)} %param.6) | copy-start | bytes 1572868
  13.8 10.4 %collective-permute-start.10 = (f32[256,128]{1,0:T(8,128)S(1)}, f32[256,128]{1,0:T(8,128)S(1)}, u32[]{:S(2)}, u32[]{:S(2)}) collective-permute-start(f32[256,128]{1,0:T(8,128)S(1)} %get-tuple-element.32), channel_id=1, source_target_pairs={{0,8},{8,0},{16,24},{24,16},{1,9},{9,1},{17,25},{25,17},{2,10},{10... | collective-permute-start | bytes 393224 | tf_op jit(solution)/shard_map/ppermute | solution.py:205
  15.5 8.7 %collective-permute-start.12 = (f32[256,128]{1,0:T(8,128)S(1)}, f32[256,128]{1,0:T(8,128)S(1)}, u32[]{:S(2)}, u32[]{:S(2)}) collective-permute-start(f32[256,128]{1,0:T(8,128)S(1)} %get-tuple-element.32), channel_id=1, source_target_pairs={{0,24},{8,16},{16,8},{24,0},{1,25},{9,17},{17,9},{25,1},{2,26},{10... | collective-permute-start | bytes 393224 | tf_op jit(solution)/shard_map/ppermute | solution.py:205
  17.0 7.4 %collective-permute-start.11 = (f32[256,128]{1,0:T(8,128)S(1)}, f32[256,128]{1,0:T(8,128)S(1)}, u32[]{:S(2)}, u32[]{:S(2)}) collective-permute-start(f32[256,128]{1,0:T(8,128)S(1)} %get-tuple-element.32), channel_id=1, source_target_pairs={{0,16},{8,24},{16,0},{24,8},{1,17},{9,25},{17,1},{25,9},{2,18},{10... | collective-permute-start | bytes 393224 | tf_op jit(solution)/shard_map/ppermute | solution.py:205
  22.9 1.3 %collective-permute-start.9 = (f32[160,128]{1,0:T(8,128)S(1)}, f32[160,128]{1,0:T(8,128)S(1)}, u32[]{:S(2)}, u32[]{:S(2)}) collective-permute-start(f32[160,128]{1,0:T(8,128)S(1)} %get-tuple-element.31), channel_id=1, source_target_pairs={{0,1},{1,0},{2,3},{3,2},{4,5},{5,4},{6,7},{7,6},{8,9},{9,8},{10,11... | collective-permute-start | bytes 245768 | tf_op jit(solution)/shard_map/ppermute | solution.py:205
  23.0 4.3 %collective-permute-start.4 = (f32[160,256]{1,0:T(8,128)S(1)}, f32[160,256]{1,0:T(8,128)S(1)}, u32[]{:S(2)}, u32[]{:S(2)}) collective-permute-start(f32[160,256]{1,0:T(8,128)S(1)} %get-tuple-element.29), channel_id=1, source_target_pairs={{0,1},{1,0},{2,3},{3,2},{4,5},{5,4},{6,7},{7,6},{8,9},{9,8},{10,11... | collective-permute-start | bytes 491528 | tf_op jit(solution)/shard_map/ppermute | solution.py:205
  24.4 6.4 %collective-permute-start.13 = (f32[160,128]{1,0:T(8,128)S(1)}, f32[160,128]{1,0:T(8,128)S(1)}, u32[]{:S(2)}, u32[]{:S(2)}) collective-permute-start(f32[160,128]{1,0:T(8,128)S(1)} %add.43), channel_id=1, source_target_pairs={{0,6},{2,4},{4,2},{6,0},{1,7},{3,5},{5,3},{7,1},{8,14},{10,12},{12... | collective-permute-start | bytes 245768 | tf_op jit(solution)/shard_map/ppermute | solution.py:205
  27.3 11.0 %collective-permute-start.7 = (f32[160,256]{1,0:T(8,128)S(1)}, f32[160,256]{1,0:T(8,128)S(1)}, u32[]{:S(2)}, u32[]{:S(2)}) collective-permute-start(f32[160,256]{1,0:T(8,128)S(1)} %add.39), channel_id=1, source_target_pairs={{0,24},{8,16},{16,8},{24,0},{1,25},{9,17},{17,9},{25,1},{2,26},{10... | collective-permute-start | bytes 491528 | tf_op jit(solution)/shard_map/ppermute | solution.py:205
  29.4 9.4 %collective-permute-start.6 = (f32[160,256]{1,0:T(8,128)S(1)}, f32[160,256]{1,0:T(8,128)S(1)}, u32[]{:S(2)}, u32[]{:S(2)}) collective-permute-start(f32[160,256]{1,0:T(8,128)S(1)} %add.39), channel_id=1, source_target_pairs={{0,16},{8,24},{16,0},{24,8},{1,17},{9,25},{17,1},{25,9},{2,18},{10... | collective-permute-start | bytes 491528 | tf_op jit(solution)/shard_map/ppermute | solution.py:205
  30.3 9.0 %collective-permute-start.5 = (f32[160,256]{1,0:T(8,128)S(1)}, f32[160,256]{1,0:T(8,128)S(1)}, u32[]{:S(2)}, u32[]{:S(2)}) collective-permute-start(f32[160,256]{1,0:T(8,128)S(1)} %add.39), channel_id=1, source_target_pairs={{0,8},{8,0},{16,24},{24,16},{1,9},{9,1},{17,25},{25,17},{2,10},{10... | collective-permute-start | bytes 491528 | tf_op jit(solution)/shard_map/ppermute | solution.py:205
  30.8 4.9 %collective-permute-start.14 = (f32[160,128]{1,0:T(8,128)S(1)}, f32[160,128]{1,0:T(8,128)S(1)}, u32[]{:S(2)}, u32[]{:S(2)}) collective-permute-start(f32[160,128]{1,0:T(8,128)S(1)} %add.47), channel_id=1, source_target_pairs={{0,2},{2,0},{4,6},{6,4},{1,3},{3,1},{5,7},{7,5},{8,10},{10,8},{12,... | collective-permute-start | bytes 245768 | tf_op jit(solution)/shard_map/ppermute | solution.py:205
  33.1 10.2 %collective-permute-start.18 = (f32[256,128]{1,0:T(8,128)S(1)}, f32[256,128]{1,0:T(8,128)S(1)}, u32[]{:S(2)}, u32[]{:S(2)}) collective-permute-start(f32[256,128]{1,0:T(8,128)S(1)} %add_add_fusion.1.mine_term_ref), channel_id=1, source_target_pairs={{0,1},{1,0},{2,3},{3,2},{4,5},{5,4},{6,7},{7,6},{8,9},{9,8},{10,11... | collective-permute-start | bytes 393224 | tf_op jit(solution)/shard_map/ppermute | solution.py:205
  35.8 5.5 %collective-permute-start.17 = (f32[160,128]{1,0:T(8,128)S(1)}, f32[160,128]{1,0:T(8,128)S(1)}, u32[]{:S(2)}, u32[]{:S(2)}) collective-permute-start(f32[160,128]{1,0:T(8,128)S(1)} %add.48), channel_id=1, source_target_pairs={{0,24},{8,16},{16,8},{24,0},{1,25},{9,17},{17,9},{25,1},{2,26},{10... | collective-permute-start | bytes 245768 | tf_op jit(solution)/shard_map/ppermute | solution.py:205
  38.2 4.4 %collective-permute-start.16 = (f32[160,128]{1,0:T(8,128)S(1)}, f32[160,128]{1,0:T(8,128)S(1)}, u32[]{:S(2)}, u32[]{:S(2)}) collective-permute-start(f32[160,128]{1,0:T(8,128)S(1)} %add.48), channel_id=1, source_target_pairs={{0,16},{8,24},{16,0},{24,8},{1,17},{9,25},{17,1},{25,9},{2,18},{10... | collective-permute-start | bytes 245768 | tf_op jit(solution)/shard_map/ppermute | solution.py:205
  38.8 4.4 %collective-permute-start.15 = (f32[160,128]{1,0:T(8,128)S(1)}, f32[160,128]{1,0:T(8,128)S(1)}, u32[]{:S(2)}, u32[]{:S(2)}) collective-permute-start(f32[160,128]{1,0:T(8,128)S(1)} %add.48), channel_id=1, source_target_pairs={{0,8},{8,0},{16,24},{24,16},{1,9},{9,1},{17,25},{25,17},{2,10},{10... | collective-permute-start | bytes 245768 | tf_op jit(solution)/shard_map/ppermute | solution.py:205
  39.4 4.0 %collective-permute-start.8 = (f32[160,256]{1,0:T(8,128)S(1)}, f32[160,256]{1,0:T(8,128)S(1)}, u32[]{:S(2)}, u32[]{:S(2)}) collective-permute-start(f32[160,256]{1,0:T(8,128)S(1)} %add_add_fusion.mine_d_ref), channel_id=1, source_target_pairs={{0,1},{1,0},{2,3},{3,2},{4,5},{5,4},{6,7},{7,6},{8,9},{9,8},{10,11... | collective-permute-start | bytes 491528 | tf_op jit(solution)/shard_map/ppermute | solution.py:205
  43.3 1.3 %collective-permute-start.19 = (f32[160,128]{1,0:T(8,128)S(1)}, f32[160,128]{1,0:T(8,128)S(1)}, u32[]{:S(2)}, u32[]{:S(2)}) collective-permute-start(f32[160,128]{1,0:T(8,128)S(1)} %add_add_fusion.2.mine_t_ref), channel_id=1, source_target_pairs={{0,1},{1,0},{2,3},{3,2},{4,5},{5,4},{6,7},{7,6},{8,9},{9,8},{10,11... | collective-permute-start | bytes 245768 | tf_op jit(solution)/shard_map/ppermute | solution.py:205

commit v25 on v19

--- a/solution.py
+++ b/solution.py
@@ -309,7 +309,7 @@
     )
 
     tie = lax.optimization_barrier
-    products, send_d, term = tie((keep_t + swap(send_t, "col", top), send_d, term))
+    products, term = tie((keep_t + swap(send_t, "col", top), term))
     term = gather_but_last(term, "col")
     products = scatter_rest(products, "col")
     for bit in bits_of(row_count)[::-1]:

time: 46.2 us -> 46.1 us (level)
  starting transfers between devices: 23.9 us -> 23.4 us
  waiting for transfers between devices: 10.9 us -> 11.4 us
    ppermute x20, starting transfers between devices: 23.9 us -> 23.4 us  [swap(): lax.ppermute(value, axis, [(i, i ^ bit) for i in range(lax.axis_size(axis...]
    ppermute x20, waiting for transfers between devices: 10.9 us -> 11.4 us  [swap(): lax.ppermute(value, axis, [(i, i ^ bit) for i in range(lax.axis_size(axis...]
where the time goes in v25:
time: 46.1 us; the launch traced here: 45.9 us
  starting transfers between devices  23.4 us (51%)
  waiting for transfers between devices  11.4 us (25%)
  Pallas kernels  7.5 us (16%)
  local copies, waits for them, and re-layouts  2.63 us (6%)
  between operations  0.76 us (2%)
    ppermute x20, starting transfers between devices, swap(): lax.ppermute(value, axis, [(i, i ^ bit) for i in range(lax.axis_size(axis...  23.4 us
    ppermute x20, waiting for transfers between devices, swap(): lax.ppermute(value, axis, [(i, i ^ bit) for i in range(lax.axis_size(axis...  11.4 us
    unnamed x10, local copies, waits for them, and re-layouts  2.63 us
    pallas_call x1, Pallas kernels, per_device(): pl.pallas_call(functools.partial(pack_kernel, supernodes, slot), in_specs...  2 us
    pallas_call x1, Pallas kernels, per_device(): pl.pallas_call(functools.partial(compute_kernel, others, col_count, super...  1.99 us
    pallas_call x1, Pallas kernels, per_device(): pl.pallas_call(functools.partial(prepare_kernel, (row_count, col_count)),...  1.38 us
    pallas_call x1, Pallas kernels, per_device(): pl.pallas_call(expand_kernel, in_specs=[VMEM_SPEC] * 9, out_specs=[VMEM_S...  1.14 us
    pallas_call x1, Pallas kernels, per_device(): pl.pallas_call(finish_kernel, in_specs=[VMEM_SPEC] * 4, out_specs=VMEM_SP...  0.99 us
  transfers between devices with their start and end apart: 20, of which 7 were waited for; matrix products, arithmetic and copies ran while one was open for 0% of the time, Pallas kernels for 10%

profile of v25, /device:TPU:0, one launch (start us, length us, event | category | flops | bytes accessed | tf_op | source)
XLA Modules:
  0.0 45.9 jit_solution(5089413465642388132)
XLA Ops:
  0.6 0.0 copy-start.2
  0.6 2.0 %pack.1.refs_0_ = bf16[640,128]{1,0:T(8,128)(2,1)} custom-call(s32[1,4]{1,0:T(1,128)} %pattern_ref.1, s32[4]{0:T(128)} %widths_ref.5, bf16[2,128,512]{2,1,0:T(8,128)(2,1)} %bitcast.7), custom_call_target="tpu_custom_call" | custom-call | tf_op jit(solution)/shard_map/pack/pallas_call | solution.py:252
  2.6 0.5 collective-permute-start
  3.1 3.6 %collective-permute-start.3 = (bf16[640,128]{1,0:T(8,128)(2,1)}, bf16[640,128]{1,0:T(8,128)(2,1)S(1)}, u32[]{:S(2)}, u32[]{:S(2)}) collective-permute-start(bf16[640,128]{1,0:T(8,128)(2,1)} %pack.1.refs_0_), channel_id=1, source_target_pairs={{0,4},{2,6},{4,0},{6,2},{1,5},{3,7},{5,1},{7,3},{8,12},{10,14},{12... | collective-permute-start | bytes 491528 | tf_op jit(solution)/shard_map/ppermute | solution.py:205
  6.7 1.4 %collective-permute-start.2 = (bf16[640,128]{1,0:T(8,128)(2,1)}, bf16[640,128]{1,0:T(8,128)(2,1)S(1)}, u32[]{:S(2)}, u32[]{:S(2)}) collective-permute-start(bf16[640,128]{1,0:T(8,128)(2,1)} %pack.1.refs_0_), channel_id=1, source_target_pairs={{0,6},{2,4},{4,2},{6,0},{1,7},{3,5},{5,3},{7,1},{8,14},{10,12},{12... | collective-permute-start | bytes 491528 | tf_op jit(solution)/shard_map/ppermute | solution.py:205
  8.0 0.2 collective-permute-start.1
  8.3 0.1 pad_add_fusion.place_ref
  8.3 0.0 collective-permute-done.refs_1_
  8.3 0.0 copy-start.3
  8.3 0.0 copy-start.4
  8.3 0.0 copy-done.2
  8.3 0.6 %copy-done.3 = s32[4]{0:T(128)S(1)} copy-done((s32[4]{0:T(128)S(1)}, s32[4]{0:T(128)}, u32[]{:S(2)}) %copy-start.3) | copy-done | bytes 40
  9.0 0.0 copy-done.4
  9.0 0.0 copy-start
  9.0 0.9 %copy-done = bf16[640,128]{1,0:T(8,128)(2,1)S(1)} copy-done((bf16[640,128]{1,0:T(8,128)(2,1)S(1)}, bf16[640,128]{1,0:T(8,128)(2,1)}, u32[]{:S(2)}) %copy-start) | copy-done | bytes 163864
  9.9 0.0 copy-start.1
  9.9 1.0 %copy-done.1 = bf16[1,2,256,4,1,128]{5,3,4,2,1,0:T(4,128)(2,1)S(1)} copy-done((bf16[1,2,256,4,1,128]{5,3,4,2,1,0:T(4,128)(2,1)S(1)}, bf16[1,2,256,4,1,128]{5,3,4,2,1,0:T(4,128)(2,1)}, u32[]{:S(2)}) %copy-start.1) | copy-done | bytes 524312
  11.0 1.4 %prepare.1 = (bf16[2,256,512]{2,1,0:T(8,128)(2,1)S(1)}, bf16[512,512]{1,0:T(8,128)(2,1)S(1)}, f32[256,128]{1,0:T(8,128)S(1)}, bf16[256,320]{1,0:T(8,128)(2,1)S(1...) custom-call(s32[4]{0:T(128)S(1)} %copy-done.3, ...), custom_call_target="tpu_custom_call" | custom-call | flops 134217728 | bytes 1048576 | tf_op jit(solution)/shard_map/prepare/pallas_call | solution.py:266
  12.4 2.5 %collective-permute-start.12 = (f32[256,128]{1,0:T(8,128)S(1)}, f32[256,128]{1,0:T(8,128)S(1)}, u32[]{:S(2)}, u32[]{:S(2)}) collective-permute-start(f32[256,128]{1,0:T(8,128)S(1)} %get-tuple-element.28), channel_id=1, source_target_pairs={{0,24},{8,16},{16,8},{24,0},{1,25},{9,17},{17,9},{25,1},{2,26},{10... | collective-permute-start | bytes 393224 | tf_op jit(solution)/shard_map/ppermute | solution.py:205
  14.9 0.5 %collective-permute-start.11 = (f32[256,128]{1,0:T(8,128)S(1)}, f32[256,128]{1,0:T(8,128)S(1)}, u32[]{:S(2)}, u32[]{:S(2)}) collective-permute-start(f32[256,128]{1,0:T(8,128)S(1)} %get-tuple-element.28), channel_id=1, source_target_pairs={{0,16},{8,24},{16,0},{24,8},{1,17},{9,25},{17,1},{25,9},{2,18},{10... | collective-permute-start | bytes 393224 | tf_op jit(solution)/shard_map/ppermute | solution.py:205
  15.4 3.6 %collective-permute-done.3.refs_3_ = bf16[640,128]{1,0:T(8,128)(2,1)S(1)} collective-permute-done((bf16[640,128]{1,0:T(8,128)(2,1)}, bf16[640,128]{1,0:T(8,128)(2,1)S(1)}, u32[]{:S(2)}, u32[]{:S(2)}) %collective-permute-start.3) | collective-permute-done | bytes 163872 | tf_op jit(solution)/shard_map/ppermute | solution.py:205
  19.0 1.7 %collective-permute-start.10 = (f32[256,128]{1,0:T(8,128)S(1)}, f32[256,128]{1,0:T(8,128)S(1)}, u32[]{:S(2)}, u32[]{:S(2)}) collective-permute-start(f32[256,128]{1,0:T(8,128)S(1)} %get-tuple-element.28), channel_id=1, source_target_pairs={{0,8},{8,0},{16,24},{24,16},{1,9},{9,1},{17,25},{25,17},{2,10},{10... | collective-permute-start | bytes 393224 | tf_op jit(solution)/shard_map/ppermute | solution.py:205
  20.8 0.0 collective-permute-done.2.refs_2_
  20.8 0.0 collective-permute-done.1.refs_1_
  20.8 2.0 %compute.1 = (f32[160,256]{1,0:T(8,128)S(1)}, f32[160,256]{1,0:T(8,128)S(1)}, f32[160,128]{1,0:T(8,128)S(1)}, f32[160,128]{1,0:T(8,128)S(1)}) custom-call(s32[4]{0:T(128)S(1)} %copy-done.3, f32[1,2]{1,0:T(1,128)S(1)} %copy-done.4, s32[2]{0:T(128)S(1)} %pad_add_fusion.place_ref, bf16[2,256,512]{2,1,0:T(8,128)(2,1)S(1)} %get-tuple-element.22.straight_ref, ...), custom_call_target="tpu_custom_call" | custom-call | tf_op jit(solution)/shard_map/compute/pallas_call | solution.py:293
  22.8 0.1 collective-permute-start.9
  22.8 0.5 %collective-permute-start.4 = (f32[160,256]{1,0:T(8,128)S(1)}, f32[160,256]{1,0:T(8,128)S(1)}, u32[]{:S(2)}, u32[]{:S(2)}) collective-permute-start(f32[160,256]{1,0:T(8,128)S(1)} %get-tuple-element.25), channel_id=1, source_target_pairs={{0,1},{1,0},{2,3},{3,2},{4,5},{5,4},{6,7},{7,6},{8,9},{9,8},{10,11... | collective-permute-start | bytes 491528 | tf_op jit(solution)/shard_map/ppermute | solution.py:205
  23.3 0.8 %collective-permute-done.9 = f32[160,128]{1,0:T(8,128)S(1)} collective-permute-done((f32[160,128]{1,0:T(8,128)S(1)}, f32[160,128]{1,0:T(8,128)S(1)}, u32[]{:S(2)}, u32[]{:S(2)}) %collective-permute-start.9) | collective-permute-done | bytes 81952 | tf_op jit(solution)/shard_map/ppermute | solution.py:205
  24.1 0.0 collective-permute-done.12
  24.1 0.0 collective-permute-done.11
  24.1 0.0 collective-permute-done.10
  24.2 3.8 %collective-permute-start.13 = (f32[160,128]{1,0:T(8,128)S(1)}, f32[160,128]{1,0:T(8,128)S(1)}, u32[]{:S(2)}, u32[]{:S(2)}) collective-permute-start(f32[160,128]{1,0:T(8,128)S(1)} %add.43), channel_id=1, source_target_pairs={{0,6},{2,4},{4,2},{6,0},{1,7},{3,5},{5,3},{7,1},{8,14},{10,12},{12... | collective-permute-start | bytes 245768 | tf_op jit(solution)/shard_map/ppermute | solution.py:205
  27.9 0.0 collective-permute-done.4
  28.0 2.5 %collective-permute-start.7 = (f32[160,256]{1,0:T(8,128)S(1)}, f32[160,256]{1,0:T(8,128)S(1)}, u32[]{:S(2)}, u32[]{:S(2)}) collective-permute-start(f32[160,256]{1,0:T(8,128)S(1)} %add.39), channel_id=1, source_target_pairs={{0,24},{8,16},{16,8},{24,0},{1,25},{9,17},{17,9},{25,1},{2,26},{10... | collective-permute-start | bytes 491528 | tf_op jit(solution)/shard_map/ppermute | solution.py:205
  30.5 0.5 %collective-permute-start.6 = (f32[160,256]{1,0:T(8,128)S(1)}, f32[160,256]{1,0:T(8,128)S(1)}, u32[]{:S(2)}, u32[]{:S(2)}) collective-permute-start(f32[160,256]{1,0:T(8,128)S(1)} %add.39), channel_id=1, source_target_pairs={{0,16},{8,24},{16,0},{24,8},{1,17},{9,25},{17,1},{25,9},{2,18},{10... | collective-permute-start | bytes 491528 | tf_op jit(solution)/shard_map/ppermute | solution.py:205
  31.0 0.5 %collective-permute-start.5 = (f32[160,256]{1,0:T(8,128)S(1)}, f32[160,256]{1,0:T(8,128)S(1)}, u32[]{:S(2)}, u32[]{:S(2)}) collective-permute-start(f32[160,256]{1,0:T(8,128)S(1)} %add.39), channel_id=1, source_target_pairs={{0,8},{8,0},{16,24},{24,16},{1,9},{9,1},{17,25},{25,17},{2,10},{10... | collective-permute-start | bytes 491528 | tf_op jit(solution)/shard_map/ppermute | solution.py:205
  31.5 0.0 collective-permute-done.13
  31.5 1.4 %collective-permute-start.14 = (f32[160,128]{1,0:T(8,128)S(1)}, f32[160,128]{1,0:T(8,128)S(1)}, u32[]{:S(2)}, u32[]{:S(2)}) collective-permute-start(f32[160,128]{1,0:T(8,128)S(1)} %add.47), channel_id=1, source_target_pairs={{0,2},{2,0},{4,6},{6,4},{1,3},{3,1},{5,7},{7,5},{8,10},{10,8},{12,... | collective-permute-start | bytes 245768 | tf_op jit(solution)/shard_map/ppermute | solution.py:205
  33.0 0.0 collective-permute-start.18
  33.0 3.1 %collective-permute-done.14 = f32[160,128]{1,0:T(8,128)S(1)} collective-permute-done((f32[160,128]{1,0:T(8,128)S(1)}, f32[160,128]{1,0:T(8,128)S(1)}, u32[]{:S(2)}, u32[]{:S(2)}) %collective-permute-start.14) | collective-permute-done | bytes 81952 | tf_op jit(solution)/shard_map/ppermute | solution.py:205
  36.1 2.5 %collective-permute-start.17 = (f32[160,128]{1,0:T(8,128)S(1)}, f32[160,128]{1,0:T(8,128)S(1)}, u32[]{:S(2)}, u32[]{:S(2)}) collective-permute-start(f32[160,128]{1,0:T(8,128)S(1)} %add.48), channel_id=1, source_target_pairs={{0,24},{8,16},{16,8},{24,0},{1,25},{9,17},{17,9},{25,1},{2,26},{10... | collective-permute-start | bytes 245768 | tf_op jit(solution)/shard_map/ppermute | solution.py:205
  38.6 0.0 collective-permute-done.7
  38.6 0.5 %collective-permute-start.16 = (f32[160,128]{1,0:T(8,128)S(1)}, f32[160,128]{1,0:T(8,128)S(1)}, u32[]{:S(2)}, u32[]{:S(2)}) collective-permute-start(f32[160,128]{1,0:T(8,128)S(1)} %add.48), channel_id=1, source_target_pairs={{0,16},{8,24},{16,0},{24,8},{1,17},{9,25},{17,1},{25,9},{2,18},{10... | collective-permute-start | bytes 245768 | tf_op jit(solution)/shard_map/ppermute | solution.py:205
  39.1 0.0 collective-permute-done.6
  39.1 0.5 %collective-permute-start.15 = (f32[160,128]{1,0:T(8,128)S(1)}, f32[160,128]{1,0:T(8,128)S(1)}, u32[]{:S(2)}, u32[]{:S(2)}) collective-permute-start(f32[160,128]{1,0:T(8,128)S(1)} %add.48), channel_id=1, source_target_pairs={{0,8},{8,0},{16,24},{24,16},{1,9},{9,1},{17,25},{25,17},{2,10},{10... | collective-permute-start | bytes 245768 | tf_op jit(solution)/shard_map/ppermute | solution.py:205
  39.6 0.0 collective-permute-done.5
  39.7 0.1 collective-permute-start.8
  39.8 1.8 %collective-permute-done.17 = f32[160,128]{1,0:T(8,128)S(1)} collective-permute-done((f32[160,128]{1,0:T(8,128)S(1)}, f32[160,128]{1,0:T(8,128)S(1)}, u32[]{:S(2)}, u32[]{:S(2)}) %collective-permute-start.17) | collective-permute-done | bytes 81952 | tf_op jit(solution)/shard_map/ppermute | solution.py:205
  41.6 1.4 %collective-permute-done.16 = f32[160,128]{1,0:T(8,128)S(1)} collective-permute-done((f32[160,128]{1,0:T(8,128)S(1)}, f32[160,128]{1,0:T(8,128)S(1)}, u32[]{:S(2)}, u32[]{:S(2)}) %collective-permute-start.16) | collective-permute-done | bytes 81952 | tf_op jit(solution)/shard_map/ppermute | solution.py:205
  43.0 0.5 %collective-permute-done.15 = f32[160,128]{1,0:T(8,128)S(1)} collective-permute-done((f32[160,128]{1,0:T(8,128)S(1)}, f32[160,128]{1,0:T(8,128)S(1)}, u32[]{:S(2)}, u32[]{:S(2)}) %collective-permute-start.15) | collective-permute-done | bytes 81952 | tf_op jit(solution)/shard_map/ppermute | solution.py:205
  43.6 0.1 collective-permute-start.19
  43.6 0.0 collective-permute-done.18.other_term_ref
  43.6 0.0 collective-permute-done.8.other_d_ref
  43.7 1.1 %expand.1 = (f32[256,256]{1,0:T(8,128)}, f32[512,128]{1,0:T(8,128)S(1)}) custom-call(bf16[256,320]{1,0:T(8,128)(2,1)S(1)} %get-tuple-element.18.pick_d_ref, bf16[512,160]{1,0:T(8,128)(2,1)S(1)} %get-tuple-element.19.pick_ref, f32[512,128]{1,0:T(8,128)S(1)} %get-tuple-element.20.keep_ref, f32[8,128]{1,0:T(8,128)S(1)} %get-tuple-element.21.upper_ref, ...), custom_call_target="tpu_custom_call" | custom-call | flops 503316480 | bytes 2097152 | tf_op jit(solution)/shard_map/expand/pallas_call | solution.py:323
  44.8 0.1 collective-permute-done.19.other_t_ref
  44.9 1.0 %finish.1 = f32[512,128]{1,0:T(8,128)} custom-call(bf16[512,160]{1,0:T(8,128)(2,1)S(1)} %get-tuple-element.32.pick_ref, f32[512,128]{1,0:T(8,128)S(1)} %get-tuple-element.20.keep_ref, f32[160,128]{1,0:T(8,128)S(1)} %collective-permute-done.19.other_t_ref, f32[512,128]{1,0:T(8,128)S(1)} %get-tuple-element.33.partial_ref), custom_call_target="tpu_custom_call" | custom-call | tf_op jit(solution)/shard_map/finish/pallas_call | solution.py:342
  (7 shorter events, 0.1 us)
Async XLA Ops:
  0.6 7.7 %copy-start.2 = (bf16[1,2,512,128]{3,2,1,0:T(8,128)(2,1)S(1)}, bf16[1,2,512,128]{3,2,1,0:T(8,128)(2,1)}, u32[]{:S(2)}) copy-start(bf16[1,2,512,128]{3,2,1,0:T(8,128)(2,1)} %param.10) | copy-start | bytes 786436
  2.6 5.7 %collective-permute-start = (bf16[640,128]{1,0:T(8,128)(2,1)}, bf16[640,128]{1,0:T(8,128)(2,1)S(1)}, u32[]{:S(2)}, u32[]{:S(2)}) collective-permute-start(bf16[640,128]{1,0:T(8,128)(2,1)} %pack.1.refs_0_), channel_id=1, source_target_pairs={{0,1},{1,0},{2,3},{3,2},{4,5},{5,4},{6,7},{7,6},{8,9},{9,8},{10,11... | collective-permute-start | bytes 491528 | tf_op jit(solution)/shard_map/ppermute | solution.py:205
  3.1 15.9 %collective-permute-start.3 = (bf16[640,128]{1,0:T(8,128)(2,1)}, bf16[640,128]{1,0:T(8,128)(2,1)S(1)}, u32[]{:S(2)}, u32[]{:S(2)}) collective-permute-start(bf16[640,128]{1,0:T(8,128)(2,1)} %pack.1.refs_0_), channel_id=1, source_target_pairs={{0,4},{2,6},{4,0},{6,2},{1,5},{3,7},{5,1},{7,3},{8,12},{10,14},{12... | collective-permute-start | bytes 491528 | tf_op jit(solution)/shard_map/ppermute | solution.py:205
  6.7 14.1 %collective-permute-start.2 = (bf16[640,128]{1,0:T(8,128)(2,1)}, bf16[640,128]{1,0:T(8,128)(2,1)S(1)}, u32[]{:S(2)}, u32[]{:S(2)}) collective-permute-start(bf16[640,128]{1,0:T(8,128)(2,1)} %pack.1.refs_0_), channel_id=1, source_target_pairs={{0,6},{2,4},{4,2},{6,0},{1,7},{3,5},{5,3},{7,1},{8,14},{10,12},{12... | collective-permute-start | bytes 491528 | tf_op jit(solution)/shard_map/ppermute | solution.py:205
  8.0 12.7 %collective-permute-start.1 = (bf16[640,128]{1,0:T(8,128)(2,1)}, bf16[640,128]{1,0:T(8,128)(2,1)S(1)}, u32[]{:S(2)}, u32[]{:S(2)}) collective-permute-start(bf16[640,128]{1,0:T(8,128)(2,1)} %pack.1.refs_0_), channel_id=1, source_target_pairs={{0,2},{2,0},{4,6},{6,4},{1,3},{3,1},{5,7},{7,5},{8,10},{10,8},{12,... | collective-permute-start | bytes 491528 | tf_op jit(solution)/shard_map/ppermute | solution.py:205
  8.3 0.7 %copy-start.3 = (s32[4]{0:T(128)S(1)}, s32[4]{0:T(128)}, u32[]{:S(2)}) copy-start(s32[4]{0:T(128)} %widths_ref.5) | copy-start | bytes 52
  8.3 0.7 %copy-start.4 = (f32[1,2]{1,0:T(1,128)S(1)}, f32[1,2]{1,0:T(1,128)}, u32[]{:S(2)}) copy-start(f32[1,2]{1,0:T(1,128)} %weights_ref.3) | copy-start | bytes 28
  9.0 0.9 %copy-start = (bf16[640,128]{1,0:T(8,128)(2,1)S(1)}, bf16[640,128]{1,0:T(8,128)(2,1)}, u32[]{:S(2)}) copy-start(bf16[640,128]{1,0:T(8,128)(2,1)} %pack.1.refs_0_) | copy-start | bytes 491524
  9.9 1.0 %copy-start.1 = (bf16[1,2,256,4,1,128]{5,3,4,2,1,0:T(4,128)(2,1)S(1)}, bf16[1,2,256,4,1,128]{5,3,4,2,1,0:T(4,128)(2,1)}, u32[]{:S(2)}) copy-start(bf16[1,2,256,4,1,128]{5,3,4,2,1,0:T(4,128)(2,1)} %param.6) | copy-start | bytes 1572868
  12.4 11.8 %collective-permute-start.12 = (f32[256,128]{1,0:T(8,128)S(1)}, f32[256,128]{1,0:T(8,128)S(1)}, u32[]{:S(2)}, u32[]{:S(2)}) collective-permute-start(f32[256,128]{1,0:T(8,128)S(1)} %get-tuple-element.28), channel_id=1, source_target_pairs={{0,24},{8,16},{16,8},{24,0},{1,25},{9,17},{17,9},{25,1},{2,26},{10... | collective-permute-start | bytes 393224 | tf_op jit(solution)/shard_map/ppermute | solution.py:205
  14.9 9.3 %collective-permute-start.11 = (f32[256,128]{1,0:T(8,128)S(1)}, f32[256,128]{1,0:T(8,128)S(1)}, u32[]{:S(2)}, u32[]{:S(2)}) collective-permute-start(f32[256,128]{1,0:T(8,128)S(1)} %get-tuple-element.28), channel_id=1, source_target_pairs={{0,16},{8,24},{16,0},{24,8},{1,17},{9,25},{17,1},{25,9},{2,18},{10... | collective-permute-start | bytes 393224 | tf_op jit(solution)/shard_map/ppermute | solution.py:205
  19.0 5.1 %collective-permute-start.10 = (f32[256,128]{1,0:T(8,128)S(1)}, f32[256,128]{1,0:T(8,128)S(1)}, u32[]{:S(2)}, u32[]{:S(2)}) collective-permute-start(f32[256,128]{1,0:T(8,128)S(1)} %get-tuple-element.28), channel_id=1, source_target_pairs={{0,8},{8,0},{16,24},{24,16},{1,9},{9,1},{17,25},{25,17},{2,10},{10... | collective-permute-start | bytes 393224 | tf_op jit(solution)/shard_map/ppermute | solution.py:205
  22.8 1.3 %collective-permute-start.9 = (f32[160,128]{1,0:T(8,128)S(1)}, f32[160,128]{1,0:T(8,128)S(1)}, u32[]{:S(2)}, u32[]{:S(2)}) collective-permute-start(f32[160,128]{1,0:T(8,128)S(1)} %get-tuple-element.27), channel_id=1, source_target_pairs={{0,1},{1,0},{2,3},{3,2},{4,5},{5,4},{6,7},{7,6},{8,9},{9,8},{10,11... | collective-permute-start | bytes 245768 | tf_op jit(solution)/shard_map/ppermute | solution.py:205
  22.8 5.1 %collective-permute-start.4 = (f32[160,256]{1,0:T(8,128)S(1)}, f32[160,256]{1,0:T(8,128)S(1)}, u32[]{:S(2)}, u32[]{:S(2)}) collective-permute-start(f32[160,256]{1,0:T(8,128)S(1)} %get-tuple-element.25), channel_id=1, source_target_pairs={{0,1},{1,0},{2,3},{3,2},{4,5},{5,4},{6,7},{7,6},{8,9},{9,8},{10,11... | collective-permute-start | bytes 491528 | tf_op jit(solution)/shard_map/ppermute | solution.py:205
  24.2 7.3 %collective-permute-start.13 = (f32[160,128]{1,0:T(8,128)S(1)}, f32[160,128]{1,0:T(8,128)S(1)}, u32[]{:S(2)}, u32[]{:S(2)}) collective-permute-start(f32[160,128]{1,0:T(8,128)S(1)} %add.43), channel_id=1, source_target_pairs={{0,6},{2,4},{4,2},{6,0},{1,7},{3,5},{5,3},{7,1},{8,14},{10,12},{12... | collective-permute-start | bytes 245768 | tf_op jit(solution)/shard_map/ppermute | solution.py:205
  28.0 10.6 %collective-permute-start.7 = (f32[160,256]{1,0:T(8,128)S(1)}, f32[160,256]{1,0:T(8,128)S(1)}, u32[]{:S(2)}, u32[]{:S(2)}) collective-permute-start(f32[160,256]{1,0:T(8,128)S(1)} %add.39), channel_id=1, source_target_pairs={{0,24},{8,16},{16,8},{24,0},{1,25},{9,17},{17,9},{25,1},{2,26},{10... | collective-permute-start | bytes 491528 | tf_op jit(solution)/shard_map/ppermute | solution.py:205
  30.5 8.6 %collective-permute-start.6 = (f32[160,256]{1,0:T(8,128)S(1)}, f32[160,256]{1,0:T(8,128)S(1)}, u32[]{:S(2)}, u32[]{:S(2)}) collective-permute-start(f32[160,256]{1,0:T(8,128)S(1)} %add.39), channel_id=1, source_target_pairs={{0,16},{8,24},{16,0},{24,8},{1,17},{9,25},{17,1},{25,9},{2,18},{10... | collective-permute-start | bytes 491528 | tf_op jit(solution)/shard_map/ppermute | solution.py:205
  31.0 8.6 %collective-permute-start.5 = (f32[160,256]{1,0:T(8,128)S(1)}, f32[160,256]{1,0:T(8,128)S(1)}, u32[]{:S(2)}, u32[]{:S(2)}) collective-permute-start(f32[160,256]{1,0:T(8,128)S(1)} %add.39), channel_id=1, source_target_pairs={{0,8},{8,0},{16,24},{24,16},{1,9},{9,1},{17,25},{25,17},{2,10},{10... | collective-permute-start | bytes 491528 | tf_op jit(solution)/shard_map/ppermute | solution.py:205
  31.5 4.5 %collective-permute-start.14 = (f32[160,128]{1,0:T(8,128)S(1)}, f32[160,128]{1,0:T(8,128)S(1)}, u32[]{:S(2)}, u32[]{:S(2)}) collective-permute-start(f32[160,128]{1,0:T(8,128)S(1)} %add.47), channel_id=1, source_target_pairs={{0,2},{2,0},{4,6},{6,4},{1,3},{3,1},{5,7},{7,5},{8,10},{10,8},{12,... | collective-permute-start | bytes 245768 | tf_op jit(solution)/shard_map/ppermute | solution.py:205
  33.0 10.7 %collective-permute-start.18 = (f32[256,128]{1,0:T(8,128)S(1)}, f32[256,128]{1,0:T(8,128)S(1)}, u32[]{:S(2)}, u32[]{:S(2)}) collective-permute-start(f32[256,128]{1,0:T(8,128)S(1)} %add_add_fusion.1.mine_term_ref), channel_id=1, source_target_pairs={{0,1},{1,0},{2,3},{3,2},{4,5},{5,4},{6,7},{7,6},{8,9},{9,8},{10,11... | collective-permute-start | bytes 393224 | tf_op jit(solution)/shard_map/ppermute | solution.py:205
  36.1 5.5 %collective-permute-start.17 = (f32[160,128]{1,0:T(8,128)S(1)}, f32[160,128]{1,0:T(8,128)S(1)}, u32[]{:S(2)}, u32[]{:S(2)}) collective-permute-start(f32[160,128]{1,0:T(8,128)S(1)} %add.48), channel_id=1, source_target_pairs={{0,24},{8,16},{16,8},{24,0},{1,25},{9,17},{17,9},{25,1},{2,26},{10... | collective-permute-start | bytes 245768 | tf_op jit(solution)/shard_map/ppermute | solution.py:205
  38.6 4.4 %collective-permute-start.16 = (f32[160,128]{1,0:T(8,128)S(1)}, f32[160,128]{1,0:T(8,128)S(1)}, u32[]{:S(2)}, u32[]{:S(2)}) collective-permute-start(f32[160,128]{1,0:T(8,128)S(1)} %add.48), channel_id=1, source_target_pairs={{0,16},{8,24},{16,0},{24,8},{1,17},{9,25},{17,1},{25,9},{2,18},{10... | collective-permute-start | bytes 245768 | tf_op jit(solution)/shard_map/ppermute | solution.py:205
  39.1 4.4 %collective-permute-start.15 = (f32[160,128]{1,0:T(8,128)S(1)}, f32[160,128]{1,0:T(8,128)S(1)}, u32[]{:S(2)}, u32[]{:S(2)}) collective-permute-start(f32[160,128]{1,0:T(8,128)S(1)} %add.48), channel_id=1, source_target_pairs={{0,8},{8,0},{16,24},{24,16},{1,9},{9,1},{17,25},{25,17},{2,10},{10... | collective-permute-start | bytes 245768 | tf_op jit(solution)/shard_map/ppermute | solution.py:205
  39.7 4.0 %collective-permute-start.8 = (f32[160,256]{1,0:T(8,128)S(1)}, f32[160,256]{1,0:T(8,128)S(1)}, u32[]{:S(2)}, u32[]{:S(2)}) collective-permute-start(f32[160,256]{1,0:T(8,128)S(1)} %add_add_fusion.mine_d_ref), channel_id=1, source_target_pairs={{0,1},{1,0},{2,3},{3,2},{4,5},{5,4},{6,7},{7,6},{8,9},{9,8},{10,11... | collective-permute-start | bytes 491528 | tf_op jit(solution)/shard_map/ppermute | solution.py:205
  43.6 1.3 %collective-permute-start.19 = (f32[160,128]{1,0:T(8,128)S(1)}, f32[160,128]{1,0:T(8,128)S(1)}, u32[]{:S(2)}, u32[]{:S(2)}) collective-permute-start(f32[160,128]{1,0:T(8,128)S(1)} %add_add_fusion.2.mine_t_ref), channel_id=1, source_target_pairs={{0,1},{1,0},{2,3},{3,2},{4,5},{5,4},{6,7},{7,6},{8,9},{9,8},{10,11... | collective-permute-start | bytes 245768 | tf_op jit(solution)/shard_map/ppermute | solution.py:205
